TPU v7x, 32 devices: a whole 2x2x4 slice. The times are simulated.
32 devices in a mesh: dp: 4 (over y, x), wide: 8 (over z, core).
Axes of the slice: x: 2, y: 2, z: 4, core: 2. Of those that a mesh axis runs over, the one named last changes fastest.
Arguments:
- tokens: bfloat16 [8192, 768], P(('dp', 'wide'))
- cluster_ids: int32 [8192, 12], P(('dp', 'wide')), may hold values from 0 to 127, as said below
- lengths: int32 [4], P('dp'), may hold values from 1793 to 2048, as said below
- top_keys: int32 [4, 12, 128, 32], P('dp', None, 'wide'), may hold values from 0 to 2047, as said below
- gain_one: float32 [768], replicated, may hold values from 0.25 to 1.75
- shift_one: float32 [768], replicated, may hold values from -1.8 to 1.8
- w_query: bfloat16 [768, 768], replicated, may hold values from -0.625 to 0.625
- w_keyval: bfloat16 [768, 1536], replicated, may hold values from -0.21875 to 0.21875
- w_out: bfloat16 [768, 768], replicated, may hold values from -6 to 6
- gain_two: float32 [768], replicated, may hold values from 0.25 to 1.75
- shift_two: float32 [768], replicated, may hold values from -1.8 to 1.8
- w_up: bfloat16 [768, 3072], replicated, may hold values from -0.21875 to 0.21875
- w_down: bfloat16 [3072, 768], replicated, may hold values from -0.109375 to 0.109375
- cotangent: bfloat16 [8192, 768], P(('dp', 'wide')), may hold values from -6 to 6
Outputs:
- output: bfloat16 [8192, 768], P(('dp', 'wide'))
- grad_tokens: bfloat16 [8192, 768], P(('dp', 'wide'))
- grad_query: float32 [768, 768], P('wide')
- grad_keyval: float32 [768, 1536], P('wide')
- grad_out: float32 [768, 768], P('wide')
- grad_up: float32 [768, 3072], P('wide')
- grad_down: float32 [3072, 768], P('wide')
- grad_gain_one: float32 [768], P('wide')
- grad_shift_one: float32 [768], P('wide')
- grad_gain_two: float32 [768], P('wide')
- grad_shift_two: float32 [768], P('wide')
Inputs may be any that keep to these rules, and one draw needn't show every extreme that they name: `cluster_ids`: within each aligned block of 256 rows (the rows of one device) and each head, at most 4 rows name the same cluster; in each head one cluster is named by exactly 4 rows of every block. `lengths`: one sequence has the full length 2048. `top_keys`: the 32 positions of a cluster are distinct and below its sequence's length.
All inputs are finite; a program needn't handle non-finite values.
Results may differ from a plain program's by a relative error of at most 0.015.
Values may be sent and summed in bfloat16 or wider, within the bound.
No kernel may reach another device: no remote copies, remote signals or barrier semaphores. Data moves between devices by JAX's collectives and lax.ppermute only.
A program may use at most 640 MiB of HBM per device.

v0:
```python
import jax
import jax.numpy as jnp
import numpy as np
from jax import lax
from jax.sharding import PartitionSpec as P

EPSILON = 1e-05
NEGATIVE = -1e30


def normalize(values, gain, shift):
    centered = values - jnp.mean(values, axis=-1, keepdims=True)
    variance = jnp.mean(centered * centered, axis=-1, keepdims=True)
    return centered * lax.rsqrt(variance + EPSILON) * gain + shift


def gelu_tanh(values):
    return jax.nn.gelu(values, approximate=True)


def matmul(left, right):
    return jnp.dot(left, right, preferred_element_type=jnp.float32)


def inner(left, right):
    return lax.dot_general(
        left, right, (((0,), (0,)), ((), ())), preferred_element_type=jnp.float32
    )


def outer_t(left, right):
    return lax.dot_general(
        left, right, (((1,), (1,)), ((), ())), preferred_element_type=jnp.float32
    )


def per_device(
    tokens,
    cluster_ids,
    lengths,
    top_keys,
    gain_one,
    shift_one,
    w_query,
    w_keyval,
    w_out,
    gain_two,
    shift_two,
    w_up,
    w_down,
    cotangent,
):
    tok_rows, width = tokens.shape
    heads = cluster_ids.shape[1]
    head_size = width // heads
    wide_count = lax.axis_size("wide")
    clus_dev = top_keys.shape[2]
    all_clusters = clus_dev * wide_count
    capacity = 2 * tok_rows // all_clusters
    seq_rows = tok_rows * wide_count
    seq_len = lengths[0]
    base_row = lax.axis_index("wide") * tok_rows
    position = base_row + jnp.arange(tok_rows, dtype=jnp.int32)
    validity = (position < seq_len).astype(jnp.float32)
    token_f = tokens.astype(jnp.float32)
    column_head = np.arange(2 * width) // (2 * head_size)
    column_within = np.arange(2 * width) % (2 * head_size)
    order_cols = np.where(
        column_within < head_size,
        column_head * head_size + column_within,
        width + column_head * head_size + column_within - head_size,
    )
    undo_cols = np.argsort(order_cols)
    w_pairs = w_keyval[:, order_cols]
    normed_one = normalize(token_f, gain_one, shift_one)
    normed_low = normed_one.astype(jnp.bfloat16)
    queries = matmul(normed_low, w_query).astype(jnp.bfloat16)
    keyvals = matmul(normed_low, w_pairs).astype(jnp.bfloat16)
    hits = (
        cluster_ids[:, :, None] == jnp.arange(all_clusters, dtype=jnp.int32)[None, None, :]
    ).astype(jnp.int32)
    slot_ids = jnp.sum((jnp.cumsum(hits, axis=0) - hits) * hits, axis=2)
    placing = (
        (hits > 0)[:, :, :, None]
        & (slot_ids[:, :, None, None] == jnp.arange(capacity, dtype=jnp.int32)[None, None, None, :])
    ).astype(jnp.bfloat16)

    def to_owner(rows):
        moved = jnp.einsum(
            "thcs,thd->chsd", placing, rows, preferred_element_type=jnp.float32
        ).astype(jnp.bfloat16)
        return moved.reshape(wide_count, clus_dev, heads, capacity * head_size)

    def from_owner(buffer):
        slots = buffer.reshape(all_clusters, heads, capacity, head_size)
        back = jnp.einsum("thcs,chsd->thd", placing, slots, preferred_element_type=jnp.float32)
        return back.astype(jnp.bfloat16).reshape(tok_rows, heads * head_size)

    flag_rows = jnp.broadcast_to(validity[:, None], (tok_rows, heads)).astype(jnp.bfloat16)
    flag_send = (
        jnp.einsum("thcs,th->chs", placing, flag_rows, preferred_element_type=jnp.float32)
        .astype(jnp.bfloat16)
        .reshape(wide_count, clus_dev, heads, capacity)
    )
    member_rows, member_flags = (
        lax.all_to_all(
            to_owner(queries.reshape(tok_rows, heads, head_size)),
            "wide",
            split_axis=0,
            concat_axis=0,
            tiled=True,
        ),
        lax.all_to_all(flag_send, "wide", split_axis=0, concat_axis=0, tiled=True),
    )
    members = member_rows.reshape(wide_count, clus_dev, heads, capacity, head_size)
    flags = member_flags.astype(jnp.float32)
    counts = jnp.sum(flags, axis=(0, 3))
    divisor = jnp.maximum(counts, 1.0)
    sums = jnp.einsum("scha,schad->chd", member_flags, members, preferred_element_type=jnp.float32)
    centroid = (sums / divisor[:, :, None]).astype(jnp.bfloat16)
    pairs_all = lax.all_gather(keyvals, "wide", axis=0, tiled=True).reshape(
        seq_rows, heads, 2 * head_size
    )
    keys_all = pairs_all[:, :, :head_size]
    values_all = pairs_all[:, :, head_size:]
    key_mask = jnp.arange(seq_rows, dtype=jnp.int32) < seq_len
    scores = (
        jnp.einsum("chd,shd->hcs", centroid, keys_all, preferred_element_type=jnp.float32) * 0.125
    )
    masked = jnp.where(key_mask[None, None, :], scores, NEGATIVE)
    peak = jnp.max(masked, axis=-1, keepdims=True)
    expo = jnp.exp(masked - peak)
    denom = jnp.sum(expo, axis=-1, keepdims=True)
    probs = expo / denom
    probs_low = probs.astype(jnp.bfloat16)
    full_out = jnp.einsum("hcs,shd->hcd", probs_low, values_all, preferred_element_type=jnp.float32)
    chosen = top_keys[0]
    head_range = jnp.arange(heads, dtype=jnp.int32)[:, None, None]
    top_pairs = pairs_all[chosen, head_range]
    top_keysh = top_pairs[..., :head_size]
    top_values = top_pairs[..., head_size:]
    prob_top = jnp.take_along_axis(probs, chosen, axis=2)
    top_mass = jnp.sum(prob_top, axis=-1)
    top_low = prob_top.astype(jnp.bfloat16)
    remainder = full_out - jnp.einsum(
        "hct,hctd->hcd", top_low, top_values, preferred_element_type=jnp.float32
    )
    mscores = (
        jnp.einsum("schad,hctd->schat", members, top_keysh, preferred_element_type=jnp.float32)
        * 0.125
    )
    mpeak = jnp.max(mscores, axis=-1, keepdims=True)
    mexpo = jnp.exp(mscores - mpeak)
    mprob = mexpo / jnp.sum(mexpo, axis=-1, keepdims=True)
    mprob_low = mprob.astype(jnp.bfloat16)
    mixed = jnp.einsum(
        "schat,hctd->schad", mprob_low, top_values, preferred_element_type=jnp.float32
    )
    mass_ch = top_mass.T
    rest_ch = remainder.transpose(1, 0, 2)
    out_rows = flags[..., None] * (
        mass_ch[None, :, :, None, None] * mixed + rest_ch[None, :, :, None, :]
    )
    out_send = out_rows.astype(jnp.bfloat16).reshape(
        wide_count, clus_dev, heads, capacity * head_size
    )
    attn = from_owner(lax.all_to_all(out_send, "wide", split_axis=0, concat_axis=0, tiled=True))
    resid = token_f + matmul(attn, w_out)
    normed_two = normalize(resid, gain_two, shift_two)
    normed_hi = normed_two.astype(jnp.bfloat16)
    up_pre = matmul(normed_hi, w_up)
    act = gelu_tanh(up_pre).astype(jnp.bfloat16)
    output = (resid + matmul(act, w_down)).astype(jnp.bfloat16)
    grad_down = inner(act, cotangent)
    grad_act = outer_t(cotangent, w_down)
    dummy, gelu_back = jax.vjp(gelu_tanh, up_pre)
    grad_pre = gelu_back(grad_act)[0].astype(jnp.bfloat16)
    grad_up = inner(normed_hi, grad_pre)
    grad_normed = outer_t(grad_pre, w_up)
    dummy, norm_back = jax.vjp(normalize, resid, gain_two, shift_two)
    grad_lntwo, grad_gain_two, grad_shift_two = norm_back(grad_normed)
    grad_resid = cotangent.astype(jnp.float32) + grad_lntwo
    grad_branch = grad_resid.astype(jnp.bfloat16)
    grad_out = inner(attn, grad_branch)
    grad_attn = outer_t(grad_branch, w_out).astype(jnp.bfloat16)
    grad_back = lax.all_to_all(
        to_owner(grad_attn.reshape(tok_rows, heads, head_size)),
        "wide",
        split_axis=0,
        concat_axis=0,
        tiled=True,
    )
    grad_member = (
        grad_back.reshape(wide_count, clus_dev, heads, capacity, head_size).astype(jnp.float32)
        * flags[..., None]
    )
    grad_mass = jnp.sum(grad_member * mixed, axis=(0, 3, 4))
    grad_remain = jnp.sum(grad_member, axis=(0, 3)).astype(jnp.bfloat16)
    grad_rest = grad_remain.transpose(1, 0, 2)
    grad_mix = (mass_ch[None, :, :, None, None] * grad_member).astype(jnp.bfloat16)
    grad_mprob = jnp.einsum(
        "schad,hctd->schat", grad_mix, top_values, preferred_element_type=jnp.float32
    )
    grad_topv = jnp.einsum(
        "schat,schad->hctd", mprob_low, grad_mix, preferred_element_type=jnp.float32
    )
    grad_mscore = (
        mprob * (grad_mprob - jnp.sum(mprob * grad_mprob, axis=-1, keepdims=True))
    ).astype(jnp.bfloat16)
    grad_members = (
        jnp.einsum("schat,hctd->schad", grad_mscore, top_keysh, preferred_element_type=jnp.float32)
        * 0.125
    )
    grad_topk = (
        jnp.einsum("schat,schad->hctd", grad_mscore, members, preferred_element_type=jnp.float32)
        * 0.125
    )
    grad_probs = jnp.einsum(
        "hcd,shd->hcs", grad_rest, values_all, preferred_element_type=jnp.float32
    )
    top_term = grad_mass.T[:, :, None] - jnp.einsum(
        "hcd,hctd->hct", grad_rest, top_values, preferred_element_type=jnp.float32
    )
    grad_topv = grad_topv - jnp.einsum(
        "hct,hcd->hctd", top_low, grad_rest, preferred_element_type=jnp.float32
    )
    clus_range = jnp.arange(clus_dev, dtype=jnp.int32)[None, :, None]
    grad_probs = grad_probs.at[head_range, clus_range, chosen].add(top_term)
    delta = jnp.sum(probs * grad_probs, axis=-1)
    grad_scores = (probs * (grad_probs - delta[:, :, None])).astype(jnp.bfloat16)
    grad_centroid = (
        jnp.einsum("hcs,shd->chd", grad_scores, keys_all, preferred_element_type=jnp.float32)
        * 0.125
    )
    grad_members = (
        grad_members + flags[..., None] * (grad_centroid / divisor[:, :, None])[None, :, :, None, :]
    )
    grad_send = grad_members.astype(jnp.bfloat16).reshape(
        wide_count, clus_dev, heads, capacity * head_size
    )
    grad_queries = from_owner(
        lax.all_to_all(grad_send, "wide", split_axis=0, concat_axis=0, tiled=True)
    )
    grad_keysall = (
        (
            jnp.einsum("hcs,chd->shd", grad_scores, centroid, preferred_element_type=jnp.float32)
            * 0.125
        )
        .at[chosen, head_range]
        .add(grad_topk)
    )
    grad_valsall = (
        jnp.einsum("hcs,hcd->shd", probs_low, grad_rest, preferred_element_type=jnp.float32)
        .at[chosen, head_range]
        .add(grad_topv)
    )
    combined = jnp.concatenate([grad_keysall, grad_valsall], axis=-1).reshape(seq_rows, 2 * width)
    grad_kv = lax.psum_scatter(combined, "wide", scatter_dimension=0, tiled=True)
    grad_kvlow = grad_kv.astype(jnp.bfloat16)
    grad_query = inner(normed_low, grad_queries)
    grad_keyval = inner(normed_low, grad_kvlow)[:, undo_cols]
    grad_normone = outer_t(grad_queries, w_query) + outer_t(grad_kvlow, w_pairs)
    dummy, norm_first = jax.vjp(normalize, token_f, gain_one, shift_one)
    grad_lnone, grad_gain_one, grad_shift_one = norm_first(grad_normone)
    grad_tokens = (grad_resid + grad_lnone).astype(jnp.bfloat16)
    scattered = (
        lax.psum_scatter(grad_query, "wide", scatter_dimension=0, tiled=True),
        lax.psum_scatter(grad_keyval, "wide", scatter_dimension=0, tiled=True),
        lax.psum_scatter(grad_out, "wide", scatter_dimension=0, tiled=True),
        lax.psum_scatter(grad_up, "wide", scatter_dimension=0, tiled=True),
        lax.psum_scatter(grad_down, "wide", scatter_dimension=0, tiled=True),
        lax.psum_scatter(grad_gain_one, "wide", scatter_dimension=0, tiled=True),
        lax.psum_scatter(grad_shift_one, "wide", scatter_dimension=0, tiled=True),
        lax.psum_scatter(grad_gain_two, "wide", scatter_dimension=0, tiled=True),
        lax.psum_scatter(grad_shift_two, "wide", scatter_dimension=0, tiled=True),
    )
    totals = (
        lax.psum(scattered[0].astype(jnp.bfloat16), "dp").astype(jnp.float32),
        lax.psum(scattered[1].astype(jnp.bfloat16), "dp").astype(jnp.float32),
        lax.psum(scattered[2].astype(jnp.bfloat16), "dp").astype(jnp.float32),
        lax.psum(scattered[3].astype(jnp.bfloat16), "dp").astype(jnp.float32),
        lax.psum(scattered[4].astype(jnp.bfloat16), "dp").astype(jnp.float32),
        lax.psum(scattered[5].astype(jnp.bfloat16), "dp").astype(jnp.float32),
        lax.psum(scattered[6].astype(jnp.bfloat16), "dp").astype(jnp.float32),
        lax.psum(scattered[7].astype(jnp.bfloat16), "dp").astype(jnp.float32),
        lax.psum(scattered[8].astype(jnp.bfloat16), "dp").astype(jnp.float32),
    )
    return (
        output,
        grad_tokens,
        totals[0],
        totals[1],
        totals[2],
        totals[3],
        totals[4],
        totals[5],
        totals[6],
        totals[7],
        totals[8],
    )


def solution(mesh):
    return jax.shard_map(
        per_device,
        mesh=mesh,
        in_specs=(
            P(("dp", "wide"), None),
            P(("dp", "wide"), None),
            P("dp"),
            P("dp", None, "wide", None),
            P(),
            P(),
            P(),
            P(),
            P(),
            P(),
            P(),
            P(),
            P(),
            P(("dp", "wide"), None),
        ),
        out_specs=(
            P(("dp", "wide"), None),
            P(("dp", "wide"), None),
            P("wide", None),
            P("wide", None),
            P("wide", None),
            P("wide", None),
            P("wide", None),
            P("wide"),
            P("wide"),
            P("wide"),
            P("wide"),
        ),
        check_vma=False,
    )
```

profile of v0, /device:TPU:8, one launch (start us, length us, event | category | flops | bytes accessed | tf_op | source)
XLA Modules:
  0.0 1355.2 jit_solution(1396724084362922253)
XLA Ops:
  13.9 5.6 gather_fusion
  31.1 5.3 all-to-all-start
  48.8 5.4 all-to-all-start.1
  58.2 34.2 %all-to-all-done.1 = bf16[8,16,12,256]{3,1,2,0:T(8,128)(2,1)} async-done(((bf16[8,16,12,256]{3,1,2,0:T(8,128)(2,1)}), bf16[8,16,12,256]{3,1,2,0:T(8,128)(2,1)}, u32[]{:S(2)}, u32[]{:S(2)}) %all-to-all-start.1) | async-done | bytes 786464 | tf_op jit(solution)/shard_map/all_to_all | solution.py:106
  100.9 8.7 copy.89
  115.2 60.7 %gather_fusion.3 = f32[6144]{0:T(1024)S(1)} fusion(f32[12,16,2048]{2,1,0:T(8,128)S(1)} %broadcast_divide_fusion.1, s32[6144]{0:T(1024)S(1)} %reshape.273), kind=kCustom, calls=%fused_computation.3 | custom fusion | bytes 122880 | tf_op jit(solution)/shard_map/jit(take_along_axis)/gather | solution.py:142
  176.8 8.6 copy.91
  185.5 98.0 %gather_fusion.1 = bf16[6144,128]{1,0:T(8,128)(2,1)} fusion(bf16[2048,12,128]{2,0,1:T(8,128)(2,1)} %copy.91, s32[6144]{0:T(1024)S(1)} %reshape.259), kind=kCustom, calls=%fused_computation.1 | custom fusion | bytes 3194880 | tf_op jit(solution)/shard_map/gather | solution.py:139
  291.4 126.3 %fusion.172 = (f32[8,16,12,4]{0,3,2,1:T(4,128)S(1)}, f32[8,16,12,4,32]{4,0,3,2,1:T(8,128)S(1)}) fusion(f32[16,12,32,8,4]{2,3,4,1,0:T(8,128)S(1)} %fusion.68), kind=kOutput, calls=%fused_computation.218 | output fusion | flops 786463 | bytes 1597440 | tf_op jit(solution)/shard_map/sub | solution.py:153
  417.8 4.4 fusion.23
  428.4 9.6 all-to-all-start.2
  438.0 5.5 fusion.179
  443.5 12.0 all-to-all-done.2
  461.1 4.5 fusion.101
  466.7 7.8 fusion.16
  490.5 7.1 all-to-all-start.3
  507.6 7.4 all-to-all-done.3
  527.1 6.1 fusion.24
  533.5 34.3 %scatter_fusion = f32[393216]{0:T(1024)S(1)} fusion(f32[393216]{0:T(1024)S(1)} %bitcast.243, s32[6144]{0:T(1024)S(1)} %copy-done.45, f32[6144]{0:T(1024)S(1)} %reshape.281), kind=kCustom, calls=%fused_computation.4 | custom fusion | flops 6144 | bytes 98304
  582.0 4.3 multiply_bitcast_fusion
  586.3 13.6 %copy.109 = f32[2048,12,64]{2,1,0:T(8,128)} copy(f32[2048,12,64]{0,2,1:T(8,128)} %multiply_bitcast_fusion) | data formatting | bytes 12582912
  599.9 15.2 %reshape.243 = f32[24576,64]{1,0:T(8,128)} reshape(f32[2048,12,64]{2,1,0:T(8,128)} %copy.109) | data formatting | bytes 12582912
  615.1 39.2 %scatter_fusion.1 = f32[24576,64]{1,0:T(8,128)} fusion(f32[24576,64]{1,0:T(8,128)} %reshape.243, s32[6144]{0:T(1024)S(1)} %copy-done.27, f32[6144,64]{1,0:T(8,128)} %bitcast.254), kind=kCustom, calls=%fused_computation.5 | custom fusion | flops 393216 | bytes 4743168
  654.3 14.8 %reshape.244 = f32[2048,12,64]{2,1,0:T(8,128)} reshape(f32[24576,64]{1,0:T(8,128)} %scatter_fusion.1) | data formatting | bytes 12582912 | tf_op jit(solution)/shard_map/scatter-add | solution.py:250
  669.1 13.6 %copy.112 = f32[2048,12,64]{2,1,0:T(8,128)} copy(f32[2048,12,64]{0,2,1:T(8,128)} %convolution_bitcast_fusion) | data formatting | bytes 12582912
  682.7 15.3 %reshape.247 = f32[24576,64]{1,0:T(8,128)} reshape(f32[2048,12,64]{2,1,0:T(8,128)} %copy.112) | data formatting | bytes 12582912
  698.0 5.3 bitcast_subtract_fusion
  703.3 39.2 %scatter_fusion.2 = f32[24576,64]{1,0:T(8,128)} fusion(f32[24576,64]{1,0:T(8,128)} %reshape.247, s32[6144]{0:T(1024)S(1)} %copy-done.27, f32[6144,64]{1,0:T(8,128)} %bitcast.255), kind=kCustom, calls=%fused_computation.6 | custom fusion | flops 393216 | bytes 4743168
  742.5 14.8 %reshape.248 = f32[2048,12,64]{2,1,0:T(8,128)} reshape(f32[24576,64]{1,0:T(8,128)} %scatter_fusion.2) | data formatting | bytes 12582912 | tf_op jit(solution)/shard_map/scatter-add | solution.py:255
  757.3 17.3 %pad_maximum_fusion = f32[2048,12,128]{2,1,0:T(8,128)} fusion(f32[2048,12,64]{2,1,0:T(8,128)} %reshape.248, f32[2048,12,64]{2,1,0:T(8,128)} %reshape.244), kind=kLoop, calls=%fused_computation.9 | loop fusion | flops 3145728 | bytes 25165824 | tf_op jit(solution)/shard_map/concatenate | solution.py:257
  774.5 16.8 %copy.115 = f32[2048,12,128]{0,2,1:T(8,128)} copy(f32[2048,12,128]{2,1,0:T(8,128)} %pad_maximum_fusion) | data formatting | bytes 25165824 | tf_op jit(solution)/shard_map/concatenate | solution.py:257
  800.4 37.2 %all_to_all.25 = bf16[8,16,12,256]{3,1,2,0:T(8,128)(2,1)S(1)} all-to-all(bf16[8,16,12,256]{3,1,2,0:T(8,128)(2,1)S(1)} %reshape.234), channel_id=1, replica_groups=mesh['dp'=4,'wide'=8] {'wide'}, dimensions={0} | all-to-all | bytes 1572864 | tf_op jit(solution)/shard_map/all_to_all | solution.py:242
  838.4 4.4 fusion.96
  845.0 7.8 fusion.162
  853.9 6.7 fusion.160
  861.3 71.2 %reduce-scatter.9.cloned.1.call-done = f32[256,1536]{0,1:T(8,128)} async-done(((f32[2048,1536]{0,1:T(8,128)}), f32[256,1536]{0,1:T(8,128)}) %reduce-scatter.9.cloned.1.call-update) | async-done | bytes 1572880 | tf_op jit(solution)/shard_map/reduce_scatter | solution.py:258
  932.5 4.5 fusion.138
  937.0 9.2 gather_fusion.2
  946.2 6.1 copy.140
  954.1 17.9 %reduce-scatter.13.cloned.1.call-done = f32[96,768]{1,0:T(8,128)} async-done(((f32[768,768]{1,0:T(8,128)}), f32[96,768]{1,0:T(8,128)}) %reduce-scatter.13.cloned.1.call-update) | async-done | bytes 294928 | tf_op jit(solution)/shard_map/reduce_scatter | solution.py:269
  973.6 36.1 %reduce-scatter.11.cloned.1.call-done = f32[96,768]{1,0:T(8,128)} async-done(((f32[768,768]{1,0:T(8,128)}), f32[96,768]{1,0:T(8,128)}) %reduce-scatter.11.cloned.1.call-update) | async-done | bytes 294928 | tf_op jit(solution)/shard_map/reduce_scatter | solution.py:267
  1011.4 100.0 %reduce-scatter.17.cloned.1.call-done = f32[384,768]{1,0:T(8,128)} async-done(((f32[3072,768]{1,0:T(8,128)}), f32[384,768]{1,0:T(8,128)}) %reduce-scatter.17.cloned.1.call-update) | async-done | bytes 1179664 | tf_op jit(solution)/shard_map/reduce_scatter | solution.py:271
  1113.6 97.9 %reduce-scatter.15.cloned.1.call-done = f32[96,3072]{1,0:T(8,128)} async-done(((f32[768,3072]{1,0:T(8,128)}), f32[96,3072]{1,0:T(8,128)}) %reduce-scatter.15.cloned.1.call-update) | async-done | bytes 1179664 | tf_op jit(solution)/shard_map/reduce_scatter | solution.py:270
  1213.6 53.1 %reduce-scatter.19.cloned.1.call-done = f32[96,1536]{1,0:T(8,128)} async-done(((f32[768,1536]{1,0:T(8,128)}), f32[96,1536]{1,0:T(8,128)}) %reduce-scatter.19.cloned.1.call-update) | async-done | bytes 589840
  1268.8 6.1 fusion.95
  1278.0 25.8 %all-reduce.4 = (bf16[768]{0:T(1024)(128)(2,1)S(1)}, bf16[768]{0:T(1024)(128)(2,1)S(1)}, bf16[768]{0:T(1024)(128)(2,1)S(1)}, bf16[768]{0:T(1024)(128)(2,1)S(1)}) all-reduce(f32[768]{0:T(1024)S(1)} %get-tuple-element.46, f32[768]{0:T(1024)S(1)} %get-tuple-element.49, ...), channel_id=8, replica_groups=mesh['dp'=4,'wide'=8] {'wide'}, use_global_device_ids=true, to_apply=%region_37.38.clone | all-reduce | flops 3072 | bytes 18432
  1304.1 10.0 all-reduce.5
  1318.1 21.5 %all-reduce.9.cloned.1.call-done = (bf16[96,1536]{0,1:T(8,128)(2,1)}, bf16[96,768]{1,0:T(8,128)(2,1)}, bf16[96,768]{1,0:T(8,128)(2,1)}, bf16[96,3072]{1,0:T(8,128)(2,1)}, bf16[384,768]{1,0:T(8,128)(2,1)}) async-done(((bf16[96,1536]{0,1:T(8,128)(2,1)}, bf16[96,768]{1,0:T(8,128)(2,1)}, bf16[96,768]{1,0:T(8,128)(2,1)}, bf16[96,3072]{1,0:T(8,128)(2,1)}, bf16[384,768]{1,0:T(8,128)(2,1)}), ...) | async-done | bytes 1769488 | tf_op jit(solution)/shard_map/psum | solution.py:279
  (324 shorter events, 162.0 us)
Async XLA Ops:
  7.2 458.4 %copy-start = (bf16[768,768]{1,0:T(8,128)(2,1)S(1)}, bf16[768,768]{1,0:T(8,128)(2,1)}, u32[]{:S(2)}) copy-start(bf16[768,768]{1,0:T(8,128)(2,1)} %param.26) | copy-start | bytes 3538948
  7.2 93.7 %all-gather.2.cloned.1.call-start = ((), (), s32[]{:S(2)}) async-start(), calls=%async_computation.11 | async-start | bytes 7077888 | tf_op jit(solution)/shard_map/all_gather | solution.py:121
  8.5 28.0 %copy-start.50 = (f32[256]{0:T(256)}, f32[256]{0:T(256)S(1)}, u32[]{:S(2)}) copy-start(f32[256]{0:T(256)S(1)} %broadcast_multiply_fusion.1) | copy-start | bytes 3076
  13.9 5.7 copy-start.47
  24.9 11.5 copy-start.2
  24.9 11.5 copy-start.63
  25.0 11.5 copy-start.67
  27.1 454.3 %copy-start.59 = (pred[256,12,4]{0,2,1:T(4,128)(4,1)}, pred[256,12,4]{0,2,1:T(4,128)(4,1)S(1)}, u32[]{:S(2)}) copy-start(pred[256,12,4]{0,2,1:T(4,128)(4,1)S(1)} %iota_compare_fusion.3) | copy-start | bytes 36868
  27.7 10.8 copy-start.35
  31.1 17.7 %all-to-all-start = ((bf16[8,2,384]{2,1,0:T(2,128)(2,1)}), bf16[8,2,384]{2,1,0:T(2,128)(2,1)S(1)}, u32[]{:S(2)}, u32[]{:S(2)}) async-start(bf16[8,2,384]{2,1,0:T(2,128)(2,1)} %reshape.319), calls=%async_computation | async-start | bytes 24576 | tf_op jit(solution)/shard_map/all_to_all | solution.py:113
  45.0 9.3 copy-start.44
  48.8 43.6 %all-to-all-start.1 = ((bf16[8,16,12,256]{3,1,2,0:T(8,128)(2,1)}), bf16[8,16,12,256]{3,1,2,0:T(8,128)(2,1)}, u32[]{:S(2)}, u32[]{:S(2)}) async-start(bf16[8,16,12,256]{3,1,2,0:T(8,128)(2,1)} %copy.87), calls=%async_computation.1 | async-start | bytes 1572864 | tf_op jit(solution)/shard_map/all_to_all | solution.py:106
  58.2 51.4 %copy-start.61 = (f32[16,12]{0,1:T(8,128)}, f32[16,12]{0,1:T(8,128)S(1)}, u32[]{:S(2)}) copy-start(f32[16,12]{0,1:T(8,128)S(1)} %broadcast_maximum_fusion) | copy-start | bytes 2308
  99.1 10.5 copy-start.54
  286.3 131.5 %copy-start.38 = (bf16[12,16,32,64]{3,2,1,0:T(8,128)(2,1)}, bf16[12,16,32,64]{3,2,1,0:T(8,128)(2,1)S(1)}, u32[]{:S(2)}) copy-start(bf16[12,16,32,64]{3,2,1,0:T(8,128)(2,1)S(1)} %get-tuple-element.68) | copy-start | bytes 2359300
  291.4 126.4 %copy-start.30 = (f32[8,16,12,4]{0,3,2,1:T(4,128)S(1)}, f32[8,16,12,4]{0,3,2,1:T(4,128)}, u32[]{:S(2)}) copy-start(f32[8,16,12,4]{0,3,2,1:T(4,128)} %copy.84) | copy-start | bytes 73732
  428.4 27.1 %all-to-all-start.2 = ((bf16[8,16,12,256]{3,1,2,0:T(8,128)(2,1)}), bf16[8,16,12,256]{3,1,2,0:T(8,128)(2,1)}, u32[]{:S(2)}, u32[]{:S(2)}) async-start(bf16[8,16,12,256]{3,1,2,0:T(8,128)(2,1)} %reshape.229), calls=%async_computation.2 | async-start | bytes 1572864 | tf_op jit(solution)/shard_map/all_to_all | solution.py:167
  461.1 5.5 copy-start.52
  461.1 5.5 copy-start.57
  465.6 8.9 slice-start
  466.4 10.4 copy-start.9
  466.4 10.4 copy-start.65
  466.6 10.2 copy-start.69
  466.6 7.8 slice-start.1
  477.2 7.2 copy-start.71
  486.6 11.0 copy-start.80
  486.6 11.1 copy-start.79
  486.6 12.0 copy-start.78
  486.6 12.1 copy-start.77
  489.5 10.0 copy-start.26
  490.5 24.6 %all-to-all-start.3 = ((bf16[8,16,12,256]{3,1,2,0:T(8,128)(2,1)}), bf16[8,16,12,256]{3,1,2,0:T(8,128)(2,1)S(1)}, u32[]{:S(2)}, u32[]{:S(2)}) async-start(bf16[8,16,12,256]{3,1,2,0:T(8,128)(2,1)} %copy.101), calls=%async_computation.3 | async-start | bytes 1572864 | tf_op jit(solution)/shard_map/all_to_all | solution.py:186
  497.6 435.0 %reduce-scatter.9.cloned.1.call-start = ((), (), s32[]{:S(2)}) async-start(), calls=%async_computation.12 | async-start | bytes 14155776 | tf_op jit(solution)/shard_map/reduce_scatter | solution.py:258
  527.1 6.4 copy-start.45
  599.9 15.2 %copy-start.27 = (s32[6144]{0:T(1024)S(1)}, s32[6144]{0:T(1024)}, u32[]{:S(2)}) copy-start(s32[6144]{0:T(1024)} %reshape.285) | copy-start | bytes 73732
  682.7 15.3 %copy-start.42 = (bf16[8,16,12,4,64]{4,0,3,2,1:T(8,128)(2,1)S(1)}, bf16[8,16,12,4,64]{4,0,3,2,1:T(8,128)(2,1)}, u32[]{:S(2)}) copy-start(bf16[8,16,12,4,64]{4,0,3,2,1:T(8,128)(2,1)} %get-tuple-element.67) | copy-start | bytes 2359300
  682.7 15.3 %copy-start.56 = (f32[12,16,32]{2,1,0:T(8,128)S(1)}, f32[12,16,32]{2,1,0:T(8,128)}, u32[]{:S(2)}) copy-start(f32[12,16,32]{2,1,0:T(8,128)} %get-tuple-element.70) | copy-start | bytes 73732
  791.3 180.7 %reduce-scatter.13.cloned.1.call-start = ((), (), s32[]{:S(2)}) async-start(), calls=%async_computation.14 | async-start | bytes 2654208 | tf_op jit(solution)/shard_map/reduce_scatter | solution.py:269
  794.3 215.5 %reduce-scatter.11.cloned.1.call-start = ((), (), s32[]{:S(2)}) async-start(), calls=%async_computation.13 | async-start | bytes 2654208 | tf_op jit(solution)/shard_map/reduce_scatter | solution.py:267
  800.4 37.9 %copy-start.37 = (pred[256,12,128]{2,0,1:T(8,128)(4,1)S(1)}, pred[256,12,128]{2,0,1:T(8,128)(4,1)}, u32[]{:S(2)}) copy-start(pred[256,12,128]{2,0,1:T(8,128)(4,1)} %copy-done.35) | copy-start | bytes 1179652
  844.9 266.5 %reduce-scatter.17.cloned.1.call-start = ((), (), s32[]{:S(2)}) async-start(), calls=%async_computation.16 | async-start | bytes 10616832 | tf_op jit(solution)/shard_map/reduce_scatter | solution.py:271
  852.8 358.7 %reduce-scatter.15.cloned.1.call-start = ((), (), s32[]{:S(2)}) async-start(), calls=%async_computation.15 | async-start | bytes 10616832 | tf_op jit(solution)/shard_map/reduce_scatter | solution.py:270
  860.6 406.1 %reduce-scatter.19.cloned.1.call-start = ((), (), s32[]{:S(2)}) async-start(), calls=%async_computation.17 | async-start | bytes 5308416
  952.3 387.3 %all-reduce.9.cloned.1.call-start = ((), (), s32[]{:S(2)}) async-start(), calls=%async_computation.18 | async-start | bytes 3735552 | tf_op jit(solution)/shard_map/psum | solution.py:279
  1268.7 6.1 copy-start.43
  1268.7 6.7 copy-start.21
  1276.6 39.6 %copy-start.13 = (f32[256,768]{1,0:T(8,128)S(1)}, f32[256,768]{1,0:T(8,128)}, u32[]{:S(2)}) copy-start(f32[256,768]{1,0:T(8,128)} %copy-done.12) | copy-start | bytes 2359300
  1316.2 32.0 %copy-start.1 = (bf16[768,768]{1,0:T(8,128)(2,1)S(1)}, bf16[768,768]{1,0:T(8,128)(2,1)}, u32[]{:S(2)}) copy-start(bf16[768,768]{1,0:T(8,128)(2,1)} %param.26) | copy-start | bytes 3538948
  1339.5 7.5 copy-start.46
  (48 other events, 128.2 us)
Sparse Core Ops, SparseCore 0:
  23.2 77.6 all-gather.1
  791.4 141.0 reduce-scatter.8
  934.9 37.1 reduce-scatter.12
  974.2 35.5 reduce-scatter.10
  1011.9 99.4 reduce-scatter.16
  1113.6 97.8 reduce-scatter.14
  1213.8 52.8 reduce-scatter.18
  1271.0 68.5 all-reduce.8
where the time goes:
time: 1370 us; the launch traced here: 1360 us
  waiting for transfers between devices  453 us (33%)
  local copies, waits for them, and re-layouts  370 us (27%)
  other arithmetic  300 us (22%)
  matrix products  114 us (8%)
  blocking collectives  73 us (5%)
  starting transfers between devices  28.3 us (2%)
  between operations  16.9 us (1%)
    sub x1, other arithmetic, per_device(): mexpo = jnp.exp(mscores - mpeak)  126 us
    unnamed x11, other arithmetic  113 us
    reduce_scatter x1, waiting for transfers between devices, per_device(): lax.psum_scatter(grad_down, 'wide', scatter_dimension=0, tiled=True)  100 us
    gather x1, local copies, waits for them, and re-layouts, per_device(): top_pairs = pairs_all[chosen, head_range]  98 us
    reduce_scatter x1, waiting for transfers between devices, per_device(): lax.psum_scatter(grad_up, 'wide', scatter_dimension=0, tiled=True)  97.9 us
    unnamed x187, local copies, waits for them, and re-layouts  81.8 us
    reduce_scatter x1, waiting for transfers between devices, per_device(): lax.psum_scatter(combined, 'wide', scatter_dimension=0, tiled=True)  71.2 us
    gather x5, local copies, waits for them, and re-layouts, per_device(): prob_top = jnp.take_along_axis(probs, chosen, axis=2)  60.9 us
  transfers between devices with their start and end apart: 12, of which 11 were waited for; matrix products, arithmetic and copies ran while one was open for 8% of the time, Pallas kernels for 0%

commit v1 on v0

v1 whole, which is shorter than its diff:
```python
import functools
import math

import jax
import jax.numpy as jnp
import numpy as np
from jax import lax
from jax.experimental import pallas as pl
from jax.experimental.pallas import tpu as pltpu
from jax.sharding import PartitionSpec as P

EPSILON = 1e-05
NEGATIVE = -1e30
EXCLUDED = -3e30
GELU_A = math.sqrt(2.0 / math.pi)
GELU_B = 0.044715
BF = jnp.bfloat16
F32 = jnp.float32


def nn(left, right):
    return lax.dot_general(left, right, (((1,), (0,)), ((), ())), preferred_element_type=F32)


def nt(left, right):
    return lax.dot_general(left, right, (((1,), (1,)), ((), ())), preferred_element_type=F32)


def tn(left, right):
    return lax.dot_general(left, right, (((0,), (0,)), ((), ())), preferred_element_type=F32)


def params(mib, dims):
    return pltpu.CompilerParams(
        vmem_limit_bytes=mib * 1024 * 1024, dimension_semantics=("arbitrary",) * dims
    )


def cost(flops, nbytes, trans=0):
    return pl.CostEstimate(flops=int(flops), bytes_accessed=int(nbytes), transcendentals=int(trans))


def split_low(values):
    high = values.astype(BF)
    return high, (values - high.astype(F32)).astype(BF)


def one_hot_t(ids_row, clusters):
    rows = lax.broadcasted_iota(jnp.int32, (clusters, ids_row.shape[1]), 0)
    return jnp.where(rows == ids_row, 1.0, 0.0).astype(BF)


def key_passes(total, size, score, weigh):
    if total == size:
        first = score(0)
        peak = jnp.max(first, axis=0, keepdims=True)
        expo = jnp.exp(first - peak)
        return peak, jnp.sum(expo, axis=0, keepdims=True), weigh(0, expo)

    def step(index, carry):
        peak, denom, sums = carry
        block = score(index)
        fresh = jnp.maximum(peak, jnp.max(block, axis=0, keepdims=True))
        expo = jnp.exp(block - fresh)
        fade = jnp.exp(peak - fresh)
        parts = weigh(index, expo)
        return (
            fresh,
            denom * fade + jnp.sum(expo, axis=0, keepdims=True),
            tuple(old * fade + new for old, new in zip(sums, parts)),
        )

    shapes = jax.eval_shape(lambda: (score(0), weigh(0, score(0))))
    lanes = shapes[0].shape[1]
    start = (
        jnp.full((1, lanes), NEGATIVE, F32),
        jnp.zeros((1, lanes), F32),
        tuple(jnp.zeros(item.shape, F32) for item in shapes[1]),
    )
    return lax.fori_loop(0, total // size, step, start)


def piece(ref, index, size, axis):
    if ref.shape[axis] == size:
        return ref[...]
    start = pl.multiple_of(index * size, size)
    if axis == 0:
        return ref[pl.ds(start, size), :]
    return ref[:, pl.ds(start, size)]


def bias_kernel(info, top_ref, bias_ref, *, groups, peers, rows):
    part = pl.program_id(0)
    owner = (
        lax.rem(info[0] + part // peers, groups) * peers + lax.rem(info[1] + part % peers, peers)
    )
    heads, picks, clusters = top_ref.shape
    place = owner * rows + lax.broadcasted_iota(jnp.int32, (rows, clusters), 0)
    outside = place >= info[2]
    for head in range(heads):
        top = top_ref[head]
        chosen = place == top[0:1, :]
        for pick in range(1, picks):
            chosen = chosen | (place == top[pick : pick + 1, :])
        value = jnp.where(chosen, 0.0, jnp.where(outside, EXCLUDED, NEGATIVE))
        bias_ref[head] = value.astype(BF)


def project_kernel(
    info, x_ref, gain_ref, shift_ref, wq_ref, wkv_ref, low_ref, qt_ref, kvt_ref, kv_ref, *, peers
):
    values = x_ref[...].astype(F32)
    centered = values - jnp.mean(values, axis=-1, keepdims=True)
    variance = jnp.mean(centered * centered, axis=-1, keepdims=True)
    normed = centered * lax.rsqrt(variance + EPSILON) * gain_ref[...] + shift_ref[...]
    low = normed.astype(BF)

    @pl.when(pl.program_id(1) == 0)
    def keep():
        low_ref[...] = low

    qt_ref[...] = (nt(wq_ref[0], low) * 0.125).astype(BF)
    pairs = nt(wkv_ref[0], low).astype(BF)
    kvt_ref[...] = pairs
    width = kv_ref.shape[2]
    for head in range(kv_ref.shape[0]):
        kv_ref[head] = pairs[head * width : (head + 1) * width].T


def forward_kernel(
    ids_all, ids_own, qt_all, qt_own, kvt, kv, bias, out, mix_ref, stat_ref, cen_ref, table, *, size
):
    hs = qt_own.shape[0]
    keys = kv.shape[1]
    clusters = bias.shape[2]
    kv_h, bias_h = kv.at[0], bias.at[0]

    @pl.when(pl.program_id(1) == 0)
    def centroid_stage():
        hot = one_hot_t(ids_all[0], clusters)
        ones = jnp.ones((16, keys), BF)
        sums = nt(jnp.concatenate([qt_all[...], ones], axis=0), hot)
        counts = sums[hs : hs + 1]
        centroid = (sums[:hs] / jnp.maximum(counts, 1.0)).astype(BF)
        padded = jnp.concatenate([centroid, jnp.zeros_like(centroid)], axis=0)

        def score(index):
            scores = nn(piece(kv_h, index, size, 0), padded)
            outside = piece(bias_h, index, size, 0).astype(F32) < 2.0 * NEGATIVE
            return jnp.where(outside, NEGATIVE, scores)

        def weigh(index, expo):
            top = piece(bias_h, index, size, 0).astype(F32) == 0.0
            mass = jnp.sum(jnp.where(top, expo, 0.0), axis=0, keepdims=True)
            other = jnp.where(top, 0.0, expo).astype(BF)
            return nn(piece(kvt, index, size, 1), other), mass

        peak, denom, (rest, mass) = key_passes(keys, size, score, weigh)
        rest = rest[hs:] / denom
        mass = mass / denom
        stats = jnp.concatenate(
            [
                rest,
                mass,
                peak + jnp.log(denom),
                counts,
                jnp.zeros((5, clusters), F32),
            ],
            axis=0,
        )
        stat_ref[0] = stats
        cen_ref[0] = centroid
        high, low = split_low(stats)
        table[...] = jnp.concatenate([high, low], axis=1)

    hot = one_hot_t(ids_own[0], clusters)
    queries = qt_own[...]
    side = jnp.concatenate([queries, jnp.zeros_like(queries), hot], axis=0)
    gathered = nn(table[...], jnp.concatenate([hot, hot], axis=0))

    def score(index):
        return nn(
            jnp.concatenate([piece(kv_h, index, size, 0), piece(bias_h, index, size, 0)], axis=1),
            side,
        )

    def weigh(index, expo):
        return (nn(piece(kvt, index, size, 1), expo.astype(BF)),)

    peak, denom, (mix,) = key_passes(keys, size, score, weigh)
    mix = mix[hs:] / denom
    out[0] = (gathered[hs : hs + 1] * mix + gathered[:hs]).astype(BF)
    mix_ref[0, 0] = jnp.concatenate(
        [mix, jnp.broadcast_to(peak + jnp.log(denom), (8, mix.shape[1]))], axis=0
    )


def sums_kernel(ids_own, grad, mix_ref, part_ref):
    hs = grad.shape[1]
    hot = one_hot_t(ids_own[0], part_ref.shape[2])
    rows = grad[0]
    along = jnp.sum(rows.astype(F32) * mix_ref[0, 0, :hs], axis=0, keepdims=True)
    high, low = split_low(along)
    pad = jnp.zeros((14, rows.shape[1]), BF)
    part = nt(jnp.concatenate([rows, high, low, pad], axis=0), hot)

    @pl.when(pl.program_id(1) == 0)
    def first():
        part_ref[0] = part

    @pl.when(pl.program_id(1) > 0)
    def later():
        part_ref[0] += part


def member_kernel(
    ids_own, qt_own, kvt, kv, bias, grad, mix_ref, stat_ref, dq_ref, own_ref, send_ref, total, *, size
):
    hs = qt_own.shape[0]
    keys = kv.shape[1]
    rows = grad.shape[2]
    clusters = bias.shape[2]
    block = pl.program_id(1)
    kv_h, bias_h = kv.at[0], bias.at[0]
    hot = one_hot_t(ids_own[0], clusters)
    queries = qt_own[...]
    blank = jnp.zeros_like(queries)
    side = jnp.concatenate([queries, blank, hot], axis=0)
    high, low = split_low(stat_ref[0, hs : hs + 8, :])
    mass = nn(jnp.concatenate([high, low], axis=1), jnp.concatenate([hot, hot], axis=0))[0:1]
    mix = mix_ref[0, 0, :hs]
    level = mix_ref[0, 0, hs : hs + 1]
    back = (mass * grad[0].astype(F32)).astype(BF)
    delta = jnp.sum(back.astype(F32) * mix, axis=0, keepdims=True)
    back_pad = jnp.concatenate([blank, back], axis=0)
    right = jnp.concatenate([jnp.concatenate([queries, blank], axis=0), back_pad], axis=1).T

    def step(index, dq):
        kv_c = piece(kv_h, index, size, 0)
        scores = nn(jnp.concatenate([kv_c, piece(bias_h, index, size, 0)], axis=1), side)
        weights = jnp.exp(scores - level)
        grad_w = nn(kv_c, back_pad)
        grad_s = (weights * (grad_w - delta)).astype(BF)
        both = nn(jnp.concatenate([grad_s, weights.astype(BF)], axis=1), right)
        spot = pl.ds(pl.multiple_of(index * size, size), size)

        @pl.when(block == 0)
        def first():
            total[spot, :] = both

        @pl.when(block > 0)
        def later():
            total[spot, :] += both

        return dq + nn(piece(kvt, index, size, 1), grad_s)

    dq = jnp.zeros((2 * hs, rows), F32)
    if keys == size:
        dq = step(0, dq)
    else:
        dq = lax.fori_loop(0, keys // size, step, dq)
    dq_ref[0] = dq[:hs] * 0.125

    @pl.when(block == pl.num_programs(1) - 1)
    def finish():
        blocks = pl.num_programs(1)
        groups = own_ref.shape[1] // rows
        peers = keys // own_ref.shape[1]
        for group in range(groups):
            base = group * peers * rows
            own_ref[0, group * rows : (group + 1) * rows, :] = total[base : base + rows, :]
            for peer in range(1, peers):
                spot = (peer - 1) * groups * rows + group * rows
                send_ref[0, spot : spot + rows, :] = total[
                    base + peer * rows : base + (peer + 1) * rows, :
                ].astype(BF)


def centroid_kernel(
    ids_own, kvt, kv, bias, part_ref, stat_ref, cen_ref, dqm_ref, own_ref, got_ref, dq_ref, dkv_ref, both, *, size
):
    hs = dq_ref.shape[1]
    keys = kv.shape[1]
    rows = dq_ref.shape[2]
    groups = dq_ref.shape[0]
    peers = keys // (groups * rows)
    clusters = bias.shape[2]
    kv_h, bias_h = kv.at[0], bias.at[0]
    stats = stat_ref[0]
    rest, mass = stats[:hs], stats[hs : hs + 1]
    level, counts = stats[hs + 1 : hs + 2], stats[hs + 2 : hs + 3]
    centroid = cen_ref[0]
    blank = jnp.zeros_like(centroid)
    part = part_ref[0]
    d_rest = part[:hs].astype(BF)
    d_mass = part[hs : hs + 1] + part[hs + 1 : hs + 2]
    delta = jnp.sum(d_rest.astype(F32) * rest, axis=0, keepdims=True) + d_mass * mass
    cen_pad = jnp.concatenate([centroid, blank], axis=0)
    rest_pad = jnp.concatenate([blank, d_rest], axis=0)
    right = jnp.concatenate([cen_pad, rest_pad], axis=1).T

    def step(index, total):
        kv_c = piece(kv_h, index, size, 0)
        marks = piece(bias_h, index, size, 0).astype(F32)
        scores = nn(kv_c, cen_pad)
        probs = jnp.where(marks < 2.0 * NEGATIVE, 0.0, jnp.exp(scores - level))
        top = marks == 0.0
        d_probs = jnp.where(top, d_mass, nn(kv_c, rest_pad))
        d_score = (probs * (d_probs - delta)).astype(BF)
        other = jnp.where(top, 0.0, probs).astype(BF)
        spot = pl.ds(pl.multiple_of(index * size, size), size)
        both[spot, :] = jnp.concatenate([d_score, other], axis=1)
        return total + nn(piece(kvt, index, size, 1), d_score)

    d_cen = jnp.zeros((2 * hs, clusters), F32)
    if keys == size:
        d_cen = step(0, d_cen)
    else:
        d_cen = lax.fori_loop(0, keys // size, step, d_cen)
    d_cen = d_cen[:hs] * 0.125 / jnp.maximum(counts, 1.0)
    high, low = split_low(d_cen)
    table = jnp.concatenate([high, low], axis=1)
    for group in range(groups):
        spot = group * peers * rows
        hot = one_hot_t(ids_own[0, :, spot : spot + rows], clusters)
        spread = nn(table, jnp.concatenate([hot, hot], axis=0))
        dq_ref[group] = (dqm_ref[group] + spread).astype(BF)
        own = nn(both[spot : spot + rows, :], right) + own_ref[0, group * rows : (group + 1) * rows, :]
        for peer in range(1, peers):
            at = (peer - 1) * groups * rows + group * rows
            own = own + got_ref[0, at : at + rows, :].astype(F32)
        dkv_ref[group] = own.astype(BF)


def block_kernel(info, *refs, groups, chunks):
    (attn, rest) = (refs[:groups], refs[groups:])
    x_ref, gain_ref, shift_ref, wo_ref, up_ref, down_ref, cot_ref = rest[:7]
    resid_ref, low_ref, act_ref, dup_ref, dres_ref, dbr_ref, dn_ref = rest[7:14]
    dat = rest[14 : 14 + groups]
    hat_ref, inv_ref, back = rest[14 + groups :]
    index = pl.program_id(0)

    @pl.when(index == 0)
    def before():
        resid = x_ref[...].astype(F32)
        for group in range(groups):
            owner = lax.rem(info[0] + groups - group, groups)
            resid = resid + tn(attn[group][...], wo_ref[owner])
        resid_ref[...] = resid
        centered = resid - jnp.mean(resid, axis=-1, keepdims=True)
        variance = jnp.mean(centered * centered, axis=-1, keepdims=True)
        inverse = lax.rsqrt(variance + EPSILON)
        hat = centered * inverse
        hat_ref[...] = hat
        inv_ref[...] = jnp.broadcast_to(inverse, inv_ref.shape)
        low_ref[...] = (hat * gain_ref[...] + shift_ref[...]).astype(BF)
        back[...] = jnp.zeros_like(back)

    up = nn(low_ref[...], up_ref[...])
    grad_act = nt(cot_ref[...], down_ref[...])
    square = up * up
    inner = GELU_A * (up + GELU_B * up * square)
    curve = jnp.tanh(inner)
    act_ref[...] = (0.5 * up * (1.0 + curve)).astype(BF)
    slope = 0.5 * (1.0 + curve) + 0.5 * up * (1.0 - curve * curve) * (
        GELU_A * (1.0 + 3.0 * GELU_B * square)
    )
    d_up = (grad_act * slope).astype(BF)
    dup_ref[...] = d_up
    back[...] += nt(d_up, up_ref[...])

    @pl.when(index == chunks - 1)
    def after():
        d_normed = back[...]
        hat = hat_ref[...]
        gain_part = jnp.sum(d_normed * hat, axis=0, keepdims=True)
        shift_part = jnp.sum(d_normed, axis=0, keepdims=True)
        dn_ref[...] = jnp.concatenate([gain_part, shift_part], axis=0)
        gy = d_normed * gain_ref[...]
        mean_one = jnp.mean(gy, axis=-1, keepdims=True)
        mean_two = jnp.mean(gy * hat, axis=-1, keepdims=True)
        d_resid = cot_ref[...].astype(F32) + inv_ref[:, 0:1] * (gy - mean_one - hat * mean_two)
        dres_ref[...] = d_resid
        branch = d_resid.astype(BF)
        dbr_ref[...] = branch
        for group in range(groups):
            owner = lax.rem(info[0] + groups - group, groups)
            dat[group][...] = nt(wo_ref[owner], branch).astype(BF)


def weights_kernel(resid_ref, low_ref, act_ref, dup_ref, down_ref, cot_ref, out_ref, gup_ref, gdown_ref, total, *, chunks):
    index = pl.program_id(0)

    @pl.when(index == 0)
    def first():
        total[...] = resid_ref[...]

    total[...] += nn(act_ref[...], down_ref[...])
    gup_ref[...] = tn(low_ref[...], dup_ref[...]).astype(BF)
    gdown_ref[...] = tn(act_ref[...], cot_ref[...]).astype(BF)

    @pl.when(index == chunks - 1)
    def last():
        out_ref[...] = total[...].astype(BF)


def final_kernel(info, *refs, groups):
    dqs, dkvs = refs[:groups], refs[groups : 2 * groups]
    x_ref, dres_ref, gain_ref, wq_ref, wkv_ref, out_ref = refs[2 * groups :]
    d_normed = jnp.zeros(dres_ref.shape, F32)
    for group in range(groups):
        owner = lax.rem(info[0] + groups - group, groups)
        d_normed = d_normed + tn(dqs[group][...], wq_ref[owner]) + nn(dkvs[group][...], wkv_ref[owner])
    values = x_ref[...].astype(F32)
    centered = values - jnp.mean(values, axis=-1, keepdims=True)
    variance = jnp.mean(centered * centered, axis=-1, keepdims=True)
    inverse = lax.rsqrt(variance + EPSILON)
    hat = centered * inverse
    gy = d_normed * gain_ref[...]
    mean_one = jnp.mean(gy, axis=-1, keepdims=True)
    mean_two = jnp.mean(gy * hat, axis=-1, keepdims=True)
    out_ref[...] = (dres_ref[...] + inverse * (gy - mean_one - hat * mean_two)).astype(BF)


def whole(shape):
    return pl.BlockSpec(shape, lambda *at: (0,) * len(shape))


def per_device(
    tokens,
    cluster_ids,
    lengths,
    top_keys,
    gain_one,
    shift_one,
    w_query,
    w_keyval,
    w_out,
    gain_two,
    shift_two,
    w_up,
    w_down,
    cotangent,
):
    rows, width = tokens.shape
    heads = cluster_ids.shape[1]
    hs = width // heads
    hidden = w_up.shape[1]
    wide = lax.axis_size("wide")
    n_dp = lax.axis_size("dp")
    groups = math.gcd(heads, wide)
    peers = wide // groups
    own_heads = heads // groups
    clusters = top_keys.shape[2] * wide
    picks = top_keys.shape[3]
    seq = rows * wide
    size = min(seq, 2048)
    feats = own_heads * hs
    me = lax.axis_index("wide")
    group_at, peer_at = me // peers, me % peers
    dp_at = lax.axis_index("dp")
    seq_len = lengths[0]
    info = jnp.stack([group_at, peer_at, seq_len]).astype(jnp.int32)

    def along_groups(values, hop):
        pairs = [
            (i, ((i // peers + hop) % groups) * peers + i % peers) for i in range(wide)
        ]
        return lax.ppermute(values, "wide", pairs)

    def along_peers(values, hop):
        pairs = [(i, (i // peers) * peers + (i % peers + hop) % peers) for i in range(wide)]
        return lax.ppermute(values, "wide", pairs)

    mine = [tokens] + [along_groups(tokens, -hop) for hop in range(1, groups)]
    blocks = []
    for item in mine:
        blocks.append(item)
        blocks += [along_peers(item, -hop) for hop in range(1, peers)]
    tokens_all = jnp.concatenate(blocks, axis=0)

    position = me * rows + jnp.arange(rows, dtype=jnp.int32)
    marked = jnp.where((position < seq_len)[:, None], cluster_ids, -1)
    packed = jnp.concatenate([marked.T.reshape(-1), top_keys[0].reshape(-1)])
    gathered = lax.all_gather(packed, "wide", axis=0, tiled=False)
    ids_all = gathered[:, : heads * rows].reshape(groups, peers, heads, rows)
    ids_all = lax.dynamic_slice_in_dim(ids_all, group_at * own_heads, own_heads, axis=2)
    ids_all = lax.dynamic_slice_in_dim(
        jnp.concatenate([ids_all, ids_all], axis=0), group_at, groups, axis=0
    )
    ids_all = lax.dynamic_slice_in_dim(
        jnp.concatenate([ids_all, ids_all], axis=1), peer_at, peers, axis=1
    )
    ids_all = ids_all.transpose(2, 0, 1, 3).reshape(own_heads, 1, seq)
    top_all = gathered[:, heads * rows :].reshape(wide, heads, clusters // wide, picks)
    top_all = lax.dynamic_slice_in_dim(top_all, group_at * own_heads, own_heads, axis=1)
    top_all = top_all.transpose(1, 3, 0, 2).reshape(own_heads, picks, clusters)

    bias = pl.pallas_call(
        functools.partial(bias_kernel, groups=groups, peers=peers, rows=rows),
        grid_spec=pltpu.PrefetchScalarGridSpec(
            num_scalar_prefetch=1,
            grid=(wide,),
            in_specs=[whole((own_heads, picks, clusters))],
            out_specs=pl.BlockSpec((own_heads, rows, clusters), lambda i, s: (0, i, 0)),
        ),
        out_shape=jax.ShapeDtypeStruct((own_heads, seq, clusters), BF),
        compiler_params=params(32, 1),
        cost_estimate=cost(own_heads * seq * clusters * picks * 8, own_heads * seq * clusters * 2),
        name="bias",
    )(info, top_all)

    wq_t = w_query.T.reshape(groups, feats, width)
    wkv_t = (
        w_keyval.T.reshape(2, heads, hs, width)
        .transpose(1, 0, 2, 3)
        .reshape(groups, 2 * feats, width)
    )
    gain_row, shift_row = gain_one[None, :], shift_one[None, :]

    normed_own, q_t, kv_t, kv = pl.pallas_call(
        functools.partial(project_kernel, peers=peers),
        grid_spec=pltpu.PrefetchScalarGridSpec(
            num_scalar_prefetch=1,
            grid=(groups, peers),
            in_specs=[
                pl.BlockSpec((rows, width), lambda g, p, s: (g * peers + p, 0)),
                whole((1, width)),
                whole((1, width)),
                pl.BlockSpec((1, feats, width), lambda g, p, s: (s[0], 0, 0)),
                pl.BlockSpec((1, 2 * feats, width), lambda g, p, s: (s[0], 0, 0)),
            ],
            out_specs=[
                pl.BlockSpec((rows, width), lambda g, p, s: (g, 0)),
                pl.BlockSpec((feats, rows), lambda g, p, s: (0, g * peers + p)),
                pl.BlockSpec((2 * feats, rows), lambda g, p, s: (0, g * peers + p)),
                pl.BlockSpec((own_heads, rows, 2 * hs), lambda g, p, s: (0, g * peers + p, 0)),
            ],
        ),
        out_shape=[
            jax.ShapeDtypeStruct((groups * rows, width), BF),
            jax.ShapeDtypeStruct((feats, seq), BF),
            jax.ShapeDtypeStruct((2 * feats, seq), BF),
            jax.ShapeDtypeStruct((own_heads, seq, 2 * hs), BF),
        ],
        compiler_params=params(32, 2),
        cost_estimate=cost(6 * seq * width * feats, seq * width * 4),
        name="project",
    )(info, tokens_all, gain_row, shift_row, wq_t, wkv_t)

    ids_full = pl.BlockSpec((1, 1, seq), lambda h, r: (h, 0, 0))
    ids_block = pl.BlockSpec((1, 1, rows), lambda h, r: (h, 0, r * peers))
    q_full = pl.BlockSpec((hs, seq), lambda h, r: (h, 0))
    q_block = pl.BlockSpec((hs, rows), lambda h, r: (h, r * peers))
    kvt_full = pl.BlockSpec((2 * hs, seq), lambda h, r: (h, 0))
    kv_full = pl.BlockSpec((1, seq, 2 * hs), lambda h, r: (h, 0, 0))
    bias_full = pl.BlockSpec((1, seq, clusters), lambda h, r: (h, 0, 0))
    head_out = pl.BlockSpec((1, hs, rows), lambda h, r: (r, h, 0))
    mix_spec = pl.BlockSpec((1, 1, hs + 8, rows), lambda h, r: (h, r, 0, 0))
    stat_spec = pl.BlockSpec((1, hs + 8, clusters), lambda h, r: (h, 0, 0))
    cen_spec = pl.BlockSpec((1, hs, clusters), lambda h, r: (h, 0, 0))
    part_spec = pl.BlockSpec((1, hs + 16, clusters), lambda h, r: (h, 0, 0))
    own_rows = groups * rows
    pair_flops = own_heads * own_rows * seq * 256

    attn_t, mixed, stats, centroid = pl.pallas_call(
        functools.partial(forward_kernel, size=size),
        grid=(own_heads, groups),
        in_specs=[ids_full, ids_block, q_full, q_block, kvt_full, kv_full, bias_full],
        out_specs=[head_out, mix_spec, stat_spec, cen_spec],
        out_shape=[
            jax.ShapeDtypeStruct((groups, feats, rows), BF),
            jax.ShapeDtypeStruct((own_heads, groups, hs + 8, rows), F32),
            jax.ShapeDtypeStruct((own_heads, hs + 8, clusters), F32),
            jax.ShapeDtypeStruct((own_heads, hs, clusters), BF),
        ],
        scratch_shapes=[pltpu.VMEM((hs + 8, 2 * clusters), BF)],
        compiler_params=params(56, 2),
        cost_estimate=cost(6 * pair_flops, 8e6, own_heads * own_rows * seq),
        name="attend",
    )(ids_all, ids_all, q_t, q_t, kv_t, kv, bias)

    arrived = [attn_t[0]] + [along_groups(attn_t[hop], hop) for hop in range(1, groups)]

    chunks = 6 if hidden % 768 == 0 else 1
    part = hidden // chunks
    w_out_g = w_out.reshape(groups, feats, width)
    gain_row2, shift_row2 = gain_two[None, :], shift_two[None, :]
    square = whole((rows, width))
    results = pl.pallas_call(
        functools.partial(block_kernel, groups=groups, chunks=chunks),
        grid_spec=pltpu.PrefetchScalarGridSpec(
            num_scalar_prefetch=1,
            grid=(chunks,),
            in_specs=[whole((feats, rows))] * groups
            + [
                square,
                whole((1, width)),
                whole((1, width)),
                whole((groups, feats, width)),
                pl.BlockSpec((width, part), lambda i, s: (0, i)),
                pl.BlockSpec((part, width), lambda i, s: (i, 0)),
                square,
            ],
            out_specs=[
                square,
                square,
                pl.BlockSpec((rows, part), lambda i, s: (0, i)),
                pl.BlockSpec((rows, part), lambda i, s: (0, i)),
                square,
                square,
                whole((2, width)),
            ]
            + [whole((feats, rows))] * groups,
            scratch_shapes=[
                pltpu.VMEM((rows, width), F32),
                pltpu.VMEM((rows, 128), F32),
                pltpu.VMEM((rows, width), F32),
            ],
        ),
        out_shape=[
            jax.ShapeDtypeStruct((rows, width), F32),
            jax.ShapeDtypeStruct((rows, width), BF),
            jax.ShapeDtypeStruct((rows, hidden), BF),
            jax.ShapeDtypeStruct((rows, hidden), BF),
            jax.ShapeDtypeStruct((rows, width), F32),
            jax.ShapeDtypeStruct((rows, width), BF),
            jax.ShapeDtypeStruct((2, width), F32),
        ]
        + [jax.ShapeDtypeStruct((feats, rows), BF)] * groups,
        compiler_params=params(48, 1),
        cost_estimate=cost(6 * rows * width * hidden, 4 * width * hidden, rows * hidden),
        name="feed",
    )(info, *arrived, tokens, gain_row2, shift_row2, w_out_g, w_up, w_down, cotangent)
    resid, normed_two, act, d_up, d_resid, d_branch, norm_two = results[:7]
    d_attn = results[7:]
    grads = [d_attn[0]] + [along_groups(d_attn[hop], -hop) for hop in range(1, groups)]
    grad_own = jnp.stack(grads)

    output, grad_up, grad_down = pl.pallas_call(
        functools.partial(weights_kernel, chunks=chunks),
        grid=(chunks,),
        in_specs=[
            square,
            square,
            pl.BlockSpec((rows, part), lambda i: (0, i)),
            pl.BlockSpec((rows, part), lambda i: (0, i)),
            pl.BlockSpec((part, width), lambda i: (i, 0)),
            square,
        ],
        out_specs=[
            square,
            pl.BlockSpec((width, part), lambda i: (0, i)),
            pl.BlockSpec((part, width), lambda i: (i, 0)),
        ],
        out_shape=[
            jax.ShapeDtypeStruct((rows, width), BF),
            jax.ShapeDtypeStruct((width, hidden), BF),
            jax.ShapeDtypeStruct((hidden, width), BF),
        ],
        scratch_shapes=[pltpu.VMEM((rows, width), F32)],
        compiler_params=params(48, 1),
        cost_estimate=cost(6 * rows * width * hidden, 6 * width * hidden),
        name="weights",
    )(resid, normed_two, act, d_up, w_down, cotangent)
    grad_out = jnp.concatenate([nn(item, d_branch).astype(BF)[None] for item in arrived], axis=0)
    grad_out = jnp.stack(
        [
            lax.dynamic_index_in_dim(grad_out, (group_at + groups - g) % groups, keepdims=False)
            for g in range(groups)
        ]
    ).reshape(width, width)

    def reduce_rows(partial, masks, axis):
        blocks = partial.reshape(groups, peers, partial.shape[0] // wide, partial.shape[1])

        def of_peer(hop):
            return lax.dynamic_index_in_dim(
                blocks, (peer_at + hop) % peers, axis=1, keepdims=False
            )

        total = of_peer(0).astype(F32)
        for hop in range(1, peers):
            total = total + along_peers(of_peer(hop), hop).astype(F32)
        total = total.astype(BF)
        for mask in masks:
            bit = (dp_at // mask) % 2
            half = total.shape[axis] // 2
            keep = lax.dynamic_slice_in_dim(total, bit * half, half, axis=axis)
            send = lax.dynamic_slice_in_dim(total, (1 - bit) * half, half, axis=axis)
            got = lax.ppermute(send, "dp", [(i, i ^ mask) for i in range(n_dp)])
            total = (keep.astype(F32) + got.astype(F32)).astype(BF)

        def of_group(hop):
            return lax.dynamic_index_in_dim(total, (group_at + hop) % groups, keepdims=False)

        done = of_group(0).astype(F32)
        for hop in range(1, groups):
            done = done + along_groups(of_group(hop), hop).astype(F32)
        return spread_dp(done.astype(BF), masks, axis - 1)

    def spread_dp(done, masks, axis):
        for mask in reversed(masks):
            bit = (dp_at // mask) % 2
            got = lax.ppermute(done, "dp", [(i, i ^ mask) for i in range(n_dp)])
            done = jnp.where(
                bit == 0,
                jnp.concatenate([done, got], axis=axis),
                jnp.concatenate([got, done], axis=axis),
            )
        return done

    masks = [1 << k for k in range(n_dp.bit_length() - 1)]
    total_up = reduce_rows(grad_up, masks, 2).astype(F32)
    total_down = reduce_rows(grad_down, masks[::-1], 2).astype(F32)
    total_out = reduce_rows(grad_out, masks, 2).astype(F32)
    norms = lax.psum(norm_two, ("dp", "wide"))

    part = pl.pallas_call(
        sums_kernel,
        grid=(own_heads, groups),
        in_specs=[ids_block, head_out, mix_spec],
        out_specs=part_spec,
        out_shape=jax.ShapeDtypeStruct((own_heads, hs + 16, clusters), F32),
        compiler_params=params(32, 2),
        cost_estimate=cost(own_heads * own_rows * clusters * 160, 2e6),
        name="sums",
    )(ids_all, grad_own, mixed)
    part_total = part
    for hop in range(1, peers):
        part_total = part_total + along_peers(part, hop)

    dq_member, dkv_own, dkv_send = pl.pallas_call(
        functools.partial(member_kernel, size=size),
        grid=(own_heads, groups),
        in_specs=[
            ids_block,
            q_block,
            kvt_full,
            kv_full,
            bias_full,
            head_out,
            mix_spec,
            stat_spec,
        ],
        out_specs=[
            head_out,
            pl.BlockSpec((1, own_rows, 2 * hs), lambda h, r: (h, 0, 0)),
            pl.BlockSpec((1, max(peers - 1, 1) * own_rows, 2 * hs), lambda h, r: (h, 0, 0)),
        ],
        out_shape=[
            jax.ShapeDtypeStruct((groups, feats, rows), F32),
            jax.ShapeDtypeStruct((own_heads, own_rows, 2 * hs), F32),
            jax.ShapeDtypeStruct((own_heads, max(peers - 1, 1) * own_rows, 2 * hs), BF),
        ],
        scratch_shapes=[pltpu.VMEM((seq, 2 * hs), F32)],
        compiler_params=params(56, 2),
        cost_estimate=cost(12 * pair_flops, 10e6, own_heads * own_rows * seq),
        name="member",
    )(ids_all, q_t, kv_t, kv, bias, grad_own, mixed, stats)
    dkv_got = [
        along_peers(dkv_send[:, (hop - 1) * own_rows : hop * own_rows], hop)
        for hop in range(1, peers)
    ]
    dkv_got = jnp.concatenate(dkv_got, axis=1) if dkv_got else jnp.zeros_like(dkv_send)

    one = [
        pl.BlockSpec(spec.block_shape, functools.partial(lambda h, f: f(h, 0), f=spec.index_map))
        for spec in (ids_full, kvt_full, kv_full, bias_full, part_spec, stat_spec, cen_spec)
    ]
    all_groups = pl.BlockSpec((groups, hs, rows), lambda h: (0, h, 0))
    d_q, d_kv = pl.pallas_call(
        functools.partial(centroid_kernel, size=size),
        grid=(own_heads,),
        in_specs=one
        + [
            all_groups,
            pl.BlockSpec((1, own_rows, 2 * hs), lambda h: (h, 0, 0)),
            pl.BlockSpec((1, max(peers - 1, 1) * own_rows, 2 * hs), lambda h: (h, 0, 0)),
        ],
        out_specs=[
            all_groups,
            pl.BlockSpec((groups, rows, 2 * hs), lambda h: (0, 0, h)),
        ],
        out_shape=[
            jax.ShapeDtypeStruct((groups, feats, rows), BF),
            jax.ShapeDtypeStruct((groups, rows, 2 * feats), BF),
        ],
        scratch_shapes=[pltpu.VMEM((seq, 2 * clusters), BF)],
        compiler_params=params(56, 1),
        cost_estimate=cost(own_heads * clusters * seq * 1024, 8e6, own_heads * clusters * seq),
        name="centroid",
    )(ids_all, kv_t, kv, bias, part_total, stats, centroid, dq_member, dkv_own, dkv_got)

    dqs = [d_q[0]] + [along_groups(d_q[hop], hop) for hop in range(1, groups)]
    dkvs = [d_kv[0]] + [along_groups(d_kv[hop], hop) for hop in range(1, groups)]

    grad_tokens = pl.pallas_call(
        functools.partial(final_kernel, groups=groups),
        grid_spec=pltpu.PrefetchScalarGridSpec(
            num_scalar_prefetch=1,
            grid=(1,),
            in_specs=[whole((feats, rows))] * groups
            + [whole((rows, 2 * feats))] * groups
            + [
                square,
                square,
                whole((1, width)),
                whole((groups, feats, width)),
                whole((groups, 2 * feats, width)),
            ],
            out_specs=square,
        ),
        out_shape=jax.ShapeDtypeStruct((rows, width), BF),
        compiler_params=params(48, 1),
        cost_estimate=cost(6 * rows * width * width, 6 * width * width),
        name="final",
    )(info, *dqs, *dkvs, tokens, d_resid, gain_row, wq_t, wkv_t)

    flat_kv = d_kv.reshape(own_rows, 2 * feats)
    grad_q = jnp.einsum("grk,gfr->kf", normed_own.reshape(groups, rows, width), d_q, preferred_element_type=F32)
    grad_kv = tn(normed_own, flat_kv)
    grad_kv = grad_kv.reshape(width, own_heads, 2, hs).transpose(0, 2, 1, 3).reshape(width, 2 * feats)
    sum_q = jnp.sum(d_q.astype(F32), axis=(0, 2))
    sum_kv = (
        jnp.sum(flat_kv.astype(F32), axis=0)
        .reshape(own_heads, 2, hs)
        .transpose(1, 0, 2)
        .reshape(2 * feats)
    )
    block_rows = width // wide
    extra = jnp.broadcast_to(jnp.concatenate([sum_q, sum_kv])[None, None, :], (wide, 8, 3 * feats))
    grad_in = jnp.concatenate([grad_q, grad_kv], axis=1).reshape(wide, block_rows, 3 * feats)
    grad_in = jnp.concatenate([grad_in, extra], axis=1).astype(BF)
    in_rows = grad_in.shape[1]

    def of_peer(hop):
        return lax.dynamic_index_in_dim(
            grad_in.reshape(groups, peers, in_rows, 3 * feats),
            (peer_at + hop) % peers,
            axis=1,
            keepdims=False,
        )

    total = of_peer(0).astype(F32)
    for hop in range(1, peers):
        total = total + along_peers(of_peer(hop), hop).astype(F32)
    total = total.astype(BF)
    for mask in masks:
        got = lax.ppermute(total, "dp", [(i, i ^ mask) for i in range(n_dp)])
        total = (total.astype(F32) + got.astype(F32)).astype(BF)
    pieces = [lax.dynamic_index_in_dim(total, group_at, keepdims=False)]
    for hop in range(1, groups):
        item = lax.dynamic_index_in_dim(total, (group_at + hop) % groups, keepdims=False)
        pieces.append(along_groups(item, hop))
    pieces = jnp.stack(pieces)
    pieces = jnp.stack(
        [
            lax.dynamic_index_in_dim(pieces, (group_at + groups - g) % groups, keepdims=False)
            for g in range(groups)
        ]
    ).astype(F32)
    q_part = pieces[:, :, :feats].transpose(1, 0, 2).reshape(in_rows, width)
    kv_part = (
        pieces[:, :, feats:]
        .reshape(groups, in_rows, 2, feats)
        .transpose(1, 2, 0, 3)
        .reshape(in_rows, 2 * width)
    )
    total_query, total_keyval = q_part[:block_rows], kv_part[:block_rows]
    at = me * block_rows
    wq_rows = lax.dynamic_slice_in_dim(w_query, at, block_rows).astype(F32)
    wkv_rows = lax.dynamic_slice_in_dim(w_keyval, at, block_rows).astype(F32)
    shift_grad = jnp.sum(wq_rows * q_part[block_rows], axis=1) + jnp.sum(
        wkv_rows * kv_part[block_rows], axis=1
    )
    along = jnp.sum(wq_rows * total_query, axis=1) + jnp.sum(wkv_rows * total_keyval, axis=1)
    gain_own = lax.dynamic_slice_in_dim(gain_one, at, block_rows)
    shift_own = lax.dynamic_slice_in_dim(shift_one, at, block_rows)
    gain_grad = (along - shift_own * shift_grad) / gain_own
    norm_two_own = lax.dynamic_slice_in_dim(norms, at, block_rows, axis=1)
    return (
        output,
        grad_tokens,
        total_query,
        total_keyval,
        total_out,
        total_up,
        total_down,
        gain_grad,
        shift_grad,
        norm_two_own[0],
        norm_two_own[1],
    )


def solution(mesh):
    return jax.shard_map(
        per_device,
        mesh=mesh,
        in_specs=(
            P(("dp", "wide"), None),
            P(("dp", "wide"), None),
            P("dp"),
            P("dp", None, "wide", None),
            P(),
            P(),
            P(),
            P(),
            P(),
            P(),
            P(),
            P(),
            P(),
            P(("dp", "wide"), None),
        ),
        out_specs=(
            P(("dp", "wide"), None),
            P(("dp", "wide"), None),
            P("wide", None),
            P("wide", None),
            P("wide", None),
            P("wide", None),
            P("wide", None),
            P("wide"),
            P("wide"),
            P("wide"),
            P("wide"),
        ),
        check_vma=False,
    )
```

time: 1370 us -> 426 us (0.31)
  waiting for transfers between devices: 453 us -> 71.5 us
  local copies, waits for them, and re-layouts: 370 us -> 75.4 us
  other arithmetic: 300 us -> 25.6 us
  matrix products: 114 us -> 5.84 us
  Pallas kernels: 0 us -> 105 us
  starting transfers between devices: 28.3 us -> 60.6 us
  between operations: 16.9 us -> 2.25 us
    reduce_scatter x5 -> x0, waiting for transfers between devices: 323 us -> none  [the longest x1 100 us: per_device(): lax.psum_scatter(grad_down, 'wide', scatter_dimension=0, tiled=True)]
    gather x8 -> x0, local copies, waits for them, and re-layouts: 174 us -> none  [the longest x1 98 us: per_device(): top_pairs = pairs_all[chosen, head_range]]
    sub x2 -> x0, other arithmetic: 126 us -> none  [the longest x1 126 us: per_device(): mexpo = jnp.exp(mscores - mpeak)]
    unnamed x11 -> x1, other arithmetic: 113 us -> 0.01 us
    pallas_call x0 -> x9, Pallas kernels: none -> 105 us  [the longest x1 27.6 us: per_device(): pl.pallas_call(functools.partial(member_kernel, size=size), grid=(own_hea...]
    dot_general x33 -> x6, matrix products: 110 us -> 5.84 us  [the longest x1 2.39 us: tn(): lax.dot_general(left, right, (((0,), (0,)), ((), ())), preferred_element_...]
    ppermute x0 -> x51, waiting for transfers between devices: none -> 71.5 us  [the longest x27 39 us: along_groups(): return lax.ppermute(values, 'wide', pairs)]
    ppermute x0 -> x51, starting transfers between devices: none -> 60.6 us  [the longest x27 41 us: along_groups(): return lax.ppermute(values, 'wide', pairs)]
  transfers between devices with their start and end apart: 12 -> 51, of which waited for: 11 -> 21; matrix products, arithmetic and copies ran while one was open for 8% -> 21% of each run, Pallas kernels for 0% -> 15%
where the time goes in v1:
time: 426 us; the launch traced here: 423 us
  Pallas kernels  105 us (25%)
  blocking collectives  76.5 us (18%)
  local copies, waits for them, and re-layouts  75.4 us (18%)
  waiting for transfers between devices  71.5 us (17%)
  starting transfers between devices  60.6 us (14%)
  other arithmetic  25.6 us (6%)
  matrix products  5.84 us (1%)
    ppermute x27, starting transfers between devices, along_groups(): return lax.ppermute(values, 'wide', pairs)  41 us
    psum x1, blocking collectives, per_device(): norms = lax.psum(norm_two, ('dp', 'wide'))  39.8 us
    ppermute x27, waiting for transfers between devices, along_groups(): return lax.ppermute(values, 'wide', pairs)  39 us
    all_gather x1, blocking collectives, per_device(): gathered = lax.all_gather(packed, 'wide', axis=0, tiled=False)  36.7 us
    unnamed x98, local copies, waits for them, and re-layouts  29.7 us
    pallas_call x1, Pallas kernels, per_device(): pl.pallas_call(functools.partial(member_kernel, size=size), grid=(own_hea...  27.6 us
    pallas_call x1, Pallas kernels, per_device(): pl.pallas_call(functools.partial(forward_kernel, size=size), grid=(own_he...  22.8 us
    ppermute x6, waiting for transfers between devices, spread_dp(): got = lax.ppermute(done, 'dp', [(i, i ^ mask) for i in range(n_dp)])  13.6 us
  transfers between devices with their start and end apart: 51, of which 21 were waited for; matrix products, arithmetic and copies ran while one was open for 21% of the time, Pallas kernels for 15%

profile of v1, /device:TPU:8, one launch (start us, length us, event | category | flops | bytes accessed | tf_op | source)
XLA Modules:
  0.0 422.6 jit_solution(9831216607767347563)
XLA Ops:
  0.8 2.9 collective-permute-start.3
  3.7 2.5 collective-permute-start.5
  8.6 36.7 %all-gather = s32[73728]{0:T(1024)S(1)} all-gather(s32[9216]{0:T(1024)S(1)} %pad_add_fusion), channel_id=2, replica_groups=mesh['dp'=4,'wide'=8] {'wide'}, dimensions={0}, use_global_device_ids=true | all-gather | bytes 331776 | tf_op jit(solution)/shard_map/all_gather | solution.py:485
  47.5 2.4 copy.117
  54.6 13.3 %bias.1 = bf16[3,2048,128]{2,1,0:T(8,128)(2,1)S(1)} custom-call(s32[3]{0:T(128)S(1)} %pad_add_fusion.1.info, s32[3,32,128]{2,1,0:T(8,128)S(1)} %copy-done.13), custom_call_target="tpu_custom_call" | custom-call | flops 201326592 | bytes 1572864 | tf_op jit(solution)/shard_map/bias/pallas_call | solution.py:499
  73.8 8.1 %project.1 = (bf16[1024,768]{1,0:T(8,128)(2,1)S(1)}, bf16[192,2048]{1,0:T(8,128)(2,1)S(1)}, bf16[384,2048]{1,0:T(8,128)(2,1)S(1)}, bf16[3,2048,128]{2,1,0:T(8,128)(2,1)S(1)}) custom-call(s32[3]{0:T(128)S(1)} %pad_add_fusion.1.info, bf16[2048,768]{1,0:T(8,128)(2,1)S(1)} %constant_dynamic-update-slice_fusion.x_ref, ...), custom_call_target="tpu_custom_call" | custom-call | flops 1811939328 | bytes 6291456 | tf_op jit(solution)/shard_map/project/pallas_call | solution.py:521
  86.3 22.8 %attend.1 = (bf16[4,192,256]{2,1,0:T(8,128)(2,1)}, f32[3,4,72,256]{3,2,1,0:T(8,128)}, f32[3,72,128]{2,1,0:T(8,128)}, bf16[3,64,128]{2,1,0:T(8,128)(2,1)}) custom-call(s32[3,1,2048]{2,1,0:T(1,128)} %reshape.117.ids_all.ids_own, s32[3,1,2048]{2,1,0:T(1,128)} %reshape.117.ids_all.ids_own, bf16[192,2048]{1,0:T(8,128)(2,1)} %copy-done.20, ...), custom_call_target="tpu_custom_call" | custom-call | flops 9663676416 | bytes 8000000 | tf_op jit(solution)/shard_map/attend/pallas_call | solution.py:566
  110.2 2.9 collective-permute-start.7
  113.1 3.2 collective-permute-start.8
  117.5 2.6 copy.121
  120.1 2.2 collective-permute-done.8.refs_2_
  122.3 2.4 collective-permute-done.9.refs_3_
  128.3 12.1 %feed.1 = (f32[256,768]{1,0:T(8,128)S(1)}, bf16[256,768]{1,0:T(8,128)(2,1)S(1)}, bf16[256,3072]{1,0:T(8,128)(2,1)}, bf16[256,3072]{1,0:T(8,128)(2,1)}, f32[256,7...) custom-call(s32[3]{0:T(128)S(1)} %pad_add_fusion.1.info, ...), custom_call_target="tpu_custom_call" | custom-call | flops 3623878656 | bytes 9437184 | tf_op jit(solution)/shard_map/feed/pallas_call | solution.py:590
  142.9 2.9 collective-permute-start.12
  148.6 9.3 %weights.1 = (bf16[256,768]{1,0:T(8,128)(2,1)}, bf16[768,3072]{1,0:T(8,128)(2,1)}, bf16[3072,768]{1,0:T(8,128)(2,1)}) custom-call(f32[256,768]{1,0:T(8,128)S(1)} %get-tuple-element.42.resid_ref, bf16[256,768]{1,0:T(8,128)(2,1)S(1)} %get-tuple-element.43.low_ref, bf16[256,3072]{1,0:T(8,128)(2,1)S(1)} %copy-done.21, bf16[256,3072]{1,0:T(8,128)(2,1)S(1)} %copy-done.22, ...), custom_call_target="tpu_custom_call" | custom-call | flops 3623878656 | bytes 14155776 | tf_op jit(solution)/shard_map/weights/pallas_call | solution.py:640
  157.9 4.9 %constant_dynamic-slice_fusion.4 = (bf16[4,1,384,768]{3,2,1,0:T(8,128)(2,1)}, bf16[4,1,384,768]{3,2,1,0:T(8,128)(2,1)}) fusion(bf16[4,2,384,768]{3,2,1,0:T(8,128)(2,1)} %bitcast.186, s32[]{:T(128)S(6)} %select_n.298, s32[]{:T(128)S(6)} %select_n.300), kind=kLoop, calls=%fused_computation.121 | loop fusion | bytes 9437192 | tf_op jit(solution)/shard_map/jit(dynamic_index_in_dim)/dynamic_slice | solution.py:678
  162.8 4.3 %copy.134 = bf16[4,1,384,768]{2,3,0,1:T(8,128)(2,1)} copy(bf16[4,1,384,768]{3,2,1,0:T(8,128)(2,1)} %get-tuple-element.94) | data formatting | bytes 4718592 | tf_op jit(solution)/shard_map/jit(dynamic_index_in_dim)/dynamic_slice | solution.py:678
  172.6 27.6 %member.1 = (f32[4,192,256]{2,1,0:T(8,128)}, f32[3,1024,128]{2,1,0:T(8,128)}, bf16[3,1024,128]{2,1,0:T(8,128)(2,1)}) custom-call(s32[3,1,2048]{2,1,0:T(1,128)} %reshape.117.ids_all.ids_own, bf16[192,2048]{1,0:T(8,128)(2,1)} %copy-done.20, bf16[384,2048]{1,0:T(8,128)(2,1)} %copy-done.3, bf16[3,2048,128]{2,1,0:T(8,128)(2,1)} %copy-done.4, ...), custom_call_target="tpu_custom_call" | custom-call | flops 19327352832 | bytes 10000000 | tf_op jit(solution)/shard_map/member/pallas_call | solution.py:733
  200.3 2.0 sums.1
  202.8 3.2 dynamic-slice_bitcast_fusion
  206.1 39.8 %psum.7 = f32[2,768]{1,0:T(2,128)S(1)} all-reduce(f32[2,768]{1,0:T(2,128)S(1)} %get-tuple-element.64), channel_id=1, replica_groups=mesh['dp'=4,'wide'=8] {'dp','wide'}, use_global_device_ids=true, to_apply=%region_6.7 | all-reduce | flops 1536 | bytes 12288 | tf_op jit(solution)/shard_map/psum | solution.py:717
  249.7 2.3 collective-permute-start.28
  251.9 6.8 %centroid.1 = (bf16[4,192,256]{2,1,0:T(8,128)(2,1)}, bf16[4,256,384]{2,1,0:T(8,128)(2,1)}) custom-call(s32[3,1,2048]{2,1,0:T(1,128)} %reshape.117.ids_all.ids_own, bf16[384,2048]{1,0:T(8,128)(2,1)} %copy-done.3, bf16[3,2048,128]{2,1,0:T(8,128)(2,1)} %copy-done.4, bf16[3,2048,128]{2,1,0:T(8,128)(2,1)} %copy-done, f32[3,80,128]{2,1,0:T(8,128)} %add.309.part_ref, ...), custom_call_target="tpu_custom_call" | custom-call | flops 805306368 | bytes 8000000 | tf_op jit(solution)/shard_map/centroid/pallas_call | solution.py:772
  261.7 2.3 copy.124
  264.0 2.4 fusion.7
  267.2 3.9 concatenate.71
  271.2 3.0 copy.126
  278.3 4.3 %copy.142 = bf16[4,1,384,768]{2,3,0,1:T(8,128)(2,1)} copy(bf16[4,1,384,768]{3,2,1,0:T(8,128)(2,1)} %get-tuple-element.93) | data formatting | bytes 4718592
  287.9 3.4 collective-permute-done.29
  294.7 5.4 %collective-permute-done.22 = bf16[4,104,576]{2,1,0:T(8,128)(2,1)S(1)} collective-permute-done((bf16[4,104,576]{2,1,0:T(8,128)(2,1)S(1)}, bf16[4,104,576]{2,1,0:T(8,128)(2,1)S(1)}, u32[]{:S(2)}, u32[]{:S(2)}) %collective-permute-start.22) | collective-permute-done | bytes 479264 | tf_op jit(solution)/shard_map/ppermute | solution.py:850
  307.2 7.7 %collective-permute-done.33 = bf16[96,192]{1,0:T(8,128)(2,1)S(1)} collective-permute-done((bf16[96,192]{1,0:T(8,128)(2,1)S(1)}, bf16[96,192]{1,0:T(8,128)(2,1)S(1)}, u32[]{:S(2)}, u32[]{:S(2)}) %collective-permute-start.33) | collective-permute-done | bytes 36896 | tf_op jit(solution)/shard_map/ppermute | solution.py:705
  318.3 2.0 collective-permute-start.16
  320.3 2.4 fusion
  326.9 3.7 collective-permute-done.15.refs_1_
  330.5 3.1 collective-permute-done.16.refs_2_
  334.7 5.0 %collective-permute-done.17.refs_3_ = bf16[192,256]{1,0:T(8,128)(2,1)S(1)} collective-permute-done((bf16[192,256]{1,0:T(8,128)(2,1)S(1)}, bf16[192,256]{1,0:T(8,128)(2,1)S(1)}, u32[]{:S(2)}, u32[]{:S(2)}) %collective-permute-start.17) | collective-permute-done | bytes 98336 | tf_op jit(solution)/shard_map/ppermute | solution.py:469
  341.9 2.1 collective-permute-start.24
  347.7 3.0 final.1
  353.0 2.1 collective-permute-done.26
  360.1 2.1 add_convert_fusion
  364.4 3.5 collective-permute-done.36
  372.7 6.6 %collective-permute-done.45 = bf16[4,384,192]{1,2,0:T(8,128)(2,1)} collective-permute-done((bf16[4,384,192]{1,2,0:T(8,128)(2,1)}, bf16[4,384,192]{1,2,0:T(8,128)(2,1)}, u32[]{:S(2)}, u32[]{:S(2)}) %collective-permute-start.45) | collective-permute-done | bytes 589856 | tf_op jit(solution)/shard_map/ppermute | solution.py:691
  382.7 2.7 collective-permute-start.47
  387.6 2.3 collective-permute-start.39
  391.6 11.0 %collective-permute-done.47 = bf16[384,192]{0,1:T(8,128)(2,1)S(1)} collective-permute-done((bf16[384,192]{0,1:T(8,128)(2,1)S(1)}, bf16[384,192]{0,1:T(8,128)(2,1)S(1)}, u32[]{:S(2)}, u32[]{:S(2)}) %collective-permute-start.47) | collective-permute-done | bytes 147488 | tf_op jit(solution)/shard_map/ppermute | solution.py:469
  406.0 2.3 collective-permute-done.40
  411.7 2.8 collective-permute-done.41
  416.9 3.0 collective-permute-done.50
  (273 shorter events, 111.3 us)
Async XLA Ops:
  0.6 45.2 %collective-permute-start.1 = (bf16[256,768]{1,0:T(8,128)(2,1)}, bf16[256,768]{1,0:T(8,128)(2,1)}, u32[]{:S(2)}, u32[]{:S(2)}) collective-permute-start(bf16[256,768]{1,0:T(8,128)(2,1)} %refs_8_.3), channel_id=1, source_target_pairs={{0,6},{1,7},{2,0},{3,1},{4,2},{5,3},{6,4},{7,5},{8,14},{9,15},{10,... | collective-permute-start | bytes 1179656 | tf_op jit(solution)/shard_map/ppermute | solution.py:469
  0.7 67.8 %collective-permute-start = (bf16[256,768]{1,0:T(8,128)(2,1)}, bf16[256,768]{1,0:T(8,128)(2,1)}, u32[]{:S(2)}, u32[]{:S(2)}) collective-permute-start(bf16[256,768]{1,0:T(8,128)(2,1)} %refs_8_.3), channel_id=1, source_target_pairs={{0,1},{1,0},{2,3},{3,2},{4,5},{5,4},{6,7},{7,6},{8,9},{9,8},{10,11... | collective-permute-start | bytes 1179656 | tf_op jit(solution)/shard_map/ppermute | solution.py:473
  0.8 67.1 %collective-permute-start.3 = (bf16[256,768]{1,0:T(8,128)(2,1)}, bf16[256,768]{1,0:T(8,128)(2,1)}, u32[]{:S(2)}, u32[]{:S(2)}) collective-permute-start(bf16[256,768]{1,0:T(8,128)(2,1)} %refs_8_.3), channel_id=1, source_target_pairs={{0,4},{1,5},{2,6},{3,7},{4,0},{5,1},{6,2},{7,3},{8,12},{9,13},{10,... | collective-permute-start | bytes 1179656 | tf_op jit(solution)/shard_map/ppermute | solution.py:469
  3.7 64.6 %collective-permute-start.5 = (bf16[256,768]{1,0:T(8,128)(2,1)}, bf16[256,768]{1,0:T(8,128)(2,1)}, u32[]{:S(2)}, u32[]{:S(2)}) collective-permute-start(bf16[256,768]{1,0:T(8,128)(2,1)} %refs_8_.3), channel_id=1, source_target_pairs={{0,2},{1,3},{2,4},{3,5},{4,6},{5,7},{6,0},{7,1},{8,10},{9,11},{10,... | collective-permute-start | bytes 1179656 | tf_op jit(solution)/shard_map/ppermute | solution.py:469
  45.8 24.8 %collective-permute-start.2 = (bf16[256,768]{1,0:T(8,128)(2,1)}, bf16[256,768]{1,0:T(8,128)(2,1)}, u32[]{:S(2)}, u32[]{:S(2)}) collective-permute-start(bf16[256,768]{1,0:T(8,128)(2,1)} %collective-permute-done.1), channel_id=1, source_target_pairs={{0,1},{1,0},{2,3},{3,2},{4,5},{5,4},{6,7},{7,6},{8,9},{9,8},{10,11... | collective-permute-start | bytes 1179656 | tf_op jit(solution)/shard_map/ppermute | solution.py:473
  110.2 9.9 %collective-permute-start.7 = (bf16[192,256]{1,0:T(8,128)(2,1)S(1)}, bf16[192,256]{1,0:T(8,128)(2,1)S(1)}, u32[]{:S(2)}, u32[]{:S(2)}) collective-permute-start(bf16[192,256]{1,0:T(8,128)(2,1)S(1)} %get-tuple-element.123), channel_id=1, source_target_pairs={{0,2},{1,3},{2,4},{3,5},{4,6},{5,7},{6,0},{7,1},{8,10},{9,11},{10,... | collective-permute-start | bytes 294920 | tf_op jit(solution)/shard_map/ppermute | solution.py:469
  113.1 9.2 %collective-permute-start.8 = (bf16[192,256]{1,0:T(8,128)(2,1)S(1)}, bf16[192,256]{1,0:T(8,128)(2,1)S(1)}, u32[]{:S(2)}, u32[]{:S(2)}) collective-permute-start(bf16[192,256]{1,0:T(8,128)(2,1)S(1)} %get-tuple-element.122), channel_id=1, source_target_pairs={{0,4},{1,5},{2,6},{3,7},{4,0},{5,1},{6,2},{7,3},{8,12},{9,13},{10,... | collective-permute-start | bytes 294920 | tf_op jit(solution)/shard_map/ppermute | solution.py:469
  116.3 8.3 %collective-permute-start.9 = (bf16[192,256]{1,0:T(8,128)(2,1)S(1)}, bf16[192,256]{1,0:T(8,128)(2,1)S(1)}, u32[]{:S(2)}, u32[]{:S(2)}) collective-permute-start(bf16[192,256]{1,0:T(8,128)(2,1)S(1)} %get-tuple-element.121), channel_id=1, source_target_pairs={{0,6},{1,7},{2,0},{3,1},{4,2},{5,3},{6,4},{7,5},{8,14},{9,15},{10,... | collective-permute-start | bytes 294920 | tf_op jit(solution)/shard_map/ppermute | solution.py:469
  141.9 29.0 %collective-permute-start.10 = (bf16[192,256]{1,0:T(8,128)(2,1)}, bf16[192,256]{1,0:T(8,128)(2,1)S(1)}, u32[]{:S(2)}, u32[]{:S(2)}) collective-permute-start(bf16[192,256]{1,0:T(8,128)(2,1)} %get-tuple-element.48), channel_id=1, source_target_pairs={{0,6},{1,7},{2,0},{3,1},{4,2},{5,3},{6,4},{7,5},{8,14},{9,15},{10,... | collective-permute-start | bytes 294920 | tf_op jit(solution)/shard_map/ppermute | solution.py:469
  142.0 28.8 %collective-permute-start.11 = (bf16[192,256]{1,0:T(8,128)(2,1)}, bf16[192,256]{1,0:T(8,128)(2,1)}, u32[]{:S(2)}, u32[]{:S(2)}) collective-permute-start(bf16[192,256]{1,0:T(8,128)(2,1)} %get-tuple-element.49), channel_id=1, source_target_pairs={{0,4},{1,5},{2,6},{3,7},{4,0},{5,1},{6,2},{7,3},{8,12},{9,13},{10,... | collective-permute-start | bytes 294920 | tf_op jit(solution)/shard_map/ppermute | solution.py:469
  142.9 28.0 %collective-permute-start.12 = (bf16[192,256]{1,0:T(8,128)(2,1)}, bf16[192,256]{1,0:T(8,128)(2,1)}, u32[]{:S(2)}, u32[]{:S(2)}) collective-permute-start(bf16[192,256]{1,0:T(8,128)(2,1)} %get-tuple-element.50), channel_id=1, source_target_pairs={{0,2},{1,3},{2,4},{3,5},{4,6},{5,7},{6,0},{7,1},{8,10},{9,11},{10,... | collective-permute-start | bytes 294920 | tf_op jit(solution)/shard_map/ppermute | solution.py:469
  167.0 151.2 %collective-permute-start.43 = (bf16[4,384,768]{1,2,0:T(8,128)(2,1)}, bf16[4,384,768]{1,2,0:T(8,128)(2,1)}, u32[]{:S(2)}, u32[]{:S(2)}) collective-permute-start(bf16[4,384,768]{1,2,0:T(8,128)(2,1)} %bitcast.189), channel_id=1, source_target_pairs={{0,1},{1,0},{2,3},{3,2},{4,5},{5,4},{6,7},{7,6},{8,9},{9,8},{10,11... | collective-permute-start | bytes 7077896 | tf_op jit(solution)/shard_map/ppermute | solution.py:473
  170.3 76.4 %collective-permute-start.27 = (bf16[4,96,768]{2,1,0:T(8,128)(2,1)}, bf16[4,96,768]{2,1,0:T(8,128)(2,1)}, u32[]{:S(2)}, u32[]{:S(2)}) collective-permute-start(bf16[4,96,768]{2,1,0:T(8,128)(2,1)} %dynamic-slice_bitcast_fusion.1), channel_id=1, source_target_pairs={{0,1},{1,0},{2,3},{3,2},{4,5},{5,4},{6,7},{7,6},{8,9},{9,8},{10,11... | collective-permute-start | bytes 1769480 | tf_op jit(solution)/shard_map/ppermute | solution.py:473
  200.2 51.7 %collective-permute-start.14 = (bf16[3,1024,128]{2,1,0:T(8,128)(2,1)}, bf16[3,1024,128]{2,1,0:T(8,128)(2,1)}, u32[]{:S(2)}, u32[]{:S(2)}) collective-permute-start(bf16[3,1024,128]{2,1,0:T(8,128)(2,1)} %get-tuple-element.56), channel_id=1, source_target_pairs={{0,1},{1,0},{2,3},{3,2},{4,5},{5,4},{6,7},{7,6},{8,9},{9,8},{10,11... | collective-permute-start | bytes 2359304 | tf_op jit(solution)/shard_map/ppermute | solution.py:473
  202.3 43.7 %collective-permute-start.13 = (f32[3,80,128]{2,1,0:T(8,128)S(1)}, f32[3,80,128]{2,1,0:T(8,128)S(1)}, u32[]{:S(2)}, u32[]{:S(2)}) collective-permute-start(f32[3,80,128]{2,1,0:T(8,128)S(1)} %sums.1), channel_id=1, source_target_pairs={{0,1},{1,0},{2,3},{3,2},{4,5},{5,4},{6,7},{7,6},{8,9},{9,8},{10,11... | collective-permute-start | bytes 368648 | tf_op jit(solution)/shard_map/ppermute | solution.py:473
  249.7 33.4 %collective-permute-start.28 = (bf16[4,96,384]{2,1,0:T(8,128)(2,1)}, bf16[4,96,384]{2,1,0:T(8,128)(2,1)S(1)}, u32[]{:S(2)}, u32[]{:S(2)}) collective-permute-start(bf16[4,96,384]{2,1,0:T(8,128)(2,1)} %constant_dynamic-slice_fusion.8), channel_id=1, source_target_pairs={{0,8},{8,0},{16,24},{24,16},{1,9},{9,1},{17,25},{25,17},{2,10},{10... | collective-permute-start | bytes 884744 | tf_op jit(solution)/shard_map/ppermute | solution.py:691
  277.7 7.2 %collective-permute-start.21 = (bf16[4,104,576]{2,1,0:T(8,128)(2,1)}, bf16[4,104,576]{2,1,0:T(8,128)(2,1)}, u32[]{:S(2)}, u32[]{:S(2)}) collective-permute-start(bf16[4,104,576]{2,1,0:T(8,128)(2,1)} %dynamic-slice_bitcast_fusion.2), channel_id=1, source_target_pairs={{0,1},{1,0},{2,3},{3,2},{4,5},{5,4},{6,7},{7,6},{8,9},{9,8},{10,11... | collective-permute-start | bytes 1437704 | tf_op jit(solution)/shard_map/ppermute | solution.py:473
  282.6 41.3 %collective-permute-start.35 = (bf16[4,96,3072]{2,1,0:T(8,128)(2,1)}, bf16[4,96,3072]{2,1,0:T(8,128)(2,1)S(1)}, u32[]{:S(2)}, u32[]{:S(2)}) collective-permute-start(bf16[4,96,3072]{2,1,0:T(8,128)(2,1)} %dynamic-slice_bitcast_fusion), channel_id=1, source_target_pairs={{0,1},{1,0},{2,3},{3,2},{4,5},{5,4},{6,7},{7,6},{8,9},{9,8},{10,11... | collective-permute-start | bytes 7077896 | tf_op jit(solution)/shard_map/ppermute | solution.py:473
  284.3 7.0 %collective-permute-start.29 = (bf16[4,96,192]{2,1,0:T(8,128)(2,1)S(1)}, bf16[4,96,192]{2,1,0:T(8,128)(2,1)S(1)}, u32[]{:S(2)}, u32[]{:S(2)}) collective-permute-start(bf16[4,96,192]{2,1,0:T(8,128)(2,1)S(1)} %constant_dynamic-slice_fusion.7), channel_id=1, source_target_pairs={{0,16},{8,24},{16,0},{24,8},{1,17},{9,25},{17,1},{25,9},{2,18},{10... | collective-permute-start | bytes 442376 | tf_op jit(solution)/shard_map/ppermute | solution.py:691
  286.2 13.9 %collective-permute-start.22 = (bf16[4,104,576]{2,1,0:T(8,128)(2,1)S(1)}, bf16[4,104,576]{2,1,0:T(8,128)(2,1)S(1)}, u32[]{:S(2)}, u32[]{:S(2)}) collective-permute-start(bf16[4,104,576]{2,1,0:T(8,128)(2,1)S(1)} %fusion.15), channel_id=1, source_target_pairs={{0,8},{8,0},{16,24},{24,16},{1,9},{9,1},{17,25},{25,17},{2,10},{10... | collective-permute-start | bytes 1437704 | tf_op jit(solution)/shard_map/ppermute | solution.py:850
  291.4 9.8 %collective-permute-start.30 = (bf16[96,192]{1,0:T(8,128)(2,1)S(1)}, bf16[96,192]{1,0:T(8,128)(2,1)S(1)}, u32[]{:S(2)}, u32[]{:S(2)}) collective-permute-start(bf16[96,192]{1,0:T(8,128)(2,1)S(1)} %get-tuple-element.125), channel_id=1, source_target_pairs={{0,2},{1,3},{2,4},{3,5},{4,6},{5,7},{6,0},{7,1},{8,10},{9,11},{10,... | collective-permute-start | bytes 110600 | tf_op jit(solution)/shard_map/ppermute | solution.py:469
  292.8 9.9 %collective-permute-start.31 = (bf16[96,192]{1,0:T(8,128)(2,1)S(1)}, bf16[96,192]{1,0:T(8,128)(2,1)S(1)}, u32[]{:S(2)}, u32[]{:S(2)}) collective-permute-start(bf16[96,192]{1,0:T(8,128)(2,1)S(1)} %get-tuple-element.127), channel_id=1, source_target_pairs={{0,4},{1,5},{2,6},{3,7},{4,0},{5,1},{6,2},{7,3},{8,12},{9,13},{10,... | collective-permute-start | bytes 110600 | tf_op jit(solution)/shard_map/ppermute | solution.py:469
  301.2 15.8 %collective-permute-start.23 = (bf16[4,104,576]{2,1,0:T(8,128)(2,1)S(1)}, bf16[4,104,576]{2,1,0:T(8,128)(2,1)S(1)}, u32[]{:S(2)}, u32[]{:S(2)}) collective-permute-start(bf16[4,104,576]{2,1,0:T(8,128)(2,1)S(1)} %add_convert_fusion.5), channel_id=1, source_target_pairs={{0,16},{8,24},{16,0},{24,8},{1,17},{9,25},{17,1},{25,9},{2,18},{10... | collective-permute-start | bytes 1437704 | tf_op jit(solution)/shard_map/ppermute | solution.py:850
  304.2 10.7 %collective-permute-start.33 = (bf16[96,192]{1,0:T(8,128)(2,1)S(1)}, bf16[96,192]{1,0:T(8,128)(2,1)S(1)}, u32[]{:S(2)}, u32[]{:S(2)}) collective-permute-start(bf16[96,192]{1,0:T(8,128)(2,1)S(1)} %fusion.33), channel_id=1, source_target_pairs={{0,16},{8,24},{16,0},{24,8},{1,17},{9,25},{17,1},{25,9},{2,18},{10... | collective-permute-start | bytes 110600 | tf_op jit(solution)/shard_map/ppermute | solution.py:705
  305.8 35.5 %collective-permute-start.18 = (bf16[256,384]{1,0:T(8,128)(2,1)S(1)}, bf16[256,384]{1,0:T(8,128)(2,1)S(1)}, u32[]{:S(2)}, u32[]{:S(2)}) collective-permute-start(bf16[256,384]{1,0:T(8,128)(2,1)S(1)} %get-tuple-element.101), channel_id=1, source_target_pairs={{0,2},{1,3},{2,4},{3,5},{4,6},{5,7},{6,0},{7,1},{8,10},{9,11},{10,... | collective-permute-start | bytes 589832 | tf_op jit(solution)/shard_map/ppermute | solution.py:469
  314.9 26.9 %collective-permute-start.19 = (bf16[256,384]{1,0:T(8,128)(2,1)S(1)}, bf16[256,384]{1,0:T(8,128)(2,1)S(1)}, u32[]{:S(2)}, u32[]{:S(2)}) collective-permute-start(bf16[256,384]{1,0:T(8,128)(2,1)S(1)} %get-tuple-element.100), channel_id=1, source_target_pairs={{0,4},{1,5},{2,6},{3,7},{4,0},{5,1},{6,2},{7,3},{8,12},{9,13},{10,... | collective-permute-start | bytes 589832 | tf_op jit(solution)/shard_map/ppermute | solution.py:469
  317.0 13.6 %collective-permute-start.15 = (bf16[192,256]{1,0:T(8,128)(2,1)S(1)}, bf16[192,256]{1,0:T(8,128)(2,1)S(1)}, u32[]{:S(2)}, u32[]{:S(2)}) collective-permute-start(bf16[192,256]{1,0:T(8,128)(2,1)S(1)} %get-tuple-element.119), channel_id=1, source_target_pairs={{0,2},{1,3},{2,4},{3,5},{4,6},{5,7},{6,0},{7,1},{8,10},{9,11},{10,... | collective-permute-start | bytes 294920 | tf_op jit(solution)/shard_map/ppermute | solution.py:469
  318.3 15.4 %collective-permute-start.16 = (bf16[192,256]{1,0:T(8,128)(2,1)S(1)}, bf16[192,256]{1,0:T(8,128)(2,1)S(1)}, u32[]{:S(2)}, u32[]{:S(2)}) collective-permute-start(bf16[192,256]{1,0:T(8,128)(2,1)S(1)} %get-tuple-element.118), channel_id=1, source_target_pairs={{0,4},{1,5},{2,6},{3,7},{4,0},{5,1},{6,2},{7,3},{8,12},{9,13},{10,... | collective-permute-start | bytes 294920 | tf_op jit(solution)/shard_map/ppermute | solution.py:469
  324.5 35.7 %collective-permute-start.44 = (bf16[4,384,384]{1,2,0:T(8,128)(2,1)}, bf16[4,384,384]{1,2,0:T(8,128)(2,1)}, u32[]{:S(2)}, u32[]{:S(2)}) collective-permute-start(bf16[4,384,384]{1,2,0:T(8,128)(2,1)} %constant_dynamic-slice_fusion.2), channel_id=1, source_target_pairs={{0,16},{8,24},{16,0},{24,8},{1,17},{9,25},{17,1},{25,9},{2,18},{10... | collective-permute-start | bytes 3538952 | tf_op jit(solution)/shard_map/ppermute | solution.py:691
  330.5 13.4 %collective-permute-start.20 = (bf16[256,384]{1,0:T(8,128)(2,1)S(1)}, bf16[256,384]{1,0:T(8,128)(2,1)S(1)}, u32[]{:S(2)}, u32[]{:S(2)}) collective-permute-start(bf16[256,384]{1,0:T(8,128)(2,1)S(1)} %get-tuple-element.99), channel_id=1, source_target_pairs={{0,6},{1,7},{2,0},{3,1},{4,2},{5,3},{6,4},{7,5},{8,14},{9,15},{10,... | collective-permute-start | bytes 589832 | tf_op jit(solution)/shard_map/ppermute | solution.py:469
  333.7 6.1 %collective-permute-start.17 = (bf16[192,256]{1,0:T(8,128)(2,1)S(1)}, bf16[192,256]{1,0:T(8,128)(2,1)S(1)}, u32[]{:S(2)}, u32[]{:S(2)}) collective-permute-start(bf16[192,256]{1,0:T(8,128)(2,1)S(1)} %get-tuple-element.117), channel_id=1, source_target_pairs={{0,6},{1,7},{2,0},{3,1},{4,2},{5,3},{6,4},{7,5},{8,14},{9,15},{10,... | collective-permute-start | bytes 294920 | tf_op jit(solution)/shard_map/ppermute | solution.py:469
  339.8 5.9 %collective-permute-start.34 = (bf16[96,384]{1,0:T(8,128)(2,1)S(1)}, bf16[96,384]{1,0:T(8,128)(2,1)S(1)}, u32[]{:S(2)}, u32[]{:S(2)}) collective-permute-start(bf16[96,384]{1,0:T(8,128)(2,1)S(1)} %maximum_select_fusion.5), channel_id=1, source_target_pairs={{0,8},{8,0},{16,24},{24,16},{1,9},{9,1},{17,25},{25,17},{2,10},{10... | collective-permute-start | bytes 221192 | tf_op jit(solution)/shard_map/ppermute | solution.py:705
  341.2 26.7 %collective-permute-start.36 = (bf16[4,96,1536]{2,1,0:T(8,128)(2,1)}, bf16[4,96,1536]{2,1,0:T(8,128)(2,1)}, u32[]{:S(2)}, u32[]{:S(2)}) collective-permute-start(bf16[4,96,1536]{2,1,0:T(8,128)(2,1)} %constant_dynamic-slice_fusion.6), channel_id=1, source_target_pairs={{0,8},{8,0},{16,24},{24,16},{1,9},{9,1},{17,25},{25,17},{2,10},{10... | collective-permute-start | bytes 3538952 | tf_op jit(solution)/shard_map/ppermute | solution.py:691
  341.9 9.5 %collective-permute-start.24 = (bf16[104,576]{1,0:T(8,128)(2,1)S(1)}, bf16[104,576]{1,0:T(8,128)(2,1)S(1)}, u32[]{:S(2)}, u32[]{:S(2)}) collective-permute-start(bf16[104,576]{1,0:T(8,128)(2,1)S(1)} %get-tuple-element.116), channel_id=1, source_target_pairs={{0,2},{1,3},{2,4},{3,5},{4,6},{5,7},{6,0},{7,1},{8,10},{9,11},{10,... | collective-permute-start | bytes 359432 | tf_op jit(solution)/shard_map/ppermute | solution.py:469
  344.0 9.0 %collective-permute-start.25 = (bf16[104,576]{1,0:T(8,128)(2,1)S(1)}, bf16[104,576]{1,0:T(8,128)(2,1)S(1)}, u32[]{:S(2)}, u32[]{:S(2)}) collective-permute-start(bf16[104,576]{1,0:T(8,128)(2,1)S(1)} %get-tuple-element.115), channel_id=1, source_target_pairs={{0,4},{1,5},{2,6},{3,7},{4,0},{5,1},{6,2},{7,3},{8,12},{9,13},{10,... | collective-permute-start | bytes 359432 | tf_op jit(solution)/shard_map/ppermute | solution.py:469
  345.7 9.4 %collective-permute-start.26 = (bf16[104,576]{1,0:T(8,128)(2,1)S(1)}, bf16[104,576]{1,0:T(8,128)(2,1)S(1)}, u32[]{:S(2)}, u32[]{:S(2)}) collective-permute-start(bf16[104,576]{1,0:T(8,128)(2,1)S(1)} %get-tuple-element.114), channel_id=1, source_target_pairs={{0,6},{1,7},{2,0},{3,1},{4,2},{5,3},{6,4},{7,5},{8,14},{9,15},{10,... | collective-permute-start | bytes 359432 | tf_op jit(solution)/shard_map/ppermute | solution.py:469
  363.2 16.1 %collective-permute-start.45 = (bf16[4,384,192]{1,2,0:T(8,128)(2,1)}, bf16[4,384,192]{1,2,0:T(8,128)(2,1)}, u32[]{:S(2)}, u32[]{:S(2)}) collective-permute-start(bf16[4,384,192]{1,2,0:T(8,128)(2,1)} %constant_dynamic-slice_fusion.1), channel_id=1, source_target_pairs={{0,8},{8,0},{16,24},{24,16},{1,9},{9,1},{17,25},{25,17},{2,10},{10... | collective-permute-start | bytes 1769480 | tf_op jit(solution)/shard_map/ppermute | solution.py:691
  369.6 17.7 %collective-permute-start.37 = (bf16[4,96,768]{2,1,0:T(8,128)(2,1)S(1)}, bf16[4,96,768]{2,1,0:T(8,128)(2,1)S(1)}, u32[]{:S(2)}, u32[]{:S(2)}) collective-permute-start(bf16[4,96,768]{2,1,0:T(8,128)(2,1)S(1)} %constant_dynamic-slice_fusion.5), channel_id=1, source_target_pairs={{0,16},{8,24},{16,0},{24,8},{1,17},{9,25},{17,1},{25,9},{2,18},{10... | collective-permute-start | bytes 1769480 | tf_op jit(solution)/shard_map/ppermute | solution.py:691
  380.7 10.9 %collective-permute-start.46 = (bf16[384,192]{0,1:T(8,128)(2,1)S(1)}, bf16[384,192]{0,1:T(8,128)(2,1)S(1)}, u32[]{:S(2)}, u32[]{:S(2)}) collective-permute-start(bf16[384,192]{0,1:T(8,128)(2,1)S(1)} %get-tuple-element.103), channel_id=1, source_target_pairs={{0,2},{1,3},{2,4},{3,5},{4,6},{5,7},{6,0},{7,1},{8,10},{9,11},{10,... | collective-permute-start | bytes 442376 | tf_op jit(solution)/shard_map/ppermute | solution.py:469
  382.7 19.9 %collective-permute-start.47 = (bf16[384,192]{0,1:T(8,128)(2,1)S(1)}, bf16[384,192]{0,1:T(8,128)(2,1)S(1)}, u32[]{:S(2)}, u32[]{:S(2)}) collective-permute-start(bf16[384,192]{0,1:T(8,128)(2,1)S(1)} %get-tuple-element.105), channel_id=1, source_target_pairs={{0,4},{1,5},{2,6},{3,7},{4,0},{5,1},{6,2},{7,3},{8,12},{9,13},{10,... | collective-permute-start | bytes 442376 | tf_op jit(solution)/shard_map/ppermute | solution.py:469
  385.3 17.7 %collective-permute-start.48 = (bf16[384,192]{0,1:T(8,128)(2,1)S(1)}, bf16[384,192]{0,1:T(8,128)(2,1)S(1)}, u32[]{:S(2)}, u32[]{:S(2)}) collective-permute-start(bf16[384,192]{0,1:T(8,128)(2,1)S(1)} %get-tuple-element.104), channel_id=1, source_target_pairs={{0,6},{1,7},{2,0},{3,1},{4,2},{5,3},{6,4},{7,5},{8,14},{9,15},{10,... | collective-permute-start | bytes 442376 | tf_op jit(solution)/shard_map/ppermute | solution.py:469
  387.5 17.0 %collective-permute-start.38 = (bf16[96,768]{1,0:T(8,128)(2,1)S(1)}, bf16[96,768]{1,0:T(8,128)(2,1)S(1)}, u32[]{:S(2)}, u32[]{:S(2)}) collective-permute-start(bf16[96,768]{1,0:T(8,128)(2,1)S(1)} %get-tuple-element.106), channel_id=1, source_target_pairs={{0,2},{1,3},{2,4},{3,5},{4,6},{5,7},{6,0},{7,1},{8,10},{9,11},{10,... | collective-permute-start | bytes 442376 | tf_op jit(solution)/shard_map/ppermute | solution.py:469
  387.6 18.4 %collective-permute-start.39 = (bf16[96,768]{1,0:T(8,128)(2,1)S(1)}, bf16[96,768]{1,0:T(8,128)(2,1)S(1)}, u32[]{:S(2)}, u32[]{:S(2)}) collective-permute-start(bf16[96,768]{1,0:T(8,128)(2,1)S(1)} %get-tuple-element.108), channel_id=1, source_target_pairs={{0,4},{1,5},{2,6},{3,7},{4,0},{5,1},{6,2},{7,3},{8,12},{9,13},{10,... | collective-permute-start | bytes 442376 | tf_op jit(solution)/shard_map/ppermute | solution.py:469
  391.6 16.7 %collective-permute-start.40 = (bf16[96,768]{1,0:T(8,128)(2,1)S(1)}, bf16[96,768]{1,0:T(8,128)(2,1)S(1)}, u32[]{:S(2)}, u32[]{:S(2)}) collective-permute-start(bf16[96,768]{1,0:T(8,128)(2,1)S(1)} %get-tuple-element.107), channel_id=1, source_target_pairs={{0,6},{1,7},{2,0},{3,1},{4,2},{5,3},{6,4},{7,5},{8,14},{9,15},{10,... | collective-permute-start | bytes 442376 | tf_op jit(solution)/shard_map/ppermute | solution.py:469
  403.1 8.2 %collective-permute-start.49 = (bf16[384,192]{0,1:T(8,128)(2,1)S(1)}, bf16[384,192]{0,1:T(8,128)(2,1)S(1)}, u32[]{:S(2)}, u32[]{:S(2)}) collective-permute-start(bf16[384,192]{0,1:T(8,128)(2,1)S(1)} %fusion.26), channel_id=1, source_target_pairs={{0,8},{8,0},{16,24},{24,16},{1,9},{9,1},{17,25},{25,17},{2,10},{10... | collective-permute-start | bytes 442376 | tf_op jit(solution)/shard_map/ppermute | solution.py:705
  408.4 6.1 %collective-permute-start.41 = (bf16[96,768]{1,0:T(8,128)(2,1)S(1)}, bf16[96,768]{1,0:T(8,128)(2,1)S(1)}, u32[]{:S(2)}, u32[]{:S(2)}) collective-permute-start(bf16[96,768]{1,0:T(8,128)(2,1)S(1)} %fusion.29), channel_id=1, source_target_pairs={{0,16},{8,24},{16,0},{24,8},{1,17},{9,25},{17,1},{25,9},{2,18},{10... | collective-permute-start | bytes 442376 | tf_op jit(solution)/shard_map/ppermute | solution.py:705
  411.4 8.6 %collective-permute-start.50 = (bf16[384,384]{0,1:T(8,128)(2,1)S(1)}, bf16[384,384]{0,1:T(8,128)(2,1)S(1)}, u32[]{:S(2)}, u32[]{:S(2)}) collective-permute-start(bf16[384,384]{0,1:T(8,128)(2,1)S(1)} %maximum_select_fusion.3), channel_id=1, source_target_pairs={{0,16},{8,24},{16,0},{24,8},{1,17},{9,25},{17,1},{25,9},{2,18},{10... | collective-permute-start | bytes 884744 | tf_op jit(solution)/shard_map/ppermute | solution.py:705
  414.6 6.8 %collective-permute-start.42 = (bf16[96,1536]{1,0:T(8,128)(2,1)S(1)}, bf16[96,1536]{1,0:T(8,128)(2,1)S(1)}, u32[]{:S(2)}, u32[]{:S(2)}) collective-permute-start(bf16[96,1536]{1,0:T(8,128)(2,1)S(1)} %maximum_select_fusion.2), channel_id=1, source_target_pairs={{0,8},{8,0},{16,24},{24,16},{1,9},{9,1},{17,25},{25,17},{2,10},{10... | collective-permute-start | bytes 884744 | tf_op jit(solution)/shard_map/ppermute | solution.py:705
  (47 other events, 380.8 us)

commit v2 on v1

v2 whole, which is shorter than its diff:
```python
import functools
import math

import jax
import jax.numpy as jnp
import numpy as np
from jax import lax
from jax.experimental import pallas as pl
from jax.experimental.pallas import tpu as pltpu
from jax.sharding import PartitionSpec as P

EPSILON = 1e-05
NEGATIVE = -1e30
EXCLUDED = -3e30
GELU_A = math.sqrt(2.0 / math.pi)
GELU_B = 0.044715
BF = jnp.bfloat16
F32 = jnp.float32


def nn(left, right):
    return lax.dot_general(left, right, (((1,), (0,)), ((), ())), preferred_element_type=F32)


def nt(left, right):
    return lax.dot_general(left, right, (((1,), (1,)), ((), ())), preferred_element_type=F32)


def tn(left, right):
    return lax.dot_general(left, right, (((0,), (0,)), ((), ())), preferred_element_type=F32)


def params(mib, dims):
    return pltpu.CompilerParams(
        vmem_limit_bytes=mib * 1024 * 1024, dimension_semantics=("arbitrary",) * dims
    )


def cost(flops, nbytes, trans=0):
    return pl.CostEstimate(flops=int(flops), bytes_accessed=int(nbytes), transcendentals=int(trans))


def split_low(values):
    high = values.astype(BF)
    return high, (values - high.astype(F32)).astype(BF)


def one_hot_t(ids_row, clusters):
    rows = lax.broadcasted_iota(jnp.int32, (clusters, ids_row.shape[1]), 0)
    return jnp.where(rows == ids_row, 1.0, 0.0).astype(BF)


def key_passes(total, size, score, weigh):
    count = total // size
    if count <= 4:
        blocks = [score(index) for index in range(count)]
        peak = functools.reduce(jnp.maximum, [jnp.max(b, axis=0, keepdims=True) for b in blocks])
        denom, sums = 0.0, None
        for index in range(count):
            expo = jnp.exp(blocks[index] - peak)
            denom = denom + jnp.sum(expo, axis=0, keepdims=True)
            parts = weigh(index, expo)
            sums = parts if sums is None else tuple(x + y for x, y in zip(sums, parts))
        return peak, denom, sums

    def step(index, carry):
        peak, denom, sums = carry
        block = score(index)
        fresh = jnp.maximum(peak, jnp.max(block, axis=0, keepdims=True))
        expo = jnp.exp(block - fresh)
        fade = jnp.exp(peak - fresh)
        parts = weigh(index, expo)
        return (
            fresh,
            denom * fade + jnp.sum(expo, axis=0, keepdims=True),
            tuple(old * fade + new for old, new in zip(sums, parts)),
        )

    shapes = jax.eval_shape(lambda: (score(0), weigh(0, score(0))))
    lanes = shapes[0].shape[1]
    start = (
        jnp.full((1, lanes), NEGATIVE, F32),
        jnp.zeros((1, lanes), F32),
        tuple(jnp.zeros(item.shape, F32) for item in shapes[1]),
    )
    return lax.fori_loop(0, count, step, start)


def key_sum(total, size, step, start):
    count = total // size
    if count <= 4:
        for index in range(count):
            start = step(index, start)
        return start
    return lax.fori_loop(0, count, step, start)


def spot_of(index, size):
    if isinstance(index, int):
        return pl.ds(index * size, size)
    return pl.ds(pl.multiple_of(index * size, size), size)


def piece(ref, index, size, axis):
    spot = spot_of(index, size)
    return ref[spot, :] if axis == 0 else ref[:, spot]


def bias_kernel(info, top_ref, bias_ref, *, groups, peers, rows):
    part = pl.program_id(0)
    owner = (
        lax.rem(info[0] + part // peers, groups) * peers + lax.rem(info[1] + part % peers, peers)
    )
    heads, picks, clusters = top_ref.shape
    place = owner * rows + lax.broadcasted_iota(jnp.int32, (rows, clusters), 0)
    outside = place >= info[2]
    for head in range(heads):
        top = top_ref[head]
        chosen = place == top[0:1, :]
        for pick in range(1, picks):
            chosen = chosen | (place == top[pick : pick + 1, :])
        value = jnp.where(chosen, 0.0, jnp.where(outside, EXCLUDED, NEGATIVE))
        bias_ref[head] = value.astype(BF)


def project_kernel(info, *refs, peers, olds):
    parts = refs[:peers]
    gain_ref, shift_ref, w_ref = refs[peers : peers + 3]
    hat_ref, feat_ref, kv_ref = refs[peers + 3 + olds :]
    rows = hat_ref.shape[0]
    for peer in range(peers):
        values = parts[peer][...].astype(F32)
        centered = values - jnp.mean(values, axis=-1, keepdims=True)
        variance = jnp.mean(centered * centered, axis=-1, keepdims=True)
        scaled = centered * lax.rsqrt(variance + EPSILON) * gain_ref[...]
        if peer == 0:
            hat_ref[...] = scaled.astype(BF)
        low = (scaled + shift_ref[...]).astype(BF)
        found = nt(w_ref[0], low)
        heads, triple = feat_ref.shape[0], feat_ref.shape[1]
        hs = triple // 3
        spot = slice(peer * rows, (peer + 1) * rows)
        for head in range(heads):
            base = head * triple
            query = (found[base : base + hs] * 0.125).astype(BF)
            pair = found[base + hs : base + triple].astype(BF)
            feat_ref[head, :hs, spot] = query
            feat_ref[head, hs:, spot] = pair
            kv_ref[head, spot, :] = pair.T


def forward_kernel(ids_all, ids_own, feat_all, feat_own, kv, bias, *refs, size, groups):
    outs = refs[:groups]
    mix_ref, stat_ref, cen_ref, table = refs[groups:]
    hs = feat_own.shape[1] // 3
    keys = kv.shape[1]
    clusters = bias.shape[2]
    kv_h, bias_h = kv.at[0], bias.at[0]
    qt_all, kvt = feat_all.at[0, :hs], feat_all.at[0, hs:]

    @pl.when(pl.program_id(1) == 0)
    def centroid_stage():
        hot = one_hot_t(ids_all[0], clusters)
        ones = jnp.ones((16, keys), BF)
        sums = nt(jnp.concatenate([qt_all[...], ones], axis=0), hot)
        counts = sums[hs : hs + 1]
        centroid = (sums[:hs] / jnp.maximum(counts, 1.0)).astype(BF)
        padded = jnp.concatenate([centroid, jnp.zeros_like(centroid)], axis=0)

        def score(index):
            scores = nn(piece(kv_h, index, size, 0), padded)
            outside = piece(bias_h, index, size, 0).astype(F32) < 2.0 * NEGATIVE
            return jnp.where(outside, NEGATIVE, scores)

        def weigh(index, expo):
            top = piece(bias_h, index, size, 0).astype(F32) == 0.0
            mass = jnp.sum(jnp.where(top, expo, 0.0), axis=0, keepdims=True)
            other = jnp.where(top, 0.0, expo).astype(BF)
            return nn(piece(kvt, index, size, 1), other), mass

        peak, denom, (rest, mass) = key_passes(keys, size, score, weigh)
        rest = rest[hs:] / denom
        mass = mass / denom
        stats = jnp.concatenate(
            [
                rest,
                mass,
                peak + jnp.log(denom),
                counts,
                jnp.zeros((5, clusters), F32),
            ],
            axis=0,
        )
        stat_ref[0] = stats
        cen_ref[0] = centroid
        high, low = split_low(stats)
        table[...] = jnp.concatenate([high, low], axis=1)

    hot = one_hot_t(ids_own[0], clusters)
    queries = feat_own[0, :hs]
    side = jnp.concatenate([queries, jnp.zeros_like(queries), hot], axis=0)
    gathered = nn(table[...], jnp.concatenate([hot, hot], axis=0))

    def score(index):
        return nn(
            jnp.concatenate([piece(kv_h, index, size, 0), piece(bias_h, index, size, 0)], axis=1),
            side,
        )

    def weigh(index, expo):
        return (nn(piece(kvt, index, size, 1), expo.astype(BF)),)

    peak, denom, (mix,) = key_passes(keys, size, score, weigh)
    mix = mix[hs:] / denom
    result = (gathered[hs : hs + 1] * mix + gathered[:hs]).astype(BF)
    for group in range(groups):

        @pl.when(pl.program_id(1) == group)
        def store(group=group):
            outs[group][...] = result

    mix_ref[0, 0] = jnp.concatenate(
        [mix, jnp.broadcast_to(peak + jnp.log(denom), (8, mix.shape[1]))], axis=0
    )


def sums_kernel(ids_own, *refs, groups):
    grads, (mix_ref, part_ref) = refs[:groups], refs[groups:]
    hs = grads[0].shape[0]
    total = None
    for group in range(groups):
        rows = grads[group].shape[1]
        step = ids_own.shape[2] // groups
        hot = one_hot_t(ids_own[0, :, group * step : group * step + rows], part_ref.shape[2])
        grad = grads[group][...]
        along = jnp.sum(grad.astype(F32) * mix_ref[0, group, :hs], axis=0, keepdims=True)
        high, low = split_low(along)
        pad = jnp.zeros((14, rows), BF)
        part = nt(jnp.concatenate([grad, high, low, pad], axis=0), hot)
        total = part if total is None else total + part
    part_ref[0] = total


def member_kernel(ids_own, feat_all, feat_own, kv, bias, *refs, size, groups):
    grads = refs[:groups]
    mix_ref, stat_ref, dq_ref, own_ref, send_ref, total, picked = refs[groups:]
    hs, rows = picked.shape
    keys = kv.shape[1]
    clusters = bias.shape[2]
    block = pl.program_id(1)
    for group in range(groups):

        @pl.when(block == group)
        def pick(group=group):
            picked[...] = grads[group][...]

    kv_h, bias_h, kvt = kv.at[0], bias.at[0], feat_all.at[0, hs:]
    hot = one_hot_t(ids_own[0], clusters)
    queries = feat_own[0, :hs]
    blank = jnp.zeros_like(queries)
    side = jnp.concatenate([queries, blank, hot], axis=0)
    high, low = split_low(stat_ref[0, hs : hs + 8, :])
    mass = nn(jnp.concatenate([high, low], axis=1), jnp.concatenate([hot, hot], axis=0))[0:1]
    mix = mix_ref[0, 0, :hs]
    level = mix_ref[0, 0, hs : hs + 1]
    back = (mass * picked[...].astype(F32)).astype(BF)
    delta = jnp.sum(back.astype(F32) * mix, axis=0, keepdims=True)
    back_pad = jnp.concatenate([blank, back], axis=0)
    right = jnp.concatenate([jnp.concatenate([queries, blank], axis=0), back_pad], axis=1).T

    @pl.when(block == 0)
    def clear():
        total[...] = jnp.zeros_like(total)

    def step(index, dq):
        kv_c = piece(kv_h, index, size, 0)
        scores = nn(jnp.concatenate([kv_c, piece(bias_h, index, size, 0)], axis=1), side)
        weights = jnp.exp(scores - level)
        grad_w = nn(kv_c, back_pad)
        grad_s = (weights * (grad_w - delta)).astype(BF)
        spot = spot_of(index, size)
        total[spot, :] += nn(jnp.concatenate([grad_s, weights.astype(BF)], axis=1), right)
        return dq + nn(piece(kvt, index, size, 1), grad_s)

    dq = key_sum(keys, size, step, jnp.zeros((2 * hs, rows), F32))
    dq_ref[0] = dq[:hs] * 0.125

    @pl.when(block == groups - 1)
    def finish():
        peers = keys // own_ref.shape[1]
        for group in range(groups):
            base = group * peers * rows
            own_ref[0, group * rows : (group + 1) * rows, :] = total[base : base + rows, :]
            for peer in range(1, peers):
                spot = (peer - 1) * groups * rows + group * rows
                send_ref[0, spot : spot + rows, :] = total[
                    base + peer * rows : base + (peer + 1) * rows, :
                ].astype(BF)


def centroid_kernel(ids_own, feat_all, kv, bias, part_ref, stat_ref, cen_ref, dqm_ref, own_ref, *refs, size, groups, gots):
    got_refs = refs[:gots]
    outs, both = refs[gots : gots + groups], refs[gots + groups]
    hs, rows = cen_ref.shape[1], outs[0].shape[2]
    keys = kv.shape[1]
    peers = keys // (groups * rows)
    clusters = bias.shape[2]
    kv_h, bias_h, kvt = kv.at[0], bias.at[0], feat_all.at[0, hs:]
    stats = stat_ref[0]
    rest, mass = stats[:hs], stats[hs : hs + 1]
    level, counts = stats[hs + 1 : hs + 2], stats[hs + 2 : hs + 3]
    centroid = cen_ref[0]
    blank = jnp.zeros_like(centroid)
    part = part_ref[0]
    d_rest = part[:hs].astype(BF)
    d_mass = part[hs : hs + 1] + part[hs + 1 : hs + 2]
    delta = jnp.sum(d_rest.astype(F32) * rest, axis=0, keepdims=True) + d_mass * mass
    cen_pad = jnp.concatenate([centroid, blank], axis=0)
    rest_pad = jnp.concatenate([blank, d_rest], axis=0)
    right = jnp.concatenate([cen_pad, rest_pad], axis=1).T

    def step(index, total):
        kv_c = piece(kv_h, index, size, 0)
        marks = piece(bias_h, index, size, 0).astype(F32)
        scores = nn(kv_c, cen_pad)
        probs = jnp.where(marks < 2.0 * NEGATIVE, 0.0, jnp.exp(scores - level))
        top = marks == 0.0
        d_probs = jnp.where(top, d_mass, nn(kv_c, rest_pad))
        d_score = (probs * (d_probs - delta)).astype(BF)
        other = jnp.where(top, 0.0, probs).astype(BF)
        both[spot_of(index, size), :] = jnp.concatenate([d_score, other], axis=1)
        return total + nn(piece(kvt, index, size, 1), d_score)

    d_cen = key_sum(keys, size, step, jnp.zeros((2 * hs, clusters), F32))
    d_cen = d_cen[:hs] * 0.125 / jnp.maximum(counts, 1.0)
    high, low = split_low(d_cen)
    table = jnp.concatenate([high, low], axis=1)
    for group in range(groups):
        spot = group * peers * rows
        hot = one_hot_t(ids_own[0, :, spot : spot + rows], clusters)
        spread = nn(table, jnp.concatenate([hot, hot], axis=0))
        own = nn(both[spot : spot + rows, :], right) + own_ref[0, group * rows : (group + 1) * rows, :]
        for got in got_refs:
            own = own + got[0, group * rows : (group + 1) * rows, :].astype(F32)
        outs[group][0, :hs] = (dqm_ref[group] + spread).astype(BF)
        outs[group][0, hs:] = own.T.astype(BF)


def block_kernel(info, *refs, groups, chunks, fast):
    (attn, rest) = (refs[:groups], refs[groups:])
    x_ref, gain_ref, shift_ref, wo_ref, up_ref, down_ref, cot_ref = rest[:7]
    out_ref, dres_ref, dn_ref, dup_ref, dbr_ref, act_ref, low_ref = rest[7:14]
    rest = rest[14:]
    if fast:
        act_far, low_far = rest[:2]
        rest = rest[2:]
    dat = rest[:groups]
    hat_ref, inv_ref, normed, back, total = rest[groups:]
    index = pl.program_id(0)

    @pl.when(index == 0)
    def before():
        resid = x_ref[...].astype(F32)
        for group in range(groups):
            owner = lax.rem(info[0] + groups - group, groups)
            resid = resid + tn(attn[group][...], wo_ref[owner])
        total[...] = resid
        centered = resid - jnp.mean(resid, axis=-1, keepdims=True)
        variance = jnp.mean(centered * centered, axis=-1, keepdims=True)
        inverse = lax.rsqrt(variance + EPSILON)
        hat = centered * inverse
        hat_ref[...] = hat
        inv_ref[...] = jnp.broadcast_to(inverse, inv_ref.shape)
        low = (hat * gain_ref[...] + shift_ref[...]).astype(BF)
        normed[...] = low
        if fast:
            feats = attn[0].shape[0]
            half = feats // 2
            turned = low.T
            for group in range(groups):
                first = turned[group * feats : group * feats + half]
                second = turned[group * feats + half : (group + 1) * feats]
                spot = slice(group * half, (group + 1) * half)
                low_ref[spot, :] = jnp.where(info[1] == 0, first, second)
                low_far[spot, :] = jnp.where(info[1] == 0, second, first)
                first = attn[group][:half]
                second = attn[group][half:]
                spot = slice((groups + group) * half, (groups + group + 1) * half)
                low_ref[spot, :] = jnp.where(info[1] == 0, first, second)
                low_far[spot, :] = jnp.where(info[1] == 0, second, first)
        else:
            low_ref[...] = low
        back[...] = jnp.zeros_like(back)

    up = nn(normed[...], up_ref[...])
    grad_act = nt(cot_ref[...], down_ref[...])
    square = up * up
    inner = GELU_A * (up + GELU_B * up * square)
    curve = jnp.tanh(inner)
    act = (0.5 * up * (1.0 + curve)).astype(BF)
    slope = 0.5 * (1.0 + curve) + 0.5 * up * (1.0 - curve * curve) * (
        GELU_A * (1.0 + 3.0 * GELU_B * square)
    )
    d_up = (grad_act * slope).astype(BF)
    dup_ref[...] = d_up
    if fast:
        half = act.shape[1] // 2
        first, second = act[:, :half], act[:, half:]
        act_ref[...] = jnp.where(info[1] == 0, first, second)
        act_far[...] = jnp.where(info[1] == 0, second, first)
    else:
        act_ref[...] = act
    back[...] += nt(d_up, up_ref[...])
    total[...] += nn(act, down_ref[...])

    @pl.when(index == chunks - 1)
    def after():
        out_ref[...] = total[...].astype(BF)
        d_normed = back[...]
        hat = hat_ref[...]
        gain_part = jnp.sum(d_normed * hat, axis=0, keepdims=True)
        shift_part = jnp.sum(d_normed, axis=0, keepdims=True)
        blank = jnp.zeros((6, d_normed.shape[1]), F32)
        dn_ref[...] = jnp.concatenate([gain_part, shift_part, blank], axis=0)
        gy = d_normed * gain_ref[...]
        mean_one = jnp.mean(gy, axis=-1, keepdims=True)
        mean_two = jnp.mean(gy * hat, axis=-1, keepdims=True)
        d_resid = cot_ref[...].astype(F32) + inv_ref[:, 0:1] * (gy - mean_one - hat * mean_two)
        dres_ref[...] = d_resid
        branch = d_resid.astype(BF)
        dbr_ref[...] = branch
        for group in range(groups):
            owner = lax.rem(info[0] + groups - group, groups)
            dat[group][...] = nt(wo_ref[owner], branch).astype(BF)


def weights_kernel(info, *refs, groups):
    (dup, dup_got, dbr, dbr_got, act, act_got, low, low_got, cot, cot_got, dn, dn_got) = refs[:12]
    send_u, keep_u, send_d, keep_d, outs = refs[12:]
    index = pl.program_id(0)
    group_at, place_u, place_d = info[0], info[3], info[4]
    rows = low.shape[0] // (2 * groups)
    quarter = rows // 4
    stay = groups * rows

    @pl.when(index == 0)
    def first():
        found = nn(low[stay:, :], dbr[...]) + nn(low_got[stay:, :], dbr_got[...])
        for group in range(groups):
            outs[group] = found[group * rows : (group + 1) * rows]

    up = nn(low[:stay, :], dup[...]) + nn(low_got[:stay, :], dup_got[...])
    at = lax.bitwise_xor(lax.bitwise_xor(index, 2), place_u)
    norms = dn[...] + dn_got[...]
    for group in range(groups):
        spot = lax.rem(group + groups - group_at, groups)
        block = up[group * rows : (group + 1) * rows].astype(BF)
        away = (groups - group) % groups
        start = pl.multiple_of(at * quarter, 8)
        other = jnp.concatenate([outs[group, pl.ds(start, quarter), :], norms], axis=0).astype(BF)

        @pl.when(index < 2)
        def leaves():
            send_u[0, spot, :rows] = block
            send_u[0, away, rows:] = other

        @pl.when(index >= 2)
        def stays():
            keep_u[0, spot, :rows] = block
            keep_u[0, away, rows:] = other

    down = tn(act[...], cot[...]) + tn(act_got[...], cot_got[...])
    spot = lax.rem(index + groups - group_at, groups)
    for part in range(4):
        block = down[part * rows : (part + 1) * rows].astype(BF)
        place = lax.bitwise_xor(part, place_d)

        @pl.when(place >= 2)
        def leaves_down():
            send_d[place - 2, spot] = block

        @pl.when(place < 2)
        def stays_down():
            keep_d[place, spot] = block


def second_kernel(keep_u, got_u, keep_d, got_d, send_u, send_d):
    send_u[...] = (keep_u[0].astype(F32) + got_u[0].astype(F32)).astype(BF)
    send_d[...] = (keep_d[0].astype(F32) + got_d[0].astype(F32)).astype(BF)


def third_kernel(keep_u, got_u, last_u, keep_d, got_d, last_d, *outs):
    rows = keep_u.shape[2]
    for group in range(len(outs)):
        up = keep_u[0, group].astype(F32) + got_u[0, group].astype(F32) + last_u[group].astype(F32)
        down = keep_d[0, group].astype(F32) + got_d[0, group].astype(F32) + last_d[group].astype(F32)
        outs[group][:rows] = up.astype(BF)
        outs[group][rows:] = down.astype(BF)


def fourth_kernel(*refs):
    parts, out = refs[:-1], refs[-1]
    total = parts[0][...].astype(F32)
    for part in parts[1:]:
        total = total + part[...].astype(F32)
    out[...] = total.astype(BF)


def spread_kernel(info, own, from_x, from_y, from_xy, up_ref, out_ref, down_ref, norm_ref):
    index = pl.program_id(0)
    rows = up_ref.shape[0]
    quarter = out_ref.shape[0]
    top = rows + quarter + 8
    for place, part in enumerate((own, from_y, from_x, from_xy)):

        @pl.when(index == place)
        def upper(part=part):
            up_ref[...] = part[:rows].astype(F32)
            tail = part[rows:top].astype(F32)
            out_ref[...] = tail[:quarter]

            @pl.when(lax.bitwise_xor(index, info[3]) == 0)
            def norms():
                norm_ref[...] = tail[quarter:]

    for place, part in enumerate((own, from_x, from_y, from_xy)):

        @pl.when(index == place)
        def lower(part=part):
            down_ref[...] = part[top:].astype(F32)


def inward_kernel(info, *refs, groups, fast):
    parts, hat_ref = refs[:groups], refs[groups]
    outs = refs[groups + 1 :]
    heads, triple, rows = parts[0].shape
    hs = triple // 3
    total, sums = None, None
    ones = jnp.ones((16, rows), BF)
    for group in range(groups):
        order = [parts[group][h, k * hs : (k + 1) * hs] for k in range(3) for h in range(heads)]
        turned = jnp.concatenate(order, axis=0)
        found = nn(turned, hat_ref[group * rows : (group + 1) * rows, :])
        more = nt(ones, turned)
        total = found if total is None else total + found
        sums = more if sums is None else sums + more
    total = total.T
    if not fast:
        outs[0][...] = total
        outs[1][...] = sums
        return
    own_ref, far_ref = outs
    block = total.shape[0] // (2 * groups)
    low_sums = sums.astype(BF)
    for group in range(groups):
        spot = lax.rem(group + groups - info[0], groups)
        first = total[2 * group * block : (2 * group + 1) * block].astype(BF)
        second = total[(2 * group + 1) * block : (2 * group + 2) * block].astype(BF)
        own_ref[spot, :block] = jnp.where(info[1] == 0, first, second)
        far_ref[spot, :block] = jnp.where(info[1] == 0, second, first)
        own_ref[spot, block:] = low_sums
        far_ref[spot, block:] = low_sums


def final_kernel(info, *refs, groups):
    parts = refs[:groups]
    x_ref, dres_ref, gain_ref, w_ref, out_ref = refs[groups:]
    d_normed = jnp.zeros(dres_ref.shape, F32)
    for group in range(groups):
        owner = lax.rem(info[0] + groups - group, groups)
        heads, triple, rows = parts[group].shape
        d_normed = d_normed + tn(parts[group][...].reshape(heads * triple, rows), w_ref[owner])
    values = x_ref[...].astype(F32)
    centered = values - jnp.mean(values, axis=-1, keepdims=True)
    variance = jnp.mean(centered * centered, axis=-1, keepdims=True)
    inverse = lax.rsqrt(variance + EPSILON)
    hat = centered * inverse
    gy = d_normed * gain_ref[...]
    mean_one = jnp.mean(gy, axis=-1, keepdims=True)
    mean_two = jnp.mean(gy * hat, axis=-1, keepdims=True)
    out_ref[...] = (dres_ref[...] + inverse * (gy - mean_one - hat * mean_two)).astype(BF)


def whole(shape):
    return pl.BlockSpec(shape, lambda *at: (0,) * len(shape))


def per_device(
    tokens,
    cluster_ids,
    lengths,
    top_keys,
    gain_one,
    shift_one,
    w_query,
    w_keyval,
    w_out,
    gain_two,
    shift_two,
    w_up,
    w_down,
    cotangent,
):
    rows, width = tokens.shape
    heads = cluster_ids.shape[1]
    hs = width // heads
    hidden = w_up.shape[1]
    wide = lax.axis_size("wide")
    n_dp = lax.axis_size("dp")
    groups = math.gcd(heads, wide)
    peers = wide // groups
    own_heads = heads // groups
    own_clusters = top_keys.shape[2]
    clusters = own_clusters * wide
    picks = top_keys.shape[3]
    seq = rows * wide
    size = 512 if seq <= 2048 else 2048
    feats = own_heads * hs
    block_rows = width // wide
    fast = peers == 2 and n_dp == 4 and block_rows % 32 == 0 and hidden % (4 * 256) == 0
    me = lax.axis_index("wide")
    group_at, peer_at = me // peers, me % peers
    dp_at = lax.axis_index("dp")
    seq_len = lengths[0]
    bit_x, bit_y = dp_at % 2, (dp_at // 2) % 2
    place_u, place_d = 2 * bit_x + bit_y, 2 * bit_y + bit_x
    info = jnp.stack([group_at, peer_at, seq_len, place_u, place_d, me]).astype(jnp.int32)

    def along_groups(values, hop):
        pairs = [(i, ((i // peers + hop) % groups) * peers + i % peers) for i in range(wide)]
        return lax.ppermute(values, "wide", pairs)

    def along_peers(values, hop):
        pairs = [(i, (i // peers) * peers + (i % peers + hop) % peers) for i in range(wide)]
        return lax.ppermute(values, "wide", pairs)

    def along_dp(values, mask):
        return lax.ppermute(values, "dp", [(i, i ^ mask) for i in range(n_dp)])

    def prefetched(kernel, grid, in_specs, out_specs, out_shape, mib, spent, name, scratch=(), alias=None):
        return pl.pallas_call(
            kernel,
            grid_spec=pltpu.PrefetchScalarGridSpec(
                num_scalar_prefetch=1,
                grid=grid,
                in_specs=in_specs,
                out_specs=out_specs,
                scratch_shapes=list(scratch),
            ),
            out_shape=out_shape,
            compiler_params=params(mib, len(grid)),
            cost_estimate=spent,
            input_output_aliases=alias or {},
            name=name,
        )

    def array(shape, dtype):
        return jax.ShapeDtypeStruct(shape, dtype)

    position = me * rows + jnp.arange(rows, dtype=jnp.int32)
    marked = jnp.where((position < seq_len)[:, None], cluster_ids, -1).T
    packed = jnp.concatenate([marked, top_keys[0].reshape(heads, own_clusters * picks)], axis=1)
    packed = packed.reshape(groups, own_heads, -1)

    def of_heads(hop):
        return lax.dynamic_index_in_dim(packed, (group_at + groups - hop) % groups, keepdims=False)

    arrived = [of_heads(0)] + [along_groups(of_heads(hop), -hop) for hop in range(1, groups)]
    arrived = jnp.stack(arrived)
    arrived = jnp.stack([arrived] + [along_peers(arrived, -hop) for hop in range(1, peers)], axis=1)
    ids_all = arrived[..., :rows].transpose(2, 0, 1, 3).reshape(own_heads, 1, seq)
    top_all = arrived[..., rows:].reshape(groups, peers, own_heads, own_clusters, picks)
    top_all = jnp.concatenate([top_all, top_all], axis=0)
    top_all = lax.dynamic_slice_in_dim(top_all, (groups - group_at) % groups, groups, axis=0)
    top_all = jnp.concatenate([top_all, top_all], axis=1)
    top_all = lax.dynamic_slice_in_dim(top_all, (peers - peer_at) % peers, peers, axis=1)
    top_all = top_all.transpose(2, 4, 0, 1, 3).reshape(own_heads, picks, clusters)

    mine = [tokens] + [along_groups(tokens, -hop) for hop in range(1, groups)]

    bias = prefetched(
        functools.partial(bias_kernel, groups=groups, peers=peers, rows=rows),
        (wide,),
        [whole((own_heads, picks, clusters))],
        pl.BlockSpec((own_heads, rows, clusters), lambda i, s: (0, i, 0)),
        array((own_heads, seq, clusters), BF),
        60,
        cost(own_heads * seq * clusters * picks * 8, own_heads * seq * clusters * 2),
        "bias",
    )(info, top_all)

    w_in = jnp.concatenate([w_query, w_keyval], axis=1).T.reshape(3, heads, hs, width)
    w_in = w_in.transpose(1, 0, 2, 3).reshape(groups, 3 * feats, width)
    gain_row, shift_row = gain_one[None, :], shift_one[None, :]
    shapes = [
        array((groups * rows, width), BF),
        array((own_heads, 3 * hs, seq), BF),
        array((own_heads, seq, 2 * hs), BF),
    ]
    held = []
    split_peers = peers if peers <= 2 else 1
    for group in range(groups):
        chunk = [mine[group]] + [along_peers(mine[group], -hop) for hop in range(1, peers)]
        if peers > 2:
            chunk = [jnp.concatenate(chunk, axis=0)]
        span = peers * rows
        if peers > 2:
            specs_in = [pl.BlockSpec((rows, width), lambda p, s: (p, 0))]
            grid = (peers,)
            outs = [
                pl.BlockSpec((rows, width), lambda p, s, g=group: (g, 0)),
                pl.BlockSpec((own_heads, 3 * hs, rows), lambda p, s, g=group: (0, 0, g * peers + p)),
                pl.BlockSpec((own_heads, rows, 2 * hs), lambda p, s, g=group: (0, g * peers + p, 0)),
            ]
        else:
            specs_in = [whole((rows, width))] * split_peers
            grid = (1,)
            outs = [
                pl.BlockSpec((rows, width), lambda p, s, g=group: (g, 0)),
                pl.BlockSpec((own_heads, 3 * hs, span), lambda p, s, g=group: (0, 0, g)),
                pl.BlockSpec((own_heads, span, 2 * hs), lambda p, s, g=group: (0, g, 0)),
            ]
        first = 1 + split_peers + 3
        held = prefetched(
            functools.partial(project_kernel, peers=split_peers, olds=len(held)),
            grid,
            specs_in
            + [
                whole((1, width)),
                whole((1, width)),
                pl.BlockSpec((1, 3 * feats, width), lambda p, s: (s[0], 0, 0)),
            ]
            + [pl.BlockSpec(memory_space=pl.ANY)] * len(held),
            outs,
            shapes,
            60,
            cost(6 * span * width * feats, span * width * 4),
            "project",
            alias={first + k: k for k in range(len(held))},
        )(info, *chunk, gain_row, shift_row, w_in, *held)
    hat_own, feat, kv = held

    ids_full = pl.BlockSpec((1, 1, seq), lambda h, r: (h, 0, 0))
    ids_block = pl.BlockSpec((1, 1, rows), lambda h, r: (h, 0, r * peers))
    feat_full = pl.BlockSpec((1, 3 * hs, seq), lambda h, r: (h, 0, 0))
    feat_block = pl.BlockSpec((1, 3 * hs, rows), lambda h, r: (h, 0, r * peers))
    kv_full = pl.BlockSpec((1, seq, 2 * hs), lambda h, r: (h, 0, 0))
    bias_full = pl.BlockSpec((1, seq, clusters), lambda h, r: (h, 0, 0))
    head_rows = pl.BlockSpec((hs, rows), lambda h, r: (h, 0))
    mix_spec = pl.BlockSpec((1, 1, hs + 8, rows), lambda h, r: (h, r, 0, 0))
    stat_spec = pl.BlockSpec((1, hs + 8, clusters), lambda h, r: (h, 0, 0))
    cen_spec = pl.BlockSpec((1, hs, clusters), lambda h, r: (h, 0, 0))
    own_rows = groups * rows
    pair_flops = own_heads * own_rows * seq * 256

    results = pl.pallas_call(
        functools.partial(forward_kernel, size=size, groups=groups),
        grid=(own_heads, groups),
        in_specs=[ids_full, ids_block, feat_full, feat_block, kv_full, bias_full],
        out_specs=[head_rows] * groups + [mix_spec, stat_spec, cen_spec],
        out_shape=[array((feats, rows), BF)] * groups
        + [
            array((own_heads, groups, hs + 8, rows), F32),
            array((own_heads, hs + 8, clusters), F32),
            array((own_heads, hs, clusters), BF),
        ],
        scratch_shapes=[pltpu.VMEM((hs + 8, 2 * clusters), BF)],
        compiler_params=params(60, 2),
        cost_estimate=cost(6 * pair_flops, 8e6, own_heads * own_rows * seq),
        name="attend",
    )(ids_all, ids_all, feat, feat, kv, bias)
    attn_t = results[:groups]
    mixed, stats, centroid = results[groups:]

    arrived = [attn_t[0]] + [along_groups(attn_t[hop], hop) for hop in range(1, groups)]

    chunks = 4
    part = hidden // chunks
    w_out_g = w_out.reshape(groups, feats, width)
    gain_row2, shift_row2 = gain_two[None, :], shift_two[None, :]
    square = whole((rows, width))
    column = pl.BlockSpec((rows, part), lambda i, s: (0, i))
    norm_spec = whole((8, width))
    if fast:
        half_column = pl.BlockSpec((rows, part // 2), lambda i, s: (0, i))
        kept = [array((rows, hidden // 2), BF), array((width, rows), BF)]
        kept_specs = [half_column, whole((width, rows))] * 2
        kept = kept * 2
    else:
        kept = [array((rows, hidden), BF), array((rows, width), BF)]
        kept_specs = [column, square]
    results = prefetched(
        functools.partial(block_kernel, groups=groups, chunks=chunks, fast=fast),
        (chunks,),
        [whole((feats, rows))] * groups
        + [
            square,
            whole((1, width)),
            whole((1, width)),
            whole((groups, feats, width)),
            pl.BlockSpec((width, part), lambda i, s: (0, i)),
            pl.BlockSpec((part, width), lambda i, s: (i, 0)),
            square,
        ],
        [square, square, norm_spec, column, square] + kept_specs + [whole((feats, rows))] * groups,
        [
            array((rows, width), BF),
            array((rows, width), F32),
            array((8, width), F32),
            array((rows, hidden), BF),
            array((rows, width), BF),
        ]
        + kept
        + [array((feats, rows), BF)] * groups,
        60,
        cost(8 * rows * width * hidden, 4 * width * hidden, rows * hidden),
        "feed",
        scratch=[
            pltpu.VMEM((rows, width), F32),
            pltpu.VMEM((rows, 128), F32),
            pltpu.VMEM((rows, width), BF),
            pltpu.VMEM((rows, width), F32),
            pltpu.VMEM((rows, width), F32),
        ],
    )(info, *arrived, tokens, gain_row2, shift_row2, w_out_g, w_up, w_down, cotangent)
    output, d_resid, norm_two, d_up, d_branch = results[:5]
    kept, d_attn = results[5:-groups], results[-groups:]
    grads = [d_attn[0]] + [along_groups(d_attn[hop], -hop) for hop in range(1, groups)]

    one = [
        pl.BlockSpec(spec.block_shape, functools.partial(lambda h, f: f(h, 0), f=spec.index_map))
        for spec in (ids_full, feat_full, kv_full, bias_full, stat_spec, cen_spec, head_rows)
    ]
    ids_one, feat_one, kv_one, bias_one, stat_one, cen_one, rows_one = one
    part_one = pl.BlockSpec((1, hs + 16, clusters), lambda h: (h, 0, 0))
    all_groups = pl.BlockSpec((groups, hs, rows), lambda h: (0, h, 0))
    own_one = pl.BlockSpec((1, own_rows, 2 * hs), lambda h: (h, 0, 0))

    share = pl.pallas_call(
        functools.partial(sums_kernel, groups=groups),
        grid=(own_heads,),
        in_specs=[ids_one]
        + [rows_one] * groups
        + [pl.BlockSpec((1, groups, hs + 8, rows), lambda h: (h, 0, 0, 0))],
        out_specs=part_one,
        out_shape=array((own_heads, hs + 16, clusters), F32),
        compiler_params=params(60, 1),
        cost_estimate=cost(own_heads * own_rows * clusters * 160, 2e6),
        name="sums",
    )(ids_all, *grads, mixed)
    share_got = [along_peers(share, hop) for hop in range(1, peers)]

    def weight_sums():
        dup_got, dbr_got = along_peers(d_up, 1), along_peers(d_branch, 1)
        act_own, low_own, act_far, low_far = kept
        act_got, low_got = along_peers(act_far, 1), along_peers(low_far, 1)
        cot_got, dn_got = along_peers(cotangent, 1), along_peers(norm_two, 1)
        high = block_rows + block_rows // 4 + 8
        chunk = pl.BlockSpec((rows, part), lambda i, s: (0, i ^ 2 ^ s[3]))
        act_spec = pl.BlockSpec((rows, part // 2), lambda i, s: (0, i))
        low_spec = whole((width, rows))
        shape_u = (2, groups, high, width)
        shape_d = (2, groups, block_rows, width)
        send_u, keep_u, send_d, keep_d = prefetched(
            functools.partial(weights_kernel, groups=groups),
            (4,),
            [chunk, chunk, square, square, act_spec, act_spec, low_spec, low_spec, square, square]
            + [norm_spec] * 2,
            [
                pl.BlockSpec((1,) + shape_u[1:], lambda i, s: (jnp.minimum(i, 1), 0, 0, 0)),
                pl.BlockSpec((1,) + shape_u[1:], lambda i, s: (jnp.maximum(i - 2, 0), 0, 0, 0)),
                whole(shape_d),
                whole(shape_d),
            ],
            [array(shape_u, BF), array(shape_u, BF), array(shape_d, BF), array(shape_d, BF)],
            60,
            cost(8 * rows * width * hidden, 6 * width * hidden),
            "weights",
            scratch=[pltpu.VMEM((groups, block_rows, width), F32)],
        )(
            info, d_up, dup_got, d_branch, dbr_got, act_own, act_got, low_own, low_got,
            cotangent, cot_got, norm_two, dn_got,
        )
        got_u, got_d = along_dp(send_u, 1), along_dp(send_d, 2)

        def block(shape, at):
            return pl.BlockSpec((1,) + shape[1:], lambda i: (at, 0, 0, 0))

        next_u, next_d = pl.pallas_call(
            second_kernel,
            grid=(1,),
            in_specs=[block(shape_u, 1), block(shape_u, 1), block(shape_d, 1), block(shape_d, 1)],
            out_specs=[whole(shape_u[1:]), whole(shape_d[1:])],
            out_shape=[array(shape_u[1:], BF), array(shape_d[1:], BF)],
            compiler_params=params(60, 1),
            cost_estimate=cost(groups * high * width * 2, groups * high * width * 12),
            name="second",
        )(keep_u, got_u, keep_d, got_d)
        last_u, last_d = along_dp(next_u, 2), along_dp(next_d, 1)
        tall = high + block_rows
        sums = pl.pallas_call(
            third_kernel,
            grid=(1,),
            in_specs=[
                block(shape_u, 0),
                block(shape_u, 0),
                whole(shape_u[1:]),
                block(shape_d, 0),
                block(shape_d, 0),
                whole(shape_d[1:]),
            ],
            out_specs=[whole((tall, width))] * groups,
            out_shape=[array((tall, width), BF)] * groups,
            compiler_params=params(60, 1),
            cost_estimate=cost(groups * tall * width * 4, groups * tall * width * 8),
            name="third",
        )(keep_u, got_u, last_u, keep_d, got_d, last_d)
        came = [sums[0]] + [along_groups(sums[hop], hop) for hop in range(1, groups)]
        done = pl.pallas_call(
            fourth_kernel,
            grid=(1,),
            in_specs=[whole((tall, width))] * groups,
            out_specs=whole((tall, width)),
            out_shape=array((tall, width), BF),
            compiler_params=params(60, 1),
            cost_estimate=cost(groups * tall * width, groups * tall * width * 2),
            name="fourth",
        )(*came)
        from_x, from_y, from_xy = (along_dp(done, mask) for mask in (1, 2, 3))
        quarter = block_rows // 4
        total_up, total_out, total_down, norms = prefetched(
            spread_kernel,
            (4,),
            [whole((tall, width))] * 4,
            [
                pl.BlockSpec((block_rows, part), lambda i, s: (0, i ^ s[3])),
                pl.BlockSpec((quarter, width), lambda i, s: (i ^ s[3], 0)),
                pl.BlockSpec((block_rows, width), lambda i, s: (i ^ s[4], 0)),
                whole((8, width)),
            ],
            [
                array((block_rows, hidden), F32),
                array((block_rows, width), F32),
                array((hidden // wide, width), F32),
                array((8, width), F32),
            ],
            60,
            cost(1e6, 4 * tall * width * 6),
            "spread",
        )(info, done, from_x, from_y, from_xy)
        norm_own = lax.dynamic_slice_in_dim(norms, me * block_rows, block_rows, axis=1)
        return total_up, total_out, total_down, norm_own

    masks = [1 << k for k in range(n_dp.bit_length() - 1)]

    def reduce_rows(partial):
        blocks = partial.reshape(groups, peers, partial.shape[0] // wide, partial.shape[1])

        def of_peer(hop):
            at = (peer_at + hop) % peers
            return lax.dynamic_index_in_dim(blocks, at, axis=1, keepdims=False)

        total = of_peer(0).astype(F32)
        for hop in range(1, peers):
            total = total + along_peers(of_peer(hop), hop).astype(F32)
        total = total.astype(BF)

        def of_group(hop):
            return lax.dynamic_index_in_dim(total, (group_at + hop) % groups, keepdims=False)

        done = of_group(0).astype(F32)
        for hop in range(1, groups):
            done = done + along_groups(of_group(hop), hop).astype(F32)
        for mask in masks:
            done = done.astype(BF)
            done = done.astype(F32) + along_dp(done, mask).astype(F32)
        return done

    if fast:
        total_up, total_out, total_down, norm_own = weight_sums()
    else:
        act, normed_two = kept
        total_up = reduce_rows(tn(normed_two, d_up).astype(BF))
        total_down = reduce_rows(tn(act, cotangent).astype(BF))
        found = jnp.stack([nn(item, d_branch).astype(BF) for item in arrived])
        found = [
            lax.dynamic_index_in_dim(found, (group_at + groups - g) % groups, keepdims=False)
            for g in range(groups)
        ]
        total_out = reduce_rows(jnp.concatenate(found, axis=0))
        norm_own = reduce_rows(norm_two[:2].T.astype(BF)).T

    dq_member, dkv_own, dkv_send = pl.pallas_call(
        functools.partial(member_kernel, size=size, groups=groups),
        grid=(own_heads, groups),
        in_specs=[ids_block, feat_full, feat_block, kv_full, bias_full]
        + [head_rows] * groups
        + [mix_spec, stat_spec],
        out_specs=[
            pl.BlockSpec((1, hs, rows), lambda h, r: (r, h, 0)),
            pl.BlockSpec((1, own_rows, 2 * hs), lambda h, r: (h, 0, 0)),
            pl.BlockSpec((1, max(peers - 1, 1) * own_rows, 2 * hs), lambda h, r: (h, 0, 0)),
        ],
        out_shape=[
            array((groups, feats, rows), F32),
            array((own_heads, own_rows, 2 * hs), F32),
            array((own_heads, max(peers - 1, 1) * own_rows, 2 * hs), BF),
        ],
        scratch_shapes=[pltpu.VMEM((seq, 2 * hs), F32), pltpu.VMEM((hs, rows), BF)],
        compiler_params=params(60, 2),
        cost_estimate=cost(12 * pair_flops, 10e6, own_heads * own_rows * seq),
        name="member",
    )(ids_all, feat, feat, kv, bias, *grads, mixed, stats)
    dkv_got = [
        along_peers(
            dkv_send if peers == 2 else dkv_send[:, (hop - 1) * own_rows : hop * own_rows], hop
        )
        for hop in range(1, peers)
    ]
    share_total = share
    for got in share_got:
        share_total = share_total + got

    d_in = pl.pallas_call(
        functools.partial(centroid_kernel, size=size, groups=groups, gots=len(dkv_got)),
        grid=(own_heads,),
        in_specs=[ids_one, feat_one, kv_one, bias_one, part_one, stat_one, cen_one, all_groups]
        + [own_one] * (1 + len(dkv_got)),
        out_specs=[pl.BlockSpec((1, 3 * hs, rows), lambda h: (h, 0, 0))] * groups,
        out_shape=[array((own_heads, 3 * hs, rows), BF)] * groups,
        scratch_shapes=[pltpu.VMEM((seq, 2 * clusters), BF)],
        compiler_params=params(60, 1),
        cost_estimate=cost(own_heads * clusters * seq * 1024, 8e6, own_heads * clusters * seq),
        name="centroid",
    )(ids_all, feat, kv, bias, share_total, stats, centroid, dq_member, dkv_own, *dkv_got)

    home = [d_in[0]] + [along_groups(d_in[hop], hop) for hop in range(1, groups)]

    tall = block_rows + 16
    part_spec = [whole((own_heads, 3 * hs, rows))] * groups + [whole((own_rows, width))]
    inward = functools.partial(
        prefetched,
        functools.partial(inward_kernel, groups=groups, fast=fast),
        (1,),
        part_spec,
    )
    spent = cost(2 * own_rows * width * 3 * feats, 4e6)
    if fast:
        half = groups // 2
        blocks = (groups, tall, 3 * feats)
        keep, far = inward(
            [whole(blocks)] * 2, [array(blocks, BF)] * 2, 60, spent, "inward"
        )(info, *d_in, hat_own)
        got = along_peers(far, 1)
        total = keep.astype(F32) + got.astype(F32)
        one_half, two_half = total[:half].astype(BF), total[half:].astype(BF)
        for mask in (1, 2):
            got_one, got_two = along_dp(one_half, mask), along_dp(two_half, 3 - mask)
            one_half = (one_half.astype(F32) + got_one.astype(F32)).astype(BF)
            two_half = (two_half.astype(F32) + got_two.astype(F32)).astype(BF)
        items = [one_half[k] for k in range(half)] + [two_half[k] for k in range(half)]
    else:
        found, more = inward(
            [whole((width, 3 * feats)), whole((16, 3 * feats))],
            [array((width, 3 * feats), F32), array((16, 3 * feats), F32)],
            60,
            spent,
            "inward",
        )(info, *d_in, hat_own)
        found = found.reshape(groups, peers, block_rows, 3 * feats)
        more = jnp.broadcast_to(more, (groups, peers, 16, 3 * feats))
        found = jnp.concatenate([found, more], axis=2).astype(BF)

        def of_peer(hop):
            at = (peer_at + hop) % peers
            return lax.dynamic_index_in_dim(found, at, axis=1, keepdims=False)

        total = of_peer(0).astype(F32)
        for hop in range(1, peers):
            total = total + along_peers(of_peer(hop), hop).astype(F32)
        for mask in masks:
            total = total.astype(BF)
            total = total.astype(F32) + along_dp(total, mask).astype(F32)
        total = total.astype(BF)
        items = [
            lax.dynamic_index_in_dim(total, (group_at + hop) % groups, keepdims=False)
            for hop in range(groups)
        ]
    pieces = [items[0]] + [along_groups(items[hop], hop) for hop in range(1, groups)]

    grad_tokens = prefetched(
        functools.partial(final_kernel, groups=groups),
        (1,),
        [whole((own_heads, 3 * hs, rows))] * groups
        + [square, square, whole((1, width)), whole((groups, 3 * feats, width))],
        square,
        array((rows, width), BF),
        60,
        cost(6 * rows * width * width, 6 * width * width),
        "final",
    )(info, *home, tokens, d_resid, gain_row, w_in)

    pieces = jnp.stack(pieces)
    pieces = jnp.stack(
        [
            lax.dynamic_index_in_dim(pieces, (group_at + groups - g) % groups, keepdims=False)
            for g in range(groups)
        ]
    ).astype(F32)
    q_part = pieces[:, :, :feats].transpose(1, 0, 2).reshape(tall, width)
    kv_part = (
        pieces[:, :, feats:]
        .reshape(groups, tall, 2, feats)
        .transpose(1, 2, 0, 3)
        .reshape(tall, 2 * width)
    )
    at = me * block_rows
    wq_rows = lax.dynamic_slice_in_dim(w_query, at, block_rows).astype(F32)
    wkv_rows = lax.dynamic_slice_in_dim(w_keyval, at, block_rows).astype(F32)
    gain_own = lax.dynamic_slice_in_dim(gain_one, at, block_rows)
    shift_own = lax.dynamic_slice_in_dim(shift_one, at, block_rows)
    q_sum, kv_sum = q_part[block_rows], kv_part[block_rows]
    q_part, kv_part = q_part[:block_rows], kv_part[:block_rows]
    shift_grad = jnp.sum(wq_rows * q_sum, axis=1) + jnp.sum(wkv_rows * kv_sum, axis=1)
    along = jnp.sum(wq_rows * q_part, axis=1) + jnp.sum(wkv_rows * kv_part, axis=1)
    return (
        output,
        grad_tokens,
        q_part + shift_own[:, None] * q_sum,
        kv_part + shift_own[:, None] * kv_sum,
        total_out,
        total_up,
        total_down,
        along / gain_own,
        shift_grad,
        norm_own[0],
        norm_own[1],
    )


def solution(mesh):
    return jax.shard_map(
        per_device,
        mesh=mesh,
        in_specs=(
            P(("dp", "wide"), None),
            P(("dp", "wide"), None),
            P("dp"),
            P("dp", None, "wide", None),
            P(),
            P(),
            P(),
            P(),
            P(),
            P(),
            P(),
            P(),
            P(),
            P(("dp", "wide"), None),
        ),
        out_specs=(
            P(("dp", "wide"), None),
            P(("dp", "wide"), None),
            P("wide", None),
            P("wide", None),
            P("wide", None),
            P("wide", None),
            P("wide", None),
            P("wide"),
            P("wide"),
            P("wide"),
            P("wide"),
        ),
        check_vma=False,
    )
```

time: 426 us -> 360 us (0.85)
  blocking collectives: 76.5 us -> 0 us
  waiting for transfers between devices: 71.5 us -> 131 us
  local copies, waits for them, and re-layouts: 75.4 us -> 28.5 us
  Pallas kernels: 105 us -> 138 us
  starting transfers between devices: 60.6 us -> 45 us
  other arithmetic: 25.6 us -> 14.5 us
  matrix products: 5.84 us -> 0 us
    psum x1 -> x0, blocking collectives: 39.8 us -> none  [per_device(): norms = lax.psum(norm_two, ('dp', 'wide'))]
    all_gather x1 -> x0, blocking collectives: 36.7 us -> none  [per_device(): gathered = lax.all_gather(packed, 'wide', axis=0, tiled=False)]
    pallas_call x9 -> x17, Pallas kernels: 105 us -> 138 us  [the longest x1 25.2 us: per_device(): pl.pallas_call(functools.partial(member_kernel, size=size, groups=groups)...]
    ppermute x27 -> x21, waiting for transfers between devices: 39 us -> 70.7 us  [along_groups(): return lax.ppermute(values, 'wide', pairs)]
    ppermute x14 -> x11, waiting for transfers between devices: 32.4 us -> 58.1 us  [along_dp(): return lax.ppermute(values, 'dp', [(i, i ^ mask) for i in range(n_dp)])]
    convert_element_type x18 -> x3, other arithmetic: 14.8 us -> 0.29 us  [the longest x2 0.21 us: per_device(): one_half = (one_half.astype(F32) + got_one.astype(F32)).astype(BF)]
    unnamed x98 -> x75, local copies, waits for them, and re-layouts: 29.7 us -> 15.4 us
    dynamic_slice x12 -> x3, local copies, waits for them, and re-layouts: 13.6 us -> 1.38 us  [the longest x1 0.78 us: weight_sums(): lax.dynamic_slice_in_dim(norms, me * block_rows, block_rows, axis=1)]
  transfers between devices with their start and end apart: 51 -> 46, of which waited for: 21 -> 21; matrix products, arithmetic and copies ran while one was open for 21% -> 8% of each run, Pallas kernels for 15% -> 14%
where the time goes in v2:
time: 360 us; the launch traced here: 359 us
  Pallas kernels  138 us (38%)
  waiting for transfers between devices  131 us (36%)
  starting transfers between devices  45 us (12%)
  local copies, waits for them, and re-layouts  28.5 us (8%)
  other arithmetic  14.5 us (4%)
    ppermute x21, waiting for transfers between devices, along_groups(): return lax.ppermute(values, 'wide', pairs)  70.7 us
    ppermute x11, waiting for transfers between devices, along_dp(): return lax.ppermute(values, 'dp', [(i, i ^ mask) for i in range(n_dp)])  58.1 us
    ppermute x21, starting transfers between devices, along_groups(): return lax.ppermute(values, 'wide', pairs)  29.5 us
    pallas_call x1, Pallas kernels, per_device(): pl.pallas_call(functools.partial(member_kernel, size=size, groups=groups)...  25.2 us
    pallas_call x1, Pallas kernels, per_device(): pl.pallas_call(functools.partial(forward_kernel, size=size, groups=groups...  22.5 us
    pallas_call x4, Pallas kernels, per_device(): prefetched(functools.partial(project_kernel, peers=split_peers, olds=len(...  16.6 us
    unnamed x75, local copies, waits for them, and re-layouts  15.4 us
    pallas_call x1, Pallas kernels, per_device(): prefetched(functools.partial(bias_kernel, groups=groups, peers=peers, row...  15 us
  transfers between devices with their start and end apart: 46, of which 21 were waited for; matrix products, arithmetic and copies ran while one was open for 8% of the time, Pallas kernels for 14%

profile of v2, /device:TPU:8, one launch (start us, length us, event | category | flops | bytes accessed | tf_op | source)
XLA Modules:
  0.0 358.9 jit_solution(6039730645158890818)
XLA Ops:
  5.9 1.9 collective-permute-start
  8.0 3.6 %collective-permute-start.6 = (bf16[256,768]{1,0:T(8,128)(2,1)}, bf16[256,768]{1,0:T(8,128)(2,1)}, u32[]{:S(2)}, u32[]{:S(2)}) collective-permute-start(bf16[256,768]{1,0:T(8,128)(2,1)} %refs_4_.3), channel_id=1, source_target_pairs={{0,4},{1,5},{2,6},{3,7},{4,0},{5,1},{6,2},{7,3},{8,12},{9,13},{10,... | collective-permute-start | bytes 1179656 | tf_op jit(solution)/shard_map/ppermute | solution.py:631
  11.6 4.3 %copy.53 = bf16[768,1536]{0,1:T(8,128)(2,1)} copy(bf16[768,1536]{1,0:T(8,128)(2,1)} %param.21) | data formatting | bytes 4718592 | tf_op args[7]
  18.6 2.2 pad_maximum_fusion
  22.0 2.0 copy.54
  25.5 9.2 %collective-permute-done.4.refs_0_ = bf16[256,768]{1,0:T(8,128)(2,1)} collective-permute-done((bf16[256,768]{1,0:T(8,128)(2,1)}, bf16[256,768]{1,0:T(8,128)(2,1)}, u32[]{:S(2)}, u32[]{:S(2)}) %collective-permute-start.4) | collective-permute-done | bytes 393248 | tf_op jit(solution)/shard_map/ppermute | solution.py:631
  34.7 7.1 %collective-permute-done.6.refs_0_ = bf16[256,768]{1,0:T(8,128)(2,1)} collective-permute-done((bf16[256,768]{1,0:T(8,128)(2,1)}, bf16[256,768]{1,0:T(8,128)(2,1)}, u32[]{:S(2)}, u32[]{:S(2)}) %collective-permute-start.6) | collective-permute-done | bytes 393248 | tf_op jit(solution)/shard_map/ppermute | solution.py:631
  41.8 2.9 collective-permute-done.8.refs_0_
  47.1 15.0 %bias.1 = bf16[3,2048,128]{2,1,0:T(8,128)(2,1)} custom-call(s32[6]{0:T(128)} %stack.64.info, s32[3,32,128]{2,1,0:T(8,128)} %copy.57.top_ref), custom_call_target="tpu_custom_call" | custom-call | flops 201326592 | bytes 1572864 | tf_op jit(solution)/shard_map/bias/pallas_call | solution.py:681
  62.1 4.2 %project.4 = (bf16[1024,768]{1,0:T(8,128)(2,1)}, bf16[3,192,2048]{2,1,0:T(8,128)(2,1)}, bf16[3,2048,128]{2,1,0:T(8,128)(2,1)}) custom-call(s32[6]{0:T(128)} %stack.64.info, bf16[256,768]{1,0:T(8,128)(2,1)} %refs_4_.3, bf16[256,768]{1,0:T(8,128)(2,1)} %collective-permute-done.10.refs_1_, f32[1,768]{1,0:T(1,128)} %broadcast_in_dim.29.refs_2_.refs_6_, ...), custom_call_target="tpu_custom_call" | custom-call | flops 452984832 | bytes 1572864 | tf_op jit(solution)/shard_map/project/pallas_call | solution.py:724
  67.0 4.1 %project.5 = (bf16[1024,768]{1,0:T(8,128)(2,1)}, bf16[3,192,2048]{2,1,0:T(8,128)(2,1)}, bf16[3,2048,128]{2,1,0:T(8,128)(2,1)}) custom-call(s32[6]{0:T(128)} %stack.64.info, bf16[256,768]{1,0:T(8,128)(2,1)} %collective-permute-done.8.refs_0_, bf16[256,768]{1,0:T(8,128)(2,1)} %copy-done.8, ...), custom_call_target="tpu_custom_call", output_to_operand_aliasing={{0}: (6, {}), {1}: (7, {}), {2}: (8, {})} | custom-call | flops 452984832 | bytes 1572864 | tf_op jit(solution)/shard_map/project/pallas_call | solution.py:724
  71.9 4.1 %project.6 = (bf16[1024,768]{1,0:T(8,128)(2,1)}, bf16[3,192,2048]{2,1,0:T(8,128)(2,1)}, bf16[3,2048,128]{2,1,0:T(8,128)(2,1)}) custom-call(s32[6]{0:T(128)} %stack.64.info, bf16[256,768]{1,0:T(8,128)(2,1)} %collective-permute-done.6.refs_0_, bf16[256,768]{1,0:T(8,128)(2,1)} %copy-done.7, ...), custom_call_target="tpu_custom_call", output_to_operand_aliasing={{0}: (6, {}), {1}: (7, {}), {2}: (8, {})} | custom-call | flops 452984832 | bytes 1572864 | tf_op jit(solution)/shard_map/project/pallas_call | solution.py:724
  76.8 4.1 %project.7 = (bf16[1024,768]{1,0:T(8,128)(2,1)}, bf16[3,192,2048]{2,1,0:T(8,128)(2,1)}, bf16[3,2048,128]{2,1,0:T(8,128)(2,1)}) custom-call(s32[6]{0:T(128)} %stack.64.info, bf16[256,768]{1,0:T(8,128)(2,1)} %collective-permute-done.4.refs_0_, bf16[256,768]{1,0:T(8,128)(2,1)} %copy-done.6, ...), custom_call_target="tpu_custom_call", output_to_operand_aliasing={{0}: (6, {}), {1}: (7, {}), {2}: (8, {})} | custom-call | flops 452984832 | bytes 1572864 | tf_op jit(solution)/shard_map/project/pallas_call | solution.py:724
  80.9 22.5 %attend.1 = (bf16[192,256]{1,0:T(8,128)(2,1)}, bf16[192,256]{1,0:T(8,128)(2,1)}, bf16[192,256]{1,0:T(8,128)(2,1)}, bf16[192,256]{1,0:T(8,128)(2,1)}, f32[3,4,72,...) custom-call(s32[3,1,2048]{2,1,0:T(1,128)} %reshape.61.ids_all.ids_own, ...), custom_call_target="tpu_custom_call" | custom-call | flops 9663676416 | bytes 8000000 | tf_op jit(solution)/shard_map/attend/pallas_call | solution.py:756
  104.5 1.9 collective-permute-start.13
  109.3 3.8 %collective-permute-done.12.refs_2_ = bf16[192,256]{1,0:T(8,128)(2,1)S(1)} collective-permute-done((bf16[192,256]{1,0:T(8,128)(2,1)}, bf16[192,256]{1,0:T(8,128)(2,1)S(1)}, u32[]{:S(2)}, u32[]{:S(2)}) %collective-permute-start.12) | collective-permute-done | bytes 98336 | tf_op jit(solution)/shard_map/ppermute | solution.py:631
  114.7 13.5 %feed.1 = (bf16[256,768]{1,0:T(8,128)(2,1)}, f32[256,768]{1,0:T(8,128)}, f32[8,768]{1,0:T(8,128)}, bf16[256,3072]{1,0:T(8,128)(2,1)}, bf16[256,768]{1,0:T(8,128)...) custom-call(s32[6]{0:T(128)} %stack.64.info, ...), custom_call_target="tpu_custom_call" | custom-call | flops 4831838208 | bytes 9437184 | tf_op jit(solution)/shard_map/feed/pallas_call | solution.py:792
  128.3 2.4 collective-permute-start.15
  130.7 2.8 collective-permute-start.16
  133.5 4.7 %collective-permute-done.15.refs_2_ = bf16[192,256]{1,0:T(8,128)(2,1)S(1)} collective-permute-done((bf16[192,256]{1,0:T(8,128)(2,1)}, bf16[192,256]{1,0:T(8,128)(2,1)S(1)}, u32[]{:S(2)}, u32[]{:S(2)}) %collective-permute-start.15) | collective-permute-done | bytes 98336 | tf_op jit(solution)/shard_map/ppermute | solution.py:631
  140.1 25.2 %member.1 = (f32[4,192,256]{2,1,0:T(8,128)}, f32[3,1024,128]{2,1,0:T(8,128)}, bf16[3,1024,128]{2,1,0:T(8,128)(2,1)}) custom-call(s32[3,1,2048]{2,1,0:T(1,128)} %reshape.61.ids_all.ids_own, bf16[3,192,2048]{2,1,0:T(8,128)(2,1)} %get-tuple-element.75.feat_all.feat_own, bf16[3,192,2048]{2,1,0:T(8,128)(2,1)} %get-tuple-element.75.feat_all.feat_own, ...), custom_call_target="tpu_custom_call" | custom-call | flops 19327352832 | bytes 10000000 | tf_op jit(solution)/shard_map/member/pallas_call | solution.py:993
  165.9 3.3 sums.1
  173.2 7.3 %centroid.1 = (bf16[3,192,256]{2,1,0:T(8,128)(2,1)}, bf16[3,192,256]{2,1,0:T(8,128)(2,1)}, bf16[3,192,256]{2,1,0:T(8,128)(2,1)}, bf16[3,192,256]{2,1,0:T(8,128)(2,1)}) custom-call(s32[3,1,2048]{2,1,0:T(1,128)} %reshape.61.ids_all.ids_own, bf16[3,192,2048]{2,1,0:T(8,128)(2,1)} %get-tuple-element.75.feat_all.feat_own, ...), custom_call_target="tpu_custom_call" | custom-call | flops 805306368 | bytes 8000000 | tf_op jit(solution)/shard_map/centroid/pallas_call | solution.py:1024
  180.5 5.0 %inward.1 = (bf16[4,112,576]{2,1,0:T(8,128)(2,1)}, bf16[4,112,576]{2,1,0:T(8,128)(2,1)}) custom-call(s32[6]{0:T(128)} %stack.64.info, bf16[3,192,256]{2,1,0:T(8,128)(2,1)} %get-tuple-element.92.refs_0_, bf16[3,192,256]{2,1,0:T(8,128)(2,1)} %get-tuple-element.93.refs_1_, bf16[3,192,256]{2,1,0:T(8,128)(2,1)} %get-tuple-element.94.refs_2_, ...), custom_call_target="tpu_custom_call" | custom-call | flops 905969664 | bytes 4000000 | tf_op jit(solution)/shard_map/inward/pallas_call | solution.py:1051
  190.0 10.9 %weights.1 = (bf16[2,4,128,768]{3,2,1,0:T(8,128)(2,1)}, bf16[2,4,128,768]{3,2,1,0:T(8,128)(2,1)}, bf16[2,4,96,768]{3,2,1,0:T(8,128)(2,1)}, bf16[2,4,96,768]{3,2,1,0:T(8,128)(2,1)}) custom-call(s32[6]{0:T(128)} %stack.64.info, bf16[256,3072]{1,0:T(8,128)(2,1)} %get-tuple-element.100.refs_0_, bf16[256,3072]{1,0:T(8,128)(2,1)} %collective-permute-done.30.refs_1_, ...), custom_call_target="tpu_custom_call" | custom-call | flops 4831838208 | bytes 14155776 | tf_op jit(solution)/shard_map/weights/pallas_call | solution.py:864
  205.2 38.8 %collective-permute-done.23 = bf16[2,112,576]{2,1,0:T(8,128)(2,1)S(1)} collective-permute-done((bf16[2,112,576]{2,1,0:T(8,128)(2,1)S(1)}, bf16[2,112,576]{2,1,0:T(8,128)(2,1)S(1)}, u32[]{:S(2)}, u32[]{:S(2)}) %collective-permute-start.23) | collective-permute-done | bytes 258080 | tf_op jit(solution)/shard_map/ppermute | solution.py:638
  247.2 2.4 collective-permute-start.19
  249.6 2.9 collective-permute-done.27
  252.5 2.1 collective-permute-start.20
  254.7 1.8 collective-permute-start.21
  259.3 3.0 second.1
  263.8 10.3 %collective-permute-done.19.refs_1_ = bf16[3,192,256]{2,1,0:T(8,128)(2,1)S(1)} collective-permute-done((bf16[3,192,256]{2,1,0:T(8,128)(2,1)}, bf16[3,192,256]{2,1,0:T(8,128)(2,1)S(1)}, u32[]{:S(2)}, u32[]{:S(2)}) %collective-permute-start.19) | collective-permute-done | bytes 294944 | tf_op jit(solution)/shard_map/ppermute | solution.py:631
  274.1 7.7 %collective-permute-done.20.refs_2_ = bf16[3,192,256]{2,1,0:T(8,128)(2,1)} collective-permute-done((bf16[3,192,256]{2,1,0:T(8,128)(2,1)}, bf16[3,192,256]{2,1,0:T(8,128)(2,1)}, u32[]{:S(2)}, u32[]{:S(2)}) %collective-permute-start.20) | collective-permute-done | bytes 294944 | tf_op jit(solution)/shard_map/ppermute | solution.py:631
  282.5 5.8 %final.1 = bf16[256,768]{1,0:T(8,128)(2,1)} custom-call(s32[6]{0:T(128)} %stack.64.info, bf16[3,192,256]{2,1,0:T(8,128)(2,1)} %get-tuple-element.92.refs_0_, bf16[3,192,256]{2,1,0:T(8,128)(2,1)} %copy-done.15, bf16[3,192,256]{2,1,0:T(8,128)(2,1)} %collective-permute-done.20.refs_2_, bf16[3,192,256]{2,1,0:T(8,128)(2,1)} %collective-permute-done.21.refs_3_, ...), custom_call_target="tpu_custom_call" | custom-call | flops 905969664 | bytes 3538944 | tf_op jit(solution)/shard_map/final/pallas_call | solution.py:1091
  290.1 3.8 %collective-permute-done.39.last_d = bf16[4,96,768]{2,1,0:T(8,128)(2,1)S(1)} collective-permute-done((bf16[4,96,768]{2,1,0:T(8,128)(2,1)}, bf16[4,96,768]{2,1,0:T(8,128)(2,1)S(1)}, u32[]{:S(2)}, u32[]{:S(2)}) %collective-permute-start.39) | collective-permute-done | bytes 589856 | tf_op jit(solution)/shard_map/ppermute | solution.py:638
  295.6 3.4 third.1
  299.0 3.9 %collective-permute-start.40 = (bf16[224,768]{1,0:T(8,128)(2,1)}, bf16[224,768]{1,0:T(8,128)(2,1)S(1)}, u32[]{:S(2)}, u32[]{:S(2)}) collective-permute-start(bf16[224,768]{1,0:T(8,128)(2,1)} %get-tuple-element.114), channel_id=1, source_target_pairs={{0,2},{1,3},{2,4},{3,5},{4,6},{5,7},{6,0},{7,1},{8,10},{9,11},{10,... | collective-permute-start | bytes 1032200 | tf_op jit(solution)/shard_map/ppermute | solution.py:631
  302.9 1.7 collective-permute-start.42
  307.0 2.0 fusion.1
  309.0 15.7 %collective-permute-done.40.refs_1_ = bf16[224,768]{1,0:T(8,128)(2,1)S(1)} collective-permute-done((bf16[224,768]{1,0:T(8,128)(2,1)}, bf16[224,768]{1,0:T(8,128)(2,1)S(1)}, u32[]{:S(2)}, u32[]{:S(2)}) %collective-permute-start.40) | collective-permute-done | bytes 344096 | tf_op jit(solution)/shard_map/ppermute | solution.py:631
  324.7 4.6 %collective-permute-done.41.refs_2_ = bf16[224,768]{1,0:T(8,128)(2,1)S(1)} collective-permute-done((bf16[224,768]{1,0:T(8,128)(2,1)}, bf16[224,768]{1,0:T(8,128)(2,1)S(1)}, u32[]{:S(2)}, u32[]{:S(2)}) %collective-permute-start.41) | collective-permute-done | bytes 344096 | tf_op jit(solution)/shard_map/ppermute | solution.py:631
  330.8 2.2 fourth.1.own
  333.0 2.4 collective-permute-start.43
  337.3 1.8 fusion.4
  340.2 4.2 %collective-permute-done.43.from_x = bf16[224,768]{1,0:T(8,128)(2,1)S(1)} collective-permute-done((bf16[224,768]{1,0:T(8,128)(2,1)}, bf16[224,768]{1,0:T(8,128)(2,1)S(1)}, u32[]{:S(2)}, u32[]{:S(2)}) %collective-permute-start.43) | collective-permute-done | bytes 344096 | tf_op jit(solution)/shard_map/ppermute | solution.py:638
  344.4 6.6 %collective-permute-done.44.from_y = bf16[224,768]{1,0:T(8,128)(2,1)S(1)} collective-permute-done((bf16[224,768]{1,0:T(8,128)(2,1)}, bf16[224,768]{1,0:T(8,128)(2,1)S(1)}, u32[]{:S(2)}, u32[]{:S(2)}) %collective-permute-start.44) | collective-permute-done | bytes 344096 | tf_op jit(solution)/shard_map/ppermute | solution.py:638
  351.0 1.8 collective-permute-done.45.from_xy
  353.5 4.0 %spread.1 = (f32[96,3072]{1,0:T(8,128)}, f32[96,768]{1,0:T(8,128)}, f32[384,768]{1,0:T(8,128)}, f32[8,768]{1,0:T(8,128)}) custom-call(s32[6]{0:T(128)} %stack.64.info, bf16[224,768]{1,0:T(8,128)(2,1)} %fourth.1.own, bf16[224,768]{1,0:T(8,128)(2,1)} %copy-done.12, bf16[224,768]{1,0:T(8,128)(2,1)} %copy-done.13, bf16[224,768]{1,0:T(8,128)(2,1)} %copy-done.14), custom_call_target="tpu_custom_call" | custom-call | flops 1000000 | bytes 4128768 | tf_op jit(solution)/shard_map/spread/pallas_call | solution.py:931
  (190 shorter events, 55.6 us)
Async XLA Ops:
  3.2 14.1 %collective-permute-start.2 = (s32[3,768]{1,0:T(4,128)S(1)}, s32[3,768]{1,0:T(4,128)S(1)}, u32[]{:S(2)}, u32[]{:S(2)}) collective-permute-start(s32[3,768]{1,0:T(4,128)S(1)} %get-tuple-element.142), channel_id=1, source_target_pairs={{0,2},{1,3},{2,4},{3,5},{4,6},{5,7},{6,0},{7,1},{8,10},{9,11},{10,... | collective-permute-start | bytes 27656 | tf_op jit(solution)/shard_map/ppermute | solution.py:631
  4.8 12.5 %collective-permute-start.1 = (s32[3,768]{1,0:T(4,128)S(1)}, s32[3,768]{1,0:T(4,128)S(1)}, u32[]{:S(2)}, u32[]{:S(2)}) collective-permute-start(s32[3,768]{1,0:T(4,128)S(1)} %get-tuple-element.143), channel_id=1, source_target_pairs={{0,4},{1,5},{2,6},{3,7},{4,0},{5,1},{6,2},{7,3},{8,12},{9,13},{10,... | collective-permute-start | bytes 27656 | tf_op jit(solution)/shard_map/ppermute | solution.py:631
  5.9 11.5 %collective-permute-start = (s32[3,768]{1,0:T(4,128)S(1)}, s32[3,768]{1,0:T(4,128)S(1)}, u32[]{:S(2)}, u32[]{:S(2)}) collective-permute-start(s32[3,768]{1,0:T(4,128)S(1)} %get-tuple-element.144), channel_id=1, source_target_pairs={{0,6},{1,7},{2,0},{3,1},{4,2},{5,3},{6,4},{7,5},{8,14},{9,15},{10,... | collective-permute-start | bytes 27656 | tf_op jit(solution)/shard_map/ppermute | solution.py:631
  7.9 26.8 %collective-permute-start.4 = (bf16[256,768]{1,0:T(8,128)(2,1)}, bf16[256,768]{1,0:T(8,128)(2,1)}, u32[]{:S(2)}, u32[]{:S(2)}) collective-permute-start(bf16[256,768]{1,0:T(8,128)(2,1)} %refs_4_.3), channel_id=1, source_target_pairs={{0,2},{1,3},{2,4},{3,5},{4,6},{5,7},{6,0},{7,1},{8,10},{9,11},{10,... | collective-permute-start | bytes 1179656 | tf_op jit(solution)/shard_map/ppermute | solution.py:631
  8.0 33.8 %collective-permute-start.6 = (bf16[256,768]{1,0:T(8,128)(2,1)}, bf16[256,768]{1,0:T(8,128)(2,1)}, u32[]{:S(2)}, u32[]{:S(2)}) collective-permute-start(bf16[256,768]{1,0:T(8,128)(2,1)} %refs_4_.3), channel_id=1, source_target_pairs={{0,4},{1,5},{2,6},{3,7},{4,0},{5,1},{6,2},{7,3},{8,12},{9,13},{10,... | collective-permute-start | bytes 1179656 | tf_op jit(solution)/shard_map/ppermute | solution.py:631
  17.3 27.4 %collective-permute-start.8 = (bf16[256,768]{1,0:T(8,128)(2,1)}, bf16[256,768]{1,0:T(8,128)(2,1)}, u32[]{:S(2)}, u32[]{:S(2)}) collective-permute-start(bf16[256,768]{1,0:T(8,128)(2,1)} %refs_4_.3), channel_id=1, source_target_pairs={{0,6},{1,7},{2,0},{3,1},{4,2},{5,3},{6,4},{7,5},{8,14},{9,15},{10,... | collective-permute-start | bytes 1179656 | tf_op jit(solution)/shard_map/ppermute | solution.py:631
  17.3 44.8 %collective-permute-start.10 = (bf16[256,768]{1,0:T(8,128)(2,1)}, bf16[256,768]{1,0:T(8,128)(2,1)}, u32[]{:S(2)}, u32[]{:S(2)}) collective-permute-start(bf16[256,768]{1,0:T(8,128)(2,1)} %refs_4_.3), channel_id=1, source_target_pairs={{0,1},{1,0},{2,3},{3,2},{4,5},{5,4},{6,7},{7,6},{8,9},{9,8},{10,11... | collective-permute-start | bytes 1179656 | tf_op jit(solution)/shard_map/ppermute | solution.py:635
  18.1 6.6 %collective-permute-start.3 = (s32[4,3,768]{2,1,0:T(4,128)}, s32[4,3,768]{2,1,0:T(4,128)}, u32[]{:S(2)}, u32[]{:S(2)}) collective-permute-start(s32[4,3,768]{2,1,0:T(4,128)} %get-tuple-element.140), channel_id=1, source_target_pairs={{0,1},{1,0},{2,3},{3,2},{4,5},{5,4},{6,7},{7,6},{8,9},{9,8},{10,11... | collective-permute-start | bytes 110600 | tf_op jit(solution)/shard_map/ppermute | solution.py:635
  34.7 41.4 %collective-permute-start.5 = (bf16[256,768]{1,0:T(8,128)(2,1)}, bf16[256,768]{1,0:T(8,128)(2,1)S(1)}, u32[]{:S(2)}, u32[]{:S(2)}) collective-permute-start(bf16[256,768]{1,0:T(8,128)(2,1)} %collective-permute-done.4.refs_0_), channel_id=1, source_target_pairs={{0,1},{1,0},{2,3},{3,2},{4,5},{5,4},{6,7},{7,6},{8,9},{9,8},{10,11... | collective-permute-start | bytes 1179656 | tf_op jit(solution)/shard_map/ppermute | solution.py:635
  41.8 29.4 %collective-permute-start.7 = (bf16[256,768]{1,0:T(8,128)(2,1)}, bf16[256,768]{1,0:T(8,128)(2,1)S(1)}, u32[]{:S(2)}, u32[]{:S(2)}) collective-permute-start(bf16[256,768]{1,0:T(8,128)(2,1)} %collective-permute-done.6.refs_0_), channel_id=1, source_target_pairs={{0,1},{1,0},{2,3},{3,2},{4,5},{5,4},{6,7},{7,6},{8,9},{9,8},{10,11... | collective-permute-start | bytes 1179656 | tf_op jit(solution)/shard_map/ppermute | solution.py:635
  44.7 21.6 %collective-permute-start.9 = (bf16[256,768]{1,0:T(8,128)(2,1)}, bf16[256,768]{1,0:T(8,128)(2,1)S(1)}, u32[]{:S(2)}, u32[]{:S(2)}) collective-permute-start(bf16[256,768]{1,0:T(8,128)(2,1)} %collective-permute-done.8.refs_0_), channel_id=1, source_target_pairs={{0,1},{1,0},{2,3},{3,2},{4,5},{5,4},{6,7},{7,6},{8,9},{9,8},{10,11... | collective-permute-start | bytes 1179656 | tf_op jit(solution)/shard_map/ppermute | solution.py:635
  103.4 5.9 %collective-permute-start.11 = (bf16[192,256]{1,0:T(8,128)(2,1)}, bf16[192,256]{1,0:T(8,128)(2,1)S(1)}, u32[]{:S(2)}, u32[]{:S(2)}) collective-permute-start(bf16[192,256]{1,0:T(8,128)(2,1)} %get-tuple-element.78), channel_id=1, source_target_pairs={{0,2},{1,3},{2,4},{3,5},{4,6},{5,7},{6,0},{7,1},{8,10},{9,11},{10,... | collective-permute-start | bytes 294920 | tf_op jit(solution)/shard_map/ppermute | solution.py:631
  103.5 9.6 %collective-permute-start.12 = (bf16[192,256]{1,0:T(8,128)(2,1)}, bf16[192,256]{1,0:T(8,128)(2,1)S(1)}, u32[]{:S(2)}, u32[]{:S(2)}) collective-permute-start(bf16[192,256]{1,0:T(8,128)(2,1)} %get-tuple-element.79), channel_id=1, source_target_pairs={{0,4},{1,5},{2,6},{3,7},{4,0},{5,1},{6,2},{7,3},{8,12},{9,13},{10,... | collective-permute-start | bytes 294920 | tf_op jit(solution)/shard_map/ppermute | solution.py:631
  104.5 9.5 %collective-permute-start.13 = (bf16[192,256]{1,0:T(8,128)(2,1)}, bf16[192,256]{1,0:T(8,128)(2,1)S(1)}, u32[]{:S(2)}, u32[]{:S(2)}) collective-permute-start(bf16[192,256]{1,0:T(8,128)(2,1)} %get-tuple-element.80), channel_id=1, source_target_pairs={{0,6},{1,7},{2,0},{3,1},{4,2},{5,3},{6,4},{7,5},{8,14},{9,15},{10,... | collective-permute-start | bytes 294920 | tf_op jit(solution)/shard_map/ppermute | solution.py:631
  128.2 5.3 %collective-permute-start.14 = (bf16[192,256]{1,0:T(8,128)(2,1)}, bf16[192,256]{1,0:T(8,128)(2,1)S(1)}, u32[]{:S(2)}, u32[]{:S(2)}) collective-permute-start(bf16[192,256]{1,0:T(8,128)(2,1)} %get-tuple-element.83), channel_id=1, source_target_pairs={{0,6},{1,7},{2,0},{3,1},{4,2},{5,3},{6,4},{7,5},{8,14},{9,15},{10,... | collective-permute-start | bytes 294920 | tf_op jit(solution)/shard_map/ppermute | solution.py:631
  128.3 10.0 %collective-permute-start.15 = (bf16[192,256]{1,0:T(8,128)(2,1)}, bf16[192,256]{1,0:T(8,128)(2,1)S(1)}, u32[]{:S(2)}, u32[]{:S(2)}) collective-permute-start(bf16[192,256]{1,0:T(8,128)(2,1)} %get-tuple-element.84), channel_id=1, source_target_pairs={{0,4},{1,5},{2,6},{3,7},{4,0},{5,1},{6,2},{7,3},{8,12},{9,13},{10,... | collective-permute-start | bytes 294920 | tf_op jit(solution)/shard_map/ppermute | solution.py:631
  130.7 8.8 %collective-permute-start.16 = (bf16[192,256]{1,0:T(8,128)(2,1)}, bf16[192,256]{1,0:T(8,128)(2,1)S(1)}, u32[]{:S(2)}, u32[]{:S(2)}) collective-permute-start(bf16[192,256]{1,0:T(8,128)(2,1)} %get-tuple-element.85), channel_id=1, source_target_pairs={{0,2},{1,3},{2,4},{3,5},{4,6},{5,7},{6,0},{7,1},{8,10},{9,11},{10,... | collective-permute-start | bytes 294920 | tf_op jit(solution)/shard_map/ppermute | solution.py:631
  140.1 29.1 %copy-start.26 = (bf16[256,768]{1,0:T(8,128)(2,1)S(1)}, bf16[256,768]{1,0:T(8,128)(2,1)}, u32[]{:S(2)}) copy-start(bf16[256,768]{1,0:T(8,128)(2,1)} %refs_8_.3) | copy-start | bytes 1179652
  140.1 29.6 %copy-start.25 = (bf16[256,1536]{1,0:T(8,128)(2,1)S(1)}, bf16[256,1536]{1,0:T(8,128)(2,1)}, u32[]{:S(2)}) copy-start(bf16[256,1536]{1,0:T(8,128)(2,1)} %get-tuple-element.103) | copy-start | bytes 2359300
  165.3 7.0 %collective-permute-start.18 = (bf16[3,1024,128]{2,1,0:T(8,128)(2,1)}, bf16[3,1024,128]{2,1,0:T(8,128)(2,1)S(1)}, u32[]{:S(2)}, u32[]{:S(2)}) collective-permute-start(bf16[3,1024,128]{2,1,0:T(8,128)(2,1)} %get-tuple-element.91), channel_id=1, source_target_pairs={{0,1},{1,0},{2,3},{3,2},{4,5},{5,4},{6,7},{7,6},{8,9},{9,8},{10,11... | collective-permute-start | bytes 2359304 | tf_op jit(solution)/shard_map/ppermute | solution.py:635
  165.4 23.7 %collective-permute-start.30 = (bf16[256,3072]{1,0:T(8,128)(2,1)S(1)}, bf16[256,3072]{1,0:T(8,128)(2,1)}, u32[]{:S(2)}, u32[]{:S(2)}) collective-permute-start(bf16[256,3072]{1,0:T(8,128)(2,1)S(1)} %copy-done.24), channel_id=1, source_target_pairs={{0,1},{1,0},{2,3},{3,2},{4,5},{5,4},{6,7},{7,6},{8,9},{9,8},{10,11... | collective-permute-start | bytes 4718600 | tf_op jit(solution)/shard_map/ppermute | solution.py:635
  169.2 1.5 collective-permute-start.17
  169.3 16.8 %collective-permute-start.34 = (bf16[256,768]{1,0:T(8,128)(2,1)S(1)}, bf16[256,768]{1,0:T(8,128)(2,1)}, u32[]{:S(2)}, u32[]{:S(2)}) collective-permute-start(bf16[256,768]{1,0:T(8,128)(2,1)S(1)} %copy-done.26), channel_id=1, source_target_pairs={{0,1},{1,0},{2,3},{3,2},{4,5},{5,4},{6,7},{7,6},{8,9},{9,8},{10,11... | collective-permute-start | bytes 1179656 | tf_op jit(solution)/shard_map/ppermute | solution.py:635
  169.7 19.5 %collective-permute-start.32 = (bf16[256,1536]{1,0:T(8,128)(2,1)S(1)}, bf16[256,1536]{1,0:T(8,128)(2,1)}, u32[]{:S(2)}, u32[]{:S(2)}) collective-permute-start(bf16[256,1536]{1,0:T(8,128)(2,1)S(1)} %copy-done.25), channel_id=1, source_target_pairs={{0,1},{1,0},{2,3},{3,2},{4,5},{5,4},{6,7},{7,6},{8,9},{9,8},{10,11... | collective-permute-start | bytes 2359304 | tf_op jit(solution)/shard_map/ppermute | solution.py:635
  185.5 2.2 collective-permute-start.22
  185.7 3.4 collective-permute-start.31
  186.1 3.1 collective-permute-start.33
  187.7 1.3 collective-permute-start.35
  200.9 57.2 %collective-permute-start.36 = (bf16[2,4,128,768]{3,2,1,0:T(8,128)(2,1)}, bf16[2,4,128,768]{3,2,1,0:T(8,128)(2,1)S(1)}, u32[]{:S(2)}, u32[]{:S(2)}) collective-permute-start(bf16[2,4,128,768]{3,2,1,0:T(8,128)(2,1)} %get-tuple-element.108), channel_id=1, source_target_pairs={{0,8},{8,0},{16,24},{24,16},{1,9},{9,1},{17,25},{25,17},{2,10},{10... | collective-permute-start | bytes 4718600 | tf_op jit(solution)/shard_map/ppermute | solution.py:638
  202.5 41.5 %collective-permute-start.23 = (bf16[2,112,576]{2,1,0:T(8,128)(2,1)S(1)}, bf16[2,112,576]{2,1,0:T(8,128)(2,1)S(1)}, u32[]{:S(2)}, u32[]{:S(2)}) collective-permute-start(bf16[2,112,576]{2,1,0:T(8,128)(2,1)S(1)} %get-tuple-element.132), channel_id=1, source_target_pairs={{0,8},{8,0},{16,24},{24,16},{1,9},{9,1},{17,25},{25,17},{2,10},{10... | collective-permute-start | bytes 774152 | tf_op jit(solution)/shard_map/ppermute | solution.py:638
  203.2 40.9 %collective-permute-start.26 = (bf16[2,112,576]{2,1,0:T(8,128)(2,1)S(1)}, bf16[2,112,576]{2,1,0:T(8,128)(2,1)S(1)}, u32[]{:S(2)}, u32[]{:S(2)}) collective-permute-start(bf16[2,112,576]{2,1,0:T(8,128)(2,1)S(1)} %get-tuple-element.133), channel_id=1, source_target_pairs={{0,16},{8,24},{16,0},{24,8},{1,17},{9,25},{17,1},{25,9},{2,18},{10... | collective-permute-start | bytes 774152 | tf_op jit(solution)/shard_map/ppermute | solution.py:638
  204.7 52.7 %collective-permute-start.37 = (bf16[2,4,96,768]{3,2,1,0:T(8,128)(2,1)}, bf16[2,4,96,768]{3,2,1,0:T(8,128)(2,1)S(1)}, u32[]{:S(2)}, u32[]{:S(2)}) collective-permute-start(bf16[2,4,96,768]{3,2,1,0:T(8,128)(2,1)} %get-tuple-element.110), channel_id=1, source_target_pairs={{0,16},{8,24},{16,0},{24,8},{1,17},{9,25},{17,1},{25,9},{2,18},{10... | collective-permute-start | bytes 3538952 | tf_op jit(solution)/shard_map/ppermute | solution.py:638
  244.2 8.3 %collective-permute-start.27 = (bf16[2,112,576]{2,1,0:T(8,128)(2,1)S(1)}, bf16[2,112,576]{2,1,0:T(8,128)(2,1)S(1)}, u32[]{:S(2)}, u32[]{:S(2)}) collective-permute-start(bf16[2,112,576]{2,1,0:T(8,128)(2,1)S(1)} %get-tuple-element.131), channel_id=1, source_target_pairs={{0,8},{8,0},{16,24},{24,16},{1,9},{9,1},{17,25},{25,17},{2,10},{10... | collective-permute-start | bytes 774152 | tf_op jit(solution)/shard_map/ppermute | solution.py:638
  245.7 9.0 %collective-permute-start.24 = (bf16[2,112,576]{2,1,0:T(8,128)(2,1)S(1)}, bf16[2,112,576]{2,1,0:T(8,128)(2,1)S(1)}, u32[]{:S(2)}, u32[]{:S(2)}) collective-permute-start(bf16[2,112,576]{2,1,0:T(8,128)(2,1)S(1)} %get-tuple-element.130), channel_id=1, source_target_pairs={{0,16},{8,24},{16,0},{24,8},{1,17},{9,25},{17,1},{25,9},{2,18},{10... | collective-permute-start | bytes 774152 | tf_op jit(solution)/shard_map/ppermute | solution.py:638
  247.2 26.9 %collective-permute-start.19 = (bf16[3,192,256]{2,1,0:T(8,128)(2,1)}, bf16[3,192,256]{2,1,0:T(8,128)(2,1)S(1)}, u32[]{:S(2)}, u32[]{:S(2)}) collective-permute-start(bf16[3,192,256]{2,1,0:T(8,128)(2,1)} %get-tuple-element.93.refs_1_), channel_id=1, source_target_pairs={{0,2},{1,3},{2,4},{3,5},{4,6},{5,7},{6,0},{7,1},{8,10},{9,11},{10,... | collective-permute-start | bytes 884744 | tf_op jit(solution)/shard_map/ppermute | solution.py:631
  252.5 29.3 %collective-permute-start.20 = (bf16[3,192,256]{2,1,0:T(8,128)(2,1)}, bf16[3,192,256]{2,1,0:T(8,128)(2,1)}, u32[]{:S(2)}, u32[]{:S(2)}) collective-permute-start(bf16[3,192,256]{2,1,0:T(8,128)(2,1)} %get-tuple-element.94.refs_2_), channel_id=1, source_target_pairs={{0,4},{1,5},{2,6},{3,7},{4,0},{5,1},{6,2},{7,3},{8,12},{9,13},{10,... | collective-permute-start | bytes 884744 | tf_op jit(solution)/shard_map/ppermute | solution.py:631
  254.7 27.1 %collective-permute-start.21 = (bf16[3,192,256]{2,1,0:T(8,128)(2,1)}, bf16[3,192,256]{2,1,0:T(8,128)(2,1)}, u32[]{:S(2)}, u32[]{:S(2)}) collective-permute-start(bf16[3,192,256]{2,1,0:T(8,128)(2,1)} %get-tuple-element.95.refs_3_), channel_id=1, source_target_pairs={{0,6},{1,7},{2,0},{3,1},{4,2},{5,3},{6,4},{7,5},{8,14},{9,15},{10,... | collective-permute-start | bytes 884744 | tf_op jit(solution)/shard_map/ppermute | solution.py:631
  257.3 31.0 %collective-permute-start.29 = (bf16[112,576]{1,0:T(8,128)(2,1)}, bf16[112,576]{1,0:T(8,128)(2,1)}, u32[]{:S(2)}, u32[]{:S(2)}) collective-permute-start(bf16[112,576]{1,0:T(8,128)(2,1)} %get-tuple-element.138), channel_id=1, source_target_pairs={{0,6},{1,7},{2,0},{3,1},{4,2},{5,3},{6,4},{7,5},{8,14},{9,15},{10,... | collective-permute-start | bytes 387080 | tf_op jit(solution)/shard_map/ppermute | solution.py:631
  262.3 31.7 %collective-permute-start.38 = (bf16[4,128,768]{2,1,0:T(8,128)(2,1)}, bf16[4,128,768]{2,1,0:T(8,128)(2,1)S(1)}, u32[]{:S(2)}, u32[]{:S(2)}) collective-permute-start(bf16[4,128,768]{2,1,0:T(8,128)(2,1)} %get-tuple-element.111), channel_id=1, source_target_pairs={{0,16},{8,24},{16,0},{24,8},{1,17},{9,25},{17,1},{25,9},{2,18},{10... | collective-permute-start | bytes 2359304 | tf_op jit(solution)/shard_map/ppermute | solution.py:638
  274.1 14.2 %collective-permute-start.28 = (bf16[112,576]{1,0:T(8,128)(2,1)}, bf16[112,576]{1,0:T(8,128)(2,1)S(1)}, u32[]{:S(2)}, u32[]{:S(2)}) collective-permute-start(bf16[112,576]{1,0:T(8,128)(2,1)} %get-tuple-element.137), channel_id=1, source_target_pairs={{0,4},{1,5},{2,6},{3,7},{4,0},{5,1},{6,2},{7,3},{8,12},{9,13},{10,... | collective-permute-start | bytes 387080 | tf_op jit(solution)/shard_map/ppermute | solution.py:631
  281.9 6.5 %collective-permute-start.25 = (bf16[112,576]{1,0:T(8,128)(2,1)S(1)}, bf16[112,576]{1,0:T(8,128)(2,1)S(1)}, u32[]{:S(2)}, u32[]{:S(2)}) collective-permute-start(bf16[112,576]{1,0:T(8,128)(2,1)S(1)} %get-tuple-element.136), channel_id=1, source_target_pairs={{0,2},{1,3},{2,4},{3,5},{4,6},{5,7},{6,0},{7,1},{8,10},{9,11},{10,... | collective-permute-start | bytes 387080 | tf_op jit(solution)/shard_map/ppermute | solution.py:631
  281.9 12.1 %collective-permute-start.39 = (bf16[4,96,768]{2,1,0:T(8,128)(2,1)}, bf16[4,96,768]{2,1,0:T(8,128)(2,1)S(1)}, u32[]{:S(2)}, u32[]{:S(2)}) collective-permute-start(bf16[4,96,768]{2,1,0:T(8,128)(2,1)} %get-tuple-element.112), channel_id=1, source_target_pairs={{0,8},{8,0},{16,24},{24,16},{1,9},{9,1},{17,25},{25,17},{2,10},{10... | collective-permute-start | bytes 1769480 | tf_op jit(solution)/shard_map/ppermute | solution.py:638
  299.0 25.7 %collective-permute-start.40 = (bf16[224,768]{1,0:T(8,128)(2,1)}, bf16[224,768]{1,0:T(8,128)(2,1)S(1)}, u32[]{:S(2)}, u32[]{:S(2)}) collective-permute-start(bf16[224,768]{1,0:T(8,128)(2,1)} %get-tuple-element.114), channel_id=1, source_target_pairs={{0,2},{1,3},{2,4},{3,5},{4,6},{5,7},{6,0},{7,1},{8,10},{9,11},{10,... | collective-permute-start | bytes 1032200 | tf_op jit(solution)/shard_map/ppermute | solution.py:631
  302.9 26.5 %collective-permute-start.41 = (bf16[224,768]{1,0:T(8,128)(2,1)}, bf16[224,768]{1,0:T(8,128)(2,1)S(1)}, u32[]{:S(2)}, u32[]{:S(2)}) collective-permute-start(bf16[224,768]{1,0:T(8,128)(2,1)} %get-tuple-element.115), channel_id=1, source_target_pairs={{0,4},{1,5},{2,6},{3,7},{4,0},{5,1},{6,2},{7,3},{8,12},{9,13},{10,... | collective-permute-start | bytes 1032200 | tf_op jit(solution)/shard_map/ppermute | solution.py:631
  302.9 27.1 %collective-permute-start.42 = (bf16[224,768]{1,0:T(8,128)(2,1)}, bf16[224,768]{1,0:T(8,128)(2,1)S(1)}, u32[]{:S(2)}, u32[]{:S(2)}) collective-permute-start(bf16[224,768]{1,0:T(8,128)(2,1)} %get-tuple-element.116), channel_id=1, source_target_pairs={{0,6},{1,7},{2,0},{3,1},{4,2},{5,3},{6,4},{7,5},{8,14},{9,15},{10,... | collective-permute-start | bytes 1032200 | tf_op jit(solution)/shard_map/ppermute | solution.py:631
  333.0 11.4 %collective-permute-start.43 = (bf16[224,768]{1,0:T(8,128)(2,1)}, bf16[224,768]{1,0:T(8,128)(2,1)S(1)}, u32[]{:S(2)}, u32[]{:S(2)}) collective-permute-start(bf16[224,768]{1,0:T(8,128)(2,1)} %fourth.1.own), channel_id=1, source_target_pairs={{0,8},{8,0},{16,24},{24,16},{1,9},{9,1},{17,25},{25,17},{2,10},{10... | collective-permute-start | bytes 1032200 | tf_op jit(solution)/shard_map/ppermute | solution.py:638
  335.4 15.6 %collective-permute-start.44 = (bf16[224,768]{1,0:T(8,128)(2,1)}, bf16[224,768]{1,0:T(8,128)(2,1)S(1)}, u32[]{:S(2)}, u32[]{:S(2)}) collective-permute-start(bf16[224,768]{1,0:T(8,128)(2,1)} %fourth.1.own), channel_id=1, source_target_pairs={{0,16},{8,24},{16,0},{24,8},{1,17},{9,25},{17,1},{25,9},{2,18},{10... | collective-permute-start | bytes 1032200 | tf_op jit(solution)/shard_map/ppermute | solution.py:638
  335.8 17.0 %collective-permute-start.45 = (bf16[224,768]{1,0:T(8,128)(2,1)}, bf16[224,768]{1,0:T(8,128)(2,1)S(1)}, u32[]{:S(2)}, u32[]{:S(2)}) collective-permute-start(bf16[224,768]{1,0:T(8,128)(2,1)} %fourth.1.own), channel_id=1, source_target_pairs={{0,24},{8,16},{16,8},{24,0},{1,25},{9,17},{17,9},{25,1},{2,26},{10... | collective-permute-start | bytes 1032200 | tf_op jit(solution)/shard_map/ppermute | solution.py:638
  (34 other events, 162.1 us)

commit v3 on v2

--- a/solution.py
+++ b/solution.py
@@ -50,10 +50,11 @@
     return jnp.where(rows == ids_row, 1.0, 0.0).astype(BF)
 
 
-def key_passes(total, size, score, weigh):
+def key_passes(total, size, score, weigh, blocks=None):
     count = total // size
     if count <= 4:
-        blocks = [score(index) for index in range(count)]
+        if blocks is None:
+            blocks = [score(index) for index in range(count)]
         peak = functools.reduce(jnp.maximum, [jnp.max(b, axis=0, keepdims=True) for b in blocks])
         denom, sums = 0.0, None
         for index in range(count):
@@ -113,13 +114,12 @@
     )
     heads, picks, clusters = top_ref.shape
     place = owner * rows + lax.broadcasted_iota(jnp.int32, (rows, clusters), 0)
-    outside = place >= info[2]
+    plain = jnp.where(place >= info[2], EXCLUDED, NEGATIVE)
     for head in range(heads):
         top = top_ref[head]
-        chosen = place == top[0:1, :]
-        for pick in range(1, picks):
-            chosen = chosen | (place == top[pick : pick + 1, :])
-        value = jnp.where(chosen, 0.0, jnp.where(outside, EXCLUDED, NEGATIVE))
+        value = plain
+        for pick in range(picks):
+            value = jnp.where(place == top[pick : pick + 1, :], 0.0, value)
         bias_ref[head] = value.astype(BF)
 
 
@@ -127,14 +127,14 @@
     parts = refs[:peers]
     gain_ref, shift_ref, w_ref = refs[peers : peers + 3]
     hat_ref, feat_ref, kv_ref = refs[peers + 3 + olds :]
-    rows = hat_ref.shape[0]
+    rows = hat_ref.shape[1]
     for peer in range(peers):
         values = parts[peer][...].astype(F32)
         centered = values - jnp.mean(values, axis=-1, keepdims=True)
         variance = jnp.mean(centered * centered, axis=-1, keepdims=True)
         scaled = centered * lax.rsqrt(variance + EPSILON) * gain_ref[...]
         if peer == 0:
-            hat_ref[...] = scaled.astype(BF)
+            hat_ref[...] = scaled.astype(BF).T
         low = (scaled + shift_ref[...]).astype(BF)
         found = nt(w_ref[0], low)
         heads, triple = feat_ref.shape[0], feat_ref.shape[1]
@@ -149,79 +149,73 @@
             kv_ref[head, spot, :] = pair.T
 
 
-def forward_kernel(ids_all, ids_own, feat_all, feat_own, kv, bias, *refs, size, groups):
+def forward_kernel(ids_all, feat, kv, bias, *refs, size, groups, rows):
     outs = refs[:groups]
-    mix_ref, stat_ref, cen_ref, table = refs[groups:]
-    hs = feat_own.shape[1] // 3
+    mix_ref, stat_ref, cen_ref = refs[groups:]
+    hs = feat.shape[1] // 3
     keys = kv.shape[1]
+    count = keys // size
     clusters = bias.shape[2]
     kv_h, bias_h = kv.at[0], bias.at[0]
-    qt_all, kvt = feat_all.at[0, :hs], feat_all.at[0, hs:]
-
-    @pl.when(pl.program_id(1) == 0)
-    def centroid_stage():
-        hot = one_hot_t(ids_all[0], clusters)
-        ones = jnp.ones((16, keys), BF)
-        sums = nt(jnp.concatenate([qt_all[...], ones], axis=0), hot)
-        counts = sums[hs : hs + 1]
-        centroid = (sums[:hs] / jnp.maximum(counts, 1.0)).astype(BF)
-        padded = jnp.concatenate([centroid, jnp.zeros_like(centroid)], axis=0)
-
-        def score(index):
-            scores = nn(piece(kv_h, index, size, 0), padded)
-            outside = piece(bias_h, index, size, 0).astype(F32) < 2.0 * NEGATIVE
-            return jnp.where(outside, NEGATIVE, scores)
-
-        def weigh(index, expo):
-            top = piece(bias_h, index, size, 0).astype(F32) == 0.0
-            mass = jnp.sum(jnp.where(top, expo, 0.0), axis=0, keepdims=True)
-            other = jnp.where(top, 0.0, expo).astype(BF)
-            return nn(piece(kvt, index, size, 1), other), mass
-
-        peak, denom, (rest, mass) = key_passes(keys, size, score, weigh)
-        rest = rest[hs:] / denom
-        mass = mass / denom
-        stats = jnp.concatenate(
-            [
-                rest,
-                mass,
-                peak + jnp.log(denom),
-                counts,
-                jnp.zeros((5, clusters), F32),
-            ],
-            axis=0,
-        )
-        stat_ref[0] = stats
-        cen_ref[0] = centroid
-        high, low = split_low(stats)
-        table[...] = jnp.concatenate([high, low], axis=1)
-
-    hot = one_hot_t(ids_own[0], clusters)
-    queries = feat_own[0, :hs]
-    side = jnp.concatenate([queries, jnp.zeros_like(queries), hot], axis=0)
-    gathered = nn(table[...], jnp.concatenate([hot, hot], axis=0))
-
-    def score(index):
-        return nn(
-            jnp.concatenate([piece(kv_h, index, size, 0), piece(bias_h, index, size, 0)], axis=1),
-            side,
-        )
-
-    def weigh(index, expo):
+    queries_all, kvt = feat.at[0, :hs], feat.at[0, hs:]
+    hot_all = one_hot_t(ids_all[0], clusters)
+    ones = jnp.ones((16, keys), BF)
+    sums = nt(jnp.concatenate([queries_all[...], ones], axis=0), hot_all)
+    counts = sums[hs : hs + 1]
+    centroid = (sums[:hs] / jnp.maximum(counts, 1.0)).astype(BF)
+    padded = jnp.concatenate([centroid, jnp.zeros_like(centroid)], axis=0)
+
+    def cluster_score(index):
+        scores = nn(piece(kv_h, index, size, 0), padded)
+        outside = piece(bias_h, index, size, 0).astype(F32) < 2.0 * NEGATIVE
+        return jnp.where(outside, NEGATIVE, scores)
+
+    def cluster_weigh(index, expo):
+        top = piece(bias_h, index, size, 0).astype(F32) == 0.0
+        mass = jnp.sum(jnp.where(top, expo, 0.0), axis=0, keepdims=True)
+        other = jnp.where(top, 0.0, expo).astype(BF)
+        return nn(piece(kvt, index, size, 1), other), mass
+
+    peers = keys // (groups * rows)
+    hots, sides = [], []
+    for group in range(groups):
+        spot = slice(group * peers * rows, group * peers * rows + rows)
+        hot = one_hot_t(ids_all[0, :, spot], clusters)
+        queries = queries_all[:, spot]
+        hots.append(hot)
+        sides.append(jnp.concatenate([queries, jnp.zeros_like(queries), hot], axis=0))
+
+    def member_score(group, index):
+        both = jnp.concatenate([piece(kv_h, index, size, 0), piece(bias_h, index, size, 0)], axis=1)
+        return nn(both, sides[group])
+
+    def member_weigh(index, expo):
         return (nn(piece(kvt, index, size, 1), expo.astype(BF)),)
 
-    peak, denom, (mix,) = key_passes(keys, size, score, weigh)
-    mix = mix[hs:] / denom
-    result = (gathered[hs : hs + 1] * mix + gathered[:hs]).astype(BF)
+    short = count <= 4
+    ahead = None
+    if short:
+        ahead = [member_score(0, index) for index in range(count)]
+    peak, denom, (rest, mass) = key_passes(keys, size, cluster_score, cluster_weigh)
+    rest = rest[hs:] / denom
+    mass = mass / denom
+    blank = jnp.zeros((5, clusters), F32)
+    stats = jnp.concatenate([rest, mass, peak + jnp.log(denom), counts, blank], axis=0)
+    stat_ref[0] = stats
+    cen_ref[0] = centroid
+    high, low = split_low(stats)
+    table = jnp.concatenate([high, low], axis=1)
     for group in range(groups):
-
-        @pl.when(pl.program_id(1) == group)
-        def store(group=group):
-            outs[group][...] = result
-
-    mix_ref[0, 0] = jnp.concatenate(
-        [mix, jnp.broadcast_to(peak + jnp.log(denom), (8, mix.shape[1]))], axis=0
-    )
+        gathered = nn(table, jnp.concatenate([hots[group], hots[group]], axis=0))
+        blocks, ahead = ahead, None
+        if short and group + 1 < groups:
+            ahead = [member_score(group + 1, index) for index in range(count)]
+        score = functools.partial(member_score, group)
+        peak, denom, (mix,) = key_passes(keys, size, score, member_weigh, blocks)
+        mix = mix[hs:] / denom
+        outs[group][...] = (gathered[hs : hs + 1] * mix + gathered[:hs]).astype(BF)
+        level = jnp.broadcast_to(peak + jnp.log(denom), (8, rows))
+        mix_ref[0, group] = jnp.concatenate([mix, level], axis=0)
 
 
 def sums_kernel(ids_own, *refs, groups):
@@ -241,61 +235,76 @@
     part_ref[0] = total
 
 
-def member_kernel(ids_own, feat_all, feat_own, kv, bias, *refs, size, groups):
+def member_kernel(ids_all, feat, kv, bias, *refs, size, groups):
     grads = refs[:groups]
-    mix_ref, stat_ref, dq_ref, own_ref, send_ref, total, picked = refs[groups:]
-    hs, rows = picked.shape
+    mix_ref, stat_ref, dq_ref, own_ref, send_ref, total = refs[groups:]
+    hs, rows = grads[0].shape
     keys = kv.shape[1]
+    count = keys // size
+    peers = keys // (groups * rows)
     clusters = bias.shape[2]
-    block = pl.program_id(1)
+    kv_h, bias_h = kv.at[0], bias.at[0]
+    queries_all, kvt = feat.at[0, :hs], feat.at[0, hs:]
+    high, low = split_low(stat_ref[0, hs : hs + 8, :])
+    table = jnp.concatenate([high, low], axis=1)
+    sides, levels, deltas, pads, rights = [], [], [], [], []
     for group in range(groups):
-
-        @pl.when(block == group)
-        def pick(group=group):
-            picked[...] = grads[group][...]
-
-    kv_h, bias_h, kvt = kv.at[0], bias.at[0], feat_all.at[0, hs:]
-    hot = one_hot_t(ids_own[0], clusters)
-    queries = feat_own[0, :hs]
-    blank = jnp.zeros_like(queries)
-    side = jnp.concatenate([queries, blank, hot], axis=0)
-    high, low = split_low(stat_ref[0, hs : hs + 8, :])
-    mass = nn(jnp.concatenate([high, low], axis=1), jnp.concatenate([hot, hot], axis=0))[0:1]
-    mix = mix_ref[0, 0, :hs]
-    level = mix_ref[0, 0, hs : hs + 1]
-    back = (mass * picked[...].astype(F32)).astype(BF)
-    delta = jnp.sum(back.astype(F32) * mix, axis=0, keepdims=True)
-    back_pad = jnp.concatenate([blank, back], axis=0)
-    right = jnp.concatenate([jnp.concatenate([queries, blank], axis=0), back_pad], axis=1).T
-
-    @pl.when(block == 0)
-    def clear():
-        total[...] = jnp.zeros_like(total)
-
-    def step(index, dq):
+        spot = slice(group * peers * rows, group * peers * rows + rows)
+        hot = one_hot_t(ids_all[0, :, spot], clusters)
+        queries = queries_all[:, spot]
+        blank = jnp.zeros_like(queries)
+        sides.append(jnp.concatenate([queries, blank, hot], axis=0))
+        mass = nn(table, jnp.concatenate([hot, hot], axis=0))[0:1]
+        back = (mass * grads[group][...].astype(F32)).astype(BF)
+        levels.append(mix_ref[0, group, hs : hs + 1])
+        deltas.append(jnp.sum(back.astype(F32) * mix_ref[0, group, :hs], axis=0, keepdims=True))
+        pads.append(jnp.concatenate([blank, back], axis=0))
+        turned = jnp.concatenate([queries, blank], axis=0)
+        rights.append(jnp.concatenate([turned, pads[group]], axis=1).T)
+
+    def scores(group, index):
         kv_c = piece(kv_h, index, size, 0)
-        scores = nn(jnp.concatenate([kv_c, piece(bias_h, index, size, 0)], axis=1), side)
-        weights = jnp.exp(scores - level)
-        grad_w = nn(kv_c, back_pad)
-        grad_s = (weights * (grad_w - delta)).astype(BF)
+        both = jnp.concatenate([kv_c, piece(bias_h, index, size, 0)], axis=1)
+        return nn(both, sides[group]), nn(kv_c, pads[group])
+
+    def finish(group, index, found, dq):
+        weights = jnp.exp(found[0] - levels[group])
+        grad_s = (weights * (found[1] - deltas[group])).astype(BF)
+        part = nn(jnp.concatenate([grad_s, weights.astype(BF)], axis=1), rights[group])
         spot = spot_of(index, size)
-        total[spot, :] += nn(jnp.concatenate([grad_s, weights.astype(BF)], axis=1), right)
+        if group == 0:
+            total[spot, :] = part
+        else:
+            total[spot, :] += part
         return dq + nn(piece(kvt, index, size, 1), grad_s)
 
-    dq = key_sum(keys, size, step, jnp.zeros((2 * hs, rows), F32))
-    dq_ref[0] = dq[:hs] * 0.125
-
-    @pl.when(block == groups - 1)
-    def finish():
-        peers = keys // own_ref.shape[1]
+    start = jnp.zeros((2 * hs, rows), F32)
+    if count <= 4:
+        tasks = [(group, index) for group in range(groups) for index in range(count)]
+        ahead = scores(*tasks[0])
+        dq = start
+        for step, (group, index) in enumerate(tasks):
+            found = ahead
+            if step + 1 < len(tasks):
+                ahead = scores(*tasks[step + 1])
+            dq = finish(group, index, found, dq)
+            if index == count - 1:
+                dq_ref[group] = dq[:hs] * 0.125
+                dq = start
+    else:
         for group in range(groups):
-            base = group * peers * rows
-            own_ref[0, group * rows : (group + 1) * rows, :] = total[base : base + rows, :]
-            for peer in range(1, peers):
-                spot = (peer - 1) * groups * rows + group * rows
-                send_ref[0, spot : spot + rows, :] = total[
-                    base + peer * rows : base + (peer + 1) * rows, :
-                ].astype(BF)
+
+            def step(index, dq, group=group):
+                return finish(group, index, scores(group, index), dq)
+
+            dq_ref[group] = lax.fori_loop(0, count, step, start)[:hs] * 0.125
+    for group in range(groups):
+        base = group * peers * rows
+        own_ref[0, group * rows : (group + 1) * rows, :] = total[base : base + rows, :]
+        for peer in range(1, peers):
+            spot = (peer - 1) * groups * rows + group * rows
+            found = total[base + peer * rows : base + (peer + 1) * rows, :]
+            send_ref[0, spot : spot + rows, :] = found.astype(BF)
 
 
 def centroid_kernel(ids_own, feat_all, kv, bias, part_ref, stat_ref, cen_ref, dqm_ref, own_ref, *refs, size, groups, gots):
@@ -540,11 +549,10 @@
     for group in range(groups):
         order = [parts[group][h, k * hs : (k + 1) * hs] for k in range(3) for h in range(heads)]
         turned = jnp.concatenate(order, axis=0)
-        found = nn(turned, hat_ref[group * rows : (group + 1) * rows, :])
+        found = nt(hat_ref[:, group * rows : (group + 1) * rows], turned)
         more = nt(ones, turned)
         total = found if total is None else total + found
         sums = more if sums is None else sums + more
-    total = total.T
     if not fast:
         outs[0][...] = total
         outs[1][...] = sums
@@ -654,6 +662,9 @@
             name=name,
         )
 
+    def after(values, *others):
+        return lax.optimization_barrier((values, others))[0]
+
     def array(shape, dtype):
         return jax.ShapeDtypeStruct(shape, dtype)
 
@@ -666,6 +677,15 @@
         return lax.dynamic_index_in_dim(packed, (group_at + groups - hop) % groups, keepdims=False)
 
     arrived = [of_heads(0)] + [along_groups(of_heads(hop), -hop) for hop in range(1, groups)]
+
+    ready = after(tokens, packed)
+    mine = {0: tokens, 1: along_groups(ready, -1)}
+    if groups > 2:
+        mine[groups - 1] = along_groups(ready, 1)
+    for hop in range(2, groups - 1):
+        ready = after(tokens, mine[1], mine[groups - 1])
+        mine[hop] = along_groups(ready, -hop)
+
     arrived = jnp.stack(arrived)
     arrived = jnp.stack([arrived] + [along_peers(arrived, -hop) for hop in range(1, peers)], axis=1)
     ids_all = arrived[..., :rows].transpose(2, 0, 1, 3).reshape(own_heads, 1, seq)
@@ -676,15 +696,13 @@
     top_all = lax.dynamic_slice_in_dim(top_all, (peers - peer_at) % peers, peers, axis=1)
     top_all = top_all.transpose(2, 4, 0, 1, 3).reshape(own_heads, picks, clusters)
 
-    mine = [tokens] + [along_groups(tokens, -hop) for hop in range(1, groups)]
-
     bias = prefetched(
         functools.partial(bias_kernel, groups=groups, peers=peers, rows=rows),
         (wide,),
         [whole((own_heads, picks, clusters))],
         pl.BlockSpec((own_heads, rows, clusters), lambda i, s: (0, i, 0)),
         array((own_heads, seq, clusters), BF),
-        60,
+        8 if fast else 60,
         cost(own_heads * seq * clusters * picks * 8, own_heads * seq * clusters * 2),
         "bias",
     )(info, top_all)
@@ -693,13 +711,13 @@
     w_in = w_in.transpose(1, 0, 2, 3).reshape(groups, 3 * feats, width)
     gain_row, shift_row = gain_one[None, :], shift_one[None, :]
     shapes = [
-        array((groups * rows, width), BF),
+        array((width, groups * rows), BF),
         array((own_heads, 3 * hs, seq), BF),
         array((own_heads, seq, 2 * hs), BF),
     ]
     held = []
     split_peers = peers if peers <= 2 else 1
-    for group in range(groups):
+    for group in sorted(range(groups), key=lambda g: min(g, groups - g)):
         chunk = [mine[group]] + [along_peers(mine[group], -hop) for hop in range(1, peers)]
         if peers > 2:
             chunk = [jnp.concatenate(chunk, axis=0)]
@@ -708,7 +726,7 @@
             specs_in = [pl.BlockSpec((rows, width), lambda p, s: (p, 0))]
             grid = (peers,)
             outs = [
-                pl.BlockSpec((rows, width), lambda p, s, g=group: (g, 0)),
+                pl.BlockSpec((width, rows), lambda p, s, g=group: (0, g)),
                 pl.BlockSpec((own_heads, 3 * hs, rows), lambda p, s, g=group: (0, 0, g * peers + p)),
                 pl.BlockSpec((own_heads, rows, 2 * hs), lambda p, s, g=group: (0, g * peers + p, 0)),
             ]
@@ -716,7 +734,7 @@
             specs_in = [whole((rows, width))] * split_peers
             grid = (1,)
             outs = [
-                pl.BlockSpec((rows, width), lambda p, s, g=group: (g, 0)),
+                pl.BlockSpec((width, rows), lambda p, s, g=group: (0, g)),
                 pl.BlockSpec((own_heads, 3 * hs, span), lambda p, s, g=group: (0, 0, g)),
                 pl.BlockSpec((own_heads, span, 2 * hs), lambda p, s, g=group: (0, g, 0)),
             ]
@@ -733,7 +751,7 @@
             + [pl.BlockSpec(memory_space=pl.ANY)] * len(held),
             outs,
             shapes,
-            60,
+            16 if fast else 60,
             cost(6 * span * width * feats, span * width * 4),
             "project",
             alias={first + k: k for k in range(len(held))},
@@ -741,9 +759,7 @@
     hat_own, feat, kv = held
 
     ids_full = pl.BlockSpec((1, 1, seq), lambda h, r: (h, 0, 0))
-    ids_block = pl.BlockSpec((1, 1, rows), lambda h, r: (h, 0, r * peers))
     feat_full = pl.BlockSpec((1, 3 * hs, seq), lambda h, r: (h, 0, 0))
-    feat_block = pl.BlockSpec((1, 3 * hs, rows), lambda h, r: (h, 0, r * peers))
     kv_full = pl.BlockSpec((1, seq, 2 * hs), lambda h, r: (h, 0, 0))
     bias_full = pl.BlockSpec((1, seq, clusters), lambda h, r: (h, 0, 0))
     head_rows = pl.BlockSpec((hs, rows), lambda h, r: (h, 0))
@@ -753,22 +769,30 @@
     own_rows = groups * rows
     pair_flops = own_heads * own_rows * seq * 256
 
+    one = [
+        pl.BlockSpec(spec.block_shape, functools.partial(lambda h, f: f(h, 0), f=spec.index_map))
+        for spec in (ids_full, feat_full, kv_full, bias_full, stat_spec, cen_spec, head_rows)
+    ]
+    ids_one, feat_one, kv_one, bias_one, stat_one, cen_one, rows_one = one
+    part_one = pl.BlockSpec((1, hs + 16, clusters), lambda h: (h, 0, 0))
+    mix_one = pl.BlockSpec((1, groups, hs + 8, rows), lambda h: (h, 0, 0, 0))
+    all_groups = pl.BlockSpec((groups, hs, rows), lambda h: (0, h, 0))
+    own_one = pl.BlockSpec((1, own_rows, 2 * hs), lambda h: (h, 0, 0))
     results = pl.pallas_call(
-        functools.partial(forward_kernel, size=size, groups=groups),
-        grid=(own_heads, groups),
-        in_specs=[ids_full, ids_block, feat_full, feat_block, kv_full, bias_full],
-        out_specs=[head_rows] * groups + [mix_spec, stat_spec, cen_spec],
+        functools.partial(forward_kernel, size=size, groups=groups, rows=rows),
+        grid=(own_heads,),
+        in_specs=[ids_one, feat_one, kv_one, bias_one],
+        out_specs=[rows_one] * groups + [mix_one, stat_one, cen_one],
         out_shape=[array((feats, rows), BF)] * groups
         + [
             array((own_heads, groups, hs + 8, rows), F32),
             array((own_heads, hs + 8, clusters), F32),
             array((own_heads, hs, clusters), BF),
         ],
-        scratch_shapes=[pltpu.VMEM((hs + 8, 2 * clusters), BF)],
-        compiler_params=params(60, 2),
+        compiler_params=params(32 if fast else 60, 1),
         cost_estimate=cost(6 * pair_flops, 8e6, own_heads * own_rows * seq),
         name="attend",
-    )(ids_all, ids_all, feat, feat, kv, bias)
+    )(ids_all, feat, kv, bias)
     attn_t = results[:groups]
     mixed, stats, centroid = results[groups:]
 
@@ -812,7 +836,7 @@
         ]
         + kept
         + [array((feats, rows), BF)] * groups,
-        60,
+        28 if fast else 60,
         cost(8 * rows * width * hidden, 4 * width * hidden, rows * hidden),
         "feed",
         scratch=[
@@ -827,30 +851,7 @@
     kept, d_attn = results[5:-groups], results[-groups:]
     grads = [d_attn[0]] + [along_groups(d_attn[hop], -hop) for hop in range(1, groups)]
 
-    one = [
-        pl.BlockSpec(spec.block_shape, functools.partial(lambda h, f: f(h, 0), f=spec.index_map))
-        for spec in (ids_full, feat_full, kv_full, bias_full, stat_spec, cen_spec, head_rows)
-    ]
-    ids_one, feat_one, kv_one, bias_one, stat_one, cen_one, rows_one = one
-    part_one = pl.BlockSpec((1, hs + 16, clusters), lambda h: (h, 0, 0))
-    all_groups = pl.BlockSpec((groups, hs, rows), lambda h: (0, h, 0))
-    own_one = pl.BlockSpec((1, own_rows, 2 * hs), lambda h: (h, 0, 0))
-
-    share = pl.pallas_call(
-        functools.partial(sums_kernel, groups=groups),
-        grid=(own_heads,),
-        in_specs=[ids_one]
-        + [rows_one] * groups
-        + [pl.BlockSpec((1, groups, hs + 8, rows), lambda h: (h, 0, 0, 0))],
-        out_specs=part_one,
-        out_shape=array((own_heads, hs + 16, clusters), F32),
-        compiler_params=params(60, 1),
-        cost_estimate=cost(own_heads * own_rows * clusters * 160, 2e6),
-        name="sums",
-    )(ids_all, *grads, mixed)
-    share_got = [along_peers(share, hop) for hop in range(1, peers)]
-
-    def weight_sums():
+    def weight_parts():
         dup_got, dbr_got = along_peers(d_up, 1), along_peers(d_branch, 1)
         act_own, low_own, act_far, low_far = kept
         act_got, low_got = along_peers(act_far, 1), along_peers(low_far, 1)
@@ -873,7 +874,7 @@
                 whole(shape_d),
             ],
             [array(shape_u, BF), array(shape_u, BF), array(shape_d, BF), array(shape_d, BF)],
-            60,
+            28,
             cost(8 * rows * width * hidden, 6 * width * hidden),
             "weights",
             scratch=[pltpu.VMEM((groups, block_rows, width), F32)],
@@ -881,7 +882,11 @@
             info, d_up, dup_got, d_branch, dbr_got, act_own, act_got, low_own, low_got,
             cotangent, cot_got, norm_two, dn_got,
         )
-        got_u, got_d = along_dp(send_u, 1), along_dp(send_d, 2)
+        return send_u, keep_u, send_d, keep_d
+
+    def weight_sums(keep_u, got_u, keep_d, got_d):
+        high = block_rows + block_rows // 4 + 8
+        shape_u, shape_d = keep_u.shape, keep_d.shape
 
         def block(shape, at):
             return pl.BlockSpec((1,) + shape[1:], lambda i: (at, 0, 0, 0))
@@ -892,7 +897,7 @@
             in_specs=[block(shape_u, 1), block(shape_u, 1), block(shape_d, 1), block(shape_d, 1)],
             out_specs=[whole(shape_u[1:]), whole(shape_d[1:])],
             out_shape=[array(shape_u[1:], BF), array(shape_d[1:], BF)],
-            compiler_params=params(60, 1),
+            compiler_params=params(20, 1),
             cost_estimate=cost(groups * high * width * 2, groups * high * width * 12),
             name="second",
         )(keep_u, got_u, keep_d, got_d)
@@ -911,7 +916,7 @@
             ],
             out_specs=[whole((tall, width))] * groups,
             out_shape=[array((tall, width), BF)] * groups,
-            compiler_params=params(60, 1),
+            compiler_params=params(24, 1),
             cost_estimate=cost(groups * tall * width * 4, groups * tall * width * 8),
             name="third",
         )(keep_u, got_u, last_u, keep_d, got_d, last_d)
@@ -922,7 +927,7 @@
             in_specs=[whole((tall, width))] * groups,
             out_specs=whole((tall, width)),
             out_shape=array((tall, width), BF),
-            compiler_params=params(60, 1),
+            compiler_params=params(12, 1),
             cost_estimate=cost(groups * tall * width, groups * tall * width * 2),
             name="fourth",
         )(*came)
@@ -944,7 +949,7 @@
                 array((hidden // wide, width), F32),
                 array((8, width), F32),
             ],
-            60,
+            16,
             cost(1e6, 4 * tall * width * 6),
             "spread",
         )(info, done, from_x, from_y, from_xy)
@@ -977,7 +982,9 @@
         return done
 
     if fast:
-        total_up, total_out, total_down, norm_own = weight_sums()
+        send_u, keep_u, send_d, keep_d = weight_parts()
+        got_u, got_d = along_dp(send_u, 1), along_dp(send_d, 2)
+        grads = after(grads, keep_u)
     else:
         act, normed_two = kept
         total_up = reduce_rows(tn(normed_two, d_up).astype(BF))
@@ -990,27 +997,42 @@
         total_out = reduce_rows(jnp.concatenate(found, axis=0))
         norm_own = reduce_rows(norm_two[:2].T.astype(BF)).T
 
+    share = pl.pallas_call(
+        functools.partial(sums_kernel, groups=groups),
+        grid=(own_heads,),
+        in_specs=[ids_one]
+        + [rows_one] * groups
+        + [mix_one],
+        out_specs=part_one,
+        out_shape=array((own_heads, hs + 16, clusters), F32),
+        compiler_params=params(16 if fast else 60, 1),
+        cost_estimate=cost(own_heads * own_rows * clusters * 160, 2e6),
+        name="sums",
+    )(ids_all, *grads, mixed)
+    share_got = [along_peers(share, hop) for hop in range(1, peers)]
+
+    grads = after(grads, share)
     dq_member, dkv_own, dkv_send = pl.pallas_call(
         functools.partial(member_kernel, size=size, groups=groups),
-        grid=(own_heads, groups),
-        in_specs=[ids_block, feat_full, feat_block, kv_full, bias_full]
-        + [head_rows] * groups
-        + [mix_spec, stat_spec],
+        grid=(own_heads,),
+        in_specs=[ids_one, feat_one, kv_one, bias_one]
+        + [rows_one] * groups
+        + [mix_one, stat_one],
         out_specs=[
-            pl.BlockSpec((1, hs, rows), lambda h, r: (r, h, 0)),
-            pl.BlockSpec((1, own_rows, 2 * hs), lambda h, r: (h, 0, 0)),
-            pl.BlockSpec((1, max(peers - 1, 1) * own_rows, 2 * hs), lambda h, r: (h, 0, 0)),
+            all_groups,
+            own_one,
+            pl.BlockSpec((1, max(peers - 1, 1) * own_rows, 2 * hs), lambda h: (h, 0, 0)),
         ],
         out_shape=[
             array((groups, feats, rows), F32),
             array((own_heads, own_rows, 2 * hs), F32),
             array((own_heads, max(peers - 1, 1) * own_rows, 2 * hs), BF),
         ],
-        scratch_shapes=[pltpu.VMEM((seq, 2 * hs), F32), pltpu.VMEM((hs, rows), BF)],
-        compiler_params=params(60, 2),
+        scratch_shapes=[pltpu.VMEM((seq, 2 * hs), F32)],
+        compiler_params=params(32 if fast else 60, 1),
         cost_estimate=cost(12 * pair_flops, 10e6, own_heads * own_rows * seq),
         name="member",
-    )(ids_all, feat, feat, kv, bias, *grads, mixed, stats)
+    )(ids_all, feat, kv, bias, *grads, mixed, stats)
     dkv_got = [
         along_peers(
             dkv_send if peers == 2 else dkv_send[:, (hop - 1) * own_rows : hop * own_rows], hop
@@ -1029,7 +1051,7 @@
         out_specs=[pl.BlockSpec((1, 3 * hs, rows), lambda h: (h, 0, 0))] * groups,
         out_shape=[array((own_heads, 3 * hs, rows), BF)] * groups,
         scratch_shapes=[pltpu.VMEM((seq, 2 * clusters), BF)],
-        compiler_params=params(60, 1),
+        compiler_params=params(28 if fast else 60, 1),
         cost_estimate=cost(own_heads * clusters * seq * 1024, 8e6, own_heads * clusters * seq),
         name="centroid",
     )(ids_all, feat, kv, bias, share_total, stats, centroid, dq_member, dkv_own, *dkv_got)
@@ -1037,7 +1059,7 @@
     home = [d_in[0]] + [along_groups(d_in[hop], hop) for hop in range(1, groups)]
 
     tall = block_rows + 16
-    part_spec = [whole((own_heads, 3 * hs, rows))] * groups + [whole((own_rows, width))]
+    part_spec = [whole((own_heads, 3 * hs, rows))] * groups + [whole((width, own_rows))]
     inward = functools.partial(
         prefetched,
         functools.partial(inward_kernel, groups=groups, fast=fast),
@@ -1049,11 +1071,14 @@
         half = groups // 2
         blocks = (groups, tall, 3 * feats)
         keep, far = inward(
-            [whole(blocks)] * 2, [array(blocks, BF)] * 2, 60, spent, "inward"
+            [whole(blocks)] * 2, [array(blocks, BF)] * 2, 24, spent, "inward"
         )(info, *d_in, hat_own)
         got = along_peers(far, 1)
         total = keep.astype(F32) + got.astype(F32)
         one_half, two_half = total[:half].astype(BF), total[half:].astype(BF)
+        total_up, total_out, total_down, norm_own = weight_sums(
+            keep_u, after(got_u, keep), keep_d, after(got_d, keep)
+        )
         for mask in (1, 2):
             got_one, got_two = along_dp(one_half, mask), along_dp(two_half, 3 - mask)
             one_half = (one_half.astype(F32) + got_one.astype(F32)).astype(BF)
@@ -1095,7 +1120,7 @@
         + [square, square, whole((1, width)), whole((groups, 3 * feats, width))],
         square,
         array((rows, width), BF),
-        60,
+        24 if fast else 60,
         cost(6 * rows * width * width, 6 * width * width),
         "final",
     )(info, *home, tokens, d_resid, gain_row, w_in)

time: 360 us -> 312 us (0.87)
  Pallas kernels: 138 us -> 87.4 us
  local copies, waits for them, and re-layouts: 28.5 us -> 35.5 us
  waiting for transfers between devices: 131 us -> 124 us
    pallas_call x1, Pallas kernels: 22.5 us -> 13.4 us  [per_device(): pl.pallas_call(functools.partial(forward_kernel, size=size, groups=groups...]
    pallas_call x1, Pallas kernels: 25.2 us -> 17 us  [per_device(): pl.pallas_call(functools.partial(member_kernel, size=size, groups=groups)...]
    pallas_call x1, Pallas kernels: 15 us -> 7.43 us  [per_device(): prefetched(functools.partial(bias_kernel, groups=groups, peers=peers, row...]
    ppermute x11, waiting for transfers between devices: 58.1 us -> 51.8 us  [along_dp(): return lax.ppermute(values, 'dp', [(i, i ^ mask) for i in range(n_dp)])]
    pallas_call x2, Pallas kernels: 15.9 us -> 10.2 us  [the longest x1 6.99 us: weight_parts(): prefetched(functools.partial(weights_kernel, groups=groups), (4,), [chunk...]
    pallas_call x4, Pallas kernels: 16.6 us -> 11.4 us  [per_device(): prefetched(functools.partial(project_kernel, peers=split_peers, olds=len(...]
    ppermute x21, waiting for transfers between devices: 70.7 us -> 65.5 us  [along_groups(): return lax.ppermute(values, 'wide', pairs)]
    ppermute x14, waiting for transfers between devices: 2.5 us -> 7.04 us  [along_peers(): return lax.ppermute(values, 'wide', pairs)]
  transfers between devices with their start and end apart: 46 -> 46, of which waited for: 21 -> 18; matrix products, arithmetic and copies ran while one was open for 8% -> 12% of each run, Pallas kernels for 14% -> 9%
where the time goes in v3:
time: 312 us; the launch traced here: 311 us
  waiting for transfers between devices  124 us (40%)
  Pallas kernels  87.4 us (28%)
  starting transfers between devices  46.6 us (15%)
  local copies, waits for them, and re-layouts  35.5 us (11%)
  other arithmetic  15.3 us (5%)
    ppermute x21, waiting for transfers between devices, along_groups(): return lax.ppermute(values, 'wide', pairs)  65.5 us
    ppermute x11, waiting for transfers between devices, along_dp(): return lax.ppermute(values, 'dp', [(i, i ^ mask) for i in range(n_dp)])  51.8 us
    ppermute x21, starting transfers between devices, along_groups(): return lax.ppermute(values, 'wide', pairs)  29.9 us
    pallas_call x1, Pallas kernels, per_device(): pl.pallas_call(functools.partial(member_kernel, size=size, groups=groups)...  17 us
    unnamed x87, local copies, waits for them, and re-layouts  15.7 us
    ppermute x11, starting transfers between devices, along_dp(): return lax.ppermute(values, 'dp', [(i, i ^ mask) for i in range(n_dp)])  14.1 us
    pallas_call x1, Pallas kernels, per_device(): pl.pallas_call(functools.partial(forward_kernel, size=size, groups=groups...  13.4 us
    pallas_call x4, Pallas kernels, per_device(): prefetched(functools.partial(project_kernel, peers=split_peers, olds=len(...  11.4 us
  transfers between devices with their start and end apart: 46, of which 18 were waited for; matrix products, arithmetic and copies ran while one was open for 12% of the time, Pallas kernels for 9%

profile of v3, /device:TPU:8, one launch (start us, length us, event | category | flops | bytes accessed | tf_op | source)
XLA Modules:
  0.0 311.1 jit_solution(14124900557639759832)
XLA Ops:
  3.1 2.0 collective-permute-start.5
  5.2 4.5 %collective-permute-start.1 = (s32[3,768]{1,0:T(4,128)S(1)}, s32[3,768]{1,0:T(4,128)S(1)}, u32[]{:S(2)}, u32[]{:S(2)}) collective-permute-start(s32[3,768]{1,0:T(4,128)S(1)} %get-tuple-element.167), channel_id=1, source_target_pairs={{0,4},{1,5},{2,6},{3,7},{4,0},{5,1},{6,2},{7,3},{8,12},{9,13},{10,... | collective-permute-start | bytes 27656 | tf_op jit(solution)/shard_map/ppermute | solution.py:639
  9.6 2.0 collective-permute-start
  11.6 2.8 copy.53
  14.5 2.4 copy.52
  16.9 7.3 %collective-permute-done.1 = s32[3,768]{1,0:T(4,128)S(1)} collective-permute-done((s32[3,768]{1,0:T(4,128)S(1)}, s32[3,768]{1,0:T(4,128)S(1)}, u32[]{:S(2)}, u32[]{:S(2)}) %collective-permute-start.1) | collective-permute-done | bytes 9248 | tf_op jit(solution)/shard_map/ppermute | solution.py:639
  26.0 2.6 collective-permute-start.6
  28.6 3.3 %pad_maximum_fusion = bf16[768,2304]{0,1:T(8,128)(2,1)} fusion(bf16[768,1536]{0,1:T(8,128)(2,1)S(1)} %copy.53, bf16[768,768]{0,1:T(8,128)(2,1)} %copy.52), kind=kLoop, calls=%fused_computation | loop fusion | flops 7077888 | bytes 7077888 | tf_op jit(solution)/shard_map/concatenate | solution.py:710
  31.9 2.3 copy.54
  35.8 1.6 reshape.64
  37.9 8.2 %collective-permute-done.6.refs_0_ = bf16[256,768]{1,0:T(8,128)(2,1)} collective-permute-done((bf16[256,768]{1,0:T(8,128)(2,1)}, bf16[256,768]{1,0:T(8,128)(2,1)}, u32[]{:S(2)}, u32[]{:S(2)}) %collective-permute-start.6) | collective-permute-done | bytes 393248 | tf_op jit(solution)/shard_map/ppermute | solution.py:639
  47.9 1.7 copy.57.top_ref
  53.1 7.4 %bias.1 = bf16[3,2048,128]{2,1,0:T(8,128)(2,1)S(1)} custom-call(s32[6]{0:T(128)S(1)} %stack.64.info, s32[3,32,128]{2,1,0:T(8,128)S(1)} %copy-done.21), custom_call_target="tpu_custom_call" | custom-call | flops 201326592 | bytes 1572864 | tf_op jit(solution)/shard_map/bias/pallas_call | solution.py:699
  60.6 2.8 project.4
  63.5 2.7 project.5
  66.2 2.7 project.6
  69.0 3.1 project.7
  72.1 13.4 %attend.1 = (bf16[192,256]{1,0:T(8,128)(2,1)S(1)}, bf16[192,256]{1,0:T(8,128)(2,1)S(1)}, bf16[192,256]{1,0:T(8,128)(2,1)S(1)}, bf16[192,256]{1,0:T(8,128)(2,1)S(...) custom-call(s32[3,1,2048]{2,1,0:T(1,128)S(1)} %copy-done.20, ...), custom_call_target="tpu_custom_call" | custom-call | flops 9663676416 | bytes 8000000 | tf_op jit(solution)/shard_map/attend/pallas_call | solution.py:781
  85.6 3.8 %collective-permute-start.12 = (bf16[192,256]{1,0:T(8,128)(2,1)S(1)}, bf16[192,256]{1,0:T(8,128)(2,1)S(1)}, u32[]{:S(2)}, u32[]{:S(2)}) collective-permute-start(bf16[192,256]{1,0:T(8,128)(2,1)S(1)} %get-tuple-element.93), channel_id=1, source_target_pairs={{0,4},{1,5},{2,6},{3,7},{4,0},{5,1},{6,2},{7,3},{8,12},{9,13},{10,... | collective-permute-start | bytes 294920 | tf_op jit(solution)/shard_map/ppermute | solution.py:639
  91.1 5.0 %collective-permute-done.12.refs_2_ = bf16[192,256]{1,0:T(8,128)(2,1)S(1)} collective-permute-done((bf16[192,256]{1,0:T(8,128)(2,1)S(1)}, bf16[192,256]{1,0:T(8,128)(2,1)S(1)}, u32[]{:S(2)}, u32[]{:S(2)}) %collective-permute-start.12) | collective-permute-done | bytes 98336 | tf_op jit(solution)/shard_map/ppermute | solution.py:639
  96.1 2.8 collective-permute-done.13.refs_3_
  99.0 11.3 %feed.1 = (bf16[256,768]{1,0:T(8,128)(2,1)}, f32[256,768]{1,0:T(8,128)S(1)}, f32[8,768]{1,0:T(8,128)S(1)}, bf16[256,3072]{1,0:T(8,128)(2,1)S(1)}, bf16[256,768]{...) custom-call(s32[6]{0:T(128)S(1)} %stack.64.info, ...), custom_call_target="tpu_custom_call" | custom-call | flops 4831838208 | bytes 9437184 | tf_op jit(solution)/shard_map/feed/pallas_call | solution.py:816
  111.4 4.0 %collective-permute-done.21.refs_9_ = bf16[256,768]{1,0:T(8,128)(2,1)S(1)} collective-permute-done((bf16[256,768]{1,0:T(8,128)(2,1)S(1)}, bf16[256,768]{1,0:T(8,128)(2,1)S(1)}, u32[]{:S(2)}, u32[]{:S(2)}) %collective-permute-start.21) | collective-permute-done | bytes 393248 | tf_op jit(solution)/shard_map/ppermute | solution.py:643
  117.7 2.5 collective-permute-start.16
  120.1 7.0 %weights.1 = (bf16[2,4,128,768]{3,2,1,0:T(8,128)(2,1)S(1)}, bf16[2,4,128,768]{3,2,1,0:T(8,128)(2,1)S(1)}, bf16[2,4,96,768]{3,2,1,0:T(8,128)(2,1)S(1)}, bf16[2,4,96,768]{3,2,1,0:T(8,128)(2,1)S(1)}) custom-call(s32[6]{0:T(128)S(1)} %stack.64.info, bf16[256,3072]{1,0:T(8,128)(2,1)S(1)} %get-tuple-element.100.refs_0_, ...), custom_call_target="tpu_custom_call" | custom-call | flops 4831838208 | bytes 14155776 | tf_op jit(solution)/shard_map/weights/pallas_call | solution.py:865
  128.0 17.0 %member.1 = (f32[4,192,256]{2,1,0:T(8,128)S(1)}, f32[3,1024,128]{2,1,0:T(8,128)S(1)}, bf16[3,1024,128]{2,1,0:T(8,128)(2,1)S(1)}) custom-call(s32[3,1,2048]{2,1,0:T(1,128)S(1)} %copy-done.20, bf16[3,192,2048]{2,1,0:T(8,128)(2,1)S(1)} %get-tuple-element.89.feat.feat_all, bf16[3,2048,128]{2,1,0:T(8,128)(2,1)S(1)} %get-tuple-element.90.kv, ...), custom_call_target="tpu_custom_call" | custom-call | flops 19327352832 | bytes 10000000 | tf_op jit(solution)/shard_map/member/pallas_call | solution.py:1015
  145.6 1.9 collective-permute-done.23
  147.6 5.3 %centroid.1 = (bf16[3,192,256]{2,1,0:T(8,128)(2,1)S(1)}, bf16[3,192,256]{2,1,0:T(8,128)(2,1)S(1)}, bf16[3,192,256]{2,1,0:T(8,128)(2,1)S(1)}, bf16[3,192,256]{2,1,0:T(8,128)(2,1)}) custom-call(s32[3,1,2048]{2,1,0:T(1,128)S(1)} %copy-done.20, bf16[3,192,2048]{2,1,0:T(8,128)(2,1)S(1)} %get-tuple-element.89.feat.feat_all, ...), custom_call_target="tpu_custom_call" | custom-call | flops 805306368 | bytes 8000000 | tf_op jit(solution)/shard_map/centroid/pallas_call | solution.py:1046
  152.9 3.2 %inward.1 = (bf16[4,112,576]{2,1,0:T(8,128)(2,1)S(1)}, bf16[4,112,576]{2,1,0:T(8,128)(2,1)S(1)}) custom-call(s32[6]{0:T(128)S(1)} %stack.64.info, bf16[3,192,256]{2,1,0:T(8,128)(2,1)S(1)} %get-tuple-element.122.refs_0_, bf16[3,192,256]{2,1,0:T(8,128)(2,1)S(1)} %get-tuple-element.123.refs_1_, bf16[3,192,256]{2,1,0:T(8,128)(2,1)S(1)} %get-tuple-element.124.refs_2_, ...), custom_call_target="tpu_custom_call" | custom-call | flops 905969664 | bytes 4000000 | tf_op jit(solution)/shard_map/inward/pallas_call | solution.py:1073
  161.4 37.7 %collective-permute-done.29 = bf16[2,112,576]{2,1,0:T(8,128)(2,1)S(1)} collective-permute-done((bf16[2,112,576]{2,1,0:T(8,128)(2,1)S(1)}, bf16[2,112,576]{2,1,0:T(8,128)(2,1)S(1)}, u32[]{:S(2)}, u32[]{:S(2)}) %collective-permute-start.29) | collective-permute-done | bytes 258080 | tf_op jit(solution)/shard_map/ppermute | solution.py:646
  202.2 3.1 collective-permute-start.26
  210.0 2.9 collective-permute-done.33
  212.9 1.7 collective-permute-start.31
  215.4 6.3 %collective-permute-done.25.refs_1_ = bf16[3,192,256]{2,1,0:T(8,128)(2,1)S(1)} collective-permute-done((bf16[3,192,256]{2,1,0:T(8,128)(2,1)S(1)}, bf16[3,192,256]{2,1,0:T(8,128)(2,1)S(1)}, u32[]{:S(2)}, u32[]{:S(2)}) %collective-permute-start.25) | collective-permute-done | bytes 294944 | tf_op jit(solution)/shard_map/ppermute | solution.py:639
  222.4 9.4 %collective-permute-done.26.refs_2_ = bf16[3,192,256]{2,1,0:T(8,128)(2,1)S(1)} collective-permute-done((bf16[3,192,256]{2,1,0:T(8,128)(2,1)S(1)}, bf16[3,192,256]{2,1,0:T(8,128)(2,1)S(1)}, u32[]{:S(2)}, u32[]{:S(2)}) %collective-permute-start.26) | collective-permute-done | bytes 294944 | tf_op jit(solution)/shard_map/ppermute | solution.py:639
  233.4 3.5 %collective-permute-done.27.refs_3_ = bf16[3,192,256]{2,1,0:T(8,128)(2,1)} collective-permute-done((bf16[3,192,256]{2,1,0:T(8,128)(2,1)}, bf16[3,192,256]{2,1,0:T(8,128)(2,1)}, u32[]{:S(2)}, u32[]{:S(2)}) %collective-permute-start.27) | collective-permute-done | bytes 294944 | tf_op jit(solution)/shard_map/ppermute | solution.py:639
  242.4 4.1 %final.1 = bf16[256,768]{1,0:T(8,128)(2,1)} custom-call(s32[6]{0:T(128)S(1)} %stack.64.info, bf16[3,192,256]{2,1,0:T(8,128)(2,1)S(1)} %copy-done.15, bf16[3,192,256]{2,1,0:T(8,128)(2,1)S(1)} %copy-done.17, bf16[3,192,256]{2,1,0:T(8,128)(2,1)S(1)} %copy-done.19, bf16[3,192,256]{2,1,0:T(8,128)(2,1)} %collective-permute-done.27.refs_3_, ...), custom_call_target="tpu_custom_call" | custom-call | flops 905969664 | bytes 3538944 | tf_op jit(solution)/shard_map/final/pallas_call | solution.py:1116
  254.6 2.0 slice.68
  259.1 2.5 third.1
  261.6 3.5 %collective-permute-start.41 = (bf16[224,768]{1,0:T(8,128)(2,1)}, bf16[224,768]{1,0:T(8,128)(2,1)S(1)}, u32[]{:S(2)}, u32[]{:S(2)}) collective-permute-start(bf16[224,768]{1,0:T(8,128)(2,1)} %get-tuple-element.139), channel_id=1, source_target_pairs={{0,4},{1,5},{2,6},{3,7},{4,0},{5,1},{6,2},{7,3},{8,12},{9,13},{10,... | collective-permute-start | bytes 1032200 | tf_op jit(solution)/shard_map/ppermute | solution.py:639
  266.0 2.3 fusion.1
  268.3 16.9 %collective-permute-done.40.refs_1_ = bf16[224,768]{1,0:T(8,128)(2,1)S(1)} collective-permute-done((bf16[224,768]{1,0:T(8,128)(2,1)}, bf16[224,768]{1,0:T(8,128)(2,1)S(1)}, u32[]{:S(2)}, u32[]{:S(2)}) %collective-permute-start.40) | collective-permute-done | bytes 344096 | tf_op jit(solution)/shard_map/ppermute | solution.py:639
  285.2 4.3 %collective-permute-done.41.refs_2_ = bf16[224,768]{1,0:T(8,128)(2,1)S(1)} collective-permute-done((bf16[224,768]{1,0:T(8,128)(2,1)}, bf16[224,768]{1,0:T(8,128)(2,1)S(1)}, u32[]{:S(2)}, u32[]{:S(2)}) %collective-permute-start.41) | collective-permute-done | bytes 344096 | tf_op jit(solution)/shard_map/ppermute | solution.py:639
  291.3 2.4 collective-permute-start.45
  293.7 1.8 fusion.4
  296.7 4.5 %collective-permute-done.43.from_x = bf16[224,768]{1,0:T(8,128)(2,1)S(1)} collective-permute-done((bf16[224,768]{1,0:T(8,128)(2,1)S(1)}, bf16[224,768]{1,0:T(8,128)(2,1)S(1)}, u32[]{:S(2)}, u32[]{:S(2)}) %collective-permute-start.43) | collective-permute-done | bytes 344096 | tf_op jit(solution)/shard_map/ppermute | solution.py:646
  301.2 6.7 %collective-permute-done.44.from_y = bf16[224,768]{1,0:T(8,128)(2,1)S(1)} collective-permute-done((bf16[224,768]{1,0:T(8,128)(2,1)S(1)}, bf16[224,768]{1,0:T(8,128)(2,1)S(1)}, u32[]{:S(2)}, u32[]{:S(2)}) %collective-permute-start.44) | collective-permute-done | bytes 344096 | tf_op jit(solution)/shard_map/ppermute | solution.py:646
  307.9 2.6 spread.1
  (204 shorter events, 54.2 us)
Async XLA Ops:
  3.1 22.9 %collective-permute-start.4 = (bf16[256,768]{1,0:T(8,128)(2,1)}, bf16[256,768]{1,0:T(8,128)(2,1)S(1)}, u32[]{:S(2)}, u32[]{:S(2)}) collective-permute-start(bf16[256,768]{1,0:T(8,128)(2,1)} %refs_4_.3), channel_id=1, source_target_pairs={{0,6},{1,7},{2,0},{3,1},{4,2},{5,3},{6,4},{7,5},{8,14},{9,15},{10,... | collective-permute-start | bytes 1179656 | tf_op jit(solution)/shard_map/ppermute | solution.py:639
  3.1 22.9 %collective-permute-start.5 = (bf16[256,768]{1,0:T(8,128)(2,1)}, bf16[256,768]{1,0:T(8,128)(2,1)S(1)}, u32[]{:S(2)}, u32[]{:S(2)}) collective-permute-start(bf16[256,768]{1,0:T(8,128)(2,1)} %refs_4_.3), channel_id=1, source_target_pairs={{0,2},{1,3},{2,4},{3,5},{4,6},{5,7},{6,0},{7,1},{8,10},{9,11},{10,... | collective-permute-start | bytes 1179656 | tf_op jit(solution)/shard_map/ppermute | solution.py:639
  5.2 19.0 %collective-permute-start.1 = (s32[3,768]{1,0:T(4,128)S(1)}, s32[3,768]{1,0:T(4,128)S(1)}, u32[]{:S(2)}, u32[]{:S(2)}) collective-permute-start(s32[3,768]{1,0:T(4,128)S(1)} %get-tuple-element.167), channel_id=1, source_target_pairs={{0,4},{1,5},{2,6},{3,7},{4,0},{5,1},{6,2},{7,3},{8,12},{9,13},{10,... | collective-permute-start | bytes 27656 | tf_op jit(solution)/shard_map/ppermute | solution.py:639
  9.6 15.7 %collective-permute-start.2 = (s32[3,768]{1,0:T(4,128)S(1)}, s32[3,768]{1,0:T(4,128)S(1)}, u32[]{:S(2)}, u32[]{:S(2)}) collective-permute-start(s32[3,768]{1,0:T(4,128)S(1)} %get-tuple-element.166), channel_id=1, source_target_pairs={{0,2},{1,3},{2,4},{3,5},{4,6},{5,7},{6,0},{7,1},{8,10},{9,11},{10,... | collective-permute-start | bytes 27656 | tf_op jit(solution)/shard_map/ppermute | solution.py:639
  9.6 15.7 %collective-permute-start = (s32[3,768]{1,0:T(4,128)S(1)}, s32[3,768]{1,0:T(4,128)S(1)}, u32[]{:S(2)}, u32[]{:S(2)}) collective-permute-start(s32[3,768]{1,0:T(4,128)S(1)} %get-tuple-element.168), channel_id=1, source_target_pairs={{0,6},{1,7},{2,0},{3,1},{4,2},{5,3},{6,4},{7,5},{8,14},{9,15},{10,... | collective-permute-start | bytes 27656 | tf_op jit(solution)/shard_map/ppermute | solution.py:639
  24.2 36.4 %collective-permute-start.10 = (bf16[256,768]{1,0:T(8,128)(2,1)}, bf16[256,768]{1,0:T(8,128)(2,1)}, u32[]{:S(2)}, u32[]{:S(2)}) collective-permute-start(bf16[256,768]{1,0:T(8,128)(2,1)} %refs_4_.3), channel_id=1, source_target_pairs={{0,1},{1,0},{2,3},{3,2},{4,5},{5,4},{6,7},{7,6},{8,9},{9,8},{10,11... | collective-permute-start | bytes 1179656 | tf_op jit(solution)/shard_map/ppermute | solution.py:643
  26.0 8.3 %collective-permute-start.3 = (s32[4,3,768]{2,1,0:T(4,128)}, s32[4,3,768]{2,1,0:T(4,128)}, u32[]{:S(2)}, u32[]{:S(2)}) collective-permute-start(s32[4,3,768]{2,1,0:T(4,128)} %get-tuple-element.164), channel_id=1, source_target_pairs={{0,1},{1,0},{2,3},{3,2},{4,5},{5,4},{6,7},{7,6},{8,9},{9,8},{10,11... | collective-permute-start | bytes 110600 | tf_op jit(solution)/shard_map/ppermute | solution.py:643
  26.0 20.1 %collective-permute-start.6 = (bf16[256,768]{1,0:T(8,128)(2,1)}, bf16[256,768]{1,0:T(8,128)(2,1)}, u32[]{:S(2)}, u32[]{:S(2)}) collective-permute-start(bf16[256,768]{1,0:T(8,128)(2,1)} %refs_4_.3), channel_id=1, source_target_pairs={{0,4},{1,5},{2,6},{3,7},{4,0},{5,1},{6,2},{7,3},{8,12},{9,13},{10,... | collective-permute-start | bytes 1179656 | tf_op jit(solution)/shard_map/ppermute | solution.py:639
  37.4 26.1 %collective-permute-start.9 = (bf16[256,768]{1,0:T(8,128)(2,1)}, bf16[256,768]{1,0:T(8,128)(2,1)}, u32[]{:S(2)}, u32[]{:S(2)}) collective-permute-start(bf16[256,768]{1,0:T(8,128)(2,1)} %copy-done.12), channel_id=1, source_target_pairs={{0,1},{1,0},{2,3},{3,2},{4,5},{5,4},{6,7},{7,6},{8,9},{9,8},{10,11... | collective-permute-start | bytes 1179656 | tf_op jit(solution)/shard_map/ppermute | solution.py:643
  37.6 28.6 %collective-permute-start.8 = (bf16[256,768]{1,0:T(8,128)(2,1)}, bf16[256,768]{1,0:T(8,128)(2,1)}, u32[]{:S(2)}, u32[]{:S(2)}) collective-permute-start(bf16[256,768]{1,0:T(8,128)(2,1)} %copy-done.10), channel_id=1, source_target_pairs={{0,1},{1,0},{2,3},{3,2},{4,5},{5,4},{6,7},{7,6},{8,9},{9,8},{10,11... | collective-permute-start | bytes 1179656 | tf_op jit(solution)/shard_map/ppermute | solution.py:643
  46.1 22.8 %collective-permute-start.7 = (bf16[256,768]{1,0:T(8,128)(2,1)}, bf16[256,768]{1,0:T(8,128)(2,1)}, u32[]{:S(2)}, u32[]{:S(2)}) collective-permute-start(bf16[256,768]{1,0:T(8,128)(2,1)} %collective-permute-done.6.refs_0_), channel_id=1, source_target_pairs={{0,1},{1,0},{2,3},{3,2},{4,5},{5,4},{6,7},{7,6},{8,9},{9,8},{10,11... | collective-permute-start | bytes 1179656 | tf_op jit(solution)/shard_map/ppermute | solution.py:643
  85.6 5.5 %collective-permute-start.11 = (bf16[192,256]{1,0:T(8,128)(2,1)S(1)}, bf16[192,256]{1,0:T(8,128)(2,1)S(1)}, u32[]{:S(2)}, u32[]{:S(2)}) collective-permute-start(bf16[192,256]{1,0:T(8,128)(2,1)S(1)} %get-tuple-element.92), channel_id=1, source_target_pairs={{0,2},{1,3},{2,4},{3,5},{4,6},{5,7},{6,0},{7,1},{8,10},{9,11},{10,... | collective-permute-start | bytes 294920 | tf_op jit(solution)/shard_map/ppermute | solution.py:639
  85.6 10.5 %collective-permute-start.12 = (bf16[192,256]{1,0:T(8,128)(2,1)S(1)}, bf16[192,256]{1,0:T(8,128)(2,1)S(1)}, u32[]{:S(2)}, u32[]{:S(2)}) collective-permute-start(bf16[192,256]{1,0:T(8,128)(2,1)S(1)} %get-tuple-element.93), channel_id=1, source_target_pairs={{0,4},{1,5},{2,6},{3,7},{4,0},{5,1},{6,2},{7,3},{8,12},{9,13},{10,... | collective-permute-start | bytes 294920 | tf_op jit(solution)/shard_map/ppermute | solution.py:639
  89.4 9.5 %collective-permute-start.13 = (bf16[192,256]{1,0:T(8,128)(2,1)S(1)}, bf16[192,256]{1,0:T(8,128)(2,1)S(1)}, u32[]{:S(2)}, u32[]{:S(2)}) collective-permute-start(bf16[192,256]{1,0:T(8,128)(2,1)S(1)} %get-tuple-element.94), channel_id=1, source_target_pairs={{0,6},{1,7},{2,0},{3,1},{4,2},{5,3},{6,4},{7,5},{8,14},{9,15},{10,... | collective-permute-start | bytes 294920 | tf_op jit(solution)/shard_map/ppermute | solution.py:639
  110.3 9.8 %collective-permute-start.17 = (bf16[256,3072]{1,0:T(8,128)(2,1)S(1)}, bf16[256,3072]{1,0:T(8,128)(2,1)S(1)}, u32[]{:S(2)}, u32[]{:S(2)}) collective-permute-start(bf16[256,3072]{1,0:T(8,128)(2,1)S(1)} %get-tuple-element.100.refs_0_), channel_id=1, source_target_pairs={{0,1},{1,0},{2,3},{3,2},{4,5},{5,4},{6,7},{7,6},{8,9},{9,8},{10,11... | collective-permute-start | bytes 4718600 | tf_op jit(solution)/shard_map/ppermute | solution.py:643
  110.4 9.7 %collective-permute-start.19 = (bf16[256,1536]{1,0:T(8,128)(2,1)S(1)}, bf16[256,1536]{1,0:T(8,128)(2,1)S(1)}, u32[]{:S(2)}, u32[]{:S(2)}) collective-permute-start(bf16[256,1536]{1,0:T(8,128)(2,1)S(1)} %get-tuple-element.103), channel_id=1, source_target_pairs={{0,1},{1,0},{2,3},{3,2},{4,5},{5,4},{6,7},{7,6},{8,9},{9,8},{10,11... | collective-permute-start | bytes 2359304 | tf_op jit(solution)/shard_map/ppermute | solution.py:643
  110.9 4.6 %collective-permute-start.21 = (bf16[256,768]{1,0:T(8,128)(2,1)S(1)}, bf16[256,768]{1,0:T(8,128)(2,1)S(1)}, u32[]{:S(2)}, u32[]{:S(2)}) collective-permute-start(bf16[256,768]{1,0:T(8,128)(2,1)S(1)} %copy-done.24), channel_id=1, source_target_pairs={{0,1},{1,0},{2,3},{3,2},{4,5},{5,4},{6,7},{7,6},{8,9},{9,8},{10,11... | collective-permute-start | bytes 1179656 | tf_op jit(solution)/shard_map/ppermute | solution.py:643
  110.9 5.7 %collective-permute-start.18 = (bf16[256,768]{1,0:T(8,128)(2,1)S(1)}, bf16[256,768]{1,0:T(8,128)(2,1)S(1)}, u32[]{:S(2)}, u32[]{:S(2)}) collective-permute-start(bf16[256,768]{1,0:T(8,128)(2,1)S(1)} %get-tuple-element.101.refs_2_), channel_id=1, source_target_pairs={{0,1},{1,0},{2,3},{3,2},{4,5},{5,4},{6,7},{7,6},{8,9},{9,8},{10,11... | collective-permute-start | bytes 1179656 | tf_op jit(solution)/shard_map/ppermute | solution.py:643
  111.4 6.3 %collective-permute-start.20 = (bf16[768,256]{1,0:T(8,128)(2,1)S(1)}, bf16[768,256]{1,0:T(8,128)(2,1)S(1)}, u32[]{:S(2)}, u32[]{:S(2)}) collective-permute-start(bf16[768,256]{1,0:T(8,128)(2,1)S(1)} %get-tuple-element.105), channel_id=1, source_target_pairs={{0,1},{1,0},{2,3},{3,2},{4,5},{5,4},{6,7},{7,6},{8,9},{9,8},{10,11... | collective-permute-start | bytes 1179656 | tf_op jit(solution)/shard_map/ppermute | solution.py:643
  115.4 1.2 collective-permute-start.22
  116.6 10.5 %collective-permute-start.14 = (bf16[192,256]{1,0:T(8,128)(2,1)S(1)}, bf16[192,256]{1,0:T(8,128)(2,1)S(1)}, u32[]{:S(2)}, u32[]{:S(2)}) collective-permute-start(bf16[192,256]{1,0:T(8,128)(2,1)S(1)} %get-tuple-element.97), channel_id=1, source_target_pairs={{0,6},{1,7},{2,0},{3,1},{4,2},{5,3},{6,4},{7,5},{8,14},{9,15},{10,... | collective-permute-start | bytes 294920 | tf_op jit(solution)/shard_map/ppermute | solution.py:639
  116.6 10.5 %collective-permute-start.15 = (bf16[192,256]{1,0:T(8,128)(2,1)S(1)}, bf16[192,256]{1,0:T(8,128)(2,1)S(1)}, u32[]{:S(2)}, u32[]{:S(2)}) collective-permute-start(bf16[192,256]{1,0:T(8,128)(2,1)S(1)} %get-tuple-element.98), channel_id=1, source_target_pairs={{0,4},{1,5},{2,6},{3,7},{4,0},{5,1},{6,2},{7,3},{8,12},{9,13},{10,... | collective-permute-start | bytes 294920 | tf_op jit(solution)/shard_map/ppermute | solution.py:639
  117.7 9.5 %collective-permute-start.16 = (bf16[192,256]{1,0:T(8,128)(2,1)S(1)}, bf16[192,256]{1,0:T(8,128)(2,1)S(1)}, u32[]{:S(2)}, u32[]{:S(2)}) collective-permute-start(bf16[192,256]{1,0:T(8,128)(2,1)S(1)} %get-tuple-element.99), channel_id=1, source_target_pairs={{0,2},{1,3},{2,4},{3,5},{4,6},{5,7},{6,0},{7,1},{8,10},{9,11},{10,... | collective-permute-start | bytes 294920 | tf_op jit(solution)/shard_map/ppermute | solution.py:639
  127.1 79.8 %copy-start = (bf16[2,4,128,768]{3,2,1,0:T(8,128)(2,1)}, bf16[2,4,128,768]{3,2,1,0:T(8,128)(2,1)S(1)}, u32[]{:S(2)}) copy-start(bf16[2,4,128,768]{3,2,1,0:T(8,128)(2,1)S(1)} %get-tuple-element.107.keep_u) | copy-start | bytes 4718596
  127.2 79.7 %copy-start.4 = (bf16[2,4,96,768]{3,2,1,0:T(8,128)(2,1)}, bf16[2,4,96,768]{3,2,1,0:T(8,128)(2,1)S(1)}, u32[]{:S(2)}) copy-start(bf16[2,4,96,768]{3,2,1,0:T(8,128)(2,1)S(1)} %get-tuple-element.132.keep_d) | copy-start | bytes 3538948
  145.0 2.5 collective-permute-start.24
  145.1 2.4 collective-permute-start.23
  156.1 3.2 %collective-permute-start.28 = (bf16[4,112,576]{2,1,0:T(8,128)(2,1)S(1)}, bf16[4,112,576]{2,1,0:T(8,128)(2,1)S(1)}, u32[]{:S(2)}, u32[]{:S(2)}) collective-permute-start(bf16[4,112,576]{2,1,0:T(8,128)(2,1)S(1)} %get-tuple-element.129), channel_id=1, source_target_pairs={{0,1},{1,0},{2,3},{3,2},{4,5},{5,4},{6,7},{7,6},{8,9},{9,8},{10,11... | collective-permute-start | bytes 1548296 | tf_op jit(solution)/shard_map/ppermute | solution.py:643
  156.3 49.0 %collective-permute-start.36 = (bf16[2,4,128,768]{3,2,1,0:T(8,128)(2,1)S(1)}, bf16[2,4,128,768]{3,2,1,0:T(8,128)(2,1)S(1)}, u32[]{:S(2)}, u32[]{:S(2)}) collective-permute-start(bf16[2,4,128,768]{3,2,1,0:T(8,128)(2,1)S(1)} %get-tuple-element.130), channel_id=1, source_target_pairs={{0,8},{8,0},{16,24},{24,16},{1,9},{9,1},{17,25},{25,17},{2,10},{10... | collective-permute-start | bytes 4718600 | tf_op jit(solution)/shard_map/ppermute | solution.py:646
  157.8 47.5 %collective-permute-start.37 = (bf16[2,4,96,768]{3,2,1,0:T(8,128)(2,1)S(1)}, bf16[2,4,96,768]{3,2,1,0:T(8,128)(2,1)S(1)}, u32[]{:S(2)}, u32[]{:S(2)}) collective-permute-start(bf16[2,4,96,768]{3,2,1,0:T(8,128)(2,1)S(1)} %get-tuple-element.133), channel_id=1, source_target_pairs={{0,16},{8,24},{16,0},{24,8},{1,17},{9,25},{17,1},{25,9},{2,18},{10... | collective-permute-start | bytes 3538952 | tf_op jit(solution)/shard_map/ppermute | solution.py:646
  159.5 39.6 %collective-permute-start.29 = (bf16[2,112,576]{2,1,0:T(8,128)(2,1)S(1)}, bf16[2,112,576]{2,1,0:T(8,128)(2,1)S(1)}, u32[]{:S(2)}, u32[]{:S(2)}) collective-permute-start(bf16[2,112,576]{2,1,0:T(8,128)(2,1)S(1)} %get-tuple-element.156), channel_id=1, source_target_pairs={{0,8},{8,0},{16,24},{24,16},{1,9},{9,1},{17,25},{25,17},{2,10},{10... | collective-permute-start | bytes 774152 | tf_op jit(solution)/shard_map/ppermute | solution.py:646
  160.2 39.0 %collective-permute-start.32 = (bf16[2,112,576]{2,1,0:T(8,128)(2,1)S(1)}, bf16[2,112,576]{2,1,0:T(8,128)(2,1)S(1)}, u32[]{:S(2)}, u32[]{:S(2)}) collective-permute-start(bf16[2,112,576]{2,1,0:T(8,128)(2,1)S(1)} %get-tuple-element.157), channel_id=1, source_target_pairs={{0,16},{8,24},{16,0},{24,8},{1,17},{9,25},{17,1},{25,9},{2,18},{10... | collective-permute-start | bytes 774152 | tf_op jit(solution)/shard_map/ppermute | solution.py:646
  199.3 8.8 %collective-permute-start.30 = (bf16[2,112,576]{2,1,0:T(8,128)(2,1)S(1)}, bf16[2,112,576]{2,1,0:T(8,128)(2,1)S(1)}, u32[]{:S(2)}, u32[]{:S(2)}) collective-permute-start(bf16[2,112,576]{2,1,0:T(8,128)(2,1)S(1)} %get-tuple-element.154), channel_id=1, source_target_pairs={{0,16},{8,24},{16,0},{24,8},{1,17},{9,25},{17,1},{25,9},{2,18},{10... | collective-permute-start | bytes 774152 | tf_op jit(solution)/shard_map/ppermute | solution.py:646
  200.9 20.8 %collective-permute-start.25 = (bf16[3,192,256]{2,1,0:T(8,128)(2,1)S(1)}, bf16[3,192,256]{2,1,0:T(8,128)(2,1)S(1)}, u32[]{:S(2)}, u32[]{:S(2)}) collective-permute-start(bf16[3,192,256]{2,1,0:T(8,128)(2,1)S(1)} %get-tuple-element.123.refs_1_), channel_id=1, source_target_pairs={{0,2},{1,3},{2,4},{3,5},{4,6},{5,7},{6,0},{7,1},{8,10},{9,11},{10,... | collective-permute-start | bytes 884744 | tf_op jit(solution)/shard_map/ppermute | solution.py:639
  202.2 29.5 %collective-permute-start.26 = (bf16[3,192,256]{2,1,0:T(8,128)(2,1)S(1)}, bf16[3,192,256]{2,1,0:T(8,128)(2,1)S(1)}, u32[]{:S(2)}, u32[]{:S(2)}) collective-permute-start(bf16[3,192,256]{2,1,0:T(8,128)(2,1)S(1)} %get-tuple-element.124.refs_2_), channel_id=1, source_target_pairs={{0,4},{1,5},{2,6},{3,7},{4,0},{5,1},{6,2},{7,3},{8,12},{9,13},{10,... | collective-permute-start | bytes 884744 | tf_op jit(solution)/shard_map/ppermute | solution.py:639
  205.3 31.6 %collective-permute-start.27 = (bf16[3,192,256]{2,1,0:T(8,128)(2,1)}, bf16[3,192,256]{2,1,0:T(8,128)(2,1)}, u32[]{:S(2)}, u32[]{:S(2)}) collective-permute-start(bf16[3,192,256]{2,1,0:T(8,128)(2,1)} %get-tuple-element.125.refs_3_), channel_id=1, source_target_pairs={{0,6},{1,7},{2,0},{3,1},{4,2},{5,3},{6,4},{7,5},{8,14},{9,15},{10,... | collective-permute-start | bytes 884744 | tf_op jit(solution)/shard_map/ppermute | solution.py:639
  205.4 7.5 %collective-permute-start.33 = (bf16[2,112,576]{2,1,0:T(8,128)(2,1)S(1)}, bf16[2,112,576]{2,1,0:T(8,128)(2,1)S(1)}, u32[]{:S(2)}, u32[]{:S(2)}) collective-permute-start(bf16[2,112,576]{2,1,0:T(8,128)(2,1)S(1)} %get-tuple-element.155), channel_id=1, source_target_pairs={{0,8},{8,0},{16,24},{24,16},{1,9},{9,1},{17,25},{25,17},{2,10},{10... | collective-permute-start | bytes 774152 | tf_op jit(solution)/shard_map/ppermute | solution.py:646
  208.1 48.5 %collective-permute-start.38 = (bf16[4,128,768]{2,1,0:T(8,128)(2,1)}, bf16[4,128,768]{2,1,0:T(8,128)(2,1)}, u32[]{:S(2)}, u32[]{:S(2)}) collective-permute-start(bf16[4,128,768]{2,1,0:T(8,128)(2,1)} %get-tuple-element.135), channel_id=1, source_target_pairs={{0,16},{8,24},{16,0},{24,8},{1,17},{9,25},{17,1},{25,9},{2,18},{10... | collective-permute-start | bytes 2359304 | tf_op jit(solution)/shard_map/ppermute | solution.py:646
  212.9 33.6 %collective-permute-start.31 = (bf16[112,576]{1,0:T(8,128)(2,1)}, bf16[112,576]{1,0:T(8,128)(2,1)}, u32[]{:S(2)}, u32[]{:S(2)}) collective-permute-start(bf16[112,576]{1,0:T(8,128)(2,1)} %get-tuple-element.160), channel_id=1, source_target_pairs={{0,2},{1,3},{2,4},{3,5},{4,6},{5,7},{6,0},{7,1},{8,10},{9,11},{10,... | collective-permute-start | bytes 387080 | tf_op jit(solution)/shard_map/ppermute | solution.py:639
  222.4 24.1 %collective-permute-start.34 = (bf16[112,576]{1,0:T(8,128)(2,1)}, bf16[112,576]{1,0:T(8,128)(2,1)}, u32[]{:S(2)}, u32[]{:S(2)}) collective-permute-start(bf16[112,576]{1,0:T(8,128)(2,1)} %get-tuple-element.161), channel_id=1, source_target_pairs={{0,4},{1,5},{2,6},{3,7},{4,0},{5,1},{6,2},{7,3},{8,12},{9,13},{10,... | collective-permute-start | bytes 387080 | tf_op jit(solution)/shard_map/ppermute | solution.py:639
  232.5 14.0 %collective-permute-start.35 = (bf16[112,576]{1,0:T(8,128)(2,1)}, bf16[112,576]{1,0:T(8,128)(2,1)}, u32[]{:S(2)}, u32[]{:S(2)}) collective-permute-start(bf16[112,576]{1,0:T(8,128)(2,1)} %get-tuple-element.162), channel_id=1, source_target_pairs={{0,6},{1,7},{2,0},{3,1},{4,2},{5,3},{6,4},{7,5},{8,14},{9,15},{10,... | collective-permute-start | bytes 387080 | tf_op jit(solution)/shard_map/ppermute | solution.py:639
  236.9 19.7 %collective-permute-start.39 = (bf16[4,96,768]{2,1,0:T(8,128)(2,1)}, bf16[4,96,768]{2,1,0:T(8,128)(2,1)}, u32[]{:S(2)}, u32[]{:S(2)}) collective-permute-start(bf16[4,96,768]{2,1,0:T(8,128)(2,1)} %copy-done.23), channel_id=1, source_target_pairs={{0,8},{8,0},{16,24},{24,16},{1,9},{9,1},{17,25},{25,17},{2,10},{10... | collective-permute-start | bytes 1769480 | tf_op jit(solution)/shard_map/ppermute | solution.py:646
  261.6 23.6 %collective-permute-start.40 = (bf16[224,768]{1,0:T(8,128)(2,1)}, bf16[224,768]{1,0:T(8,128)(2,1)S(1)}, u32[]{:S(2)}, u32[]{:S(2)}) collective-permute-start(bf16[224,768]{1,0:T(8,128)(2,1)} %get-tuple-element.138), channel_id=1, source_target_pairs={{0,2},{1,3},{2,4},{3,5},{4,6},{5,7},{6,0},{7,1},{8,10},{9,11},{10,... | collective-permute-start | bytes 1032200 | tf_op jit(solution)/shard_map/ppermute | solution.py:639
  261.6 27.9 %collective-permute-start.41 = (bf16[224,768]{1,0:T(8,128)(2,1)}, bf16[224,768]{1,0:T(8,128)(2,1)S(1)}, u32[]{:S(2)}, u32[]{:S(2)}) collective-permute-start(bf16[224,768]{1,0:T(8,128)(2,1)} %get-tuple-element.139), channel_id=1, source_target_pairs={{0,4},{1,5},{2,6},{3,7},{4,0},{5,1},{6,2},{7,3},{8,12},{9,13},{10,... | collective-permute-start | bytes 1032200 | tf_op jit(solution)/shard_map/ppermute | solution.py:639
  265.2 24.9 %collective-permute-start.42 = (bf16[224,768]{1,0:T(8,128)(2,1)}, bf16[224,768]{1,0:T(8,128)(2,1)S(1)}, u32[]{:S(2)}, u32[]{:S(2)}) collective-permute-start(bf16[224,768]{1,0:T(8,128)(2,1)} %get-tuple-element.140), channel_id=1, source_target_pairs={{0,6},{1,7},{2,0},{3,1},{4,2},{5,3},{6,4},{7,5},{8,14},{9,15},{10,... | collective-permute-start | bytes 1032200 | tf_op jit(solution)/shard_map/ppermute | solution.py:639
  290.2 11.0 %collective-permute-start.43 = (bf16[224,768]{1,0:T(8,128)(2,1)S(1)}, bf16[224,768]{1,0:T(8,128)(2,1)S(1)}, u32[]{:S(2)}, u32[]{:S(2)}) collective-permute-start(bf16[224,768]{1,0:T(8,128)(2,1)S(1)} %fourth.1.own), channel_id=1, source_target_pairs={{0,8},{8,0},{16,24},{24,16},{1,9},{9,1},{17,25},{25,17},{2,10},{10... | collective-permute-start | bytes 1032200 | tf_op jit(solution)/shard_map/ppermute | solution.py:646
  290.8 17.1 %collective-permute-start.44 = (bf16[224,768]{1,0:T(8,128)(2,1)S(1)}, bf16[224,768]{1,0:T(8,128)(2,1)S(1)}, u32[]{:S(2)}, u32[]{:S(2)}) collective-permute-start(bf16[224,768]{1,0:T(8,128)(2,1)S(1)} %fourth.1.own), channel_id=1, source_target_pairs={{0,16},{8,24},{16,0},{24,8},{1,17},{9,25},{17,1},{25,9},{2,18},{10... | collective-permute-start | bytes 1032200 | tf_op jit(solution)/shard_map/ppermute | solution.py:646
  291.3 16.6 %collective-permute-start.45 = (bf16[224,768]{1,0:T(8,128)(2,1)S(1)}, bf16[224,768]{1,0:T(8,128)(2,1)S(1)}, u32[]{:S(2)}, u32[]{:S(2)}) collective-permute-start(bf16[224,768]{1,0:T(8,128)(2,1)S(1)} %fourth.1.own), channel_id=1, source_target_pairs={{0,24},{8,16},{16,8},{24,0},{1,25},{9,17},{17,9},{25,1},{2,26},{10... | collective-permute-start | bytes 1032200 | tf_op jit(solution)/shard_map/ppermute | solution.py:646
  (40 other events, 337.5 us)

commit v4 on v3

--- a/solution.py
+++ b/solution.py
@@ -235,9 +235,11 @@
     part_ref[0] = total
 
 
-def member_kernel(ids_all, feat, kv, bias, *refs, size, groups):
+def back_kernel(ids_all, feat, kv, bias, *refs, size, groups, gots):
     grads = refs[:groups]
-    mix_ref, stat_ref, dq_ref, own_ref, send_ref, total = refs[groups:]
+    mix_ref, stat_ref, cen_ref = refs[groups : groups + 3]
+    shares = refs[groups + 3 : groups + 4 + gots]
+    dq_ref, own_ref, send_ref, total, both = refs[groups + 4 + gots :]
     hs, rows = grads[0].shape
     keys = kv.shape[1]
     count = keys // size
@@ -245,16 +247,18 @@
     clusters = bias.shape[2]
     kv_h, bias_h = kv.at[0], bias.at[0]
     queries_all, kvt = feat.at[0, :hs], feat.at[0, hs:]
-    high, low = split_low(stat_ref[0, hs : hs + 8, :])
+    stats = stat_ref[0]
+    high, low = split_low(stats[hs : hs + 8])
     table = jnp.concatenate([high, low], axis=1)
-    sides, levels, deltas, pads, rights = [], [], [], [], []
+    hots, sides, levels, deltas, pads, rights = [], [], [], [], [], []
     for group in range(groups):
         spot = slice(group * peers * rows, group * peers * rows + rows)
         hot = one_hot_t(ids_all[0, :, spot], clusters)
         queries = queries_all[:, spot]
         blank = jnp.zeros_like(queries)
+        hots.append(jnp.concatenate([hot, hot], axis=0))
         sides.append(jnp.concatenate([queries, blank, hot], axis=0))
-        mass = nn(table, jnp.concatenate([hot, hot], axis=0))[0:1]
+        mass = nn(table, hots[group])[0:1]
         back = (mass * grads[group][...].astype(F32)).astype(BF)
         levels.append(mix_ref[0, group, hs : hs + 1])
         deltas.append(jnp.sum(back.astype(F32) * mix_ref[0, group, :hs], axis=0, keepdims=True))
@@ -264,8 +268,8 @@
 
     def scores(group, index):
         kv_c = piece(kv_h, index, size, 0)
-        both = jnp.concatenate([kv_c, piece(bias_h, index, size, 0)], axis=1)
-        return nn(both, sides[group]), nn(kv_c, pads[group])
+        pair = jnp.concatenate([kv_c, piece(bias_h, index, size, 0)], axis=1)
+        return nn(pair, sides[group]), nn(kv_c, pads[group])
 
     def finish(group, index, found, dq):
         weights = jnp.exp(found[0] - levels[group])
@@ -278,10 +282,38 @@
             total[spot, :] += part
         return dq + nn(piece(kvt, index, size, 1), grad_s)
 
+    rest, mass = stats[:hs], stats[hs : hs + 1]
+    level, counts = stats[hs + 1 : hs + 2], stats[hs + 2 : hs + 3]
+    centroid = cen_ref[0]
+    part = shares[0][0]
+    for share in shares[1:]:
+        part = part + share[0]
+    d_rest = part[:hs].astype(BF)
+    d_mass = part[hs : hs + 1] + part[hs + 1 : hs + 2]
+    delta = jnp.sum(d_rest.astype(F32) * rest, axis=0, keepdims=True) + d_mass * mass
+    cen_pad = jnp.concatenate([centroid, jnp.zeros_like(centroid)], axis=0)
+    rest_pad = jnp.concatenate([jnp.zeros_like(centroid), d_rest], axis=0)
+    right = jnp.concatenate([cen_pad, rest_pad], axis=1).T
+
+    def cluster_step(index, summed):
+        kv_c = piece(kv_h, index, size, 0)
+        marks = piece(bias_h, index, size, 0).astype(F32)
+        probs = jnp.exp(nn(kv_c, cen_pad) - level)
+        probs = jnp.where(marks < 2.0 * NEGATIVE, 0.0, probs)
+        top = marks == 0.0
+        d_probs = jnp.where(top, d_mass, nn(kv_c, rest_pad))
+        d_score = (probs * (d_probs - delta)).astype(BF)
+        other = jnp.where(top, 0.0, probs).astype(BF)
+        both[spot_of(index, size), :] = jnp.concatenate([d_score, other], axis=1)
+        return summed + nn(piece(kvt, index, size, 1), d_score)
+
     start = jnp.zeros((2 * hs, rows), F32)
+    zero = jnp.zeros((2 * hs, clusters), F32)
+    member_dq = []
     if count <= 4:
         tasks = [(group, index) for group in range(groups) for index in range(count)]
         ahead = scores(*tasks[0])
+        d_cen = key_sum(keys, size, cluster_step, zero)
         dq = start
         for step, (group, index) in enumerate(tasks):
             found = ahead
@@ -289,80 +321,55 @@
                 ahead = scores(*tasks[step + 1])
             dq = finish(group, index, found, dq)
             if index == count - 1:
-                dq_ref[group] = dq[:hs] * 0.125
+                member_dq.append(dq[:hs] * 0.125)
                 dq = start
     else:
+        d_cen = key_sum(keys, size, cluster_step, zero)
         for group in range(groups):
 
             def step(index, dq, group=group):
                 return finish(group, index, scores(group, index), dq)
 
-            dq_ref[group] = lax.fori_loop(0, count, step, start)[:hs] * 0.125
-    for group in range(groups):
-        base = group * peers * rows
-        own_ref[0, group * rows : (group + 1) * rows, :] = total[base : base + rows, :]
-        for peer in range(1, peers):
-            spot = (peer - 1) * groups * rows + group * rows
-            found = total[base + peer * rows : base + (peer + 1) * rows, :]
-            send_ref[0, spot : spot + rows, :] = found.astype(BF)
-
-
-def centroid_kernel(ids_own, feat_all, kv, bias, part_ref, stat_ref, cen_ref, dqm_ref, own_ref, *refs, size, groups, gots):
-    got_refs = refs[:gots]
-    outs, both = refs[gots : gots + groups], refs[gots + groups]
-    hs, rows = cen_ref.shape[1], outs[0].shape[2]
-    keys = kv.shape[1]
-    peers = keys // (groups * rows)
-    clusters = bias.shape[2]
-    kv_h, bias_h, kvt = kv.at[0], bias.at[0], feat_all.at[0, hs:]
-    stats = stat_ref[0]
-    rest, mass = stats[:hs], stats[hs : hs + 1]
-    level, counts = stats[hs + 1 : hs + 2], stats[hs + 2 : hs + 3]
-    centroid = cen_ref[0]
-    blank = jnp.zeros_like(centroid)
-    part = part_ref[0]
-    d_rest = part[:hs].astype(BF)
-    d_mass = part[hs : hs + 1] + part[hs + 1 : hs + 2]
-    delta = jnp.sum(d_rest.astype(F32) * rest, axis=0, keepdims=True) + d_mass * mass
-    cen_pad = jnp.concatenate([centroid, blank], axis=0)
-    rest_pad = jnp.concatenate([blank, d_rest], axis=0)
-    right = jnp.concatenate([cen_pad, rest_pad], axis=1).T
-
-    def step(index, total):
-        kv_c = piece(kv_h, index, size, 0)
-        marks = piece(bias_h, index, size, 0).astype(F32)
-        scores = nn(kv_c, cen_pad)
-        probs = jnp.where(marks < 2.0 * NEGATIVE, 0.0, jnp.exp(scores - level))
-        top = marks == 0.0
-        d_probs = jnp.where(top, d_mass, nn(kv_c, rest_pad))
-        d_score = (probs * (d_probs - delta)).astype(BF)
-        other = jnp.where(top, 0.0, probs).astype(BF)
-        both[spot_of(index, size), :] = jnp.concatenate([d_score, other], axis=1)
-        return total + nn(piece(kvt, index, size, 1), d_score)
-
-    d_cen = key_sum(keys, size, step, jnp.zeros((2 * hs, clusters), F32))
+            member_dq.append(lax.fori_loop(0, count, step, start)[:hs] * 0.125)
     d_cen = d_cen[:hs] * 0.125 / jnp.maximum(counts, 1.0)
     high, low = split_low(d_cen)
     table = jnp.concatenate([high, low], axis=1)
     for group in range(groups):
-        spot = group * peers * rows
-        hot = one_hot_t(ids_own[0, :, spot : spot + rows], clusters)
-        spread = nn(table, jnp.concatenate([hot, hot], axis=0))
-        own = nn(both[spot : spot + rows, :], right) + own_ref[0, group * rows : (group + 1) * rows, :]
-        for got in got_refs:
-            own = own + got[0, group * rows : (group + 1) * rows, :].astype(F32)
-        outs[group][0, :hs] = (dqm_ref[group] + spread).astype(BF)
-        outs[group][0, hs:] = own.T.astype(BF)
+        base = group * peers * rows
+        dq_ref[group] = (member_dq[group] + nn(table, hots[group])).astype(BF)
+        own = total[base : base + rows, :] + nn(both[base : base + rows, :], right)
+        own_ref[0, :, group * rows : (group + 1) * rows] = own.T
+        for peer in range(1, peers):
+            spot = (peer - 1) * groups * rows + group * rows
+            found = total[base + peer * rows : base + (peer + 1) * rows, :]
+            send_ref[0, :, spot : spot + rows] = found.astype(BF).T
+
+
+def join_kernel(dq_ref, own_ref, *refs, groups):
+    gots, outs = refs[:-groups], refs[-groups:]
+    heads, _, rows = outs[0].shape
+    hs = dq_ref.shape[1] // heads
+    for head in range(heads):
+        for group in range(groups):
+            spot = slice(group * rows, (group + 1) * rows)
+            pair = own_ref[head, :, spot]
+            for got in gots:
+                pair = pair + got[head, :, spot].astype(F32)
+            outs[group][head, :hs] = dq_ref[group, head * hs : (head + 1) * hs]
+            outs[group][head, hs:] = pair.astype(BF)
 
 
 def block_kernel(info, *refs, groups, chunks, fast):
     (attn, rest) = (refs[:groups], refs[groups:])
     x_ref, gain_ref, shift_ref, wo_ref, up_ref, down_ref, cot_ref = rest[:7]
-    out_ref, dres_ref, dn_ref, dup_ref, dbr_ref, act_ref, low_ref = rest[7:14]
-    rest = rest[14:]
+    out_ref, dres_ref = rest[7:9]
     if fast:
-        act_far, low_far = rest[:2]
-        rest = rest[2:]
+        far_ref, low_far, act_ref, low_ref = rest[9:13]
+        rest = rest[13:]
+        hidden = far_ref.shape[1] * 4 // 7
+    else:
+        dn_ref, dup_ref, dbr_ref, act_ref, low_ref = rest[9:14]
+        rest = rest[14:]
     dat = rest[:groups]
     hat_ref, inv_ref, normed, back, total = rest[groups:]
     index = pl.program_id(0)
@@ -411,13 +418,16 @@
         GELU_A * (1.0 + 3.0 * GELU_B * square)
     )
     d_up = (grad_act * slope).astype(BF)
-    dup_ref[...] = d_up
     if fast:
-        half = act.shape[1] // 2
+        part = act.shape[1]
+        half = part // 2
         first, second = act[:, :half], act[:, half:]
         act_ref[...] = jnp.where(info[1] == 0, first, second)
-        act_far[...] = jnp.where(info[1] == 0, second, first)
+        far_ref[:, pl.ds(pl.multiple_of(index * part, part), part)] = d_up
+        spot = pl.ds(pl.multiple_of(hidden + index * half, half), half)
+        far_ref[:, spot] = jnp.where(info[1] == 0, second, first)
     else:
+        dup_ref[...] = d_up
         act_ref[...] = act
     back[...] += nt(d_up, up_ref[...])
     total[...] += nn(act, down_ref[...])
@@ -429,38 +439,59 @@
         hat = hat_ref[...]
         gain_part = jnp.sum(d_normed * hat, axis=0, keepdims=True)
         shift_part = jnp.sum(d_normed, axis=0, keepdims=True)
-        blank = jnp.zeros((6, d_normed.shape[1]), F32)
-        dn_ref[...] = jnp.concatenate([gain_part, shift_part, blank], axis=0)
+        if fast:
+            rows, width = low_far.shape[1], d_normed.shape[1]
+            fold = []
+            for part_row in split_low(gain_part) + split_low(shift_part):
+                fold += [part_row[:, k : k + rows].astype(F32) for k in range(0, width, rows)]
+            fold.append(jnp.zeros((low_far.shape[0] - width - len(fold), rows), F32))
+            folded = jnp.concatenate(fold, axis=0).astype(BF)
+            low_far[width:, :] = folded
+            low_ref[width:, :] = folded
+        else:
+            blank = jnp.zeros((6, d_normed.shape[1]), F32)
+            dn_ref[...] = jnp.concatenate([gain_part, shift_part, blank], axis=0)
         gy = d_normed * gain_ref[...]
         mean_one = jnp.mean(gy, axis=-1, keepdims=True)
         mean_two = jnp.mean(gy * hat, axis=-1, keepdims=True)
         d_resid = cot_ref[...].astype(F32) + inv_ref[:, 0:1] * (gy - mean_one - hat * mean_two)
         dres_ref[...] = d_resid
         branch = d_resid.astype(BF)
-        dbr_ref[...] = branch
+        if fast:
+            far_ref[:, hidden * 3 // 2 :] = branch
+        else:
+            dbr_ref[...] = branch
         for group in range(groups):
             owner = lax.rem(info[0] + groups - group, groups)
             dat[group][...] = nt(wo_ref[owner], branch).astype(BF)
 
 
 def weights_kernel(info, *refs, groups):
-    (dup, dup_got, dbr, dbr_got, act, act_got, low, low_got, cot, cot_got, dn, dn_got) = refs[:12]
-    send_u, keep_u, send_d, keep_d, outs = refs[12:]
+    (dup, dup_got, dbr, dbr_got, act, act_got, low, low_got, cot, cot_got) = refs[:10]
+    send_u, keep_u, send_d, keep_d, outs = refs[10:]
+    width = cot.shape[1]
     index = pl.program_id(0)
     group_at, place_u, place_d = info[0], info[3], info[4]
-    rows = low.shape[0] // (2 * groups)
+    rows = width // (2 * groups)
     quarter = rows // 4
     stay = groups * rows
 
     @pl.when(index == 0)
     def first():
-        found = nn(low[stay:, :], dbr[...]) + nn(low_got[stay:, :], dbr_got[...])
+        found = nn(low[stay:width, :], dbr[...]) + nn(low_got[stay:width, :], dbr_got[...])
         for group in range(groups):
             outs[group] = found[group * rows : (group + 1) * rows]
 
     up = nn(low[:stay, :], dup[...]) + nn(low_got[:stay, :], dup_got[...])
     at = lax.bitwise_xor(lax.bitwise_xor(index, 2), place_u)
-    norms = dn[...] + dn_got[...]
+    fold = low[width:, :].astype(F32) + low_got[width:, :].astype(F32)
+    times = width // fold.shape[1]
+    norms = []
+    for part in range(2):
+        both = fold[2 * part * times : (2 * part + 1) * times]
+        both = both + fold[(2 * part + 1) * times : (2 * part + 2) * times]
+        norms.append(jnp.concatenate([both[k : k + 1] for k in range(times)], axis=1))
+    norms = jnp.concatenate(norms + [jnp.zeros((6, width), F32)], axis=0)
     for group in range(groups):
         spot = lax.rem(group + groups - group_at, groups)
         block = up[group * rows : (group + 1) * rows].astype(BF)
@@ -625,7 +656,7 @@
     size = 512 if seq <= 2048 else 2048
     feats = own_heads * hs
     block_rows = width // wide
-    fast = peers == 2 and n_dp == 4 and block_rows % 32 == 0 and hidden % (4 * 256) == 0
+    fast = peers == 2 and n_dp == 4 and block_rows % 32 == 0 and hidden == 4 * width and width % 256 == 0 and rows % 128 == 0
     me = lax.axis_index("wide")
     group_at, peer_at = me // peers, me % peers
     dp_at = lax.axis_index("dp")
@@ -670,7 +701,9 @@
 
     position = me * rows + jnp.arange(rows, dtype=jnp.int32)
     marked = jnp.where((position < seq_len)[:, None], cluster_ids, -1).T
-    packed = jnp.concatenate([marked, top_keys[0].reshape(heads, own_clusters * picks)], axis=1)
+    packed = jnp.concatenate(
+        [marked, top_keys[0].transpose(0, 2, 1).reshape(heads, own_clusters * picks)], axis=1
+    )
     packed = packed.reshape(groups, own_heads, -1)
 
     def of_heads(hop):
@@ -687,14 +720,26 @@
         mine[hop] = along_groups(ready, -hop)
 
     arrived = jnp.stack(arrived)
-    arrived = jnp.stack([arrived] + [along_peers(arrived, -hop) for hop in range(1, peers)], axis=1)
-    ids_all = arrived[..., :rows].transpose(2, 0, 1, 3).reshape(own_heads, 1, seq)
-    top_all = arrived[..., rows:].reshape(groups, peers, own_heads, own_clusters, picks)
-    top_all = jnp.concatenate([top_all, top_all], axis=0)
-    top_all = lax.dynamic_slice_in_dim(top_all, (groups - group_at) % groups, groups, axis=0)
-    top_all = jnp.concatenate([top_all, top_all], axis=1)
-    top_all = lax.dynamic_slice_in_dim(top_all, (peers - peer_at) % peers, peers, axis=1)
-    top_all = top_all.transpose(2, 4, 0, 1, 3).reshape(own_heads, picks, clusters)
+    others = [arrived] + [along_peers(arrived, -hop) for hop in range(1, peers)]
+    ids_all = jnp.stack([item[..., :rows] for item in others], axis=1)
+    ids_all = ids_all.transpose(2, 0, 1, 3).reshape(own_heads, 1, seq)
+    turned = (ids_all + (clusters - group_at * (clusters // groups))) % clusters
+    ids_all = jnp.where(ids_all < 0, -1, turned)
+    tops = [item[..., rows:] for item in others]
+    if peers == 2:
+        tops = [
+            jnp.where(peer_at == 0, tops[0], tops[1]),
+            jnp.where(peer_at == 0, tops[1], tops[0]),
+        ]
+    else:
+        tops = jnp.stack(tops)
+        tops = [
+            lax.dynamic_index_in_dim(tops, (p + peers - peer_at) % peers, keepdims=False)
+            for p in range(peers)
+        ]
+    top_all = jnp.stack(tops, axis=1).reshape(groups, peers, own_heads, picks, own_clusters)
+    top_all = top_all.transpose(2, 3, 0, 1, 4).reshape(own_heads, picks, clusters)
+    cot_got = [along_peers(cotangent, hop) for hop in range(1, peers)] if fast else []
 
     bias = prefetched(
         functools.partial(bias_kernel, groups=groups, peers=peers, rows=rows),
@@ -718,7 +763,10 @@
     held = []
     split_peers = peers if peers <= 2 else 1
     for group in sorted(range(groups), key=lambda g: min(g, groups - g)):
-        chunk = [mine[group]] + [along_peers(mine[group], -hop) for hop in range(1, peers)]
+        arrival = mine[group]
+        if 1 < group < groups - 1:
+            arrival = after(arrival, bias, held, cot_got)
+        chunk = [arrival] + [along_peers(arrival, -hop) for hop in range(1, peers)]
         if peers > 2:
             chunk = [jnp.concatenate(chunk, axis=0)]
         span = peers * rows
@@ -806,13 +854,23 @@
     column = pl.BlockSpec((rows, part), lambda i, s: (0, i))
     norm_spec = whole((8, width))
     if fast:
-        half_column = pl.BlockSpec((rows, part // 2), lambda i, s: (0, i))
-        kept = [array((rows, hidden // 2), BF), array((width, rows), BF)]
-        kept_specs = [half_column, whole((width, rows))] * 2
-        kept = kept * 2
+        kept_shapes = [
+            array((rows, hidden + hidden // 2 + width), BF),
+            array((width + 16, rows), BF),
+            array((rows, hidden // 2), BF),
+            array((width + 16, rows), BF),
+        ]
+        kept_specs = [whole(item.shape) for item in kept_shapes]
+        kept_specs[2] = pl.BlockSpec((rows, part // 2), lambda i, s: (0, i))
     else:
-        kept = [array((rows, hidden), BF), array((rows, width), BF)]
-        kept_specs = [column, square]
+        kept_shapes = [
+            array((8, width), F32),
+            array((rows, hidden), BF),
+            array((rows, width), BF),
+            array((rows, hidden), BF),
+            array((rows, width), BF),
+        ]
+        kept_specs = [norm_spec, column, square, column, square]
     results = prefetched(
         functools.partial(block_kernel, groups=groups, chunks=chunks, fast=fast),
         (chunks,),
@@ -826,15 +884,9 @@
             pl.BlockSpec((part, width), lambda i, s: (i, 0)),
             square,
         ],
-        [square, square, norm_spec, column, square] + kept_specs + [whole((feats, rows))] * groups,
-        [
-            array((rows, width), BF),
-            array((rows, width), F32),
-            array((8, width), F32),
-            array((rows, hidden), BF),
-            array((rows, width), BF),
-        ]
-        + kept
+        [square, square] + kept_specs + [whole((feats, rows))] * groups,
+        [array((rows, width), BF), array((rows, width), F32)]
+        + kept_shapes
         + [array((feats, rows), BF)] * groups,
         28 if fast else 60,
         cost(8 * rows * width * hidden, 4 * width * hidden, rows * hidden),
@@ -847,26 +899,25 @@
             pltpu.VMEM((rows, width), F32),
         ],
     )(info, *arrived, tokens, gain_row2, shift_row2, w_out_g, w_up, w_down, cotangent)
-    output, d_resid, norm_two, d_up, d_branch = results[:5]
-    kept, d_attn = results[5:-groups], results[-groups:]
+    output, d_resid = results[:2]
+    kept, d_attn = results[2:-groups], results[-groups:]
     grads = [d_attn[0]] + [along_groups(d_attn[hop], -hop) for hop in range(1, groups)]
 
     def weight_parts():
-        dup_got, dbr_got = along_peers(d_up, 1), along_peers(d_branch, 1)
-        act_own, low_own, act_far, low_far = kept
-        act_got, low_got = along_peers(act_far, 1), along_peers(low_far, 1)
-        cot_got, dn_got = along_peers(cotangent, 1), along_peers(norm_two, 1)
+        far, low_far, act_own, low_own = kept
+        got, low_got = along_peers(far, 1), along_peers(low_far, 1)
         high = block_rows + block_rows // 4 + 8
         chunk = pl.BlockSpec((rows, part), lambda i, s: (0, i ^ 2 ^ s[3]))
+        branch = pl.BlockSpec((rows, width), lambda i, s: (0, hidden * 3 // 2 // width))
         act_spec = pl.BlockSpec((rows, part // 2), lambda i, s: (0, i))
-        low_spec = whole((width, rows))
+        act_there = pl.BlockSpec((rows, part // 2), lambda i, s: (0, 2 * hidden // part + i))
+        low_spec = whole((width + 16, rows))
         shape_u = (2, groups, high, width)
         shape_d = (2, groups, block_rows, width)
         send_u, keep_u, send_d, keep_d = prefetched(
             functools.partial(weights_kernel, groups=groups),
             (4,),
-            [chunk, chunk, square, square, act_spec, act_spec, low_spec, low_spec, square, square]
-            + [norm_spec] * 2,
+            [chunk, chunk, branch, branch, act_spec, act_there, low_spec, low_spec, square, square],
             [
                 pl.BlockSpec((1,) + shape_u[1:], lambda i, s: (jnp.minimum(i, 1), 0, 0, 0)),
                 pl.BlockSpec((1,) + shape_u[1:], lambda i, s: (jnp.maximum(i - 2, 0), 0, 0, 0)),
@@ -878,15 +929,12 @@
             cost(8 * rows * width * hidden, 6 * width * hidden),
             "weights",
             scratch=[pltpu.VMEM((groups, block_rows, width), F32)],
-        )(
-            info, d_up, dup_got, d_branch, dbr_got, act_own, act_got, low_own, low_got,
-            cotangent, cot_got, norm_two, dn_got,
-        )
+        )(info, far, got, far, got, act_own, got, low_own, low_got, cotangent, *cot_got)
         return send_u, keep_u, send_d, keep_d
 
-    def weight_sums(keep_u, got_u, keep_d, got_d):
-        high = block_rows + block_rows // 4 + 8
+    def weight_second(keep_u, got_u, keep_d, got_d):
         shape_u, shape_d = keep_u.shape, keep_d.shape
+        high = shape_u[2]
 
         def block(shape, at):
             return pl.BlockSpec((1,) + shape[1:], lambda i: (at, 0, 0, 0))
@@ -901,7 +949,15 @@
             cost_estimate=cost(groups * high * width * 2, groups * high * width * 12),
             name="second",
         )(keep_u, got_u, keep_d, got_d)
-        last_u, last_d = along_dp(next_u, 2), along_dp(next_d, 1)
+        return next_u, next_d
+
+    def weight_third(keep_u, got_u, last_u, keep_d, got_d, last_d):
+        shape_u, shape_d = keep_u.shape, keep_d.shape
+        high = shape_u[2]
+
+        def block(shape, at):
+            return pl.BlockSpec((1,) + shape[1:], lambda i: (at, 0, 0, 0))
+
         tall = high + block_rows
         sums = pl.pallas_call(
             third_kernel,
@@ -921,6 +977,10 @@
             name="third",
         )(keep_u, got_u, last_u, keep_d, got_d, last_d)
         came = [sums[0]] + [along_groups(sums[hop], hop) for hop in range(1, groups)]
+        return came
+
+    def weight_sums(came, shape_u, shape_d):
+        tall = shape_u[2] + shape_d[2]
         done = pl.pallas_call(
             fourth_kernel,
             grid=(1,),
@@ -986,7 +1046,7 @@
         got_u, got_d = along_dp(send_u, 1), along_dp(send_d, 2)
         grads = after(grads, keep_u)
     else:
-        act, normed_two = kept
+        norm_two, d_up, d_branch, act, normed_two = kept
         total_up = reduce_rows(tn(normed_two, d_up).astype(BF))
         total_down = reduce_rows(tn(act, cotangent).astype(BF))
         found = jnp.stack([nn(item, d_branch).astype(BF) for item in arrived])
@@ -1011,50 +1071,48 @@
     )(ids_all, *grads, mixed)
     share_got = [along_peers(share, hop) for hop in range(1, peers)]
 
-    grads = after(grads, share)
-    dq_member, dkv_own, dkv_send = pl.pallas_call(
-        functools.partial(member_kernel, size=size, groups=groups),
+    back_shapes = [
+        array((groups, feats, rows), BF),
+        array((own_heads, 2 * hs, own_rows), F32),
+        array((own_heads, 2 * hs, max(peers - 1, 1) * own_rows), BF),
+    ]
+    dq, dkv_own, dkv_send = pl.pallas_call(
+        functools.partial(back_kernel, size=size, groups=groups, gots=len(share_got)),
         grid=(own_heads,),
         in_specs=[ids_one, feat_one, kv_one, bias_one]
         + [rows_one] * groups
-        + [mix_one, stat_one],
+        + [mix_one, stat_one, cen_one]
+        + [part_one] * (1 + len(share_got)),
         out_specs=[
             all_groups,
-            own_one,
-            pl.BlockSpec((1, max(peers - 1, 1) * own_rows, 2 * hs), lambda h: (h, 0, 0)),
+            pl.BlockSpec((1,) + back_shapes[1].shape[1:], lambda h: (h, 0, 0)),
+            pl.BlockSpec((1,) + back_shapes[2].shape[1:], lambda h: (h, 0, 0)),
         ],
-        out_shape=[
-            array((groups, feats, rows), F32),
-            array((own_heads, own_rows, 2 * hs), F32),
-            array((own_heads, max(peers - 1, 1) * own_rows, 2 * hs), BF),
-        ],
-        scratch_shapes=[pltpu.VMEM((seq, 2 * hs), F32)],
-        compiler_params=params(32 if fast else 60, 1),
-        cost_estimate=cost(12 * pair_flops, 10e6, own_heads * own_rows * seq),
-        name="member",
-    )(ids_all, feat, kv, bias, *grads, mixed, stats)
+        out_shape=back_shapes,
+        scratch_shapes=[pltpu.VMEM((seq, 2 * hs), F32), pltpu.VMEM((seq, 2 * clusters), BF)],
+        compiler_params=params(36 if fast else 62, 1),
+        cost_estimate=cost(14 * pair_flops, 10e6, own_heads * own_rows * seq),
+        name="back",
+    )(ids_all, feat, kv, bias, *grads, mixed, stats, centroid, share, *share_got)
     dkv_got = [
         along_peers(
-            dkv_send if peers == 2 else dkv_send[:, (hop - 1) * own_rows : hop * own_rows], hop
+            dkv_send if peers == 2 else dkv_send[..., (hop - 1) * own_rows : hop * own_rows], hop
         )
         for hop in range(1, peers)
     ]
-    share_total = share
-    for got in share_got:
-        share_total = share_total + got
-
+    if fast:
+        dkv_own = after(dkv_own, got_d)
     d_in = pl.pallas_call(
-        functools.partial(centroid_kernel, size=size, groups=groups, gots=len(dkv_got)),
-        grid=(own_heads,),
-        in_specs=[ids_one, feat_one, kv_one, bias_one, part_one, stat_one, cen_one, all_groups]
-        + [own_one] * (1 + len(dkv_got)),
-        out_specs=[pl.BlockSpec((1, 3 * hs, rows), lambda h: (h, 0, 0))] * groups,
+        functools.partial(join_kernel, groups=groups),
+        grid=(1,),
+        in_specs=[whole(back_shapes[0].shape), whole(back_shapes[1].shape)]
+        + [whole(back_shapes[1].shape)] * len(dkv_got),
+        out_specs=[whole((own_heads, 3 * hs, rows))] * groups,
         out_shape=[array((own_heads, 3 * hs, rows), BF)] * groups,
-        scratch_shapes=[pltpu.VMEM((seq, 2 * clusters), BF)],
-        compiler_params=params(28 if fast else 60, 1),
-        cost_estimate=cost(own_heads * clusters * seq * 1024, 8e6, own_heads * clusters * seq),
-        name="centroid",
-    )(ids_all, feat, kv, bias, share_total, stats, centroid, dq_member, dkv_own, *dkv_got)
+        compiler_params=params(20, 1),
+        cost_estimate=cost(own_rows * feats * 8, own_rows * feats * 16),
+        name="join",
+    )(dq, dkv_own, *dkv_got)
 
     home = [d_in[0]] + [along_groups(d_in[hop], hop) for hop in range(1, groups)]
 
@@ -1070,19 +1128,24 @@
     if fast:
         half = groups // 2
         blocks = (groups, tall, 3 * feats)
+        next_u, next_d = weight_second(keep_u, after(got_u, dq), keep_d, after(got_d, dq))
+        last_u, last_d = along_dp(next_u, 2), along_dp(next_d, 1)
         keep, far = inward(
             [whole(blocks)] * 2, [array(blocks, BF)] * 2, 24, spent, "inward"
-        )(info, *d_in, hat_own)
-        got = along_peers(far, 1)
+        )(info, *after(d_in, last_u, last_d), hat_own)
+        came = weight_third(keep_u, got_u, last_u, keep_d, got_d, last_d)
+        got = along_peers(after(far, home, came[0]), 1)
         total = keep.astype(F32) + got.astype(F32)
         one_half, two_half = total[:half].astype(BF), total[half:].astype(BF)
-        total_up, total_out, total_down, norm_own = weight_sums(
-            keep_u, after(got_u, keep), keep_d, after(got_d, keep)
-        )
         for mask in (1, 2):
             got_one, got_two = along_dp(one_half, mask), along_dp(two_half, 3 - mask)
             one_half = (one_half.astype(F32) + got_one.astype(F32)).astype(BF)
             two_half = (two_half.astype(F32) + got_two.astype(F32)).astype(BF)
+            if mask == 1:
+                one_half, two_half = after((one_half, two_half), came)
+        total_up, total_out, total_down, norm_own = weight_sums(
+            came, keep_u.shape, keep_d.shape
+        )
         items = [one_half[k] for k in range(half)] + [two_half[k] for k in range(half)]
     else:
         found, more = inward(

time: 312 us -> 266 us (0.85)
  waiting for transfers between devices: 124 us -> 87.7 us
  Pallas kernels: 87.4 us -> 81.9 us
  starting transfers between devices: 46.6 us -> 42.3 us
    ppermute x11, waiting for transfers between devices: 51.8 us -> 35.3 us  [along_dp(): return lax.ppermute(values, 'dp', [(i, i ^ mask) for i in range(n_dp)])]
    ppermute x21, waiting for transfers between devices: 65.5 us -> 50 us  [along_groups(): return lax.ppermute(values, 'wide', pairs)]
    pallas_call x4, Pallas kernels: 25.9 us -> 21.3 us  [the longest x1 20.3 us: per_device(): pl.pallas_call(functools.partial(back_kernel, size=size, groups=groups, g...]
    ppermute x14 -> x11, waiting for transfers between devices: 7.04 us -> 2.42 us  [along_peers(): return lax.ppermute(values, 'wide', pairs)]
    another operation x0 -> x4, local copies, waits for them, and re-layouts: none -> 4.28 us  [the longest x2 3.06 us: per_device(): jnp.stack(tops, axis=1)]
    ppermute x21, starting transfers between devices: 29.9 us -> 26.5 us  [along_groups(): return lax.ppermute(values, 'wide', pairs)]
    unnamed x87 -> x57, local copies, waits for them, and re-layouts: 15.7 us -> 12.3 us
    slice x5 -> x6, local copies, waits for them, and re-layouts: 4.98 us -> 1.65 us  [per_device(): q_part, kv_part = (q_part[:block_rows], kv_part[:block_rows])]
  transfers between devices with their start and end apart: 46 -> 43, of which waited for: 18 -> 21; matrix products, arithmetic and copies ran while one was open for 12% -> 13% of each run, Pallas kernels for 9% -> 21%
where the time goes in v4:
time: 266 us; the launch traced here: 263 us
  waiting for transfers between devices  87.7 us (33%)
  Pallas kernels  81.9 us (31%)
  starting transfers between devices  42.3 us (16%)
  local copies, waits for them, and re-layouts  34.5 us (13%)
  other arithmetic  15.1 us (6%)
    ppermute x21, waiting for transfers between devices, along_groups(): return lax.ppermute(values, 'wide', pairs)  50 us
    ppermute x11, waiting for transfers between devices, along_dp(): return lax.ppermute(values, 'dp', [(i, i ^ mask) for i in range(n_dp)])  35.3 us
    ppermute x21, starting transfers between devices, along_groups(): return lax.ppermute(values, 'wide', pairs)  26.5 us
    pallas_call x1, Pallas kernels, per_device(): pl.pallas_call(functools.partial(back_kernel, size=size, groups=groups, g...  20.3 us
    ppermute x11, starting transfers between devices, along_dp(): return lax.ppermute(values, 'dp', [(i, i ^ mask) for i in range(n_dp)])  13.7 us
    pallas_call x1, Pallas kernels, per_device(): pl.pallas_call(functools.partial(forward_kernel, size=size, groups=groups...  13 us
    unnamed x57, local copies, waits for them, and re-layouts  12.3 us
    pallas_call x4, Pallas kernels, per_device(): prefetched(functools.partial(project_kernel, peers=split_peers, olds=len(...  11.3 us
  transfers between devices with their start and end apart: 43, of which 21 were waited for; matrix products, arithmetic and copies ran while one was open for 13% of the time, Pallas kernels for 21%

profile of v4, /device:TPU:8, one launch (start us, length us, event | category | flops | bytes accessed | tf_op | source)
XLA Modules:
  0.0 263.5 jit_solution(16860018207554256394)
XLA Ops:
  4.1 3.9 %collective-permute-start = (s32[3,768]{1,0:T(4,128)}, s32[3,768]{1,0:T(4,128)}, u32[]{:S(2)}, u32[]{:S(2)}) collective-permute-start(s32[3,768]{1,0:T(4,128)} %get-tuple-element.172), channel_id=1, source_target_pairs={{0,6},{1,7},{2,0},{3,1},{4,2},{5,3},{6,4},{7,5},{8,14},{9,15},{10,... | collective-permute-start | bytes 27656 | tf_op jit(solution)/shard_map/ppermute | solution.py:670
  8.0 1.9 collective-permute-start.2
  9.9 2.8 %copy.63 = bf16[768,1536]{0,1:T(8,128)(2,1)S(1)} copy(bf16[768,1536]{1,0:T(8,128)(2,1)} %param.21) | data formatting | bytes 4718592 | tf_op args[7]
  12.8 1.6 copy.62
  14.4 2.0 pad_maximum_fusion
  16.4 2.3 copy.64
  18.8 1.6 collective-permute-start.5
  24.5 1.5 stack.81
  27.4 1.5 stack.82
  31.5 1.8 add_bitcast_fusion
  33.3 1.8 copy.60
  35.1 1.7 copy.61.top_ref
  43.0 7.4 %bias.1 = bf16[3,2048,128]{2,1,0:T(8,128)(2,1)S(1)} custom-call(s32[6]{0:T(128)S(1)} %stack.73.info, s32[3,32,128]{2,1,0:T(8,128)S(1)} %copy-done.12), custom_call_target="tpu_custom_call" | custom-call | flops 201326592 | bytes 1572864 | tf_op jit(solution)/shard_map/bias/pallas_call | solution.py:744
  50.5 2.7 %project.4 = (bf16[768,1024]{1,0:T(8,128)(2,1)S(1)}, bf16[3,192,2048]{2,1,0:T(8,128)(2,1)S(1)}, bf16[3,2048,128]{2,1,0:T(8,128)(2,1)S(1)}) custom-call(s32[6]{0:T(128)S(1)} %stack.73.info, bf16[256,768]{1,0:T(8,128)(2,1)S(1)} %copy-done, bf16[256,768]{1,0:T(8,128)(2,1)} %collective-permute-done.9.refs_1_, f32[1,768]{1,0:T(1,128)S(1)} %broadcast_in_dim.34.refs_2_.refs_6_, ...), custom_call_target="tpu_custom_call" | custom-call | flops 452984832 | bytes 1572864 | tf_op jit(solution)/shard_map/project/pallas_call | solution.py:790
  53.2 2.8 %project.5 = (bf16[768,1024]{1,0:T(8,128)(2,1)S(1)}, bf16[3,192,2048]{2,1,0:T(8,128)(2,1)S(1)}, bf16[3,2048,128]{2,1,0:T(8,128)(2,1)S(1)}) custom-call(s32[6]{0:T(128)S(1)} %stack.73.info, bf16[256,768]{1,0:T(8,128)(2,1)} %collective-permute-done.4.refs_0_, ...), custom_call_target="tpu_custom_call", output_to_operand_aliasing={{0}: (6, {}), {1}: (7, {}), {2}: (8, {})} | custom-call | flops 452984832 | bytes 1572864 | tf_op jit(solution)/shard_map/project/pallas_call | solution.py:790
  56.1 2.8 %project.6 = (bf16[768,1024]{1,0:T(8,128)(2,1)S(1)}, bf16[3,192,2048]{2,1,0:T(8,128)(2,1)S(1)}, bf16[3,2048,128]{2,1,0:T(8,128)(2,1)S(1)}) custom-call(s32[6]{0:T(128)S(1)} %stack.73.info, bf16[256,768]{1,0:T(8,128)(2,1)} %collective-permute-done.5.refs_0_, ...), custom_call_target="tpu_custom_call", output_to_operand_aliasing={{0}: (6, {}), {1}: (7, {}), {2}: (8, {})} | custom-call | flops 452984832 | bytes 1572864 | tf_op jit(solution)/shard_map/project/pallas_call | solution.py:790
  59.1 1.8 collective-permute-done.11.refs_1_
  60.9 3.0 %project.7 = (bf16[768,1024]{1,0:T(8,128)(2,1)S(1)}, bf16[3,192,2048]{2,1,0:T(8,128)(2,1)S(1)}, bf16[3,2048,128]{2,1,0:T(8,128)(2,1)S(1)}) custom-call(s32[6]{0:T(128)S(1)} %stack.73.info, bf16[256,768]{1,0:T(8,128)(2,1)} %collective-permute-done.6.refs_0_, ...), custom_call_target="tpu_custom_call", output_to_operand_aliasing={{0}: (6, {}), {1}: (7, {}), {2}: (8, {})} | custom-call | flops 452984832 | bytes 1572864 | tf_op jit(solution)/shard_map/project/pallas_call | solution.py:790
  64.0 13.0 %attend.1 = (bf16[192,256]{1,0:T(8,128)(2,1)S(1)}, bf16[192,256]{1,0:T(8,128)(2,1)S(1)}, bf16[192,256]{1,0:T(8,128)(2,1)S(1)}, bf16[192,256]{1,0:T(8,128)(2,1)S(...) custom-call(s32[3,1,2048]{2,1,0:T(1,128)S(1)} %fusion.5.ids_all.ids_own, ...), custom_call_target="tpu_custom_call" | custom-call | flops 9663676416 | bytes 8000000 | tf_op jit(solution)/shard_map/attend/pallas_call | solution.py:829
  77.0 2.2 collective-permute-start.12
  79.3 1.7 collective-permute-start.13
  81.0 5.6 %collective-permute-done.12.refs_1_ = bf16[192,256]{1,0:T(8,128)(2,1)S(1)} collective-permute-done((bf16[192,256]{1,0:T(8,128)(2,1)S(1)}, bf16[192,256]{1,0:T(8,128)(2,1)S(1)}, u32[]{:S(2)}, u32[]{:S(2)}) %collective-permute-start.12) | collective-permute-done | bytes 98336 | tf_op jit(solution)/shard_map/ppermute | solution.py:670
  89.5 10.0 %feed.1 = (bf16[256,768]{1,0:T(8,128)(2,1)}, f32[256,768]{1,0:T(8,128)S(1)}, bf16[256,5376]{1,0:T(8,128)(2,1)S(1)}, bf16[784,256]{1,0:T(8,128)(2,1)S(1)}, bf16[2...) custom-call(s32[6]{0:T(128)S(1)} %stack.73.info, ...), custom_call_target="tpu_custom_call" | custom-call | flops 4831838208 | bytes 9437184 | tf_op jit(solution)/shard_map/feed/pallas_call | solution.py:874
  101.1 1.7 collective-permute-start.16
  102.8 2.9 %collective-permute-start.17 = (bf16[192,256]{1,0:T(8,128)(2,1)S(1)}, bf16[192,256]{1,0:T(8,128)(2,1)S(1)}, u32[]{:S(2)}, u32[]{:S(2)}) collective-permute-start(bf16[192,256]{1,0:T(8,128)(2,1)S(1)} %get-tuple-element.102), channel_id=1, source_target_pairs={{0,2},{1,3},{2,4},{3,5},{4,6},{5,7},{6,0},{7,1},{8,10},{9,11},{10,... | collective-permute-start | bytes 294920 | tf_op jit(solution)/shard_map/ppermute | solution.py:670
  106.1 8.0 %weights.1 = (bf16[2,4,128,768]{3,2,1,0:T(8,128)(2,1)S(1)}, bf16[2,4,128,768]{3,2,1,0:T(8,128)(2,1)S(1)}, bf16[2,4,96,768]{3,2,1,0:T(8,128)(2,1)S(1)}, bf16[2,4,96,768]{3,2,1,0:T(8,128)(2,1)S(1)}) custom-call(s32[6]{0:T(128)S(1)} %stack.73.info, bf16[256,5376]{1,0:T(8,128)(2,1)S(1)} %get-tuple-element.103.refs_0_.refs_2_, ...), custom_call_target="tpu_custom_call" | custom-call | flops 4831838208 | bytes 14155776 | tf_op jit(solution)/shard_map/weights/pallas_call | solution.py:917
  115.1 1.5 collective-permute-start.21
  118.1 20.3 %back.1 = (bf16[4,192,256]{2,1,0:T(8,128)(2,1)S(1)}, f32[3,128,1024]{2,1,0:T(8,128)S(1)}, bf16[3,128,1024]{2,1,0:T(8,128)(2,1)S(1)}) custom-call(s32[3,1,2048]{2,1,0:T(1,128)S(1)} %fusion.5.ids_all.ids_own, bf16[3,192,2048]{2,1,0:T(8,128)(2,1)S(1)} %get-tuple-element.92.feat, bf16[3,2048,128]{2,1,0:T(8,128)(2,1)S(1)} %get-tuple-element.93.kv, ...), custom_call_target="tpu_custom_call" | custom-call | flops 22548578304 | bytes 10000000 | tf_op jit(solution)/shard_map/back/pallas_call | solution.py:1079
  138.5 4.9 %collective-permute-done.21.got_d = bf16[2,4,96,768]{3,2,1,0:T(8,128)(2,1)S(1)} collective-permute-done((bf16[2,4,96,768]{3,2,1,0:T(8,128)(2,1)S(1)}, bf16[2,4,96,768]{3,2,1,0:T(8,128)(2,1)S(1)}, u32[]{:S(2)}, u32[]{:S(2)}) %collective-permute-start.21) | collective-permute-done | bytes 1179680 | tf_op jit(solution)/shard_map/ppermute | solution.py:677
  143.4 9.6 %collective-permute-done.26.got_u = bf16[2,4,128,768]{3,2,1,0:T(8,128)(2,1)S(1)} collective-permute-done((bf16[2,4,128,768]{3,2,1,0:T(8,128)(2,1)S(1)}, bf16[2,4,128,768]{3,2,1,0:T(8,128)(2,1)S(1)}, u32[]{:S(2)}, u32[]{:S(2)}) %collective-permute-start.26) | collective-permute-done | bytes 1572896 | tf_op jit(solution)/shard_map/ppermute | solution.py:677
  155.7 2.5 collective-permute-start.24
  159.6 8.5 %collective-permute-done.28.last_d = bf16[4,96,768]{2,1,0:T(8,128)(2,1)S(1)} collective-permute-done((bf16[4,96,768]{2,1,0:T(8,128)(2,1)S(1)}, bf16[4,96,768]{2,1,0:T(8,128)(2,1)S(1)}, u32[]{:S(2)}, u32[]{:S(2)}) %collective-permute-start.28) | collective-permute-done | bytes 589856 | tf_op jit(solution)/shard_map/ppermute | solution.py:677
  168.1 4.0 %collective-permute-done.27.last_u = bf16[4,128,768]{2,1,0:T(8,128)(2,1)S(1)} collective-permute-done((bf16[4,128,768]{2,1,0:T(8,128)(2,1)S(1)}, bf16[4,128,768]{2,1,0:T(8,128)(2,1)S(1)}, u32[]{:S(2)}, u32[]{:S(2)}) %collective-permute-start.27) | collective-permute-done | bytes 786464 | tf_op jit(solution)/shard_map/ppermute | solution.py:677
  172.6 2.3 inward.1
  175.7 4.4 %collective-permute-done.24.refs_2_ = bf16[3,192,256]{2,1,0:T(8,128)(2,1)S(1)} collective-permute-done((bf16[3,192,256]{2,1,0:T(8,128)(2,1)S(1)}, bf16[3,192,256]{2,1,0:T(8,128)(2,1)S(1)}, u32[]{:S(2)}, u32[]{:S(2)}) %collective-permute-start.24) | collective-permute-done | bytes 294944 | tf_op jit(solution)/shard_map/ppermute | solution.py:670
  180.1 2.8 %collective-permute-done.25.refs_3_ = bf16[3,192,256]{2,1,0:T(8,128)(2,1)S(1)} collective-permute-done((bf16[3,192,256]{2,1,0:T(8,128)(2,1)S(1)}, bf16[3,192,256]{2,1,0:T(8,128)(2,1)S(1)}, u32[]{:S(2)}, u32[]{:S(2)}) %collective-permute-start.25) | collective-permute-done | bytes 294944 | tf_op jit(solution)/shard_map/ppermute | solution.py:670
  183.7 1.9 collective-permute-start.34
  187.9 5.8 %collective-permute-done.32.refs_1_ = bf16[224,768]{1,0:T(8,128)(2,1)S(1)} collective-permute-done((bf16[224,768]{1,0:T(8,128)(2,1)S(1)}, bf16[224,768]{1,0:T(8,128)(2,1)S(1)}, u32[]{:S(2)}, u32[]{:S(2)}) %collective-permute-start.32) | collective-permute-done | bytes 344096 | tf_op jit(solution)/shard_map/ppermute | solution.py:670
  193.7 19.5 %collective-permute-done.33.refs_2_ = bf16[224,768]{1,0:T(8,128)(2,1)S(1)} collective-permute-done((bf16[224,768]{1,0:T(8,128)(2,1)S(1)}, bf16[224,768]{1,0:T(8,128)(2,1)S(1)}, u32[]{:S(2)}, u32[]{:S(2)}) %collective-permute-start.33) | collective-permute-done | bytes 344096 | tf_op jit(solution)/shard_map/ppermute | solution.py:670
  228.1 2.9 %final.1 = bf16[256,768]{1,0:T(8,128)(2,1)} custom-call(s32[6]{0:T(128)S(1)} %stack.73.info, bf16[3,192,256]{2,1,0:T(8,128)(2,1)S(1)} %copy-done.5, bf16[3,192,256]{2,1,0:T(8,128)(2,1)S(1)} %copy-done.7, bf16[3,192,256]{2,1,0:T(8,128)(2,1)S(1)} %copy-done.9, bf16[3,192,256]{2,1,0:T(8,128)(2,1)S(1)} %copy-done.11, bf16[256,768]{1,0:T(8,128)(2,1)S(1)} %copy-done.1, ...), custom_call_target="tpu_custom_call" | custom-call | flops 905969664 | bytes 3538944 | tf_op jit(solution)/shard_map/final/pallas_call | solution.py:1179
  231.0 3.6 %collective-permute-done.41.from_y = bf16[224,768]{1,0:T(8,128)(2,1)} collective-permute-done((bf16[224,768]{1,0:T(8,128)(2,1)}, bf16[224,768]{1,0:T(8,128)(2,1)}, u32[]{:S(2)}, u32[]{:S(2)}) %collective-permute-start.41) | collective-permute-done | bytes 344096 | tf_op jit(solution)/shard_map/ppermute | solution.py:677
  234.6 3.9 %spread.1 = (f32[96,3072]{1,0:T(8,128)}, f32[96,768]{1,0:T(8,128)}, f32[384,768]{1,0:T(8,128)}, f32[8,768]{1,0:T(8,128)S(1)}) custom-call(s32[6]{0:T(128)S(1)} %stack.73.info, bf16[224,768]{1,0:T(8,128)(2,1)} %fourth.1.own, bf16[224,768]{1,0:T(8,128)(2,1)} %collective-permute-done.40.from_x, bf16[224,768]{1,0:T(8,128)(2,1)} %collective-permute-done.41.from_y, ...), custom_call_target="tpu_custom_call" | custom-call | flops 1000000 | bytes 4128768 | tf_op jit(solution)/shard_map/spread/pallas_call | solution.py:996
  238.6 1.5 collective-permute-start.37
  241.3 4.7 %collective-permute-done.37 = bf16[2,112,576]{2,1,0:T(8,128)(2,1)S(1)} collective-permute-done((bf16[2,112,576]{2,1,0:T(8,128)(2,1)S(1)}, bf16[2,112,576]{2,1,0:T(8,128)(2,1)S(1)}, u32[]{:S(2)}, u32[]{:S(2)}) %collective-permute-start.37) | collective-permute-done | bytes 258080 | tf_op jit(solution)/shard_map/ppermute | solution.py:677
  246.1 2.0 collective-permute-start.38
  248.6 5.7 %collective-permute-done.38 = bf16[112,576]{1,0:T(8,128)(2,1)S(1)} collective-permute-done((bf16[112,576]{1,0:T(8,128)(2,1)S(1)}, bf16[112,576]{1,0:T(8,128)(2,1)S(1)}, u32[]{:S(2)}, u32[]{:S(2)}) %collective-permute-start.38) | collective-permute-done | bytes 129056 | tf_op jit(solution)/shard_map/ppermute | solution.py:670
  258.5 2.0 fusion.1
  260.5 1.8 fusion.4
  (176 shorter events, 55.0 us)
Async XLA Ops:
  0.6 49.8 %collective-permute-start.9 = (bf16[256,768]{1,0:T(8,128)(2,1)}, bf16[256,768]{1,0:T(8,128)(2,1)}, u32[]{:S(2)}, u32[]{:S(2)}) collective-permute-start(bf16[256,768]{1,0:T(8,128)(2,1)} %refs_4_.3), channel_id=1, source_target_pairs={{0,1},{1,0},{2,3},{3,2},{4,5},{5,4},{6,7},{7,6},{8,9},{9,8},{10,11... | collective-permute-start | bytes 1179656 | tf_op jit(solution)/shard_map/ppermute | solution.py:674
  3.3 25.6 %collective-permute-start.4 = (bf16[256,768]{1,0:T(8,128)(2,1)}, bf16[256,768]{1,0:T(8,128)(2,1)}, u32[]{:S(2)}, u32[]{:S(2)}) collective-permute-start(bf16[256,768]{1,0:T(8,128)(2,1)} %refs_4_.3), channel_id=1, source_target_pairs={{0,6},{1,7},{2,0},{3,1},{4,2},{5,3},{6,4},{7,5},{8,14},{9,15},{10,... | collective-permute-start | bytes 1179656 | tf_op jit(solution)/shard_map/ppermute | solution.py:670
  4.1 14.7 %collective-permute-start = (s32[3,768]{1,0:T(4,128)}, s32[3,768]{1,0:T(4,128)}, u32[]{:S(2)}, u32[]{:S(2)}) collective-permute-start(s32[3,768]{1,0:T(4,128)} %get-tuple-element.172), channel_id=1, source_target_pairs={{0,6},{1,7},{2,0},{3,1},{4,2},{5,3},{6,4},{7,5},{8,14},{9,15},{10,... | collective-permute-start | bytes 27656 | tf_op jit(solution)/shard_map/ppermute | solution.py:670
  8.0 12.3 %collective-permute-start.1 = (s32[3,768]{1,0:T(4,128)}, s32[3,768]{1,0:T(4,128)}, u32[]{:S(2)}, u32[]{:S(2)}) collective-permute-start(s32[3,768]{1,0:T(4,128)} %get-tuple-element.171), channel_id=1, source_target_pairs={{0,4},{1,5},{2,6},{3,7},{4,0},{5,1},{6,2},{7,3},{8,12},{9,13},{10,... | collective-permute-start | bytes 27656 | tf_op jit(solution)/shard_map/ppermute | solution.py:670
  8.0 12.3 %collective-permute-start.2 = (s32[3,768]{1,0:T(4,128)}, s32[3,768]{1,0:T(4,128)}, u32[]{:S(2)}, u32[]{:S(2)}) collective-permute-start(s32[3,768]{1,0:T(4,128)} %get-tuple-element.170), channel_id=1, source_target_pairs={{0,2},{1,3},{2,4},{3,5},{4,6},{5,7},{6,0},{7,1},{8,10},{9,11},{10,... | collective-permute-start | bytes 27656 | tf_op jit(solution)/shard_map/ppermute | solution.py:670
  18.8 10.7 %collective-permute-start.5 = (bf16[256,768]{1,0:T(8,128)(2,1)}, bf16[256,768]{1,0:T(8,128)(2,1)}, u32[]{:S(2)}, u32[]{:S(2)}) collective-permute-start(bf16[256,768]{1,0:T(8,128)(2,1)} %refs_4_.3), channel_id=1, source_target_pairs={{0,2},{1,3},{2,4},{3,5},{4,6},{5,7},{6,0},{7,1},{8,10},{9,11},{10,... | collective-permute-start | bytes 1179656 | tf_op jit(solution)/shard_map/ppermute | solution.py:670
  20.4 38.6 %collective-permute-start.10 = (bf16[256,768]{1,0:T(8,128)(2,1)}, bf16[256,768]{1,0:T(8,128)(2,1)}, u32[]{:S(2)}, u32[]{:S(2)}) collective-permute-start(bf16[256,768]{1,0:T(8,128)(2,1)} %refs_8_.3), channel_id=1, source_target_pairs={{0,1},{1,0},{2,3},{3,2},{4,5},{5,4},{6,7},{7,6},{8,9},{9,8},{10,11... | collective-permute-start | bytes 1179656 | tf_op jit(solution)/shard_map/ppermute | solution.py:674
  21.1 1.5 collective-permute-start.3
  29.5 29.4 %collective-permute-start.6 = (bf16[256,768]{1,0:T(8,128)(2,1)}, bf16[256,768]{1,0:T(8,128)(2,1)}, u32[]{:S(2)}, u32[]{:S(2)}) collective-permute-start(bf16[256,768]{1,0:T(8,128)(2,1)} %refs_4_.3), channel_id=1, source_target_pairs={{0,4},{1,5},{2,6},{3,7},{4,0},{5,1},{6,2},{7,3},{8,12},{9,13},{10,... | collective-permute-start | bytes 1179656 | tf_op jit(solution)/shard_map/ppermute | solution.py:670
  31.0 22.2 %collective-permute-start.8 = (bf16[256,768]{1,0:T(8,128)(2,1)}, bf16[256,768]{1,0:T(8,128)(2,1)}, u32[]{:S(2)}, u32[]{:S(2)}) collective-permute-start(bf16[256,768]{1,0:T(8,128)(2,1)} %collective-permute-done.4.refs_0_), channel_id=1, source_target_pairs={{0,1},{1,0},{2,3},{3,2},{4,5},{5,4},{6,7},{7,6},{8,9},{9,8},{10,11... | collective-permute-start | bytes 1179656 | tf_op jit(solution)/shard_map/ppermute | solution.py:674
  31.0 25.1 %collective-permute-start.7 = (bf16[256,768]{1,0:T(8,128)(2,1)}, bf16[256,768]{1,0:T(8,128)(2,1)}, u32[]{:S(2)}, u32[]{:S(2)}) collective-permute-start(bf16[256,768]{1,0:T(8,128)(2,1)} %collective-permute-done.5.refs_0_), channel_id=1, source_target_pairs={{0,1},{1,0},{2,3},{3,2},{4,5},{5,4},{6,7},{7,6},{8,9},{9,8},{10,11... | collective-permute-start | bytes 1179656 | tf_op jit(solution)/shard_map/ppermute | solution.py:674
  58.9 2.0 collective-permute-start.11
  60.9 28.5 %slice-start = ((s8[4718592]{0:T(1024)(128)(4,1)}), s8[4194304]{0:T(1024)(128)(4,1)S(1)}, s32[]{:S(2)}) async-start(s8[4718592]{0:T(1024)(128)(4,1)} %bitcast.67), calls=%async_computation | async-start | bytes 8388608
  60.9 28.5 %slice-start.2 = ((s8[4718592]{0:T(1024)(128)(4,1)}), s8[524288]{0:T(1024)(128)(4,1)S(1)}, s32[]{:S(2)}) async-start(s8[4718592]{0:T(1024)(128)(4,1)} %bitcast.69), calls=%async_computation.2 | async-start | bytes 1048576
  77.0 9.6 %collective-permute-start.12 = (bf16[192,256]{1,0:T(8,128)(2,1)S(1)}, bf16[192,256]{1,0:T(8,128)(2,1)S(1)}, u32[]{:S(2)}, u32[]{:S(2)}) collective-permute-start(bf16[192,256]{1,0:T(8,128)(2,1)S(1)} %get-tuple-element.95), channel_id=1, source_target_pairs={{0,2},{1,3},{2,4},{3,5},{4,6},{5,7},{6,0},{7,1},{8,10},{9,11},{10,... | collective-permute-start | bytes 294920 | tf_op jit(solution)/shard_map/ppermute | solution.py:670
  79.3 8.7 %collective-permute-start.13 = (bf16[192,256]{1,0:T(8,128)(2,1)S(1)}, bf16[192,256]{1,0:T(8,128)(2,1)S(1)}, u32[]{:S(2)}, u32[]{:S(2)}) collective-permute-start(bf16[192,256]{1,0:T(8,128)(2,1)S(1)} %get-tuple-element.96), channel_id=1, source_target_pairs={{0,4},{1,5},{2,6},{3,7},{4,0},{5,1},{6,2},{7,3},{8,12},{9,13},{10,... | collective-permute-start | bytes 294920 | tf_op jit(solution)/shard_map/ppermute | solution.py:670
  81.0 8.4 %collective-permute-start.14 = (bf16[192,256]{1,0:T(8,128)(2,1)S(1)}, bf16[192,256]{1,0:T(8,128)(2,1)S(1)}, u32[]{:S(2)}, u32[]{:S(2)}) collective-permute-start(bf16[192,256]{1,0:T(8,128)(2,1)S(1)} %get-tuple-element.97), channel_id=1, source_target_pairs={{0,6},{1,7},{2,0},{3,1},{4,2},{5,3},{6,4},{7,5},{8,14},{9,15},{10,... | collective-permute-start | bytes 294920 | tf_op jit(solution)/shard_map/ppermute | solution.py:670
  100.4 5.7 %collective-permute-start.18 = (bf16[256,5376]{1,0:T(8,128)(2,1)S(1)}, bf16[256,5376]{1,0:T(8,128)(2,1)S(1)}, u32[]{:S(2)}, u32[]{:S(2)}) collective-permute-start(bf16[256,5376]{1,0:T(8,128)(2,1)S(1)} %get-tuple-element.103.refs_0_.refs_2_), channel_id=1, source_target_pairs={{0,1},{1,0},{2,3},{3,2},{4,5},{5,4},{6,7},{7,6},{8,9},{9,8},{10,11... | collective-permute-start | bytes 8257544 | tf_op jit(solution)/shard_map/ppermute | solution.py:674
  100.4 5.7 %collective-permute-start.19 = (bf16[784,256]{1,0:T(8,128)(2,1)S(1)}, bf16[784,256]{1,0:T(8,128)(2,1)S(1)}, u32[]{:S(2)}, u32[]{:S(2)}) collective-permute-start(bf16[784,256]{1,0:T(8,128)(2,1)S(1)} %get-tuple-element.106), channel_id=1, source_target_pairs={{0,1},{1,0},{2,3},{3,2},{4,5},{5,4},{6,7},{7,6},{8,9},{9,8},{10,11... | collective-permute-start | bytes 1204232 | tf_op jit(solution)/shard_map/ppermute | solution.py:674
  100.9 13.2 %collective-permute-start.15 = (bf16[192,256]{1,0:T(8,128)(2,1)S(1)}, bf16[192,256]{1,0:T(8,128)(2,1)S(1)}, u32[]{:S(2)}, u32[]{:S(2)}) collective-permute-start(bf16[192,256]{1,0:T(8,128)(2,1)S(1)} %get-tuple-element.100), channel_id=1, source_target_pairs={{0,6},{1,7},{2,0},{3,1},{4,2},{5,3},{6,4},{7,5},{8,14},{9,15},{10,... | collective-permute-start | bytes 294920 | tf_op jit(solution)/shard_map/ppermute | solution.py:670
  101.1 13.0 %collective-permute-start.16 = (bf16[192,256]{1,0:T(8,128)(2,1)S(1)}, bf16[192,256]{1,0:T(8,128)(2,1)S(1)}, u32[]{:S(2)}, u32[]{:S(2)}) collective-permute-start(bf16[192,256]{1,0:T(8,128)(2,1)S(1)} %get-tuple-element.101), channel_id=1, source_target_pairs={{0,4},{1,5},{2,6},{3,7},{4,0},{5,1},{6,2},{7,3},{8,12},{9,13},{10,... | collective-permute-start | bytes 294920 | tf_op jit(solution)/shard_map/ppermute | solution.py:670
  102.8 11.3 %collective-permute-start.17 = (bf16[192,256]{1,0:T(8,128)(2,1)S(1)}, bf16[192,256]{1,0:T(8,128)(2,1)S(1)}, u32[]{:S(2)}, u32[]{:S(2)}) collective-permute-start(bf16[192,256]{1,0:T(8,128)(2,1)S(1)} %get-tuple-element.102), channel_id=1, source_target_pairs={{0,2},{1,3},{2,4},{3,5},{4,6},{5,7},{6,0},{7,1},{8,10},{9,11},{10,... | collective-permute-start | bytes 294920 | tf_op jit(solution)/shard_map/ppermute | solution.py:670
  114.9 3.2 %collective-permute-start.20 = (f32[3,80,128]{2,1,0:T(8,128)S(1)}, f32[3,80,128]{2,1,0:T(8,128)S(1)}, u32[]{:S(2)}, u32[]{:S(2)}) collective-permute-start(f32[3,80,128]{2,1,0:T(8,128)S(1)} %sums.1.refs_7_), channel_id=1, source_target_pairs={{0,1},{1,0},{2,3},{3,2},{4,5},{5,4},{6,7},{7,6},{8,9},{9,8},{10,11... | collective-permute-start | bytes 368648 | tf_op jit(solution)/shard_map/ppermute | solution.py:674
  115.1 28.3 %collective-permute-start.21 = (bf16[2,4,96,768]{3,2,1,0:T(8,128)(2,1)S(1)}, bf16[2,4,96,768]{3,2,1,0:T(8,128)(2,1)S(1)}, u32[]{:S(2)}, u32[]{:S(2)}) collective-permute-start(bf16[2,4,96,768]{3,2,1,0:T(8,128)(2,1)S(1)} %get-tuple-element.117), channel_id=1, source_target_pairs={{0,16},{8,24},{16,0},{24,8},{1,17},{9,25},{17,1},{25,9},{2,18},{10... | collective-permute-start | bytes 3538952 | tf_op jit(solution)/shard_map/ppermute | solution.py:677
  116.7 36.4 %collective-permute-start.26 = (bf16[2,4,128,768]{3,2,1,0:T(8,128)(2,1)S(1)}, bf16[2,4,128,768]{3,2,1,0:T(8,128)(2,1)S(1)}, u32[]{:S(2)}, u32[]{:S(2)}) collective-permute-start(bf16[2,4,128,768]{3,2,1,0:T(8,128)(2,1)S(1)} %get-tuple-element.125), channel_id=1, source_target_pairs={{0,8},{8,0},{16,24},{24,16},{1,9},{9,1},{17,25},{25,17},{2,10},{10... | collective-permute-start | bytes 4718600 | tf_op jit(solution)/shard_map/ppermute | solution.py:677
  138.4 17.0 %collective-permute-start.22 = (bf16[3,128,1024]{2,1,0:T(8,128)(2,1)S(1)}, bf16[3,128,1024]{2,1,0:T(8,128)(2,1)S(1)}, u32[]{:S(2)}, u32[]{:S(2)}) collective-permute-start(bf16[3,128,1024]{2,1,0:T(8,128)(2,1)S(1)} %get-tuple-element.119), channel_id=1, source_target_pairs={{0,1},{1,0},{2,3},{3,2},{4,5},{5,4},{6,7},{7,6},{8,9},{9,8},{10,11... | collective-permute-start | bytes 2359304 | tf_op jit(solution)/shard_map/ppermute | solution.py:674
  153.3 18.8 %collective-permute-start.27 = (bf16[4,128,768]{2,1,0:T(8,128)(2,1)S(1)}, bf16[4,128,768]{2,1,0:T(8,128)(2,1)S(1)}, u32[]{:S(2)}, u32[]{:S(2)}) collective-permute-start(bf16[4,128,768]{2,1,0:T(8,128)(2,1)S(1)} %get-tuple-element.129), channel_id=1, source_target_pairs={{0,16},{8,24},{16,0},{24,8},{1,17},{9,25},{17,1},{25,9},{2,18},{10... | collective-permute-start | bytes 2359304 | tf_op jit(solution)/shard_map/ppermute | solution.py:677
  153.9 14.2 %collective-permute-start.28 = (bf16[4,96,768]{2,1,0:T(8,128)(2,1)S(1)}, bf16[4,96,768]{2,1,0:T(8,128)(2,1)S(1)}, u32[]{:S(2)}, u32[]{:S(2)}) collective-permute-start(bf16[4,96,768]{2,1,0:T(8,128)(2,1)S(1)} %get-tuple-element.130), channel_id=1, source_target_pairs={{0,8},{8,0},{16,24},{24,16},{1,9},{9,1},{17,25},{25,17},{2,10},{10... | collective-permute-start | bytes 1769480 | tf_op jit(solution)/shard_map/ppermute | solution.py:677
  155.7 20.0 %collective-permute-start.23 = (bf16[3,192,256]{2,1,0:T(8,128)(2,1)S(1)}, bf16[3,192,256]{2,1,0:T(8,128)(2,1)S(1)}, u32[]{:S(2)}, u32[]{:S(2)}) collective-permute-start(bf16[3,192,256]{2,1,0:T(8,128)(2,1)S(1)} %get-tuple-element.132.refs_1_), channel_id=1, source_target_pairs={{0,2},{1,3},{2,4},{3,5},{4,6},{5,7},{6,0},{7,1},{8,10},{9,11},{10,... | collective-permute-start | bytes 884744 | tf_op jit(solution)/shard_map/ppermute | solution.py:670
  155.7 24.3 %collective-permute-start.24 = (bf16[3,192,256]{2,1,0:T(8,128)(2,1)S(1)}, bf16[3,192,256]{2,1,0:T(8,128)(2,1)S(1)}, u32[]{:S(2)}, u32[]{:S(2)}) collective-permute-start(bf16[3,192,256]{2,1,0:T(8,128)(2,1)S(1)} %get-tuple-element.133.refs_2_), channel_id=1, source_target_pairs={{0,4},{1,5},{2,6},{3,7},{4,0},{5,1},{6,2},{7,3},{8,12},{9,13},{10,... | collective-permute-start | bytes 884744 | tf_op jit(solution)/shard_map/ppermute | solution.py:670
  158.3 24.6 %collective-permute-start.25 = (bf16[3,192,256]{2,1,0:T(8,128)(2,1)S(1)}, bf16[3,192,256]{2,1,0:T(8,128)(2,1)S(1)}, u32[]{:S(2)}, u32[]{:S(2)}) collective-permute-start(bf16[3,192,256]{2,1,0:T(8,128)(2,1)S(1)} %get-tuple-element.134.refs_3_), channel_id=1, source_target_pairs={{0,6},{1,7},{2,0},{3,1},{4,2},{5,3},{6,4},{7,5},{8,14},{9,15},{10,... | collective-permute-start | bytes 884744 | tf_op jit(solution)/shard_map/ppermute | solution.py:670
  175.7 39.6 %copy-start.6 = (bf16[3,192,256]{2,1,0:T(8,128)(2,1)}, bf16[3,192,256]{2,1,0:T(8,128)(2,1)S(1)}, u32[]{:S(2)}) copy-start(bf16[3,192,256]{2,1,0:T(8,128)(2,1)S(1)} %collective-permute-done.23.refs_1_) | copy-start | bytes 884740
  180.1 35.2 %copy-start.8 = (bf16[3,192,256]{2,1,0:T(8,128)(2,1)}, bf16[3,192,256]{2,1,0:T(8,128)(2,1)S(1)}, u32[]{:S(2)}) copy-start(bf16[3,192,256]{2,1,0:T(8,128)(2,1)S(1)} %collective-permute-done.24.refs_2_) | copy-start | bytes 884740
  182.8 32.5 %copy-start.10 = (bf16[3,192,256]{2,1,0:T(8,128)(2,1)}, bf16[3,192,256]{2,1,0:T(8,128)(2,1)S(1)}, u32[]{:S(2)}) copy-start(bf16[3,192,256]{2,1,0:T(8,128)(2,1)S(1)} %collective-permute-done.25.refs_3_) | copy-start | bytes 884740
  182.8 2.8 %collective-permute-start.29 = (bf16[4,112,576]{2,1,0:T(8,128)(2,1)S(1)}, bf16[4,112,576]{2,1,0:T(8,128)(2,1)S(1)}, u32[]{:S(2)}, u32[]{:S(2)}) collective-permute-start(bf16[4,112,576]{2,1,0:T(8,128)(2,1)S(1)} %get-tuple-element.139), channel_id=1, source_target_pairs={{0,1},{1,0},{2,3},{3,2},{4,5},{5,4},{6,7},{7,6},{8,9},{9,8},{10,11... | collective-permute-start | bytes 1548296 | tf_op jit(solution)/shard_map/ppermute | solution.py:674
  182.9 10.9 %collective-permute-start.32 = (bf16[224,768]{1,0:T(8,128)(2,1)S(1)}, bf16[224,768]{1,0:T(8,128)(2,1)S(1)}, u32[]{:S(2)}, u32[]{:S(2)}) collective-permute-start(bf16[224,768]{1,0:T(8,128)(2,1)S(1)} %get-tuple-element.140), channel_id=1, source_target_pairs={{0,2},{1,3},{2,4},{3,5},{4,6},{5,7},{6,0},{7,1},{8,10},{9,11},{10,... | collective-permute-start | bytes 1032200 | tf_op jit(solution)/shard_map/ppermute | solution.py:670
  182.9 30.4 %collective-permute-start.33 = (bf16[224,768]{1,0:T(8,128)(2,1)S(1)}, bf16[224,768]{1,0:T(8,128)(2,1)S(1)}, u32[]{:S(2)}, u32[]{:S(2)}) collective-permute-start(bf16[224,768]{1,0:T(8,128)(2,1)S(1)} %get-tuple-element.141), channel_id=1, source_target_pairs={{0,4},{1,5},{2,6},{3,7},{4,0},{5,1},{6,2},{7,3},{8,12},{9,13},{10,... | collective-permute-start | bytes 1032200 | tf_op jit(solution)/shard_map/ppermute | solution.py:670
  183.7 30.7 %collective-permute-start.34 = (bf16[224,768]{1,0:T(8,128)(2,1)S(1)}, bf16[224,768]{1,0:T(8,128)(2,1)S(1)}, u32[]{:S(2)}, u32[]{:S(2)}) collective-permute-start(bf16[224,768]{1,0:T(8,128)(2,1)S(1)} %get-tuple-element.142), channel_id=1, source_target_pairs={{0,6},{1,7},{2,0},{3,1},{4,2},{5,3},{6,4},{7,5},{8,14},{9,15},{10,... | collective-permute-start | bytes 1032200 | tf_op jit(solution)/shard_map/ppermute | solution.py:670
  185.8 33.1 %collective-permute-start.30 = (bf16[2,112,576]{2,1,0:T(8,128)(2,1)S(1)}, bf16[2,112,576]{2,1,0:T(8,128)(2,1)S(1)}, u32[]{:S(2)}, u32[]{:S(2)}) collective-permute-start(bf16[2,112,576]{2,1,0:T(8,128)(2,1)S(1)} %get-tuple-element.161), channel_id=1, source_target_pairs={{0,8},{8,0},{16,24},{24,16},{1,9},{9,1},{17,25},{25,17},{2,10},{10... | collective-permute-start | bytes 774152 | tf_op jit(solution)/shard_map/ppermute | solution.py:677
  186.4 32.5 %collective-permute-start.31 = (bf16[2,112,576]{2,1,0:T(8,128)(2,1)S(1)}, bf16[2,112,576]{2,1,0:T(8,128)(2,1)S(1)}, u32[]{:S(2)}, u32[]{:S(2)}) collective-permute-start(bf16[2,112,576]{2,1,0:T(8,128)(2,1)S(1)} %get-tuple-element.160), channel_id=1, source_target_pairs={{0,16},{8,24},{16,0},{24,8},{1,17},{9,25},{17,1},{25,9},{2,18},{10... | collective-permute-start | bytes 774152 | tf_op jit(solution)/shard_map/ppermute | solution.py:677
  215.3 15.7 %collective-permute-start.40 = (bf16[224,768]{1,0:T(8,128)(2,1)}, bf16[224,768]{1,0:T(8,128)(2,1)}, u32[]{:S(2)}, u32[]{:S(2)}) collective-permute-start(bf16[224,768]{1,0:T(8,128)(2,1)} %fourth.1.own), channel_id=1, source_target_pairs={{0,8},{8,0},{16,24},{24,16},{1,9},{9,1},{17,25},{25,17},{2,10},{10... | collective-permute-start | bytes 1032200 | tf_op jit(solution)/shard_map/ppermute | solution.py:677
  215.9 18.6 %collective-permute-start.41 = (bf16[224,768]{1,0:T(8,128)(2,1)}, bf16[224,768]{1,0:T(8,128)(2,1)}, u32[]{:S(2)}, u32[]{:S(2)}) collective-permute-start(bf16[224,768]{1,0:T(8,128)(2,1)} %fourth.1.own), channel_id=1, source_target_pairs={{0,16},{8,24},{16,0},{24,8},{1,17},{9,25},{17,1},{25,9},{2,18},{10... | collective-permute-start | bytes 1032200 | tf_op jit(solution)/shard_map/ppermute | solution.py:677
  217.4 17.2 %collective-permute-start.42 = (bf16[224,768]{1,0:T(8,128)(2,1)}, bf16[224,768]{1,0:T(8,128)(2,1)}, u32[]{:S(2)}, u32[]{:S(2)}) collective-permute-start(bf16[224,768]{1,0:T(8,128)(2,1)} %fourth.1.own), channel_id=1, source_target_pairs={{0,24},{8,16},{16,8},{24,0},{1,25},{9,17},{17,9},{25,1},{2,26},{10... | collective-permute-start | bytes 1032200 | tf_op jit(solution)/shard_map/ppermute | solution.py:677
  219.8 20.2 %collective-permute-start.35 = (bf16[2,112,576]{2,1,0:T(8,128)(2,1)}, bf16[2,112,576]{2,1,0:T(8,128)(2,1)}, u32[]{:S(2)}, u32[]{:S(2)}) collective-permute-start(bf16[2,112,576]{2,1,0:T(8,128)(2,1)} %get-tuple-element.143), channel_id=1, source_target_pairs={{0,16},{8,24},{16,0},{24,8},{1,17},{9,25},{17,1},{25,9},{2,18},{10... | collective-permute-start | bytes 774152 | tf_op jit(solution)/shard_map/ppermute | solution.py:677
  238.6 7.4 %collective-permute-start.37 = (bf16[2,112,576]{2,1,0:T(8,128)(2,1)S(1)}, bf16[2,112,576]{2,1,0:T(8,128)(2,1)S(1)}, u32[]{:S(2)}, u32[]{:S(2)}) collective-permute-start(bf16[2,112,576]{2,1,0:T(8,128)(2,1)S(1)} %copy-done.16), channel_id=1, source_target_pairs={{0,8},{8,0},{16,24},{24,16},{1,9},{9,1},{17,25},{25,17},{2,10},{10... | collective-permute-start | bytes 774152 | tf_op jit(solution)/shard_map/ppermute | solution.py:677
  241.2 7.4 %collective-permute-start.36 = (bf16[112,576]{1,0:T(8,128)(2,1)S(1)}, bf16[112,576]{1,0:T(8,128)(2,1)S(1)}, u32[]{:S(2)}, u32[]{:S(2)}) collective-permute-start(bf16[112,576]{1,0:T(8,128)(2,1)S(1)} %get-tuple-element.164), channel_id=1, source_target_pairs={{0,2},{1,3},{2,4},{3,5},{4,6},{5,7},{6,0},{7,1},{8,10},{9,11},{10,... | collective-permute-start | bytes 387080 | tf_op jit(solution)/shard_map/ppermute | solution.py:670
  246.1 8.2 %collective-permute-start.38 = (bf16[112,576]{1,0:T(8,128)(2,1)S(1)}, bf16[112,576]{1,0:T(8,128)(2,1)S(1)}, u32[]{:S(2)}, u32[]{:S(2)}) collective-permute-start(bf16[112,576]{1,0:T(8,128)(2,1)S(1)} %get-tuple-element.165), channel_id=1, source_target_pairs={{0,4},{1,5},{2,6},{3,7},{4,0},{5,1},{6,2},{7,3},{8,12},{9,13},{10,... | collective-permute-start | bytes 387080 | tf_op jit(solution)/shard_map/ppermute | solution.py:670
  248.1 7.0 %collective-permute-start.39 = (bf16[112,576]{1,0:T(8,128)(2,1)S(1)}, bf16[112,576]{1,0:T(8,128)(2,1)S(1)}, u32[]{:S(2)}, u32[]{:S(2)}) collective-permute-start(bf16[112,576]{1,0:T(8,128)(2,1)S(1)} %get-tuple-element.166), channel_id=1, source_target_pairs={{0,6},{1,7},{2,0},{3,1},{4,2},{5,3},{6,4},{7,5},{8,14},{9,15},{10,... | collective-permute-start | bytes 387080 | tf_op jit(solution)/shard_map/ppermute | solution.py:670
  (23 other events, 191.6 us)

commit v5 on v4

--- a/solution.py
+++ b/solution.py
@@ -107,20 +107,46 @@
     return ref[spot, :] if axis == 0 else ref[:, spot]
 
 
-def bias_kernel(info, top_ref, bias_ref, *, groups, peers, rows):
+def table_kernel(*refs, picks):
+    parts, out = refs[:-1], refs[-1]
+    total = parts[0][:, :picks]
+    for part in parts[1:]:
+        total = total + part[:, :picks]
+    out[:, :picks] = total
+    rows = parts[0].shape[1] - picks
+    for group, part in enumerate(parts):
+        out[:, picks + group * rows : picks + (group + 1) * rows] = part[:, picks:]
+
+
+def bias_kernel(info, *refs, groups, peers, rows, picks):
+    tables, (bias_ref, ids_ref) = refs[:peers], refs[peers:]
     part = pl.program_id(0)
     owner = (
         lax.rem(info[0] + part // peers, groups) * peers + lax.rem(info[1] + part % peers, peers)
     )
-    heads, picks, clusters = top_ref.shape
+    heads, _, clusters = tables[0].shape
     place = owner * rows + lax.broadcasted_iota(jnp.int32, (rows, clusters), 0)
     plain = jnp.where(place >= info[2], EXCLUDED, NEGATIVE)
     for head in range(heads):
-        top = top_ref[head]
+        top = tables[0][head, :picks]
+        for table in tables[1:]:
+            top = top + table[head, :picks]
         value = plain
         for pick in range(picks):
             value = jnp.where(place == top[pick : pick + 1, :], 0.0, value)
         bias_ref[head] = value.astype(BF)
+
+    @pl.when(part == 0)
+    def ids():
+        lines = rows // clusters
+        for head in range(heads):
+            row = []
+            for group in range(groups):
+                for table in tables:
+                    for line in range(lines):
+                        at = picks + group * lines + line
+                        row.append(table[head, at : at + 1, :])
+            ids_ref[head] = jnp.concatenate(row, axis=1)
 
 
 def project_kernel(info, *refs, peers, olds):
@@ -479,25 +505,38 @@
     @pl.when(index == 0)
     def first():
         found = nn(low[stay:width, :], dbr[...]) + nn(low_got[stay:width, :], dbr_got[...])
+        fold = low[width:, :].astype(F32) + low_got[width:, :].astype(F32)
+        times = width // fold.shape[1]
+        norms = []
+        for part in range(2):
+            both = fold[2 * part * times : (2 * part + 1) * times]
+            both = both + fold[(2 * part + 1) * times : (2 * part + 2) * times]
+            norms.append(jnp.concatenate([both[k : k + 1] for k in range(times)], axis=1))
+        norms = jnp.concatenate(norms + [jnp.zeros((6, width), F32)], axis=0)
         for group in range(groups):
-            outs[group] = found[group * rows : (group + 1) * rows]
+            block = found[group * rows : (group + 1) * rows]
+            outs[group] = block
+            for part in range(4):
+                tail = block[part * quarter + 16 : (part + 1) * quarter]
+                tail = jnp.concatenate([tail, norms], axis=0).astype(BF)
+                place = lax.bitwise_xor(part, place_d)
+
+                @pl.when(place >= 2)
+                def leaves_more():
+                    send_d[place - 2, (groups - group) % groups, rows:] = tail
+
+                @pl.when(place < 2)
+                def stays_more():
+                    keep_d[place, (groups - group) % groups, rows:] = tail
 
     up = nn(low[:stay, :], dup[...]) + nn(low_got[:stay, :], dup_got[...])
     at = lax.bitwise_xor(lax.bitwise_xor(index, 2), place_u)
-    fold = low[width:, :].astype(F32) + low_got[width:, :].astype(F32)
-    times = width // fold.shape[1]
-    norms = []
-    for part in range(2):
-        both = fold[2 * part * times : (2 * part + 1) * times]
-        both = both + fold[(2 * part + 1) * times : (2 * part + 2) * times]
-        norms.append(jnp.concatenate([both[k : k + 1] for k in range(times)], axis=1))
-    norms = jnp.concatenate(norms + [jnp.zeros((6, width), F32)], axis=0)
     for group in range(groups):
         spot = lax.rem(group + groups - group_at, groups)
         block = up[group * rows : (group + 1) * rows].astype(BF)
         away = (groups - group) % groups
         start = pl.multiple_of(at * quarter, 8)
-        other = jnp.concatenate([outs[group, pl.ds(start, quarter), :], norms], axis=0).astype(BF)
+        other = outs[group, pl.ds(start, 16), :].astype(BF)
 
         @pl.when(index < 2)
         def leaves():
@@ -517,11 +556,11 @@
 
         @pl.when(place >= 2)
         def leaves_down():
-            send_d[place - 2, spot] = block
+            send_d[place - 2, spot, :rows] = block
 
         @pl.when(place < 2)
         def stays_down():
-            keep_d[place, spot] = block
+            keep_d[place, spot, :rows] = block
 
 
 def second_kernel(keep_u, got_u, keep_d, got_d, send_u, send_d):
@@ -549,25 +588,28 @@
 def spread_kernel(info, own, from_x, from_y, from_xy, up_ref, out_ref, down_ref, norm_ref):
     index = pl.program_id(0)
     rows = up_ref.shape[0]
-    quarter = out_ref.shape[0]
-    top = rows + quarter + 8
+    quarter = out_ref.shape[0] // 4
+    high = own.shape[0] // 2
     for place, part in enumerate((own, from_y, from_x, from_xy)):
 
         @pl.when(index == place)
         def upper(part=part):
             up_ref[...] = part[:rows].astype(F32)
-            tail = part[rows:top].astype(F32)
-            out_ref[...] = tail[:quarter]
-
-            @pl.when(lax.bitwise_xor(index, info[3]) == 0)
-            def norms():
-                norm_ref[...] = tail[quarter:]
+            at = pl.multiple_of(lax.bitwise_xor(index, info[3]) * quarter, 8)
+            out_ref[pl.ds(at, 16), :] = part[rows:high].astype(F32)
 
     for place, part in enumerate((own, from_x, from_y, from_xy)):
 
         @pl.when(index == place)
         def lower(part=part):
-            down_ref[...] = part[top:].astype(F32)
+            down_ref[...] = part[high : high + rows].astype(F32)
+            tail = part[high + rows :].astype(F32)
+            at = pl.multiple_of(lax.bitwise_xor(index, info[4]) * quarter + 16, 8)
+            out_ref[pl.ds(at, quarter - 16), :] = tail[: quarter - 16]
+
+            @pl.when(lax.bitwise_xor(index, info[4]) == 0)
+            def norms():
+                norm_ref[...] = tail[quarter - 16 :]
 
 
 def inward_kernel(info, *refs, groups, fast):
@@ -656,7 +698,7 @@
     size = 512 if seq <= 2048 else 2048
     feats = own_heads * hs
     block_rows = width // wide
-    fast = peers == 2 and n_dp == 4 and block_rows % 32 == 0 and hidden == 4 * width and width % 256 == 0 and rows % 128 == 0
+    fast = peers == 2 and n_dp == 4 and block_rows == 96 and hidden == 4 * width and width % 256 == 0 and rows % 128 == 0
     me = lax.axis_index("wide")
     group_at, peer_at = me // peers, me % peers
     dp_at = lax.axis_index("dp")
@@ -701,10 +743,13 @@
 
     position = me * rows + jnp.arange(rows, dtype=jnp.int32)
     marked = jnp.where((position < seq_len)[:, None], cluster_ids, -1).T
-    packed = jnp.concatenate(
-        [marked, top_keys[0].transpose(0, 2, 1).reshape(heads, own_clusters * picks)], axis=1
+    tops = jnp.zeros((heads, picks, clusters), jnp.int32)
+    tops = lax.dynamic_update_slice(
+        tops, top_keys[0].transpose(0, 2, 1), (0, 0, me * own_clusters)
     )
-    packed = packed.reshape(groups, own_heads, -1)
+    lines = rows // clusters
+    packed = jnp.concatenate([tops, marked.reshape(heads, lines, clusters)], axis=1)
+    packed = packed.reshape(groups, own_heads, picks + lines, clusters)
 
     def of_heads(hop):
         return lax.dynamic_index_in_dim(packed, (group_at + groups - hop) % groups, keepdims=False)
@@ -715,45 +760,40 @@
     mine = {0: tokens, 1: along_groups(ready, -1)}
     if groups > 2:
         mine[groups - 1] = along_groups(ready, 1)
+    ready = after(tokens, arrived)
     for hop in range(2, groups - 1):
-        ready = after(tokens, mine[1], mine[groups - 1])
         mine[hop] = along_groups(ready, -hop)
 
-    arrived = jnp.stack(arrived)
-    others = [arrived] + [along_peers(arrived, -hop) for hop in range(1, peers)]
-    ids_all = jnp.stack([item[..., :rows] for item in others], axis=1)
-    ids_all = ids_all.transpose(2, 0, 1, 3).reshape(own_heads, 1, seq)
-    turned = (ids_all + (clusters - group_at * (clusters // groups))) % clusters
-    ids_all = jnp.where(ids_all < 0, -1, turned)
-    tops = [item[..., rows:] for item in others]
-    if peers == 2:
-        tops = [
-            jnp.where(peer_at == 0, tops[0], tops[1]),
-            jnp.where(peer_at == 0, tops[1], tops[0]),
-        ]
-    else:
-        tops = jnp.stack(tops)
-        tops = [
-            lax.dynamic_index_in_dim(tops, (p + peers - peer_at) % peers, keepdims=False)
-            for p in range(peers)
-        ]
-    top_all = jnp.stack(tops, axis=1).reshape(groups, peers, own_heads, picks, own_clusters)
-    top_all = top_all.transpose(2, 3, 0, 1, 4).reshape(own_heads, picks, clusters)
-    cot_got = [along_peers(cotangent, hop) for hop in range(1, peers)] if fast else []
-
-    bias = prefetched(
-        functools.partial(bias_kernel, groups=groups, peers=peers, rows=rows),
+    w_in = jnp.concatenate([w_query, w_keyval], axis=1).T.reshape(3, heads, hs, width)
+    w_in = w_in.transpose(1, 0, 2, 3).reshape(groups, 3 * feats, width)
+    table_shape = (own_heads, picks + groups * lines, clusters)
+    table = pl.pallas_call(
+        functools.partial(table_kernel, picks=picks),
+        grid=(1,),
+        in_specs=[whole((own_heads, picks + lines, clusters))] * groups,
+        out_specs=whole(table_shape),
+        out_shape=array(table_shape, jnp.int32),
+        compiler_params=params(8, 1),
+        cost_estimate=cost(1e5, 1e6),
+        name="table",
+    )(*after(arrived, w_in))
+    tables = [table] + [along_peers(table, -hop) for hop in range(1, peers)]
+    cot_got = [along_peers(after(cotangent, arrived), hop) for hop in range(1, peers)]
+    cot_got = cot_got if fast else []
+    bias, ids_all = prefetched(
+        functools.partial(bias_kernel, groups=groups, peers=peers, rows=rows, picks=picks),
         (wide,),
-        [whole((own_heads, picks, clusters))],
-        pl.BlockSpec((own_heads, rows, clusters), lambda i, s: (0, i, 0)),
-        array((own_heads, seq, clusters), BF),
-        8 if fast else 60,
+        [whole(table_shape)] * peers,
+        [
+            pl.BlockSpec((own_heads, rows, clusters), lambda i, s: (0, i, 0)),
+            whole((own_heads, 1, seq)),
+        ],
+        [array((own_heads, seq, clusters), BF), array((own_heads, 1, seq), jnp.int32)],
+        12 if fast else 60,
         cost(own_heads * seq * clusters * picks * 8, own_heads * seq * clusters * 2),
         "bias",
-    )(info, top_all)
-
-    w_in = jnp.concatenate([w_query, w_keyval], axis=1).T.reshape(3, heads, hs, width)
-    w_in = w_in.transpose(1, 0, 2, 3).reshape(groups, 3 * feats, width)
+    )(info, *tables)
+
     gain_row, shift_row = gain_one[None, :], shift_one[None, :]
     shapes = [
         array((width, groups * rows), BF),
@@ -763,9 +803,11 @@
     held = []
     split_peers = peers if peers <= 2 else 1
     for group in sorted(range(groups), key=lambda g: min(g, groups - g)):
-        arrival = mine[group]
+        arrival = mine[group] if group else ready
         if 1 < group < groups - 1:
-            arrival = after(arrival, bias, held, cot_got)
+            arrival = after(arrival, held, cot_got)
+        elif group:
+            arrival = after(arrival, bias)
         chunk = [arrival] + [along_peers(arrival, -hop) for hop in range(1, peers)]
         if peers > 2:
             chunk = [jnp.concatenate(chunk, axis=0)]
@@ -906,14 +948,14 @@
     def weight_parts():
         far, low_far, act_own, low_own = kept
         got, low_got = along_peers(far, 1), along_peers(low_far, 1)
-        high = block_rows + block_rows // 4 + 8
+        high = block_rows + 16
         chunk = pl.BlockSpec((rows, part), lambda i, s: (0, i ^ 2 ^ s[3]))
         branch = pl.BlockSpec((rows, width), lambda i, s: (0, hidden * 3 // 2 // width))
         act_spec = pl.BlockSpec((rows, part // 2), lambda i, s: (0, i))
         act_there = pl.BlockSpec((rows, part // 2), lambda i, s: (0, 2 * hidden // part + i))
         low_spec = whole((width + 16, rows))
         shape_u = (2, groups, high, width)
-        shape_d = (2, groups, block_rows, width)
+        shape_d = (2, groups, high, width)
         send_u, keep_u, send_d, keep_d = prefetched(
             functools.partial(weights_kernel, groups=groups),
             (4,),
@@ -958,7 +1000,7 @@
         def block(shape, at):
             return pl.BlockSpec((1,) + shape[1:], lambda i: (at, 0, 0, 0))
 
-        tall = high + block_rows
+        tall = shape_u[2] + shape_d[2]
         sums = pl.pallas_call(
             third_kernel,
             grid=(1,),
@@ -992,14 +1034,13 @@
             name="fourth",
         )(*came)
         from_x, from_y, from_xy = (along_dp(done, mask) for mask in (1, 2, 3))
-        quarter = block_rows // 4
         total_up, total_out, total_down, norms = prefetched(
             spread_kernel,
             (4,),
             [whole((tall, width))] * 4,
             [
                 pl.BlockSpec((block_rows, part), lambda i, s: (0, i ^ s[3])),
-                pl.BlockSpec((quarter, width), lambda i, s: (i ^ s[3], 0)),
+                whole((block_rows, width)),
                 pl.BlockSpec((block_rows, width), lambda i, s: (i ^ s[4], 0)),
                 whole((8, width)),
             ],
@@ -1100,8 +1141,6 @@
         )
         for hop in range(1, peers)
     ]
-    if fast:
-        dkv_own = after(dkv_own, got_d)
     d_in = pl.pallas_call(
         functools.partial(join_kernel, groups=groups),
         grid=(1,),
@@ -1128,23 +1167,24 @@
     if fast:
         half = groups // 2
         blocks = (groups, tall, 3 * feats)
-        next_u, next_d = weight_second(keep_u, after(got_u, dq), keep_d, after(got_d, dq))
+        next_u, next_d = weight_second(
+            keep_u, after(got_u, home[1]), keep_d, after(got_d, home[1])
+        )
         last_u, last_d = along_dp(next_u, 2), along_dp(next_d, 1)
+        came = weight_third(keep_u, got_u, last_u, keep_d, got_d, last_d)
         keep, far = inward(
             [whole(blocks)] * 2, [array(blocks, BF)] * 2, 24, spent, "inward"
-        )(info, *after(d_in, last_u, last_d), hat_own)
-        came = weight_third(keep_u, got_u, last_u, keep_d, got_d, last_d)
-        got = along_peers(after(far, home, came[0]), 1)
+        )(info, *after(d_in, home, came[0]), hat_own)
+        got = along_peers(far, 1)
         total = keep.astype(F32) + got.astype(F32)
         one_half, two_half = total[:half].astype(BF), total[half:].astype(BF)
         for mask in (1, 2):
+            one_half, two_half = after((one_half, two_half), came[mask])
             got_one, got_two = along_dp(one_half, mask), along_dp(two_half, 3 - mask)
             one_half = (one_half.astype(F32) + got_one.astype(F32)).astype(BF)
             two_half = (two_half.astype(F32) + got_two.astype(F32)).astype(BF)
-            if mask == 1:
-                one_half, two_half = after((one_half, two_half), came)
         total_up, total_out, total_down, norm_own = weight_sums(
-            came, keep_u.shape, keep_d.shape
+            after(came, one_half, two_half), keep_u.shape, keep_d.shape
         )
         items = [one_half[k] for k in range(half)] + [two_half[k] for k in range(half)]
     else:

time: 266 us -> 258 us (0.970)
  other arithmetic: 15.1 us -> 8.46 us
  local copies, waits for them, and re-layouts: 34.5 us -> 27.9 us
  starting transfers between devices: 42.3 us -> 45.4 us
  Pallas kernels: 81.9 us -> 85 us
    ppermute x11, waiting for transfers between devices: 35.3 us -> 24.8 us  [along_dp(): return lax.ppermute(values, 'dp', [(i, i ^ mask) for i in range(n_dp)])]
    ppermute x21, starting transfers between devices: 26.5 us -> 31.5 us  [along_groups(): return lax.ppermute(values, 'wide', pairs)]
    unnamed x57 -> x64, local copies, waits for them, and re-layouts: 12.3 us -> 16.8 us
    another operation x4 -> x0, local copies, waits for them, and re-layouts: 4.28 us -> none  [the longest x2 3.06 us: per_device(): jnp.stack(tops, axis=1)]
    ppermute x11, waiting for transfers between devices: 2.42 us -> 6.69 us  [along_peers(): return lax.ppermute(values, 'wide', pairs)]
    ppermute x21, waiting for transfers between devices: 50 us -> 54 us  [along_groups(): return lax.ppermute(values, 'wide', pairs)]
  transfers between devices with their start and end apart: 43 -> 43, of which waited for: 21 -> 23; matrix products, arithmetic and copies ran while one was open for 13% -> 9% of each run, Pallas kernels for 21% -> 21%
where the time goes in v5:
time: 258 us; the launch traced here: 254 us
  waiting for transfers between devices  85.6 us (33%)
  Pallas kernels  85 us (33%)
  starting transfers between devices  45.4 us (18%)
  local copies, waits for them, and re-layouts  27.9 us (11%)
  other arithmetic  8.46 us (3%)
    ppermute x21, waiting for transfers between devices, along_groups(): return lax.ppermute(values, 'wide', pairs)  54 us
    ppermute x21, starting transfers between devices, along_groups(): return lax.ppermute(values, 'wide', pairs)  31.5 us
    ppermute x11, waiting for transfers between devices, along_dp(): return lax.ppermute(values, 'dp', [(i, i ^ mask) for i in range(n_dp)])  24.8 us
    pallas_call x1, Pallas kernels, per_device(): pl.pallas_call(functools.partial(back_kernel, size=size, groups=groups, g...  20.7 us
    unnamed x64, local copies, waits for them, and re-layouts  16.8 us
    pallas_call x1, Pallas kernels, per_device(): pl.pallas_call(functools.partial(forward_kernel, size=size, groups=groups...  13.5 us
    ppermute x11, starting transfers between devices, along_dp(): return lax.ppermute(values, 'dp', [(i, i ^ mask) for i in range(n_dp)])  11.9 us
    pallas_call x1, Pallas kernels, per_device(): prefetched(functools.partial(block_kernel, groups=groups, chunks=chunks,...  11 us
  transfers between devices with their start and end apart: 43, of which 23 were waited for; matrix products, arithmetic and copies ran while one was open for 9% of the time, Pallas kernels for 21%

profile of v5, /device:TPU:8, one launch (start us, length us, event | category | flops | bytes accessed | tf_op | source)
XLA Modules:
  0.0 254.2 jit_solution(11834070280921589338)
XLA Ops:
  0.7 2.0 collective-permute-start.5
  5.2 2.1 dynamic_update_slice.3
  8.3 4.1 %collective-permute-start.1 = (s32[3,34,128]{2,1,0:T(8,128)}, s32[3,34,128]{2,1,0:T(8,128)}, u32[]{:S(2)}, u32[]{:S(2)}) collective-permute-start(s32[3,34,128]{2,1,0:T(8,128)} %get-tuple-element.193), channel_id=1, source_target_pairs={{0,4},{1,5},{2,6},{3,7},{4,0},{5,1},{6,2},{7,3},{8,12},{9,13},{10,... | collective-permute-start | bytes 156680 | tf_op jit(solution)/shard_map/ppermute | solution.py:712
  12.4 2.9 %collective-permute-start.2 = (s32[3,34,128]{2,1,0:T(8,128)}, s32[3,34,128]{2,1,0:T(8,128)}, u32[]{:S(2)}, u32[]{:S(2)}) collective-permute-start(s32[3,34,128]{2,1,0:T(8,128)} %get-tuple-element.191), channel_id=1, source_target_pairs={{0,2},{1,3},{2,4},{3,5},{4,6},{5,7},{6,0},{7,1},{8,10},{9,11},{10,... | collective-permute-start | bytes 156680 | tf_op jit(solution)/shard_map/ppermute | solution.py:712
  15.3 2.8 %copy.46 = bf16[768,1536]{0,1:T(8,128)(2,1)S(1)} copy(bf16[768,1536]{1,0:T(8,128)(2,1)} %param.21) | data formatting | bytes 4718592 | tf_op args[7]
  18.1 1.6 copy.45
  21.0 3.7 %collective-permute-done.1.refs_2_ = s32[3,34,128]{2,1,0:T(8,128)} collective-permute-done((s32[3,34,128]{2,1,0:T(8,128)}, s32[3,34,128]{2,1,0:T(8,128)}, u32[]{:S(2)}, u32[]{:S(2)}) %collective-permute-start.1) | collective-permute-done | bytes 52256 | tf_op jit(solution)/shard_map/ppermute | solution.py:712
  24.6 1.7 collective-permute-done.2.refs_3_
  26.3 1.5 table.1.refs_0_
  29.4 8.5 %bias.1 = (bf16[3,2048,128]{2,1,0:T(8,128)(2,1)S(1)}, s32[3,1,2048]{2,1,0:T(1,128)S(1)}) custom-call(s32[6]{0:T(128)S(1)} %stack.42.info, s32[3,40,128]{2,1,0:T(8,128)} %table.1.refs_0_, s32[3,40,128]{2,1,0:T(8,128)} %collective-permute-done.3.refs_1_), custom_call_target="tpu_custom_call" | custom-call | flops 201326592 | bytes 1572864 | tf_op jit(solution)/shard_map/bias/pallas_call | solution.py:783
  39.6 2.8 %project.4 = (bf16[768,1024]{1,0:T(8,128)(2,1)S(1)}, bf16[3,192,2048]{2,1,0:T(8,128)(2,1)S(1)}, bf16[3,2048,128]{2,1,0:T(8,128)(2,1)S(1)}) custom-call(s32[6]{0:T(128)S(1)} %stack.42.info, bf16[256,768]{1,0:T(8,128)(2,1)} %refs_4_.3, bf16[256,768]{1,0:T(8,128)(2,1)} %collective-permute-done.9.refs_1_, f32[1,768]{1,0:T(1,128)S(1)} %broadcast_in_dim.33.refs_2_.refs_6_, ...), custom_call_target="tpu_custom_call" | custom-call | flops 452984832 | bytes 1572864 | tf_op jit(solution)/shard_map/project/pallas_call | solution.py:832
  42.4 2.7 %project.5 = (bf16[768,1024]{1,0:T(8,128)(2,1)S(1)}, bf16[3,192,2048]{2,1,0:T(8,128)(2,1)S(1)}, bf16[3,2048,128]{2,1,0:T(8,128)(2,1)S(1)}) custom-call(s32[6]{0:T(128)S(1)} %stack.42.info, bf16[256,768]{1,0:T(8,128)(2,1)} %collective-permute-done.7.refs_0_, ...), custom_call_target="tpu_custom_call", output_to_operand_aliasing={{0}: (6, {}), {1}: (7, {}), {2}: (8, {})} | custom-call | flops 452984832 | bytes 1572864 | tf_op jit(solution)/shard_map/project/pallas_call | solution.py:832
  45.2 2.7 %project.6 = (bf16[768,1024]{1,0:T(8,128)(2,1)S(1)}, bf16[3,192,2048]{2,1,0:T(8,128)(2,1)S(1)}, bf16[3,2048,128]{2,1,0:T(8,128)(2,1)S(1)}) custom-call(s32[6]{0:T(128)S(1)} %stack.42.info, bf16[256,768]{1,0:T(8,128)(2,1)} %collective-permute-done.5.refs_0_, ...), custom_call_target="tpu_custom_call", output_to_operand_aliasing={{0}: (6, {}), {1}: (7, {}), {2}: (8, {})} | custom-call | flops 452984832 | bytes 1572864 | tf_op jit(solution)/shard_map/project/pallas_call | solution.py:832
  47.9 9.3 %collective-permute-done.4.refs_0_ = bf16[256,768]{1,0:T(8,128)(2,1)S(1)} collective-permute-done((bf16[256,768]{1,0:T(8,128)(2,1)}, bf16[256,768]{1,0:T(8,128)(2,1)S(1)}, u32[]{:S(2)}, u32[]{:S(2)}) %collective-permute-start.4) | collective-permute-done | bytes 393248 | tf_op jit(solution)/shard_map/ppermute | solution.py:712
  57.2 1.7 collective-permute-done.11.refs_1_
  58.9 1.7 project.7
  60.7 13.5 %attend.1 = (bf16[192,256]{1,0:T(8,128)(2,1)S(1)}, bf16[192,256]{1,0:T(8,128)(2,1)S(1)}, bf16[192,256]{1,0:T(8,128)(2,1)S(1)}, bf16[192,256]{1,0:T(8,128)(2,1)S(...) custom-call(s32[3,1,2048]{2,1,0:T(1,128)S(1)} %get-tuple-element.97.ids_all.ids_own, ...), custom_call_target="tpu_custom_call" | custom-call | flops 9663676416 | bytes 8000000 | tf_op jit(solution)/shard_map/attend/pallas_call | solution.py:871
  75.6 4.2 %collective-permute-start.13 = (bf16[192,256]{1,0:T(8,128)(2,1)S(1)}, bf16[192,256]{1,0:T(8,128)(2,1)S(1)}, u32[]{:S(2)}, u32[]{:S(2)}) collective-permute-start(bf16[192,256]{1,0:T(8,128)(2,1)S(1)} %get-tuple-element.118), channel_id=1, source_target_pairs={{0,4},{1,5},{2,6},{3,7},{4,0},{5,1},{6,2},{7,3},{8,12},{9,13},{10,... | collective-permute-start | bytes 294920 | tf_op jit(solution)/shard_map/ppermute | solution.py:712
  81.0 4.7 %collective-permute-done.13.refs_2_ = bf16[192,256]{1,0:T(8,128)(2,1)S(1)} collective-permute-done((bf16[192,256]{1,0:T(8,128)(2,1)S(1)}, bf16[192,256]{1,0:T(8,128)(2,1)S(1)}, u32[]{:S(2)}, u32[]{:S(2)}) %collective-permute-start.13) | collective-permute-done | bytes 98336 | tf_op jit(solution)/shard_map/ppermute | solution.py:712
  85.7 2.4 collective-permute-done.14.refs_3_
  88.1 2.3 copy-done.17
  90.4 11.0 %feed.1 = (bf16[256,768]{1,0:T(8,128)(2,1)}, f32[256,768]{1,0:T(8,128)S(1)}, bf16[256,5376]{1,0:T(8,128)(2,1)S(1)}, bf16[784,256]{1,0:T(8,128)(2,1)S(1)}, bf16[2...) custom-call(s32[6]{0:T(128)S(1)} %stack.42.info, ...), custom_call_target="tpu_custom_call" | custom-call | flops 4831838208 | bytes 9437184 | tf_op jit(solution)/shard_map/feed/pallas_call | solution.py:916
  105.3 2.9 %collective-permute-start.17 = (bf16[192,256]{1,0:T(8,128)(2,1)S(1)}, bf16[192,256]{1,0:T(8,128)(2,1)S(1)}, u32[]{:S(2)}, u32[]{:S(2)}) collective-permute-start(bf16[192,256]{1,0:T(8,128)(2,1)S(1)} %get-tuple-element.124), channel_id=1, source_target_pairs={{0,2},{1,3},{2,4},{3,5},{4,6},{5,7},{6,0},{7,1},{8,10},{9,11},{10,... | collective-permute-start | bytes 294920 | tf_op jit(solution)/shard_map/ppermute | solution.py:712
  108.3 1.8 copy-done.19
  110.0 7.2 %weights.1 = (bf16[2,4,112,768]{3,2,1,0:T(8,128)(2,1)S(1)}, bf16[2,4,112,768]{3,2,1,0:T(8,128)(2,1)S(1)}, bf16[2,4,112,768]{3,2,1,0:T(8,128)(2,1)S(1)}, bf16[2,4,112,768]{3,2,1,0:T(8,128)(2,1)S(1)}) custom-call(s32[6]{0:T(128)S(1)} %stack.42.info, bf16[256,5376]{1,0:T(8,128)(2,1)S(1)} %copy-done.19, ...), custom_call_target="tpu_custom_call" | custom-call | flops 4831838208 | bytes 14155776 | tf_op jit(solution)/shard_map/weights/pallas_call | solution.py:959
  118.2 1.6 collective-permute-start.26
  121.3 20.7 %back.1 = (bf16[4,192,256]{2,1,0:T(8,128)(2,1)S(1)}, f32[3,128,1024]{2,1,0:T(8,128)S(1)}, bf16[3,128,1024]{2,1,0:T(8,128)(2,1)S(1)}) custom-call(s32[3,1,2048]{2,1,0:T(1,128)S(1)} %get-tuple-element.97.ids_all.ids_own, bf16[3,192,2048]{2,1,0:T(8,128)(2,1)S(1)} %get-tuple-element.114.feat, bf16[3,2048,128]{2,1,0:T(8,128)(2,1)S(1)} %get-tuple-element.115.kv, ...), custom_call_target="tpu_custom_call" | custom-call | flops 22548578304 | bytes 10000000 | tf_op jit(solution)/shard_map/back/pallas_call | solution.py:1120
  142.1 2.3 collective-permute-done.21.refs_0_
  144.6 9.0 %collective-permute-done.22.refs_1_ = bf16[3,192,256]{2,1,0:T(8,128)(2,1)S(1)} collective-permute-done((bf16[3,192,256]{2,1,0:T(8,128)(2,1)S(1)}, bf16[3,192,256]{2,1,0:T(8,128)(2,1)S(1)}, u32[]{:S(2)}, u32[]{:S(2)}) %collective-permute-start.22) | collective-permute-done | bytes 294944 | tf_op jit(solution)/shard_map/ppermute | solution.py:712
  155.6 1.9 collective-permute-start.23
  157.6 13.5 %collective-permute-done.27.last_u = bf16[4,112,768]{2,1,0:T(8,128)(2,1)S(1)} collective-permute-done((bf16[4,112,768]{2,1,0:T(8,128)(2,1)S(1)}, bf16[4,112,768]{2,1,0:T(8,128)(2,1)S(1)}, u32[]{:S(2)}, u32[]{:S(2)}) %collective-permute-start.27) | collective-permute-done | bytes 688160 | tf_op jit(solution)/shard_map/ppermute | solution.py:719
  172.4 2.5 collective-permute-done.23.refs_2_
  175.0 1.9 collective-permute-done.24.refs_3_
  176.8 2.3 inward.1
  179.5 1.7 collective-permute-done.29
  181.4 8.3 %collective-permute-done.30.refs_1_ = bf16[224,768]{1,0:T(8,128)(2,1)S(1)} collective-permute-done((bf16[224,768]{1,0:T(8,128)(2,1)S(1)}, bf16[224,768]{1,0:T(8,128)(2,1)S(1)}, u32[]{:S(2)}, u32[]{:S(2)}) %collective-permute-start.30) | collective-permute-done | bytes 344096 | tf_op jit(solution)/shard_map/ppermute | solution.py:712
  192.5 1.5 collective-permute-start.33
  194.0 3.8 %collective-permute-done.32 = bf16[2,112,576]{2,1,0:T(8,128)(2,1)S(1)} collective-permute-done((bf16[2,112,576]{2,1,0:T(8,128)(2,1)S(1)}, bf16[2,112,576]{2,1,0:T(8,128)(2,1)S(1)}, u32[]{:S(2)}, u32[]{:S(2)}) %collective-permute-start.32) | collective-permute-done | bytes 258080 | tf_op jit(solution)/shard_map/ppermute | solution.py:719
  198.9 8.7 %collective-permute-done.33.refs_2_ = bf16[224,768]{1,0:T(8,128)(2,1)S(1)} collective-permute-done((bf16[224,768]{1,0:T(8,128)(2,1)S(1)}, bf16[224,768]{1,0:T(8,128)(2,1)S(1)}, u32[]{:S(2)}, u32[]{:S(2)}) %collective-permute-start.33) | collective-permute-done | bytes 344096 | tf_op jit(solution)/shard_map/ppermute | solution.py:712
  208.2 3.3 %collective-permute-start.39 = (bf16[224,768]{1,0:T(8,128)(2,1)}, bf16[224,768]{1,0:T(8,128)(2,1)}, u32[]{:S(2)}, u32[]{:S(2)}) collective-permute-start(bf16[224,768]{1,0:T(8,128)(2,1)} %get-tuple-element.166), channel_id=1, source_target_pairs={{0,6},{1,7},{2,0},{3,1},{4,2},{5,3},{6,4},{7,5},{8,14},{9,15},{10,... | collective-permute-start | bytes 1032200 | tf_op jit(solution)/shard_map/ppermute | solution.py:712
  212.3 4.1 %collective-permute-done.34 = bf16[2,112,576]{2,1,0:T(8,128)(2,1)S(1)} collective-permute-done((bf16[2,112,576]{2,1,0:T(8,128)(2,1)S(1)}, bf16[2,112,576]{2,1,0:T(8,128)(2,1)S(1)}, u32[]{:S(2)}, u32[]{:S(2)}) %collective-permute-start.34) | collective-permute-done | bytes 258080 | tf_op jit(solution)/shard_map/ppermute | solution.py:719
  220.6 3.2 %collective-permute-start.37 = (bf16[112,576]{1,0:T(8,128)(2,1)}, bf16[112,576]{1,0:T(8,128)(2,1)}, u32[]{:S(2)}, u32[]{:S(2)}) collective-permute-start(bf16[112,576]{1,0:T(8,128)(2,1)} %get-tuple-element.189), channel_id=1, source_target_pairs={{0,4},{1,5},{2,6},{3,7},{4,0},{5,1},{6,2},{7,3},{8,12},{9,13},{10,... | collective-permute-start | bytes 387080 | tf_op jit(solution)/shard_map/ppermute | solution.py:712
  229.4 4.0 %final.1 = bf16[256,768]{1,0:T(8,128)(2,1)} custom-call(s32[6]{0:T(128)S(1)} %stack.42.info, bf16[3,192,256]{2,1,0:T(8,128)(2,1)S(1)} %copy-done.9, bf16[3,192,256]{2,1,0:T(8,128)(2,1)S(1)} %copy-done.11, bf16[3,192,256]{2,1,0:T(8,128)(2,1)S(1)} %copy-done.13, bf16[3,192,256]{2,1,0:T(8,128)(2,1)S(1)} %copy-done.15, bf16[256,768]{1,0:T(8,128)(2,1)} %refs_4_.3, ...), custom_call_target="tpu_custom_call" | custom-call | flops 905969664 | bytes 3538944 | tf_op jit(solution)/shard_map/final/pallas_call | solution.py:1219
  235.9 2.2 collective-permute-start.42
  241.9 1.9 slice.64
  244.8 2.0 fusion.1
  246.8 1.8 fusion.4
  250.9 2.7 %spread.1 = (f32[96,3072]{1,0:T(8,128)}, f32[96,768]{1,0:T(8,128)}, f32[384,768]{1,0:T(8,128)}, f32[8,768]{1,0:T(8,128)S(1)}) custom-call(s32[6]{0:T(128)S(1)} %stack.42.info, bf16[224,768]{1,0:T(8,128)(2,1)S(1)} %fourth.1.own, bf16[224,768]{1,0:T(8,128)(2,1)S(1)} %collective-permute-done.40.from_x, bf16[224,768]{1,0:T(8,128)(2,1)S(1)} %collective-permute-done.41.from_y, ...), custom_call_target="tpu_custom_call" | custom-call | flops 1000000 | bytes 4128768 | tf_op jit(solution)/shard_map/spread/pallas_call | solution.py:1037
  (166 shorter events, 45.4 us)
Async XLA Ops:
  0.6 37.3 %collective-permute-start.7 = (bf16[256,768]{1,0:T(8,128)(2,1)}, bf16[256,768]{1,0:T(8,128)(2,1)}, u32[]{:S(2)}, u32[]{:S(2)}) collective-permute-start(bf16[256,768]{1,0:T(8,128)(2,1)} %refs_4_.3), channel_id=1, source_target_pairs={{0,6},{1,7},{2,0},{3,1},{4,2},{5,3},{6,4},{7,5},{8,14},{9,15},{10,... | collective-permute-start | bytes 1179656 | tf_op jit(solution)/shard_map/ppermute | solution.py:712
  0.7 37.5 %collective-permute-start.5 = (bf16[256,768]{1,0:T(8,128)(2,1)}, bf16[256,768]{1,0:T(8,128)(2,1)}, u32[]{:S(2)}, u32[]{:S(2)}) collective-permute-start(bf16[256,768]{1,0:T(8,128)(2,1)} %refs_4_.3), channel_id=1, source_target_pairs={{0,2},{1,3},{2,4},{3,5},{4,6},{5,7},{6,0},{7,1},{8,10},{9,11},{10,... | collective-permute-start | bytes 1179656 | tf_op jit(solution)/shard_map/ppermute | solution.py:712
  8.0 13.0 %collective-permute-start = (s32[3,34,128]{2,1,0:T(8,128)}, s32[3,34,128]{2,1,0:T(8,128)}, u32[]{:S(2)}, u32[]{:S(2)}) collective-permute-start(s32[3,34,128]{2,1,0:T(8,128)} %get-tuple-element.192), channel_id=1, source_target_pairs={{0,6},{1,7},{2,0},{3,1},{4,2},{5,3},{6,4},{7,5},{8,14},{9,15},{10,... | collective-permute-start | bytes 156680 | tf_op jit(solution)/shard_map/ppermute | solution.py:712
  8.3 16.3 %collective-permute-start.1 = (s32[3,34,128]{2,1,0:T(8,128)}, s32[3,34,128]{2,1,0:T(8,128)}, u32[]{:S(2)}, u32[]{:S(2)}) collective-permute-start(s32[3,34,128]{2,1,0:T(8,128)} %get-tuple-element.193), channel_id=1, source_target_pairs={{0,4},{1,5},{2,6},{3,7},{4,0},{5,1},{6,2},{7,3},{8,12},{9,13},{10,... | collective-permute-start | bytes 156680 | tf_op jit(solution)/shard_map/ppermute | solution.py:712
  12.4 13.9 %collective-permute-start.2 = (s32[3,34,128]{2,1,0:T(8,128)}, s32[3,34,128]{2,1,0:T(8,128)}, u32[]{:S(2)}, u32[]{:S(2)}) collective-permute-start(s32[3,34,128]{2,1,0:T(8,128)} %get-tuple-element.191), channel_id=1, source_target_pairs={{0,2},{1,3},{2,4},{3,5},{4,6},{5,7},{6,0},{7,1},{8,10},{9,11},{10,... | collective-permute-start | bytes 156680 | tf_op jit(solution)/shard_map/ppermute | solution.py:712
  27.8 1.6 collective-permute-start.3
  27.8 11.7 %collective-permute-start.9 = (bf16[256,768]{1,0:T(8,128)(2,1)}, bf16[256,768]{1,0:T(8,128)(2,1)}, u32[]{:S(2)}, u32[]{:S(2)}) collective-permute-start(bf16[256,768]{1,0:T(8,128)(2,1)} %refs_4_.3), channel_id=1, source_target_pairs={{0,1},{1,0},{2,3},{3,2},{4,5},{5,4},{6,7},{7,6},{8,9},{9,8},{10,11... | collective-permute-start | bytes 1179656 | tf_op jit(solution)/shard_map/ppermute | solution.py:716
  38.0 4.5 %collective-permute-start.8 = (bf16[256,768]{1,0:T(8,128)(2,1)}, bf16[256,768]{1,0:T(8,128)(2,1)S(1)}, u32[]{:S(2)}, u32[]{:S(2)}) collective-permute-start(bf16[256,768]{1,0:T(8,128)(2,1)} %collective-permute-done.7.refs_0_), channel_id=1, source_target_pairs={{0,1},{1,0},{2,3},{3,2},{4,5},{5,4},{6,7},{7,6},{8,9},{9,8},{10,11... | collective-permute-start | bytes 1179656 | tf_op jit(solution)/shard_map/ppermute | solution.py:716
  38.2 7.0 %collective-permute-start.6 = (bf16[256,768]{1,0:T(8,128)(2,1)}, bf16[256,768]{1,0:T(8,128)(2,1)S(1)}, u32[]{:S(2)}, u32[]{:S(2)}) collective-permute-start(bf16[256,768]{1,0:T(8,128)(2,1)} %collective-permute-done.5.refs_0_), channel_id=1, source_target_pairs={{0,1},{1,0},{2,3},{3,2},{4,5},{5,4},{6,7},{7,6},{8,9},{9,8},{10,11... | collective-permute-start | bytes 1179656 | tf_op jit(solution)/shard_map/ppermute | solution.py:716
  38.6 9.3 %collective-permute-start.10 = (bf16[256,768]{1,0:T(8,128)(2,1)}, bf16[256,768]{1,0:T(8,128)(2,1)S(1)}, u32[]{:S(2)}, u32[]{:S(2)}) collective-permute-start(bf16[256,768]{1,0:T(8,128)(2,1)} %refs_8_.3), channel_id=1, source_target_pairs={{0,1},{1,0},{2,3},{3,2},{4,5},{5,4},{6,7},{7,6},{8,9},{9,8},{10,11... | collective-permute-start | bytes 1179656 | tf_op jit(solution)/shard_map/ppermute | solution.py:716
  38.7 18.5 %collective-permute-start.4 = (bf16[256,768]{1,0:T(8,128)(2,1)}, bf16[256,768]{1,0:T(8,128)(2,1)S(1)}, u32[]{:S(2)}, u32[]{:S(2)}) collective-permute-start(bf16[256,768]{1,0:T(8,128)(2,1)} %refs_4_.3), channel_id=1, source_target_pairs={{0,4},{1,5},{2,6},{3,7},{4,0},{5,1},{6,2},{7,3},{8,12},{9,13},{10,... | collective-permute-start | bytes 1179656 | tf_op jit(solution)/shard_map/ppermute | solution.py:712
  57.2 1.7 collective-permute-start.11
  58.9 29.2 %slice-start = ((s8[4718592]{0:T(1024)(128)(4,1)}), s8[4194304]{0:T(1024)(128)(4,1)S(1)}, s32[]{:S(2)}) async-start(s8[4718592]{0:T(1024)(128)(4,1)} %bitcast.52), calls=%async_computation | async-start | bytes 8388608
  60.7 27.4 %slice-start.1 = ((s8[4718592]{0:T(1024)(128)(4,1)}), s8[524288]{0:T(1024)(128)(4,1)S(1)}, s32[]{:S(2)}) async-start(s8[4718592]{0:T(1024)(128)(4,1)} %bitcast.52), calls=%async_computation.1 | async-start | bytes 1048576
  60.7 27.4 %copy-start.20 = (bf16[768,768]{1,0:T(8,128)(2,1)S(1)}, bf16[768,768]{1,0:T(8,128)(2,1)}, u32[]{:S(2)}) copy-start(bf16[768,768]{1,0:T(8,128)(2,1)} %param.22) | copy-start | bytes 3538948
  74.2 6.8 %collective-permute-start.12 = (bf16[192,256]{1,0:T(8,128)(2,1)S(1)}, bf16[192,256]{1,0:T(8,128)(2,1)S(1)}, u32[]{:S(2)}, u32[]{:S(2)}) collective-permute-start(bf16[192,256]{1,0:T(8,128)(2,1)S(1)} %get-tuple-element.117), channel_id=1, source_target_pairs={{0,2},{1,3},{2,4},{3,5},{4,6},{5,7},{6,0},{7,1},{8,10},{9,11},{10,... | collective-permute-start | bytes 294920 | tf_op jit(solution)/shard_map/ppermute | solution.py:712
  75.6 10.1 %collective-permute-start.13 = (bf16[192,256]{1,0:T(8,128)(2,1)S(1)}, bf16[192,256]{1,0:T(8,128)(2,1)S(1)}, u32[]{:S(2)}, u32[]{:S(2)}) collective-permute-start(bf16[192,256]{1,0:T(8,128)(2,1)S(1)} %get-tuple-element.118), channel_id=1, source_target_pairs={{0,4},{1,5},{2,6},{3,7},{4,0},{5,1},{6,2},{7,3},{8,12},{9,13},{10,... | collective-permute-start | bytes 294920 | tf_op jit(solution)/shard_map/ppermute | solution.py:712
  79.7 8.3 %collective-permute-start.14 = (bf16[192,256]{1,0:T(8,128)(2,1)S(1)}, bf16[192,256]{1,0:T(8,128)(2,1)S(1)}, u32[]{:S(2)}, u32[]{:S(2)}) collective-permute-start(bf16[192,256]{1,0:T(8,128)(2,1)S(1)} %get-tuple-element.119), channel_id=1, source_target_pairs={{0,6},{1,7},{2,0},{3,1},{4,2},{5,3},{6,4},{7,5},{8,14},{9,15},{10,... | collective-permute-start | bytes 294920 | tf_op jit(solution)/shard_map/ppermute | solution.py:712
  102.3 5.9 %collective-permute-start.18 = (bf16[256,5376]{1,0:T(8,128)(2,1)S(1)}, bf16[256,5376]{1,0:T(8,128)(2,1)S(1)}, u32[]{:S(2)}, u32[]{:S(2)}) collective-permute-start(bf16[256,5376]{1,0:T(8,128)(2,1)S(1)} %get-tuple-element.125.refs_0_.refs_2_), channel_id=1, source_target_pairs={{0,1},{1,0},{2,3},{3,2},{4,5},{5,4},{6,7},{7,6},{8,9},{9,8},{10,11... | collective-permute-start | bytes 8257544 | tf_op jit(solution)/shard_map/ppermute | solution.py:716
  103.8 4.4 %collective-permute-start.19 = (bf16[784,256]{1,0:T(8,128)(2,1)S(1)}, bf16[784,256]{1,0:T(8,128)(2,1)S(1)}, u32[]{:S(2)}, u32[]{:S(2)}) collective-permute-start(bf16[784,256]{1,0:T(8,128)(2,1)S(1)} %get-tuple-element.128), channel_id=1, source_target_pairs={{0,1},{1,0},{2,3},{3,2},{4,5},{5,4},{6,7},{7,6},{8,9},{9,8},{10,11... | collective-permute-start | bytes 1204232 | tf_op jit(solution)/shard_map/ppermute | solution.py:716
  104.3 13.0 %collective-permute-start.15 = (bf16[192,256]{1,0:T(8,128)(2,1)S(1)}, bf16[192,256]{1,0:T(8,128)(2,1)S(1)}, u32[]{:S(2)}, u32[]{:S(2)}) collective-permute-start(bf16[192,256]{1,0:T(8,128)(2,1)S(1)} %get-tuple-element.122), channel_id=1, source_target_pairs={{0,6},{1,7},{2,0},{3,1},{4,2},{5,3},{6,4},{7,5},{8,14},{9,15},{10,... | collective-permute-start | bytes 294920 | tf_op jit(solution)/shard_map/ppermute | solution.py:712
  104.5 12.8 %collective-permute-start.16 = (bf16[192,256]{1,0:T(8,128)(2,1)S(1)}, bf16[192,256]{1,0:T(8,128)(2,1)S(1)}, u32[]{:S(2)}, u32[]{:S(2)}) collective-permute-start(bf16[192,256]{1,0:T(8,128)(2,1)S(1)} %get-tuple-element.123), channel_id=1, source_target_pairs={{0,4},{1,5},{2,6},{3,7},{4,0},{5,1},{6,2},{7,3},{8,12},{9,13},{10,... | collective-permute-start | bytes 294920 | tf_op jit(solution)/shard_map/ppermute | solution.py:712
  105.3 12.0 %collective-permute-start.17 = (bf16[192,256]{1,0:T(8,128)(2,1)S(1)}, bf16[192,256]{1,0:T(8,128)(2,1)S(1)}, u32[]{:S(2)}, u32[]{:S(2)}) collective-permute-start(bf16[192,256]{1,0:T(8,128)(2,1)S(1)} %get-tuple-element.124), channel_id=1, source_target_pairs={{0,2},{1,3},{2,4},{3,5},{4,6},{5,7},{6,0},{7,1},{8,10},{9,11},{10,... | collective-permute-start | bytes 294920 | tf_op jit(solution)/shard_map/ppermute | solution.py:712
  118.2 3.1 %collective-permute-start.20 = (f32[3,80,128]{2,1,0:T(8,128)S(1)}, f32[3,80,128]{2,1,0:T(8,128)S(1)}, u32[]{:S(2)}, u32[]{:S(2)}) collective-permute-start(f32[3,80,128]{2,1,0:T(8,128)S(1)} %sums.1.refs_7_), channel_id=1, source_target_pairs={{0,1},{1,0},{2,3},{3,2},{4,5},{5,4},{6,7},{7,6},{8,9},{9,8},{10,11... | collective-permute-start | bytes 368648 | tf_op jit(solution)/shard_map/ppermute | solution.py:716
  118.2 35.4 %collective-permute-start.26 = (bf16[2,4,112,768]{3,2,1,0:T(8,128)(2,1)S(1)}, bf16[2,4,112,768]{3,2,1,0:T(8,128)(2,1)S(1)}, u32[]{:S(2)}, u32[]{:S(2)}) collective-permute-start(bf16[2,4,112,768]{3,2,1,0:T(8,128)(2,1)S(1)} %get-tuple-element.148), channel_id=1, source_target_pairs={{0,16},{8,24},{16,0},{24,8},{1,17},{9,25},{17,1},{25,9},{2,18},{10... | collective-permute-start | bytes 4128776 | tf_op jit(solution)/shard_map/ppermute | solution.py:719
  119.8 33.8 %collective-permute-start.25 = (bf16[2,4,112,768]{3,2,1,0:T(8,128)(2,1)S(1)}, bf16[2,4,112,768]{3,2,1,0:T(8,128)(2,1)S(1)}, u32[]{:S(2)}, u32[]{:S(2)}) collective-permute-start(bf16[2,4,112,768]{3,2,1,0:T(8,128)(2,1)S(1)} %get-tuple-element.145), channel_id=1, source_target_pairs={{0,8},{8,0},{16,24},{24,16},{1,9},{9,1},{17,25},{25,17},{2,10},{10... | collective-permute-start | bytes 4128776 | tf_op jit(solution)/shard_map/ppermute | solution.py:719
  142.0 2.4 collective-permute-start.21
  144.5 32.3 %copy-start.8 = (bf16[3,192,256]{2,1,0:T(8,128)(2,1)}, bf16[3,192,256]{2,1,0:T(8,128)(2,1)S(1)}, u32[]{:S(2)}) copy-start(bf16[3,192,256]{2,1,0:T(8,128)(2,1)S(1)} %get-tuple-element.153.refs_0_) | copy-start | bytes 884740
  144.5 9.1 %collective-permute-start.22 = (bf16[3,192,256]{2,1,0:T(8,128)(2,1)S(1)}, bf16[3,192,256]{2,1,0:T(8,128)(2,1)S(1)}, u32[]{:S(2)}, u32[]{:S(2)}) collective-permute-start(bf16[3,192,256]{2,1,0:T(8,128)(2,1)S(1)} %get-tuple-element.154.refs_1_), channel_id=1, source_target_pairs={{0,2},{1,3},{2,4},{3,5},{4,6},{5,7},{6,0},{7,1},{8,10},{9,11},{10,... | collective-permute-start | bytes 884744 | tf_op jit(solution)/shard_map/ppermute | solution.py:712
  154.4 16.6 %collective-permute-start.27 = (bf16[4,112,768]{2,1,0:T(8,128)(2,1)S(1)}, bf16[4,112,768]{2,1,0:T(8,128)(2,1)S(1)}, u32[]{:S(2)}, u32[]{:S(2)}) collective-permute-start(bf16[4,112,768]{2,1,0:T(8,128)(2,1)S(1)} %get-tuple-element.150), channel_id=1, source_target_pairs={{0,16},{8,24},{16,0},{24,8},{1,17},{9,25},{17,1},{25,9},{2,18},{10... | collective-permute-start | bytes 2064392 | tf_op jit(solution)/shard_map/ppermute | solution.py:719
  154.9 16.4 %collective-permute-start.28 = (bf16[4,112,768]{2,1,0:T(8,128)(2,1)S(1)}, bf16[4,112,768]{2,1,0:T(8,128)(2,1)S(1)}, u32[]{:S(2)}, u32[]{:S(2)}) collective-permute-start(bf16[4,112,768]{2,1,0:T(8,128)(2,1)S(1)} %get-tuple-element.151), channel_id=1, source_target_pairs={{0,8},{8,0},{16,24},{24,16},{1,9},{9,1},{17,25},{25,17},{2,10},{10... | collective-permute-start | bytes 2064392 | tf_op jit(solution)/shard_map/ppermute | solution.py:719
  155.6 19.3 %collective-permute-start.23 = (bf16[3,192,256]{2,1,0:T(8,128)(2,1)S(1)}, bf16[3,192,256]{2,1,0:T(8,128)(2,1)S(1)}, u32[]{:S(2)}, u32[]{:S(2)}) collective-permute-start(bf16[3,192,256]{2,1,0:T(8,128)(2,1)S(1)} %get-tuple-element.155.refs_2_), channel_id=1, source_target_pairs={{0,4},{1,5},{2,6},{3,7},{4,0},{5,1},{6,2},{7,3},{8,12},{9,13},{10,... | collective-permute-start | bytes 884744 | tf_op jit(solution)/shard_map/ppermute | solution.py:712
  157.6 19.3 %collective-permute-start.24 = (bf16[3,192,256]{2,1,0:T(8,128)(2,1)S(1)}, bf16[3,192,256]{2,1,0:T(8,128)(2,1)S(1)}, u32[]{:S(2)}, u32[]{:S(2)}) collective-permute-start(bf16[3,192,256]{2,1,0:T(8,128)(2,1)S(1)} %get-tuple-element.156.refs_3_), channel_id=1, source_target_pairs={{0,6},{1,7},{2,0},{3,1},{4,2},{5,3},{6,4},{7,5},{8,14},{9,15},{10,... | collective-permute-start | bytes 884744 | tf_op jit(solution)/shard_map/ppermute | solution.py:712
  179.1 2.0 collective-permute-start.29
  179.2 10.5 %collective-permute-start.30 = (bf16[224,768]{1,0:T(8,128)(2,1)S(1)}, bf16[224,768]{1,0:T(8,128)(2,1)S(1)}, u32[]{:S(2)}, u32[]{:S(2)}) collective-permute-start(bf16[224,768]{1,0:T(8,128)(2,1)S(1)} %get-tuple-element.160), channel_id=1, source_target_pairs={{0,2},{1,3},{2,4},{3,5},{4,6},{5,7},{6,0},{7,1},{8,10},{9,11},{10,... | collective-permute-start | bytes 1032200 | tf_op jit(solution)/shard_map/ppermute | solution.py:712
  189.7 27.6 %copy-start.4 = (bf16[224,768]{1,0:T(8,128)(2,1)}, bf16[224,768]{1,0:T(8,128)(2,1)S(1)}, u32[]{:S(2)}) copy-start(bf16[224,768]{1,0:T(8,128)(2,1)S(1)} %collective-permute-done.30.refs_1_) | copy-start | bytes 1032196
  189.7 8.1 %collective-permute-start.32 = (bf16[2,112,576]{2,1,0:T(8,128)(2,1)S(1)}, bf16[2,112,576]{2,1,0:T(8,128)(2,1)S(1)}, u32[]{:S(2)}, u32[]{:S(2)}) collective-permute-start(bf16[2,112,576]{2,1,0:T(8,128)(2,1)S(1)} %get-tuple-element.162), channel_id=1, source_target_pairs={{0,16},{8,24},{16,0},{24,8},{1,17},{9,25},{17,1},{25,9},{2,18},{10... | collective-permute-start | bytes 774152 | tf_op jit(solution)/shard_map/ppermute | solution.py:719
  191.0 7.9 %collective-permute-start.31 = (bf16[2,112,576]{2,1,0:T(8,128)(2,1)S(1)}, bf16[2,112,576]{2,1,0:T(8,128)(2,1)S(1)}, u32[]{:S(2)}, u32[]{:S(2)}) collective-permute-start(bf16[2,112,576]{2,1,0:T(8,128)(2,1)S(1)} %get-tuple-element.161), channel_id=1, source_target_pairs={{0,8},{8,0},{16,24},{24,16},{1,9},{9,1},{17,25},{25,17},{2,10},{10... | collective-permute-start | bytes 774152 | tf_op jit(solution)/shard_map/ppermute | solution.py:719
  192.5 15.2 %collective-permute-start.33 = (bf16[224,768]{1,0:T(8,128)(2,1)S(1)}, bf16[224,768]{1,0:T(8,128)(2,1)S(1)}, u32[]{:S(2)}, u32[]{:S(2)}) collective-permute-start(bf16[224,768]{1,0:T(8,128)(2,1)S(1)} %get-tuple-element.163), channel_id=1, source_target_pairs={{0,4},{1,5},{2,6},{3,7},{4,0},{5,1},{6,2},{7,3},{8,12},{9,13},{10,... | collective-permute-start | bytes 1032200 | tf_op jit(solution)/shard_map/ppermute | solution.py:712
  207.7 8.8 %collective-permute-start.34 = (bf16[2,112,576]{2,1,0:T(8,128)(2,1)S(1)}, bf16[2,112,576]{2,1,0:T(8,128)(2,1)S(1)}, u32[]{:S(2)}, u32[]{:S(2)}) collective-permute-start(bf16[2,112,576]{2,1,0:T(8,128)(2,1)S(1)} %add_convert_fusion.4), channel_id=1, source_target_pairs={{0,16},{8,24},{16,0},{24,8},{1,17},{9,25},{17,1},{25,9},{2,18},{10... | collective-permute-start | bytes 774152 | tf_op jit(solution)/shard_map/ppermute | solution.py:719
  208.2 25.1 %collective-permute-start.39 = (bf16[224,768]{1,0:T(8,128)(2,1)}, bf16[224,768]{1,0:T(8,128)(2,1)}, u32[]{:S(2)}, u32[]{:S(2)}) collective-permute-start(bf16[224,768]{1,0:T(8,128)(2,1)} %get-tuple-element.166), channel_id=1, source_target_pairs={{0,6},{1,7},{2,0},{3,1},{4,2},{5,3},{6,4},{7,5},{8,14},{9,15},{10,... | collective-permute-start | bytes 1032200 | tf_op jit(solution)/shard_map/ppermute | solution.py:712
  211.6 8.2 %collective-permute-start.36 = (bf16[2,112,576]{2,1,0:T(8,128)(2,1)S(1)}, bf16[2,112,576]{2,1,0:T(8,128)(2,1)S(1)}, u32[]{:S(2)}, u32[]{:S(2)}) collective-permute-start(bf16[2,112,576]{2,1,0:T(8,128)(2,1)S(1)} %add_convert_fusion.3), channel_id=1, source_target_pairs={{0,8},{8,0},{16,24},{24,16},{1,9},{9,1},{17,25},{25,17},{2,10},{10... | collective-permute-start | bytes 774152 | tf_op jit(solution)/shard_map/ppermute | solution.py:719
  217.2 18.6 %collective-permute-start.35 = (bf16[112,576]{1,0:T(8,128)(2,1)}, bf16[112,576]{1,0:T(8,128)(2,1)}, u32[]{:S(2)}, u32[]{:S(2)}) collective-permute-start(bf16[112,576]{1,0:T(8,128)(2,1)} %get-tuple-element.188), channel_id=1, source_target_pairs={{0,2},{1,3},{2,4},{3,5},{4,6},{5,7},{6,0},{7,1},{8,10},{9,11},{10,... | collective-permute-start | bytes 387080 | tf_op jit(solution)/shard_map/ppermute | solution.py:712
  220.6 17.5 %collective-permute-start.37 = (bf16[112,576]{1,0:T(8,128)(2,1)}, bf16[112,576]{1,0:T(8,128)(2,1)}, u32[]{:S(2)}, u32[]{:S(2)}) collective-permute-start(bf16[112,576]{1,0:T(8,128)(2,1)} %get-tuple-element.189), channel_id=1, source_target_pairs={{0,4},{1,5},{2,6},{3,7},{4,0},{5,1},{6,2},{7,3},{8,12},{9,13},{10,... | collective-permute-start | bytes 387080 | tf_op jit(solution)/shard_map/ppermute | solution.py:712
  223.8 14.3 %collective-permute-start.38 = (bf16[112,576]{1,0:T(8,128)(2,1)}, bf16[112,576]{1,0:T(8,128)(2,1)}, u32[]{:S(2)}, u32[]{:S(2)}) collective-permute-start(bf16[112,576]{1,0:T(8,128)(2,1)} %get-tuple-element.190), channel_id=1, source_target_pairs={{0,6},{1,7},{2,0},{3,1},{4,2},{5,3},{6,4},{7,5},{8,14},{9,15},{10,... | collective-permute-start | bytes 387080 | tf_op jit(solution)/shard_map/ppermute | solution.py:712
  234.6 15.2 %collective-permute-start.40 = (bf16[224,768]{1,0:T(8,128)(2,1)S(1)}, bf16[224,768]{1,0:T(8,128)(2,1)S(1)}, u32[]{:S(2)}, u32[]{:S(2)}) collective-permute-start(bf16[224,768]{1,0:T(8,128)(2,1)S(1)} %fourth.1.own), channel_id=1, source_target_pairs={{0,8},{8,0},{16,24},{24,16},{1,9},{9,1},{17,25},{25,17},{2,10},{10... | collective-permute-start | bytes 1032200 | tf_op jit(solution)/shard_map/ppermute | solution.py:719
  235.2 15.8 %collective-permute-start.41 = (bf16[224,768]{1,0:T(8,128)(2,1)S(1)}, bf16[224,768]{1,0:T(8,128)(2,1)S(1)}, u32[]{:S(2)}, u32[]{:S(2)}) collective-permute-start(bf16[224,768]{1,0:T(8,128)(2,1)S(1)} %fourth.1.own), channel_id=1, source_target_pairs={{0,16},{8,24},{16,0},{24,8},{1,17},{9,25},{17,1},{25,9},{2,18},{10... | collective-permute-start | bytes 1032200 | tf_op jit(solution)/shard_map/ppermute | solution.py:719
  235.9 15.1 %collective-permute-start.42 = (bf16[224,768]{1,0:T(8,128)(2,1)S(1)}, bf16[224,768]{1,0:T(8,128)(2,1)S(1)}, u32[]{:S(2)}, u32[]{:S(2)}) collective-permute-start(bf16[224,768]{1,0:T(8,128)(2,1)S(1)} %fourth.1.own), channel_id=1, source_target_pairs={{0,24},{8,16},{16,8},{24,0},{1,25},{9,17},{17,9},{25,1},{2,26},{10... | collective-permute-start | bytes 1032200 | tf_op jit(solution)/shard_map/ppermute | solution.py:719
  (27 other events, 168.8 us)

commit v6 on v5

--- a/solution.py
+++ b/solution.py
@@ -749,17 +749,17 @@
     )
     lines = rows // clusters
     packed = jnp.concatenate([tops, marked.reshape(heads, lines, clusters)], axis=1)
-    packed = packed.reshape(groups, own_heads, picks + lines, clusters)
+    early = [along_peers(tokens, -hop) for hop in range(1, peers)]
+    packed = after(packed.reshape(groups, own_heads, picks + lines, clusters), early)
 
     def of_heads(hop):
         return lax.dynamic_index_in_dim(packed, (group_at + groups - hop) % groups, keepdims=False)
 
     arrived = [of_heads(0)] + [along_groups(of_heads(hop), -hop) for hop in range(1, groups)]
 
-    ready = after(tokens, packed)
-    mine = {0: tokens, 1: along_groups(ready, -1)}
+    mine = {0: tokens, 1: along_groups(tokens, -1)}
     if groups > 2:
-        mine[groups - 1] = along_groups(ready, 1)
+        mine[groups - 1] = along_groups(tokens, 1)
     ready = after(tokens, arrived)
     for hop in range(2, groups - 1):
         mine[hop] = along_groups(ready, -hop)
@@ -803,12 +803,15 @@
     held = []
     split_peers = peers if peers <= 2 else 1
     for group in sorted(range(groups), key=lambda g: min(g, groups - g)):
-        arrival = mine[group] if group else ready
+        arrival = mine[group]
         if 1 < group < groups - 1:
             arrival = after(arrival, held, cot_got)
+        elif group == 1:
+            arrival = after(arrival, bias)
         elif group:
-            arrival = after(arrival, bias)
-        chunk = [arrival] + [along_peers(arrival, -hop) for hop in range(1, peers)]
+            arrival = after(arrival, bias, [mine[hop] for hop in range(2, group)])
+        chunk = [arrival]
+        chunk += early if group == 0 else [along_peers(arrival, -hop) for hop in range(1, peers)]
         if peers > 2:
             chunk = [jnp.concatenate(chunk, axis=0)]
         span = peers * rows
@@ -1055,7 +1058,7 @@
             "spread",
         )(info, done, from_x, from_y, from_xy)
         norm_own = lax.dynamic_slice_in_dim(norms, me * block_rows, block_rows, axis=1)
-        return total_up, total_out, total_down, norm_own
+        return total_up, total_out, total_down, norm_own, done
 
     masks = [1 << k for k in range(n_dp.bit_length() - 1)]
 
@@ -1167,25 +1170,26 @@
     if fast:
         half = groups // 2
         blocks = (groups, tall, 3 * feats)
-        next_u, next_d = weight_second(
-            keep_u, after(got_u, home[1]), keep_d, after(got_d, home[1])
-        )
-        last_u, last_d = along_dp(next_u, 2), along_dp(next_d, 1)
-        came = weight_third(keep_u, got_u, last_u, keep_d, got_d, last_d)
+        got_u, got_d = after((got_u, got_d), home[1])
+        next_u, next_d = weight_second(keep_u, got_u, keep_d, got_d)
         keep, far = inward(
             [whole(blocks)] * 2, [array(blocks, BF)] * 2, 24, spent, "inward"
-        )(info, *after(d_in, home, came[0]), hat_own)
+        )(info, *after(d_in, next_u, next_d), hat_own)
         got = along_peers(far, 1)
         total = keep.astype(F32) + got.astype(F32)
         one_half, two_half = total[:half].astype(BF), total[half:].astype(BF)
+        last_u, last_d = along_dp(next_u, 2), along_dp(next_d, 1)
+        last_u, last_d = after((last_u, last_d), home)
+        came = weight_third(keep_u, got_u, last_u, keep_d, got_d, last_d)
         for mask in (1, 2):
             one_half, two_half = after((one_half, two_half), came[mask])
             got_one, got_two = along_dp(one_half, mask), along_dp(two_half, 3 - mask)
             one_half = (one_half.astype(F32) + got_one.astype(F32)).astype(BF)
             two_half = (two_half.astype(F32) + got_two.astype(F32)).astype(BF)
-        total_up, total_out, total_down, norm_own = weight_sums(
+        total_up, total_out, total_down, norm_own, done = weight_sums(
             after(came, one_half, two_half), keep_u.shape, keep_d.shape
         )
+        home = after(home, done)
         items = [one_half[k] for k in range(half)] + [two_half[k] for k in range(half)]
     else:
         found, more = inward(

time: 258 us -> 259 us (level)
  starting transfers between devices: 45.4 us -> 42.7 us
    ppermute x21, waiting for transfers between devices: 54 us -> 72.3 us  [along_groups(): return lax.ppermute(values, 'wide', pairs)]
    ppermute x11, waiting for transfers between devices: 24.8 us -> 8.5 us  [along_dp(): return lax.ppermute(values, 'dp', [(i, i ^ mask) for i in range(n_dp)])]
    unnamed x64 -> x80, local copies, waits for them, and re-layouts: 16.8 us -> 19.2 us
  transfers between devices with their start and end apart: 43 -> 43, of which waited for: 23 -> 16; matrix products, arithmetic and copies ran while one was open for 9% -> 9% of each run, Pallas kernels for 21% -> 21%
where the time goes in v6:
time: 259 us; the launch traced here: 257 us
  Pallas kernels  87.3 us (34%)
  waiting for transfers between devices  86.6 us (33%)
  starting transfers between devices  42.7 us (16%)
  local copies, waits for them, and re-layouts  29 us (11%)
  other arithmetic  9.07 us (4%)
    ppermute x21, waiting for transfers between devices, along_groups(): return lax.ppermute(values, 'wide', pairs)  72.3 us
    ppermute x21, starting transfers between devices, along_groups(): return lax.ppermute(values, 'wide', pairs)  29.5 us
    pallas_call x1, Pallas kernels, per_device(): pl.pallas_call(functools.partial(back_kernel, size=size, groups=groups, g...  20.7 us
    unnamed x80, local copies, waits for them, and re-layouts  19.2 us
    pallas_call x1, Pallas kernels, per_device(): pl.pallas_call(functools.partial(forward_kernel, size=size, groups=groups...  13.5 us
    ppermute x11, starting transfers between devices, along_dp(): return lax.ppermute(values, 'dp', [(i, i ^ mask) for i in range(n_dp)])  11.9 us
    pallas_call x4, Pallas kernels, per_device(): prefetched(functools.partial(project_kernel, peers=split_peers, olds=len(...  11.1 us
    pallas_call x1, Pallas kernels, per_device(): prefetched(functools.partial(block_kernel, groups=groups, chunks=chunks,...  11 us
  transfers between devices with their start and end apart: 43, of which 16 were waited for; matrix products, arithmetic and copies ran while one was open for 9% of the time, Pallas kernels for 21%

profile of v6, /device:TPU:8, one launch (start us, length us, event | category | flops | bytes accessed | tf_op | source)
XLA Modules:
  0.0 256.7 jit_solution(4635620878390221898)
XLA Ops:
  3.3 2.1 dynamic_update_slice.3
  6.1 3.0 %collective-permute-start.2 = (s32[3,34,128]{2,1,0:T(8,128)S(1)}, s32[3,34,128]{2,1,0:T(8,128)S(1)}, u32[]{:S(2)}, u32[]{:S(2)}) collective-permute-start(s32[3,34,128]{2,1,0:T(8,128)S(1)} %get-tuple-element.204), channel_id=1, source_target_pairs={{0,4},{1,5},{2,6},{3,7},{4,0},{5,1},{6,2},{7,3},{8,12},{9,13},{10,... | collective-permute-start | bytes 156680 | tf_op jit(solution)/shard_map/ppermute | solution.py:712
  9.2 2.5 collective-permute-start.3
  11.7 2.0 collective-permute-start.6
  13.7 2.8 %copy.46 = bf16[768,1536]{0,1:T(8,128)(2,1)S(1)} copy(bf16[768,1536]{1,0:T(8,128)(2,1)} %param.21) | data formatting | bytes 4718592 | tf_op args[7]
  16.5 2.4 copy.45
  18.9 4.8 %collective-permute-done.3.refs_3_ = s32[3,34,128]{2,1,0:T(8,128)S(1)} collective-permute-done((s32[3,34,128]{2,1,0:T(8,128)S(1)}, s32[3,34,128]{2,1,0:T(8,128)S(1)}, u32[]{:S(2)}, u32[]{:S(2)}) %collective-permute-start.3) | collective-permute-done | bytes 52256 | tf_op jit(solution)/shard_map/ppermute | solution.py:712
  23.7 1.5 pad_maximum_fusion
  26.9 1.5 collective-permute-done.4.refs_1_
  28.4 8.5 %bias.1 = (bf16[3,2048,128]{2,1,0:T(8,128)(2,1)S(1)}, s32[3,1,2048]{2,1,0:T(1,128)S(1)}) custom-call(s32[6]{0:T(128)S(1)} %stack.42.info, s32[3,40,128]{2,1,0:T(8,128)} %table.1.refs_0_, s32[3,40,128]{2,1,0:T(8,128)} %collective-permute-done.4.refs_1_), custom_call_target="tpu_custom_call" | custom-call | flops 201326592 | bytes 1572864 | tf_op jit(solution)/shard_map/bias/pallas_call | solution.py:783
  36.9 4.3 %collective-permute-done.8.refs_0_ = bf16[256,768]{1,0:T(8,128)(2,1)} collective-permute-done((bf16[256,768]{1,0:T(8,128)(2,1)}, bf16[256,768]{1,0:T(8,128)(2,1)}, u32[]{:S(2)}, u32[]{:S(2)}) %collective-permute-start.8) | collective-permute-done | bytes 393248 | tf_op jit(solution)/shard_map/ppermute | solution.py:712
  41.3 7.4 %collective-permute-done.5.refs_0_ = bf16[256,768]{1,0:T(8,128)(2,1)} collective-permute-done((bf16[256,768]{1,0:T(8,128)(2,1)}, bf16[256,768]{1,0:T(8,128)(2,1)}, u32[]{:S(2)}, u32[]{:S(2)}) %collective-permute-start.5) | collective-permute-done | bytes 393248 | tf_op jit(solution)/shard_map/ppermute | solution.py:712
  50.2 2.7 %project.4 = (bf16[768,1024]{1,0:T(8,128)(2,1)S(1)}, bf16[3,192,2048]{2,1,0:T(8,128)(2,1)S(1)}, bf16[3,2048,128]{2,1,0:T(8,128)(2,1)S(1)}) custom-call(s32[6]{0:T(128)S(1)} %stack.42.info, bf16[256,768]{1,0:T(8,128)(2,1)} %refs_4_.3, bf16[256,768]{1,0:T(8,128)(2,1)S(1)} %copy-done.3, f32[1,768]{1,0:T(1,128)S(1)} %broadcast_in_dim.33.refs_2_.refs_6_, ...), custom_call_target="tpu_custom_call" | custom-call | flops 452984832 | bytes 1572864 | tf_op jit(solution)/shard_map/project/pallas_call | solution.py:835
  52.9 2.7 %project.5 = (bf16[768,1024]{1,0:T(8,128)(2,1)S(1)}, bf16[3,192,2048]{2,1,0:T(8,128)(2,1)S(1)}, bf16[3,2048,128]{2,1,0:T(8,128)(2,1)S(1)}) custom-call(s32[6]{0:T(128)S(1)} %stack.42.info, bf16[256,768]{1,0:T(8,128)(2,1)} %collective-permute-done.8.refs_0_, ...), custom_call_target="tpu_custom_call", output_to_operand_aliasing={{0}: (6, {}), {1}: (7, {}), {2}: (8, {})} | custom-call | flops 452984832 | bytes 1572864 | tf_op jit(solution)/shard_map/project/pallas_call | solution.py:835
  55.6 2.7 %project.6 = (bf16[768,1024]{1,0:T(8,128)(2,1)S(1)}, bf16[3,192,2048]{2,1,0:T(8,128)(2,1)S(1)}, bf16[3,2048,128]{2,1,0:T(8,128)(2,1)S(1)}) custom-call(s32[6]{0:T(128)S(1)} %stack.42.info, bf16[256,768]{1,0:T(8,128)(2,1)} %collective-permute-done.6.refs_0_, ...), custom_call_target="tpu_custom_call", output_to_operand_aliasing={{0}: (6, {}), {1}: (7, {}), {2}: (8, {})} | custom-call | flops 452984832 | bytes 1572864 | tf_op jit(solution)/shard_map/project/pallas_call | solution.py:835
  58.5 1.9 collective-permute-done.11.refs_1_
  60.4 3.0 %project.7 = (bf16[768,1024]{1,0:T(8,128)(2,1)S(1)}, bf16[3,192,2048]{2,1,0:T(8,128)(2,1)S(1)}, bf16[3,2048,128]{2,1,0:T(8,128)(2,1)S(1)}) custom-call(s32[6]{0:T(128)S(1)} %stack.42.info, bf16[256,768]{1,0:T(8,128)(2,1)} %collective-permute-done.5.refs_0_, ...), custom_call_target="tpu_custom_call", output_to_operand_aliasing={{0}: (6, {}), {1}: (7, {}), {2}: (8, {})} | custom-call | flops 452984832 | bytes 1572864 | tf_op jit(solution)/shard_map/project/pallas_call | solution.py:835
  63.4 13.5 %attend.1 = (bf16[192,256]{1,0:T(8,128)(2,1)S(1)}, bf16[192,256]{1,0:T(8,128)(2,1)S(1)}, bf16[192,256]{1,0:T(8,128)(2,1)S(1)}, bf16[192,256]{1,0:T(8,128)(2,1)S(...) custom-call(s32[3,1,2048]{2,1,0:T(1,128)S(1)} %get-tuple-element.104.ids_all.ids_own, ...), custom_call_target="tpu_custom_call" | custom-call | flops 9663676416 | bytes 8000000 | tf_op jit(solution)/shard_map/attend/pallas_call | solution.py:874
  77.2 4.3 %collective-permute-start.13 = (bf16[192,256]{1,0:T(8,128)(2,1)S(1)}, bf16[192,256]{1,0:T(8,128)(2,1)S(1)}, u32[]{:S(2)}, u32[]{:S(2)}) collective-permute-start(bf16[192,256]{1,0:T(8,128)(2,1)S(1)} %get-tuple-element.124), channel_id=1, source_target_pairs={{0,4},{1,5},{2,6},{3,7},{4,0},{5,1},{6,2},{7,3},{8,12},{9,13},{10,... | collective-permute-start | bytes 294920 | tf_op jit(solution)/shard_map/ppermute | solution.py:712
  82.4 5.4 %collective-permute-done.13.refs_2_ = bf16[192,256]{1,0:T(8,128)(2,1)S(1)} collective-permute-done((bf16[192,256]{1,0:T(8,128)(2,1)S(1)}, bf16[192,256]{1,0:T(8,128)(2,1)S(1)}, u32[]{:S(2)}, u32[]{:S(2)}) %collective-permute-start.13) | collective-permute-done | bytes 98336 | tf_op jit(solution)/shard_map/ppermute | solution.py:712
  87.8 2.3 collective-permute-done.14.refs_3_
  90.1 2.3 copy-done.25
  92.4 11.0 %feed.1 = (bf16[256,768]{1,0:T(8,128)(2,1)}, f32[256,768]{1,0:T(8,128)S(1)}, bf16[256,5376]{1,0:T(8,128)(2,1)S(1)}, bf16[784,256]{1,0:T(8,128)(2,1)S(1)}, bf16[2...) custom-call(s32[6]{0:T(128)S(1)} %stack.42.info, ...), custom_call_target="tpu_custom_call" | custom-call | flops 4831838208 | bytes 9437184 | tf_op jit(solution)/shard_map/feed/pallas_call | solution.py:919
  107.5 2.9 %collective-permute-start.17 = (bf16[192,256]{1,0:T(8,128)(2,1)S(1)}, bf16[192,256]{1,0:T(8,128)(2,1)S(1)}, u32[]{:S(2)}, u32[]{:S(2)}) collective-permute-start(bf16[192,256]{1,0:T(8,128)(2,1)S(1)} %get-tuple-element.130), channel_id=1, source_target_pairs={{0,2},{1,3},{2,4},{3,5},{4,6},{5,7},{6,0},{7,1},{8,10},{9,11},{10,... | collective-permute-start | bytes 294920 | tf_op jit(solution)/shard_map/ppermute | solution.py:712
  110.4 1.8 copy-done.27
  112.2 7.2 %weights.1 = (bf16[2,4,112,768]{3,2,1,0:T(8,128)(2,1)S(1)}, bf16[2,4,112,768]{3,2,1,0:T(8,128)(2,1)S(1)}, bf16[2,4,112,768]{3,2,1,0:T(8,128)(2,1)S(1)}, bf16[2,4,112,768]{3,2,1,0:T(8,128)(2,1)S(1)}) custom-call(s32[6]{0:T(128)S(1)} %stack.42.info, bf16[256,5376]{1,0:T(8,128)(2,1)S(1)} %copy-done.27, ...), custom_call_target="tpu_custom_call" | custom-call | flops 4831838208 | bytes 14155776 | tf_op jit(solution)/shard_map/weights/pallas_call | solution.py:962
  121.9 1.5 collective-permute-start.26
  123.4 20.7 %back.1 = (bf16[4,192,256]{2,1,0:T(8,128)(2,1)S(1)}, f32[3,128,1024]{2,1,0:T(8,128)S(1)}, bf16[3,128,1024]{2,1,0:T(8,128)(2,1)S(1)}) custom-call(s32[3,1,2048]{2,1,0:T(1,128)S(1)} %get-tuple-element.104.ids_all.ids_own, bf16[3,192,2048]{2,1,0:T(8,128)(2,1)S(1)} %get-tuple-element.120.feat, bf16[3,2048,128]{2,1,0:T(8,128)(2,1)S(1)} %get-tuple-element.121.kv, ...), custom_call_target="tpu_custom_call" | custom-call | flops 22548578304 | bytes 10000000 | tf_op jit(solution)/shard_map/back/pallas_call | solution.py:1123
  144.2 2.3 collective-permute-done.21.refs_0_
  146.7 9.0 %collective-permute-done.22.refs_1_ = bf16[3,192,256]{2,1,0:T(8,128)(2,1)S(1)} collective-permute-done((bf16[3,192,256]{2,1,0:T(8,128)(2,1)S(1)}, bf16[3,192,256]{2,1,0:T(8,128)(2,1)S(1)}, u32[]{:S(2)}, u32[]{:S(2)}) %collective-permute-start.22) | collective-permute-done | bytes 294944 | tf_op jit(solution)/shard_map/ppermute | solution.py:712
  157.8 2.3 inward.1
  160.1 1.9 collective-permute-start.23
  162.0 19.0 %collective-permute-done.23.refs_2_ = bf16[3,192,256]{2,1,0:T(8,128)(2,1)S(1)} collective-permute-done((bf16[3,192,256]{2,1,0:T(8,128)(2,1)S(1)}, bf16[3,192,256]{2,1,0:T(8,128)(2,1)S(1)}, u32[]{:S(2)}, u32[]{:S(2)}) %collective-permute-start.23) | collective-permute-done | bytes 294944 | tf_op jit(solution)/shard_map/ppermute | solution.py:712
  185.2 9.8 %collective-permute-done.29.refs_1_ = bf16[224,768]{1,0:T(8,128)(2,1)S(1)} collective-permute-done((bf16[224,768]{1,0:T(8,128)(2,1)S(1)}, bf16[224,768]{1,0:T(8,128)(2,1)S(1)}, u32[]{:S(2)}, u32[]{:S(2)}) %collective-permute-start.29) | collective-permute-done | bytes 344096 | tf_op jit(solution)/shard_map/ppermute | solution.py:712
  196.3 1.5 collective-permute-start.33
  197.8 2.0 collective-permute-start.30
  199.8 3.2 %collective-permute-done.34 = bf16[2,112,576]{2,1,0:T(8,128)(2,1)S(1)} collective-permute-done((bf16[2,112,576]{2,1,0:T(8,128)(2,1)S(1)}, bf16[2,112,576]{2,1,0:T(8,128)(2,1)S(1)}, u32[]{:S(2)}, u32[]{:S(2)}) %collective-permute-start.34) | collective-permute-done | bytes 258080 | tf_op jit(solution)/shard_map/ppermute | solution.py:719
  204.1 9.0 %collective-permute-done.30.refs_2_ = bf16[224,768]{1,0:T(8,128)(2,1)S(1)} collective-permute-done((bf16[224,768]{1,0:T(8,128)(2,1)S(1)}, bf16[224,768]{1,0:T(8,128)(2,1)S(1)}, u32[]{:S(2)}, u32[]{:S(2)}) %collective-permute-start.30) | collective-permute-done | bytes 344096 | tf_op jit(solution)/shard_map/ppermute | solution.py:712
  213.6 3.1 %collective-permute-start.31 = (bf16[224,768]{1,0:T(8,128)(2,1)}, bf16[224,768]{1,0:T(8,128)(2,1)}, u32[]{:S(2)}, u32[]{:S(2)}) collective-permute-start(bf16[224,768]{1,0:T(8,128)(2,1)} %get-tuple-element.162), channel_id=1, source_target_pairs={{0,6},{1,7},{2,0},{3,1},{4,2},{5,3},{6,4},{7,5},{8,14},{9,15},{10,... | collective-permute-start | bytes 1032200 | tf_op jit(solution)/shard_map/ppermute | solution.py:712
  217.4 4.4 %collective-permute-done.36 = bf16[2,112,576]{2,1,0:T(8,128)(2,1)S(1)} collective-permute-done((bf16[2,112,576]{2,1,0:T(8,128)(2,1)S(1)}, bf16[2,112,576]{2,1,0:T(8,128)(2,1)S(1)}, u32[]{:S(2)}, u32[]{:S(2)}) %collective-permute-start.36) | collective-permute-done | bytes 258080 | tf_op jit(solution)/shard_map/ppermute | solution.py:719
  222.6 3.4 %collective-permute-start.38 = (bf16[112,576]{1,0:T(8,128)(2,1)}, bf16[112,576]{1,0:T(8,128)(2,1)}, u32[]{:S(2)}, u32[]{:S(2)}) collective-permute-start(bf16[112,576]{1,0:T(8,128)(2,1)} %get-tuple-element.201), channel_id=1, source_target_pairs={{0,4},{1,5},{2,6},{3,7},{4,0},{5,1},{6,2},{7,3},{8,12},{9,13},{10,... | collective-permute-start | bytes 387080 | tf_op jit(solution)/shard_map/ppermute | solution.py:712
  226.9 2.0 collective-permute-start.37
  232.4 2.0 fourth.1.own
  236.6 4.0 %final.1 = bf16[256,768]{1,0:T(8,128)(2,1)} custom-call(s32[6]{0:T(128)S(1)} %stack.42.info, bf16[3,192,256]{2,1,0:T(8,128)(2,1)S(1)} %copy-done.11, bf16[3,192,256]{2,1,0:T(8,128)(2,1)S(1)} %copy-done.13, bf16[3,192,256]{2,1,0:T(8,128)(2,1)S(1)} %copy-done.15, bf16[3,192,256]{2,1,0:T(8,128)(2,1)S(1)} %copy-done.17, bf16[256,768]{1,0:T(8,128)(2,1)} %refs_4_.3, ...), custom_call_target="tpu_custom_call" | custom-call | flops 905969664 | bytes 3538944 | tf_op jit(solution)/shard_map/final/pallas_call | solution.py:1223
  240.6 2.2 collective-permute-start.42
  247.3 2.0 fusion.1
  249.3 1.8 fusion.4
  252.3 3.8 %spread.1 = (f32[96,3072]{1,0:T(8,128)}, f32[96,768]{1,0:T(8,128)}, f32[384,768]{1,0:T(8,128)}, f32[8,768]{1,0:T(8,128)S(1)}) custom-call(s32[6]{0:T(128)S(1)} %stack.42.info, bf16[224,768]{1,0:T(8,128)(2,1)} %fourth.1.own, bf16[224,768]{1,0:T(8,128)(2,1)} %collective-permute-done.40.from_x, bf16[224,768]{1,0:T(8,128)(2,1)} %collective-permute-done.41.from_y, ...), custom_call_target="tpu_custom_call" | custom-call | flops 1000000 | bytes 4128768 | tf_op jit(solution)/shard_map/spread/pallas_call | solution.py:1040
  (183 shorter events, 37.2 us)
Async XLA Ops:
  0.6 4.8 %collective-permute-start = (bf16[256,768]{1,0:T(8,128)(2,1)}, bf16[256,768]{1,0:T(8,128)(2,1)S(1)}, u32[]{:S(2)}, u32[]{:S(2)}) collective-permute-start(bf16[256,768]{1,0:T(8,128)(2,1)} %refs_4_.3), channel_id=1, source_target_pairs={{0,1},{1,0},{2,3},{3,2},{4,5},{5,4},{6,7},{7,6},{8,9},{9,8},{10,11... | collective-permute-start | bytes 1179656 | tf_op jit(solution)/shard_map/ppermute | solution.py:716
  6.1 12.8 %collective-permute-start.1 = (s32[3,34,128]{2,1,0:T(8,128)S(1)}, s32[3,34,128]{2,1,0:T(8,128)S(1)}, u32[]{:S(2)}, u32[]{:S(2)}) collective-permute-start(s32[3,34,128]{2,1,0:T(8,128)S(1)} %get-tuple-element.205), channel_id=1, source_target_pairs={{0,6},{1,7},{2,0},{3,1},{4,2},{5,3},{6,4},{7,5},{8,14},{9,15},{10,... | collective-permute-start | bytes 156680 | tf_op jit(solution)/shard_map/ppermute | solution.py:712
  6.1 12.8 %collective-permute-start.2 = (s32[3,34,128]{2,1,0:T(8,128)S(1)}, s32[3,34,128]{2,1,0:T(8,128)S(1)}, u32[]{:S(2)}, u32[]{:S(2)}) collective-permute-start(s32[3,34,128]{2,1,0:T(8,128)S(1)} %get-tuple-element.204), channel_id=1, source_target_pairs={{0,4},{1,5},{2,6},{3,7},{4,0},{5,1},{6,2},{7,3},{8,12},{9,13},{10,... | collective-permute-start | bytes 156680 | tf_op jit(solution)/shard_map/ppermute | solution.py:712
  9.2 14.5 %collective-permute-start.3 = (s32[3,34,128]{2,1,0:T(8,128)S(1)}, s32[3,34,128]{2,1,0:T(8,128)S(1)}, u32[]{:S(2)}, u32[]{:S(2)}) collective-permute-start(s32[3,34,128]{2,1,0:T(8,128)S(1)} %get-tuple-element.203), channel_id=1, source_target_pairs={{0,2},{1,3},{2,4},{3,5},{4,6},{5,7},{6,0},{7,1},{8,10},{9,11},{10,... | collective-permute-start | bytes 156680 | tf_op jit(solution)/shard_map/ppermute | solution.py:712
  11.7 29.6 %collective-permute-start.8 = (bf16[256,768]{1,0:T(8,128)(2,1)}, bf16[256,768]{1,0:T(8,128)(2,1)}, u32[]{:S(2)}, u32[]{:S(2)}) collective-permute-start(bf16[256,768]{1,0:T(8,128)(2,1)} %refs_4_.3), channel_id=1, source_target_pairs={{0,6},{1,7},{2,0},{3,1},{4,2},{5,3},{6,4},{7,5},{8,14},{9,15},{10,... | collective-permute-start | bytes 1179656 | tf_op jit(solution)/shard_map/ppermute | solution.py:712
  11.7 29.6 %collective-permute-start.6 = (bf16[256,768]{1,0:T(8,128)(2,1)}, bf16[256,768]{1,0:T(8,128)(2,1)}, u32[]{:S(2)}, u32[]{:S(2)}) collective-permute-start(bf16[256,768]{1,0:T(8,128)(2,1)} %refs_4_.3), channel_id=1, source_target_pairs={{0,2},{1,3},{2,4},{3,5},{4,6},{5,7},{6,0},{7,1},{8,10},{9,11},{10,... | collective-permute-start | bytes 1179656 | tf_op jit(solution)/shard_map/ppermute | solution.py:712
  23.7 25.0 %collective-permute-start.5 = (bf16[256,768]{1,0:T(8,128)(2,1)}, bf16[256,768]{1,0:T(8,128)(2,1)}, u32[]{:S(2)}, u32[]{:S(2)}) collective-permute-start(bf16[256,768]{1,0:T(8,128)(2,1)} %refs_4_.3), channel_id=1, source_target_pairs={{0,4},{1,5},{2,6},{3,7},{4,0},{5,1},{6,2},{7,3},{8,12},{9,13},{10,... | collective-permute-start | bytes 1179656 | tf_op jit(solution)/shard_map/ppermute | solution.py:712
  26.8 1.6 collective-permute-start.4
  41.2 11.7 %collective-permute-start.9 = (bf16[256,768]{1,0:T(8,128)(2,1)}, bf16[256,768]{1,0:T(8,128)(2,1)S(1)}, u32[]{:S(2)}, u32[]{:S(2)}) collective-permute-start(bf16[256,768]{1,0:T(8,128)(2,1)} %collective-permute-done.8.refs_0_), channel_id=1, source_target_pairs={{0,1},{1,0},{2,3},{3,2},{4,5},{5,4},{6,7},{7,6},{8,9},{9,8},{10,11... | collective-permute-start | bytes 1179656 | tf_op jit(solution)/shard_map/ppermute | solution.py:716
  48.7 7.0 %collective-permute-start.7 = (bf16[256,768]{1,0:T(8,128)(2,1)}, bf16[256,768]{1,0:T(8,128)(2,1)S(1)}, u32[]{:S(2)}, u32[]{:S(2)}) collective-permute-start(bf16[256,768]{1,0:T(8,128)(2,1)} %collective-permute-done.6.refs_0_), channel_id=1, source_target_pairs={{0,1},{1,0},{2,3},{3,2},{4,5},{5,4},{6,7},{7,6},{8,9},{9,8},{10,11... | collective-permute-start | bytes 1179656 | tf_op jit(solution)/shard_map/ppermute | solution.py:716
  48.7 9.7 %collective-permute-start.10 = (bf16[256,768]{1,0:T(8,128)(2,1)}, bf16[256,768]{1,0:T(8,128)(2,1)S(1)}, u32[]{:S(2)}, u32[]{:S(2)}) collective-permute-start(bf16[256,768]{1,0:T(8,128)(2,1)} %refs_8_.3), channel_id=1, source_target_pairs={{0,1},{1,0},{2,3},{3,2},{4,5},{5,4},{6,7},{7,6},{8,9},{9,8},{10,11... | collective-permute-start | bytes 1179656 | tf_op jit(solution)/shard_map/ppermute | solution.py:716
  58.4 2.0 collective-permute-start.11
  60.4 29.7 %slice-start = ((s8[4718592]{0:T(1024)(128)(4,1)}), s8[4194304]{0:T(1024)(128)(4,1)S(1)}, s32[]{:S(2)}) async-start(s8[4718592]{0:T(1024)(128)(4,1)} %bitcast.52), calls=%async_computation | async-start | bytes 8388608
  63.4 26.7 %slice-start.1 = ((s8[4718592]{0:T(1024)(128)(4,1)}), s8[524288]{0:T(1024)(128)(4,1)S(1)}, s32[]{:S(2)}) async-start(s8[4718592]{0:T(1024)(128)(4,1)} %bitcast.52), calls=%async_computation.1 | async-start | bytes 1048576
  63.4 26.7 %copy-start.28 = (bf16[768,768]{1,0:T(8,128)(2,1)S(1)}, bf16[768,768]{1,0:T(8,128)(2,1)}, u32[]{:S(2)}) copy-start(bf16[768,768]{1,0:T(8,128)(2,1)} %param.22) | copy-start | bytes 3538948
  63.4 26.7 %copy-start.29 = (bf16[256,768]{1,0:T(8,128)(2,1)S(1)}, bf16[256,768]{1,0:T(8,128)(2,1)}, u32[]{:S(2)}) copy-start(bf16[256,768]{1,0:T(8,128)(2,1)} %refs_8_.3) | copy-start | bytes 1179652
  76.9 5.5 %collective-permute-start.12 = (bf16[192,256]{1,0:T(8,128)(2,1)S(1)}, bf16[192,256]{1,0:T(8,128)(2,1)S(1)}, u32[]{:S(2)}, u32[]{:S(2)}) collective-permute-start(bf16[192,256]{1,0:T(8,128)(2,1)S(1)} %get-tuple-element.123), channel_id=1, source_target_pairs={{0,2},{1,3},{2,4},{3,5},{4,6},{5,7},{6,0},{7,1},{8,10},{9,11},{10,... | collective-permute-start | bytes 294920 | tf_op jit(solution)/shard_map/ppermute | solution.py:712
  77.2 10.6 %collective-permute-start.13 = (bf16[192,256]{1,0:T(8,128)(2,1)S(1)}, bf16[192,256]{1,0:T(8,128)(2,1)S(1)}, u32[]{:S(2)}, u32[]{:S(2)}) collective-permute-start(bf16[192,256]{1,0:T(8,128)(2,1)S(1)} %get-tuple-element.124), channel_id=1, source_target_pairs={{0,4},{1,5},{2,6},{3,7},{4,0},{5,1},{6,2},{7,3},{8,12},{9,13},{10,... | collective-permute-start | bytes 294920 | tf_op jit(solution)/shard_map/ppermute | solution.py:712
  81.5 8.5 %collective-permute-start.14 = (bf16[192,256]{1,0:T(8,128)(2,1)S(1)}, bf16[192,256]{1,0:T(8,128)(2,1)S(1)}, u32[]{:S(2)}, u32[]{:S(2)}) collective-permute-start(bf16[192,256]{1,0:T(8,128)(2,1)S(1)} %get-tuple-element.125), channel_id=1, source_target_pairs={{0,6},{1,7},{2,0},{3,1},{4,2},{5,3},{6,4},{7,5},{8,14},{9,15},{10,... | collective-permute-start | bytes 294920 | tf_op jit(solution)/shard_map/ppermute | solution.py:712
  104.3 6.1 %collective-permute-start.18 = (bf16[256,5376]{1,0:T(8,128)(2,1)S(1)}, bf16[256,5376]{1,0:T(8,128)(2,1)S(1)}, u32[]{:S(2)}, u32[]{:S(2)}) collective-permute-start(bf16[256,5376]{1,0:T(8,128)(2,1)S(1)} %get-tuple-element.131.refs_0_.refs_2_), channel_id=1, source_target_pairs={{0,1},{1,0},{2,3},{3,2},{4,5},{5,4},{6,7},{7,6},{8,9},{9,8},{10,11... | collective-permute-start | bytes 8257544 | tf_op jit(solution)/shard_map/ppermute | solution.py:716
  105.8 4.6 %collective-permute-start.19 = (bf16[784,256]{1,0:T(8,128)(2,1)S(1)}, bf16[784,256]{1,0:T(8,128)(2,1)S(1)}, u32[]{:S(2)}, u32[]{:S(2)}) collective-permute-start(bf16[784,256]{1,0:T(8,128)(2,1)S(1)} %get-tuple-element.134), channel_id=1, source_target_pairs={{0,1},{1,0},{2,3},{3,2},{4,5},{5,4},{6,7},{7,6},{8,9},{9,8},{10,11... | collective-permute-start | bytes 1204232 | tf_op jit(solution)/shard_map/ppermute | solution.py:716
  106.4 13.1 %collective-permute-start.15 = (bf16[192,256]{1,0:T(8,128)(2,1)S(1)}, bf16[192,256]{1,0:T(8,128)(2,1)S(1)}, u32[]{:S(2)}, u32[]{:S(2)}) collective-permute-start(bf16[192,256]{1,0:T(8,128)(2,1)S(1)} %get-tuple-element.128), channel_id=1, source_target_pairs={{0,6},{1,7},{2,0},{3,1},{4,2},{5,3},{6,4},{7,5},{8,14},{9,15},{10,... | collective-permute-start | bytes 294920 | tf_op jit(solution)/shard_map/ppermute | solution.py:712
  106.4 13.1 %collective-permute-start.16 = (bf16[192,256]{1,0:T(8,128)(2,1)S(1)}, bf16[192,256]{1,0:T(8,128)(2,1)S(1)}, u32[]{:S(2)}, u32[]{:S(2)}) collective-permute-start(bf16[192,256]{1,0:T(8,128)(2,1)S(1)} %get-tuple-element.129), channel_id=1, source_target_pairs={{0,4},{1,5},{2,6},{3,7},{4,0},{5,1},{6,2},{7,3},{8,12},{9,13},{10,... | collective-permute-start | bytes 294920 | tf_op jit(solution)/shard_map/ppermute | solution.py:712
  107.5 12.0 %collective-permute-start.17 = (bf16[192,256]{1,0:T(8,128)(2,1)S(1)}, bf16[192,256]{1,0:T(8,128)(2,1)S(1)}, u32[]{:S(2)}, u32[]{:S(2)}) collective-permute-start(bf16[192,256]{1,0:T(8,128)(2,1)S(1)} %get-tuple-element.130), channel_id=1, source_target_pairs={{0,2},{1,3},{2,4},{3,5},{4,6},{5,7},{6,0},{7,1},{8,10},{9,11},{10,... | collective-permute-start | bytes 294920 | tf_op jit(solution)/shard_map/ppermute | solution.py:712
  120.3 3.1 %collective-permute-start.20 = (f32[3,80,128]{2,1,0:T(8,128)S(1)}, f32[3,80,128]{2,1,0:T(8,128)S(1)}, u32[]{:S(2)}, u32[]{:S(2)}) collective-permute-start(f32[3,80,128]{2,1,0:T(8,128)S(1)} %sums.1.refs_7_), channel_id=1, source_target_pairs={{0,1},{1,0},{2,3},{3,2},{4,5},{5,4},{6,7},{7,6},{8,9},{9,8},{10,11... | collective-permute-start | bytes 368648 | tf_op jit(solution)/shard_map/ppermute | solution.py:716
  120.4 35.4 %collective-permute-start.25 = (bf16[2,4,112,768]{3,2,1,0:T(8,128)(2,1)S(1)}, bf16[2,4,112,768]{3,2,1,0:T(8,128)(2,1)S(1)}, u32[]{:S(2)}, u32[]{:S(2)}) collective-permute-start(bf16[2,4,112,768]{3,2,1,0:T(8,128)(2,1)S(1)} %get-tuple-element.150), channel_id=1, source_target_pairs={{0,8},{8,0},{16,24},{24,16},{1,9},{9,1},{17,25},{25,17},{2,10},{10... | collective-permute-start | bytes 4128776 | tf_op jit(solution)/shard_map/ppermute | solution.py:719
  121.9 33.9 %collective-permute-start.26 = (bf16[2,4,112,768]{3,2,1,0:T(8,128)(2,1)S(1)}, bf16[2,4,112,768]{3,2,1,0:T(8,128)(2,1)S(1)}, u32[]{:S(2)}, u32[]{:S(2)}) collective-permute-start(bf16[2,4,112,768]{3,2,1,0:T(8,128)(2,1)S(1)} %get-tuple-element.151), channel_id=1, source_target_pairs={{0,16},{8,24},{16,0},{24,8},{1,17},{9,25},{17,1},{25,9},{2,18},{10... | collective-permute-start | bytes 4128776 | tf_op jit(solution)/shard_map/ppermute | solution.py:719
  144.1 2.4 collective-permute-start.21
  146.7 9.1 %collective-permute-start.22 = (bf16[3,192,256]{2,1,0:T(8,128)(2,1)S(1)}, bf16[3,192,256]{2,1,0:T(8,128)(2,1)S(1)}, u32[]{:S(2)}, u32[]{:S(2)}) collective-permute-start(bf16[3,192,256]{2,1,0:T(8,128)(2,1)S(1)} %get-tuple-element.164.refs_1_), channel_id=1, source_target_pairs={{0,2},{1,3},{2,4},{3,5},{4,6},{5,7},{6,0},{7,1},{8,10},{9,11},{10,... | collective-permute-start | bytes 884744 | tf_op jit(solution)/shard_map/ppermute | solution.py:712
  156.5 27.3 %collective-permute-start.27 = (bf16[4,112,768]{2,1,0:T(8,128)(2,1)S(1)}, bf16[4,112,768]{2,1,0:T(8,128)(2,1)S(1)}, u32[]{:S(2)}, u32[]{:S(2)}) collective-permute-start(bf16[4,112,768]{2,1,0:T(8,128)(2,1)S(1)} %get-tuple-element.155), channel_id=1, source_target_pairs={{0,16},{8,24},{16,0},{24,8},{1,17},{9,25},{17,1},{25,9},{2,18},{10... | collective-permute-start | bytes 2064392 | tf_op jit(solution)/shard_map/ppermute | solution.py:719
  157.0 26.9 %collective-permute-start.28 = (bf16[4,112,768]{2,1,0:T(8,128)(2,1)S(1)}, bf16[4,112,768]{2,1,0:T(8,128)(2,1)S(1)}, u32[]{:S(2)}, u32[]{:S(2)}) collective-permute-start(bf16[4,112,768]{2,1,0:T(8,128)(2,1)S(1)} %get-tuple-element.156), channel_id=1, source_target_pairs={{0,8},{8,0},{16,24},{24,16},{1,9},{9,1},{17,25},{25,17},{2,10},{10... | collective-permute-start | bytes 2064392 | tf_op jit(solution)/shard_map/ppermute | solution.py:719
  160.0 24.9 %collective-permute-start.32 = (bf16[4,112,576]{2,1,0:T(8,128)(2,1)S(1)}, bf16[4,112,576]{2,1,0:T(8,128)(2,1)S(1)}, u32[]{:S(2)}, u32[]{:S(2)}) collective-permute-start(bf16[4,112,576]{2,1,0:T(8,128)(2,1)S(1)} %get-tuple-element.169), channel_id=1, source_target_pairs={{0,1},{1,0},{2,3},{3,2},{4,5},{5,4},{6,7},{7,6},{8,9},{9,8},{10,11... | collective-permute-start | bytes 1548296 | tf_op jit(solution)/shard_map/ppermute | solution.py:716
  160.1 20.8 %collective-permute-start.23 = (bf16[3,192,256]{2,1,0:T(8,128)(2,1)S(1)}, bf16[3,192,256]{2,1,0:T(8,128)(2,1)S(1)}, u32[]{:S(2)}, u32[]{:S(2)}) collective-permute-start(bf16[3,192,256]{2,1,0:T(8,128)(2,1)S(1)} %get-tuple-element.165.refs_2_), channel_id=1, source_target_pairs={{0,4},{1,5},{2,6},{3,7},{4,0},{5,1},{6,2},{7,3},{8,12},{9,13},{10,... | collective-permute-start | bytes 884744 | tf_op jit(solution)/shard_map/ppermute | solution.py:712
  162.0 21.1 %collective-permute-start.24 = (bf16[3,192,256]{2,1,0:T(8,128)(2,1)S(1)}, bf16[3,192,256]{2,1,0:T(8,128)(2,1)S(1)}, u32[]{:S(2)}, u32[]{:S(2)}) collective-permute-start(bf16[3,192,256]{2,1,0:T(8,128)(2,1)S(1)} %get-tuple-element.166.refs_3_), channel_id=1, source_target_pairs={{0,6},{1,7},{2,0},{3,1},{4,2},{5,3},{6,4},{7,5},{8,14},{9,15},{10,... | collective-permute-start | bytes 884744 | tf_op jit(solution)/shard_map/ppermute | solution.py:712
  185.0 10.0 %collective-permute-start.29 = (bf16[224,768]{1,0:T(8,128)(2,1)S(1)}, bf16[224,768]{1,0:T(8,128)(2,1)S(1)}, u32[]{:S(2)}, u32[]{:S(2)}) collective-permute-start(bf16[224,768]{1,0:T(8,128)(2,1)S(1)} %get-tuple-element.160), channel_id=1, source_target_pairs={{0,2},{1,3},{2,4},{3,5},{4,6},{5,7},{6,0},{7,1},{8,10},{9,11},{10,... | collective-permute-start | bytes 1032200 | tf_op jit(solution)/shard_map/ppermute | solution.py:712
  195.0 27.6 %copy-start.6 = (bf16[224,768]{1,0:T(8,128)(2,1)}, bf16[224,768]{1,0:T(8,128)(2,1)S(1)}, u32[]{:S(2)}) copy-start(bf16[224,768]{1,0:T(8,128)(2,1)S(1)} %collective-permute-done.29.refs_1_) | copy-start | bytes 1032196
  195.0 8.0 %collective-permute-start.34 = (bf16[2,112,576]{2,1,0:T(8,128)(2,1)S(1)}, bf16[2,112,576]{2,1,0:T(8,128)(2,1)S(1)}, u32[]{:S(2)}, u32[]{:S(2)}) collective-permute-start(bf16[2,112,576]{2,1,0:T(8,128)(2,1)S(1)} %get-tuple-element.171), channel_id=1, source_target_pairs={{0,16},{8,24},{16,0},{24,8},{1,17},{9,25},{17,1},{25,9},{2,18},{10... | collective-permute-start | bytes 774152 | tf_op jit(solution)/shard_map/ppermute | solution.py:719
  196.3 7.7 %collective-permute-start.33 = (bf16[2,112,576]{2,1,0:T(8,128)(2,1)S(1)}, bf16[2,112,576]{2,1,0:T(8,128)(2,1)S(1)}, u32[]{:S(2)}, u32[]{:S(2)}) collective-permute-start(bf16[2,112,576]{2,1,0:T(8,128)(2,1)S(1)} %get-tuple-element.170), channel_id=1, source_target_pairs={{0,8},{8,0},{16,24},{24,16},{1,9},{9,1},{17,25},{25,17},{2,10},{10... | collective-permute-start | bytes 774152 | tf_op jit(solution)/shard_map/ppermute | solution.py:719
  197.8 15.2 %collective-permute-start.30 = (bf16[224,768]{1,0:T(8,128)(2,1)S(1)}, bf16[224,768]{1,0:T(8,128)(2,1)S(1)}, u32[]{:S(2)}, u32[]{:S(2)}) collective-permute-start(bf16[224,768]{1,0:T(8,128)(2,1)S(1)} %get-tuple-element.161), channel_id=1, source_target_pairs={{0,4},{1,5},{2,6},{3,7},{4,0},{5,1},{6,2},{7,3},{8,12},{9,13},{10,... | collective-permute-start | bytes 1032200 | tf_op jit(solution)/shard_map/ppermute | solution.py:712
  213.1 8.8 %collective-permute-start.36 = (bf16[2,112,576]{2,1,0:T(8,128)(2,1)S(1)}, bf16[2,112,576]{2,1,0:T(8,128)(2,1)S(1)}, u32[]{:S(2)}, u32[]{:S(2)}) collective-permute-start(bf16[2,112,576]{2,1,0:T(8,128)(2,1)S(1)} %add_convert_fusion.3), channel_id=1, source_target_pairs={{0,8},{8,0},{16,24},{24,16},{1,9},{9,1},{17,25},{25,17},{2,10},{10... | collective-permute-start | bytes 774152 | tf_op jit(solution)/shard_map/ppermute | solution.py:719
  213.6 15.9 %collective-permute-start.31 = (bf16[224,768]{1,0:T(8,128)(2,1)}, bf16[224,768]{1,0:T(8,128)(2,1)}, u32[]{:S(2)}, u32[]{:S(2)}) collective-permute-start(bf16[224,768]{1,0:T(8,128)(2,1)} %get-tuple-element.162), channel_id=1, source_target_pairs={{0,6},{1,7},{2,0},{3,1},{4,2},{5,3},{6,4},{7,5},{8,14},{9,15},{10,... | collective-permute-start | bytes 1032200 | tf_op jit(solution)/shard_map/ppermute | solution.py:712
  216.7 9.3 %collective-permute-start.35 = (bf16[2,112,576]{2,1,0:T(8,128)(2,1)S(1)}, bf16[2,112,576]{2,1,0:T(8,128)(2,1)S(1)}, u32[]{:S(2)}, u32[]{:S(2)}) collective-permute-start(bf16[2,112,576]{2,1,0:T(8,128)(2,1)S(1)} %add_convert_fusion.4), channel_id=1, source_target_pairs={{0,16},{8,24},{16,0},{24,8},{1,17},{9,25},{17,1},{25,9},{2,18},{10... | collective-permute-start | bytes 774152 | tf_op jit(solution)/shard_map/ppermute | solution.py:719
  222.6 18.0 %collective-permute-start.38 = (bf16[112,576]{1,0:T(8,128)(2,1)}, bf16[112,576]{1,0:T(8,128)(2,1)}, u32[]{:S(2)}, u32[]{:S(2)}) collective-permute-start(bf16[112,576]{1,0:T(8,128)(2,1)} %get-tuple-element.201), channel_id=1, source_target_pairs={{0,4},{1,5},{2,6},{3,7},{4,0},{5,1},{6,2},{7,3},{8,12},{9,13},{10,... | collective-permute-start | bytes 387080 | tf_op jit(solution)/shard_map/ppermute | solution.py:712
  226.0 16.8 %collective-permute-start.39 = (bf16[112,576]{1,0:T(8,128)(2,1)}, bf16[112,576]{1,0:T(8,128)(2,1)}, u32[]{:S(2)}, u32[]{:S(2)}) collective-permute-start(bf16[112,576]{1,0:T(8,128)(2,1)} %get-tuple-element.202), channel_id=1, source_target_pairs={{0,6},{1,7},{2,0},{3,1},{4,2},{5,3},{6,4},{7,5},{8,14},{9,15},{10,... | collective-permute-start | bytes 387080 | tf_op jit(solution)/shard_map/ppermute | solution.py:712
  226.9 16.0 %collective-permute-start.37 = (bf16[112,576]{1,0:T(8,128)(2,1)}, bf16[112,576]{1,0:T(8,128)(2,1)}, u32[]{:S(2)}, u32[]{:S(2)}) collective-permute-start(bf16[112,576]{1,0:T(8,128)(2,1)} %get-tuple-element.200), channel_id=1, source_target_pairs={{0,2},{1,3},{2,4},{3,5},{4,6},{5,7},{6,0},{7,1},{8,10},{9,11},{10,... | collective-permute-start | bytes 387080 | tf_op jit(solution)/shard_map/ppermute | solution.py:712
  234.4 17.8 %collective-permute-start.40 = (bf16[224,768]{1,0:T(8,128)(2,1)}, bf16[224,768]{1,0:T(8,128)(2,1)}, u32[]{:S(2)}, u32[]{:S(2)}) collective-permute-start(bf16[224,768]{1,0:T(8,128)(2,1)} %fourth.1.own), channel_id=1, source_target_pairs={{0,8},{8,0},{16,24},{24,16},{1,9},{9,1},{17,25},{25,17},{2,10},{10... | collective-permute-start | bytes 1032200 | tf_op jit(solution)/shard_map/ppermute | solution.py:719
  234.9 17.3 %collective-permute-start.41 = (bf16[224,768]{1,0:T(8,128)(2,1)}, bf16[224,768]{1,0:T(8,128)(2,1)}, u32[]{:S(2)}, u32[]{:S(2)}) collective-permute-start(bf16[224,768]{1,0:T(8,128)(2,1)} %fourth.1.own), channel_id=1, source_target_pairs={{0,16},{8,24},{16,0},{24,8},{1,17},{9,25},{17,1},{25,9},{2,18},{10... | collective-permute-start | bytes 1032200 | tf_op jit(solution)/shard_map/ppermute | solution.py:719
  240.6 11.6 %collective-permute-start.42 = (bf16[224,768]{1,0:T(8,128)(2,1)}, bf16[224,768]{1,0:T(8,128)(2,1)S(1)}, u32[]{:S(2)}, u32[]{:S(2)}) collective-permute-start(bf16[224,768]{1,0:T(8,128)(2,1)} %fourth.1.own), channel_id=1, source_target_pairs={{0,24},{8,16},{16,8},{24,0},{1,25},{9,17},{17,9},{25,1},{2,26},{10... | collective-permute-start | bytes 1032200 | tf_op jit(solution)/shard_map/ppermute | solution.py:719
  (35 other events, 193.7 us)

commit v7 on v6

--- a/solution.py
+++ b/solution.py
@@ -563,47 +563,99 @@
             keep_d[place, spot, :rows] = block
 
 
-def second_kernel(keep_u, got_u, keep_d, got_d, send_u, send_d):
-    send_u[...] = (keep_u[0].astype(F32) + got_u[0].astype(F32)).astype(BF)
-    send_d[...] = (keep_d[0].astype(F32) + got_d[0].astype(F32)).astype(BF)
-
-
-def third_kernel(keep_u, got_u, last_u, keep_d, got_d, last_d, *outs):
+def second_kernel(keep_u, got_u, keep_d, got_d, inner, inner_got, to_y, to_x, to_xy):
+    rows = keep_u.shape[2]
+    to_y[:, :rows] = (keep_u[0].astype(F32) + got_u[0].astype(F32)).astype(BF)
+    to_x[:, :rows] = (keep_d[0].astype(F32) + got_d[0].astype(F32)).astype(BF)
+    to_y[:, rows:] = (inner[1].astype(F32) + inner_got[1].astype(F32)).astype(BF)
+    to_x[:, rows:] = (inner[2].astype(F32) + inner_got[2].astype(F32)).astype(BF)
+    to_xy[...] = (inner[3].astype(F32) + inner_got[3].astype(F32)).astype(BF)
+
+
+def third_kernel(keep_u, got_u, keep_d, got_d, inner, inner_got, by_y, by_x, by_xy, *outs):
     rows = keep_u.shape[2]
     for group in range(len(outs)):
-        up = keep_u[0, group].astype(F32) + got_u[0, group].astype(F32) + last_u[group].astype(F32)
-        down = keep_d[0, group].astype(F32) + got_d[0, group].astype(F32) + last_d[group].astype(F32)
-        outs[group][:rows] = up.astype(BF)
-        outs[group][rows:] = down.astype(BF)
-
-
-def fourth_kernel(*refs):
-    parts, out = refs[:-1], refs[-1]
-    total = parts[0][...].astype(F32)
+        up = keep_u[0, group].astype(F32) + got_u[0, group].astype(F32)
+        down = keep_d[0, group].astype(F32) + got_d[0, group].astype(F32)
+        both = inner[0, group].astype(F32) + inner_got[0, group].astype(F32)
+        outs[group][:rows] = (up + by_y[group, :rows].astype(F32)).astype(BF)
+        outs[group][rows : 2 * rows] = (down + by_x[group, :rows].astype(F32)).astype(BF)
+        both = both + by_y[group, rows:].astype(F32) + by_x[group, rows:].astype(F32)
+        outs[group][2 * rows :] = (both + by_xy[group].astype(F32)).astype(BF)
+
+
+def fourth_kernel(info, *refs, groups, high, feats):
+    parts, out, turned = refs[:groups], refs[groups], refs[groups + 1]
+    total = parts[0][: 2 * high].astype(F32)
     for part in parts[1:]:
-        total = total + part[...].astype(F32)
-    out[...] = total.astype(BF)
-
-
-def spread_kernel(info, own, from_x, from_y, from_xy, up_ref, out_ref, down_ref, norm_ref):
+        total = total + part[: 2 * high].astype(F32)
+    out[: 2 * high] = total.astype(BF)
+    third = feats // 3
+    lines = turned.shape[1]
+    for group in range(groups):
+        turned[group] = parts[group][2 * high :].astype(F32)
+    for kind in range(3):
+        found = []
+        for owner in range(groups):
+            spot = lax.rem(info[0] + groups - owner, groups)
+            found.append(turned[spot, :, kind * third : (kind + 1) * third])
+        at = 2 * high + kind * lines
+        out[at : at + lines] = jnp.concatenate(found, axis=1).astype(BF)
+
+
+def spread_kernel(
+    info, own, from_x, from_y, from_xy, wq, wkv, pair,
+    up_ref, out_ref, down_ref, norm_ref, gq_ref, gkv_ref, vec_ref, sums, *, high,
+):
     index = pl.program_id(0)
-    rows = up_ref.shape[0]
-    quarter = out_ref.shape[0] // 4
-    high = own.shape[0] // 2
-    for place, part in enumerate((own, from_y, from_x, from_xy)):
+    rows, width = down_ref.shape
+    quarter = rows // 4
+    lines = quarter + 8
+    order_u = (own, from_y, from_x, from_xy)
+    order_d = (own, from_x, from_y, from_xy)
+
+    @pl.when(index == 0)
+    def first():
+        for place, part in enumerate(order_u):
+
+            @pl.when(info[3] == place)
+            def take(part=part):
+                for kind in range(3):
+                    at = 2 * high + kind * lines
+                    sums[kind] = part[at : at + lines].astype(F32)[quarter:]
+
+    for place, part in enumerate(order_u):
 
         @pl.when(index == place)
         def upper(part=part):
             up_ref[...] = part[:rows].astype(F32)
             at = pl.multiple_of(lax.bitwise_xor(index, info[3]) * quarter, 8)
             out_ref[pl.ds(at, 16), :] = part[rows:high].astype(F32)
-
-    for place, part in enumerate((own, from_x, from_y, from_xy)):
+            spot = pl.ds(at, quarter)
+            shift, gain = pair[spot, 0:1], pair[spot, 1:2]
+            gain_sum, shift_sum = 0.0, 0.0
+            for kind in range(3):
+                base = 2 * high + kind * lines
+                block = part[base : base + lines].astype(F32)[:quarter]
+                line = sums[kind, 0:1]
+                if kind == 0:
+                    weight = wq[spot, :]
+                    gq_ref[spot, :] = block + shift * line
+                else:
+                    lanes = slice((kind - 1) * width, kind * width)
+                    weight = wkv[spot, lanes]
+                    gkv_ref[spot, lanes] = block + shift * line
+                gain_sum = gain_sum + jnp.sum(weight * block, axis=1, keepdims=True)
+                shift_sum = shift_sum + jnp.sum(weight * line, axis=1, keepdims=True)
+            lane = lax.broadcasted_iota(jnp.int32, (quarter, vec_ref.shape[1]), 1)
+            vec_ref[spot, :] = jnp.where(lane == 0, gain_sum / gain, shift_sum)
+
+    for place, part in enumerate(order_d):
 
         @pl.when(index == place)
         def lower(part=part):
             down_ref[...] = part[high : high + rows].astype(F32)
-            tail = part[high + rows :].astype(F32)
+            tail = part[high + rows : 2 * high].astype(F32)
             at = pl.multiple_of(lax.bitwise_xor(index, info[4]) * quarter + 16, 8)
             out_ref[pl.ds(at, quarter - 16), :] = tail[: quarter - 16]
 
@@ -612,9 +664,11 @@
                 norm_ref[...] = tail[quarter - 16 :]
 
 
-def inward_kernel(info, *refs, groups, fast):
-    parts, hat_ref = refs[:groups], refs[groups]
-    outs = refs[groups + 1 :]
+def inward_kernel(info, *refs, groups, gots, fast):
+    join_refs, hat_ref = refs[: 2 + gots], refs[2 + gots]
+    parts = refs[3 + gots : 3 + gots + groups]
+    outs = refs[3 + gots + groups :]
+    join_kernel(*join_refs, *parts, groups=groups)
     heads, triple, rows = parts[0].shape
     hs = triple // 3
     total, sums = None, None
@@ -632,15 +686,23 @@
         return
     own_ref, far_ref = outs
     block = total.shape[0] // (2 * groups)
-    low_sums = sums.astype(BF)
+    quarter = block // 4
+    wide = total.shape[1]
+    edge = wide // 128 * 128
+    blank = jnp.zeros(own_ref.shape[:3] + (own_ref.shape[3] - edge,), BF)
+    own_ref[..., edge:] = blank
+    far_ref[..., edge:] = blank
     for group in range(groups):
         spot = lax.rem(group + groups - info[0], groups)
-        first = total[2 * group * block : (2 * group + 1) * block].astype(BF)
-        second = total[(2 * group + 1) * block : (2 * group + 2) * block].astype(BF)
-        own_ref[spot, :block] = jnp.where(info[1] == 0, first, second)
-        far_ref[spot, :block] = jnp.where(info[1] == 0, second, first)
-        own_ref[spot, block:] = low_sums
-        far_ref[spot, block:] = low_sums
+        for part in range(4):
+            place = lax.bitwise_xor(part, info[3])
+            found = []
+            for parity in range(2):
+                at = (2 * group + parity) * block + part * quarter
+                lines = jnp.concatenate([total[at : at + quarter], sums[:8]], axis=0)
+                found.append(lines.astype(BF))
+            own_ref[place, spot, :, :wide] = jnp.where(info[1] == 0, found[0], found[1])
+            far_ref[place, spot, :, :wide] = jnp.where(info[1] == 0, found[1], found[0])
 
 
 def final_kernel(info, *refs, groups):
@@ -804,12 +866,8 @@
     split_peers = peers if peers <= 2 else 1
     for group in sorted(range(groups), key=lambda g: min(g, groups - g)):
         arrival = mine[group]
-        if 1 < group < groups - 1:
-            arrival = after(arrival, held, cot_got)
-        elif group == 1:
-            arrival = after(arrival, bias)
-        elif group:
-            arrival = after(arrival, bias, [mine[hop] for hop in range(2, group)])
+        if group == 1:
+            arrival = after(arrival, bias, held, cot_got, [mine[hop] for hop in range(2, groups)])
         chunk = [arrival]
         chunk += early if group == 0 else [along_peers(arrival, -hop) for hop in range(1, peers)]
         if peers > 2:
@@ -977,88 +1035,94 @@
         )(info, far, got, far, got, act_own, got, low_own, low_got, cotangent, *cot_got)
         return send_u, keep_u, send_d, keep_d
 
-    def weight_second(keep_u, got_u, keep_d, got_d):
-        shape_u, shape_d = keep_u.shape, keep_d.shape
-        high = shape_u[2]
-
+    def weight_second(keep_u, got_u, keep_d, got_d, inner, inner_got):
         def block(shape, at):
             return pl.BlockSpec((1,) + shape[1:], lambda i: (at, 0, 0, 0))
 
-        next_u, next_d = pl.pallas_call(
+        shape_u = keep_u.shape
+        lines = inner.shape[2]
+        shape = (groups, shape_u[2] + lines, width)
+        small = (groups, lines, width)
+        return pl.pallas_call(
             second_kernel,
             grid=(1,),
-            in_specs=[block(shape_u, 1), block(shape_u, 1), block(shape_d, 1), block(shape_d, 1)],
-            out_specs=[whole(shape_u[1:]), whole(shape_d[1:])],
-            out_shape=[array(shape_u[1:], BF), array(shape_d[1:], BF)],
+            in_specs=[block(shape_u, 1)] * 4 + [whole(inner.shape)] * 2,
+            out_specs=[whole(shape), whole(shape), whole(small)],
+            out_shape=[array(shape, BF), array(shape, BF), array(small, BF)],
             compiler_params=params(20, 1),
-            cost_estimate=cost(groups * high * width * 2, groups * high * width * 12),
+            cost_estimate=cost(groups * shape[1] * width * 2, groups * shape[1] * width * 12),
             name="second",
-        )(keep_u, got_u, keep_d, got_d)
-        return next_u, next_d
-
-    def weight_third(keep_u, got_u, last_u, keep_d, got_d, last_d):
-        shape_u, shape_d = keep_u.shape, keep_d.shape
-        high = shape_u[2]
-
+        )(keep_u, got_u, keep_d, got_d, inner, inner_got)
+
+    def weight_third(keep_u, got_u, keep_d, got_d, inner, inner_got, by_y, by_x, by_xy):
         def block(shape, at):
             return pl.BlockSpec((1,) + shape[1:], lambda i: (at, 0, 0, 0))
 
-        tall = shape_u[2] + shape_d[2]
+        high = keep_u.shape[2]
+        tall = 2 * high + inner.shape[2]
         sums = pl.pallas_call(
             third_kernel,
             grid=(1,),
-            in_specs=[
-                block(shape_u, 0),
-                block(shape_u, 0),
-                whole(shape_u[1:]),
-                block(shape_d, 0),
-                block(shape_d, 0),
-                whole(shape_d[1:]),
-            ],
+            in_specs=[block(keep_u.shape, 0)] * 4
+            + [block(inner.shape, 0)] * 2
+            + [whole(by_y.shape), whole(by_x.shape), whole(by_xy.shape)],
             out_specs=[whole((tall, width))] * groups,
             out_shape=[array((tall, width), BF)] * groups,
             compiler_params=params(24, 1),
             cost_estimate=cost(groups * tall * width * 4, groups * tall * width * 8),
             name="third",
-        )(keep_u, got_u, last_u, keep_d, got_d, last_d)
-        came = [sums[0]] + [along_groups(sums[hop], hop) for hop in range(1, groups)]
-        return came
-
-    def weight_sums(came, shape_u, shape_d):
-        tall = shape_u[2] + shape_d[2]
-        done = pl.pallas_call(
-            fourth_kernel,
-            grid=(1,),
-            in_specs=[whole((tall, width))] * groups,
-            out_specs=whole((tall, width)),
-            out_shape=array((tall, width), BF),
-            compiler_params=params(12, 1),
-            cost_estimate=cost(groups * tall * width, groups * tall * width * 2),
-            name="fourth",
-        )(*came)
+        )(keep_u, got_u, keep_d, got_d, inner, inner_got, by_y, by_x, by_xy)
+        return [sums[0]] + [along_groups(sums[hop], hop) for hop in range(1, groups)]
+
+    def weight_sums(came, high, lines):
+        tall = 2 * high + 3 * lines
+        done = prefetched(
+            functools.partial(fourth_kernel, groups=groups, high=high, feats=3 * feats),
+            (1,),
+            [whole(came[0].shape)] * groups,
+            whole((tall, width)),
+            array((tall, width), BF),
+            16,
+            cost(groups * tall * width, groups * tall * width * 2),
+            "fourth",
+            scratch=[pltpu.VMEM((groups, lines, width), F32)],
+        )(info, *came)
         from_x, from_y, from_xy = (along_dp(done, mask) for mask in (1, 2, 3))
-        total_up, total_out, total_down, norms = prefetched(
-            spread_kernel,
+        at = me * block_rows
+        wq_rows = lax.dynamic_slice_in_dim(w_query, at, block_rows).astype(F32)
+        wkv_rows = lax.dynamic_slice_in_dim(w_keyval, at, block_rows).astype(F32)
+        pair = jnp.stack([shift_one, gain_one] + [shift_one] * 6, axis=1)
+        pair = lax.dynamic_slice_in_dim(pair, at, block_rows)
+        pair, wq_rows, wkv_rows = after((pair, wq_rows, wkv_rows), came[0])
+        found = prefetched(
+            functools.partial(spread_kernel, high=high),
             (4,),
-            [whole((tall, width))] * 4,
+            [whole((tall, width))] * 4
+            + [whole(wq_rows.shape), whole(wkv_rows.shape), whole(pair.shape)],
             [
                 pl.BlockSpec((block_rows, part), lambda i, s: (0, i ^ s[3])),
                 whole((block_rows, width)),
                 pl.BlockSpec((block_rows, width), lambda i, s: (i ^ s[4], 0)),
                 whole((8, width)),
+                whole((block_rows, width)),
+                whole((block_rows, 2 * width)),
+                whole((block_rows, 128)),
             ],
             [
                 array((block_rows, hidden), F32),
                 array((block_rows, width), F32),
                 array((hidden // wide, width), F32),
                 array((8, width), F32),
+                array((block_rows, width), F32),
+                array((block_rows, 2 * width), F32),
+                array((block_rows, 128), F32),
             ],
-            16,
+            20,
             cost(1e6, 4 * tall * width * 6),
             "spread",
-        )(info, done, from_x, from_y, from_xy)
-        norm_own = lax.dynamic_slice_in_dim(norms, me * block_rows, block_rows, axis=1)
-        return total_up, total_out, total_down, norm_own, done
+            scratch=[pltpu.VMEM((3, 8, width), F32)],
+        )(info, done, from_x, from_y, from_xy, wq_rows, wkv_rows, pair)
+        return done, found
 
     masks = [1 << k for k in range(n_dp.bit_length() - 1)]
 
@@ -1144,61 +1208,47 @@
         )
         for hop in range(1, peers)
     ]
-    d_in = pl.pallas_call(
-        functools.partial(join_kernel, groups=groups),
-        grid=(1,),
-        in_specs=[whole(back_shapes[0].shape), whole(back_shapes[1].shape)]
-        + [whole(back_shapes[1].shape)] * len(dkv_got),
-        out_specs=[whole((own_heads, 3 * hs, rows))] * groups,
-        out_shape=[array((own_heads, 3 * hs, rows), BF)] * groups,
-        compiler_params=params(20, 1),
-        cost_estimate=cost(own_rows * feats * 8, own_rows * feats * 16),
-        name="join",
-    )(dq, dkv_own, *dkv_got)
-
-    home = [d_in[0]] + [along_groups(d_in[hop], hop) for hop in range(1, groups)]
-
     tall = block_rows + 16
-    part_spec = [whole((own_heads, 3 * hs, rows))] * groups + [whole((width, own_rows))]
-    inward = functools.partial(
-        prefetched,
-        functools.partial(inward_kernel, groups=groups, fast=fast),
-        (1,),
-        part_spec,
-    )
     spent = cost(2 * own_rows * width * 3 * feats, 4e6)
     if fast:
-        half = groups // 2
-        blocks = (groups, tall, 3 * feats)
+        lines = block_rows // 4 + 8
+        more = [array((4, groups, lines, width), BF)] * 2
+    else:
+        more = [array((width, 3 * feats), F32), array((16, 3 * feats), F32)]
+    if fast:
+        dkv_own = after(dkv_own, got_u, got_d)
+    results = prefetched(
+        functools.partial(inward_kernel, groups=groups, gots=len(dkv_got), fast=fast),
+        (1,),
+        [whole(back_shapes[0].shape)]
+        + [whole(back_shapes[1].shape)] * (1 + len(dkv_got))
+        + [whole((width, own_rows))],
+        [whole((own_heads, 3 * hs, rows))] * groups + [whole(item.shape) for item in more],
+        [array((own_heads, 3 * hs, rows), BF)] * groups + more,
+        28 if fast else 60,
+        spent,
+        "inward",
+    )(info, dq, dkv_own, *dkv_got, hat_own)
+    d_in, more = results[:groups], results[groups:]
+    home = [d_in[0]] + [along_groups(d_in[hop], hop) for hop in range(1, groups)]
+
+    if fast:
+        keep, far = more
+        inner_got = along_peers(far, 1)
         got_u, got_d = after((got_u, got_d), home[1])
-        next_u, next_d = weight_second(keep_u, got_u, keep_d, got_d)
-        keep, far = inward(
-            [whole(blocks)] * 2, [array(blocks, BF)] * 2, 24, spent, "inward"
-        )(info, *after(d_in, next_u, next_d), hat_own)
-        got = along_peers(far, 1)
-        total = keep.astype(F32) + got.astype(F32)
-        one_half, two_half = total[:half].astype(BF), total[half:].astype(BF)
-        last_u, last_d = along_dp(next_u, 2), along_dp(next_d, 1)
-        last_u, last_d = after((last_u, last_d), home)
-        came = weight_third(keep_u, got_u, last_u, keep_d, got_d, last_d)
-        for mask in (1, 2):
-            one_half, two_half = after((one_half, two_half), came[mask])
-            got_one, got_two = along_dp(one_half, mask), along_dp(two_half, 3 - mask)
-            one_half = (one_half.astype(F32) + got_one.astype(F32)).astype(BF)
-            two_half = (two_half.astype(F32) + got_two.astype(F32)).astype(BF)
-        total_up, total_out, total_down, norm_own, done = weight_sums(
-            after(came, one_half, two_half), keep_u.shape, keep_d.shape
+        to_y, to_x, to_xy = weight_second(keep_u, got_u, keep_d, got_d, keep, inner_got)
+        by_y, by_x, by_xy = along_dp(to_y, 2), along_dp(to_x, 1), along_dp(to_xy, 3)
+        by_y, by_x = after((by_y, by_x), home)
+        came = weight_third(
+            keep_u, got_u, keep_d, got_d, keep, inner_got, by_y, by_x, by_xy
         )
+        done, found = weight_sums(came, keep_u.shape[2], lines)
         home = after(home, done)
-        items = [one_half[k] for k in range(half)] + [two_half[k] for k in range(half)]
+        total_up, total_out, total_down, norms, total_query, total_keyval, vector = found
+        norm_own = lax.dynamic_slice_in_dim(norms, me * block_rows, block_rows, axis=1)
+        gain_grad, shift_grad = vector[:, 0], vector[:, 1]
     else:
-        found, more = inward(
-            [whole((width, 3 * feats)), whole((16, 3 * feats))],
-            [array((width, 3 * feats), F32), array((16, 3 * feats), F32)],
-            60,
-            spent,
-            "inward",
-        )(info, *d_in, hat_own)
+        found, more = more
         found = found.reshape(groups, peers, block_rows, 3 * feats)
         more = jnp.broadcast_to(more, (groups, peers, 16, 3 * feats))
         found = jnp.concatenate([found, more], axis=2).astype(BF)
@@ -1218,7 +1268,33 @@
             lax.dynamic_index_in_dim(total, (group_at + hop) % groups, keepdims=False)
             for hop in range(groups)
         ]
-    pieces = [items[0]] + [along_groups(items[hop], hop) for hop in range(1, groups)]
+        pieces = [items[0]] + [along_groups(items[hop], hop) for hop in range(1, groups)]
+        pieces = jnp.stack(pieces)
+        pieces = jnp.stack(
+            [
+                lax.dynamic_index_in_dim(pieces, (group_at + groups - g) % groups, keepdims=False)
+                for g in range(groups)
+            ]
+        ).astype(F32)
+        q_part = pieces[:, :, :feats].transpose(1, 0, 2).reshape(tall, width)
+        kv_part = (
+            pieces[:, :, feats:]
+            .reshape(groups, tall, 2, feats)
+            .transpose(1, 2, 0, 3)
+            .reshape(tall, 2 * width)
+        )
+        at = me * block_rows
+        wq_rows = lax.dynamic_slice_in_dim(w_query, at, block_rows).astype(F32)
+        wkv_rows = lax.dynamic_slice_in_dim(w_keyval, at, block_rows).astype(F32)
+        gain_own = lax.dynamic_slice_in_dim(gain_one, at, block_rows)
+        shift_own = lax.dynamic_slice_in_dim(shift_one, at, block_rows)
+        q_sum, kv_sum = q_part[block_rows], kv_part[block_rows]
+        q_part, kv_part = q_part[:block_rows], kv_part[:block_rows]
+        shift_grad = jnp.sum(wq_rows * q_sum, axis=1) + jnp.sum(wkv_rows * kv_sum, axis=1)
+        along = jnp.sum(wq_rows * q_part, axis=1) + jnp.sum(wkv_rows * kv_part, axis=1)
+        total_query = q_part + shift_own[:, None] * q_sum
+        total_keyval = kv_part + shift_own[:, None] * kv_sum
+        gain_grad = along / gain_own
 
     grad_tokens = prefetched(
         functools.partial(final_kernel, groups=groups),
@@ -1232,38 +1308,15 @@
         "final",
     )(info, *home, tokens, d_resid, gain_row, w_in)
 
-    pieces = jnp.stack(pieces)
-    pieces = jnp.stack(
-        [
-            lax.dynamic_index_in_dim(pieces, (group_at + groups - g) % groups, keepdims=False)
-            for g in range(groups)
-        ]
-    ).astype(F32)
-    q_part = pieces[:, :, :feats].transpose(1, 0, 2).reshape(tall, width)
-    kv_part = (
-        pieces[:, :, feats:]
-        .reshape(groups, tall, 2, feats)
-        .transpose(1, 2, 0, 3)
-        .reshape(tall, 2 * width)
-    )
-    at = me * block_rows
-    wq_rows = lax.dynamic_slice_in_dim(w_query, at, block_rows).astype(F32)
-    wkv_rows = lax.dynamic_slice_in_dim(w_keyval, at, block_rows).astype(F32)
-    gain_own = lax.dynamic_slice_in_dim(gain_one, at, block_rows)
-    shift_own = lax.dynamic_slice_in_dim(shift_one, at, block_rows)
-    q_sum, kv_sum = q_part[block_rows], kv_part[block_rows]
-    q_part, kv_part = q_part[:block_rows], kv_part[:block_rows]
-    shift_grad = jnp.sum(wq_rows * q_sum, axis=1) + jnp.sum(wkv_rows * kv_sum, axis=1)
-    along = jnp.sum(wq_rows * q_part, axis=1) + jnp.sum(wkv_rows * kv_part, axis=1)
     return (
         output,
         grad_tokens,
-        q_part + shift_own[:, None] * q_sum,
-        kv_part + shift_own[:, None] * kv_sum,
+        total_query,
+        total_keyval,
         total_out,
         total_up,
         total_down,
-        along / gain_own,
+        gain_grad,
         shift_grad,
         norm_own[0],
         norm_own[1],

time: 259 us -> 265 us (1.023)
  waiting for transfers between devices: 86.6 us -> 104 us
  starting transfers between devices: 42.7 us -> 35.2 us
  other arithmetic: 9.07 us -> 4.27 us
    ppermute x11 -> x8, waiting for transfers between devices: 8.5 us -> 22.4 us  [along_dp(): return lax.ppermute(values, 'dp', [(i, i ^ mask) for i in range(n_dp)])]
    ppermute x21 -> x18, waiting for transfers between devices: 72.3 us -> 80.2 us  [along_groups(): return lax.ppermute(values, 'wide', pairs)]
    ppermute x21 -> x18, starting transfers between devices: 29.5 us -> 23.7 us  [along_groups(): return lax.ppermute(values, 'wide', pairs)]
    ppermute x11, waiting for transfers between devices: 5.72 us -> 1.45 us  [along_peers(): return lax.ppermute(values, 'wide', pairs)]
    reduce_sum x2 -> x0, other arithmetic: 3.85 us -> none  [the longest x1 2.03 us: per_device(): jnp.sum(wkv_rows * kv_sum, axis=1)]
    pallas_call x6 -> x5, Pallas kernels: 9.76 us -> 11.9 us  [the longest x1 4.84 us: weight_sums(): prefetched(functools.partial(spread_kernel, high=high), (4,), [whole((tal...]
    ppermute x11 -> x8, starting transfers between devices: 11.9 us -> 10.1 us  [along_dp(): return lax.ppermute(values, 'dp', [(i, i ^ mask) for i in range(n_dp)])]
  transfers between devices with their start and end apart: 43 -> 37, of which waited for: 16 -> 17; matrix products, arithmetic and copies ran while one was open for 9% -> 6% of each run, Pallas kernels for 21% -> 19%
where the time goes in v7:
time: 265 us; the launch traced here: 264 us
  waiting for transfers between devices  104 us (39%)
  Pallas kernels  89.9 us (34%)
  starting transfers between devices  35.2 us (13%)
  local copies, waits for them, and re-layouts  28.9 us (11%)
  other arithmetic  4.27 us (2%)
    ppermute x18, waiting for transfers between devices, along_groups(): return lax.ppermute(values, 'wide', pairs)  80.2 us
    ppermute x18, starting transfers between devices, along_groups(): return lax.ppermute(values, 'wide', pairs)  23.7 us
    ppermute x8, waiting for transfers between devices, along_dp(): return lax.ppermute(values, 'dp', [(i, i ^ mask) for i in range(n_dp)])  22.4 us
    unnamed x80, local copies, waits for them, and re-layouts  21.3 us
    pallas_call x1, Pallas kernels, per_device(): pl.pallas_call(functools.partial(back_kernel, size=size, groups=groups, g...  20.4 us
    pallas_call x1, Pallas kernels, per_device(): pl.pallas_call(functools.partial(forward_kernel, size=size, groups=groups...  13.2 us
    pallas_call x1, Pallas kernels, per_device(): prefetched(functools.partial(block_kernel, groups=groups, chunks=chunks,...  11.2 us
    pallas_call x4, Pallas kernels, per_device(): prefetched(functools.partial(project_kernel, peers=split_peers, olds=len(...  11.1 us
  transfers between devices with their start and end apart: 37, of which 17 were waited for; matrix products, arithmetic and copies ran while one was open for 6% of the time, Pallas kernels for 19%

profile of v7, /device:TPU:8, one launch (start us, length us, event | category | flops | bytes accessed | tf_op | source)
XLA Modules:
  0.0 264.3 jit_solution(128852193975683486)
XLA Ops:
  3.3 2.1 dynamic_update_slice.3
  6.1 3.0 %collective-permute-start.2 = (s32[3,34,128]{2,1,0:T(8,128)S(1)}, s32[3,34,128]{2,1,0:T(8,128)S(1)}, u32[]{:S(2)}, u32[]{:S(2)}) collective-permute-start(s32[3,34,128]{2,1,0:T(8,128)S(1)} %get-tuple-element.178), channel_id=1, source_target_pairs={{0,4},{1,5},{2,6},{3,7},{4,0},{5,1},{6,2},{7,3},{8,12},{9,13},{10,... | collective-permute-start | bytes 156680 | tf_op jit(solution)/shard_map/ppermute | solution.py:774
  9.2 2.5 collective-permute-start.3
  11.7 2.0 collective-permute-start.9
  13.7 2.8 %copy.50 = bf16[768,1536]{0,1:T(8,128)(2,1)S(1)} copy(bf16[768,1536]{1,0:T(8,128)(2,1)} %param.21) | data formatting | bytes 4718592 | tf_op args[7]
  16.5 2.4 copy.49
  20.0 1.5 pad_maximum_fusion
  24.4 2.7 %project.4 = (bf16[768,1024]{1,0:T(8,128)(2,1)S(1)}, bf16[3,192,2048]{2,1,0:T(8,128)(2,1)S(1)}, bf16[3,2048,128]{2,1,0:T(8,128)(2,1)S(1)}) custom-call(s32[6]{0:T(128)S(1)} %stack.38.info, bf16[256,768]{1,0:T(8,128)(2,1)} %refs_4_.3, bf16[256,768]{1,0:T(8,128)(2,1)S(1)} %copy-done.3, f32[1,768]{1,0:T(1,128)S(1)} %broadcast_in_dim.31.refs_2_.refs_6_, ...), custom_call_target="tpu_custom_call" | custom-call | flops 452984832 | bytes 1572864 | tf_op jit(solution)/shard_map/project/pallas_call | solution.py:893
  27.1 8.5 %bias.1 = (bf16[3,2048,128]{2,1,0:T(8,128)(2,1)S(1)}, s32[3,1,2048]{2,1,0:T(1,128)S(1)}) custom-call(s32[6]{0:T(128)S(1)} %stack.38.info, s32[3,40,128]{2,1,0:T(8,128)} %table.1.refs_0_, s32[3,40,128]{2,1,0:T(8,128)} %collective-permute-done.4.refs_1_), custom_call_target="tpu_custom_call" | custom-call | flops 201326592 | bytes 1572864 | tf_op jit(solution)/shard_map/bias/pallas_call | solution.py:845
  35.6 5.1 %collective-permute-done.7.refs_0_ = bf16[256,768]{1,0:T(8,128)(2,1)} collective-permute-done((bf16[256,768]{1,0:T(8,128)(2,1)}, bf16[256,768]{1,0:T(8,128)(2,1)}, u32[]{:S(2)}, u32[]{:S(2)}) %collective-permute-start.7) | collective-permute-done | bytes 393248 | tf_op jit(solution)/shard_map/ppermute | solution.py:774
  41.2 7.4 %collective-permute-done.5.refs_0_ = bf16[256,768]{1,0:T(8,128)(2,1)} collective-permute-done((bf16[256,768]{1,0:T(8,128)(2,1)}, bf16[256,768]{1,0:T(8,128)(2,1)}, u32[]{:S(2)}, u32[]{:S(2)}) %collective-permute-start.5) | collective-permute-done | bytes 393248 | tf_op jit(solution)/shard_map/ppermute | solution.py:774
  49.2 1.4 collective-permute-done.11.refs_1_
  50.6 2.7 %project.5 = (bf16[768,1024]{1,0:T(8,128)(2,1)S(1)}, bf16[3,192,2048]{2,1,0:T(8,128)(2,1)S(1)}, bf16[3,2048,128]{2,1,0:T(8,128)(2,1)S(1)}) custom-call(s32[6]{0:T(128)S(1)} %stack.38.info, bf16[256,768]{1,0:T(8,128)(2,1)} %collective-permute-done.9.refs_0_, ...), custom_call_target="tpu_custom_call", output_to_operand_aliasing={{0}: (6, {}), {1}: (7, {}), {2}: (8, {})} | custom-call | flops 452984832 | bytes 1572864 | tf_op jit(solution)/shard_map/project/pallas_call | solution.py:893
  53.3 2.7 %project.6 = (bf16[768,1024]{1,0:T(8,128)(2,1)S(1)}, bf16[3,192,2048]{2,1,0:T(8,128)(2,1)S(1)}, bf16[3,2048,128]{2,1,0:T(8,128)(2,1)S(1)}) custom-call(s32[6]{0:T(128)S(1)} %stack.38.info, bf16[256,768]{1,0:T(8,128)(2,1)} %collective-permute-done.7.refs_0_, ...), custom_call_target="tpu_custom_call", output_to_operand_aliasing={{0}: (6, {}), {1}: (7, {}), {2}: (8, {})} | custom-call | flops 452984832 | bytes 1572864 | tf_op jit(solution)/shard_map/project/pallas_call | solution.py:893
  56.0 3.0 %project.7 = (bf16[768,1024]{1,0:T(8,128)(2,1)S(1)}, bf16[3,192,2048]{2,1,0:T(8,128)(2,1)S(1)}, bf16[3,2048,128]{2,1,0:T(8,128)(2,1)S(1)}) custom-call(s32[6]{0:T(128)S(1)} %stack.38.info, bf16[256,768]{1,0:T(8,128)(2,1)} %collective-permute-done.5.refs_0_, ...), custom_call_target="tpu_custom_call", output_to_operand_aliasing={{0}: (6, {}), {1}: (7, {}), {2}: (8, {})} | custom-call | flops 452984832 | bytes 1572864 | tf_op jit(solution)/shard_map/project/pallas_call | solution.py:893
  59.1 13.2 %attend.1 = (bf16[192,256]{1,0:T(8,128)(2,1)S(1)}, bf16[192,256]{1,0:T(8,128)(2,1)S(1)}, bf16[192,256]{1,0:T(8,128)(2,1)S(1)}, bf16[192,256]{1,0:T(8,128)(2,1)S(...) custom-call(s32[3,1,2048]{2,1,0:T(1,128)S(1)} %get-tuple-element.98.ids_all.ids_own, ...), custom_call_target="tpu_custom_call" | custom-call | flops 9663676416 | bytes 8000000 | tf_op jit(solution)/shard_map/attend/pallas_call | solution.py:932
  73.8 4.3 %collective-permute-start.13 = (bf16[192,256]{1,0:T(8,128)(2,1)S(1)}, bf16[192,256]{1,0:T(8,128)(2,1)S(1)}, u32[]{:S(2)}, u32[]{:S(2)}) collective-permute-start(bf16[192,256]{1,0:T(8,128)(2,1)S(1)} %get-tuple-element.116), channel_id=1, source_target_pairs={{0,4},{1,5},{2,6},{3,7},{4,0},{5,1},{6,2},{7,3},{8,12},{9,13},{10,... | collective-permute-start | bytes 294920 | tf_op jit(solution)/shard_map/ppermute | solution.py:774
  79.0 5.4 %collective-permute-done.13.refs_2_ = bf16[192,256]{1,0:T(8,128)(2,1)S(1)} collective-permute-done((bf16[192,256]{1,0:T(8,128)(2,1)S(1)}, bf16[192,256]{1,0:T(8,128)(2,1)S(1)}, u32[]{:S(2)}, u32[]{:S(2)}) %collective-permute-start.13) | collective-permute-done | bytes 98336 | tf_op jit(solution)/shard_map/ppermute | solution.py:774
  84.4 2.3 collective-permute-done.14.refs_3_
  86.6 2.3 copy-done.22
  89.0 11.2 %feed.1 = (bf16[256,768]{1,0:T(8,128)(2,1)}, f32[256,768]{1,0:T(8,128)S(1)}, bf16[256,5376]{1,0:T(8,128)(2,1)S(1)}, bf16[784,256]{1,0:T(8,128)(2,1)S(1)}, bf16[2...) custom-call(s32[6]{0:T(128)S(1)} %stack.38.info, ...), custom_call_target="tpu_custom_call" | custom-call | flops 4831838208 | bytes 9437184 | tf_op jit(solution)/shard_map/feed/pallas_call | solution.py:977
  101.0 1.5 copy-done.23
  104.2 2.9 %collective-permute-start.17 = (bf16[192,256]{1,0:T(8,128)(2,1)S(1)}, bf16[192,256]{1,0:T(8,128)(2,1)S(1)}, u32[]{:S(2)}, u32[]{:S(2)}) collective-permute-start(bf16[192,256]{1,0:T(8,128)(2,1)S(1)} %get-tuple-element.122), channel_id=1, source_target_pairs={{0,2},{1,3},{2,4},{3,5},{4,6},{5,7},{6,0},{7,1},{8,10},{9,11},{10,... | collective-permute-start | bytes 294920 | tf_op jit(solution)/shard_map/ppermute | solution.py:774
  107.1 1.8 copy-done.24
  108.9 8.3 %weights.1 = (bf16[2,4,112,768]{3,2,1,0:T(8,128)(2,1)S(1)}, bf16[2,4,112,768]{3,2,1,0:T(8,128)(2,1)S(1)}, bf16[2,4,112,768]{3,2,1,0:T(8,128)(2,1)S(1)}, bf16[2,4,112,768]{3,2,1,0:T(8,128)(2,1)S(1)}) custom-call(s32[6]{0:T(128)S(1)} %stack.38.info, bf16[256,5376]{1,0:T(8,128)(2,1)S(1)} %copy-done.24, ...), custom_call_target="tpu_custom_call" | custom-call | flops 4831838208 | bytes 14155776 | tf_op jit(solution)/shard_map/weights/pallas_call | solution.py:1020
  118.1 1.6 collective-permute-start.21
  119.7 1.5 collective-permute-start.22
  121.2 20.4 %back.1 = (bf16[4,192,256]{2,1,0:T(8,128)(2,1)S(1)}, f32[3,128,1024]{2,1,0:T(8,128)S(1)}, bf16[3,128,1024]{2,1,0:T(8,128)(2,1)S(1)}) custom-call(s32[3,1,2048]{2,1,0:T(1,128)S(1)} %get-tuple-element.98.ids_all.ids_own, bf16[3,192,2048]{2,1,0:T(8,128)(2,1)S(1)} %get-tuple-element.112.feat, bf16[3,2048,128]{2,1,0:T(8,128)(2,1)S(1)} %get-tuple-element.113.kv, ...), custom_call_target="tpu_custom_call" | custom-call | flops 22548578304 | bytes 10000000 | tf_op jit(solution)/shard_map/back/pallas_call | solution.py:1187
  141.7 9.0 %collective-permute-done.21.got_u = bf16[2,4,112,768]{3,2,1,0:T(8,128)(2,1)S(1)} collective-permute-done((bf16[2,4,112,768]{3,2,1,0:T(8,128)(2,1)S(1)}, bf16[2,4,112,768]{3,2,1,0:T(8,128)(2,1)S(1)}, u32[]{:S(2)}, u32[]{:S(2)}) %collective-permute-start.21) | collective-permute-done | bytes 1376288 | tf_op jit(solution)/shard_map/ppermute | solution.py:781
  151.9 2.4 inward.1
  155.1 9.4 %collective-permute-done.24.refs_1_ = bf16[3,192,256]{2,1,0:T(8,128)(2,1)S(1)} collective-permute-done((bf16[3,192,256]{2,1,0:T(8,128)(2,1)S(1)}, bf16[3,192,256]{2,1,0:T(8,128)(2,1)S(1)}, u32[]{:S(2)}, u32[]{:S(2)}) %collective-permute-start.24) | collective-permute-done | bytes 294944 | tf_op jit(solution)/shard_map/ppermute | solution.py:774
  165.2 1.5 collective-permute-start.28
  167.2 1.8 collective-permute-start.25
  169.0 1.5 collective-permute-start.30
  170.5 16.4 %collective-permute-done.25.refs_2_ = bf16[3,192,256]{2,1,0:T(8,128)(2,1)S(1)} collective-permute-done((bf16[3,192,256]{2,1,0:T(8,128)(2,1)S(1)}, bf16[3,192,256]{2,1,0:T(8,128)(2,1)S(1)}, u32[]{:S(2)}, u32[]{:S(2)}) %collective-permute-start.25) | collective-permute-done | bytes 294944 | tf_op jit(solution)/shard_map/ppermute | solution.py:774
  186.8 2.0 collective-permute-done.26.refs_3_
  189.3 2.6 collective-permute-done.30.by_xy
  191.9 1.3 third.1
  194.4 3.4 %collective-permute-start.32 = (bf16[256,768]{1,0:T(8,128)(2,1)}, bf16[256,768]{1,0:T(8,128)(2,1)}, u32[]{:S(2)}, u32[]{:S(2)}) collective-permute-start(bf16[256,768]{1,0:T(8,128)(2,1)} %get-tuple-element.158), channel_id=1, source_target_pairs={{0,4},{1,5},{2,6},{3,7},{4,0},{5,1},{6,2},{7,3},{8,12},{9,13},{10,... | collective-permute-start | bytes 1179656 | tf_op jit(solution)/shard_map/ppermute | solution.py:774
  198.5 22.6 %collective-permute-done.31.refs_1_ = bf16[256,768]{1,0:T(8,128)(2,1)} collective-permute-done((bf16[256,768]{1,0:T(8,128)(2,1)}, bf16[256,768]{1,0:T(8,128)(2,1)}, u32[]{:S(2)}, u32[]{:S(2)}) %collective-permute-start.31) | collective-permute-done | bytes 393248 | tf_op jit(solution)/shard_map/ppermute | solution.py:774
  221.1 6.1 %collective-permute-done.32.refs_2_ = bf16[256,768]{1,0:T(8,128)(2,1)} collective-permute-done((bf16[256,768]{1,0:T(8,128)(2,1)}, bf16[256,768]{1,0:T(8,128)(2,1)}, u32[]{:S(2)}, u32[]{:S(2)}) %collective-permute-start.32) | collective-permute-done | bytes 393248 | tf_op jit(solution)/shard_map/ppermute | solution.py:774
  227.3 3.0 %collective-permute-done.33.refs_3_ = bf16[256,768]{1,0:T(8,128)(2,1)} collective-permute-done((bf16[256,768]{1,0:T(8,128)(2,1)}, bf16[256,768]{1,0:T(8,128)(2,1)}, u32[]{:S(2)}, u32[]{:S(2)}) %collective-permute-start.33) | collective-permute-done | bytes 393248 | tf_op jit(solution)/shard_map/ppermute | solution.py:774
  231.3 2.9 %fourth.1.own = bf16[320,768]{1,0:T(8,128)(2,1)} custom-call(s32[6]{0:T(128)S(1)} %stack.38.info, bf16[256,768]{1,0:T(8,128)(2,1)S(1)} %copy-done.5, bf16[256,768]{1,0:T(8,128)(2,1)} %collective-permute-done.31.refs_1_, bf16[256,768]{1,0:T(8,128)(2,1)} %collective-permute-done.32.refs_2_, bf16[256,768]{1,0:T(8,128)(2,1)} %collective-permute-done.33.refs_3_), custom_call_target="tpu_custom_call" | custom-call | flops 983040 | bytes 1966080 | tf_op jit(solution)/shard_map/fourth/pallas_call | solution.py:1079
  234.8 1.5 collective-permute-start.35
  236.2 1.5 collective-permute-start.36
  245.1 3.9 %final.1 = bf16[256,768]{1,0:T(8,128)(2,1)} custom-call(s32[6]{0:T(128)S(1)} %stack.38.info, bf16[3,192,256]{2,1,0:T(8,128)(2,1)S(1)} %copy-done.7, bf16[3,192,256]{2,1,0:T(8,128)(2,1)S(1)} %copy-done.9, bf16[3,192,256]{2,1,0:T(8,128)(2,1)S(1)} %copy-done.11, bf16[3,192,256]{2,1,0:T(8,128)(2,1)S(1)} %copy-done.13, bf16[256,768]{1,0:T(8,128)(2,1)} %refs_4_.3, ...), custom_call_target="tpu_custom_call" | custom-call | flops 905969664 | bytes 3538944 | tf_op jit(solution)/shard_map/final/pallas_call | solution.py:1299
  249.0 9.2 %collective-permute-done.36.from_xy = bf16[320,768]{1,0:T(8,128)(2,1)} collective-permute-done((bf16[320,768]{1,0:T(8,128)(2,1)}, bf16[320,768]{1,0:T(8,128)(2,1)}, u32[]{:S(2)}, u32[]{:S(2)}) %collective-permute-start.36) | collective-permute-done | bytes 491552 | tf_op jit(solution)/shard_map/ppermute | solution.py:781
  258.2 4.8 %spread.1 = (f32[96,3072]{1,0:T(8,128)}, f32[96,768]{1,0:T(8,128)}, f32[384,768]{1,0:T(8,128)}, f32[8,768]{1,0:T(8,128)S(1)}, f32[96,768]{1,0:T(8,128)}, /*index=5*/f32[96,1536]{1,0:T(8,128)}, f32[96,128]{1,0:T(8,128)S(1)}) custom-call(s32[6]{0:T(128)S(1)} %stack.38.info, bf16[320,768]{1,0:T(8,128)(2,1)} %fourth.1.own, ...), custom_call_target="tpu_custom_call" | custom-call | flops 1000000 | bytes 5898240 | tf_op jit(solution)/shard_map/spread/pallas_call | solution.py:1097
  (149 shorter events, 29.1 us)
Async XLA Ops:
  0.6 4.8 %collective-permute-start = (bf16[256,768]{1,0:T(8,128)(2,1)}, bf16[256,768]{1,0:T(8,128)(2,1)S(1)}, u32[]{:S(2)}, u32[]{:S(2)}) collective-permute-start(bf16[256,768]{1,0:T(8,128)(2,1)} %refs_4_.3), channel_id=1, source_target_pairs={{0,1},{1,0},{2,3},{3,2},{4,5},{5,4},{6,7},{7,6},{8,9},{9,8},{10,11... | collective-permute-start | bytes 1179656 | tf_op jit(solution)/shard_map/ppermute | solution.py:778
  5.4 11.1 %copy-start.2 = (bf16[256,768]{1,0:T(8,128)(2,1)}, bf16[256,768]{1,0:T(8,128)(2,1)S(1)}, u32[]{:S(2)}) copy-start(bf16[256,768]{1,0:T(8,128)(2,1)S(1)} %collective-permute-done.refs_1_) | copy-start | bytes 1179652
  6.1 12.8 %collective-permute-start.1 = (s32[3,34,128]{2,1,0:T(8,128)S(1)}, s32[3,34,128]{2,1,0:T(8,128)S(1)}, u32[]{:S(2)}, u32[]{:S(2)}) collective-permute-start(s32[3,34,128]{2,1,0:T(8,128)S(1)} %get-tuple-element.179), channel_id=1, source_target_pairs={{0,6},{1,7},{2,0},{3,1},{4,2},{5,3},{6,4},{7,5},{8,14},{9,15},{10,... | collective-permute-start | bytes 156680 | tf_op jit(solution)/shard_map/ppermute | solution.py:774
  6.1 12.8 %collective-permute-start.2 = (s32[3,34,128]{2,1,0:T(8,128)S(1)}, s32[3,34,128]{2,1,0:T(8,128)S(1)}, u32[]{:S(2)}, u32[]{:S(2)}) collective-permute-start(s32[3,34,128]{2,1,0:T(8,128)S(1)} %get-tuple-element.178), channel_id=1, source_target_pairs={{0,4},{1,5},{2,6},{3,7},{4,0},{5,1},{6,2},{7,3},{8,12},{9,13},{10,... | collective-permute-start | bytes 156680 | tf_op jit(solution)/shard_map/ppermute | solution.py:774
  9.2 9.8 %collective-permute-start.3 = (s32[3,34,128]{2,1,0:T(8,128)S(1)}, s32[3,34,128]{2,1,0:T(8,128)S(1)}, u32[]{:S(2)}, u32[]{:S(2)}) collective-permute-start(s32[3,34,128]{2,1,0:T(8,128)S(1)} %get-tuple-element.177), channel_id=1, source_target_pairs={{0,2},{1,3},{2,4},{3,5},{4,6},{5,7},{6,0},{7,1},{8,10},{9,11},{10,... | collective-permute-start | bytes 156680 | tf_op jit(solution)/shard_map/ppermute | solution.py:774
  11.7 29.1 %collective-permute-start.7 = (bf16[256,768]{1,0:T(8,128)(2,1)}, bf16[256,768]{1,0:T(8,128)(2,1)}, u32[]{:S(2)}, u32[]{:S(2)}) collective-permute-start(bf16[256,768]{1,0:T(8,128)(2,1)} %refs_4_.3), channel_id=1, source_target_pairs={{0,2},{1,3},{2,4},{3,5},{4,6},{5,7},{6,0},{7,1},{8,10},{9,11},{10,... | collective-permute-start | bytes 1179656 | tf_op jit(solution)/shard_map/ppermute | solution.py:774
  11.7 29.6 %collective-permute-start.9 = (bf16[256,768]{1,0:T(8,128)(2,1)}, bf16[256,768]{1,0:T(8,128)(2,1)}, u32[]{:S(2)}, u32[]{:S(2)}) collective-permute-start(bf16[256,768]{1,0:T(8,128)(2,1)} %refs_4_.3), channel_id=1, source_target_pairs={{0,6},{1,7},{2,0},{3,1},{4,2},{5,3},{6,4},{7,5},{8,14},{9,15},{10,... | collective-permute-start | bytes 1179656 | tf_op jit(solution)/shard_map/ppermute | solution.py:774
  19.0 22.3 %collective-permute-start.10 = (bf16[256,768]{1,0:T(8,128)(2,1)}, bf16[256,768]{1,0:T(8,128)(2,1)}, u32[]{:S(2)}, u32[]{:S(2)}) collective-permute-start(bf16[256,768]{1,0:T(8,128)(2,1)} %refs_8_.3), channel_id=1, source_target_pairs={{0,1},{1,0},{2,3},{3,2},{4,5},{5,4},{6,7},{7,6},{8,9},{9,8},{10,11... | collective-permute-start | bytes 1179656 | tf_op jit(solution)/shard_map/ppermute | solution.py:778
  19.0 29.6 %collective-permute-start.5 = (bf16[256,768]{1,0:T(8,128)(2,1)}, bf16[256,768]{1,0:T(8,128)(2,1)}, u32[]{:S(2)}, u32[]{:S(2)}) collective-permute-start(bf16[256,768]{1,0:T(8,128)(2,1)} %refs_4_.3), channel_id=1, source_target_pairs={{0,4},{1,5},{2,6},{3,7},{4,0},{5,1},{6,2},{7,3},{8,12},{9,13},{10,... | collective-permute-start | bytes 1179656 | tf_op jit(solution)/shard_map/ppermute | solution.py:774
  23.1 4.0 %collective-permute-start.4 = (s32[3,40,128]{2,1,0:T(8,128)}, s32[3,40,128]{2,1,0:T(8,128)}, u32[]{:S(2)}, u32[]{:S(2)}) collective-permute-start(s32[3,40,128]{2,1,0:T(8,128)} %table.1.refs_0_), channel_id=1, source_target_pairs={{0,1},{1,0},{2,3},{3,2},{4,5},{5,4},{6,7},{7,6},{8,9},{9,8},{10,11... | collective-permute-start | bytes 184328 | tf_op jit(solution)/shard_map/ppermute | solution.py:778
  35.6 23.4 %copy-start.26 = (bf16[3,2048,128]{2,1,0:T(8,128)(2,1)}, bf16[3,2048,128]{2,1,0:T(8,128)(2,1)S(1)}, u32[]{:S(2)}) copy-start(bf16[3,2048,128]{2,1,0:T(8,128)(2,1)S(1)} %get-tuple-element.100.bias) | copy-start | bytes 4718596
  48.7 1.9 collective-permute-start.11
  48.7 4.6 %collective-permute-start.8 = (bf16[256,768]{1,0:T(8,128)(2,1)}, bf16[256,768]{1,0:T(8,128)(2,1)S(1)}, u32[]{:S(2)}, u32[]{:S(2)}) collective-permute-start(bf16[256,768]{1,0:T(8,128)(2,1)} %collective-permute-done.7.refs_0_), channel_id=1, source_target_pairs={{0,1},{1,0},{2,3},{3,2},{4,5},{5,4},{6,7},{7,6},{8,9},{9,8},{10,11... | collective-permute-start | bytes 1179656 | tf_op jit(solution)/shard_map/ppermute | solution.py:778
  49.2 6.9 %collective-permute-start.6 = (bf16[256,768]{1,0:T(8,128)(2,1)}, bf16[256,768]{1,0:T(8,128)(2,1)S(1)}, u32[]{:S(2)}, u32[]{:S(2)}) collective-permute-start(bf16[256,768]{1,0:T(8,128)(2,1)} %collective-permute-done.5.refs_0_), channel_id=1, source_target_pairs={{0,1},{1,0},{2,3},{3,2},{4,5},{5,4},{6,7},{7,6},{8,9},{9,8},{10,11... | collective-permute-start | bytes 1179656 | tf_op jit(solution)/shard_map/ppermute | solution.py:778
  56.0 30.6 %slice-start = ((s8[4718592]{0:T(1024)(128)(4,1)}), s8[4194304]{0:T(1024)(128)(4,1)S(1)}, s32[]{:S(2)}) async-start(s8[4718592]{0:T(1024)(128)(4,1)} %bitcast.37), calls=%async_computation | async-start | bytes 8388608
  59.0 19.9 %copy-start.35 = (f32[768]{0:T(1024)S(1)}, f32[768]{0:T(1024)}, u32[]{:S(2)}) copy-start(f32[768]{0:T(1024)} %param.23) | copy-start | bytes 9220
  59.1 19.9 %copy-start.36 = (f32[768]{0:T(1024)S(1)}, f32[768]{0:T(1024)}, u32[]{:S(2)}) copy-start(f32[768]{0:T(1024)} %param.24) | copy-start | bytes 9220
  59.1 27.6 %slice-start.1 = ((s8[4718592]{0:T(1024)(128)(4,1)}), s8[524288]{0:T(1024)(128)(4,1)S(1)}, s32[]{:S(2)}) async-start(s8[4718592]{0:T(1024)(128)(4,1)} %bitcast.37), calls=%async_computation.1 | async-start | bytes 1048576
  59.1 27.5 %copy-start.25 = (bf16[768,768]{1,0:T(8,128)(2,1)S(1)}, bf16[768,768]{1,0:T(8,128)(2,1)}, u32[]{:S(2)}) copy-start(bf16[768,768]{1,0:T(8,128)(2,1)} %param.22) | copy-start | bytes 3538948
  73.5 5.4 %collective-permute-start.12 = (bf16[192,256]{1,0:T(8,128)(2,1)S(1)}, bf16[192,256]{1,0:T(8,128)(2,1)S(1)}, u32[]{:S(2)}, u32[]{:S(2)}) collective-permute-start(bf16[192,256]{1,0:T(8,128)(2,1)S(1)} %get-tuple-element.115), channel_id=1, source_target_pairs={{0,2},{1,3},{2,4},{3,5},{4,6},{5,7},{6,0},{7,1},{8,10},{9,11},{10,... | collective-permute-start | bytes 294920 | tf_op jit(solution)/shard_map/ppermute | solution.py:774
  73.8 10.6 %collective-permute-start.13 = (bf16[192,256]{1,0:T(8,128)(2,1)S(1)}, bf16[192,256]{1,0:T(8,128)(2,1)S(1)}, u32[]{:S(2)}, u32[]{:S(2)}) collective-permute-start(bf16[192,256]{1,0:T(8,128)(2,1)S(1)} %get-tuple-element.116), channel_id=1, source_target_pairs={{0,4},{1,5},{2,6},{3,7},{4,0},{5,1},{6,2},{7,3},{8,12},{9,13},{10,... | collective-permute-start | bytes 294920 | tf_op jit(solution)/shard_map/ppermute | solution.py:774
  78.1 8.5 %collective-permute-start.14 = (bf16[192,256]{1,0:T(8,128)(2,1)S(1)}, bf16[192,256]{1,0:T(8,128)(2,1)S(1)}, u32[]{:S(2)}, u32[]{:S(2)}) collective-permute-start(bf16[192,256]{1,0:T(8,128)(2,1)S(1)} %get-tuple-element.117), channel_id=1, source_target_pairs={{0,6},{1,7},{2,0},{3,1},{4,2},{5,3},{6,4},{7,5},{8,14},{9,15},{10,... | collective-permute-start | bytes 294920 | tf_op jit(solution)/shard_map/ppermute | solution.py:774
  101.0 6.1 %collective-permute-start.18 = (bf16[256,5376]{1,0:T(8,128)(2,1)S(1)}, bf16[256,5376]{1,0:T(8,128)(2,1)S(1)}, u32[]{:S(2)}, u32[]{:S(2)}) collective-permute-start(bf16[256,5376]{1,0:T(8,128)(2,1)S(1)} %get-tuple-element.123.refs_0_.refs_2_), channel_id=1, source_target_pairs={{0,1},{1,0},{2,3},{3,2},{4,5},{5,4},{6,7},{7,6},{8,9},{9,8},{10,11... | collective-permute-start | bytes 8257544 | tf_op jit(solution)/shard_map/ppermute | solution.py:778
  102.5 4.6 %collective-permute-start.19 = (bf16[784,256]{1,0:T(8,128)(2,1)S(1)}, bf16[784,256]{1,0:T(8,128)(2,1)S(1)}, u32[]{:S(2)}, u32[]{:S(2)}) collective-permute-start(bf16[784,256]{1,0:T(8,128)(2,1)S(1)} %get-tuple-element.126), channel_id=1, source_target_pairs={{0,1},{1,0},{2,3},{3,2},{4,5},{5,4},{6,7},{7,6},{8,9},{9,8},{10,11... | collective-permute-start | bytes 1204232 | tf_op jit(solution)/shard_map/ppermute | solution.py:778
  103.0 14.1 %collective-permute-start.15 = (bf16[192,256]{1,0:T(8,128)(2,1)S(1)}, bf16[192,256]{1,0:T(8,128)(2,1)S(1)}, u32[]{:S(2)}, u32[]{:S(2)}) collective-permute-start(bf16[192,256]{1,0:T(8,128)(2,1)S(1)} %get-tuple-element.120), channel_id=1, source_target_pairs={{0,6},{1,7},{2,0},{3,1},{4,2},{5,3},{6,4},{7,5},{8,14},{9,15},{10,... | collective-permute-start | bytes 294920 | tf_op jit(solution)/shard_map/ppermute | solution.py:774
  103.1 14.1 %collective-permute-start.16 = (bf16[192,256]{1,0:T(8,128)(2,1)S(1)}, bf16[192,256]{1,0:T(8,128)(2,1)S(1)}, u32[]{:S(2)}, u32[]{:S(2)}) collective-permute-start(bf16[192,256]{1,0:T(8,128)(2,1)S(1)} %get-tuple-element.121), channel_id=1, source_target_pairs={{0,4},{1,5},{2,6},{3,7},{4,0},{5,1},{6,2},{7,3},{8,12},{9,13},{10,... | collective-permute-start | bytes 294920 | tf_op jit(solution)/shard_map/ppermute | solution.py:774
  104.2 13.0 %collective-permute-start.17 = (bf16[192,256]{1,0:T(8,128)(2,1)S(1)}, bf16[192,256]{1,0:T(8,128)(2,1)S(1)}, u32[]{:S(2)}, u32[]{:S(2)}) collective-permute-start(bf16[192,256]{1,0:T(8,128)(2,1)S(1)} %get-tuple-element.122), channel_id=1, source_target_pairs={{0,2},{1,3},{2,4},{3,5},{4,6},{5,7},{6,0},{7,1},{8,10},{9,11},{10,... | collective-permute-start | bytes 294920 | tf_op jit(solution)/shard_map/ppermute | solution.py:774
  108.9 12.3 %copy-start.27 = (bf16[3,2048,128]{2,1,0:T(8,128)(2,1)S(1)}, bf16[3,2048,128]{2,1,0:T(8,128)(2,1)}, u32[]{:S(2)}) copy-start(bf16[3,2048,128]{2,1,0:T(8,128)(2,1)} %copy-done.26) | copy-start | bytes 4718596
  108.9 12.3 %copy-start.29 = (f32[3,72,128]{2,1,0:T(8,128)S(1)}, f32[3,72,128]{2,1,0:T(8,128)}, u32[]{:S(2)}) copy-start(f32[3,72,128]{2,1,0:T(8,128)} %copy-done.28) | copy-start | bytes 331780
  108.9 12.3 %copy-start.31 = (bf16[3,64,128]{2,1,0:T(8,128)(2,1)S(1)}, bf16[3,64,128]{2,1,0:T(8,128)(2,1)}, u32[]{:S(2)}) copy-start(bf16[3,64,128]{2,1,0:T(8,128)(2,1)} %copy-done.30) | copy-start | bytes 147460
  118.0 3.2 %collective-permute-start.20 = (f32[3,80,128]{2,1,0:T(8,128)S(1)}, f32[3,80,128]{2,1,0:T(8,128)S(1)}, u32[]{:S(2)}, u32[]{:S(2)}) collective-permute-start(f32[3,80,128]{2,1,0:T(8,128)S(1)} %sums.1.refs_7_), channel_id=1, source_target_pairs={{0,1},{1,0},{2,3},{3,2},{4,5},{5,4},{6,7},{7,6},{8,9},{9,8},{10,11... | collective-permute-start | bytes 368648 | tf_op jit(solution)/shard_map/ppermute | solution.py:778
  118.1 32.6 %collective-permute-start.21 = (bf16[2,4,112,768]{3,2,1,0:T(8,128)(2,1)S(1)}, bf16[2,4,112,768]{3,2,1,0:T(8,128)(2,1)S(1)}, u32[]{:S(2)}, u32[]{:S(2)}) collective-permute-start(bf16[2,4,112,768]{3,2,1,0:T(8,128)(2,1)S(1)} %get-tuple-element.137), channel_id=1, source_target_pairs={{0,8},{8,0},{16,24},{24,16},{1,9},{9,1},{17,25},{25,17},{2,10},{10... | collective-permute-start | bytes 4128776 | tf_op jit(solution)/shard_map/ppermute | solution.py:781
  119.7 32.3 %collective-permute-start.22 = (bf16[2,4,112,768]{3,2,1,0:T(8,128)(2,1)S(1)}, bf16[2,4,112,768]{3,2,1,0:T(8,128)(2,1)S(1)}, u32[]{:S(2)}, u32[]{:S(2)}) collective-permute-start(bf16[2,4,112,768]{3,2,1,0:T(8,128)(2,1)S(1)} %get-tuple-element.138), channel_id=1, source_target_pairs={{0,16},{8,24},{16,0},{24,8},{1,17},{9,25},{17,1},{25,9},{2,18},{10... | collective-permute-start | bytes 4128776 | tf_op jit(solution)/shard_map/ppermute | solution.py:781
  141.6 10.3 %collective-permute-start.23 = (bf16[3,128,1024]{2,1,0:T(8,128)(2,1)S(1)}, bf16[3,128,1024]{2,1,0:T(8,128)(2,1)S(1)}, u32[]{:S(2)}, u32[]{:S(2)}) collective-permute-start(bf16[3,128,1024]{2,1,0:T(8,128)(2,1)S(1)} %get-tuple-element.140), channel_id=1, source_target_pairs={{0,1},{1,0},{2,3},{3,2},{4,5},{5,4},{6,7},{7,6},{8,9},{9,8},{10,11... | collective-permute-start | bytes 2359304 | tf_op jit(solution)/shard_map/ppermute | solution.py:778
  155.0 9.4 %collective-permute-start.27 = (bf16[4,4,32,768]{3,2,1,0:T(8,128)(2,1)S(1)}, bf16[4,4,32,768]{3,2,1,0:T(8,128)(2,1)S(1)}, u32[]{:S(2)}, u32[]{:S(2)}) collective-permute-start(bf16[4,4,32,768]{3,2,1,0:T(8,128)(2,1)S(1)} %get-tuple-element.150), channel_id=1, source_target_pairs={{0,1},{1,0},{2,3},{3,2},{4,5},{5,4},{6,7},{7,6},{8,9},{9,8},{10,11... | collective-permute-start | bytes 2359304 | tf_op jit(solution)/shard_map/ppermute | solution.py:778
  155.0 9.4 %collective-permute-start.24 = (bf16[3,192,256]{2,1,0:T(8,128)(2,1)S(1)}, bf16[3,192,256]{2,1,0:T(8,128)(2,1)S(1)}, u32[]{:S(2)}, u32[]{:S(2)}) collective-permute-start(bf16[3,192,256]{2,1,0:T(8,128)(2,1)S(1)} %get-tuple-element.143), channel_id=1, source_target_pairs={{0,2},{1,3},{2,4},{3,5},{4,6},{5,7},{6,0},{7,1},{8,10},{9,11},{10,... | collective-permute-start | bytes 884744 | tf_op jit(solution)/shard_map/ppermute | solution.py:774
  165.2 23.7 %collective-permute-start.28 = (bf16[4,144,768]{2,1,0:T(8,128)(2,1)S(1)}, bf16[4,144,768]{2,1,0:T(8,128)(2,1)S(1)}, u32[]{:S(2)}, u32[]{:S(2)}) collective-permute-start(bf16[4,144,768]{2,1,0:T(8,128)(2,1)S(1)} %get-tuple-element.151), channel_id=1, source_target_pairs={{0,16},{8,24},{16,0},{24,8},{1,17},{9,25},{17,1},{25,9},{2,18},{10... | collective-permute-start | bytes 2654216 | tf_op jit(solution)/shard_map/ppermute | solution.py:781
  166.7 22.6 %collective-permute-start.29 = (bf16[4,144,768]{2,1,0:T(8,128)(2,1)S(1)}, bf16[4,144,768]{2,1,0:T(8,128)(2,1)S(1)}, u32[]{:S(2)}, u32[]{:S(2)}) collective-permute-start(bf16[4,144,768]{2,1,0:T(8,128)(2,1)S(1)} %get-tuple-element.152), channel_id=1, source_target_pairs={{0,8},{8,0},{16,24},{24,16},{1,9},{9,1},{17,25},{25,17},{2,10},{10... | collective-permute-start | bytes 2654216 | tf_op jit(solution)/shard_map/ppermute | solution.py:781
  167.2 19.6 %collective-permute-start.25 = (bf16[3,192,256]{2,1,0:T(8,128)(2,1)S(1)}, bf16[3,192,256]{2,1,0:T(8,128)(2,1)S(1)}, u32[]{:S(2)}, u32[]{:S(2)}) collective-permute-start(bf16[3,192,256]{2,1,0:T(8,128)(2,1)S(1)} %get-tuple-element.144), channel_id=1, source_target_pairs={{0,4},{1,5},{2,6},{3,7},{4,0},{5,1},{6,2},{7,3},{8,12},{9,13},{10,... | collective-permute-start | bytes 884744 | tf_op jit(solution)/shard_map/ppermute | solution.py:774
  169.0 19.9 %collective-permute-start.26 = (bf16[3,192,256]{2,1,0:T(8,128)(2,1)S(1)}, bf16[3,192,256]{2,1,0:T(8,128)(2,1)S(1)}, u32[]{:S(2)}, u32[]{:S(2)}) collective-permute-start(bf16[3,192,256]{2,1,0:T(8,128)(2,1)S(1)} %get-tuple-element.145), channel_id=1, source_target_pairs={{0,6},{1,7},{2,0},{3,1},{4,2},{5,3},{6,4},{7,5},{8,14},{9,15},{10,... | collective-permute-start | bytes 884744 | tf_op jit(solution)/shard_map/ppermute | solution.py:774
  169.0 22.9 %collective-permute-start.30 = (bf16[4,32,768]{2,1,0:T(8,128)(2,1)S(1)}, bf16[4,32,768]{2,1,0:T(8,128)(2,1)S(1)}, u32[]{:S(2)}, u32[]{:S(2)}) collective-permute-start(bf16[4,32,768]{2,1,0:T(8,128)(2,1)S(1)} %get-tuple-element.155), channel_id=1, source_target_pairs={{0,24},{8,16},{16,8},{24,0},{1,25},{9,17},{17,9},{25,1},{2,26},{10... | collective-permute-start | bytes 589832 | tf_op jit(solution)/shard_map/ppermute | solution.py:781
  193.9 27.2 %collective-permute-start.31 = (bf16[256,768]{1,0:T(8,128)(2,1)}, bf16[256,768]{1,0:T(8,128)(2,1)}, u32[]{:S(2)}, u32[]{:S(2)}) collective-permute-start(bf16[256,768]{1,0:T(8,128)(2,1)} %get-tuple-element.157), channel_id=1, source_target_pairs={{0,2},{1,3},{2,4},{3,5},{4,6},{5,7},{6,0},{7,1},{8,10},{9,11},{10,... | collective-permute-start | bytes 1179656 | tf_op jit(solution)/shard_map/ppermute | solution.py:774
  194.4 32.9 %collective-permute-start.32 = (bf16[256,768]{1,0:T(8,128)(2,1)}, bf16[256,768]{1,0:T(8,128)(2,1)}, u32[]{:S(2)}, u32[]{:S(2)}) collective-permute-start(bf16[256,768]{1,0:T(8,128)(2,1)} %get-tuple-element.158), channel_id=1, source_target_pairs={{0,4},{1,5},{2,6},{3,7},{4,0},{5,1},{6,2},{7,3},{8,12},{9,13},{10,... | collective-permute-start | bytes 1179656 | tf_op jit(solution)/shard_map/ppermute | solution.py:774
  197.8 32.4 %collective-permute-start.33 = (bf16[256,768]{1,0:T(8,128)(2,1)}, bf16[256,768]{1,0:T(8,128)(2,1)}, u32[]{:S(2)}, u32[]{:S(2)}) collective-permute-start(bf16[256,768]{1,0:T(8,128)(2,1)} %get-tuple-element.159), channel_id=1, source_target_pairs={{0,6},{1,7},{2,0},{3,1},{4,2},{5,3},{6,4},{7,5},{8,14},{9,15},{10,... | collective-permute-start | bytes 1179656 | tf_op jit(solution)/shard_map/ppermute | solution.py:774
  234.2 14.8 %collective-permute-start.34 = (bf16[320,768]{1,0:T(8,128)(2,1)}, bf16[320,768]{1,0:T(8,128)(2,1)}, u32[]{:S(2)}, u32[]{:S(2)}) collective-permute-start(bf16[320,768]{1,0:T(8,128)(2,1)} %fourth.1.own), channel_id=1, source_target_pairs={{0,8},{8,0},{16,24},{24,16},{1,9},{9,1},{17,25},{25,17},{2,10},{10... | collective-permute-start | bytes 1474568 | tf_op jit(solution)/shard_map/ppermute | solution.py:781
  234.8 14.2 %collective-permute-start.35 = (bf16[320,768]{1,0:T(8,128)(2,1)}, bf16[320,768]{1,0:T(8,128)(2,1)}, u32[]{:S(2)}, u32[]{:S(2)}) collective-permute-start(bf16[320,768]{1,0:T(8,128)(2,1)} %fourth.1.own), channel_id=1, source_target_pairs={{0,16},{8,24},{16,0},{24,8},{1,17},{9,25},{17,1},{25,9},{2,18},{10... | collective-permute-start | bytes 1474568 | tf_op jit(solution)/shard_map/ppermute | solution.py:781
  236.2 21.9 %collective-permute-start.36 = (bf16[320,768]{1,0:T(8,128)(2,1)}, bf16[320,768]{1,0:T(8,128)(2,1)}, u32[]{:S(2)}, u32[]{:S(2)}) collective-permute-start(bf16[320,768]{1,0:T(8,128)(2,1)} %fourth.1.own), channel_id=1, source_target_pairs={{0,24},{8,16},{16,8},{24,0},{1,25},{9,17},{17,9},{25,1},{2,26},{10... | collective-permute-start | bytes 1474568 | tf_op jit(solution)/shard_map/ppermute | solution.py:781
  245.1 13.1 %copy-start.15 = (f32[96,8]{1,0:T(8,128)S(1)}, f32[96,8]{1,0:T(8,128)}, u32[]{:S(2)}) copy-start(f32[96,8]{1,0:T(8,128)} %copy.53.pair) | copy-start | bytes 9220
  (28 other events, 51.6 us)

commit v8 on v7

--- a/solution.py
+++ b/solution.py
@@ -107,7 +107,7 @@
     return ref[spot, :] if axis == 0 else ref[:, spot]
 
 
-def table_kernel(*refs, picks):
+def table_kernel(info, *refs, picks):
     parts, out = refs[:-1], refs[-1]
     total = parts[0][:, :picks]
     for part in parts[1:]:
@@ -244,7 +244,7 @@
         mix_ref[0, group] = jnp.concatenate([mix, level], axis=0)
 
 
-def sums_kernel(ids_own, *refs, groups):
+def sums_kernel(info, ids_own, *refs, groups):
     grads, (mix_ref, part_ref) = refs[:groups], refs[groups:]
     hs = grads[0].shape[0]
     total = None
@@ -494,8 +494,19 @@
 
 def weights_kernel(info, *refs, groups):
     (dup, dup_got, dbr, dbr_got, act, act_got, low, low_got, cot, cot_got) = refs[:10]
-    send_u, keep_u, send_d, keep_d, outs = refs[10:]
+    send_u, keep_u, send_d, keep_d, outs = refs[10:13], refs[13], refs[14:17], refs[17], refs[18]
     width = cot.shape[1]
+    lead = send_u[0].shape[2]
+
+    def leave(send, turn, spot, block, first):
+        if turn:
+            send[2][0, spot, first : first + block.shape[0]] = block
+        elif first:
+            send[1][0, spot, first - lead : first - lead + block.shape[0]] = block
+        else:
+            send[0][0, spot] = block[:lead]
+            send[1][0, spot, : block.shape[0] - lead] = block[lead:]
+
     index = pl.program_id(0)
     group_at, place_u, place_d = info[0], info[3], info[4]
     rows = width // (2 * groups)
@@ -521,9 +532,11 @@
                 tail = jnp.concatenate([tail, norms], axis=0).astype(BF)
                 place = lax.bitwise_xor(part, place_d)
 
-                @pl.when(place >= 2)
-                def leaves_more():
-                    send_d[place - 2, (groups - group) % groups, rows:] = tail
+                for turn in range(2):
+
+                    @pl.when(place == 2 + turn)
+                    def leaves_more(turn=turn, tail=tail, group=group):
+                        leave(send_d, turn, (groups - group) % groups, tail, rows)
 
                 @pl.when(place < 2)
                 def stays_more():
@@ -538,10 +551,12 @@
         start = pl.multiple_of(at * quarter, 8)
         other = outs[group, pl.ds(start, 16), :].astype(BF)
 
-        @pl.when(index < 2)
-        def leaves():
-            send_u[0, spot, :rows] = block
-            send_u[0, away, rows:] = other
+        for turn in range(2):
+
+            @pl.when(index == turn)
+            def leaves(turn=turn, spot=spot, block=block, away=away, other=other):
+                leave(send_u, turn, spot, block, 0)
+                leave(send_u, turn, away, other, rows)
 
         @pl.when(index >= 2)
         def stays():
@@ -554,42 +569,59 @@
         block = down[part * rows : (part + 1) * rows].astype(BF)
         place = lax.bitwise_xor(part, place_d)
 
-        @pl.when(place >= 2)
-        def leaves_down():
-            send_d[place - 2, spot, :rows] = block
+        for turn in range(2):
+
+            @pl.when(place == 2 + turn)
+            def leaves_down(turn=turn, block=block):
+                leave(send_d, turn, spot, block, 0)
 
         @pl.when(place < 2)
         def stays_down():
             keep_d[place, spot, :rows] = block
 
 
-def second_kernel(keep_u, got_u, keep_d, got_d, inner, inner_got, to_y, to_x, to_xy):
-    rows = keep_u.shape[2]
+def second_kernel(keep_u, got_u, keep_d, got_d, inner, inner_got, late_u, late_d, to_y, to_x, to_xy):
+    rows, lines = keep_u.shape[2], inner.shape[2]
     to_y[:, :rows] = (keep_u[0].astype(F32) + got_u[0].astype(F32)).astype(BF)
     to_x[:, :rows] = (keep_d[0].astype(F32) + got_d[0].astype(F32)).astype(BF)
-    to_y[:, rows:] = (inner[1].astype(F32) + inner_got[1].astype(F32)).astype(BF)
-    to_x[:, rows:] = (inner[2].astype(F32) + inner_got[2].astype(F32)).astype(BF)
+    to_y[:, rows : rows + lines] = (inner[1].astype(F32) + inner_got[1].astype(F32)).astype(BF)
+    to_x[:, rows : rows + lines] = (inner[2].astype(F32) + inner_got[2].astype(F32)).astype(BF)
     to_xy[...] = (inner[3].astype(F32) + inner_got[3].astype(F32)).astype(BF)
-
-
-def third_kernel(keep_u, got_u, keep_d, got_d, inner, inner_got, by_y, by_x, by_xy, *outs):
-    rows = keep_u.shape[2]
-    for group in range(len(outs)):
-        up = keep_u[0, group].astype(F32) + got_u[0, group].astype(F32)
-        down = keep_d[0, group].astype(F32) + got_d[0, group].astype(F32)
+    to_y[:, rows + lines :] = late_d[0]
+    to_x[:, rows + lines :] = late_u[0]
+
+
+def third_kernel(info, keep_u, one_u, keep_d, one_d, by_y, by_x, inner, inner_got, by_xy, *outs):
+    rows, lead, lines = keep_u.shape[2], one_u.shape[2], inner.shape[2]
+    groups = len(outs) // 2
+    left = rows - lead
+    head, tail, late = slice(0, lead), slice(lead, rows), slice(rows + lines, None)
+    mid = slice(rows, rows + lines)
+
+    def added(keep, got, by, group, spot):
+        total = keep[0, group, spot].astype(F32) + got.astype(F32)
+        return (total + by[group, spot].astype(F32)).astype(BF)
+
+    for group in range(groups):
+        first, last = outs[group], outs[groups + group]
+        first[:lead] = added(keep_u, one_u[0, group], by_y, group, head)
+        first[lead:] = added(keep_d, one_d[0, group], by_x, group, head)
+        last[:left] = added(keep_u, by_x[group, late], by_y, group, tail)
+        last[left : 2 * left] = added(keep_d, by_y[group, late], by_x, group, tail)
         both = inner[0, group].astype(F32) + inner_got[0, group].astype(F32)
-        outs[group][:rows] = (up + by_y[group, :rows].astype(F32)).astype(BF)
-        outs[group][rows : 2 * rows] = (down + by_x[group, :rows].astype(F32)).astype(BF)
-        both = both + by_y[group, rows:].astype(F32) + by_x[group, rows:].astype(F32)
-        outs[group][2 * rows :] = (both + by_xy[group].astype(F32)).astype(BF)
+        both = both + by_y[group, mid].astype(F32) + by_x[group, mid].astype(F32)
+        last[2 * left :] = (both + by_xy[group].astype(F32)).astype(BF)
 
 
 def fourth_kernel(info, *refs, groups, high, feats):
-    parts, out, turned = refs[:groups], refs[groups], refs[groups + 1]
+    parts, out = refs[:groups], refs[groups]
     total = parts[0][: 2 * high].astype(F32)
     for part in parts[1:]:
         total = total + part[: 2 * high].astype(F32)
     out[: 2 * high] = total.astype(BF)
+    if parts[0].shape[0] == 2 * high:
+        return
+    turned = refs[groups + 1]
     third = feats // 3
     lines = turned.shape[1]
     for group in range(groups):
@@ -603,34 +635,35 @@
         out[at : at + lines] = jnp.concatenate(found, axis=1).astype(BF)
 
 
-def spread_kernel(
-    info, own, from_x, from_y, from_xy, wq, wkv, pair,
-    up_ref, out_ref, down_ref, norm_ref, gq_ref, gkv_ref, vec_ref, sums, *, high,
-):
+def spread_kernel(info, *refs, lead, high):
+    firsts, lasts, (wq, wkv, pair) = refs[:4], refs[4:8], refs[8:11]
+    up_ref, out_ref, down_ref, norm_ref, gq_ref, gkv_ref, vec_ref, sums = refs[11:]
     index = pl.program_id(0)
     rows, width = down_ref.shape
     quarter = rows // 4
     lines = quarter + 8
-    order_u = (own, from_y, from_x, from_xy)
-    order_d = (own, from_x, from_y, from_xy)
+    left = rows - lead
+    order_u, order_d = (0, 2, 1, 3), (0, 1, 2, 3)
 
     @pl.when(index == 0)
     def first():
-        for place, part in enumerate(order_u):
+        for place, source in enumerate(order_u):
 
             @pl.when(info[3] == place)
-            def take(part=part):
+            def take(source=source):
                 for kind in range(3):
                     at = 2 * high + kind * lines
-                    sums[kind] = part[at : at + lines].astype(F32)[quarter:]
-
-    for place, part in enumerate(order_u):
+                    sums[kind] = lasts[source][at : at + lines].astype(F32)[quarter:]
+
+    for place, source in enumerate(order_u):
 
         @pl.when(index == place)
-        def upper(part=part):
-            up_ref[...] = part[:rows].astype(F32)
+        def upper(source=source):
+            part = lasts[source]
+            up_ref[:lead] = firsts[source][:lead].astype(F32)
+            up_ref[lead:] = part[:left].astype(F32)
             at = pl.multiple_of(lax.bitwise_xor(index, info[3]) * quarter, 8)
-            out_ref[pl.ds(at, 16), :] = part[rows:high].astype(F32)
+            out_ref[pl.ds(at, 16), :] = part[left:high].astype(F32)
             spot = pl.ds(at, quarter)
             shift, gain = pair[spot, 0:1], pair[spot, 1:2]
             gain_sum, shift_sum = 0.0, 0.0
@@ -650,12 +683,14 @@
             lane = lax.broadcasted_iota(jnp.int32, (quarter, vec_ref.shape[1]), 1)
             vec_ref[spot, :] = jnp.where(lane == 0, gain_sum / gain, shift_sum)
 
-    for place, part in enumerate(order_d):
+    for place, source in enumerate(order_d):
 
         @pl.when(index == place)
-        def lower(part=part):
-            down_ref[...] = part[high : high + rows].astype(F32)
-            tail = part[high + rows : 2 * high].astype(F32)
+        def lower(source=source):
+            part = lasts[source]
+            down_ref[:lead] = firsts[source][lead:].astype(F32)
+            down_ref[lead:] = part[high : high + left].astype(F32)
+            tail = part[high + left : 2 * high].astype(F32)
             at = pl.multiple_of(lax.bitwise_xor(index, info[4]) * quarter + 16, 8)
             out_ref[pl.ds(at, quarter - 16), :] = tail[: quarter - 16]
 
@@ -722,6 +757,13 @@
     mean_one = jnp.mean(gy, axis=-1, keepdims=True)
     mean_two = jnp.mean(gy * hat, axis=-1, keepdims=True)
     out_ref[...] = (dres_ref[...] + inverse * (gy - mean_one - hat * mean_two)).astype(BF)
+
+
+def ordered(kernel, inputs, later):
+    def run(*refs):
+        kernel(*refs[:inputs], *refs[inputs + later :])
+
+    return run if later else kernel
 
 
 def whole(shape):
@@ -780,13 +822,16 @@
     def along_dp(values, mask):
         return lax.ppermute(values, "dp", [(i, i ^ mask) for i in range(n_dp)])
 
-    def prefetched(kernel, grid, in_specs, out_specs, out_shape, mib, spent, name, scratch=(), alias=None):
-        return pl.pallas_call(
-            kernel,
+    def prefetched(
+        kernel, grid, in_specs, out_specs, out_shape, mib, spent, name, scratch=(), alias=None, first=()
+    ):
+        first = jax.tree.leaves(first)
+        call = pl.pallas_call(
+            ordered(kernel, 1 + len(in_specs), len(first)),
             grid_spec=pltpu.PrefetchScalarGridSpec(
                 num_scalar_prefetch=1,
                 grid=grid,
-                in_specs=in_specs,
+                in_specs=in_specs + [pl.BlockSpec(memory_space=pl.ANY)] * len(first),
                 out_specs=out_specs,
                 scratch_shapes=list(scratch),
             ),
@@ -796,9 +841,13 @@
             input_output_aliases=alias or {},
             name=name,
         )
+        return lambda *inputs: call(*inputs, *first)
 
     def after(values, *others):
         return lax.optimization_barrier((values, others))[0]
+
+    def scalar(spec):
+        return pl.BlockSpec(spec.block_shape, lambda *at: spec.index_map(*at[:-1]))
 
     def array(shape, dtype):
         return jax.ShapeDtypeStruct(shape, dtype)
@@ -829,16 +878,17 @@
     w_in = jnp.concatenate([w_query, w_keyval], axis=1).T.reshape(3, heads, hs, width)
     w_in = w_in.transpose(1, 0, 2, 3).reshape(groups, 3 * feats, width)
     table_shape = (own_heads, picks + groups * lines, clusters)
-    table = pl.pallas_call(
+    table = prefetched(
         functools.partial(table_kernel, picks=picks),
-        grid=(1,),
-        in_specs=[whole((own_heads, picks + lines, clusters))] * groups,
-        out_specs=whole(table_shape),
-        out_shape=array(table_shape, jnp.int32),
-        compiler_params=params(8, 1),
-        cost_estimate=cost(1e5, 1e6),
-        name="table",
-    )(*after(arrived, w_in))
+        (1,),
+        [whole((own_heads, picks + lines, clusters))] * groups,
+        whole(table_shape),
+        array(table_shape, jnp.int32),
+        8,
+        cost(1e5, 1e6),
+        "table",
+        first=w_in,
+    )(info, *arrived)
     tables = [table] + [along_peers(table, -hop) for hop in range(1, peers)]
     cot_got = [along_peers(after(cotangent, arrived), hop) for hop in range(1, peers)]
     cot_got = cot_got if fast else []
@@ -866,6 +916,7 @@
     split_peers = peers if peers <= 2 else 1
     for group in sorted(range(groups), key=lambda g: min(g, groups - g)):
         arrival = mine[group]
+        first = ()
         if group == 1:
             arrival = after(arrival, bias, held, cot_got, [mine[hop] for hop in range(2, groups)])
         chunk = [arrival]
@@ -889,7 +940,7 @@
                 pl.BlockSpec((own_heads, 3 * hs, span), lambda p, s, g=group: (0, 0, g)),
                 pl.BlockSpec((own_heads, span, 2 * hs), lambda p, s, g=group: (0, g, 0)),
             ]
-        first = 1 + split_peers + 3
+        old = 1 + split_peers + 3
         held = prefetched(
             functools.partial(project_kernel, peers=split_peers, olds=len(held)),
             grid,
@@ -905,7 +956,8 @@
             16 if fast else 60,
             cost(6 * span * width * feats, span * width * 4),
             "project",
-            alias={first + k: k for k in range(len(held))},
+            alias={old + k: k for k in range(len(held))},
+            first=first,
         )(info, *chunk, gain_row, shift_row, w_in, *held)
     hat_own, feat, kv = held
 
@@ -951,6 +1003,7 @@
 
     chunks = 4
     part = hidden // chunks
+    lead = 64
     w_out_g = w_out.reshape(groups, feats, width)
     gain_row2, shift_row2 = gain_two[None, :], shift_two[None, :]
     square = whole((rows, width))
@@ -1017,64 +1070,66 @@
         low_spec = whole((width + 16, rows))
         shape_u = (2, groups, high, width)
         shape_d = (2, groups, high, width)
-        send_u, keep_u, send_d, keep_d = prefetched(
+        parts = [(1, groups, tall, width) for tall in (lead, high - lead, high)]
+        results = prefetched(
             functools.partial(weights_kernel, groups=groups),
             (4,),
             [chunk, chunk, branch, branch, act_spec, act_there, low_spec, low_spec, square, square],
-            [
-                pl.BlockSpec((1,) + shape_u[1:], lambda i, s: (jnp.minimum(i, 1), 0, 0, 0)),
-                pl.BlockSpec((1,) + shape_u[1:], lambda i, s: (jnp.maximum(i - 2, 0), 0, 0, 0)),
-                whole(shape_d),
-                whole(shape_d),
-            ],
-            [array(shape_u, BF), array(shape_u, BF), array(shape_d, BF), array(shape_d, BF)],
+            [whole(item) for item in parts]
+            + [pl.BlockSpec((1,) + shape_u[1:], lambda i, s: (jnp.maximum(i - 2, 0), 0, 0, 0))]
+            + [whole(item) for item in parts]
+            + [whole(shape_d)],
+            ([array(item, BF) for item in parts] + [array(shape_u, BF)]) * 2,
             28,
             cost(8 * rows * width * hidden, 6 * width * hidden),
             "weights",
             scratch=[pltpu.VMEM((groups, block_rows, width), F32)],
         )(info, far, got, far, got, act_own, got, low_own, low_got, cotangent, *cot_got)
-        return send_u, keep_u, send_d, keep_d
-
-    def weight_second(keep_u, got_u, keep_d, got_d, inner, inner_got):
+        return results[:3], results[3], results[4:7], results[7]
+
+    def weight_second(keep_u, got_u, keep_d, got_d, inner, inner_got, late_u, late_d):
         def block(shape, at):
             return pl.BlockSpec((1,) + shape[1:], lambda i: (at, 0, 0, 0))
 
-        shape_u = keep_u.shape
-        lines = inner.shape[2]
-        shape = (groups, shape_u[2] + lines, width)
-        small = (groups, lines, width)
+        high, lines = keep_u.shape[2], inner.shape[2]
+        shapes = [(groups, high + lines + late_u.shape[2], width)] * 2 + [(groups, lines, width)]
         return pl.pallas_call(
             second_kernel,
             grid=(1,),
-            in_specs=[block(shape_u, 1)] * 4 + [whole(inner.shape)] * 2,
-            out_specs=[whole(shape), whole(shape), whole(small)],
-            out_shape=[array(shape, BF), array(shape, BF), array(small, BF)],
-            compiler_params=params(20, 1),
-            cost_estimate=cost(groups * shape[1] * width * 2, groups * shape[1] * width * 12),
+            in_specs=[
+                block(item.shape, item.shape[0] - 1) for item in (keep_u, got_u, keep_d, got_d)
+            ]
+            + [whole(item.shape) for item in (inner, inner_got, late_u, late_d)],
+            out_specs=[whole(shape) for shape in shapes],
+            out_shape=[array(shape, BF) for shape in shapes],
+            compiler_params=params(24, 1),
+            cost_estimate=cost(groups * high * width * 2, groups * high * width * 12),
             name="second",
-        )(keep_u, got_u, keep_d, got_d, inner, inner_got)
-
-    def weight_third(keep_u, got_u, keep_d, got_d, inner, inner_got, by_y, by_x, by_xy):
+        )(keep_u, got_u, keep_d, got_d, inner, inner_got, late_u, late_d)
+
+    def weight_third(keep_u, got_u, keep_d, got_d, by_y, by_x, inner, inner_got, by_xy):
         def block(shape, at):
-            return pl.BlockSpec((1,) + shape[1:], lambda i: (at, 0, 0, 0))
-
-        high = keep_u.shape[2]
-        tall = 2 * high + inner.shape[2]
-        sums = pl.pallas_call(
+            return pl.BlockSpec((1,) + shape[1:], lambda i, s: (at, 0, 0, 0))
+
+        left = keep_u.shape[2] - lead
+        talls = [(2 * lead, width)] * groups + [(2 * left + inner.shape[2], width)] * groups
+        more = (by_y, by_x)
+        return prefetched(
             third_kernel,
-            grid=(1,),
-            in_specs=[block(keep_u.shape, 0)] * 4
+            (1,),
+            [block(item.shape, 0) for item in (keep_u, got_u, keep_d, got_d)]
+            + [whole(by_y.shape), whole(by_x.shape)]
             + [block(inner.shape, 0)] * 2
-            + [whole(by_y.shape), whole(by_x.shape), whole(by_xy.shape)],
-            out_specs=[whole((tall, width))] * groups,
-            out_shape=[array((tall, width), BF)] * groups,
-            compiler_params=params(24, 1),
-            cost_estimate=cost(groups * tall * width * 4, groups * tall * width * 8),
-            name="third",
-        )(keep_u, got_u, keep_d, got_d, inner, inner_got, by_y, by_x, by_xy)
-        return [sums[0]] + [along_groups(sums[hop], hop) for hop in range(1, groups)]
-
-    def weight_sums(came, high, lines):
+            + [whole(by_xy.shape)],
+            [whole(tall) for tall in talls],
+            [array(tall, BF) for tall in talls],
+            24,
+            cost(groups * 256 * width * 4, groups * 256 * width * 8),
+            "third",
+            first=home,
+        )(info, keep_u, got_u, keep_d, got_d, by_y, by_x, inner, inner_got, by_xy)
+
+    def weight_fourth(came, high, lines, first):
         tall = 2 * high + 3 * lines
         done = prefetched(
             functools.partial(fourth_kernel, groups=groups, high=high, feats=3 * feats),
@@ -1085,19 +1140,21 @@
             16,
             cost(groups * tall * width, groups * tall * width * 2),
             "fourth",
-            scratch=[pltpu.VMEM((groups, lines, width), F32)],
+            scratch=[pltpu.VMEM((groups, lines, width), F32)] if lines else [],
+            first=first,
         )(info, *came)
-        from_x, from_y, from_xy = (along_dp(done, mask) for mask in (1, 2, 3))
+        return [done] + [along_dp(done, mask) for mask in (1, 2, 3)]
+
+    def weight_spread(firsts, lasts, high, ready):
         at = me * block_rows
         wq_rows = lax.dynamic_slice_in_dim(w_query, at, block_rows).astype(F32)
         wkv_rows = lax.dynamic_slice_in_dim(w_keyval, at, block_rows).astype(F32)
         pair = jnp.stack([shift_one, gain_one] + [shift_one] * 6, axis=1)
         pair = lax.dynamic_slice_in_dim(pair, at, block_rows)
-        pair, wq_rows, wkv_rows = after((pair, wq_rows, wkv_rows), came[0])
-        found = prefetched(
-            functools.partial(spread_kernel, high=high),
+        return prefetched(
+            functools.partial(spread_kernel, lead=lead, high=high),
             (4,),
-            [whole((tall, width))] * 4
+            [whole(item.shape) for item in firsts + lasts]
             + [whole(wq_rows.shape), whole(wkv_rows.shape), whole(pair.shape)],
             [
                 pl.BlockSpec((block_rows, part), lambda i, s: (0, i ^ s[3])),
@@ -1118,11 +1175,10 @@
                 array((block_rows, 128), F32),
             ],
             20,
-            cost(1e6, 4 * tall * width * 6),
+            cost(1e6, 8 * block_rows * width * 6),
             "spread",
             scratch=[pltpu.VMEM((3, 8, width), F32)],
-        )(info, done, from_x, from_y, from_xy, wq_rows, wkv_rows, pair)
-        return done, found
+        )(info, *firsts, *lasts, wq_rows, wkv_rows, pair)
 
     masks = [1 << k for k in range(n_dp.bit_length() - 1)]
 
@@ -1151,8 +1207,8 @@
 
     if fast:
         send_u, keep_u, send_d, keep_d = weight_parts()
-        got_u, got_d = along_dp(send_u, 1), along_dp(send_d, 2)
-        grads = after(grads, keep_u)
+        got_u = [along_dp(item, 1) for item in (send_u[0], send_u[2])]
+        got_d = [along_dp(item, 2) for item in (send_d[0], send_d[2])]
     else:
         norm_two, d_up, d_branch, act, normed_two = kept
         total_up = reduce_rows(tn(normed_two, d_up).astype(BF))
@@ -1165,18 +1221,17 @@
         total_out = reduce_rows(jnp.concatenate(found, axis=0))
         norm_own = reduce_rows(norm_two[:2].T.astype(BF)).T
 
-    share = pl.pallas_call(
+    share = prefetched(
         functools.partial(sums_kernel, groups=groups),
-        grid=(own_heads,),
-        in_specs=[ids_one]
-        + [rows_one] * groups
-        + [mix_one],
-        out_specs=part_one,
-        out_shape=array((own_heads, hs + 16, clusters), F32),
-        compiler_params=params(16 if fast else 60, 1),
-        cost_estimate=cost(own_heads * own_rows * clusters * 160, 2e6),
-        name="sums",
-    )(ids_all, *grads, mixed)
+        (own_heads,),
+        [scalar(spec) for spec in (ids_one, *[rows_one] * groups, mix_one)],
+        scalar(part_one),
+        array((own_heads, hs + 16, clusters), F32),
+        16 if fast else 60,
+        cost(own_heads * own_rows * clusters * 160, 2e6),
+        "sums",
+        first=(keep_u, keep_d) if fast else (),
+    )(info, ids_all, *grads, mixed)
     share_got = [along_peers(share, hop) for hop in range(1, peers)]
 
     back_shapes = [
@@ -1202,6 +1257,8 @@
         cost_estimate=cost(14 * pair_flops, 10e6, own_heads * own_rows * seq),
         name="back",
     )(ids_all, feat, kv, bias, *grads, mixed, stats, centroid, share, *share_got)
+    if fast:
+        dkv_send = after(dkv_send, got_u, got_d)
     dkv_got = [
         along_peers(
             dkv_send if peers == 2 else dkv_send[..., (hop - 1) * own_rows : hop * own_rows], hop
@@ -1215,8 +1272,6 @@
         more = [array((4, groups, lines, width), BF)] * 2
     else:
         more = [array((width, 3 * feats), F32), array((16, 3 * feats), F32)]
-    if fast:
-        dkv_own = after(dkv_own, got_u, got_d)
     results = prefetched(
         functools.partial(inward_kernel, groups=groups, gots=len(dkv_got), fast=fast),
         (1,),
@@ -1232,18 +1287,36 @@
     d_in, more = results[:groups], results[groups:]
     home = [d_in[0]] + [along_groups(d_in[hop], hop) for hop in range(1, groups)]
 
+    grad_tokens = prefetched(
+        functools.partial(final_kernel, groups=groups),
+        (1,),
+        [whole((own_heads, 3 * hs, rows))] * groups
+        + [square, square, whole((1, width)), whole((groups, 3 * feats, width))],
+        square,
+        array((rows, width), BF),
+        24 if fast else 60,
+        cost(6 * rows * width * width, 6 * width * width),
+        "final",
+    )(info, *home, tokens, d_resid, gain_row, w_in)
+
     if fast:
         keep, far = more
         inner_got = along_peers(far, 1)
-        got_u, got_d = after((got_u, got_d), home[1])
-        to_y, to_x, to_xy = weight_second(keep_u, got_u, keep_d, got_d, keep, inner_got)
+        to_y, to_x, to_xy = weight_second(
+            keep_u, got_u[1], keep_d, got_d[1], keep, inner_got, send_u[1], send_d[1]
+        )
         by_y, by_x, by_xy = along_dp(to_y, 2), along_dp(to_x, 1), along_dp(to_xy, 3)
-        by_y, by_x = after((by_y, by_x), home)
-        came = weight_third(
-            keep_u, got_u, keep_d, got_d, keep, inner_got, by_y, by_x, by_xy
+        sums = weight_third(
+            keep_u, got_u[0], keep_d, got_d[0], by_y, by_x, keep, inner_got, by_xy
         )
-        done, found = weight_sums(came, keep_u.shape[2], lines)
-        home = after(home, done)
+        came_a, came_b = [sums[0]], [sums[groups]]
+        came_a += [along_groups(sums[hop], hop) for hop in range(1, groups)]
+        late = after(sums[groups + 1 :], came_a[1])
+        came_b += [along_groups(late[hop - 1], hop) for hop in range(1, groups)]
+        spread_a = weight_fourth(came_a, lead, 0, (came_b[1], grad_tokens))
+        high = keep_u.shape[2] - lead
+        spread_b = weight_fourth(came_b, high, lines, spread_a)
+        found = weight_spread(spread_a, spread_b, high, came_a[0])
         total_up, total_out, total_down, norms, total_query, total_keyval, vector = found
         norm_own = lax.dynamic_slice_in_dim(norms, me * block_rows, block_rows, axis=1)
         gain_grad, shift_grad = vector[:, 0], vector[:, 1]
@@ -1296,17 +1369,6 @@
         total_keyval = kv_part + shift_own[:, None] * kv_sum
         gain_grad = along / gain_own
 
-    grad_tokens = prefetched(
-        functools.partial(final_kernel, groups=groups),
-        (1,),
-        [whole((own_heads, 3 * hs, rows))] * groups
-        + [square, square, whole((1, width)), whole((groups, 3 * feats, width))],
-        square,
-        array((rows, width), BF),
-        24 if fast else 60,
-        cost(6 * rows * width * width, 6 * width * width),
-        "final",
-    )(info, *home, tokens, d_resid, gain_row, w_in)
 
     return (
         output,

time: 265 us -> 248 us (0.936)
  waiting for transfers between devices: 104 us -> 84.5 us
  starting transfers between devices: 35.2 us -> 46.8 us
  local copies, waits for them, and re-layouts: 28.9 us -> 22 us
  Pallas kernels: 89.9 us -> 87.2 us
    ppermute x18 -> x21, waiting for transfers between devices: 80.2 us -> 61.2 us  [along_groups(): return lax.ppermute(values, 'wide', pairs)]
    ppermute x18 -> x21, starting transfers between devices: 23.7 us -> 30.1 us  [along_groups(): return lax.ppermute(values, 'wide', pairs)]
    unnamed x80 -> x51, local copies, waits for them, and re-layouts: 21.3 us -> 16.3 us
    ppermute x8 -> x13, waiting for transfers between devices: 22.4 us -> 17.5 us  [along_dp(): return lax.ppermute(values, 'dp', [(i, i ^ mask) for i in range(n_dp)])]
    ppermute x8 -> x13, starting transfers between devices: 10.1 us -> 14.8 us  [along_dp(): return lax.ppermute(values, 'dp', [(i, i ^ mask) for i in range(n_dp)])]
    ppermute x11, waiting for transfers between devices: 1.45 us -> 5.87 us  [along_peers(): return lax.ppermute(values, 'wide', pairs)]
    pallas_call x15 -> x16, Pallas kernels: 56.3 us -> 53.1 us  [the longest x15 52.6 us: prefetched(): return lambda *inputs: call(*inputs, *first)]
  transfers between devices with their start and end apart: 37 -> 45, of which waited for: 17 -> 24; matrix products, arithmetic and copies ran while one was open for 6% -> 5% of each run, Pallas kernels for 19% -> 20%
where the time goes in v8:
time: 248 us; the launch traced here: 247 us
  Pallas kernels  87.2 us (35%)
  waiting for transfers between devices  84.5 us (34%)
  starting transfers between devices  46.8 us (19%)
  local copies, waits for them, and re-layouts  22 us (9%)
  other arithmetic  4.19 us (2%)
    ppermute x21, waiting for transfers between devices, along_groups(): return lax.ppermute(values, 'wide', pairs)  61.2 us
    pallas_call x15, Pallas kernels, prefetched(): return lambda *inputs: call(*inputs, *first)  52.6 us
    ppermute x21, starting transfers between devices, along_groups(): return lax.ppermute(values, 'wide', pairs)  30.1 us
    pallas_call x1, Pallas kernels, per_device(): pl.pallas_call(functools.partial(back_kernel, size=size, groups=groups, g...  20.6 us
    ppermute x13, waiting for transfers between devices, along_dp(): return lax.ppermute(values, 'dp', [(i, i ^ mask) for i in range(n_dp)])  17.5 us
    unnamed x51, local copies, waits for them, and re-layouts  16.3 us
    ppermute x13, starting transfers between devices, along_dp(): return lax.ppermute(values, 'dp', [(i, i ^ mask) for i in range(n_dp)])  14.8 us
    pallas_call x1, Pallas kernels, per_device(): pl.pallas_call(functools.partial(forward_kernel, size=size, groups=groups...  13.4 us
  transfers between devices with their start and end apart: 45, of which 24 were waited for; matrix products, arithmetic and copies ran while one was open for 5% of the time, Pallas kernels for 20%

profile of v8, /device:TPU:8, one launch (start us, length us, event | category | flops | bytes accessed | tf_op | source)
XLA Modules:
  0.0 246.7 jit_solution(11565806347344396816)
XLA Ops:
  3.3 2.1 dynamic_update_slice.3
  6.1 3.0 %collective-permute-start.2 = (s32[3,34,128]{2,1,0:T(8,128)S(1)}, s32[3,34,128]{2,1,0:T(8,128)S(1)}, u32[]{:S(2)}, u32[]{:S(2)}) collective-permute-start(s32[3,34,128]{2,1,0:T(8,128)S(1)} %get-tuple-element.162), channel_id=1, source_target_pairs={{0,4},{1,5},{2,6},{3,7},{4,0},{5,1},{6,2},{7,3},{8,12},{9,13},{10,... | collective-permute-start | bytes 156680 | tf_op jit(solution)/shard_map/ppermute | solution.py:816
  9.2 2.5 %collective-permute-start.3 = (s32[3,34,128]{2,1,0:T(8,128)S(1)}, s32[3,34,128]{2,1,0:T(8,128)S(1)}, u32[]{:S(2)}, u32[]{:S(2)}) collective-permute-start(s32[3,34,128]{2,1,0:T(8,128)S(1)} %get-tuple-element.161), channel_id=1, source_target_pairs={{0,2},{1,3},{2,4},{3,5},{4,6},{5,7},{6,0},{7,1},{8,10},{9,11},{10,... | collective-permute-start | bytes 156680 | tf_op jit(solution)/shard_map/ppermute | solution.py:816
  11.7 2.0 collective-permute-start.9
  13.7 2.8 %copy.50 = bf16[768,1536]{0,1:T(8,128)(2,1)S(1)} copy(bf16[768,1536]{1,0:T(8,128)(2,1)} %param.21) | data formatting | bytes 4718592 | tf_op args[7]
  16.5 2.4 copy.49
  26.4 2.7 %project.4 = (bf16[768,1024]{1,0:T(8,128)(2,1)S(1)}, bf16[3,192,2048]{2,1,0:T(8,128)(2,1)S(1)}, bf16[3,2048,128]{2,1,0:T(8,128)(2,1)S(1)}) custom-call(s32[6]{0:T(128)S(1)} %stack.38.refs_0_.info, bf16[256,768]{1,0:T(8,128)(2,1)} %refs_4_.3, bf16[256,768]{1,0:T(8,128)(2,1)S(1)} %copy-done.4, f32[1,768]{1,0:T(1,128)S(1)} %broadcast_in_dim.31.refs_2_.refs_6_, ...), custom_call_target="tpu_custom_call" | custom-call | flops 452984832 | bytes 1572864 | tf_op jit(solution)/shard_map/project/pallas_call | solution.py:844
  29.1 7.6 %bias.1 = (bf16[3,2048,128]{2,1,0:T(8,128)(2,1)S(1)}, s32[3,1,2048]{2,1,0:T(1,128)S(1)}) custom-call(s32[6]{0:T(128)S(1)} %stack.38.refs_0_.info, s32[3,40,128]{2,1,0:T(8,128)S(1)} %table.1.refs_0_, s32[3,40,128]{2,1,0:T(8,128)S(1)} %collective-permute-done.4.refs_1_), custom_call_target="tpu_custom_call" | custom-call | flops 201326592 | bytes 1572864 | tf_op jit(solution)/shard_map/bias/pallas_call | solution.py:844
  36.8 4.0 %collective-permute-done.7.refs_0_ = bf16[256,768]{1,0:T(8,128)(2,1)} collective-permute-done((bf16[256,768]{1,0:T(8,128)(2,1)}, bf16[256,768]{1,0:T(8,128)(2,1)}, u32[]{:S(2)}, u32[]{:S(2)}) %collective-permute-start.7) | collective-permute-done | bytes 393248 | tf_op jit(solution)/shard_map/ppermute | solution.py:816
  41.2 7.4 %collective-permute-done.5.refs_0_ = bf16[256,768]{1,0:T(8,128)(2,1)} collective-permute-done((bf16[256,768]{1,0:T(8,128)(2,1)}, bf16[256,768]{1,0:T(8,128)(2,1)}, u32[]{:S(2)}, u32[]{:S(2)}) %collective-permute-start.5) | collective-permute-done | bytes 393248 | tf_op jit(solution)/shard_map/ppermute | solution.py:816
  50.6 2.7 %project.5 = (bf16[768,1024]{1,0:T(8,128)(2,1)S(1)}, bf16[3,192,2048]{2,1,0:T(8,128)(2,1)S(1)}, bf16[3,2048,128]{2,1,0:T(8,128)(2,1)S(1)}) custom-call(s32[6]{0:T(128)S(1)} %stack.38.refs_0_.info, bf16[256,768]{1,0:T(8,128)(2,1)} %collective-permute-done.9.refs_0_, ...), custom_call_target="tpu_custom_call", output_to_operand_aliasing={{0}: (6, {}), {1}: (7, {}), {2}: (8, {})} | custom-call | flops 452984832 | bytes 1572864 | tf_op jit(solution)/shard_map/project/pallas_call | solution.py:844
  53.3 2.7 %project.6 = (bf16[768,1024]{1,0:T(8,128)(2,1)S(1)}, bf16[3,192,2048]{2,1,0:T(8,128)(2,1)S(1)}, bf16[3,2048,128]{2,1,0:T(8,128)(2,1)S(1)}) custom-call(s32[6]{0:T(128)S(1)} %stack.38.refs_0_.info, bf16[256,768]{1,0:T(8,128)(2,1)} %collective-permute-done.7.refs_0_, ...), custom_call_target="tpu_custom_call", output_to_operand_aliasing={{0}: (6, {}), {1}: (7, {}), {2}: (8, {})} | custom-call | flops 452984832 | bytes 1572864 | tf_op jit(solution)/shard_map/project/pallas_call | solution.py:844
  56.1 3.0 %project.7 = (bf16[768,1024]{1,0:T(8,128)(2,1)S(1)}, bf16[3,192,2048]{2,1,0:T(8,128)(2,1)S(1)}, bf16[3,2048,128]{2,1,0:T(8,128)(2,1)S(1)}) custom-call(s32[6]{0:T(128)S(1)} %stack.38.refs_0_.info, bf16[256,768]{1,0:T(8,128)(2,1)} %collective-permute-done.5.refs_0_, ...), custom_call_target="tpu_custom_call", output_to_operand_aliasing={{0}: (6, {}), {1}: (7, {}), {2}: (8, {})} | custom-call | flops 452984832 | bytes 1572864 | tf_op jit(solution)/shard_map/project/pallas_call | solution.py:844
  59.1 13.4 %attend.1 = (bf16[192,256]{1,0:T(8,128)(2,1)S(1)}, bf16[192,256]{1,0:T(8,128)(2,1)S(1)}, bf16[192,256]{1,0:T(8,128)(2,1)S(1)}, bf16[192,256]{1,0:T(8,128)(2,1)S(...) custom-call(s32[3,1,2048]{2,1,0:T(1,128)S(1)} %get-tuple-element.86.ids_all.refs_1_, ...), custom_call_target="tpu_custom_call" | custom-call | flops 9663676416 | bytes 8000000 | tf_op jit(solution)/shard_map/attend/pallas_call | solution.py:984
  72.8 4.3 %collective-permute-start.13 = (bf16[192,256]{1,0:T(8,128)(2,1)S(1)}, bf16[192,256]{1,0:T(8,128)(2,1)S(1)}, u32[]{:S(2)}, u32[]{:S(2)}) collective-permute-start(bf16[192,256]{1,0:T(8,128)(2,1)S(1)} %get-tuple-element.104), channel_id=1, source_target_pairs={{0,4},{1,5},{2,6},{3,7},{4,0},{5,1},{6,2},{7,3},{8,12},{9,13},{10,... | collective-permute-start | bytes 294920 | tf_op jit(solution)/shard_map/ppermute | solution.py:816
  78.0 5.4 %collective-permute-done.13.refs_2_ = bf16[192,256]{1,0:T(8,128)(2,1)S(1)} collective-permute-done((bf16[192,256]{1,0:T(8,128)(2,1)S(1)}, bf16[192,256]{1,0:T(8,128)(2,1)S(1)}, u32[]{:S(2)}, u32[]{:S(2)}) %collective-permute-start.13) | collective-permute-done | bytes 98336 | tf_op jit(solution)/shard_map/ppermute | solution.py:816
  83.4 2.2 collective-permute-done.14.refs_3_
  85.7 2.3 copy-done.14
  88.0 10.9 %feed.1 = (bf16[256,768]{1,0:T(8,128)(2,1)}, f32[256,768]{1,0:T(8,128)S(1)}, bf16[256,5376]{1,0:T(8,128)(2,1)S(1)}, bf16[784,256]{1,0:T(8,128)(2,1)S(1)}, bf16[2...) custom-call(s32[6]{0:T(128)S(1)} %stack.38.refs_0_.info, ...), custom_call_target="tpu_custom_call" | custom-call | flops 4831838208 | bytes 9437184 | tf_op jit(solution)/shard_map/feed/pallas_call | solution.py:844
  102.1 2.9 %collective-permute-start.17 = (bf16[192,256]{1,0:T(8,128)(2,1)S(1)}, bf16[192,256]{1,0:T(8,128)(2,1)S(1)}, u32[]{:S(2)}, u32[]{:S(2)}) collective-permute-start(bf16[192,256]{1,0:T(8,128)(2,1)S(1)} %get-tuple-element.110), channel_id=1, source_target_pairs={{0,2},{1,3},{2,4},{3,5},{4,6},{5,7},{6,0},{7,1},{8,10},{9,11},{10,... | collective-permute-start | bytes 294920 | tf_op jit(solution)/shard_map/ppermute | solution.py:816
  105.0 1.8 copy-done.16
  106.8 8.4 %weights.1 = (bf16[1,4,64,768]{3,2,1,0:T(8,128)(2,1)S(1)}, bf16[1,4,48,768]{3,2,1,0:T(8,128)(2,1)S(1)}, bf16[1,4,112,768]{3,2,1,0:T(8,128)(2,1)S(1)}, bf16[2,4,1...) custom-call(s32[6]{0:T(128)S(1)} %stack.38.refs_0_.info, ...), custom_call_target="tpu_custom_call" | custom-call | flops 4831838208 | bytes 14155776 | tf_op jit(solution)/shard_map/weights/pallas_call | solution.py:844
  120.8 20.6 %back.1 = (bf16[4,192,256]{2,1,0:T(8,128)(2,1)S(1)}, f32[3,128,1024]{2,1,0:T(8,128)S(1)}, bf16[3,128,1024]{2,1,0:T(8,128)(2,1)S(1)}) custom-call(s32[3,1,2048]{2,1,0:T(1,128)S(1)} %get-tuple-element.86.ids_all.refs_1_, bf16[3,192,2048]{2,1,0:T(8,128)(2,1)S(1)} %get-tuple-element.100.feat, bf16[3,2048,128]{2,1,0:T(8,128)(2,1)S(1)} %get-tuple-element.101.kv, ...), custom_call_target="tpu_custom_call" | custom-call | flops 22548578304 | bytes 10000000 | tf_op jit(solution)/shard_map/back/pallas_call | solution.py:1242
  144.5 2.3 collective-permute-done.25.refs_2_
  146.7 2.4 inward.1
  149.4 2.1 collective-permute-done.29.inner_got.refs_8_
  152.0 1.6 collective-permute-start.30
  155.0 2.0 collective-permute-start.27
  157.0 1.9 collective-permute-start.28
  158.9 6.1 %collective-permute-done.26.refs_1_.refs_11_ = bf16[3,192,256]{2,1,0:T(8,128)(2,1)S(1)} collective-permute-done((bf16[3,192,256]{2,1,0:T(8,128)(2,1)S(1)}, bf16[3,192,256]{2,1,0:T(8,128)(2,1)S(1)}, u32[]{:S(2)}, u32[]{:S(2)}) %collective-permute-start.26) | collective-permute-done | bytes 294944 | tf_op jit(solution)/shard_map/ppermute | solution.py:816
  165.5 14.8 %collective-permute-done.27.refs_2_.refs_12_ = bf16[3,192,256]{2,1,0:T(8,128)(2,1)S(1)} collective-permute-done((bf16[3,192,256]{2,1,0:T(8,128)(2,1)S(1)}, bf16[3,192,256]{2,1,0:T(8,128)(2,1)S(1)}, u32[]{:S(2)}, u32[]{:S(2)}) %collective-permute-start.27) | collective-permute-done | bytes 294944 | tf_op jit(solution)/shard_map/ppermute | solution.py:816
  180.3 2.3 collective-permute-done.28.refs_3_.refs_13_
  182.6 2.9 %collective-permute-done.32.refs_9_ = bf16[4,32,768]{2,1,0:T(8,128)(2,1)S(1)} collective-permute-done((bf16[4,32,768]{2,1,0:T(8,128)(2,1)S(1)}, bf16[4,32,768]{2,1,0:T(8,128)(2,1)S(1)}, u32[]{:S(2)}, u32[]{:S(2)}) %collective-permute-start.32) | collective-permute-done | bytes 196640 | tf_op jit(solution)/shard_map/ppermute | solution.py:823
  185.5 1.5 third.1
  187.0 2.0 collective-permute-start.34
  188.9 1.8 collective-permute-start.35
  190.7 8.0 %collective-permute-done.33.refs_2_ = bf16[128,768]{1,0:T(8,128)(2,1)S(1)} collective-permute-done((bf16[128,768]{1,0:T(8,128)(2,1)S(1)}, bf16[128,768]{1,0:T(8,128)(2,1)S(1)}, u32[]{:S(2)}, u32[]{:S(2)}) %collective-permute-start.33) | collective-permute-done | bytes 196640 | tf_op jit(solution)/shard_map/ppermute | solution.py:816
  198.8 3.0 %collective-permute-start.36 = (bf16[128,768]{1,0:T(8,128)(2,1)S(1)}, bf16[128,768]{1,0:T(8,128)(2,1)S(1)}, u32[]{:S(2)}, u32[]{:S(2)}) collective-permute-start(bf16[128,768]{1,0:T(8,128)(2,1)S(1)} %get-tuple-element.148), channel_id=1, source_target_pairs={{0,2},{1,3},{2,4},{3,5},{4,6},{5,7},{6,0},{7,1},{8,10},{9,11},{10,... | collective-permute-start | bytes 589832 | tf_op jit(solution)/shard_map/ppermute | solution.py:816
  201.7 4.0 %final.1.refs_6_ = bf16[256,768]{1,0:T(8,128)(2,1)} custom-call(s32[6]{0:T(128)S(1)} %stack.38.refs_0_.info, bf16[3,192,256]{2,1,0:T(8,128)(2,1)S(1)} %get-tuple-element.129.refs_0_.refs_10_, bf16[3,192,256]{2,1,0:T(8,128)(2,1)S(1)} %collective-permute-done.26.refs_1_.refs_11_, bf16[3,192,256]{2,1,0:T(8,128)(2,1)S(1)} %collective-permute-done.27.refs_2_.refs_12_, ...), custom_call_target="tpu_custom_call" | custom-call | flops 905969664 | bytes 3538944 | tf_op jit(solution)/shard_map/final/pallas_call | solution.py:844
  207.2 6.1 %collective-permute-done.34.refs_3_ = bf16[128,768]{1,0:T(8,128)(2,1)S(1)} collective-permute-done((bf16[128,768]{1,0:T(8,128)(2,1)S(1)}, bf16[128,768]{1,0:T(8,128)(2,1)S(1)}, u32[]{:S(2)}, u32[]{:S(2)}) %collective-permute-start.34) | collective-permute-done | bytes 196640 | tf_op jit(solution)/shard_map/ppermute | solution.py:816
  213.9 3.7 %collective-permute-done.36.refs_5_.refs_2_ = bf16[128,768]{1,0:T(8,128)(2,1)S(1)} collective-permute-done((bf16[128,768]{1,0:T(8,128)(2,1)S(1)}, bf16[128,768]{1,0:T(8,128)(2,1)S(1)}, u32[]{:S(2)}, u32[]{:S(2)}) %collective-permute-start.36) | collective-permute-done | bytes 196640 | tf_op jit(solution)/shard_map/ppermute | solution.py:816
  220.8 1.5 collective-permute-start.38
  225.2 2.5 %collective-permute-done.38.refs_7_.refs_2_ = bf16[128,768]{1,0:T(8,128)(2,1)S(1)} collective-permute-done((bf16[128,768]{1,0:T(8,128)(2,1)S(1)}, bf16[128,768]{1,0:T(8,128)(2,1)S(1)}, u32[]{:S(2)}, u32[]{:S(2)}) %collective-permute-start.38) | collective-permute-done | bytes 196640 | tf_op jit(solution)/shard_map/ppermute | solution.py:823
  232.4 1.7 collective-permute-start.44
  235.3 2.3 collective-permute-done.42.refs_5_
  237.6 2.7 %collective-permute-done.43.refs_6_ = bf16[192,768]{1,0:T(8,128)(2,1)S(1)} collective-permute-done((bf16[192,768]{1,0:T(8,128)(2,1)S(1)}, bf16[192,768]{1,0:T(8,128)(2,1)S(1)}, u32[]{:S(2)}, u32[]{:S(2)}) %collective-permute-start.43) | collective-permute-done | bytes 294944 | tf_op jit(solution)/shard_map/ppermute | solution.py:823
  240.3 1.6 collective-permute-done.44.refs_7_
  242.0 3.4 %spread.1 = (f32[96,3072]{1,0:T(8,128)}, f32[96,768]{1,0:T(8,128)}, f32[384,768]{1,0:T(8,128)}, f32[8,768]{1,0:T(8,128)S(1)}, f32[96,768]{1,0:T(8,128)}, /*index=5*/f32[96,1536]{1,0:T(8,128)}, f32[96,128]{1,0:T(8,128)S(1)}) custom-call(s32[6]{0:T(128)S(1)} %stack.38.refs_0_.info, bf16[128,768]{1,0:T(8,128)(2,1)S(1)} %fourth.2.refs_5_.refs_0_, ...), custom_call_target="tpu_custom_call" | custom-call | flops 1000000 | bytes 3538944 | tf_op jit(solution)/shard_map/spread/pallas_call | solution.py:844
  (136 shorter events, 43.3 us)
Async XLA Ops:
  0.6 4.8 %collective-permute-start = (bf16[256,768]{1,0:T(8,128)(2,1)}, bf16[256,768]{1,0:T(8,128)(2,1)S(1)}, u32[]{:S(2)}, u32[]{:S(2)}) collective-permute-start(bf16[256,768]{1,0:T(8,128)(2,1)} %refs_4_.3), channel_id=1, source_target_pairs={{0,1},{1,0},{2,3},{3,2},{4,5},{5,4},{6,7},{7,6},{8,9},{9,8},{10,11... | collective-permute-start | bytes 1179656 | tf_op jit(solution)/shard_map/ppermute | solution.py:820
  6.1 12.8 %collective-permute-start.1 = (s32[3,34,128]{2,1,0:T(8,128)S(1)}, s32[3,34,128]{2,1,0:T(8,128)S(1)}, u32[]{:S(2)}, u32[]{:S(2)}) collective-permute-start(s32[3,34,128]{2,1,0:T(8,128)S(1)} %get-tuple-element.163), channel_id=1, source_target_pairs={{0,6},{1,7},{2,0},{3,1},{4,2},{5,3},{6,4},{7,5},{8,14},{9,15},{10,... | collective-permute-start | bytes 156680 | tf_op jit(solution)/shard_map/ppermute | solution.py:816
  6.1 12.8 %collective-permute-start.2 = (s32[3,34,128]{2,1,0:T(8,128)S(1)}, s32[3,34,128]{2,1,0:T(8,128)S(1)}, u32[]{:S(2)}, u32[]{:S(2)}) collective-permute-start(s32[3,34,128]{2,1,0:T(8,128)S(1)} %get-tuple-element.162), channel_id=1, source_target_pairs={{0,4},{1,5},{2,6},{3,7},{4,0},{5,1},{6,2},{7,3},{8,12},{9,13},{10,... | collective-permute-start | bytes 156680 | tf_op jit(solution)/shard_map/ppermute | solution.py:816
  9.2 9.8 %collective-permute-start.3 = (s32[3,34,128]{2,1,0:T(8,128)S(1)}, s32[3,34,128]{2,1,0:T(8,128)S(1)}, u32[]{:S(2)}, u32[]{:S(2)}) collective-permute-start(s32[3,34,128]{2,1,0:T(8,128)S(1)} %get-tuple-element.161), channel_id=1, source_target_pairs={{0,2},{1,3},{2,4},{3,5},{4,6},{5,7},{6,0},{7,1},{8,10},{9,11},{10,... | collective-permute-start | bytes 156680 | tf_op jit(solution)/shard_map/ppermute | solution.py:816
  11.7 29.1 %collective-permute-start.7 = (bf16[256,768]{1,0:T(8,128)(2,1)}, bf16[256,768]{1,0:T(8,128)(2,1)}, u32[]{:S(2)}, u32[]{:S(2)}) collective-permute-start(bf16[256,768]{1,0:T(8,128)(2,1)} %refs_4_.3), channel_id=1, source_target_pairs={{0,2},{1,3},{2,4},{3,5},{4,6},{5,7},{6,0},{7,1},{8,10},{9,11},{10,... | collective-permute-start | bytes 1179656 | tf_op jit(solution)/shard_map/ppermute | solution.py:816
  11.7 29.6 %collective-permute-start.9 = (bf16[256,768]{1,0:T(8,128)(2,1)}, bf16[256,768]{1,0:T(8,128)(2,1)}, u32[]{:S(2)}, u32[]{:S(2)}) collective-permute-start(bf16[256,768]{1,0:T(8,128)(2,1)} %refs_4_.3), channel_id=1, source_target_pairs={{0,6},{1,7},{2,0},{3,1},{4,2},{5,3},{6,4},{7,5},{8,14},{9,15},{10,... | collective-permute-start | bytes 1179656 | tf_op jit(solution)/shard_map/ppermute | solution.py:816
  19.0 29.7 %collective-permute-start.5 = (bf16[256,768]{1,0:T(8,128)(2,1)}, bf16[256,768]{1,0:T(8,128)(2,1)}, u32[]{:S(2)}, u32[]{:S(2)}) collective-permute-start(bf16[256,768]{1,0:T(8,128)(2,1)} %refs_4_.3), channel_id=1, source_target_pairs={{0,4},{1,5},{2,6},{3,7},{4,0},{5,1},{6,2},{7,3},{8,12},{9,13},{10,... | collective-permute-start | bytes 1179656 | tf_op jit(solution)/shard_map/ppermute | solution.py:816
  19.9 28.7 %collective-permute-start.10 = (bf16[256,768]{1,0:T(8,128)(2,1)}, bf16[256,768]{1,0:T(8,128)(2,1)}, u32[]{:S(2)}, u32[]{:S(2)}) collective-permute-start(bf16[256,768]{1,0:T(8,128)(2,1)} %refs_8_.3), channel_id=1, source_target_pairs={{0,1},{1,0},{2,3},{3,2},{4,5},{5,4},{6,7},{7,6},{8,9},{9,8},{10,11... | collective-permute-start | bytes 1179656 | tf_op jit(solution)/shard_map/ppermute | solution.py:820
  25.8 3.3 %collective-permute-start.4 = (s32[3,40,128]{2,1,0:T(8,128)S(1)}, s32[3,40,128]{2,1,0:T(8,128)S(1)}, u32[]{:S(2)}, u32[]{:S(2)}) collective-permute-start(s32[3,40,128]{2,1,0:T(8,128)S(1)} %table.1.refs_0_), channel_id=1, source_target_pairs={{0,1},{1,0},{2,3},{3,2},{4,5},{5,4},{6,7},{7,6},{8,9},{9,8},{10,11... | collective-permute-start | bytes 184328 | tf_op jit(solution)/shard_map/ppermute | solution.py:820
  48.7 1.9 collective-permute-start.11
  48.7 4.7 %collective-permute-start.8 = (bf16[256,768]{1,0:T(8,128)(2,1)}, bf16[256,768]{1,0:T(8,128)(2,1)S(1)}, u32[]{:S(2)}, u32[]{:S(2)}) collective-permute-start(bf16[256,768]{1,0:T(8,128)(2,1)} %collective-permute-done.7.refs_0_), channel_id=1, source_target_pairs={{0,1},{1,0},{2,3},{3,2},{4,5},{5,4},{6,7},{7,6},{8,9},{9,8},{10,11... | collective-permute-start | bytes 1179656 | tf_op jit(solution)/shard_map/ppermute | solution.py:820
  49.2 6.9 %collective-permute-start.6 = (bf16[256,768]{1,0:T(8,128)(2,1)}, bf16[256,768]{1,0:T(8,128)(2,1)S(1)}, u32[]{:S(2)}, u32[]{:S(2)}) collective-permute-start(bf16[256,768]{1,0:T(8,128)(2,1)} %collective-permute-done.5.refs_0_), channel_id=1, source_target_pairs={{0,1},{1,0},{2,3},{3,2},{4,5},{5,4},{6,7},{7,6},{8,9},{9,8},{10,11... | collective-permute-start | bytes 1179656 | tf_op jit(solution)/shard_map/ppermute | solution.py:820
  56.1 29.6 %slice-start = ((s8[4718592]{0:T(1024)(128)(4,1)}), s8[4194304]{0:T(1024)(128)(4,1)S(1)}, s32[]{:S(2)}) async-start(s8[4718592]{0:T(1024)(128)(4,1)} %bitcast.38), calls=%async_computation | async-start | bytes 8388608
  59.1 26.6 %slice-start.1 = ((s8[4718592]{0:T(1024)(128)(4,1)}), s8[524288]{0:T(1024)(128)(4,1)S(1)}, s32[]{:S(2)}) async-start(s8[4718592]{0:T(1024)(128)(4,1)} %bitcast.38), calls=%async_computation.1 | async-start | bytes 1048576
  59.1 26.5 %copy-start.17 = (bf16[768,768]{1,0:T(8,128)(2,1)S(1)}, bf16[768,768]{1,0:T(8,128)(2,1)}, u32[]{:S(2)}) copy-start(bf16[768,768]{1,0:T(8,128)(2,1)} %param.22) | copy-start | bytes 3538948
  72.5 5.5 %collective-permute-start.12 = (bf16[192,256]{1,0:T(8,128)(2,1)S(1)}, bf16[192,256]{1,0:T(8,128)(2,1)S(1)}, u32[]{:S(2)}, u32[]{:S(2)}) collective-permute-start(bf16[192,256]{1,0:T(8,128)(2,1)S(1)} %get-tuple-element.103), channel_id=1, source_target_pairs={{0,2},{1,3},{2,4},{3,5},{4,6},{5,7},{6,0},{7,1},{8,10},{9,11},{10,... | collective-permute-start | bytes 294920 | tf_op jit(solution)/shard_map/ppermute | solution.py:816
  72.8 10.6 %collective-permute-start.13 = (bf16[192,256]{1,0:T(8,128)(2,1)S(1)}, bf16[192,256]{1,0:T(8,128)(2,1)S(1)}, u32[]{:S(2)}, u32[]{:S(2)}) collective-permute-start(bf16[192,256]{1,0:T(8,128)(2,1)S(1)} %get-tuple-element.104), channel_id=1, source_target_pairs={{0,4},{1,5},{2,6},{3,7},{4,0},{5,1},{6,2},{7,3},{8,12},{9,13},{10,... | collective-permute-start | bytes 294920 | tf_op jit(solution)/shard_map/ppermute | solution.py:816
  77.1 8.5 %collective-permute-start.14 = (bf16[192,256]{1,0:T(8,128)(2,1)S(1)}, bf16[192,256]{1,0:T(8,128)(2,1)S(1)}, u32[]{:S(2)}, u32[]{:S(2)}) collective-permute-start(bf16[192,256]{1,0:T(8,128)(2,1)S(1)} %get-tuple-element.105), channel_id=1, source_target_pairs={{0,6},{1,7},{2,0},{3,1},{4,2},{5,3},{6,4},{7,5},{8,14},{9,15},{10,... | collective-permute-start | bytes 294920 | tf_op jit(solution)/shard_map/ppermute | solution.py:816
  98.9 6.1 %collective-permute-start.18 = (bf16[256,5376]{1,0:T(8,128)(2,1)S(1)}, bf16[256,5376]{1,0:T(8,128)(2,1)S(1)}, u32[]{:S(2)}, u32[]{:S(2)}) collective-permute-start(bf16[256,5376]{1,0:T(8,128)(2,1)S(1)} %get-tuple-element.114.refs_0_.refs_2_), channel_id=1, source_target_pairs={{0,1},{1,0},{2,3},{3,2},{4,5},{5,4},{6,7},{7,6},{8,9},{9,8},{10,11... | collective-permute-start | bytes 8257544 | tf_op jit(solution)/shard_map/ppermute | solution.py:820
  100.4 4.6 %collective-permute-start.19 = (bf16[784,256]{1,0:T(8,128)(2,1)S(1)}, bf16[784,256]{1,0:T(8,128)(2,1)S(1)}, u32[]{:S(2)}, u32[]{:S(2)}) collective-permute-start(bf16[784,256]{1,0:T(8,128)(2,1)S(1)} %get-tuple-element.117), channel_id=1, source_target_pairs={{0,1},{1,0},{2,3},{3,2},{4,5},{5,4},{6,7},{7,6},{8,9},{9,8},{10,11... | collective-permute-start | bytes 1204232 | tf_op jit(solution)/shard_map/ppermute | solution.py:820
  100.9 14.3 %collective-permute-start.15 = (bf16[192,256]{1,0:T(8,128)(2,1)S(1)}, bf16[192,256]{1,0:T(8,128)(2,1)S(1)}, u32[]{:S(2)}, u32[]{:S(2)}) collective-permute-start(bf16[192,256]{1,0:T(8,128)(2,1)S(1)} %get-tuple-element.108), channel_id=1, source_target_pairs={{0,6},{1,7},{2,0},{3,1},{4,2},{5,3},{6,4},{7,5},{8,14},{9,15},{10,... | collective-permute-start | bytes 294920 | tf_op jit(solution)/shard_map/ppermute | solution.py:816
  101.0 14.3 %collective-permute-start.16 = (bf16[192,256]{1,0:T(8,128)(2,1)S(1)}, bf16[192,256]{1,0:T(8,128)(2,1)S(1)}, u32[]{:S(2)}, u32[]{:S(2)}) collective-permute-start(bf16[192,256]{1,0:T(8,128)(2,1)S(1)} %get-tuple-element.109), channel_id=1, source_target_pairs={{0,4},{1,5},{2,6},{3,7},{4,0},{5,1},{6,2},{7,3},{8,12},{9,13},{10,... | collective-permute-start | bytes 294920 | tf_op jit(solution)/shard_map/ppermute | solution.py:816
  102.1 13.2 %collective-permute-start.17 = (bf16[192,256]{1,0:T(8,128)(2,1)S(1)}, bf16[192,256]{1,0:T(8,128)(2,1)S(1)}, u32[]{:S(2)}, u32[]{:S(2)}) collective-permute-start(bf16[192,256]{1,0:T(8,128)(2,1)S(1)} %get-tuple-element.110), channel_id=1, source_target_pairs={{0,2},{1,3},{2,4},{3,5},{4,6},{5,7},{6,0},{7,1},{8,10},{9,11},{10,... | collective-permute-start | bytes 294920 | tf_op jit(solution)/shard_map/ppermute | solution.py:816
  116.6 4.2 %collective-permute-start.20 = (f32[3,80,128]{2,1,0:T(8,128)S(1)}, f32[3,80,128]{2,1,0:T(8,128)S(1)}, u32[]{:S(2)}, u32[]{:S(2)}) collective-permute-start(f32[3,80,128]{2,1,0:T(8,128)S(1)} %sums.1.refs_7_), channel_id=1, source_target_pairs={{0,1},{1,0},{2,3},{3,2},{4,5},{5,4},{6,7},{7,6},{8,9},{9,8},{10,11... | collective-permute-start | bytes 368648 | tf_op jit(solution)/shard_map/ppermute | solution.py:820
  116.7 24.8 %collective-permute-start.21 = (bf16[1,4,64,768]{3,2,1,0:T(8,128)(2,1)S(1)}, bf16[1,4,64,768]{3,2,1,0:T(8,128)(2,1)S(1)}, u32[]{:S(2)}, u32[]{:S(2)}) collective-permute-start(bf16[1,4,64,768]{3,2,1,0:T(8,128)(2,1)S(1)} %get-tuple-element.123), channel_id=1, source_target_pairs={{0,8},{8,0},{16,24},{24,16},{1,9},{9,1},{17,25},{25,17},{2,10},{10... | collective-permute-start | bytes 1179656 | tf_op jit(solution)/shard_map/ppermute | solution.py:823
  118.2 24.8 %collective-permute-start.22 = (bf16[1,4,112,768]{3,2,1,0:T(8,128)(2,1)S(1)}, bf16[1,4,112,768]{3,2,1,0:T(8,128)(2,1)S(1)}, u32[]{:S(2)}, u32[]{:S(2)}) collective-permute-start(bf16[1,4,112,768]{3,2,1,0:T(8,128)(2,1)S(1)} %get-tuple-element.124), channel_id=1, source_target_pairs={{0,8},{8,0},{16,24},{24,16},{1,9},{9,1},{17,25},{25,17},{2,10},{10... | collective-permute-start | bytes 2064392 | tf_op jit(solution)/shard_map/ppermute | solution.py:823
  118.8 22.7 %collective-permute-start.23 = (bf16[1,4,64,768]{3,2,1,0:T(8,128)(2,1)S(1)}, bf16[1,4,64,768]{3,2,1,0:T(8,128)(2,1)S(1)}, u32[]{:S(2)}, u32[]{:S(2)}) collective-permute-start(bf16[1,4,64,768]{3,2,1,0:T(8,128)(2,1)S(1)} %get-tuple-element.125), channel_id=1, source_target_pairs={{0,16},{8,24},{16,0},{24,8},{1,17},{9,25},{17,1},{25,9},{2,18},{10... | collective-permute-start | bytes 1179656 | tf_op jit(solution)/shard_map/ppermute | solution.py:823
  120.3 24.2 %collective-permute-start.24 = (bf16[1,4,112,768]{3,2,1,0:T(8,128)(2,1)S(1)}, bf16[1,4,112,768]{3,2,1,0:T(8,128)(2,1)S(1)}, u32[]{:S(2)}, u32[]{:S(2)}) collective-permute-start(bf16[1,4,112,768]{3,2,1,0:T(8,128)(2,1)S(1)} %get-tuple-element.126), channel_id=1, source_target_pairs={{0,16},{8,24},{16,0},{24,8},{1,17},{9,25},{17,1},{25,9},{2,18},{10... | collective-permute-start | bytes 2064392 | tf_op jit(solution)/shard_map/ppermute | solution.py:823
  144.5 2.3 collective-permute-start.25
  149.1 2.4 collective-permute-start.29
  152.0 33.5 %collective-permute-start.30 = (bf16[4,192,768]{2,1,0:T(8,128)(2,1)S(1)}, bf16[4,192,768]{2,1,0:T(8,128)(2,1)S(1)}, u32[]{:S(2)}, u32[]{:S(2)}) collective-permute-start(bf16[4,192,768]{2,1,0:T(8,128)(2,1)S(1)} %get-tuple-element.138), channel_id=1, source_target_pairs={{0,16},{8,24},{16,0},{24,8},{1,17},{9,25},{17,1},{25,9},{2,18},{10... | collective-permute-start | bytes 3538952 | tf_op jit(solution)/shard_map/ppermute | solution.py:823
  153.5 31.9 %collective-permute-start.31 = (bf16[4,192,768]{2,1,0:T(8,128)(2,1)S(1)}, bf16[4,192,768]{2,1,0:T(8,128)(2,1)S(1)}, u32[]{:S(2)}, u32[]{:S(2)}) collective-permute-start(bf16[4,192,768]{2,1,0:T(8,128)(2,1)S(1)} %get-tuple-element.139), channel_id=1, source_target_pairs={{0,8},{8,0},{16,24},{24,16},{1,9},{9,1},{17,25},{25,17},{2,10},{10... | collective-permute-start | bytes 3538952 | tf_op jit(solution)/shard_map/ppermute | solution.py:823
  155.0 9.9 %collective-permute-start.26 = (bf16[3,192,256]{2,1,0:T(8,128)(2,1)S(1)}, bf16[3,192,256]{2,1,0:T(8,128)(2,1)S(1)}, u32[]{:S(2)}, u32[]{:S(2)}) collective-permute-start(bf16[3,192,256]{2,1,0:T(8,128)(2,1)S(1)} %get-tuple-element.130), channel_id=1, source_target_pairs={{0,2},{1,3},{2,4},{3,5},{4,6},{5,7},{6,0},{7,1},{8,10},{9,11},{10,... | collective-permute-start | bytes 884744 | tf_op jit(solution)/shard_map/ppermute | solution.py:816
  155.0 25.2 %collective-permute-start.27 = (bf16[3,192,256]{2,1,0:T(8,128)(2,1)S(1)}, bf16[3,192,256]{2,1,0:T(8,128)(2,1)S(1)}, u32[]{:S(2)}, u32[]{:S(2)}) collective-permute-start(bf16[3,192,256]{2,1,0:T(8,128)(2,1)S(1)} %get-tuple-element.131), channel_id=1, source_target_pairs={{0,4},{1,5},{2,6},{3,7},{4,0},{5,1},{6,2},{7,3},{8,12},{9,13},{10,... | collective-permute-start | bytes 884744 | tf_op jit(solution)/shard_map/ppermute | solution.py:816
  157.0 25.6 %collective-permute-start.28 = (bf16[3,192,256]{2,1,0:T(8,128)(2,1)S(1)}, bf16[3,192,256]{2,1,0:T(8,128)(2,1)S(1)}, u32[]{:S(2)}, u32[]{:S(2)}) collective-permute-start(bf16[3,192,256]{2,1,0:T(8,128)(2,1)S(1)} %get-tuple-element.132), channel_id=1, source_target_pairs={{0,6},{1,7},{2,0},{3,1},{4,2},{5,3},{6,4},{7,5},{8,14},{9,15},{10,... | collective-permute-start | bytes 884744 | tf_op jit(solution)/shard_map/ppermute | solution.py:816
  164.9 20.5 %collective-permute-start.32 = (bf16[4,32,768]{2,1,0:T(8,128)(2,1)S(1)}, bf16[4,32,768]{2,1,0:T(8,128)(2,1)S(1)}, u32[]{:S(2)}, u32[]{:S(2)}) collective-permute-start(bf16[4,32,768]{2,1,0:T(8,128)(2,1)S(1)} %get-tuple-element.140), channel_id=1, source_target_pairs={{0,24},{8,16},{16,8},{24,0},{1,25},{9,17},{17,9},{25,1},{2,26},{10... | collective-permute-start | bytes 589832 | tf_op jit(solution)/shard_map/ppermute | solution.py:823
  187.0 11.8 %collective-permute-start.33 = (bf16[128,768]{1,0:T(8,128)(2,1)S(1)}, bf16[128,768]{1,0:T(8,128)(2,1)S(1)}, u32[]{:S(2)}, u32[]{:S(2)}) collective-permute-start(bf16[128,768]{1,0:T(8,128)(2,1)S(1)} %get-tuple-element.142), channel_id=1, source_target_pairs={{0,2},{1,3},{2,4},{3,5},{4,6},{5,7},{6,0},{7,1},{8,10},{9,11},{10,... | collective-permute-start | bytes 589832 | tf_op jit(solution)/shard_map/ppermute | solution.py:816
  187.0 26.3 %collective-permute-start.34 = (bf16[128,768]{1,0:T(8,128)(2,1)S(1)}, bf16[128,768]{1,0:T(8,128)(2,1)S(1)}, u32[]{:S(2)}, u32[]{:S(2)}) collective-permute-start(bf16[128,768]{1,0:T(8,128)(2,1)S(1)} %get-tuple-element.143), channel_id=1, source_target_pairs={{0,4},{1,5},{2,6},{3,7},{4,0},{5,1},{6,2},{7,3},{8,12},{9,13},{10,... | collective-permute-start | bytes 589832 | tf_op jit(solution)/shard_map/ppermute | solution.py:816
  188.9 25.0 %collective-permute-start.35 = (bf16[128,768]{1,0:T(8,128)(2,1)S(1)}, bf16[128,768]{1,0:T(8,128)(2,1)S(1)}, u32[]{:S(2)}, u32[]{:S(2)}) collective-permute-start(bf16[128,768]{1,0:T(8,128)(2,1)S(1)} %get-tuple-element.144), channel_id=1, source_target_pairs={{0,6},{1,7},{2,0},{3,1},{4,2},{5,3},{6,4},{7,5},{8,14},{9,15},{10,... | collective-permute-start | bytes 589832 | tf_op jit(solution)/shard_map/ppermute | solution.py:816
  198.8 18.9 %collective-permute-start.36 = (bf16[128,768]{1,0:T(8,128)(2,1)S(1)}, bf16[128,768]{1,0:T(8,128)(2,1)S(1)}, u32[]{:S(2)}, u32[]{:S(2)}) collective-permute-start(bf16[128,768]{1,0:T(8,128)(2,1)S(1)} %get-tuple-element.148), channel_id=1, source_target_pairs={{0,2},{1,3},{2,4},{3,5},{4,6},{5,7},{6,0},{7,1},{8,10},{9,11},{10,... | collective-permute-start | bytes 589832 | tf_op jit(solution)/shard_map/ppermute | solution.py:816
  205.7 18.2 %collective-permute-start.40 = (bf16[128,768]{1,0:T(8,128)(2,1)}, bf16[128,768]{1,0:T(8,128)(2,1)S(1)}, u32[]{:S(2)}, u32[]{:S(2)}) collective-permute-start(bf16[128,768]{1,0:T(8,128)(2,1)} %get-tuple-element.150), channel_id=1, source_target_pairs={{0,4},{1,5},{2,6},{3,7},{4,0},{5,1},{6,2},{7,3},{8,12},{9,13},{10,... | collective-permute-start | bytes 589832 | tf_op jit(solution)/shard_map/ppermute | solution.py:816
  205.7 18.2 %collective-permute-start.41 = (bf16[128,768]{1,0:T(8,128)(2,1)}, bf16[128,768]{1,0:T(8,128)(2,1)S(1)}, u32[]{:S(2)}, u32[]{:S(2)}) collective-permute-start(bf16[128,768]{1,0:T(8,128)(2,1)} %get-tuple-element.151), channel_id=1, source_target_pairs={{0,6},{1,7},{2,0},{3,1},{4,2},{5,3},{6,4},{7,5},{8,14},{9,15},{10,... | collective-permute-start | bytes 589832 | tf_op jit(solution)/shard_map/ppermute | solution.py:816
  219.3 5.9 %collective-permute-start.37 = (bf16[128,768]{1,0:T(8,128)(2,1)S(1)}, bf16[128,768]{1,0:T(8,128)(2,1)S(1)}, u32[]{:S(2)}, u32[]{:S(2)}) collective-permute-start(bf16[128,768]{1,0:T(8,128)(2,1)S(1)} %fourth.2.refs_5_.refs_0_), channel_id=1, source_target_pairs={{0,8},{8,0},{16,24},{24,16},{1,9},{9,1},{17,25},{25,17},{2,10},{10... | collective-permute-start | bytes 589832 | tf_op jit(solution)/shard_map/ppermute | solution.py:823
  220.8 6.9 %collective-permute-start.38 = (bf16[128,768]{1,0:T(8,128)(2,1)S(1)}, bf16[128,768]{1,0:T(8,128)(2,1)S(1)}, u32[]{:S(2)}, u32[]{:S(2)}) collective-permute-start(bf16[128,768]{1,0:T(8,128)(2,1)S(1)} %fourth.2.refs_5_.refs_0_), channel_id=1, source_target_pairs={{0,16},{8,24},{16,0},{24,8},{1,17},{9,25},{17,1},{25,9},{2,18},{10... | collective-permute-start | bytes 589832 | tf_op jit(solution)/shard_map/ppermute | solution.py:823
  222.4 6.6 %collective-permute-start.39 = (bf16[128,768]{1,0:T(8,128)(2,1)S(1)}, bf16[128,768]{1,0:T(8,128)(2,1)S(1)}, u32[]{:S(2)}, u32[]{:S(2)}) collective-permute-start(bf16[128,768]{1,0:T(8,128)(2,1)S(1)} %fourth.2.refs_5_.refs_0_), channel_id=1, source_target_pairs={{0,24},{8,16},{16,8},{24,0},{1,25},{9,17},{17,9},{25,1},{2,26},{10... | collective-permute-start | bytes 589832 | tf_op jit(solution)/shard_map/ppermute | solution.py:823
  230.6 7.1 %collective-permute-start.42 = (bf16[192,768]{1,0:T(8,128)(2,1)S(1)}, bf16[192,768]{1,0:T(8,128)(2,1)S(1)}, u32[]{:S(2)}, u32[]{:S(2)}) collective-permute-start(bf16[192,768]{1,0:T(8,128)(2,1)S(1)} %fourth.3.refs_4_), channel_id=1, source_target_pairs={{0,8},{8,0},{16,24},{24,16},{1,9},{9,1},{17,25},{25,17},{2,10},{10... | collective-permute-start | bytes 884744 | tf_op jit(solution)/shard_map/ppermute | solution.py:823
  231.3 9.1 %collective-permute-start.43 = (bf16[192,768]{1,0:T(8,128)(2,1)S(1)}, bf16[192,768]{1,0:T(8,128)(2,1)S(1)}, u32[]{:S(2)}, u32[]{:S(2)}) collective-permute-start(bf16[192,768]{1,0:T(8,128)(2,1)S(1)} %fourth.3.refs_4_), channel_id=1, source_target_pairs={{0,16},{8,24},{16,0},{24,8},{1,17},{9,25},{17,1},{25,9},{2,18},{10... | collective-permute-start | bytes 884744 | tf_op jit(solution)/shard_map/ppermute | solution.py:823
  232.4 9.6 %collective-permute-start.44 = (bf16[192,768]{1,0:T(8,128)(2,1)S(1)}, bf16[192,768]{1,0:T(8,128)(2,1)S(1)}, u32[]{:S(2)}, u32[]{:S(2)}) collective-permute-start(bf16[192,768]{1,0:T(8,128)(2,1)S(1)} %fourth.3.refs_4_), channel_id=1, source_target_pairs={{0,24},{8,16},{16,8},{24,0},{1,25},{9,17},{17,9},{25,1},{2,26},{10... | collective-permute-start | bytes 884744 | tf_op jit(solution)/shard_map/ppermute | solution.py:823
  (21 other events, 103.1 us)

commit v9 on v8

--- a/solution.py
+++ b/solution.py
@@ -584,19 +584,20 @@
     rows, lines = keep_u.shape[2], inner.shape[2]
     to_y[:, :rows] = (keep_u[0].astype(F32) + got_u[0].astype(F32)).astype(BF)
     to_x[:, :rows] = (keep_d[0].astype(F32) + got_d[0].astype(F32)).astype(BF)
-    to_y[:, rows : rows + lines] = (inner[1].astype(F32) + inner_got[1].astype(F32)).astype(BF)
-    to_x[:, rows : rows + lines] = (inner[2].astype(F32) + inner_got[2].astype(F32)).astype(BF)
+    last = to_y.shape[1] - lines
+    to_y[:, last:] = (inner[1].astype(F32) + inner_got[1].astype(F32)).astype(BF)
+    to_x[:, last:] = (inner[2].astype(F32) + inner_got[2].astype(F32)).astype(BF)
     to_xy[...] = (inner[3].astype(F32) + inner_got[3].astype(F32)).astype(BF)
-    to_y[:, rows + lines :] = late_d[0]
-    to_x[:, rows + lines :] = late_u[0]
+    to_y[:, rows:last] = late_d[0]
+    to_x[:, rows:last] = late_u[0]
 
 
 def third_kernel(info, keep_u, one_u, keep_d, one_d, by_y, by_x, inner, inner_got, by_xy, *outs):
     rows, lead, lines = keep_u.shape[2], one_u.shape[2], inner.shape[2]
     groups = len(outs) // 2
     left = rows - lead
-    head, tail, late = slice(0, lead), slice(lead, rows), slice(rows + lines, None)
-    mid = slice(rows, rows + lines)
+    head, tail, late = slice(0, lead), slice(lead, rows), slice(rows, rows + left)
+    mid = slice(rows + left, None)
 
     def added(keep, got, by, group, spot):
         total = keep[0, group, spot].astype(F32) + got.astype(F32)
@@ -623,16 +624,17 @@
         return
     turned = refs[groups + 1]
     third = feats // 3
-    lines = turned.shape[1]
     for group in range(groups):
         turned[group] = parts[group][2 * high :].astype(F32)
+    spots = [lax.rem(info[0] + groups - owner, groups) for owner in range(groups)]
+    found, sums = [], []
     for kind in range(3):
-        found = []
-        for owner in range(groups):
-            spot = lax.rem(info[0] + groups - owner, groups)
-            found.append(turned[spot, :, kind * third : (kind + 1) * third])
-        at = 2 * high + kind * lines
-        out[at : at + lines] = jnp.concatenate(found, axis=1).astype(BF)
+        lanes = slice(kind * third, (kind + 1) * third)
+        found.append(jnp.concatenate([turned[spot, :, lanes] for spot in spots], axis=1))
+        line = [turned[spot, 8 * kind : 8 * kind + 8, 3 * third :] for spot in spots]
+        sums.append(jnp.concatenate(line, axis=1)[:1])
+    sums.append(jnp.zeros((5, out.shape[1]), F32))
+    out[2 * high :] = jnp.concatenate(found + sums, axis=0).astype(BF)
 
 
 def spread_kernel(info, *refs, lead, high):
@@ -641,7 +643,6 @@
     index = pl.program_id(0)
     rows, width = down_ref.shape
     quarter = rows // 4
-    lines = quarter + 8
     left = rows - lead
     order_u, order_d = (0, 2, 1, 3), (0, 1, 2, 3)
 
@@ -651,9 +652,7 @@
 
             @pl.when(info[3] == place)
             def take(source=source):
-                for kind in range(3):
-                    at = 2 * high + kind * lines
-                    sums[kind] = lasts[source][at : at + lines].astype(F32)[quarter:]
+                sums[...] = lasts[source][2 * high :].astype(F32)[3 * quarter :]
 
     for place, source in enumerate(order_u):
 
@@ -667,10 +666,10 @@
             spot = pl.ds(at, quarter)
             shift, gain = pair[spot, 0:1], pair[spot, 1:2]
             gain_sum, shift_sum = 0.0, 0.0
+            blocks = part[2 * high :].astype(F32)
             for kind in range(3):
-                base = 2 * high + kind * lines
-                block = part[base : base + lines].astype(F32)[:quarter]
-                line = sums[kind, 0:1]
+                block = blocks[kind * quarter : (kind + 1) * quarter]
+                line = sums[kind : kind + 1]
                 if kind == 0:
                     weight = wq[spot, :]
                     gq_ref[spot, :] = block + shift * line
@@ -722,11 +721,9 @@
     own_ref, far_ref = outs
     block = total.shape[0] // (2 * groups)
     quarter = block // 4
-    wide = total.shape[1]
-    edge = wide // 128 * 128
-    blank = jnp.zeros(own_ref.shape[:3] + (own_ref.shape[3] - edge,), BF)
-    own_ref[..., edge:] = blank
-    far_ref[..., edge:] = blank
+    third = total.shape[1] // 3
+    more = [sums[:8, kind * third : (kind + 1) * third] for kind in range(3)]
+    more = jnp.concatenate(more, axis=0)
     for group in range(groups):
         spot = lax.rem(group + groups - info[0], groups)
         for part in range(4):
@@ -734,10 +731,10 @@
             found = []
             for parity in range(2):
                 at = (2 * group + parity) * block + part * quarter
-                lines = jnp.concatenate([total[at : at + quarter], sums[:8]], axis=0)
+                lines = jnp.concatenate([total[at : at + quarter], more], axis=1)
                 found.append(lines.astype(BF))
-            own_ref[place, spot, :, :wide] = jnp.where(info[1] == 0, found[0], found[1])
-            far_ref[place, spot, :, :wide] = jnp.where(info[1] == 0, found[1], found[0])
+            own_ref[place, spot] = jnp.where(info[1] == 0, found[0], found[1])
+            far_ref[place, spot] = jnp.where(info[1] == 0, found[1], found[0])
 
 
 def final_kernel(info, *refs, groups):
@@ -887,7 +884,6 @@
         8,
         cost(1e5, 1e6),
         "table",
-        first=w_in,
     )(info, *arrived)
     tables = [table] + [along_peers(table, -hop) for hop in range(1, peers)]
     cot_got = [along_peers(after(cotangent, arrived), hop) for hop in range(1, peers)]
@@ -1003,7 +999,7 @@
 
     chunks = 4
     part = hidden // chunks
-    lead = 64
+    lead = 80
     w_out_g = w_out.reshape(groups, feats, width)
     gain_row2, shift_row2 = gain_two[None, :], shift_two[None, :]
     square = whole((rows, width))
@@ -1130,7 +1126,7 @@
         )(info, keep_u, got_u, keep_d, got_d, by_y, by_x, inner, inner_got, by_xy)
 
     def weight_fourth(came, high, lines, first):
-        tall = 2 * high + 3 * lines
+        tall = 2 * high + (3 * lines + 8 if lines else 0)
         done = prefetched(
             functools.partial(fourth_kernel, groups=groups, high=high, feats=3 * feats),
             (1,),
@@ -1177,7 +1173,7 @@
             20,
             cost(1e6, 8 * block_rows * width * 6),
             "spread",
-            scratch=[pltpu.VMEM((3, 8, width), F32)],
+            scratch=[pltpu.VMEM((8, width), F32)],
         )(info, *firsts, *lasts, wq_rows, wkv_rows, pair)
 
     masks = [1 << k for k in range(n_dp.bit_length() - 1)]
@@ -1268,7 +1264,7 @@
     tall = block_rows + 16
     spent = cost(2 * own_rows * width * 3 * feats, 4e6)
     if fast:
-        lines = block_rows // 4 + 8
+        lines = block_rows // 4
         more = [array((4, groups, lines, width), BF)] * 2
     else:
         more = [array((width, 3 * feats), F32), array((16, 3 * feats), F32)]

time: 248 us -> 238 us (0.960)
  Pallas kernels: 87.2 us -> 79.6 us
  waiting for transfers between devices: 84.5 us -> 89.5 us
  local copies, waits for them, and re-layouts: 22 us -> 17.4 us
    ppermute x21, waiting for transfers between devices: 61.2 us -> 70.3 us  [along_groups(): return lax.ppermute(values, 'wide', pairs)]
    pallas_call x15, Pallas kernels: 52.6 us -> 45.2 us  [prefetched(): return lambda *inputs: call(*inputs, *first)]
    ppermute x13, waiting for transfers between devices: 17.5 us -> 12.7 us  [along_dp(): return lax.ppermute(values, 'dp', [(i, i ^ mask) for i in range(n_dp)])]
    unnamed x51 -> x27, local copies, waits for them, and re-layouts: 16.3 us -> 12.5 us
  transfers between devices with their start and end apart: 45 -> 45, of which waited for: 24 -> 21; matrix products, arithmetic and copies ran while one was open for 5% -> 6% of each run, Pallas kernels for 20% -> 19%
where the time goes in v9:
time: 238 us
  waiting for transfers between devices  89.5 us (38%)
  Pallas kernels  79.6 us (33%)
  starting transfers between devices  44.6 us (19%)
  local copies, waits for them, and re-layouts  17.4 us (7%)
  other arithmetic  4.9 us (2%)
    ppermute x21, waiting for transfers between devices, along_groups(): return lax.ppermute(values, 'wide', pairs)  70.3 us
    pallas_call x15, Pallas kernels, prefetched(): return lambda *inputs: call(*inputs, *first)  45.2 us
    ppermute x21, starting transfers between devices, along_groups(): return lax.ppermute(values, 'wide', pairs)  28.2 us
    pallas_call x1, Pallas kernels, per_device(): pl.pallas_call(functools.partial(back_kernel, size=size, groups=groups, g...  20.6 us
    ppermute x13, starting transfers between devices, along_dp(): return lax.ppermute(values, 'dp', [(i, i ^ mask) for i in range(n_dp)])  14.7 us
    pallas_call x1, Pallas kernels, per_device(): pl.pallas_call(functools.partial(forward_kernel, size=size, groups=groups...  13.4 us
    ppermute x13, waiting for transfers between devices, along_dp(): return lax.ppermute(values, 'dp', [(i, i ^ mask) for i in range(n_dp)])  12.7 us
    unnamed x27, local copies, waits for them, and re-layouts  12.5 us
  transfers between devices with their start and end apart: 45, of which 21 were waited for; matrix products, arithmetic and copies ran while one was open for 6% of the time, Pallas kernels for 19%

profile of v9, /device:TPU:8, one launch (start us, length us, event | category | flops | bytes accessed | tf_op | source)
XLA Modules:
  0.0 237.9 jit_solution(16472044224929957550)
XLA Ops:
  3.3 2.1 dynamic_update_slice.3
  5.5 3.0 %collective-permute-start.2 = (s32[3,34,128]{2,1,0:T(8,128)S(1)}, s32[3,34,128]{2,1,0:T(8,128)S(1)}, u32[]{:S(2)}, u32[]{:S(2)}) collective-permute-start(s32[3,34,128]{2,1,0:T(8,128)S(1)} %get-tuple-element.162), channel_id=1, source_target_pairs={{0,4},{1,5},{2,6},{3,7},{4,0},{5,1},{6,2},{7,3},{8,12},{9,13},{10,... | collective-permute-start | bytes 156680 | tf_op jit(solution)/shard_map/ppermute | solution.py:813
  8.5 2.5 %collective-permute-start.3 = (s32[3,34,128]{2,1,0:T(8,128)S(1)}, s32[3,34,128]{2,1,0:T(8,128)S(1)}, u32[]{:S(2)}, u32[]{:S(2)}) collective-permute-start(s32[3,34,128]{2,1,0:T(8,128)S(1)} %get-tuple-element.161), channel_id=1, source_target_pairs={{0,2},{1,3},{2,4},{3,5},{4,6},{5,7},{6,0},{7,1},{8,10},{9,11},{10,... | collective-permute-start | bytes 156680 | tf_op jit(solution)/shard_map/ppermute | solution.py:813
  11.0 2.0 collective-permute-start.9
  13.0 4.3 %copy.50 = bf16[768,1536]{0,1:T(8,128)(2,1)} copy(bf16[768,1536]{1,0:T(8,128)(2,1)} %param.21) | data formatting | bytes 4718592 | tf_op args[7]
  17.3 2.4 %copy.49 = bf16[768,768]{0,1:T(8,128)(2,1)} copy(bf16[768,768]{1,0:T(8,128)(2,1)} %param.20) | data formatting | bytes 2359296 | tf_op args[6]
  21.7 2.2 pad_maximum_fusion
  24.2 1.7 project.4
  25.9 7.6 %bias.1 = (bf16[3,2048,128]{2,1,0:T(8,128)(2,1)S(1)}, s32[3,1,2048]{2,1,0:T(1,128)S(1)}) custom-call(s32[6]{0:T(128)S(1)} %stack.38.info.refs_0_, s32[3,40,128]{2,1,0:T(8,128)S(1)} %table.1.refs_0_, s32[3,40,128]{2,1,0:T(8,128)S(1)} %collective-permute-done.4.refs_1_), custom_call_target="tpu_custom_call" | custom-call | flops 201326592 | bytes 1572864 | tf_op jit(solution)/shard_map/bias/pallas_call | solution.py:841
  33.5 6.6 %collective-permute-done.7.refs_0_ = bf16[256,768]{1,0:T(8,128)(2,1)S(1)} collective-permute-done((bf16[256,768]{1,0:T(8,128)(2,1)}, bf16[256,768]{1,0:T(8,128)(2,1)S(1)}, u32[]{:S(2)}, u32[]{:S(2)}) %collective-permute-start.7) | collective-permute-done | bytes 393248 | tf_op jit(solution)/shard_map/ppermute | solution.py:813
  40.5 7.4 %collective-permute-done.5.refs_0_ = bf16[256,768]{1,0:T(8,128)(2,1)S(1)} collective-permute-done((bf16[256,768]{1,0:T(8,128)(2,1)S(1)}, bf16[256,768]{1,0:T(8,128)(2,1)S(1)}, u32[]{:S(2)}, u32[]{:S(2)}) %collective-permute-start.5) | collective-permute-done | bytes 393248 | tf_op jit(solution)/shard_map/ppermute | solution.py:813
  49.6 1.7 project.5
  51.4 1.7 project.6
  53.1 1.7 project.7
  54.9 13.4 %attend.1 = (bf16[192,256]{1,0:T(8,128)(2,1)S(1)}, bf16[192,256]{1,0:T(8,128)(2,1)S(1)}, bf16[192,256]{1,0:T(8,128)(2,1)S(1)}, bf16[192,256]{1,0:T(8,128)(2,1)S(...) custom-call(s32[3,1,2048]{2,1,0:T(1,128)S(1)} %get-tuple-element.86.ids_all.refs_1_, ...), custom_call_target="tpu_custom_call" | custom-call | flops 9663676416 | bytes 8000000 | tf_op jit(solution)/shard_map/attend/pallas_call | solution.py:980
  68.6 4.3 %collective-permute-start.13 = (bf16[192,256]{1,0:T(8,128)(2,1)S(1)}, bf16[192,256]{1,0:T(8,128)(2,1)S(1)}, u32[]{:S(2)}, u32[]{:S(2)}) collective-permute-start(bf16[192,256]{1,0:T(8,128)(2,1)S(1)} %get-tuple-element.104), channel_id=1, source_target_pairs={{0,4},{1,5},{2,6},{3,7},{4,0},{5,1},{6,2},{7,3},{8,12},{9,13},{10,... | collective-permute-start | bytes 294920 | tf_op jit(solution)/shard_map/ppermute | solution.py:813
  73.8 5.4 %collective-permute-done.13.refs_2_ = bf16[192,256]{1,0:T(8,128)(2,1)S(1)} collective-permute-done((bf16[192,256]{1,0:T(8,128)(2,1)S(1)}, bf16[192,256]{1,0:T(8,128)(2,1)S(1)}, u32[]{:S(2)}, u32[]{:S(2)}) %collective-permute-start.13) | collective-permute-done | bytes 98336 | tf_op jit(solution)/shard_map/ppermute | solution.py:813
  79.2 2.2 collective-permute-done.14.refs_3_
  81.4 2.3 copy-done.2
  83.8 2.3 copy-done.3
  86.1 10.0 %feed.1 = (bf16[256,768]{1,0:T(8,128)(2,1)}, f32[256,768]{1,0:T(8,128)S(1)}, bf16[256,5376]{1,0:T(8,128)(2,1)S(1)}, bf16[784,256]{1,0:T(8,128)(2,1)S(1)}, bf16[2...) custom-call(s32[6]{0:T(128)S(1)} %stack.38.info.refs_0_, ...), custom_call_target="tpu_custom_call" | custom-call | flops 4831838208 | bytes 9437184 | tf_op jit(solution)/shard_map/feed/pallas_call | solution.py:841
  97.8 2.9 %collective-permute-start.17 = (bf16[192,256]{1,0:T(8,128)(2,1)S(1)}, bf16[192,256]{1,0:T(8,128)(2,1)S(1)}, u32[]{:S(2)}, u32[]{:S(2)}) collective-permute-start(bf16[192,256]{1,0:T(8,128)(2,1)S(1)} %get-tuple-element.110), channel_id=1, source_target_pairs={{0,2},{1,3},{2,4},{3,5},{4,6},{5,7},{6,0},{7,1},{8,10},{9,11},{10,... | collective-permute-start | bytes 294920 | tf_op jit(solution)/shard_map/ppermute | solution.py:813
  101.8 7.4 %weights.1 = (bf16[1,4,80,768]{3,2,1,0:T(8,128)(2,1)S(1)}, bf16[1,4,32,768]{3,2,1,0:T(8,128)(2,1)S(1)}, bf16[1,4,112,768]{3,2,1,0:T(8,128)(2,1)S(1)}, bf16[2,4,1...) custom-call(s32[6]{0:T(128)S(1)} %stack.38.info.refs_0_, ...), custom_call_target="tpu_custom_call" | custom-call | flops 4831838208 | bytes 14155776 | tf_op jit(solution)/shard_map/weights/pallas_call | solution.py:841
  110.8 1.5 collective-permute-start.21
  112.9 1.5 collective-permute-start.23
  114.9 20.6 %back.1 = (bf16[4,192,256]{2,1,0:T(8,128)(2,1)S(1)}, f32[3,128,1024]{2,1,0:T(8,128)S(1)}, bf16[3,128,1024]{2,1,0:T(8,128)(2,1)S(1)}) custom-call(s32[3,1,2048]{2,1,0:T(1,128)S(1)} %get-tuple-element.86.ids_all.refs_1_, bf16[3,192,2048]{2,1,0:T(8,128)(2,1)S(1)} %get-tuple-element.100.feat, bf16[3,2048,128]{2,1,0:T(8,128)(2,1)S(1)} %get-tuple-element.101.kv, ...), custom_call_target="tpu_custom_call" | custom-call | flops 22548578304 | bytes 10000000 | tf_op jit(solution)/shard_map/back/pallas_call | solution.py:1238
  135.5 3.6 %collective-permute-done.22.got_u = bf16[1,4,112,768]{3,2,1,0:T(8,128)(2,1)S(1)} collective-permute-done((bf16[1,4,112,768]{3,2,1,0:T(8,128)(2,1)S(1)}, bf16[1,4,112,768]{3,2,1,0:T(8,128)(2,1)S(1)}, u32[]{:S(2)}, u32[]{:S(2)}) %collective-permute-start.22) | collective-permute-done | bytes 688160 | tf_op jit(solution)/shard_map/ppermute | solution.py:820
  140.5 2.3 collective-permute-done.25.refs_2_
  142.8 2.5 %inward.1 = (bf16[3,192,256]{2,1,0:T(8,128)(2,1)S(1)}, bf16[3,192,256]{2,1,0:T(8,128)(2,1)S(1)}, bf16[3,192,256]{2,1,0:T(8,128)(2,1)S(1)}, bf16[3,192,256]{2,1,0...) custom-call(s32[6]{0:T(128)S(1)} %stack.38.info.refs_0_, ...), custom_call_target="tpu_custom_call" | custom-call | flops 905969664 | bytes 4000000 | tf_op jit(solution)/shard_map/inward/pallas_call | solution.py:841
  145.5 1.9 collective-permute-done.29.inner_got.refs_8_
  147.8 1.6 collective-permute-start.30
  149.4 1.5 collective-permute-start.31
  150.9 2.4 collective-permute-start.27
  154.0 6.8 %collective-permute-done.26.refs_1_.refs_11_ = bf16[3,192,256]{2,1,0:T(8,128)(2,1)S(1)} collective-permute-done((bf16[3,192,256]{2,1,0:T(8,128)(2,1)S(1)}, bf16[3,192,256]{2,1,0:T(8,128)(2,1)S(1)}, u32[]{:S(2)}, u32[]{:S(2)}) %collective-permute-start.26) | collective-permute-done | bytes 294944 | tf_op jit(solution)/shard_map/ppermute | solution.py:813
  161.3 14.8 %collective-permute-done.27.refs_2_.refs_12_ = bf16[3,192,256]{2,1,0:T(8,128)(2,1)S(1)} collective-permute-done((bf16[3,192,256]{2,1,0:T(8,128)(2,1)S(1)}, bf16[3,192,256]{2,1,0:T(8,128)(2,1)S(1)}, u32[]{:S(2)}, u32[]{:S(2)}) %collective-permute-start.27) | collective-permute-done | bytes 294944 | tf_op jit(solution)/shard_map/ppermute | solution.py:813
  176.1 2.6 %collective-permute-done.28.refs_3_.refs_13_ = bf16[3,192,256]{2,1,0:T(8,128)(2,1)S(1)} collective-permute-done((bf16[3,192,256]{2,1,0:T(8,128)(2,1)S(1)}, bf16[3,192,256]{2,1,0:T(8,128)(2,1)S(1)}, u32[]{:S(2)}, u32[]{:S(2)}) %collective-permute-start.28) | collective-permute-done | bytes 294944 | tf_op jit(solution)/shard_map/ppermute | solution.py:813
  180.8 1.9 collective-permute-start.35
  182.8 6.0 %collective-permute-done.33.refs_2_ = bf16[160,768]{1,0:T(8,128)(2,1)S(1)} collective-permute-done((bf16[160,768]{1,0:T(8,128)(2,1)S(1)}, bf16[160,768]{1,0:T(8,128)(2,1)S(1)}, u32[]{:S(2)}, u32[]{:S(2)}) %collective-permute-start.33) | collective-permute-done | bytes 245792 | tf_op jit(solution)/shard_map/ppermute | solution.py:813
  189.1 3.0 %final.1.refs_6_ = bf16[256,768]{1,0:T(8,128)(2,1)} custom-call(s32[6]{0:T(128)S(1)} %stack.38.info.refs_0_, bf16[3,192,256]{2,1,0:T(8,128)(2,1)S(1)} %get-tuple-element.129.refs_0_.refs_10_, bf16[3,192,256]{2,1,0:T(8,128)(2,1)S(1)} %collective-permute-done.26.refs_1_.refs_11_, bf16[3,192,256]{2,1,0:T(8,128)(2,1)S(1)} %collective-permute-done.27.refs_2_.refs_12_, ...), custom_call_target="tpu_custom_call" | custom-call | flops 905969664 | bytes 3538944 | tf_op jit(solution)/shard_map/final/pallas_call | solution.py:841
  192.1 10.0 %collective-permute-done.34.refs_3_ = bf16[160,768]{1,0:T(8,128)(2,1)S(1)} collective-permute-done((bf16[160,768]{1,0:T(8,128)(2,1)S(1)}, bf16[160,768]{1,0:T(8,128)(2,1)S(1)}, u32[]{:S(2)}, u32[]{:S(2)}) %collective-permute-start.34) | collective-permute-done | bytes 245792 | tf_op jit(solution)/shard_map/ppermute | solution.py:813
  202.0 2.5 %collective-permute-done.35.refs_4_ = bf16[160,768]{1,0:T(8,128)(2,1)S(1)} collective-permute-done((bf16[160,768]{1,0:T(8,128)(2,1)S(1)}, bf16[160,768]{1,0:T(8,128)(2,1)S(1)}, u32[]{:S(2)}, u32[]{:S(2)}) %collective-permute-start.35) | collective-permute-done | bytes 245792 | tf_op jit(solution)/shard_map/ppermute | solution.py:813
  207.4 1.5 collective-permute-start.38
  210.8 2.8 %collective-permute-start.41 = (bf16[88,768]{1,0:T(8,128)(2,1)S(1)}, bf16[88,768]{1,0:T(8,128)(2,1)S(1)}, u32[]{:S(2)}, u32[]{:S(2)}) collective-permute-start(bf16[88,768]{1,0:T(8,128)(2,1)S(1)} %get-tuple-element.151), channel_id=1, source_target_pairs={{0,6},{1,7},{2,0},{3,1},{4,2},{5,3},{6,4},{7,5},{8,14},{9,15},{10,... | collective-permute-start | bytes 405512 | tf_op jit(solution)/shard_map/ppermute | solution.py:813
  214.7 4.3 %collective-permute-done.40.refs_3_ = bf16[88,768]{1,0:T(8,128)(2,1)S(1)} collective-permute-done((bf16[88,768]{1,0:T(8,128)(2,1)S(1)}, bf16[88,768]{1,0:T(8,128)(2,1)S(1)}, u32[]{:S(2)}, u32[]{:S(2)}) %collective-permute-start.40) | collective-permute-done | bytes 135200 | tf_op jit(solution)/shard_map/ppermute | solution.py:813
  223.1 1.5 collective-permute-start.44
  225.6 3.9 %collective-permute-done.42.refs_5_ = bf16[144,768]{1,0:T(8,128)(2,1)S(1)} collective-permute-done((bf16[144,768]{1,0:T(8,128)(2,1)S(1)}, bf16[144,768]{1,0:T(8,128)(2,1)S(1)}, u32[]{:S(2)}, u32[]{:S(2)}) %collective-permute-start.42) | collective-permute-done | bytes 221216 | tf_op jit(solution)/shard_map/ppermute | solution.py:820
  229.5 3.8 %collective-permute-done.43.refs_6_ = bf16[144,768]{1,0:T(8,128)(2,1)S(1)} collective-permute-done((bf16[144,768]{1,0:T(8,128)(2,1)S(1)}, bf16[144,768]{1,0:T(8,128)(2,1)S(1)}, u32[]{:S(2)}, u32[]{:S(2)}) %collective-permute-start.43) | collective-permute-done | bytes 221216 | tf_op jit(solution)/shard_map/ppermute | solution.py:820
  233.2 3.4 %spread.1 = (f32[96,3072]{1,0:T(8,128)}, f32[96,768]{1,0:T(8,128)}, f32[384,768]{1,0:T(8,128)}, f32[8,768]{1,0:T(8,128)S(1)}, f32[96,768]{1,0:T(8,128)}, /*index=5*/f32[96,1536]{1,0:T(8,128)}, f32[96,128]{1,0:T(8,128)S(1)}) custom-call(s32[6]{0:T(128)S(1)} %stack.38.info.refs_0_, bf16[160,768]{1,0:T(8,128)(2,1)S(1)} %fourth.2.refs_5_.refs_0_, ...), custom_call_target="tpu_custom_call" | custom-call | flops 1000000 | bytes 3538944 | tf_op jit(solution)/shard_map/spread/pallas_call | solution.py:841
  (111 shorter events, 30.6 us)
Async XLA Ops:
  0.6 4.8 %collective-permute-start = (bf16[256,768]{1,0:T(8,128)(2,1)}, bf16[256,768]{1,0:T(8,128)(2,1)S(1)}, u32[]{:S(2)}, u32[]{:S(2)}) collective-permute-start(bf16[256,768]{1,0:T(8,128)(2,1)} %refs_4_.3), channel_id=1, source_target_pairs={{0,1},{1,0},{2,3},{3,2},{4,5},{5,4},{6,7},{7,6},{8,9},{9,8},{10,11... | collective-permute-start | bytes 1179656 | tf_op jit(solution)/shard_map/ppermute | solution.py:817
  5.4 14.4 %collective-permute-start.1 = (s32[3,34,128]{2,1,0:T(8,128)S(1)}, s32[3,34,128]{2,1,0:T(8,128)S(1)}, u32[]{:S(2)}, u32[]{:S(2)}) collective-permute-start(s32[3,34,128]{2,1,0:T(8,128)S(1)} %get-tuple-element.163), channel_id=1, source_target_pairs={{0,6},{1,7},{2,0},{3,1},{4,2},{5,3},{6,4},{7,5},{8,14},{9,15},{10,... | collective-permute-start | bytes 156680 | tf_op jit(solution)/shard_map/ppermute | solution.py:813
  5.5 14.3 %collective-permute-start.2 = (s32[3,34,128]{2,1,0:T(8,128)S(1)}, s32[3,34,128]{2,1,0:T(8,128)S(1)}, u32[]{:S(2)}, u32[]{:S(2)}) collective-permute-start(s32[3,34,128]{2,1,0:T(8,128)S(1)} %get-tuple-element.162), channel_id=1, source_target_pairs={{0,4},{1,5},{2,6},{3,7},{4,0},{5,1},{6,2},{7,3},{8,12},{9,13},{10,... | collective-permute-start | bytes 156680 | tf_op jit(solution)/shard_map/ppermute | solution.py:813
  8.5 11.3 %collective-permute-start.3 = (s32[3,34,128]{2,1,0:T(8,128)S(1)}, s32[3,34,128]{2,1,0:T(8,128)S(1)}, u32[]{:S(2)}, u32[]{:S(2)}) collective-permute-start(s32[3,34,128]{2,1,0:T(8,128)S(1)} %get-tuple-element.161), channel_id=1, source_target_pairs={{0,2},{1,3},{2,4},{3,5},{4,6},{5,7},{6,0},{7,1},{8,10},{9,11},{10,... | collective-permute-start | bytes 156680 | tf_op jit(solution)/shard_map/ppermute | solution.py:813
  11.0 29.1 %collective-permute-start.7 = (bf16[256,768]{1,0:T(8,128)(2,1)}, bf16[256,768]{1,0:T(8,128)(2,1)S(1)}, u32[]{:S(2)}, u32[]{:S(2)}) collective-permute-start(bf16[256,768]{1,0:T(8,128)(2,1)} %refs_4_.3), channel_id=1, source_target_pairs={{0,2},{1,3},{2,4},{3,5},{4,6},{5,7},{6,0},{7,1},{8,10},{9,11},{10,... | collective-permute-start | bytes 1179656 | tf_op jit(solution)/shard_map/ppermute | solution.py:813
  11.0 29.5 %collective-permute-start.9 = (bf16[256,768]{1,0:T(8,128)(2,1)}, bf16[256,768]{1,0:T(8,128)(2,1)S(1)}, u32[]{:S(2)}, u32[]{:S(2)}) collective-permute-start(bf16[256,768]{1,0:T(8,128)(2,1)} %refs_4_.3), channel_id=1, source_target_pairs={{0,6},{1,7},{2,0},{3,1},{4,2},{5,3},{6,4},{7,5},{8,14},{9,15},{10,... | collective-permute-start | bytes 1179656 | tf_op jit(solution)/shard_map/ppermute | solution.py:813
  20.4 5.4 %collective-permute-start.4 = (s32[3,40,128]{2,1,0:T(8,128)S(1)}, s32[3,40,128]{2,1,0:T(8,128)S(1)}, u32[]{:S(2)}, u32[]{:S(2)}) collective-permute-start(s32[3,40,128]{2,1,0:T(8,128)S(1)} %table.1.refs_0_), channel_id=1, source_target_pairs={{0,1},{1,0},{2,3},{3,2},{4,5},{5,4},{6,7},{7,6},{8,9},{9,8},{10,11... | collective-permute-start | bytes 184328 | tf_op jit(solution)/shard_map/ppermute | solution.py:817
  20.5 27.4 %collective-permute-start.5 = (bf16[256,768]{1,0:T(8,128)(2,1)S(1)}, bf16[256,768]{1,0:T(8,128)(2,1)S(1)}, u32[]{:S(2)}, u32[]{:S(2)}) collective-permute-start(bf16[256,768]{1,0:T(8,128)(2,1)S(1)} %copy-done), channel_id=1, source_target_pairs={{0,4},{1,5},{2,6},{3,7},{4,0},{5,1},{6,2},{7,3},{8,12},{9,13},{10,... | collective-permute-start | bytes 1179656 | tf_op jit(solution)/shard_map/ppermute | solution.py:813
  21.5 26.4 %collective-permute-start.10 = (bf16[256,768]{1,0:T(8,128)(2,1)S(1)}, bf16[256,768]{1,0:T(8,128)(2,1)S(1)}, u32[]{:S(2)}, u32[]{:S(2)}) collective-permute-start(bf16[256,768]{1,0:T(8,128)(2,1)S(1)} %copy-done.5), channel_id=1, source_target_pairs={{0,1},{1,0},{2,3},{3,2},{4,5},{5,4},{6,7},{7,6},{8,9},{9,8},{10,11... | collective-permute-start | bytes 1179656 | tf_op jit(solution)/shard_map/ppermute | solution.py:817
  33.5 21.3 %copy-start.6 = (bf16[3,2048,128]{2,1,0:T(8,128)(2,1)}, bf16[3,2048,128]{2,1,0:T(8,128)(2,1)S(1)}, u32[]{:S(2)}) copy-start(bf16[3,2048,128]{2,1,0:T(8,128)(2,1)S(1)} %get-tuple-element.88.bias) | copy-start | bytes 4718596
  47.9 1.7 collective-permute-start.11
  47.9 3.4 %collective-permute-start.8 = (bf16[256,768]{1,0:T(8,128)(2,1)S(1)}, bf16[256,768]{1,0:T(8,128)(2,1)S(1)}, u32[]{:S(2)}, u32[]{:S(2)}) collective-permute-start(bf16[256,768]{1,0:T(8,128)(2,1)S(1)} %collective-permute-done.7.refs_0_), channel_id=1, source_target_pairs={{0,1},{1,0},{2,3},{3,2},{4,5},{5,4},{6,7},{7,6},{8,9},{9,8},{10,11... | collective-permute-start | bytes 1179656 | tf_op jit(solution)/shard_map/ppermute | solution.py:817
  48.4 4.7 %collective-permute-start.6 = (bf16[256,768]{1,0:T(8,128)(2,1)S(1)}, bf16[256,768]{1,0:T(8,128)(2,1)S(1)}, u32[]{:S(2)}, u32[]{:S(2)}) collective-permute-start(bf16[256,768]{1,0:T(8,128)(2,1)S(1)} %collective-permute-done.5.refs_0_), channel_id=1, source_target_pairs={{0,1},{1,0},{2,3},{3,2},{4,5},{5,4},{6,7},{7,6},{8,9},{9,8},{10,11... | collective-permute-start | bytes 1179656 | tf_op jit(solution)/shard_map/ppermute | solution.py:817
  54.8 18.9 %copy-start.10 = (f32[768]{0:T(1024)S(1)}, f32[768]{0:T(1024)}, u32[]{:S(2)}) copy-start(f32[768]{0:T(1024)} %param.23) | copy-start | bytes 9220
  54.9 26.6 %copy-start.4 = (bf16[768,768]{1,0:T(8,128)(2,1)S(1)}, bf16[768,768]{1,0:T(8,128)(2,1)}, u32[]{:S(2)}) copy-start(bf16[768,768]{1,0:T(8,128)(2,1)} %param.22) | copy-start | bytes 3538948
  68.3 5.4 %collective-permute-start.12 = (bf16[192,256]{1,0:T(8,128)(2,1)S(1)}, bf16[192,256]{1,0:T(8,128)(2,1)S(1)}, u32[]{:S(2)}, u32[]{:S(2)}) collective-permute-start(bf16[192,256]{1,0:T(8,128)(2,1)S(1)} %get-tuple-element.103), channel_id=1, source_target_pairs={{0,2},{1,3},{2,4},{3,5},{4,6},{5,7},{6,0},{7,1},{8,10},{9,11},{10,... | collective-permute-start | bytes 294920 | tf_op jit(solution)/shard_map/ppermute | solution.py:813
  68.6 10.6 %collective-permute-start.13 = (bf16[192,256]{1,0:T(8,128)(2,1)S(1)}, bf16[192,256]{1,0:T(8,128)(2,1)S(1)}, u32[]{:S(2)}, u32[]{:S(2)}) collective-permute-start(bf16[192,256]{1,0:T(8,128)(2,1)S(1)} %get-tuple-element.104), channel_id=1, source_target_pairs={{0,4},{1,5},{2,6},{3,7},{4,0},{5,1},{6,2},{7,3},{8,12},{9,13},{10,... | collective-permute-start | bytes 294920 | tf_op jit(solution)/shard_map/ppermute | solution.py:813
  72.9 8.6 %collective-permute-start.14 = (bf16[192,256]{1,0:T(8,128)(2,1)S(1)}, bf16[192,256]{1,0:T(8,128)(2,1)S(1)}, u32[]{:S(2)}, u32[]{:S(2)}) collective-permute-start(bf16[192,256]{1,0:T(8,128)(2,1)S(1)} %get-tuple-element.105), channel_id=1, source_target_pairs={{0,6},{1,7},{2,0},{3,1},{4,2},{5,3},{6,4},{7,5},{8,14},{9,15},{10,... | collective-permute-start | bytes 294920 | tf_op jit(solution)/shard_map/ppermute | solution.py:813
  96.1 5.7 %collective-permute-start.18 = (bf16[256,5376]{1,0:T(8,128)(2,1)S(1)}, bf16[256,5376]{1,0:T(8,128)(2,1)S(1)}, u32[]{:S(2)}, u32[]{:S(2)}) collective-permute-start(bf16[256,5376]{1,0:T(8,128)(2,1)S(1)} %get-tuple-element.114.refs_0_.refs_2_), channel_id=1, source_target_pairs={{0,1},{1,0},{2,3},{3,2},{4,5},{5,4},{6,7},{7,6},{8,9},{9,8},{10,11... | collective-permute-start | bytes 8257544 | tf_op jit(solution)/shard_map/ppermute | solution.py:817
  96.1 5.7 %collective-permute-start.19 = (bf16[784,256]{1,0:T(8,128)(2,1)S(1)}, bf16[784,256]{1,0:T(8,128)(2,1)S(1)}, u32[]{:S(2)}, u32[]{:S(2)}) collective-permute-start(bf16[784,256]{1,0:T(8,128)(2,1)S(1)} %get-tuple-element.117), channel_id=1, source_target_pairs={{0,1},{1,0},{2,3},{3,2},{4,5},{5,4},{6,7},{7,6},{8,9},{9,8},{10,11... | collective-permute-start | bytes 1204232 | tf_op jit(solution)/shard_map/ppermute | solution.py:817
  96.6 12.6 %collective-permute-start.15 = (bf16[192,256]{1,0:T(8,128)(2,1)S(1)}, bf16[192,256]{1,0:T(8,128)(2,1)S(1)}, u32[]{:S(2)}, u32[]{:S(2)}) collective-permute-start(bf16[192,256]{1,0:T(8,128)(2,1)S(1)} %get-tuple-element.108), channel_id=1, source_target_pairs={{0,6},{1,7},{2,0},{3,1},{4,2},{5,3},{6,4},{7,5},{8,14},{9,15},{10,... | collective-permute-start | bytes 294920 | tf_op jit(solution)/shard_map/ppermute | solution.py:813
  96.7 12.6 %collective-permute-start.16 = (bf16[192,256]{1,0:T(8,128)(2,1)S(1)}, bf16[192,256]{1,0:T(8,128)(2,1)S(1)}, u32[]{:S(2)}, u32[]{:S(2)}) collective-permute-start(bf16[192,256]{1,0:T(8,128)(2,1)S(1)} %get-tuple-element.109), channel_id=1, source_target_pairs={{0,4},{1,5},{2,6},{3,7},{4,0},{5,1},{6,2},{7,3},{8,12},{9,13},{10,... | collective-permute-start | bytes 294920 | tf_op jit(solution)/shard_map/ppermute | solution.py:813
  97.8 11.5 %collective-permute-start.17 = (bf16[192,256]{1,0:T(8,128)(2,1)S(1)}, bf16[192,256]{1,0:T(8,128)(2,1)S(1)}, u32[]{:S(2)}, u32[]{:S(2)}) collective-permute-start(bf16[192,256]{1,0:T(8,128)(2,1)S(1)} %get-tuple-element.110), channel_id=1, source_target_pairs={{0,2},{1,3},{2,4},{3,5},{4,6},{5,7},{6,0},{7,1},{8,10},{9,11},{10,... | collective-permute-start | bytes 294920 | tf_op jit(solution)/shard_map/ppermute | solution.py:813
  110.6 4.3 %collective-permute-start.20 = (f32[3,80,128]{2,1,0:T(8,128)S(1)}, f32[3,80,128]{2,1,0:T(8,128)S(1)}, u32[]{:S(2)}, u32[]{:S(2)}) collective-permute-start(f32[3,80,128]{2,1,0:T(8,128)S(1)} %sums.1.refs_7_), channel_id=1, source_target_pairs={{0,1},{1,0},{2,3},{3,2},{4,5},{5,4},{6,7},{7,6},{8,9},{9,8},{10,11... | collective-permute-start | bytes 368648 | tf_op jit(solution)/shard_map/ppermute | solution.py:817
  110.8 24.7 %collective-permute-start.21 = (bf16[1,4,80,768]{3,2,1,0:T(8,128)(2,1)S(1)}, bf16[1,4,80,768]{3,2,1,0:T(8,128)(2,1)S(1)}, u32[]{:S(2)}, u32[]{:S(2)}) collective-permute-start(bf16[1,4,80,768]{3,2,1,0:T(8,128)(2,1)S(1)} %get-tuple-element.123), channel_id=1, source_target_pairs={{0,8},{8,0},{16,24},{24,16},{1,9},{9,1},{17,25},{25,17},{2,10},{10... | collective-permute-start | bytes 1474568 | tf_op jit(solution)/shard_map/ppermute | solution.py:820
  112.3 26.7 %collective-permute-start.22 = (bf16[1,4,112,768]{3,2,1,0:T(8,128)(2,1)S(1)}, bf16[1,4,112,768]{3,2,1,0:T(8,128)(2,1)S(1)}, u32[]{:S(2)}, u32[]{:S(2)}) collective-permute-start(bf16[1,4,112,768]{3,2,1,0:T(8,128)(2,1)S(1)} %get-tuple-element.124), channel_id=1, source_target_pairs={{0,8},{8,0},{16,24},{24,16},{1,9},{9,1},{17,25},{25,17},{2,10},{10... | collective-permute-start | bytes 2064392 | tf_op jit(solution)/shard_map/ppermute | solution.py:820
  112.9 22.6 %collective-permute-start.23 = (bf16[1,4,80,768]{3,2,1,0:T(8,128)(2,1)S(1)}, bf16[1,4,80,768]{3,2,1,0:T(8,128)(2,1)S(1)}, u32[]{:S(2)}, u32[]{:S(2)}) collective-permute-start(bf16[1,4,80,768]{3,2,1,0:T(8,128)(2,1)S(1)} %get-tuple-element.125), channel_id=1, source_target_pairs={{0,16},{8,24},{16,0},{24,8},{1,17},{9,25},{17,1},{25,9},{2,18},{10... | collective-permute-start | bytes 1474568 | tf_op jit(solution)/shard_map/ppermute | solution.py:820
  114.4 26.1 %collective-permute-start.24 = (bf16[1,4,112,768]{3,2,1,0:T(8,128)(2,1)S(1)}, bf16[1,4,112,768]{3,2,1,0:T(8,128)(2,1)S(1)}, u32[]{:S(2)}, u32[]{:S(2)}) collective-permute-start(bf16[1,4,112,768]{3,2,1,0:T(8,128)(2,1)S(1)} %get-tuple-element.126), channel_id=1, source_target_pairs={{0,16},{8,24},{16,0},{24,8},{1,17},{9,25},{17,1},{25,9},{2,18},{10... | collective-permute-start | bytes 2064392 | tf_op jit(solution)/shard_map/ppermute | solution.py:820
  140.5 2.3 collective-permute-start.25
  145.3 2.1 collective-permute-start.29
  147.8 30.9 %collective-permute-start.30 = (bf16[4,168,768]{2,1,0:T(8,128)(2,1)S(1)}, bf16[4,168,768]{2,1,0:T(8,128)(2,1)S(1)}, u32[]{:S(2)}, u32[]{:S(2)}) collective-permute-start(bf16[4,168,768]{2,1,0:T(8,128)(2,1)S(1)} %get-tuple-element.138), channel_id=1, source_target_pairs={{0,16},{8,24},{16,0},{24,8},{1,17},{9,25},{17,1},{25,9},{2,18},{10... | collective-permute-start | bytes 3096584 | tf_op jit(solution)/shard_map/ppermute | solution.py:820
  149.4 29.3 %collective-permute-start.31 = (bf16[4,168,768]{2,1,0:T(8,128)(2,1)S(1)}, bf16[4,168,768]{2,1,0:T(8,128)(2,1)S(1)}, u32[]{:S(2)}, u32[]{:S(2)}) collective-permute-start(bf16[4,168,768]{2,1,0:T(8,128)(2,1)S(1)} %get-tuple-element.139), channel_id=1, source_target_pairs={{0,8},{8,0},{16,24},{24,16},{1,9},{9,1},{17,25},{25,17},{2,10},{10... | collective-permute-start | bytes 3096584 | tf_op jit(solution)/shard_map/ppermute | solution.py:820
  150.9 9.9 %collective-permute-start.26 = (bf16[3,192,256]{2,1,0:T(8,128)(2,1)S(1)}, bf16[3,192,256]{2,1,0:T(8,128)(2,1)S(1)}, u32[]{:S(2)}, u32[]{:S(2)}) collective-permute-start(bf16[3,192,256]{2,1,0:T(8,128)(2,1)S(1)} %get-tuple-element.130), channel_id=1, source_target_pairs={{0,2},{1,3},{2,4},{3,5},{4,6},{5,7},{6,0},{7,1},{8,10},{9,11},{10,... | collective-permute-start | bytes 884744 | tf_op jit(solution)/shard_map/ppermute | solution.py:813
  150.9 25.2 %collective-permute-start.27 = (bf16[3,192,256]{2,1,0:T(8,128)(2,1)S(1)}, bf16[3,192,256]{2,1,0:T(8,128)(2,1)S(1)}, u32[]{:S(2)}, u32[]{:S(2)}) collective-permute-start(bf16[3,192,256]{2,1,0:T(8,128)(2,1)S(1)} %get-tuple-element.131), channel_id=1, source_target_pairs={{0,4},{1,5},{2,6},{3,7},{4,0},{5,1},{6,2},{7,3},{8,12},{9,13},{10,... | collective-permute-start | bytes 884744 | tf_op jit(solution)/shard_map/ppermute | solution.py:813
  153.3 25.5 %collective-permute-start.28 = (bf16[3,192,256]{2,1,0:T(8,128)(2,1)S(1)}, bf16[3,192,256]{2,1,0:T(8,128)(2,1)S(1)}, u32[]{:S(2)}, u32[]{:S(2)}) collective-permute-start(bf16[3,192,256]{2,1,0:T(8,128)(2,1)S(1)} %get-tuple-element.132), channel_id=1, source_target_pairs={{0,6},{1,7},{2,0},{3,1},{4,2},{5,3},{6,4},{7,5},{8,14},{9,15},{10,... | collective-permute-start | bytes 884744 | tf_op jit(solution)/shard_map/ppermute | solution.py:813
  160.8 17.9 %collective-permute-start.32 = (bf16[4,24,768]{2,1,0:T(8,128)(2,1)S(1)}, bf16[4,24,768]{2,1,0:T(8,128)(2,1)S(1)}, u32[]{:S(2)}, u32[]{:S(2)}) collective-permute-start(bf16[4,24,768]{2,1,0:T(8,128)(2,1)S(1)} %get-tuple-element.140), channel_id=1, source_target_pairs={{0,24},{8,16},{16,8},{24,0},{1,25},{9,17},{17,9},{25,1},{2,26},{10... | collective-permute-start | bytes 442376 | tf_op jit(solution)/shard_map/ppermute | solution.py:820
  179.9 8.9 %collective-permute-start.33 = (bf16[160,768]{1,0:T(8,128)(2,1)S(1)}, bf16[160,768]{1,0:T(8,128)(2,1)S(1)}, u32[]{:S(2)}, u32[]{:S(2)}) collective-permute-start(bf16[160,768]{1,0:T(8,128)(2,1)S(1)} %get-tuple-element.142), channel_id=1, source_target_pairs={{0,2},{1,3},{2,4},{3,5},{4,6},{5,7},{6,0},{7,1},{8,10},{9,11},{10,... | collective-permute-start | bytes 737288 | tf_op jit(solution)/shard_map/ppermute | solution.py:813
  180.0 22.1 %collective-permute-start.34 = (bf16[160,768]{1,0:T(8,128)(2,1)S(1)}, bf16[160,768]{1,0:T(8,128)(2,1)S(1)}, u32[]{:S(2)}, u32[]{:S(2)}) collective-permute-start(bf16[160,768]{1,0:T(8,128)(2,1)S(1)} %get-tuple-element.143), channel_id=1, source_target_pairs={{0,4},{1,5},{2,6},{3,7},{4,0},{5,1},{6,2},{7,3},{8,12},{9,13},{10,... | collective-permute-start | bytes 737288 | tf_op jit(solution)/shard_map/ppermute | solution.py:813
  180.8 23.7 %collective-permute-start.35 = (bf16[160,768]{1,0:T(8,128)(2,1)S(1)}, bf16[160,768]{1,0:T(8,128)(2,1)S(1)}, u32[]{:S(2)}, u32[]{:S(2)}) collective-permute-start(bf16[160,768]{1,0:T(8,128)(2,1)S(1)} %get-tuple-element.144), channel_id=1, source_target_pairs={{0,6},{1,7},{2,0},{3,1},{4,2},{5,3},{6,4},{7,5},{8,14},{9,15},{10,... | collective-permute-start | bytes 737288 | tf_op jit(solution)/shard_map/ppermute | solution.py:813
  188.8 15.8 %collective-permute-start.36 = (bf16[88,768]{1,0:T(8,128)(2,1)S(1)}, bf16[88,768]{1,0:T(8,128)(2,1)S(1)}, u32[]{:S(2)}, u32[]{:S(2)}) collective-permute-start(bf16[88,768]{1,0:T(8,128)(2,1)S(1)} %get-tuple-element.148), channel_id=1, source_target_pairs={{0,2},{1,3},{2,4},{3,5},{4,6},{5,7},{6,0},{7,1},{8,10},{9,11},{10,... | collective-permute-start | bytes 405512 | tf_op jit(solution)/shard_map/ppermute | solution.py:813
  206.2 14.1 %collective-permute-start.37 = (bf16[160,768]{1,0:T(8,128)(2,1)S(1)}, bf16[160,768]{1,0:T(8,128)(2,1)S(1)}, u32[]{:S(2)}, u32[]{:S(2)}) collective-permute-start(bf16[160,768]{1,0:T(8,128)(2,1)S(1)} %fourth.2.refs_5_.refs_0_), channel_id=1, source_target_pairs={{0,8},{8,0},{16,24},{24,16},{1,9},{9,1},{17,25},{25,17},{2,10},{10... | collective-permute-start | bytes 737288 | tf_op jit(solution)/shard_map/ppermute | solution.py:820
  207.4 12.9 %collective-permute-start.38 = (bf16[160,768]{1,0:T(8,128)(2,1)S(1)}, bf16[160,768]{1,0:T(8,128)(2,1)S(1)}, u32[]{:S(2)}, u32[]{:S(2)}) collective-permute-start(bf16[160,768]{1,0:T(8,128)(2,1)S(1)} %fourth.2.refs_5_.refs_0_), channel_id=1, source_target_pairs={{0,16},{8,24},{16,0},{24,8},{1,17},{9,25},{17,1},{25,9},{2,18},{10... | collective-permute-start | bytes 737288 | tf_op jit(solution)/shard_map/ppermute | solution.py:820
  208.9 11.4 %collective-permute-start.39 = (bf16[160,768]{1,0:T(8,128)(2,1)S(1)}, bf16[160,768]{1,0:T(8,128)(2,1)S(1)}, u32[]{:S(2)}, u32[]{:S(2)}) collective-permute-start(bf16[160,768]{1,0:T(8,128)(2,1)S(1)} %fourth.2.refs_5_.refs_0_), channel_id=1, source_target_pairs={{0,24},{8,16},{16,8},{24,0},{1,25},{9,17},{17,9},{25,1},{2,26},{10... | collective-permute-start | bytes 737288 | tf_op jit(solution)/shard_map/ppermute | solution.py:820
  209.8 9.2 %collective-permute-start.40 = (bf16[88,768]{1,0:T(8,128)(2,1)S(1)}, bf16[88,768]{1,0:T(8,128)(2,1)S(1)}, u32[]{:S(2)}, u32[]{:S(2)}) collective-permute-start(bf16[88,768]{1,0:T(8,128)(2,1)S(1)} %get-tuple-element.150), channel_id=1, source_target_pairs={{0,4},{1,5},{2,6},{3,7},{4,0},{5,1},{6,2},{7,3},{8,12},{9,13},{10,... | collective-permute-start | bytes 405512 | tf_op jit(solution)/shard_map/ppermute | solution.py:813
  210.8 9.6 %collective-permute-start.41 = (bf16[88,768]{1,0:T(8,128)(2,1)S(1)}, bf16[88,768]{1,0:T(8,128)(2,1)S(1)}, u32[]{:S(2)}, u32[]{:S(2)}) collective-permute-start(bf16[88,768]{1,0:T(8,128)(2,1)S(1)} %get-tuple-element.151), channel_id=1, source_target_pairs={{0,6},{1,7},{2,0},{3,1},{4,2},{5,3},{6,4},{7,5},{8,14},{9,15},{10,... | collective-permute-start | bytes 405512 | tf_op jit(solution)/shard_map/ppermute | solution.py:813
  221.0 8.4 %collective-permute-start.42 = (bf16[144,768]{1,0:T(8,128)(2,1)S(1)}, bf16[144,768]{1,0:T(8,128)(2,1)S(1)}, u32[]{:S(2)}, u32[]{:S(2)}) collective-permute-start(bf16[144,768]{1,0:T(8,128)(2,1)S(1)} %fourth.3.refs_4_), channel_id=1, source_target_pairs={{0,8},{8,0},{16,24},{24,16},{1,9},{9,1},{17,25},{25,17},{2,10},{10... | collective-permute-start | bytes 663560 | tf_op jit(solution)/shard_map/ppermute | solution.py:820
  222.3 11.0 %collective-permute-start.43 = (bf16[144,768]{1,0:T(8,128)(2,1)S(1)}, bf16[144,768]{1,0:T(8,128)(2,1)S(1)}, u32[]{:S(2)}, u32[]{:S(2)}) collective-permute-start(bf16[144,768]{1,0:T(8,128)(2,1)S(1)} %fourth.3.refs_4_), channel_id=1, source_target_pairs={{0,16},{8,24},{16,0},{24,8},{1,17},{9,25},{17,1},{25,9},{2,18},{10... | collective-permute-start | bytes 663560 | tf_op jit(solution)/shard_map/ppermute | solution.py:820
  223.1 10.1 %collective-permute-start.44 = (bf16[144,768]{1,0:T(8,128)(2,1)S(1)}, bf16[144,768]{1,0:T(8,128)(2,1)S(1)}, u32[]{:S(2)}, u32[]{:S(2)}) collective-permute-start(bf16[144,768]{1,0:T(8,128)(2,1)S(1)} %fourth.3.refs_4_), channel_id=1, source_target_pairs={{0,24},{8,16},{16,8},{24,0},{1,25},{9,17},{17,9},{25,1},{2,26},{10... | collective-permute-start | bytes 663560 | tf_op jit(solution)/shard_map/ppermute | solution.py:820
  (9 other events, 44.6 us)

commit v10 on v9

--- a/solution.py
+++ b/solution.py
@@ -494,17 +494,17 @@
 
 def weights_kernel(info, *refs, groups):
     (dup, dup_got, dbr, dbr_got, act, act_got, low, low_got, cot, cot_got) = refs[:10]
-    send_u, keep_u, send_d, keep_d, outs = refs[10:13], refs[13], refs[14:17], refs[17], refs[18]
+    send_u, keep_u, send_d, keep_d, outs = refs[10:12], refs[12], refs[13:15], refs[15], refs[16]
     width = cot.shape[1]
-    lead = send_u[0].shape[2]
+    lead = send_u[0].shape[2] - keep_u.shape[2]
 
     def leave(send, turn, spot, block, first):
         if turn:
-            send[2][0, spot, first : first + block.shape[0]] = block
+            send[0][0, spot, lead + first : lead + first + block.shape[0]] = block
         elif first:
             send[1][0, spot, first - lead : first - lead + block.shape[0]] = block
         else:
-            send[0][0, spot] = block[:lead]
+            send[0][0, spot, :lead] = block[:lead]
             send[1][0, spot, : block.shape[0] - lead] = block[lead:]
 
     index = pl.program_id(0)
@@ -582,8 +582,9 @@
 
 def second_kernel(keep_u, got_u, keep_d, got_d, inner, inner_got, late_u, late_d, to_y, to_x, to_xy):
     rows, lines = keep_u.shape[2], inner.shape[2]
-    to_y[:, :rows] = (keep_u[0].astype(F32) + got_u[0].astype(F32)).astype(BF)
-    to_x[:, :rows] = (keep_d[0].astype(F32) + got_d[0].astype(F32)).astype(BF)
+    lead = got_u.shape[2] - rows
+    to_y[:, :rows] = (keep_u[0].astype(F32) + got_u[0, :, lead:].astype(F32)).astype(BF)
+    to_x[:, :rows] = (keep_d[0].astype(F32) + got_d[0, :, lead:].astype(F32)).astype(BF)
     last = to_y.shape[1] - lines
     to_y[:, last:] = (inner[1].astype(F32) + inner_got[1].astype(F32)).astype(BF)
     to_x[:, last:] = (inner[2].astype(F32) + inner_got[2].astype(F32)).astype(BF)
@@ -593,22 +594,26 @@
 
 
 def third_kernel(info, keep_u, one_u, keep_d, one_d, by_y, by_x, inner, inner_got, by_xy, *outs):
-    rows, lead, lines = keep_u.shape[2], one_u.shape[2], inner.shape[2]
+    rows, lines = keep_u.shape[2], inner.shape[2]
+    early = one_u.shape[2] - rows
     groups = len(outs) // 2
+    lead = outs[0].shape[0] // 2
     left = rows - lead
-    head, tail, late = slice(0, lead), slice(lead, rows), slice(rows, rows + left)
-    mid = slice(rows + left, None)
-
-    def added(keep, got, by, group, spot):
-        total = keep[0, group, spot].astype(F32) + got.astype(F32)
-        return (total + by[group, spot].astype(F32)).astype(BF)
+    late, mid = slice(rows, 2 * rows - early), slice(2 * rows - early, None)
+
+    def added(keep, one, rest, by, group):
+        got = jnp.concatenate([one[0, group, :early], rest[group, late]], axis=0)
+        total = keep[0, group].astype(F32) + got.astype(F32)
+        return (total + by[group, :rows].astype(F32)).astype(BF)
 
     for group in range(groups):
         first, last = outs[group], outs[groups + group]
-        first[:lead] = added(keep_u, one_u[0, group], by_y, group, head)
-        first[lead:] = added(keep_d, one_d[0, group], by_x, group, head)
-        last[:left] = added(keep_u, by_x[group, late], by_y, group, tail)
-        last[left : 2 * left] = added(keep_d, by_y[group, late], by_x, group, tail)
+        up = added(keep_u, one_u, by_x, by_y, group)
+        down = added(keep_d, one_d, by_y, by_x, group)
+        first[:lead] = up[:lead]
+        first[lead:] = down[:lead]
+        last[:left] = up[lead:]
+        last[left : 2 * left] = down[lead:]
         both = inner[0, group].astype(F32) + inner_got[0, group].astype(F32)
         both = both + by_y[group, mid].astype(F32) + by_x[group, mid].astype(F32)
         last[2 * left :] = (both + by_xy[group].astype(F32)).astype(BF)
@@ -857,8 +862,8 @@
     )
     lines = rows // clusters
     packed = jnp.concatenate([tops, marked.reshape(heads, lines, clusters)], axis=1)
-    early = [along_peers(tokens, -hop) for hop in range(1, peers)]
-    packed = after(packed.reshape(groups, own_heads, picks + lines, clusters), early)
+    near = [along_peers(tokens, -hop) for hop in range(1, peers)]
+    packed = after(packed.reshape(groups, own_heads, picks + lines, clusters), near)
 
     def of_heads(hop):
         return lax.dynamic_index_in_dim(packed, (group_at + groups - hop) % groups, keepdims=False)
@@ -916,7 +921,7 @@
         if group == 1:
             arrival = after(arrival, bias, held, cot_got, [mine[hop] for hop in range(2, groups)])
         chunk = [arrival]
-        chunk += early if group == 0 else [along_peers(arrival, -hop) for hop in range(1, peers)]
+        chunk += near if group == 0 else [along_peers(arrival, -hop) for hop in range(1, peers)]
         if peers > 2:
             chunk = [jnp.concatenate(chunk, axis=0)]
         span = peers * rows
@@ -988,7 +993,7 @@
             array((own_heads, hs + 8, clusters), F32),
             array((own_heads, hs, clusters), BF),
         ],
-        compiler_params=params(32 if fast else 60, 1),
+        compiler_params=params(16 if fast else 60, 1),
         cost_estimate=cost(6 * pair_flops, 8e6, own_heads * own_rows * seq),
         name="attend",
     )(ids_all, feat, kv, bias)
@@ -999,7 +1004,7 @@
 
     chunks = 4
     part = hidden // chunks
-    lead = 80
+    early, lead = 64, 80
     w_out_g = w_out.reshape(groups, feats, width)
     gain_row2, shift_row2 = gain_two[None, :], shift_two[None, :]
     square = whole((rows, width))
@@ -1066,7 +1071,7 @@
         low_spec = whole((width + 16, rows))
         shape_u = (2, groups, high, width)
         shape_d = (2, groups, high, width)
-        parts = [(1, groups, tall, width) for tall in (lead, high - lead, high)]
+        parts = [(1, groups, tall, width) for tall in (early + high, high - early)]
         results = prefetched(
             functools.partial(weights_kernel, groups=groups),
             (4,),
@@ -1081,7 +1086,7 @@
             "weights",
             scratch=[pltpu.VMEM((groups, block_rows, width), F32)],
         )(info, far, got, far, got, act_own, got, low_own, low_got, cotangent, *cot_got)
-        return results[:3], results[3], results[4:7], results[7]
+        return results[:2], results[2], results[3:5], results[5]
 
     def weight_second(keep_u, got_u, keep_d, got_d, inner, inner_got, late_u, late_d):
         def block(shape, at):
@@ -1203,8 +1208,7 @@
 
     if fast:
         send_u, keep_u, send_d, keep_d = weight_parts()
-        got_u = [along_dp(item, 1) for item in (send_u[0], send_u[2])]
-        got_d = [along_dp(item, 2) for item in (send_d[0], send_d[2])]
+        got_u, got_d = along_dp(send_u[0], 1), along_dp(send_d[0], 2)
     else:
         norm_two, d_up, d_branch, act, normed_two = kept
         total_up = reduce_rows(tn(normed_two, d_up).astype(BF))
@@ -1249,7 +1253,7 @@
         ],
         out_shape=back_shapes,
         scratch_shapes=[pltpu.VMEM((seq, 2 * hs), F32), pltpu.VMEM((seq, 2 * clusters), BF)],
-        compiler_params=params(36 if fast else 62, 1),
+        compiler_params=params(24 if fast else 62, 1),
         cost_estimate=cost(14 * pair_flops, 10e6, own_heads * own_rows * seq),
         name="back",
     )(ids_all, feat, kv, bias, *grads, mixed, stats, centroid, share, *share_got)
@@ -1299,11 +1303,11 @@
         keep, far = more
         inner_got = along_peers(far, 1)
         to_y, to_x, to_xy = weight_second(
-            keep_u, got_u[1], keep_d, got_d[1], keep, inner_got, send_u[1], send_d[1]
+            keep_u, got_u, keep_d, got_d, keep, inner_got, send_u[1], send_d[1]
         )
         by_y, by_x, by_xy = along_dp(to_y, 2), along_dp(to_x, 1), along_dp(to_xy, 3)
         sums = weight_third(
-            keep_u, got_u[0], keep_d, got_d[0], by_y, by_x, keep, inner_got, by_xy
+            keep_u, got_u, keep_d, got_d, by_y, by_x, keep, inner_got, by_xy
         )
         came_a, came_b = [sums[0]], [sums[groups]]
         came_a += [along_groups(sums[hop], hop) for hop in range(1, groups)]

time: 238 us -> 233 us (0.979)
  local copies, waits for them, and re-layouts: 17.4 us -> 12.7 us
    unnamed x27, local copies, waits for them, and re-layouts: 12.5 us -> 7.05 us
    ppermute x13 -> x11, waiting for transfers between devices: 12.7 us -> 14.3 us  [along_dp(): return lax.ppermute(values, 'dp', [(i, i ^ mask) for i in range(n_dp)])]
    ppermute x13 -> x11, starting transfers between devices: 14.7 us -> 13.7 us  [along_dp(): return lax.ppermute(values, 'dp', [(i, i ^ mask) for i in range(n_dp)])]
  transfers between devices with their start and end apart: 45 -> 43, of which waited for: 21 -> 23; matrix products, arithmetic and copies ran while one was open for 6% -> 6% of each run, Pallas kernels for 19% -> 19%
where the time goes in v10:
time: 233 us; the launch traced here: 232 us
  waiting for transfers between devices  90 us (39%)
  Pallas kernels  78.8 us (34%)
  starting transfers between devices  44.4 us (19%)
  local copies, waits for them, and re-layouts  12.7 us (5%)
  other arithmetic  4.58 us (2%)
    ppermute x21, waiting for transfers between devices, along_groups(): return lax.ppermute(values, 'wide', pairs)  69.4 us
    pallas_call x15, Pallas kernels, prefetched(): return lambda *inputs: call(*inputs, *first)  45 us
    ppermute x21, starting transfers between devices, along_groups(): return lax.ppermute(values, 'wide', pairs)  29 us
    pallas_call x1, Pallas kernels, per_device(): pl.pallas_call(functools.partial(back_kernel, size=size, groups=groups, g...  20.3 us
    ppermute x11, waiting for transfers between devices, along_dp(): return lax.ppermute(values, 'dp', [(i, i ^ mask) for i in range(n_dp)])  14.3 us
    ppermute x11, starting transfers between devices, along_dp(): return lax.ppermute(values, 'dp', [(i, i ^ mask) for i in range(n_dp)])  13.7 us
    pallas_call x1, Pallas kernels, per_device(): pl.pallas_call(functools.partial(forward_kernel, size=size, groups=groups...  13.1 us
    unnamed x27, local copies, waits for them, and re-layouts  7.05 us
  transfers between devices with their start and end apart: 43, of which 23 were waited for; matrix products, arithmetic and copies ran while one was open for 6% of the time, Pallas kernels for 19%

profile of v10, /device:TPU:8, one launch (start us, length us, event | category | flops | bytes accessed | tf_op | source)
XLA Modules:
  0.0 232.4 jit_solution(13225808859015834267)
XLA Ops:
  3.3 2.1 dynamic_update_slice.3
  6.1 3.0 %collective-permute-start.2 = (s32[3,34,128]{2,1,0:T(8,128)S(1)}, s32[3,34,128]{2,1,0:T(8,128)S(1)}, u32[]{:S(2)}, u32[]{:S(2)}) collective-permute-start(s32[3,34,128]{2,1,0:T(8,128)S(1)} %get-tuple-element.158), channel_id=1, source_target_pairs={{0,4},{1,5},{2,6},{3,7},{4,0},{5,1},{6,2},{7,3},{8,12},{9,13},{10,... | collective-permute-start | bytes 156680 | tf_op jit(solution)/shard_map/ppermute | solution.py:818
  9.1 2.5 %collective-permute-start.3 = (s32[3,34,128]{2,1,0:T(8,128)S(1)}, s32[3,34,128]{2,1,0:T(8,128)S(1)}, u32[]{:S(2)}, u32[]{:S(2)}) collective-permute-start(s32[3,34,128]{2,1,0:T(8,128)S(1)} %get-tuple-element.157), channel_id=1, source_target_pairs={{0,2},{1,3},{2,4},{3,5},{4,6},{5,7},{6,0},{7,1},{8,10},{9,11},{10,... | collective-permute-start | bytes 156680 | tf_op jit(solution)/shard_map/ppermute | solution.py:818
  11.7 2.0 collective-permute-start.9
  13.7 4.3 %copy.50 = bf16[768,1536]{0,1:T(8,128)(2,1)} copy(bf16[768,1536]{1,0:T(8,128)(2,1)} %param.21) | data formatting | bytes 4718592 | tf_op args[7]
  17.9 1.6 copy.49
  21.5 1.9 pad_maximum_fusion
  23.8 1.7 project.4
  25.5 7.6 %bias.1 = (bf16[3,2048,128]{2,1,0:T(8,128)(2,1)S(1)}, s32[3,1,2048]{2,1,0:T(1,128)S(1)}) custom-call(s32[6]{0:T(128)S(1)} %stack.38.info.refs_0_, s32[3,40,128]{2,1,0:T(8,128)S(1)} %table.1.refs_0_, s32[3,40,128]{2,1,0:T(8,128)S(1)} %collective-permute-done.4.refs_1_), custom_call_target="tpu_custom_call" | custom-call | flops 201326592 | bytes 1572864 | tf_op jit(solution)/shard_map/bias/pallas_call | solution.py:846
  33.2 7.2 %collective-permute-done.7.refs_0_ = bf16[256,768]{1,0:T(8,128)(2,1)S(1)} collective-permute-done((bf16[256,768]{1,0:T(8,128)(2,1)S(1)}, bf16[256,768]{1,0:T(8,128)(2,1)S(1)}, u32[]{:S(2)}, u32[]{:S(2)}) %collective-permute-start.7) | collective-permute-done | bytes 393248 | tf_op jit(solution)/shard_map/ppermute | solution.py:818
  41.1 7.4 %collective-permute-done.5.refs_0_ = bf16[256,768]{1,0:T(8,128)(2,1)S(1)} collective-permute-done((bf16[256,768]{1,0:T(8,128)(2,1)S(1)}, bf16[256,768]{1,0:T(8,128)(2,1)S(1)}, u32[]{:S(2)}, u32[]{:S(2)}) %collective-permute-start.5) | collective-permute-done | bytes 393248 | tf_op jit(solution)/shard_map/ppermute | solution.py:818
  50.3 1.7 project.5
  52.0 1.7 project.6
  53.8 1.7 project.7
  55.6 13.1 %attend.1 = (bf16[192,256]{1,0:T(8,128)(2,1)S(1)}, bf16[192,256]{1,0:T(8,128)(2,1)S(1)}, bf16[192,256]{1,0:T(8,128)(2,1)S(1)}, bf16[192,256]{1,0:T(8,128)(2,1)S(...) custom-call(s32[3,1,2048]{2,1,0:T(1,128)S(1)} %get-tuple-element.84.ids_all.refs_1_, ...), custom_call_target="tpu_custom_call" | custom-call | flops 9663676416 | bytes 8000000 | tf_op jit(solution)/shard_map/attend/pallas_call | solution.py:985
  69.0 4.3 %collective-permute-start.13 = (bf16[192,256]{1,0:T(8,128)(2,1)S(1)}, bf16[192,256]{1,0:T(8,128)(2,1)S(1)}, u32[]{:S(2)}, u32[]{:S(2)}) collective-permute-start(bf16[192,256]{1,0:T(8,128)(2,1)S(1)} %get-tuple-element.102), channel_id=1, source_target_pairs={{0,4},{1,5},{2,6},{3,7},{4,0},{5,1},{6,2},{7,3},{8,12},{9,13},{10,... | collective-permute-start | bytes 294920 | tf_op jit(solution)/shard_map/ppermute | solution.py:818
  74.1 5.6 %collective-permute-done.13.refs_2_ = bf16[192,256]{1,0:T(8,128)(2,1)S(1)} collective-permute-done((bf16[192,256]{1,0:T(8,128)(2,1)S(1)}, bf16[192,256]{1,0:T(8,128)(2,1)S(1)}, u32[]{:S(2)}, u32[]{:S(2)}) %collective-permute-start.13) | collective-permute-done | bytes 98336 | tf_op jit(solution)/shard_map/ppermute | solution.py:818
  79.6 2.1 collective-permute-done.14.refs_3_
  81.8 9.9 %feed.1 = (bf16[256,768]{1,0:T(8,128)(2,1)}, f32[256,768]{1,0:T(8,128)S(1)}, bf16[256,5376]{1,0:T(8,128)(2,1)S(1)}, bf16[784,256]{1,0:T(8,128)(2,1)S(1)}, bf16[2...) custom-call(s32[6]{0:T(128)S(1)} %stack.38.info.refs_0_, ...), custom_call_target="tpu_custom_call" | custom-call | flops 4831838208 | bytes 9437184 | tf_op jit(solution)/shard_map/feed/pallas_call | solution.py:846
  93.5 2.9 %collective-permute-start.17 = (bf16[192,256]{1,0:T(8,128)(2,1)S(1)}, bf16[192,256]{1,0:T(8,128)(2,1)S(1)}, u32[]{:S(2)}, u32[]{:S(2)}) collective-permute-start(bf16[192,256]{1,0:T(8,128)(2,1)S(1)} %get-tuple-element.108), channel_id=1, source_target_pairs={{0,2},{1,3},{2,4},{3,5},{4,6},{5,7},{6,0},{7,1},{8,10},{9,11},{10,... | collective-permute-start | bytes 294920 | tf_op jit(solution)/shard_map/ppermute | solution.py:818
  97.4 7.4 %weights.1 = (bf16[1,4,176,768]{3,2,1,0:T(8,128)(2,1)S(1)}, bf16[1,4,48,768]{3,2,1,0:T(8,128)(2,1)S(1)}, bf16[2,4,112,768]{3,2,1,0:T(8,128)(2,1)S(1)}, bf16[1,4,...) custom-call(s32[6]{0:T(128)S(1)} %stack.38.info.refs_0_, ...), custom_call_target="tpu_custom_call" | custom-call | flops 4831838208 | bytes 14155776 | tf_op jit(solution)/shard_map/weights/pallas_call | solution.py:846
  104.9 1.3 sums.1.refs_7_
  106.4 1.5 collective-permute-start.21
  107.9 1.5 collective-permute-start.22
  109.4 20.3 %back.1 = (bf16[4,192,256]{2,1,0:T(8,128)(2,1)S(1)}, f32[3,128,1024]{2,1,0:T(8,128)S(1)}, bf16[3,128,1024]{2,1,0:T(8,128)(2,1)S(1)}) custom-call(s32[3,1,2048]{2,1,0:T(1,128)S(1)} %get-tuple-element.84.ids_all.refs_1_, bf16[3,192,2048]{2,1,0:T(8,128)(2,1)S(1)} %get-tuple-element.98.feat, bf16[3,2048,128]{2,1,0:T(8,128)(2,1)S(1)} %get-tuple-element.99.kv, ...), custom_call_target="tpu_custom_call" | custom-call | flops 22548578304 | bytes 10000000 | tf_op jit(solution)/shard_map/back/pallas_call | solution.py:1242
  129.7 2.9 %collective-permute-done.21.got_u.refs_2_ = bf16[1,4,176,768]{3,2,1,0:T(8,128)(2,1)S(1)} collective-permute-done((bf16[1,4,176,768]{3,2,1,0:T(8,128)(2,1)S(1)}, bf16[1,4,176,768]{3,2,1,0:T(8,128)(2,1)S(1)}, u32[]{:S(2)}, u32[]{:S(2)}) %collective-permute-start.21) | collective-permute-done | bytes 1081376 | tf_op jit(solution)/shard_map/ppermute | solution.py:825
  133.8 2.3 collective-permute-done.23.refs_2_
  136.0 2.5 %inward.1 = (bf16[3,192,256]{2,1,0:T(8,128)(2,1)S(1)}, bf16[3,192,256]{2,1,0:T(8,128)(2,1)S(1)}, bf16[3,192,256]{2,1,0:T(8,128)(2,1)S(1)}, bf16[3,192,256]{2,1,0...) custom-call(s32[6]{0:T(128)S(1)} %stack.38.info.refs_0_, ...), custom_call_target="tpu_custom_call" | custom-call | flops 905969664 | bytes 4000000 | tf_op jit(solution)/shard_map/inward/pallas_call | solution.py:846
  138.7 1.9 collective-permute-done.27.inner_got.refs_8_
  141.0 1.6 collective-permute-start.28
  143.1 2.5 %collective-permute-start.25 = (bf16[3,192,256]{2,1,0:T(8,128)(2,1)S(1)}, bf16[3,192,256]{2,1,0:T(8,128)(2,1)S(1)}, u32[]{:S(2)}, u32[]{:S(2)}) collective-permute-start(bf16[3,192,256]{2,1,0:T(8,128)(2,1)S(1)} %get-tuple-element.127), channel_id=1, source_target_pairs={{0,4},{1,5},{2,6},{3,7},{4,0},{5,1},{6,2},{7,3},{8,12},{9,13},{10,... | collective-permute-start | bytes 884744 | tf_op jit(solution)/shard_map/ppermute | solution.py:818
  146.4 6.6 %collective-permute-done.24.refs_1_.refs_11_ = bf16[3,192,256]{2,1,0:T(8,128)(2,1)S(1)} collective-permute-done((bf16[3,192,256]{2,1,0:T(8,128)(2,1)S(1)}, bf16[3,192,256]{2,1,0:T(8,128)(2,1)S(1)}, u32[]{:S(2)}, u32[]{:S(2)}) %collective-permute-start.24) | collective-permute-done | bytes 294944 | tf_op jit(solution)/shard_map/ppermute | solution.py:818
  153.0 1.5 collective-permute-start.30
  154.5 13.9 %collective-permute-done.25.refs_2_.refs_12_ = bf16[3,192,256]{2,1,0:T(8,128)(2,1)S(1)} collective-permute-done((bf16[3,192,256]{2,1,0:T(8,128)(2,1)S(1)}, bf16[3,192,256]{2,1,0:T(8,128)(2,1)S(1)}, u32[]{:S(2)}, u32[]{:S(2)}) %collective-permute-start.25) | collective-permute-done | bytes 294944 | tf_op jit(solution)/shard_map/ppermute | solution.py:818
  168.4 2.7 %collective-permute-done.26.refs_3_.refs_13_ = bf16[3,192,256]{2,1,0:T(8,128)(2,1)S(1)} collective-permute-done((bf16[3,192,256]{2,1,0:T(8,128)(2,1)S(1)}, bf16[3,192,256]{2,1,0:T(8,128)(2,1)S(1)}, u32[]{:S(2)}, u32[]{:S(2)}) %collective-permute-start.26) | collective-permute-done | bytes 294944 | tf_op jit(solution)/shard_map/ppermute | solution.py:818
  173.6 2.5 %collective-permute-start.32 = (bf16[160,768]{1,0:T(8,128)(2,1)S(1)}, bf16[160,768]{1,0:T(8,128)(2,1)S(1)}, u32[]{:S(2)}, u32[]{:S(2)}) collective-permute-start(bf16[160,768]{1,0:T(8,128)(2,1)S(1)} %get-tuple-element.139), channel_id=1, source_target_pairs={{0,4},{1,5},{2,6},{3,7},{4,0},{5,1},{6,2},{7,3},{8,12},{9,13},{10,... | collective-permute-start | bytes 737288 | tf_op jit(solution)/shard_map/ppermute | solution.py:818
  176.9 11.7 %collective-permute-done.31.refs_2_ = bf16[160,768]{1,0:T(8,128)(2,1)S(1)} collective-permute-done((bf16[160,768]{1,0:T(8,128)(2,1)S(1)}, bf16[160,768]{1,0:T(8,128)(2,1)S(1)}, u32[]{:S(2)}, u32[]{:S(2)}) %collective-permute-start.31) | collective-permute-done | bytes 245792 | tf_op jit(solution)/shard_map/ppermute | solution.py:818
  188.5 3.0 %collective-permute-start.34 = (bf16[88,768]{1,0:T(8,128)(2,1)S(1)}, bf16[88,768]{1,0:T(8,128)(2,1)S(1)}, u32[]{:S(2)}, u32[]{:S(2)}) collective-permute-start(bf16[88,768]{1,0:T(8,128)(2,1)S(1)} %get-tuple-element.144), channel_id=1, source_target_pairs={{0,2},{1,3},{2,4},{3,5},{4,6},{5,7},{6,0},{7,1},{8,10},{9,11},{10,... | collective-permute-start | bytes 405512 | tf_op jit(solution)/shard_map/ppermute | solution.py:818
  191.5 2.9 %final.1.refs_6_ = bf16[256,768]{1,0:T(8,128)(2,1)} custom-call(s32[6]{0:T(128)S(1)} %stack.38.info.refs_0_, bf16[3,192,256]{2,1,0:T(8,128)(2,1)S(1)} %get-tuple-element.125.refs_0_.refs_10_, bf16[3,192,256]{2,1,0:T(8,128)(2,1)S(1)} %collective-permute-done.24.refs_1_.refs_11_, bf16[3,192,256]{2,1,0:T(8,128)(2,1)S(1)} %collective-permute-done.25.refs_2_.refs_12_, ...), custom_call_target="tpu_custom_call" | custom-call | flops 905969664 | bytes 3538944 | tf_op jit(solution)/shard_map/final/pallas_call | solution.py:846
  195.5 4.2 %collective-permute-done.33.refs_4_ = bf16[160,768]{1,0:T(8,128)(2,1)S(1)} collective-permute-done((bf16[160,768]{1,0:T(8,128)(2,1)S(1)}, bf16[160,768]{1,0:T(8,128)(2,1)S(1)}, u32[]{:S(2)}, u32[]{:S(2)}) %collective-permute-start.33) | collective-permute-done | bytes 245792 | tf_op jit(solution)/shard_map/ppermute | solution.py:818
  201.9 1.5 collective-permute-start.36
  203.4 1.5 collective-permute-start.37
  207.3 6.0 %collective-permute-done.38.refs_3_ = bf16[88,768]{1,0:T(8,128)(2,1)S(1)} collective-permute-done((bf16[88,768]{1,0:T(8,128)(2,1)S(1)}, bf16[88,768]{1,0:T(8,128)(2,1)S(1)}, u32[]{:S(2)}, u32[]{:S(2)}) %collective-permute-start.38) | collective-permute-done | bytes 135200 | tf_op jit(solution)/shard_map/ppermute | solution.py:818
  213.5 2.0 collective-permute-done.37.refs_8_.refs_3_
  217.0 1.5 collective-permute-start.41
  220.8 3.9 %collective-permute-done.40.refs_5_ = bf16[144,768]{1,0:T(8,128)(2,1)S(1)} collective-permute-done((bf16[144,768]{1,0:T(8,128)(2,1)S(1)}, bf16[144,768]{1,0:T(8,128)(2,1)S(1)}, u32[]{:S(2)}, u32[]{:S(2)}) %collective-permute-start.40) | collective-permute-done | bytes 221216 | tf_op jit(solution)/shard_map/ppermute | solution.py:825
  224.6 3.1 %collective-permute-done.41.refs_6_ = bf16[144,768]{1,0:T(8,128)(2,1)S(1)} collective-permute-done((bf16[144,768]{1,0:T(8,128)(2,1)S(1)}, bf16[144,768]{1,0:T(8,128)(2,1)S(1)}, u32[]{:S(2)}, u32[]{:S(2)}) %collective-permute-start.41) | collective-permute-done | bytes 221216 | tf_op jit(solution)/shard_map/ppermute | solution.py:825
  227.7 3.4 %spread.1 = (f32[96,3072]{1,0:T(8,128)}, f32[96,768]{1,0:T(8,128)}, f32[384,768]{1,0:T(8,128)}, f32[8,768]{1,0:T(8,128)S(1)}, f32[96,768]{1,0:T(8,128)}, /*index=5*/f32[96,1536]{1,0:T(8,128)}, f32[96,128]{1,0:T(8,128)S(1)}) custom-call(s32[6]{0:T(128)S(1)} %stack.38.info.refs_0_, bf16[160,768]{1,0:T(8,128)(2,1)S(1)} %fourth.2.refs_5_.refs_0_, ...), custom_call_target="tpu_custom_call" | custom-call | flops 1000000 | bytes 3538944 | tf_op jit(solution)/shard_map/spread/pallas_call | solution.py:846
  (109 shorter events, 28.7 us)
Async XLA Ops:
  0.7 4.8 %collective-permute-start = (bf16[256,768]{1,0:T(8,128)(2,1)}, bf16[256,768]{1,0:T(8,128)(2,1)S(1)}, u32[]{:S(2)}, u32[]{:S(2)}) collective-permute-start(bf16[256,768]{1,0:T(8,128)(2,1)} %refs_4_.3), channel_id=1, source_target_pairs={{0,1},{1,0},{2,3},{3,2},{4,5},{5,4},{6,7},{7,6},{8,9},{9,8},{10,11... | collective-permute-start | bytes 1179656 | tf_op jit(solution)/shard_map/ppermute | solution.py:822
  6.1 13.5 %collective-permute-start.1 = (s32[3,34,128]{2,1,0:T(8,128)}, s32[3,34,128]{2,1,0:T(8,128)S(1)}, u32[]{:S(2)}, u32[]{:S(2)}) collective-permute-start(s32[3,34,128]{2,1,0:T(8,128)} %get-tuple-element.159), channel_id=1, source_target_pairs={{0,6},{1,7},{2,0},{3,1},{4,2},{5,3},{6,4},{7,5},{8,14},{9,15},{10,... | collective-permute-start | bytes 156680 | tf_op jit(solution)/shard_map/ppermute | solution.py:818
  6.1 13.5 %collective-permute-start.2 = (s32[3,34,128]{2,1,0:T(8,128)S(1)}, s32[3,34,128]{2,1,0:T(8,128)S(1)}, u32[]{:S(2)}, u32[]{:S(2)}) collective-permute-start(s32[3,34,128]{2,1,0:T(8,128)S(1)} %get-tuple-element.158), channel_id=1, source_target_pairs={{0,4},{1,5},{2,6},{3,7},{4,0},{5,1},{6,2},{7,3},{8,12},{9,13},{10,... | collective-permute-start | bytes 156680 | tf_op jit(solution)/shard_map/ppermute | solution.py:818
  9.1 10.5 %collective-permute-start.3 = (s32[3,34,128]{2,1,0:T(8,128)S(1)}, s32[3,34,128]{2,1,0:T(8,128)S(1)}, u32[]{:S(2)}, u32[]{:S(2)}) collective-permute-start(s32[3,34,128]{2,1,0:T(8,128)S(1)} %get-tuple-element.157), channel_id=1, source_target_pairs={{0,2},{1,3},{2,4},{3,5},{4,6},{5,7},{6,0},{7,1},{8,10},{9,11},{10,... | collective-permute-start | bytes 156680 | tf_op jit(solution)/shard_map/ppermute | solution.py:818
  11.6 28.8 %collective-permute-start.7 = (bf16[256,768]{1,0:T(8,128)(2,1)S(1)}, bf16[256,768]{1,0:T(8,128)(2,1)S(1)}, u32[]{:S(2)}, u32[]{:S(2)}) collective-permute-start(bf16[256,768]{1,0:T(8,128)(2,1)S(1)} %copy-done), channel_id=1, source_target_pairs={{0,2},{1,3},{2,4},{3,5},{4,6},{5,7},{6,0},{7,1},{8,10},{9,11},{10,... | collective-permute-start | bytes 1179656 | tf_op jit(solution)/shard_map/ppermute | solution.py:818
  11.7 29.5 %collective-permute-start.9 = (bf16[256,768]{1,0:T(8,128)(2,1)S(1)}, bf16[256,768]{1,0:T(8,128)(2,1)S(1)}, u32[]{:S(2)}, u32[]{:S(2)}) collective-permute-start(bf16[256,768]{1,0:T(8,128)(2,1)S(1)} %copy-done), channel_id=1, source_target_pairs={{0,6},{1,7},{2,0},{3,1},{4,2},{5,3},{6,4},{7,5},{8,14},{9,15},{10,... | collective-permute-start | bytes 1179656 | tf_op jit(solution)/shard_map/ppermute | solution.py:818
  20.2 5.3 %collective-permute-start.4 = (s32[3,40,128]{2,1,0:T(8,128)S(1)}, s32[3,40,128]{2,1,0:T(8,128)S(1)}, u32[]{:S(2)}, u32[]{:S(2)}) collective-permute-start(s32[3,40,128]{2,1,0:T(8,128)S(1)} %table.1.refs_0_), channel_id=1, source_target_pairs={{0,1},{1,0},{2,3},{3,2},{4,5},{5,4},{6,7},{7,6},{8,9},{9,8},{10,11... | collective-permute-start | bytes 184328 | tf_op jit(solution)/shard_map/ppermute | solution.py:822
  20.3 28.2 %collective-permute-start.5 = (bf16[256,768]{1,0:T(8,128)(2,1)S(1)}, bf16[256,768]{1,0:T(8,128)(2,1)S(1)}, u32[]{:S(2)}, u32[]{:S(2)}) collective-permute-start(bf16[256,768]{1,0:T(8,128)(2,1)S(1)} %copy-done), channel_id=1, source_target_pairs={{0,4},{1,5},{2,6},{3,7},{4,0},{5,1},{6,2},{7,3},{8,12},{9,13},{10,... | collective-permute-start | bytes 1179656 | tf_op jit(solution)/shard_map/ppermute | solution.py:818
  21.3 27.2 %collective-permute-start.10 = (bf16[256,768]{1,0:T(8,128)(2,1)S(1)}, bf16[256,768]{1,0:T(8,128)(2,1)S(1)}, u32[]{:S(2)}, u32[]{:S(2)}) collective-permute-start(bf16[256,768]{1,0:T(8,128)(2,1)S(1)} %copy-done.3), channel_id=1, source_target_pairs={{0,1},{1,0},{2,3},{3,2},{4,5},{5,4},{6,7},{7,6},{8,9},{9,8},{10,11... | collective-permute-start | bytes 1179656 | tf_op jit(solution)/shard_map/ppermute | solution.py:822
  48.5 1.7 collective-permute-start.11
  48.5 3.4 %collective-permute-start.8 = (bf16[256,768]{1,0:T(8,128)(2,1)S(1)}, bf16[256,768]{1,0:T(8,128)(2,1)S(1)}, u32[]{:S(2)}, u32[]{:S(2)}) collective-permute-start(bf16[256,768]{1,0:T(8,128)(2,1)S(1)} %collective-permute-done.7.refs_0_), channel_id=1, source_target_pairs={{0,1},{1,0},{2,3},{3,2},{4,5},{5,4},{6,7},{7,6},{8,9},{9,8},{10,11... | collective-permute-start | bytes 1179656 | tf_op jit(solution)/shard_map/ppermute | solution.py:822
  49.1 4.7 %collective-permute-start.6 = (bf16[256,768]{1,0:T(8,128)(2,1)S(1)}, bf16[256,768]{1,0:T(8,128)(2,1)S(1)}, u32[]{:S(2)}, u32[]{:S(2)}) collective-permute-start(bf16[256,768]{1,0:T(8,128)(2,1)S(1)} %collective-permute-done.5.refs_0_), channel_id=1, source_target_pairs={{0,1},{1,0},{2,3},{3,2},{4,5},{5,4},{6,7},{7,6},{8,9},{9,8},{10,11... | collective-permute-start | bytes 1179656 | tf_op jit(solution)/shard_map/ppermute | solution.py:822
  53.7 28.0 %slice-start = ((s8[4718592]{0:T(1024)(128)(4,1)}), s8[4194304]{0:T(1024)(128)(4,1)S(1)}, s32[]{:S(2)}) async-start(s8[4718592]{0:T(1024)(128)(4,1)} %bitcast.37), calls=%async_computation | async-start | bytes 8388608
  53.8 28.0 %slice-start.2 = ((s8[4718592]{0:T(1024)(128)(4,1)}), s8[4194304]{0:T(1024)(128)(4,1)S(1)}, s32[]{:S(2)}) async-start(s8[4718592]{0:T(1024)(128)(4,1)} %bitcast.39), calls=%async_computation.2 | async-start | bytes 8388608
  55.5 26.2 %slice-start.1 = ((s8[4718592]{0:T(1024)(128)(4,1)}), s8[524288]{0:T(1024)(128)(4,1)S(1)}, s32[]{:S(2)}) async-start(s8[4718592]{0:T(1024)(128)(4,1)} %bitcast.37), calls=%async_computation.1 | async-start | bytes 1048576
  55.5 26.2 %slice-start.3 = ((s8[4718592]{0:T(1024)(128)(4,1)}), s8[524288]{0:T(1024)(128)(4,1)S(1)}, s32[]{:S(2)}) async-start(s8[4718592]{0:T(1024)(128)(4,1)} %bitcast.39), calls=%async_computation.3 | async-start | bytes 1048576
  55.5 26.2 %copy-start.2 = (bf16[768,768]{1,0:T(8,128)(2,1)S(1)}, bf16[768,768]{1,0:T(8,128)(2,1)}, u32[]{:S(2)}) copy-start(bf16[768,768]{1,0:T(8,128)(2,1)} %param.22) | copy-start | bytes 3538948
  68.6 5.5 %collective-permute-start.12 = (bf16[192,256]{1,0:T(8,128)(2,1)S(1)}, bf16[192,256]{1,0:T(8,128)(2,1)S(1)}, u32[]{:S(2)}, u32[]{:S(2)}) collective-permute-start(bf16[192,256]{1,0:T(8,128)(2,1)S(1)} %get-tuple-element.101), channel_id=1, source_target_pairs={{0,2},{1,3},{2,4},{3,5},{4,6},{5,7},{6,0},{7,1},{8,10},{9,11},{10,... | collective-permute-start | bytes 294920 | tf_op jit(solution)/shard_map/ppermute | solution.py:818
  69.0 10.6 %collective-permute-start.13 = (bf16[192,256]{1,0:T(8,128)(2,1)S(1)}, bf16[192,256]{1,0:T(8,128)(2,1)S(1)}, u32[]{:S(2)}, u32[]{:S(2)}) collective-permute-start(bf16[192,256]{1,0:T(8,128)(2,1)S(1)} %get-tuple-element.102), channel_id=1, source_target_pairs={{0,4},{1,5},{2,6},{3,7},{4,0},{5,1},{6,2},{7,3},{8,12},{9,13},{10,... | collective-permute-start | bytes 294920 | tf_op jit(solution)/shard_map/ppermute | solution.py:818
  73.3 8.4 %collective-permute-start.14 = (bf16[192,256]{1,0:T(8,128)(2,1)S(1)}, bf16[192,256]{1,0:T(8,128)(2,1)S(1)}, u32[]{:S(2)}, u32[]{:S(2)}) collective-permute-start(bf16[192,256]{1,0:T(8,128)(2,1)S(1)} %get-tuple-element.103), channel_id=1, source_target_pairs={{0,6},{1,7},{2,0},{3,1},{4,2},{5,3},{6,4},{7,5},{8,14},{9,15},{10,... | collective-permute-start | bytes 294920 | tf_op jit(solution)/shard_map/ppermute | solution.py:818
  91.7 5.7 %collective-permute-start.18 = (bf16[256,5376]{1,0:T(8,128)(2,1)S(1)}, bf16[256,5376]{1,0:T(8,128)(2,1)S(1)}, u32[]{:S(2)}, u32[]{:S(2)}) collective-permute-start(bf16[256,5376]{1,0:T(8,128)(2,1)S(1)} %get-tuple-element.112.refs_0_.refs_2_), channel_id=1, source_target_pairs={{0,1},{1,0},{2,3},{3,2},{4,5},{5,4},{6,7},{7,6},{8,9},{9,8},{10,11... | collective-permute-start | bytes 8257544 | tf_op jit(solution)/shard_map/ppermute | solution.py:822
  91.7 5.7 %collective-permute-start.19 = (bf16[784,256]{1,0:T(8,128)(2,1)S(1)}, bf16[784,256]{1,0:T(8,128)(2,1)S(1)}, u32[]{:S(2)}, u32[]{:S(2)}) collective-permute-start(bf16[784,256]{1,0:T(8,128)(2,1)S(1)} %get-tuple-element.115), channel_id=1, source_target_pairs={{0,1},{1,0},{2,3},{3,2},{4,5},{5,4},{6,7},{7,6},{8,9},{9,8},{10,11... | collective-permute-start | bytes 1204232 | tf_op jit(solution)/shard_map/ppermute | solution.py:822
  92.2 12.6 %collective-permute-start.15 = (bf16[192,256]{1,0:T(8,128)(2,1)S(1)}, bf16[192,256]{1,0:T(8,128)(2,1)S(1)}, u32[]{:S(2)}, u32[]{:S(2)}) collective-permute-start(bf16[192,256]{1,0:T(8,128)(2,1)S(1)} %get-tuple-element.106), channel_id=1, source_target_pairs={{0,6},{1,7},{2,0},{3,1},{4,2},{5,3},{6,4},{7,5},{8,14},{9,15},{10,... | collective-permute-start | bytes 294920 | tf_op jit(solution)/shard_map/ppermute | solution.py:818
  92.4 12.5 %collective-permute-start.16 = (bf16[192,256]{1,0:T(8,128)(2,1)S(1)}, bf16[192,256]{1,0:T(8,128)(2,1)S(1)}, u32[]{:S(2)}, u32[]{:S(2)}) collective-permute-start(bf16[192,256]{1,0:T(8,128)(2,1)S(1)} %get-tuple-element.107), channel_id=1, source_target_pairs={{0,4},{1,5},{2,6},{3,7},{4,0},{5,1},{6,2},{7,3},{8,12},{9,13},{10,... | collective-permute-start | bytes 294920 | tf_op jit(solution)/shard_map/ppermute | solution.py:818
  93.5 11.3 %collective-permute-start.17 = (bf16[192,256]{1,0:T(8,128)(2,1)S(1)}, bf16[192,256]{1,0:T(8,128)(2,1)S(1)}, u32[]{:S(2)}, u32[]{:S(2)}) collective-permute-start(bf16[192,256]{1,0:T(8,128)(2,1)S(1)} %get-tuple-element.108), channel_id=1, source_target_pairs={{0,2},{1,3},{2,4},{3,5},{4,6},{5,7},{6,0},{7,1},{8,10},{9,11},{10,... | collective-permute-start | bytes 294920 | tf_op jit(solution)/shard_map/ppermute | solution.py:818
  106.2 3.2 %collective-permute-start.20 = (f32[3,80,128]{2,1,0:T(8,128)S(1)}, f32[3,80,128]{2,1,0:T(8,128)S(1)}, u32[]{:S(2)}, u32[]{:S(2)}) collective-permute-start(f32[3,80,128]{2,1,0:T(8,128)S(1)} %sums.1.refs_7_), channel_id=1, source_target_pairs={{0,1},{1,0},{2,3},{3,2},{4,5},{5,4},{6,7},{7,6},{8,9},{9,8},{10,11... | collective-permute-start | bytes 368648 | tf_op jit(solution)/shard_map/ppermute | solution.py:822
  106.4 26.2 %collective-permute-start.21 = (bf16[1,4,176,768]{3,2,1,0:T(8,128)(2,1)S(1)}, bf16[1,4,176,768]{3,2,1,0:T(8,128)(2,1)S(1)}, u32[]{:S(2)}, u32[]{:S(2)}) collective-permute-start(bf16[1,4,176,768]{3,2,1,0:T(8,128)(2,1)S(1)} %get-tuple-element.121), channel_id=1, source_target_pairs={{0,8},{8,0},{16,24},{24,16},{1,9},{9,1},{17,25},{25,17},{2,10},{10... | collective-permute-start | bytes 3244040 | tf_op jit(solution)/shard_map/ppermute | solution.py:825
  107.9 25.8 %collective-permute-start.22 = (bf16[1,4,176,768]{3,2,1,0:T(8,128)(2,1)S(1)}, bf16[1,4,176,768]{3,2,1,0:T(8,128)(2,1)S(1)}, u32[]{:S(2)}, u32[]{:S(2)}) collective-permute-start(bf16[1,4,176,768]{3,2,1,0:T(8,128)(2,1)S(1)} %get-tuple-element.122), channel_id=1, source_target_pairs={{0,16},{8,24},{16,0},{24,8},{1,17},{9,25},{17,1},{25,9},{2,18},{10... | collective-permute-start | bytes 3244040 | tf_op jit(solution)/shard_map/ppermute | solution.py:825
  133.8 2.3 collective-permute-start.23
  138.5 2.1 collective-permute-start.27
  141.0 31.4 %collective-permute-start.28 = (bf16[4,184,768]{2,1,0:T(8,128)(2,1)S(1)}, bf16[4,184,768]{2,1,0:T(8,128)(2,1)S(1)}, u32[]{:S(2)}, u32[]{:S(2)}) collective-permute-start(bf16[4,184,768]{2,1,0:T(8,128)(2,1)S(1)} %get-tuple-element.134), channel_id=1, source_target_pairs={{0,16},{8,24},{16,0},{24,8},{1,17},{9,25},{17,1},{25,9},{2,18},{10... | collective-permute-start | bytes 3391496 | tf_op jit(solution)/shard_map/ppermute | solution.py:825
  142.6 29.8 %collective-permute-start.29 = (bf16[4,184,768]{2,1,0:T(8,128)(2,1)S(1)}, bf16[4,184,768]{2,1,0:T(8,128)(2,1)S(1)}, u32[]{:S(2)}, u32[]{:S(2)}) collective-permute-start(bf16[4,184,768]{2,1,0:T(8,128)(2,1)S(1)} %get-tuple-element.135), channel_id=1, source_target_pairs={{0,8},{8,0},{16,24},{24,16},{1,9},{9,1},{17,25},{25,17},{2,10},{10... | collective-permute-start | bytes 3391496 | tf_op jit(solution)/shard_map/ppermute | solution.py:825
  143.1 9.9 %collective-permute-start.24 = (bf16[3,192,256]{2,1,0:T(8,128)(2,1)S(1)}, bf16[3,192,256]{2,1,0:T(8,128)(2,1)S(1)}, u32[]{:S(2)}, u32[]{:S(2)}) collective-permute-start(bf16[3,192,256]{2,1,0:T(8,128)(2,1)S(1)} %get-tuple-element.126), channel_id=1, source_target_pairs={{0,2},{1,3},{2,4},{3,5},{4,6},{5,7},{6,0},{7,1},{8,10},{9,11},{10,... | collective-permute-start | bytes 884744 | tf_op jit(solution)/shard_map/ppermute | solution.py:818
  143.1 25.2 %collective-permute-start.25 = (bf16[3,192,256]{2,1,0:T(8,128)(2,1)S(1)}, bf16[3,192,256]{2,1,0:T(8,128)(2,1)S(1)}, u32[]{:S(2)}, u32[]{:S(2)}) collective-permute-start(bf16[3,192,256]{2,1,0:T(8,128)(2,1)S(1)} %get-tuple-element.127), channel_id=1, source_target_pairs={{0,4},{1,5},{2,6},{3,7},{4,0},{5,1},{6,2},{7,3},{8,12},{9,13},{10,... | collective-permute-start | bytes 884744 | tf_op jit(solution)/shard_map/ppermute | solution.py:818
  145.6 25.5 %collective-permute-start.26 = (bf16[3,192,256]{2,1,0:T(8,128)(2,1)S(1)}, bf16[3,192,256]{2,1,0:T(8,128)(2,1)S(1)}, u32[]{:S(2)}, u32[]{:S(2)}) collective-permute-start(bf16[3,192,256]{2,1,0:T(8,128)(2,1)S(1)} %get-tuple-element.128), channel_id=1, source_target_pairs={{0,6},{1,7},{2,0},{3,1},{4,2},{5,3},{6,4},{7,5},{8,14},{9,15},{10,... | collective-permute-start | bytes 884744 | tf_op jit(solution)/shard_map/ppermute | solution.py:818
  153.0 19.3 %collective-permute-start.30 = (bf16[4,24,768]{2,1,0:T(8,128)(2,1)S(1)}, bf16[4,24,768]{2,1,0:T(8,128)(2,1)S(1)}, u32[]{:S(2)}, u32[]{:S(2)}) collective-permute-start(bf16[4,24,768]{2,1,0:T(8,128)(2,1)S(1)} %get-tuple-element.136), channel_id=1, source_target_pairs={{0,24},{8,16},{16,8},{24,0},{1,25},{9,17},{17,9},{25,1},{2,26},{10... | collective-permute-start | bytes 442376 | tf_op jit(solution)/shard_map/ppermute | solution.py:825
  173.5 15.0 %collective-permute-start.31 = (bf16[160,768]{1,0:T(8,128)(2,1)S(1)}, bf16[160,768]{1,0:T(8,128)(2,1)S(1)}, u32[]{:S(2)}, u32[]{:S(2)}) collective-permute-start(bf16[160,768]{1,0:T(8,128)(2,1)S(1)} %get-tuple-element.138), channel_id=1, source_target_pairs={{0,2},{1,3},{2,4},{3,5},{4,6},{5,7},{6,0},{7,1},{8,10},{9,11},{10,... | collective-permute-start | bytes 737288 | tf_op jit(solution)/shard_map/ppermute | solution.py:818
  173.6 21.9 %collective-permute-start.32 = (bf16[160,768]{1,0:T(8,128)(2,1)S(1)}, bf16[160,768]{1,0:T(8,128)(2,1)S(1)}, u32[]{:S(2)}, u32[]{:S(2)}) collective-permute-start(bf16[160,768]{1,0:T(8,128)(2,1)S(1)} %get-tuple-element.139), channel_id=1, source_target_pairs={{0,4},{1,5},{2,6},{3,7},{4,0},{5,1},{6,2},{7,3},{8,12},{9,13},{10,... | collective-permute-start | bytes 737288 | tf_op jit(solution)/shard_map/ppermute | solution.py:818
  176.1 23.6 %collective-permute-start.33 = (bf16[160,768]{1,0:T(8,128)(2,1)S(1)}, bf16[160,768]{1,0:T(8,128)(2,1)S(1)}, u32[]{:S(2)}, u32[]{:S(2)}) collective-permute-start(bf16[160,768]{1,0:T(8,128)(2,1)S(1)} %get-tuple-element.140), channel_id=1, source_target_pairs={{0,6},{1,7},{2,0},{3,1},{4,2},{5,3},{6,4},{7,5},{8,14},{9,15},{10,... | collective-permute-start | bytes 737288 | tf_op jit(solution)/shard_map/ppermute | solution.py:818
  188.5 11.1 %collective-permute-start.34 = (bf16[88,768]{1,0:T(8,128)(2,1)S(1)}, bf16[88,768]{1,0:T(8,128)(2,1)S(1)}, u32[]{:S(2)}, u32[]{:S(2)}) collective-permute-start(bf16[88,768]{1,0:T(8,128)(2,1)S(1)} %get-tuple-element.144), channel_id=1, source_target_pairs={{0,2},{1,3},{2,4},{3,5},{4,6},{5,7},{6,0},{7,1},{8,10},{9,11},{10,... | collective-permute-start | bytes 405512 | tf_op jit(solution)/shard_map/ppermute | solution.py:818
  201.3 12.2 %collective-permute-start.35 = (bf16[160,768]{1,0:T(8,128)(2,1)S(1)}, bf16[160,768]{1,0:T(8,128)(2,1)S(1)}, u32[]{:S(2)}, u32[]{:S(2)}) collective-permute-start(bf16[160,768]{1,0:T(8,128)(2,1)S(1)} %fourth.2.refs_5_.refs_0_), channel_id=1, source_target_pairs={{0,8},{8,0},{16,24},{24,16},{1,9},{9,1},{17,25},{25,17},{2,10},{10... | collective-permute-start | bytes 737288 | tf_op jit(solution)/shard_map/ppermute | solution.py:825
  201.9 11.6 %collective-permute-start.36 = (bf16[160,768]{1,0:T(8,128)(2,1)S(1)}, bf16[160,768]{1,0:T(8,128)(2,1)S(1)}, u32[]{:S(2)}, u32[]{:S(2)}) collective-permute-start(bf16[160,768]{1,0:T(8,128)(2,1)S(1)} %fourth.2.refs_5_.refs_0_), channel_id=1, source_target_pairs={{0,16},{8,24},{16,0},{24,8},{1,17},{9,25},{17,1},{25,9},{2,18},{10... | collective-permute-start | bytes 737288 | tf_op jit(solution)/shard_map/ppermute | solution.py:825
  203.4 12.1 %collective-permute-start.37 = (bf16[160,768]{1,0:T(8,128)(2,1)S(1)}, bf16[160,768]{1,0:T(8,128)(2,1)S(1)}, u32[]{:S(2)}, u32[]{:S(2)}) collective-permute-start(bf16[160,768]{1,0:T(8,128)(2,1)S(1)} %fourth.2.refs_5_.refs_0_), channel_id=1, source_target_pairs={{0,24},{8,16},{16,8},{24,0},{1,25},{9,17},{17,9},{25,1},{2,26},{10... | collective-permute-start | bytes 737288 | tf_op jit(solution)/shard_map/ppermute | solution.py:825
  204.9 8.3 %collective-permute-start.38 = (bf16[88,768]{1,0:T(8,128)(2,1)S(1)}, bf16[88,768]{1,0:T(8,128)(2,1)S(1)}, u32[]{:S(2)}, u32[]{:S(2)}) collective-permute-start(bf16[88,768]{1,0:T(8,128)(2,1)S(1)} %get-tuple-element.146), channel_id=1, source_target_pairs={{0,4},{1,5},{2,6},{3,7},{4,0},{5,1},{6,2},{7,3},{8,12},{9,13},{10,... | collective-permute-start | bytes 405512 | tf_op jit(solution)/shard_map/ppermute | solution.py:818
  205.0 8.5 %collective-permute-start.39 = (bf16[88,768]{1,0:T(8,128)(2,1)S(1)}, bf16[88,768]{1,0:T(8,128)(2,1)S(1)}, u32[]{:S(2)}, u32[]{:S(2)}) collective-permute-start(bf16[88,768]{1,0:T(8,128)(2,1)S(1)} %get-tuple-element.147), channel_id=1, source_target_pairs={{0,6},{1,7},{2,0},{3,1},{4,2},{5,3},{6,4},{7,5},{8,14},{9,15},{10,... | collective-permute-start | bytes 405512 | tf_op jit(solution)/shard_map/ppermute | solution.py:818
  216.2 8.4 %collective-permute-start.40 = (bf16[144,768]{1,0:T(8,128)(2,1)S(1)}, bf16[144,768]{1,0:T(8,128)(2,1)S(1)}, u32[]{:S(2)}, u32[]{:S(2)}) collective-permute-start(bf16[144,768]{1,0:T(8,128)(2,1)S(1)} %fourth.3.refs_4_), channel_id=1, source_target_pairs={{0,8},{8,0},{16,24},{24,16},{1,9},{9,1},{17,25},{25,17},{2,10},{10... | collective-permute-start | bytes 663560 | tf_op jit(solution)/shard_map/ppermute | solution.py:825
  217.0 10.7 %collective-permute-start.41 = (bf16[144,768]{1,0:T(8,128)(2,1)S(1)}, bf16[144,768]{1,0:T(8,128)(2,1)S(1)}, u32[]{:S(2)}, u32[]{:S(2)}) collective-permute-start(bf16[144,768]{1,0:T(8,128)(2,1)S(1)} %fourth.3.refs_4_), channel_id=1, source_target_pairs={{0,16},{8,24},{16,0},{24,8},{1,17},{9,25},{17,1},{25,9},{2,18},{10... | collective-permute-start | bytes 663560 | tf_op jit(solution)/shard_map/ppermute | solution.py:825
  218.6 9.2 %collective-permute-start.42 = (bf16[144,768]{1,0:T(8,128)(2,1)S(1)}, bf16[144,768]{1,0:T(8,128)(2,1)S(1)}, u32[]{:S(2)}, u32[]{:S(2)}) collective-permute-start(bf16[144,768]{1,0:T(8,128)(2,1)S(1)} %fourth.3.refs_4_), channel_id=1, source_target_pairs={{0,24},{8,16},{16,8},{24,0},{1,25},{9,17},{17,9},{25,1},{2,26},{10... | collective-permute-start | bytes 663560 | tf_op jit(solution)/shard_map/ppermute | solution.py:825
  (7 other events, 58.7 us)

commit v11 on v10

--- a/solution.py
+++ b/solution.py
@@ -856,10 +856,9 @@
 
     position = me * rows + jnp.arange(rows, dtype=jnp.int32)
     marked = jnp.where((position < seq_len)[:, None], cluster_ids, -1).T
-    tops = jnp.zeros((heads, picks, clusters), jnp.int32)
-    tops = lax.dynamic_update_slice(
-        tops, top_keys[0].transpose(0, 2, 1), (0, 0, me * own_clusters)
-    )
+    tops = top_keys[0].transpose(0, 2, 1)[:, :, None, :]
+    mine_lanes = (jnp.arange(wide, dtype=jnp.int32) == me)[None, None, :, None]
+    tops = jnp.where(mine_lanes, tops, 0).reshape(heads, picks, clusters)
     lines = rows // clusters
     packed = jnp.concatenate([tops, marked.reshape(heads, lines, clusters)], axis=1)
     near = [along_peers(tokens, -hop) for hop in range(1, peers)]

time: 233 us -> 231 us (level)
    unnamed x27 -> x31, local copies, waits for them, and re-layouts: 7.05 us -> 7.7 us
where the time goes in v11:
time: 231 us; the launch traced here: 230 us
  waiting for transfers between devices  89.5 us (39%)
  Pallas kernels  78.7 us (34%)
  starting transfers between devices  44.2 us (19%)
  local copies, waits for them, and re-layouts  11.2 us (5%)
  other arithmetic  4.72 us (2%)
    ppermute x21, waiting for transfers between devices, along_groups(): return lax.ppermute(values, 'wide', pairs)  68.7 us
    pallas_call x15, Pallas kernels, prefetched(): return lambda *inputs: call(*inputs, *first)  45 us
    ppermute x21, starting transfers between devices, along_groups(): return lax.ppermute(values, 'wide', pairs)  28.7 us
    pallas_call x1, Pallas kernels, per_device(): pl.pallas_call(functools.partial(back_kernel, size=size, groups=groups, g...  20.2 us
    ppermute x11, waiting for transfers between devices, along_dp(): return lax.ppermute(values, 'dp', [(i, i ^ mask) for i in range(n_dp)])  14.3 us
    ppermute x11, starting transfers between devices, along_dp(): return lax.ppermute(values, 'dp', [(i, i ^ mask) for i in range(n_dp)])  13.7 us
    pallas_call x1, Pallas kernels, per_device(): pl.pallas_call(functools.partial(forward_kernel, size=size, groups=groups...  13 us
    unnamed x31, local copies, waits for them, and re-layouts  7.7 us
  transfers between devices with their start and end apart: 43, of which 23 were waited for; matrix products, arithmetic and copies ran while one was open for 6% of the time, Pallas kernels for 19%

profile of v11, /device:TPU:8, one launch (start us, length us, event | category | flops | bytes accessed | tf_op | source)
XLA Modules:
  0.0 230.2 jit_solution(14867796773741223141)
XLA Ops:
  4.0 3.0 %collective-permute-start.2 = (s32[3,34,128]{2,1,0:T(8,128)S(1)}, s32[3,34,128]{2,1,0:T(8,128)S(1)}, u32[]{:S(2)}, u32[]{:S(2)}) collective-permute-start(s32[3,34,128]{2,1,0:T(8,128)S(1)} %bitcast.51), channel_id=1, source_target_pairs={{0,4},{1,5},{2,6},{3,7},{4,0},{5,1},{6,2},{7,3},{8,12},{9,13},{10,... | collective-permute-start | bytes 156680 | tf_op jit(solution)/shard_map/ppermute | solution.py:818
  7.7 2.5 %collective-permute-start.3 = (s32[3,34,128]{2,1,0:T(8,128)}, s32[3,34,128]{2,1,0:T(8,128)S(1)}, u32[]{:S(2)}, u32[]{:S(2)}) collective-permute-start(s32[3,34,128]{2,1,0:T(8,128)} %bitcast.31), channel_id=1, source_target_pairs={{0,2},{1,3},{2,4},{3,5},{4,6},{5,7},{6,0},{7,1},{8,10},{9,11},{10,... | collective-permute-start | bytes 156680 | tf_op jit(solution)/shard_map/ppermute | solution.py:818
  10.2 2.0 collective-permute-start.9
  12.2 4.3 %copy.70 = bf16[768,1536]{0,1:T(8,128)(2,1)} copy(bf16[768,1536]{1,0:T(8,128)(2,1)} %param.21) | data formatting | bytes 4718592 | tf_op args[7]
  16.5 1.6 copy.69
  20.0 1.9 pad_maximum_fusion
  22.3 1.7 project.4
  24.1 7.6 %bias.1 = (bf16[3,2048,128]{2,1,0:T(8,128)(2,1)S(1)}, s32[3,1,2048]{2,1,0:T(1,128)S(1)}) custom-call(s32[6]{0:T(128)S(1)} %stack.38.info.refs_0_, s32[3,40,128]{2,1,0:T(8,128)S(1)} %table.1.refs_0_, s32[3,40,128]{2,1,0:T(8,128)S(1)} %collective-permute-done.4.refs_1_), custom_call_target="tpu_custom_call" | custom-call | flops 201326592 | bytes 1572864 | tf_op jit(solution)/shard_map/bias/pallas_call | solution.py:846
  31.7 6.8 %collective-permute-done.7.refs_0_ = bf16[256,768]{1,0:T(8,128)(2,1)S(1)} collective-permute-done((bf16[256,768]{1,0:T(8,128)(2,1)S(1)}, bf16[256,768]{1,0:T(8,128)(2,1)S(1)}, u32[]{:S(2)}, u32[]{:S(2)}) %collective-permute-start.7) | collective-permute-done | bytes 393248 | tf_op jit(solution)/shard_map/ppermute | solution.py:818
  38.6 7.9 %collective-permute-done.5.refs_0_ = bf16[256,768]{1,0:T(8,128)(2,1)S(1)} collective-permute-done((bf16[256,768]{1,0:T(8,128)(2,1)S(1)}, bf16[256,768]{1,0:T(8,128)(2,1)S(1)}, u32[]{:S(2)}, u32[]{:S(2)}) %collective-permute-start.5) | collective-permute-done | bytes 393248 | tf_op jit(solution)/shard_map/ppermute | solution.py:818
  48.1 1.7 project.5
  49.9 1.7 project.6
  51.7 1.7 project.7
  53.4 13.0 %attend.1 = (bf16[192,256]{1,0:T(8,128)(2,1)S(1)}, bf16[192,256]{1,0:T(8,128)(2,1)S(1)}, bf16[192,256]{1,0:T(8,128)(2,1)S(1)}, bf16[192,256]{1,0:T(8,128)(2,1)S(...) custom-call(s32[3,1,2048]{2,1,0:T(1,128)S(1)} %get-tuple-element.84.ids_all.refs_1_, ...), custom_call_target="tpu_custom_call" | custom-call | flops 9663676416 | bytes 8000000 | tf_op jit(solution)/shard_map/attend/pallas_call | solution.py:984
  66.7 4.3 %collective-permute-start.13 = (bf16[192,256]{1,0:T(8,128)(2,1)S(1)}, bf16[192,256]{1,0:T(8,128)(2,1)S(1)}, u32[]{:S(2)}, u32[]{:S(2)}) collective-permute-start(bf16[192,256]{1,0:T(8,128)(2,1)S(1)} %get-tuple-element.102), channel_id=1, source_target_pairs={{0,4},{1,5},{2,6},{3,7},{4,0},{5,1},{6,2},{7,3},{8,12},{9,13},{10,... | collective-permute-start | bytes 294920 | tf_op jit(solution)/shard_map/ppermute | solution.py:818
  72.0 5.3 %collective-permute-done.13.refs_2_ = bf16[192,256]{1,0:T(8,128)(2,1)S(1)} collective-permute-done((bf16[192,256]{1,0:T(8,128)(2,1)S(1)}, bf16[192,256]{1,0:T(8,128)(2,1)S(1)}, u32[]{:S(2)}, u32[]{:S(2)}) %collective-permute-start.13) | collective-permute-done | bytes 98336 | tf_op jit(solution)/shard_map/ppermute | solution.py:818
  77.3 2.3 collective-permute-done.14.refs_3_
  79.6 10.0 %feed.1 = (bf16[256,768]{1,0:T(8,128)(2,1)}, f32[256,768]{1,0:T(8,128)S(1)}, bf16[256,5376]{1,0:T(8,128)(2,1)S(1)}, bf16[784,256]{1,0:T(8,128)(2,1)S(1)}, bf16[2...) custom-call(s32[6]{0:T(128)S(1)} %stack.38.info.refs_0_, ...), custom_call_target="tpu_custom_call" | custom-call | flops 4831838208 | bytes 9437184 | tf_op jit(solution)/shard_map/feed/pallas_call | solution.py:846
  91.2 2.9 %collective-permute-start.17 = (bf16[192,256]{1,0:T(8,128)(2,1)S(1)}, bf16[192,256]{1,0:T(8,128)(2,1)S(1)}, u32[]{:S(2)}, u32[]{:S(2)}) collective-permute-start(bf16[192,256]{1,0:T(8,128)(2,1)S(1)} %get-tuple-element.108), channel_id=1, source_target_pairs={{0,2},{1,3},{2,4},{3,5},{4,6},{5,7},{6,0},{7,1},{8,10},{9,11},{10,... | collective-permute-start | bytes 294920 | tf_op jit(solution)/shard_map/ppermute | solution.py:818
  95.3 7.4 %weights.1 = (bf16[1,4,176,768]{3,2,1,0:T(8,128)(2,1)S(1)}, bf16[1,4,48,768]{3,2,1,0:T(8,128)(2,1)S(1)}, bf16[2,4,112,768]{3,2,1,0:T(8,128)(2,1)S(1)}, bf16[1,4,...) custom-call(s32[6]{0:T(128)S(1)} %stack.38.info.refs_0_, ...), custom_call_target="tpu_custom_call" | custom-call | flops 4831838208 | bytes 14155776 | tf_op jit(solution)/shard_map/weights/pallas_call | solution.py:846
  104.3 1.5 collective-permute-start.21
  105.7 1.6 collective-permute-start.22
  107.3 20.2 %back.1 = (bf16[4,192,256]{2,1,0:T(8,128)(2,1)S(1)}, f32[3,128,1024]{2,1,0:T(8,128)S(1)}, bf16[3,128,1024]{2,1,0:T(8,128)(2,1)S(1)}) custom-call(s32[3,1,2048]{2,1,0:T(1,128)S(1)} %get-tuple-element.84.ids_all.refs_1_, bf16[3,192,2048]{2,1,0:T(8,128)(2,1)S(1)} %get-tuple-element.98.feat, bf16[3,2048,128]{2,1,0:T(8,128)(2,1)S(1)} %get-tuple-element.99.kv, ...), custom_call_target="tpu_custom_call" | custom-call | flops 22548578304 | bytes 10000000 | tf_op jit(solution)/shard_map/back/pallas_call | solution.py:1241
  127.6 2.8 %collective-permute-done.21.got_u.refs_2_ = bf16[1,4,176,768]{3,2,1,0:T(8,128)(2,1)S(1)} collective-permute-done((bf16[1,4,176,768]{3,2,1,0:T(8,128)(2,1)S(1)}, bf16[1,4,176,768]{3,2,1,0:T(8,128)(2,1)S(1)}, u32[]{:S(2)}, u32[]{:S(2)}) %collective-permute-start.21) | collective-permute-done | bytes 1081376 | tf_op jit(solution)/shard_map/ppermute | solution.py:825
  131.6 2.3 collective-permute-done.23.refs_2_
  133.9 2.5 %inward.1 = (bf16[3,192,256]{2,1,0:T(8,128)(2,1)S(1)}, bf16[3,192,256]{2,1,0:T(8,128)(2,1)S(1)}, bf16[3,192,256]{2,1,0:T(8,128)(2,1)S(1)}, bf16[3,192,256]{2,1,0...) custom-call(s32[6]{0:T(128)S(1)} %stack.38.info.refs_0_, ...), custom_call_target="tpu_custom_call" | custom-call | flops 905969664 | bytes 4000000 | tf_op jit(solution)/shard_map/inward/pallas_call | solution.py:846
  136.5 1.9 collective-permute-done.27.inner_got.refs_8_
  138.8 1.6 collective-permute-start.28
  141.0 2.3 %collective-permute-start.25 = (bf16[3,192,256]{2,1,0:T(8,128)(2,1)S(1)}, bf16[3,192,256]{2,1,0:T(8,128)(2,1)S(1)}, u32[]{:S(2)}, u32[]{:S(2)}) collective-permute-start(bf16[3,192,256]{2,1,0:T(8,128)(2,1)S(1)} %get-tuple-element.127), channel_id=1, source_target_pairs={{0,4},{1,5},{2,6},{3,7},{4,0},{5,1},{6,2},{7,3},{8,12},{9,13},{10,... | collective-permute-start | bytes 884744 | tf_op jit(solution)/shard_map/ppermute | solution.py:818
  144.1 6.8 %collective-permute-done.24.refs_1_.refs_11_ = bf16[3,192,256]{2,1,0:T(8,128)(2,1)S(1)} collective-permute-done((bf16[3,192,256]{2,1,0:T(8,128)(2,1)S(1)}, bf16[3,192,256]{2,1,0:T(8,128)(2,1)S(1)}, u32[]{:S(2)}, u32[]{:S(2)}) %collective-permute-start.24) | collective-permute-done | bytes 294944 | tf_op jit(solution)/shard_map/ppermute | solution.py:818
  150.9 1.4 collective-permute-start.30
  152.3 13.9 %collective-permute-done.25.refs_2_.refs_12_ = bf16[3,192,256]{2,1,0:T(8,128)(2,1)S(1)} collective-permute-done((bf16[3,192,256]{2,1,0:T(8,128)(2,1)S(1)}, bf16[3,192,256]{2,1,0:T(8,128)(2,1)S(1)}, u32[]{:S(2)}, u32[]{:S(2)}) %collective-permute-start.25) | collective-permute-done | bytes 294944 | tf_op jit(solution)/shard_map/ppermute | solution.py:818
  166.3 2.6 %collective-permute-done.26.refs_3_.refs_13_ = bf16[3,192,256]{2,1,0:T(8,128)(2,1)S(1)} collective-permute-done((bf16[3,192,256]{2,1,0:T(8,128)(2,1)S(1)}, bf16[3,192,256]{2,1,0:T(8,128)(2,1)S(1)}, u32[]{:S(2)}, u32[]{:S(2)}) %collective-permute-start.26) | collective-permute-done | bytes 294944 | tf_op jit(solution)/shard_map/ppermute | solution.py:818
  168.8 1.4 collective-permute-done.30.refs_9_
  171.4 2.4 %collective-permute-start.32 = (bf16[160,768]{1,0:T(8,128)(2,1)S(1)}, bf16[160,768]{1,0:T(8,128)(2,1)S(1)}, u32[]{:S(2)}, u32[]{:S(2)}) collective-permute-start(bf16[160,768]{1,0:T(8,128)(2,1)S(1)} %get-tuple-element.139), channel_id=1, source_target_pairs={{0,4},{1,5},{2,6},{3,7},{4,0},{5,1},{6,2},{7,3},{8,12},{9,13},{10,... | collective-permute-start | bytes 737288 | tf_op jit(solution)/shard_map/ppermute | solution.py:818
  174.5 11.8 %collective-permute-done.31.refs_2_ = bf16[160,768]{1,0:T(8,128)(2,1)S(1)} collective-permute-done((bf16[160,768]{1,0:T(8,128)(2,1)S(1)}, bf16[160,768]{1,0:T(8,128)(2,1)S(1)}, u32[]{:S(2)}, u32[]{:S(2)}) %collective-permute-start.31) | collective-permute-done | bytes 245792 | tf_op jit(solution)/shard_map/ppermute | solution.py:818
  186.3 3.0 %collective-permute-start.34 = (bf16[88,768]{1,0:T(8,128)(2,1)S(1)}, bf16[88,768]{1,0:T(8,128)(2,1)S(1)}, u32[]{:S(2)}, u32[]{:S(2)}) collective-permute-start(bf16[88,768]{1,0:T(8,128)(2,1)S(1)} %get-tuple-element.144), channel_id=1, source_target_pairs={{0,2},{1,3},{2,4},{3,5},{4,6},{5,7},{6,0},{7,1},{8,10},{9,11},{10,... | collective-permute-start | bytes 405512 | tf_op jit(solution)/shard_map/ppermute | solution.py:818
  189.3 2.9 %final.1.refs_6_ = bf16[256,768]{1,0:T(8,128)(2,1)} custom-call(s32[6]{0:T(128)S(1)} %stack.38.info.refs_0_, bf16[3,192,256]{2,1,0:T(8,128)(2,1)S(1)} %get-tuple-element.125.refs_0_.refs_10_, bf16[3,192,256]{2,1,0:T(8,128)(2,1)S(1)} %collective-permute-done.24.refs_1_.refs_11_, bf16[3,192,256]{2,1,0:T(8,128)(2,1)S(1)} %collective-permute-done.25.refs_2_.refs_12_, ...), custom_call_target="tpu_custom_call" | custom-call | flops 905969664 | bytes 3538944 | tf_op jit(solution)/shard_map/final/pallas_call | solution.py:846
  193.3 4.0 %collective-permute-done.33.refs_4_ = bf16[160,768]{1,0:T(8,128)(2,1)S(1)} collective-permute-done((bf16[160,768]{1,0:T(8,128)(2,1)S(1)}, bf16[160,768]{1,0:T(8,128)(2,1)S(1)}, u32[]{:S(2)}, u32[]{:S(2)}) %collective-permute-start.33) | collective-permute-done | bytes 245792 | tf_op jit(solution)/shard_map/ppermute | solution.py:818
  199.6 1.6 collective-permute-start.36
  201.1 1.4 collective-permute-start.37
  202.7 1.3 collective-permute-start.39
  205.1 5.8 %collective-permute-done.38.refs_3_ = bf16[88,768]{1,0:T(8,128)(2,1)S(1)} collective-permute-done((bf16[88,768]{1,0:T(8,128)(2,1)S(1)}, bf16[88,768]{1,0:T(8,128)(2,1)S(1)}, u32[]{:S(2)}, u32[]{:S(2)}) %collective-permute-start.38) | collective-permute-done | bytes 135200 | tf_op jit(solution)/shard_map/ppermute | solution.py:818
  211.6 1.6 collective-permute-done.37.refs_8_.refs_3_
  214.7 1.5 collective-permute-start.41
  218.4 3.9 %collective-permute-done.40.refs_5_ = bf16[144,768]{1,0:T(8,128)(2,1)S(1)} collective-permute-done((bf16[144,768]{1,0:T(8,128)(2,1)S(1)}, bf16[144,768]{1,0:T(8,128)(2,1)S(1)}, u32[]{:S(2)}, u32[]{:S(2)}) %collective-permute-start.40) | collective-permute-done | bytes 221216 | tf_op jit(solution)/shard_map/ppermute | solution.py:825
  222.2 3.2 %collective-permute-done.41.refs_6_ = bf16[144,768]{1,0:T(8,128)(2,1)S(1)} collective-permute-done((bf16[144,768]{1,0:T(8,128)(2,1)S(1)}, bf16[144,768]{1,0:T(8,128)(2,1)S(1)}, u32[]{:S(2)}, u32[]{:S(2)}) %collective-permute-start.41) | collective-permute-done | bytes 221216 | tf_op jit(solution)/shard_map/ppermute | solution.py:825
  225.5 3.4 %spread.1 = (f32[96,3072]{1,0:T(8,128)}, f32[96,768]{1,0:T(8,128)}, f32[384,768]{1,0:T(8,128)}, f32[8,768]{1,0:T(8,128)S(1)}, f32[96,768]{1,0:T(8,128)}, /*index=5*/f32[96,1536]{1,0:T(8,128)}, f32[96,128]{1,0:T(8,128)S(1)}) custom-call(s32[6]{0:T(128)S(1)} %stack.38.info.refs_0_, bf16[160,768]{1,0:T(8,128)(2,1)S(1)} %fourth.2.refs_5_.refs_0_, ...), custom_call_target="tpu_custom_call" | custom-call | flops 1000000 | bytes 3538944 | tf_op jit(solution)/shard_map/spread/pallas_call | solution.py:846
  (117 shorter events, 28.0 us)
Async XLA Ops:
  0.6 3.1 %collective-permute-start = (bf16[256,768]{1,0:T(8,128)(2,1)}, bf16[256,768]{1,0:T(8,128)(2,1)S(1)}, u32[]{:S(2)}, u32[]{:S(2)}) collective-permute-start(bf16[256,768]{1,0:T(8,128)(2,1)} %refs_4_.3), channel_id=1, source_target_pairs={{0,1},{1,0},{2,3},{3,2},{4,5},{5,4},{6,7},{7,6},{8,9},{9,8},{10,11... | collective-permute-start | bytes 1179656 | tf_op jit(solution)/shard_map/ppermute | solution.py:822
  4.0 14.2 %collective-permute-start.1 = (s32[3,34,128]{2,1,0:T(8,128)S(1)}, s32[3,34,128]{2,1,0:T(8,128)S(1)}, u32[]{:S(2)}, u32[]{:S(2)}) collective-permute-start(s32[3,34,128]{2,1,0:T(8,128)S(1)} %bitcast.50), channel_id=1, source_target_pairs={{0,6},{1,7},{2,0},{3,1},{4,2},{5,3},{6,4},{7,5},{8,14},{9,15},{10,... | collective-permute-start | bytes 156680 | tf_op jit(solution)/shard_map/ppermute | solution.py:818
  4.0 14.2 %collective-permute-start.2 = (s32[3,34,128]{2,1,0:T(8,128)S(1)}, s32[3,34,128]{2,1,0:T(8,128)S(1)}, u32[]{:S(2)}, u32[]{:S(2)}) collective-permute-start(s32[3,34,128]{2,1,0:T(8,128)S(1)} %bitcast.51), channel_id=1, source_target_pairs={{0,4},{1,5},{2,6},{3,7},{4,0},{5,1},{6,2},{7,3},{8,12},{9,13},{10,... | collective-permute-start | bytes 156680 | tf_op jit(solution)/shard_map/ppermute | solution.py:818
  7.7 10.5 %collective-permute-start.3 = (s32[3,34,128]{2,1,0:T(8,128)}, s32[3,34,128]{2,1,0:T(8,128)S(1)}, u32[]{:S(2)}, u32[]{:S(2)}) collective-permute-start(s32[3,34,128]{2,1,0:T(8,128)} %bitcast.31), channel_id=1, source_target_pairs={{0,2},{1,3},{2,4},{3,5},{4,6},{5,7},{6,0},{7,1},{8,10},{9,11},{10,... | collective-permute-start | bytes 156680 | tf_op jit(solution)/shard_map/ppermute | solution.py:818
  10.2 28.4 %collective-permute-start.7 = (bf16[256,768]{1,0:T(8,128)(2,1)S(1)}, bf16[256,768]{1,0:T(8,128)(2,1)S(1)}, u32[]{:S(2)}, u32[]{:S(2)}) collective-permute-start(bf16[256,768]{1,0:T(8,128)(2,1)S(1)} %copy-done), channel_id=1, source_target_pairs={{0,2},{1,3},{2,4},{3,5},{4,6},{5,7},{6,0},{7,1},{8,10},{9,11},{10,... | collective-permute-start | bytes 1179656 | tf_op jit(solution)/shard_map/ppermute | solution.py:818
  10.2 28.4 %collective-permute-start.9 = (bf16[256,768]{1,0:T(8,128)(2,1)S(1)}, bf16[256,768]{1,0:T(8,128)(2,1)S(1)}, u32[]{:S(2)}, u32[]{:S(2)}) collective-permute-start(bf16[256,768]{1,0:T(8,128)(2,1)S(1)} %copy-done), channel_id=1, source_target_pairs={{0,6},{1,7},{2,0},{3,1},{4,2},{5,3},{6,4},{7,5},{8,14},{9,15},{10,... | collective-permute-start | bytes 1179656 | tf_op jit(solution)/shard_map/ppermute | solution.py:818
  18.8 5.3 %collective-permute-start.4 = (s32[3,40,128]{2,1,0:T(8,128)S(1)}, s32[3,40,128]{2,1,0:T(8,128)S(1)}, u32[]{:S(2)}, u32[]{:S(2)}) collective-permute-start(s32[3,40,128]{2,1,0:T(8,128)S(1)} %table.1.refs_0_), channel_id=1, source_target_pairs={{0,1},{1,0},{2,3},{3,2},{4,5},{5,4},{6,7},{7,6},{8,9},{9,8},{10,11... | collective-permute-start | bytes 184328 | tf_op jit(solution)/shard_map/ppermute | solution.py:822
  18.9 27.5 %collective-permute-start.5 = (bf16[256,768]{1,0:T(8,128)(2,1)S(1)}, bf16[256,768]{1,0:T(8,128)(2,1)S(1)}, u32[]{:S(2)}, u32[]{:S(2)}) collective-permute-start(bf16[256,768]{1,0:T(8,128)(2,1)S(1)} %copy-done), channel_id=1, source_target_pairs={{0,4},{1,5},{2,6},{3,7},{4,0},{5,1},{6,2},{7,3},{8,12},{9,13},{10,... | collective-permute-start | bytes 1179656 | tf_op jit(solution)/shard_map/ppermute | solution.py:818
  19.9 26.6 %collective-permute-start.10 = (bf16[256,768]{1,0:T(8,128)(2,1)S(1)}, bf16[256,768]{1,0:T(8,128)(2,1)S(1)}, u32[]{:S(2)}, u32[]{:S(2)}) collective-permute-start(bf16[256,768]{1,0:T(8,128)(2,1)S(1)} %copy-done.3), channel_id=1, source_target_pairs={{0,1},{1,0},{2,3},{3,2},{4,5},{5,4},{6,7},{7,6},{8,9},{9,8},{10,11... | collective-permute-start | bytes 1179656 | tf_op jit(solution)/shard_map/ppermute | solution.py:822
  46.4 1.7 collective-permute-start.11
  46.4 3.5 %collective-permute-start.8 = (bf16[256,768]{1,0:T(8,128)(2,1)S(1)}, bf16[256,768]{1,0:T(8,128)(2,1)S(1)}, u32[]{:S(2)}, u32[]{:S(2)}) collective-permute-start(bf16[256,768]{1,0:T(8,128)(2,1)S(1)} %collective-permute-done.7.refs_0_), channel_id=1, source_target_pairs={{0,1},{1,0},{2,3},{3,2},{4,5},{5,4},{6,7},{7,6},{8,9},{9,8},{10,11... | collective-permute-start | bytes 1179656 | tf_op jit(solution)/shard_map/ppermute | solution.py:822
  46.9 4.7 %collective-permute-start.6 = (bf16[256,768]{1,0:T(8,128)(2,1)S(1)}, bf16[256,768]{1,0:T(8,128)(2,1)S(1)}, u32[]{:S(2)}, u32[]{:S(2)}) collective-permute-start(bf16[256,768]{1,0:T(8,128)(2,1)S(1)} %collective-permute-done.5.refs_0_), channel_id=1, source_target_pairs={{0,1},{1,0},{2,3},{3,2},{4,5},{5,4},{6,7},{7,6},{8,9},{9,8},{10,11... | collective-permute-start | bytes 1179656 | tf_op jit(solution)/shard_map/ppermute | solution.py:822
  51.6 28.0 %slice-start = ((s8[4718592]{0:T(1024)(128)(4,1)}), s8[4194304]{0:T(1024)(128)(4,1)S(1)}, s32[]{:S(2)}) async-start(s8[4718592]{0:T(1024)(128)(4,1)} %bitcast.42), calls=%async_computation | async-start | bytes 8388608
  51.6 28.0 %slice-start.2 = ((s8[4718592]{0:T(1024)(128)(4,1)}), s8[4194304]{0:T(1024)(128)(4,1)S(1)}, s32[]{:S(2)}) async-start(s8[4718592]{0:T(1024)(128)(4,1)} %bitcast.44), calls=%async_computation.2 | async-start | bytes 8388608
  53.4 26.2 %slice-start.1 = ((s8[4718592]{0:T(1024)(128)(4,1)}), s8[524288]{0:T(1024)(128)(4,1)S(1)}, s32[]{:S(2)}) async-start(s8[4718592]{0:T(1024)(128)(4,1)} %bitcast.42), calls=%async_computation.1 | async-start | bytes 1048576
  53.4 26.2 %slice-start.3 = ((s8[4718592]{0:T(1024)(128)(4,1)}), s8[524288]{0:T(1024)(128)(4,1)S(1)}, s32[]{:S(2)}) async-start(s8[4718592]{0:T(1024)(128)(4,1)} %bitcast.44), calls=%async_computation.3 | async-start | bytes 1048576
  53.4 26.2 %copy-start.2 = (bf16[768,768]{1,0:T(8,128)(2,1)S(1)}, bf16[768,768]{1,0:T(8,128)(2,1)}, u32[]{:S(2)}) copy-start(bf16[768,768]{1,0:T(8,128)(2,1)} %param.22) | copy-start | bytes 3538948
  66.5 5.5 %collective-permute-start.12 = (bf16[192,256]{1,0:T(8,128)(2,1)S(1)}, bf16[192,256]{1,0:T(8,128)(2,1)S(1)}, u32[]{:S(2)}, u32[]{:S(2)}) collective-permute-start(bf16[192,256]{1,0:T(8,128)(2,1)S(1)} %get-tuple-element.101), channel_id=1, source_target_pairs={{0,2},{1,3},{2,4},{3,5},{4,6},{5,7},{6,0},{7,1},{8,10},{9,11},{10,... | collective-permute-start | bytes 294920 | tf_op jit(solution)/shard_map/ppermute | solution.py:818
  66.7 10.6 %collective-permute-start.13 = (bf16[192,256]{1,0:T(8,128)(2,1)S(1)}, bf16[192,256]{1,0:T(8,128)(2,1)S(1)}, u32[]{:S(2)}, u32[]{:S(2)}) collective-permute-start(bf16[192,256]{1,0:T(8,128)(2,1)S(1)} %get-tuple-element.102), channel_id=1, source_target_pairs={{0,4},{1,5},{2,6},{3,7},{4,0},{5,1},{6,2},{7,3},{8,12},{9,13},{10,... | collective-permute-start | bytes 294920 | tf_op jit(solution)/shard_map/ppermute | solution.py:818
  71.0 8.6 %collective-permute-start.14 = (bf16[192,256]{1,0:T(8,128)(2,1)S(1)}, bf16[192,256]{1,0:T(8,128)(2,1)S(1)}, u32[]{:S(2)}, u32[]{:S(2)}) collective-permute-start(bf16[192,256]{1,0:T(8,128)(2,1)S(1)} %get-tuple-element.103), channel_id=1, source_target_pairs={{0,6},{1,7},{2,0},{3,1},{4,2},{5,3},{6,4},{7,5},{8,14},{9,15},{10,... | collective-permute-start | bytes 294920 | tf_op jit(solution)/shard_map/ppermute | solution.py:818
  89.6 5.7 %collective-permute-start.18 = (bf16[256,5376]{1,0:T(8,128)(2,1)S(1)}, bf16[256,5376]{1,0:T(8,128)(2,1)S(1)}, u32[]{:S(2)}, u32[]{:S(2)}) collective-permute-start(bf16[256,5376]{1,0:T(8,128)(2,1)S(1)} %get-tuple-element.112.refs_0_.refs_2_), channel_id=1, source_target_pairs={{0,1},{1,0},{2,3},{3,2},{4,5},{5,4},{6,7},{7,6},{8,9},{9,8},{10,11... | collective-permute-start | bytes 8257544 | tf_op jit(solution)/shard_map/ppermute | solution.py:822
  89.6 5.7 %collective-permute-start.19 = (bf16[784,256]{1,0:T(8,128)(2,1)S(1)}, bf16[784,256]{1,0:T(8,128)(2,1)S(1)}, u32[]{:S(2)}, u32[]{:S(2)}) collective-permute-start(bf16[784,256]{1,0:T(8,128)(2,1)S(1)} %get-tuple-element.115), channel_id=1, source_target_pairs={{0,1},{1,0},{2,3},{3,2},{4,5},{5,4},{6,7},{7,6},{8,9},{9,8},{10,11... | collective-permute-start | bytes 1204232 | tf_op jit(solution)/shard_map/ppermute | solution.py:822
  90.1 12.6 %collective-permute-start.15 = (bf16[192,256]{1,0:T(8,128)(2,1)S(1)}, bf16[192,256]{1,0:T(8,128)(2,1)S(1)}, u32[]{:S(2)}, u32[]{:S(2)}) collective-permute-start(bf16[192,256]{1,0:T(8,128)(2,1)S(1)} %get-tuple-element.106), channel_id=1, source_target_pairs={{0,6},{1,7},{2,0},{3,1},{4,2},{5,3},{6,4},{7,5},{8,14},{9,15},{10,... | collective-permute-start | bytes 294920 | tf_op jit(solution)/shard_map/ppermute | solution.py:818
  90.1 12.6 %collective-permute-start.16 = (bf16[192,256]{1,0:T(8,128)(2,1)S(1)}, bf16[192,256]{1,0:T(8,128)(2,1)S(1)}, u32[]{:S(2)}, u32[]{:S(2)}) collective-permute-start(bf16[192,256]{1,0:T(8,128)(2,1)S(1)} %get-tuple-element.107), channel_id=1, source_target_pairs={{0,4},{1,5},{2,6},{3,7},{4,0},{5,1},{6,2},{7,3},{8,12},{9,13},{10,... | collective-permute-start | bytes 294920 | tf_op jit(solution)/shard_map/ppermute | solution.py:818
  91.2 11.5 %collective-permute-start.17 = (bf16[192,256]{1,0:T(8,128)(2,1)S(1)}, bf16[192,256]{1,0:T(8,128)(2,1)S(1)}, u32[]{:S(2)}, u32[]{:S(2)}) collective-permute-start(bf16[192,256]{1,0:T(8,128)(2,1)S(1)} %get-tuple-element.108), channel_id=1, source_target_pairs={{0,2},{1,3},{2,4},{3,5},{4,6},{5,7},{6,0},{7,1},{8,10},{9,11},{10,... | collective-permute-start | bytes 294920 | tf_op jit(solution)/shard_map/ppermute | solution.py:818
  104.1 3.3 %collective-permute-start.20 = (f32[3,80,128]{2,1,0:T(8,128)S(1)}, f32[3,80,128]{2,1,0:T(8,128)S(1)}, u32[]{:S(2)}, u32[]{:S(2)}) collective-permute-start(f32[3,80,128]{2,1,0:T(8,128)S(1)} %sums.1.refs_7_), channel_id=1, source_target_pairs={{0,1},{1,0},{2,3},{3,2},{4,5},{5,4},{6,7},{7,6},{8,9},{9,8},{10,11... | collective-permute-start | bytes 368648 | tf_op jit(solution)/shard_map/ppermute | solution.py:822
  104.3 26.1 %collective-permute-start.21 = (bf16[1,4,176,768]{3,2,1,0:T(8,128)(2,1)S(1)}, bf16[1,4,176,768]{3,2,1,0:T(8,128)(2,1)S(1)}, u32[]{:S(2)}, u32[]{:S(2)}) collective-permute-start(bf16[1,4,176,768]{3,2,1,0:T(8,128)(2,1)S(1)} %get-tuple-element.121), channel_id=1, source_target_pairs={{0,8},{8,0},{16,24},{24,16},{1,9},{9,1},{17,25},{25,17},{2,10},{10... | collective-permute-start | bytes 3244040 | tf_op jit(solution)/shard_map/ppermute | solution.py:825
  105.7 25.8 %collective-permute-start.22 = (bf16[1,4,176,768]{3,2,1,0:T(8,128)(2,1)S(1)}, bf16[1,4,176,768]{3,2,1,0:T(8,128)(2,1)S(1)}, u32[]{:S(2)}, u32[]{:S(2)}) collective-permute-start(bf16[1,4,176,768]{3,2,1,0:T(8,128)(2,1)S(1)} %get-tuple-element.122), channel_id=1, source_target_pairs={{0,16},{8,24},{16,0},{24,8},{1,17},{9,25},{17,1},{25,9},{2,18},{10... | collective-permute-start | bytes 3244040 | tf_op jit(solution)/shard_map/ppermute | solution.py:825
  131.6 2.3 collective-permute-start.23
  136.3 2.1 collective-permute-start.27
  138.8 31.4 %collective-permute-start.28 = (bf16[4,184,768]{2,1,0:T(8,128)(2,1)S(1)}, bf16[4,184,768]{2,1,0:T(8,128)(2,1)S(1)}, u32[]{:S(2)}, u32[]{:S(2)}) collective-permute-start(bf16[4,184,768]{2,1,0:T(8,128)(2,1)S(1)} %get-tuple-element.134), channel_id=1, source_target_pairs={{0,16},{8,24},{16,0},{24,8},{1,17},{9,25},{17,1},{25,9},{2,18},{10... | collective-permute-start | bytes 3391496 | tf_op jit(solution)/shard_map/ppermute | solution.py:825
  140.5 29.7 %collective-permute-start.29 = (bf16[4,184,768]{2,1,0:T(8,128)(2,1)S(1)}, bf16[4,184,768]{2,1,0:T(8,128)(2,1)S(1)}, u32[]{:S(2)}, u32[]{:S(2)}) collective-permute-start(bf16[4,184,768]{2,1,0:T(8,128)(2,1)S(1)} %get-tuple-element.135), channel_id=1, source_target_pairs={{0,8},{8,0},{16,24},{24,16},{1,9},{9,1},{17,25},{25,17},{2,10},{10... | collective-permute-start | bytes 3391496 | tf_op jit(solution)/shard_map/ppermute | solution.py:825
  141.0 9.9 %collective-permute-start.24 = (bf16[3,192,256]{2,1,0:T(8,128)(2,1)S(1)}, bf16[3,192,256]{2,1,0:T(8,128)(2,1)S(1)}, u32[]{:S(2)}, u32[]{:S(2)}) collective-permute-start(bf16[3,192,256]{2,1,0:T(8,128)(2,1)S(1)} %get-tuple-element.126), channel_id=1, source_target_pairs={{0,2},{1,3},{2,4},{3,5},{4,6},{5,7},{6,0},{7,1},{8,10},{9,11},{10,... | collective-permute-start | bytes 884744 | tf_op jit(solution)/shard_map/ppermute | solution.py:818
  141.0 25.3 %collective-permute-start.25 = (bf16[3,192,256]{2,1,0:T(8,128)(2,1)S(1)}, bf16[3,192,256]{2,1,0:T(8,128)(2,1)S(1)}, u32[]{:S(2)}, u32[]{:S(2)}) collective-permute-start(bf16[3,192,256]{2,1,0:T(8,128)(2,1)S(1)} %get-tuple-element.127), channel_id=1, source_target_pairs={{0,4},{1,5},{2,6},{3,7},{4,0},{5,1},{6,2},{7,3},{8,12},{9,13},{10,... | collective-permute-start | bytes 884744 | tf_op jit(solution)/shard_map/ppermute | solution.py:818
  143.3 25.5 %collective-permute-start.26 = (bf16[3,192,256]{2,1,0:T(8,128)(2,1)S(1)}, bf16[3,192,256]{2,1,0:T(8,128)(2,1)S(1)}, u32[]{:S(2)}, u32[]{:S(2)}) collective-permute-start(bf16[3,192,256]{2,1,0:T(8,128)(2,1)S(1)} %get-tuple-element.128), channel_id=1, source_target_pairs={{0,6},{1,7},{2,0},{3,1},{4,2},{5,3},{6,4},{7,5},{8,14},{9,15},{10,... | collective-permute-start | bytes 884744 | tf_op jit(solution)/shard_map/ppermute | solution.py:818
  150.9 19.3 %collective-permute-start.30 = (bf16[4,24,768]{2,1,0:T(8,128)(2,1)S(1)}, bf16[4,24,768]{2,1,0:T(8,128)(2,1)S(1)}, u32[]{:S(2)}, u32[]{:S(2)}) collective-permute-start(bf16[4,24,768]{2,1,0:T(8,128)(2,1)S(1)} %get-tuple-element.136), channel_id=1, source_target_pairs={{0,24},{8,16},{16,8},{24,0},{1,25},{9,17},{17,9},{25,1},{2,26},{10... | collective-permute-start | bytes 442376 | tf_op jit(solution)/shard_map/ppermute | solution.py:825
  171.3 15.0 %collective-permute-start.31 = (bf16[160,768]{1,0:T(8,128)(2,1)S(1)}, bf16[160,768]{1,0:T(8,128)(2,1)S(1)}, u32[]{:S(2)}, u32[]{:S(2)}) collective-permute-start(bf16[160,768]{1,0:T(8,128)(2,1)S(1)} %get-tuple-element.138), channel_id=1, source_target_pairs={{0,2},{1,3},{2,4},{3,5},{4,6},{5,7},{6,0},{7,1},{8,10},{9,11},{10,... | collective-permute-start | bytes 737288 | tf_op jit(solution)/shard_map/ppermute | solution.py:818
  171.4 21.9 %collective-permute-start.32 = (bf16[160,768]{1,0:T(8,128)(2,1)S(1)}, bf16[160,768]{1,0:T(8,128)(2,1)S(1)}, u32[]{:S(2)}, u32[]{:S(2)}) collective-permute-start(bf16[160,768]{1,0:T(8,128)(2,1)S(1)} %get-tuple-element.139), channel_id=1, source_target_pairs={{0,4},{1,5},{2,6},{3,7},{4,0},{5,1},{6,2},{7,3},{8,12},{9,13},{10,... | collective-permute-start | bytes 737288 | tf_op jit(solution)/shard_map/ppermute | solution.py:818
  173.8 23.6 %collective-permute-start.33 = (bf16[160,768]{1,0:T(8,128)(2,1)S(1)}, bf16[160,768]{1,0:T(8,128)(2,1)S(1)}, u32[]{:S(2)}, u32[]{:S(2)}) collective-permute-start(bf16[160,768]{1,0:T(8,128)(2,1)S(1)} %get-tuple-element.140), channel_id=1, source_target_pairs={{0,6},{1,7},{2,0},{3,1},{4,2},{5,3},{6,4},{7,5},{8,14},{9,15},{10,... | collective-permute-start | bytes 737288 | tf_op jit(solution)/shard_map/ppermute | solution.py:818
  186.3 11.0 %collective-permute-start.34 = (bf16[88,768]{1,0:T(8,128)(2,1)S(1)}, bf16[88,768]{1,0:T(8,128)(2,1)S(1)}, u32[]{:S(2)}, u32[]{:S(2)}) collective-permute-start(bf16[88,768]{1,0:T(8,128)(2,1)S(1)} %get-tuple-element.144), channel_id=1, source_target_pairs={{0,2},{1,3},{2,4},{3,5},{4,6},{5,7},{6,0},{7,1},{8,10},{9,11},{10,... | collective-permute-start | bytes 405512 | tf_op jit(solution)/shard_map/ppermute | solution.py:818
  199.0 12.4 %collective-permute-start.35 = (bf16[160,768]{1,0:T(8,128)(2,1)S(1)}, bf16[160,768]{1,0:T(8,128)(2,1)S(1)}, u32[]{:S(2)}, u32[]{:S(2)}) collective-permute-start(bf16[160,768]{1,0:T(8,128)(2,1)S(1)} %fourth.2.refs_5_.refs_0_), channel_id=1, source_target_pairs={{0,8},{8,0},{16,24},{24,16},{1,9},{9,1},{17,25},{25,17},{2,10},{10... | collective-permute-start | bytes 737288 | tf_op jit(solution)/shard_map/ppermute | solution.py:825
  199.6 12.0 %collective-permute-start.36 = (bf16[160,768]{1,0:T(8,128)(2,1)S(1)}, bf16[160,768]{1,0:T(8,128)(2,1)S(1)}, u32[]{:S(2)}, u32[]{:S(2)}) collective-permute-start(bf16[160,768]{1,0:T(8,128)(2,1)S(1)} %fourth.2.refs_5_.refs_0_), channel_id=1, source_target_pairs={{0,16},{8,24},{16,0},{24,8},{1,17},{9,25},{17,1},{25,9},{2,18},{10... | collective-permute-start | bytes 737288 | tf_op jit(solution)/shard_map/ppermute | solution.py:825
  201.1 12.0 %collective-permute-start.37 = (bf16[160,768]{1,0:T(8,128)(2,1)S(1)}, bf16[160,768]{1,0:T(8,128)(2,1)S(1)}, u32[]{:S(2)}, u32[]{:S(2)}) collective-permute-start(bf16[160,768]{1,0:T(8,128)(2,1)S(1)} %fourth.2.refs_5_.refs_0_), channel_id=1, source_target_pairs={{0,24},{8,16},{16,8},{24,0},{1,25},{9,17},{17,9},{25,1},{2,26},{10... | collective-permute-start | bytes 737288 | tf_op jit(solution)/shard_map/ppermute | solution.py:825
  202.6 8.3 %collective-permute-start.38 = (bf16[88,768]{1,0:T(8,128)(2,1)S(1)}, bf16[88,768]{1,0:T(8,128)(2,1)S(1)}, u32[]{:S(2)}, u32[]{:S(2)}) collective-permute-start(bf16[88,768]{1,0:T(8,128)(2,1)S(1)} %get-tuple-element.146), channel_id=1, source_target_pairs={{0,4},{1,5},{2,6},{3,7},{4,0},{5,1},{6,2},{7,3},{8,12},{9,13},{10,... | collective-permute-start | bytes 405512 | tf_op jit(solution)/shard_map/ppermute | solution.py:818
  202.7 8.7 %collective-permute-start.39 = (bf16[88,768]{1,0:T(8,128)(2,1)S(1)}, bf16[88,768]{1,0:T(8,128)(2,1)S(1)}, u32[]{:S(2)}, u32[]{:S(2)}) collective-permute-start(bf16[88,768]{1,0:T(8,128)(2,1)S(1)} %get-tuple-element.147), channel_id=1, source_target_pairs={{0,6},{1,7},{2,0},{3,1},{4,2},{5,3},{6,4},{7,5},{8,14},{9,15},{10,... | collective-permute-start | bytes 405512 | tf_op jit(solution)/shard_map/ppermute | solution.py:818
  213.8 8.4 %collective-permute-start.40 = (bf16[144,768]{1,0:T(8,128)(2,1)S(1)}, bf16[144,768]{1,0:T(8,128)(2,1)S(1)}, u32[]{:S(2)}, u32[]{:S(2)}) collective-permute-start(bf16[144,768]{1,0:T(8,128)(2,1)S(1)} %fourth.3.refs_4_), channel_id=1, source_target_pairs={{0,8},{8,0},{16,24},{24,16},{1,9},{9,1},{17,25},{25,17},{2,10},{10... | collective-permute-start | bytes 663560 | tf_op jit(solution)/shard_map/ppermute | solution.py:825
  214.7 10.8 %collective-permute-start.41 = (bf16[144,768]{1,0:T(8,128)(2,1)S(1)}, bf16[144,768]{1,0:T(8,128)(2,1)S(1)}, u32[]{:S(2)}, u32[]{:S(2)}) collective-permute-start(bf16[144,768]{1,0:T(8,128)(2,1)S(1)} %fourth.3.refs_4_), channel_id=1, source_target_pairs={{0,16},{8,24},{16,0},{24,8},{1,17},{9,25},{17,1},{25,9},{2,18},{10... | collective-permute-start | bytes 663560 | tf_op jit(solution)/shard_map/ppermute | solution.py:825
  216.2 9.3 %collective-permute-start.42 = (bf16[144,768]{1,0:T(8,128)(2,1)S(1)}, bf16[144,768]{1,0:T(8,128)(2,1)S(1)}, u32[]{:S(2)}, u32[]{:S(2)}) collective-permute-start(bf16[144,768]{1,0:T(8,128)(2,1)S(1)} %fourth.3.refs_4_), channel_id=1, source_target_pairs={{0,24},{8,16},{16,8},{24,0},{1,25},{9,17},{17,9},{25,1},{2,26},{10... | collective-permute-start | bytes 663560 | tf_op jit(solution)/shard_map/ppermute | solution.py:825
  (7 other events, 54.8 us)

commit v12 on v11

--- a/solution.py
+++ b/solution.py
@@ -113,9 +113,9 @@
     for part in parts[1:]:
         total = total + part[:, :picks]
     out[:, :picks] = total
-    rows = parts[0].shape[1] - picks
+    rows = (out.shape[1] - picks) // len(parts)
     for group, part in enumerate(parts):
-        out[:, picks + group * rows : picks + (group + 1) * rows] = part[:, picks:]
+        out[:, picks + group * rows : picks + (group + 1) * rows] = part[:, picks : picks + rows]
 
 
 def bias_kernel(info, *refs, groups, peers, rows, picks):
@@ -629,13 +629,14 @@
         return
     turned = refs[groups + 1]
     third = feats // 3
+    quarter = turned.shape[1] - 8
     for group in range(groups):
         turned[group] = parts[group][2 * high :].astype(F32)
     spots = [lax.rem(info[0] + groups - owner, groups) for owner in range(groups)]
     found, sums = [], []
     for kind in range(3):
         lanes = slice(kind * third, (kind + 1) * third)
-        found.append(jnp.concatenate([turned[spot, :, lanes] for spot in spots], axis=1))
+        found.append(jnp.concatenate([turned[spot, :quarter, lanes] for spot in spots], axis=1))
         line = [turned[spot, 8 * kind : 8 * kind + 8, 3 * third :] for spot in spots]
         sums.append(jnp.concatenate(line, axis=1)[:1])
     sums.append(jnp.zeros((5, out.shape[1]), F32))
@@ -737,6 +738,7 @@
             for parity in range(2):
                 at = (2 * group + parity) * block + part * quarter
                 lines = jnp.concatenate([total[at : at + quarter], more], axis=1)
+                lines = jnp.concatenate([lines, jnp.zeros_like(lines[:8])], axis=0)
                 found.append(lines.astype(BF))
             own_ref[place, spot] = jnp.where(info[1] == 0, found[0], found[1])
             far_ref[place, spot] = jnp.where(info[1] == 0, found[1], found[0])
@@ -860,9 +862,11 @@
     mine_lanes = (jnp.arange(wide, dtype=jnp.int32) == me)[None, None, :, None]
     tops = jnp.where(mine_lanes, tops, 0).reshape(heads, picks, clusters)
     lines = rows // clusters
-    packed = jnp.concatenate([tops, marked.reshape(heads, lines, clusters)], axis=1)
+    marked = marked.reshape(heads, lines, clusters)
+    fill = jnp.zeros((heads, -lines % 8, clusters), jnp.int32)
+    packed = jnp.concatenate([tops, marked, fill], axis=1)
     near = [along_peers(tokens, -hop) for hop in range(1, peers)]
-    packed = after(packed.reshape(groups, own_heads, picks + lines, clusters), near)
+    packed = after(packed.reshape(groups, own_heads, -1, clusters), near)
 
     def of_heads(hop):
         return lax.dynamic_index_in_dim(packed, (group_at + groups - hop) % groups, keepdims=False)
@@ -882,7 +886,7 @@
     table = prefetched(
         functools.partial(table_kernel, picks=picks),
         (1,),
-        [whole((own_heads, picks + lines, clusters))] * groups,
+        [whole(packed.shape[1:])] * groups,
         whole(table_shape),
         array(table_shape, jnp.int32),
         8,
@@ -1130,7 +1134,7 @@
         )(info, keep_u, got_u, keep_d, got_d, by_y, by_x, inner, inner_got, by_xy)
 
     def weight_fourth(came, high, lines, first):
-        tall = 2 * high + (3 * lines + 8 if lines else 0)
+        tall = 2 * high + (3 * (block_rows // 4) + 8 if lines else 0)
         done = prefetched(
             functools.partial(fourth_kernel, groups=groups, high=high, feats=3 * feats),
             (1,),
@@ -1267,7 +1271,7 @@
     tall = block_rows + 16
     spent = cost(2 * own_rows * width * 3 * feats, 4e6)
     if fast:
-        lines = block_rows // 4
+        lines = block_rows // 4 + 8
         more = [array((4, groups, lines, width), BF)] * 2
     else:
         more = [array((width, 3 * feats), F32), array((16, 3 * feats), F32)]

time: 231 us -> 235 us (1.017)
  waiting for transfers between devices: 89.5 us -> 92.3 us
    unnamed x31 -> x27, local copies, waits for them, and re-layouts: 7.7 us -> 7.05 us
  transfers between devices with their start and end apart: 43 -> 43, of which waited for: 23 -> 24; matrix products, arithmetic and copies ran while one was open for 6% -> 5% of each run, Pallas kernels for 19% -> 19%
where the time goes in v12:
time: 235 us; the launch traced here: 234 us
  waiting for transfers between devices  92.3 us (39%)
  Pallas kernels  79.7 us (34%)
  starting transfers between devices  44.4 us (19%)
  local copies, waits for them, and re-layouts  11 us (5%)
  other arithmetic  4.8 us (2%)
    ppermute x21, waiting for transfers between devices, along_groups(): return lax.ppermute(values, 'wide', pairs)  70.3 us
    pallas_call x15, Pallas kernels, prefetched(): return lambda *inputs: call(*inputs, *first)  45.2 us
    ppermute x21, starting transfers between devices, along_groups(): return lax.ppermute(values, 'wide', pairs)  28.9 us
    pallas_call x1, Pallas kernels, per_device(): pl.pallas_call(functools.partial(back_kernel, size=size, groups=groups, g...  20.6 us
    ppermute x11, waiting for transfers between devices, along_dp(): return lax.ppermute(values, 'dp', [(i, i ^ mask) for i in range(n_dp)])  15.4 us
    ppermute x11, starting transfers between devices, along_dp(): return lax.ppermute(values, 'dp', [(i, i ^ mask) for i in range(n_dp)])  13.7 us
    pallas_call x1, Pallas kernels, per_device(): pl.pallas_call(functools.partial(forward_kernel, size=size, groups=groups...  13.4 us
    unnamed x27, local copies, waits for them, and re-layouts  7.05 us
  transfers between devices with their start and end apart: 43, of which 24 were waited for; matrix products, arithmetic and copies ran while one was open for 5% of the time, Pallas kernels for 19%

profile of v12, /device:TPU:8, one launch (start us, length us, event | category | flops | bytes accessed | tf_op | source)
XLA Modules:
  0.0 234.1 jit_solution(10134282814271173285)
XLA Ops:
  4.6 3.1 %collective-permute-start.2 = (s32[3,40,128]{2,1,0:T(8,128)S(1)}, s32[3,40,128]{2,1,0:T(8,128)S(1)}, u32[]{:S(2)}, u32[]{:S(2)}) collective-permute-start(s32[3,40,128]{2,1,0:T(8,128)S(1)} %get-tuple-element.158), channel_id=1, source_target_pairs={{0,4},{1,5},{2,6},{3,7},{4,0},{5,1},{6,2},{7,3},{8,12},{9,13},{10,... | collective-permute-start | bytes 184328 | tf_op jit(solution)/shard_map/ppermute | solution.py:820
  7.7 2.5 %collective-permute-start.3 = (s32[3,40,128]{2,1,0:T(8,128)S(1)}, s32[3,40,128]{2,1,0:T(8,128)S(1)}, u32[]{:S(2)}, u32[]{:S(2)}) collective-permute-start(s32[3,40,128]{2,1,0:T(8,128)S(1)} %get-tuple-element.157), channel_id=1, source_target_pairs={{0,2},{1,3},{2,4},{3,5},{4,6},{5,7},{6,0},{7,1},{8,10},{9,11},{10,... | collective-permute-start | bytes 184328 | tf_op jit(solution)/shard_map/ppermute | solution.py:820
  10.2 2.0 collective-permute-start.9
  12.2 4.3 %copy.69 = bf16[768,1536]{0,1:T(8,128)(2,1)} copy(bf16[768,1536]{1,0:T(8,128)(2,1)} %param.21) | data formatting | bytes 4718592 | tf_op args[7]
  16.5 1.6 copy.68
  20.0 1.9 pad_maximum_fusion
  22.3 1.7 project.4
  24.0 7.6 %bias.1 = (bf16[3,2048,128]{2,1,0:T(8,128)(2,1)S(1)}, s32[3,1,2048]{2,1,0:T(1,128)S(1)}) custom-call(s32[6]{0:T(128)S(1)} %stack.38.info.refs_0_, s32[3,40,128]{2,1,0:T(8,128)S(1)} %table.1.refs_0_, s32[3,40,128]{2,1,0:T(8,128)S(1)} %collective-permute-done.4.refs_1_), custom_call_target="tpu_custom_call" | custom-call | flops 201326592 | bytes 1572864 | tf_op jit(solution)/shard_map/bias/pallas_call | solution.py:848
  31.7 7.5 %collective-permute-done.7.refs_0_ = bf16[256,768]{1,0:T(8,128)(2,1)S(1)} collective-permute-done((bf16[256,768]{1,0:T(8,128)(2,1)S(1)}, bf16[256,768]{1,0:T(8,128)(2,1)S(1)}, u32[]{:S(2)}, u32[]{:S(2)}) %collective-permute-start.7) | collective-permute-done | bytes 393248 | tf_op jit(solution)/shard_map/ppermute | solution.py:820
  39.6 7.4 %collective-permute-done.5.refs_0_ = bf16[256,768]{1,0:T(8,128)(2,1)S(1)} collective-permute-done((bf16[256,768]{1,0:T(8,128)(2,1)S(1)}, bf16[256,768]{1,0:T(8,128)(2,1)S(1)}, u32[]{:S(2)}, u32[]{:S(2)}) %collective-permute-start.5) | collective-permute-done | bytes 393248 | tf_op jit(solution)/shard_map/ppermute | solution.py:820
  48.8 1.7 project.5
  50.5 1.7 project.6
  52.3 1.7 project.7
  54.1 13.4 %attend.1 = (bf16[192,256]{1,0:T(8,128)(2,1)S(1)}, bf16[192,256]{1,0:T(8,128)(2,1)S(1)}, bf16[192,256]{1,0:T(8,128)(2,1)S(1)}, bf16[192,256]{1,0:T(8,128)(2,1)S(...) custom-call(s32[3,1,2048]{2,1,0:T(1,128)S(1)} %get-tuple-element.84.ids_all.refs_1_, ...), custom_call_target="tpu_custom_call" | custom-call | flops 9663676416 | bytes 8000000 | tf_op jit(solution)/shard_map/attend/pallas_call | solution.py:988
  67.8 4.3 %collective-permute-start.13 = (bf16[192,256]{1,0:T(8,128)(2,1)S(1)}, bf16[192,256]{1,0:T(8,128)(2,1)S(1)}, u32[]{:S(2)}, u32[]{:S(2)}) collective-permute-start(bf16[192,256]{1,0:T(8,128)(2,1)S(1)} %get-tuple-element.102), channel_id=1, source_target_pairs={{0,4},{1,5},{2,6},{3,7},{4,0},{5,1},{6,2},{7,3},{8,12},{9,13},{10,... | collective-permute-start | bytes 294920 | tf_op jit(solution)/shard_map/ppermute | solution.py:820
  73.0 5.5 %collective-permute-done.13.refs_2_ = bf16[192,256]{1,0:T(8,128)(2,1)S(1)} collective-permute-done((bf16[192,256]{1,0:T(8,128)(2,1)S(1)}, bf16[192,256]{1,0:T(8,128)(2,1)S(1)}, u32[]{:S(2)}, u32[]{:S(2)}) %collective-permute-start.13) | collective-permute-done | bytes 98336 | tf_op jit(solution)/shard_map/ppermute | solution.py:820
  78.4 2.2 collective-permute-done.14.refs_3_
  80.7 9.9 %feed.1 = (bf16[256,768]{1,0:T(8,128)(2,1)}, f32[256,768]{1,0:T(8,128)S(1)}, bf16[256,5376]{1,0:T(8,128)(2,1)S(1)}, bf16[784,256]{1,0:T(8,128)(2,1)S(1)}, bf16[2...) custom-call(s32[6]{0:T(128)S(1)} %stack.38.info.refs_0_, ...), custom_call_target="tpu_custom_call" | custom-call | flops 4831838208 | bytes 9437184 | tf_op jit(solution)/shard_map/feed/pallas_call | solution.py:848
  92.3 2.9 %collective-permute-start.17 = (bf16[192,256]{1,0:T(8,128)(2,1)S(1)}, bf16[192,256]{1,0:T(8,128)(2,1)S(1)}, u32[]{:S(2)}, u32[]{:S(2)}) collective-permute-start(bf16[192,256]{1,0:T(8,128)(2,1)S(1)} %get-tuple-element.108), channel_id=1, source_target_pairs={{0,2},{1,3},{2,4},{3,5},{4,6},{5,7},{6,0},{7,1},{8,10},{9,11},{10,... | collective-permute-start | bytes 294920 | tf_op jit(solution)/shard_map/ppermute | solution.py:820
  96.3 7.4 %weights.1 = (bf16[1,4,176,768]{3,2,1,0:T(8,128)(2,1)S(1)}, bf16[1,4,48,768]{3,2,1,0:T(8,128)(2,1)S(1)}, bf16[2,4,112,768]{3,2,1,0:T(8,128)(2,1)S(1)}, bf16[1,4,...) custom-call(s32[6]{0:T(128)S(1)} %stack.38.info.refs_0_, ...), custom_call_target="tpu_custom_call" | custom-call | flops 4831838208 | bytes 14155776 | tf_op jit(solution)/shard_map/weights/pallas_call | solution.py:848
  103.7 1.4 sums.1.refs_7_
  105.3 1.5 collective-permute-start.21
  106.8 1.5 collective-permute-start.22
  108.3 20.6 %back.1 = (bf16[4,192,256]{2,1,0:T(8,128)(2,1)S(1)}, f32[3,128,1024]{2,1,0:T(8,128)S(1)}, bf16[3,128,1024]{2,1,0:T(8,128)(2,1)S(1)}) custom-call(s32[3,1,2048]{2,1,0:T(1,128)S(1)} %get-tuple-element.84.ids_all.refs_1_, bf16[3,192,2048]{2,1,0:T(8,128)(2,1)S(1)} %get-tuple-element.98.feat, bf16[3,2048,128]{2,1,0:T(8,128)(2,1)S(1)} %get-tuple-element.99.kv, ...), custom_call_target="tpu_custom_call" | custom-call | flops 22548578304 | bytes 10000000 | tf_op jit(solution)/shard_map/back/pallas_call | solution.py:1245
  129.0 2.5 %collective-permute-done.21.got_u.refs_2_ = bf16[1,4,176,768]{3,2,1,0:T(8,128)(2,1)S(1)} collective-permute-done((bf16[1,4,176,768]{3,2,1,0:T(8,128)(2,1)S(1)}, bf16[1,4,176,768]{3,2,1,0:T(8,128)(2,1)S(1)}, u32[]{:S(2)}, u32[]{:S(2)}) %collective-permute-start.21) | collective-permute-done | bytes 1081376 | tf_op jit(solution)/shard_map/ppermute | solution.py:827
  132.7 2.3 collective-permute-done.23.refs_2_
  134.9 2.5 %inward.1 = (bf16[3,192,256]{2,1,0:T(8,128)(2,1)S(1)}, bf16[3,192,256]{2,1,0:T(8,128)(2,1)S(1)}, bf16[3,192,256]{2,1,0:T(8,128)(2,1)S(1)}, bf16[3,192,256]{2,1,0...) custom-call(s32[6]{0:T(128)S(1)} %stack.38.info.refs_0_, ...), custom_call_target="tpu_custom_call" | custom-call | flops 905969664 | bytes 4000000 | tf_op jit(solution)/shard_map/inward/pallas_call | solution.py:848
  137.7 2.2 collective-permute-done.27.inner_got.refs_8_
  140.3 1.6 collective-permute-start.28
  142.5 2.4 %collective-permute-start.25 = (bf16[3,192,256]{2,1,0:T(8,128)(2,1)S(1)}, bf16[3,192,256]{2,1,0:T(8,128)(2,1)S(1)}, u32[]{:S(2)}, u32[]{:S(2)}) collective-permute-start(bf16[3,192,256]{2,1,0:T(8,128)(2,1)S(1)} %get-tuple-element.127), channel_id=1, source_target_pairs={{0,4},{1,5},{2,6},{3,7},{4,0},{5,1},{6,2},{7,3},{8,12},{9,13},{10,... | collective-permute-start | bytes 884744 | tf_op jit(solution)/shard_map/ppermute | solution.py:820
  145.7 6.7 %collective-permute-done.24.refs_1_.refs_11_ = bf16[3,192,256]{2,1,0:T(8,128)(2,1)S(1)} collective-permute-done((bf16[3,192,256]{2,1,0:T(8,128)(2,1)S(1)}, bf16[3,192,256]{2,1,0:T(8,128)(2,1)S(1)}, u32[]{:S(2)}, u32[]{:S(2)}) %collective-permute-start.24) | collective-permute-done | bytes 294944 | tf_op jit(solution)/shard_map/ppermute | solution.py:820
  152.4 1.4 collective-permute-start.30
  153.8 13.9 %collective-permute-done.25.refs_2_.refs_12_ = bf16[3,192,256]{2,1,0:T(8,128)(2,1)S(1)} collective-permute-done((bf16[3,192,256]{2,1,0:T(8,128)(2,1)S(1)}, bf16[3,192,256]{2,1,0:T(8,128)(2,1)S(1)}, u32[]{:S(2)}, u32[]{:S(2)}) %collective-permute-start.25) | collective-permute-done | bytes 294944 | tf_op jit(solution)/shard_map/ppermute | solution.py:820
  167.7 2.7 %collective-permute-done.26.refs_3_.refs_13_ = bf16[3,192,256]{2,1,0:T(8,128)(2,1)S(1)} collective-permute-done((bf16[3,192,256]{2,1,0:T(8,128)(2,1)S(1)}, bf16[3,192,256]{2,1,0:T(8,128)(2,1)S(1)}, u32[]{:S(2)}, u32[]{:S(2)}) %collective-permute-start.26) | collective-permute-done | bytes 294944 | tf_op jit(solution)/shard_map/ppermute | solution.py:820
  170.4 3.4 %collective-permute-done.30.refs_9_ = bf16[4,32,768]{2,1,0:T(8,128)(2,1)S(1)} collective-permute-done((bf16[4,32,768]{2,1,0:T(8,128)(2,1)S(1)}, bf16[4,32,768]{2,1,0:T(8,128)(2,1)S(1)}, u32[]{:S(2)}, u32[]{:S(2)}) %collective-permute-start.30) | collective-permute-done | bytes 196640 | tf_op jit(solution)/shard_map/ppermute | solution.py:827
  175.0 2.4 %collective-permute-start.32 = (bf16[160,768]{1,0:T(8,128)(2,1)S(1)}, bf16[160,768]{1,0:T(8,128)(2,1)S(1)}, u32[]{:S(2)}, u32[]{:S(2)}) collective-permute-start(bf16[160,768]{1,0:T(8,128)(2,1)S(1)} %get-tuple-element.139), channel_id=1, source_target_pairs={{0,4},{1,5},{2,6},{3,7},{4,0},{5,1},{6,2},{7,3},{8,12},{9,13},{10,... | collective-permute-start | bytes 737288 | tf_op jit(solution)/shard_map/ppermute | solution.py:820
  178.2 11.7 %collective-permute-done.31.refs_2_ = bf16[160,768]{1,0:T(8,128)(2,1)S(1)} collective-permute-done((bf16[160,768]{1,0:T(8,128)(2,1)S(1)}, bf16[160,768]{1,0:T(8,128)(2,1)S(1)}, u32[]{:S(2)}, u32[]{:S(2)}) %collective-permute-start.31) | collective-permute-done | bytes 245792 | tf_op jit(solution)/shard_map/ppermute | solution.py:820
  190.0 3.0 %collective-permute-start.34 = (bf16[96,768]{1,0:T(8,128)(2,1)S(1)}, bf16[96,768]{1,0:T(8,128)(2,1)S(1)}, u32[]{:S(2)}, u32[]{:S(2)}) collective-permute-start(bf16[96,768]{1,0:T(8,128)(2,1)S(1)} %get-tuple-element.144), channel_id=1, source_target_pairs={{0,2},{1,3},{2,4},{3,5},{4,6},{5,7},{6,0},{7,1},{8,10},{9,11},{10,... | collective-permute-start | bytes 442376 | tf_op jit(solution)/shard_map/ppermute | solution.py:820
  192.9 3.0 %final.1.refs_6_ = bf16[256,768]{1,0:T(8,128)(2,1)} custom-call(s32[6]{0:T(128)S(1)} %stack.38.info.refs_0_, bf16[3,192,256]{2,1,0:T(8,128)(2,1)S(1)} %get-tuple-element.125.refs_0_.refs_10_, bf16[3,192,256]{2,1,0:T(8,128)(2,1)S(1)} %collective-permute-done.24.refs_1_.refs_11_, bf16[3,192,256]{2,1,0:T(8,128)(2,1)S(1)} %collective-permute-done.25.refs_2_.refs_12_, ...), custom_call_target="tpu_custom_call" | custom-call | flops 905969664 | bytes 3538944 | tf_op jit(solution)/shard_map/final/pallas_call | solution.py:848
  197.0 4.2 %collective-permute-done.33.refs_4_ = bf16[160,768]{1,0:T(8,128)(2,1)S(1)} collective-permute-done((bf16[160,768]{1,0:T(8,128)(2,1)S(1)}, bf16[160,768]{1,0:T(8,128)(2,1)S(1)}, u32[]{:S(2)}, u32[]{:S(2)}) %collective-permute-start.33) | collective-permute-done | bytes 245792 | tf_op jit(solution)/shard_map/ppermute | solution.py:820
  203.6 1.5 collective-permute-start.36
  205.1 1.4 collective-permute-start.37
  206.6 1.3 collective-permute-start.39
  209.0 6.7 %collective-permute-done.38.refs_3_ = bf16[96,768]{1,0:T(8,128)(2,1)S(1)} collective-permute-done((bf16[96,768]{1,0:T(8,128)(2,1)S(1)}, bf16[96,768]{1,0:T(8,128)(2,1)S(1)}, u32[]{:S(2)}, u32[]{:S(2)}) %collective-permute-start.38) | collective-permute-done | bytes 147488 | tf_op jit(solution)/shard_map/ppermute | solution.py:820
  218.7 1.6 collective-permute-start.41
  222.4 3.9 %collective-permute-done.40.refs_5_ = bf16[144,768]{1,0:T(8,128)(2,1)S(1)} collective-permute-done((bf16[144,768]{1,0:T(8,128)(2,1)S(1)}, bf16[144,768]{1,0:T(8,128)(2,1)S(1)}, u32[]{:S(2)}, u32[]{:S(2)}) %collective-permute-start.40) | collective-permute-done | bytes 221216 | tf_op jit(solution)/shard_map/ppermute | solution.py:827
  226.3 2.2 collective-permute-done.41.refs_6_
  229.4 3.4 %spread.1 = (f32[96,3072]{1,0:T(8,128)}, f32[96,768]{1,0:T(8,128)}, f32[384,768]{1,0:T(8,128)}, f32[8,768]{1,0:T(8,128)S(1)}, f32[96,768]{1,0:T(8,128)}, /*index=5*/f32[96,1536]{1,0:T(8,128)}, f32[96,128]{1,0:T(8,128)S(1)}) custom-call(s32[6]{0:T(128)S(1)} %stack.38.info.refs_0_, bf16[160,768]{1,0:T(8,128)(2,1)S(1)} %fourth.2.refs_5_.refs_0_, ...), custom_call_target="tpu_custom_call" | custom-call | flops 1000000 | bytes 3538944 | tf_op jit(solution)/shard_map/spread/pallas_call | solution.py:848
  (114 shorter events, 29.2 us)
Async XLA Ops:
  0.6 3.3 %collective-permute-start = (bf16[256,768]{1,0:T(8,128)(2,1)}, bf16[256,768]{1,0:T(8,128)(2,1)S(1)}, u32[]{:S(2)}, u32[]{:S(2)}) collective-permute-start(bf16[256,768]{1,0:T(8,128)(2,1)} %refs_4_.3), channel_id=1, source_target_pairs={{0,1},{1,0},{2,3},{3,2},{4,5},{5,4},{6,7},{7,6},{8,9},{9,8},{10,11... | collective-permute-start | bytes 1179656 | tf_op jit(solution)/shard_map/ppermute | solution.py:824
  4.6 13.6 %collective-permute-start.1 = (s32[3,40,128]{2,1,0:T(8,128)}, s32[3,40,128]{2,1,0:T(8,128)S(1)}, u32[]{:S(2)}, u32[]{:S(2)}) collective-permute-start(s32[3,40,128]{2,1,0:T(8,128)} %get-tuple-element.159), channel_id=1, source_target_pairs={{0,6},{1,7},{2,0},{3,1},{4,2},{5,3},{6,4},{7,5},{8,14},{9,15},{10,... | collective-permute-start | bytes 184328 | tf_op jit(solution)/shard_map/ppermute | solution.py:820
  4.6 13.6 %collective-permute-start.2 = (s32[3,40,128]{2,1,0:T(8,128)S(1)}, s32[3,40,128]{2,1,0:T(8,128)S(1)}, u32[]{:S(2)}, u32[]{:S(2)}) collective-permute-start(s32[3,40,128]{2,1,0:T(8,128)S(1)} %get-tuple-element.158), channel_id=1, source_target_pairs={{0,4},{1,5},{2,6},{3,7},{4,0},{5,1},{6,2},{7,3},{8,12},{9,13},{10,... | collective-permute-start | bytes 184328 | tf_op jit(solution)/shard_map/ppermute | solution.py:820
  7.7 10.5 %collective-permute-start.3 = (s32[3,40,128]{2,1,0:T(8,128)S(1)}, s32[3,40,128]{2,1,0:T(8,128)S(1)}, u32[]{:S(2)}, u32[]{:S(2)}) collective-permute-start(s32[3,40,128]{2,1,0:T(8,128)S(1)} %get-tuple-element.157), channel_id=1, source_target_pairs={{0,2},{1,3},{2,4},{3,5},{4,6},{5,7},{6,0},{7,1},{8,10},{9,11},{10,... | collective-permute-start | bytes 184328 | tf_op jit(solution)/shard_map/ppermute | solution.py:820
  10.2 29.0 %collective-permute-start.7 = (bf16[256,768]{1,0:T(8,128)(2,1)S(1)}, bf16[256,768]{1,0:T(8,128)(2,1)S(1)}, u32[]{:S(2)}, u32[]{:S(2)}) collective-permute-start(bf16[256,768]{1,0:T(8,128)(2,1)S(1)} %copy-done), channel_id=1, source_target_pairs={{0,2},{1,3},{2,4},{3,5},{4,6},{5,7},{6,0},{7,1},{8,10},{9,11},{10,... | collective-permute-start | bytes 1179656 | tf_op jit(solution)/shard_map/ppermute | solution.py:820
  10.2 29.5 %collective-permute-start.9 = (bf16[256,768]{1,0:T(8,128)(2,1)S(1)}, bf16[256,768]{1,0:T(8,128)(2,1)S(1)}, u32[]{:S(2)}, u32[]{:S(2)}) collective-permute-start(bf16[256,768]{1,0:T(8,128)(2,1)S(1)} %copy-done), channel_id=1, source_target_pairs={{0,6},{1,7},{2,0},{3,1},{4,2},{5,3},{6,4},{7,5},{8,14},{9,15},{10,... | collective-permute-start | bytes 1179656 | tf_op jit(solution)/shard_map/ppermute | solution.py:820
  18.8 5.3 %collective-permute-start.4 = (s32[3,40,128]{2,1,0:T(8,128)S(1)}, s32[3,40,128]{2,1,0:T(8,128)S(1)}, u32[]{:S(2)}, u32[]{:S(2)}) collective-permute-start(s32[3,40,128]{2,1,0:T(8,128)S(1)} %table.1.refs_0_), channel_id=1, source_target_pairs={{0,1},{1,0},{2,3},{3,2},{4,5},{5,4},{6,7},{7,6},{8,9},{9,8},{10,11... | collective-permute-start | bytes 184328 | tf_op jit(solution)/shard_map/ppermute | solution.py:824
  18.9 28.2 %collective-permute-start.5 = (bf16[256,768]{1,0:T(8,128)(2,1)S(1)}, bf16[256,768]{1,0:T(8,128)(2,1)S(1)}, u32[]{:S(2)}, u32[]{:S(2)}) collective-permute-start(bf16[256,768]{1,0:T(8,128)(2,1)S(1)} %copy-done), channel_id=1, source_target_pairs={{0,4},{1,5},{2,6},{3,7},{4,0},{5,1},{6,2},{7,3},{8,12},{9,13},{10,... | collective-permute-start | bytes 1179656 | tf_op jit(solution)/shard_map/ppermute | solution.py:820
  19.8 27.2 %collective-permute-start.10 = (bf16[256,768]{1,0:T(8,128)(2,1)S(1)}, bf16[256,768]{1,0:T(8,128)(2,1)S(1)}, u32[]{:S(2)}, u32[]{:S(2)}) collective-permute-start(bf16[256,768]{1,0:T(8,128)(2,1)S(1)} %copy-done.3), channel_id=1, source_target_pairs={{0,1},{1,0},{2,3},{3,2},{4,5},{5,4},{6,7},{7,6},{8,9},{9,8},{10,11... | collective-permute-start | bytes 1179656 | tf_op jit(solution)/shard_map/ppermute | solution.py:824
  47.1 1.7 collective-permute-start.11
  47.1 3.4 %collective-permute-start.8 = (bf16[256,768]{1,0:T(8,128)(2,1)S(1)}, bf16[256,768]{1,0:T(8,128)(2,1)S(1)}, u32[]{:S(2)}, u32[]{:S(2)}) collective-permute-start(bf16[256,768]{1,0:T(8,128)(2,1)S(1)} %collective-permute-done.7.refs_0_), channel_id=1, source_target_pairs={{0,1},{1,0},{2,3},{3,2},{4,5},{5,4},{6,7},{7,6},{8,9},{9,8},{10,11... | collective-permute-start | bytes 1179656 | tf_op jit(solution)/shard_map/ppermute | solution.py:824
  47.6 4.7 %collective-permute-start.6 = (bf16[256,768]{1,0:T(8,128)(2,1)S(1)}, bf16[256,768]{1,0:T(8,128)(2,1)S(1)}, u32[]{:S(2)}, u32[]{:S(2)}) collective-permute-start(bf16[256,768]{1,0:T(8,128)(2,1)S(1)} %collective-permute-done.5.refs_0_), channel_id=1, source_target_pairs={{0,1},{1,0},{2,3},{3,2},{4,5},{5,4},{6,7},{7,6},{8,9},{9,8},{10,11... | collective-permute-start | bytes 1179656 | tf_op jit(solution)/shard_map/ppermute | solution.py:824
  52.3 28.4 %slice-start = ((s8[4718592]{0:T(1024)(128)(4,1)}), s8[4194304]{0:T(1024)(128)(4,1)S(1)}, s32[]{:S(2)}) async-start(s8[4718592]{0:T(1024)(128)(4,1)} %bitcast.37), calls=%async_computation | async-start | bytes 8388608
  52.3 28.4 %slice-start.2 = ((s8[4718592]{0:T(1024)(128)(4,1)}), s8[4194304]{0:T(1024)(128)(4,1)S(1)}, s32[]{:S(2)}) async-start(s8[4718592]{0:T(1024)(128)(4,1)} %bitcast.39), calls=%async_computation.2 | async-start | bytes 8388608
  54.0 26.6 %slice-start.1 = ((s8[4718592]{0:T(1024)(128)(4,1)}), s8[524288]{0:T(1024)(128)(4,1)S(1)}, s32[]{:S(2)}) async-start(s8[4718592]{0:T(1024)(128)(4,1)} %bitcast.37), calls=%async_computation.1 | async-start | bytes 1048576
  54.1 26.6 %slice-start.3 = ((s8[4718592]{0:T(1024)(128)(4,1)}), s8[524288]{0:T(1024)(128)(4,1)S(1)}, s32[]{:S(2)}) async-start(s8[4718592]{0:T(1024)(128)(4,1)} %bitcast.39), calls=%async_computation.3 | async-start | bytes 1048576
  54.1 26.6 %copy-start.2 = (bf16[768,768]{1,0:T(8,128)(2,1)S(1)}, bf16[768,768]{1,0:T(8,128)(2,1)}, u32[]{:S(2)}) copy-start(bf16[768,768]{1,0:T(8,128)(2,1)} %param.22) | copy-start | bytes 3538948
  67.5 5.5 %collective-permute-start.12 = (bf16[192,256]{1,0:T(8,128)(2,1)S(1)}, bf16[192,256]{1,0:T(8,128)(2,1)S(1)}, u32[]{:S(2)}, u32[]{:S(2)}) collective-permute-start(bf16[192,256]{1,0:T(8,128)(2,1)S(1)} %get-tuple-element.101), channel_id=1, source_target_pairs={{0,2},{1,3},{2,4},{3,5},{4,6},{5,7},{6,0},{7,1},{8,10},{9,11},{10,... | collective-permute-start | bytes 294920 | tf_op jit(solution)/shard_map/ppermute | solution.py:820
  67.8 10.6 %collective-permute-start.13 = (bf16[192,256]{1,0:T(8,128)(2,1)S(1)}, bf16[192,256]{1,0:T(8,128)(2,1)S(1)}, u32[]{:S(2)}, u32[]{:S(2)}) collective-permute-start(bf16[192,256]{1,0:T(8,128)(2,1)S(1)} %get-tuple-element.102), channel_id=1, source_target_pairs={{0,4},{1,5},{2,6},{3,7},{4,0},{5,1},{6,2},{7,3},{8,12},{9,13},{10,... | collective-permute-start | bytes 294920 | tf_op jit(solution)/shard_map/ppermute | solution.py:820
  72.1 8.5 %collective-permute-start.14 = (bf16[192,256]{1,0:T(8,128)(2,1)S(1)}, bf16[192,256]{1,0:T(8,128)(2,1)S(1)}, u32[]{:S(2)}, u32[]{:S(2)}) collective-permute-start(bf16[192,256]{1,0:T(8,128)(2,1)S(1)} %get-tuple-element.103), channel_id=1, source_target_pairs={{0,6},{1,7},{2,0},{3,1},{4,2},{5,3},{6,4},{7,5},{8,14},{9,15},{10,... | collective-permute-start | bytes 294920 | tf_op jit(solution)/shard_map/ppermute | solution.py:820
  90.6 5.7 %collective-permute-start.18 = (bf16[256,5376]{1,0:T(8,128)(2,1)S(1)}, bf16[256,5376]{1,0:T(8,128)(2,1)S(1)}, u32[]{:S(2)}, u32[]{:S(2)}) collective-permute-start(bf16[256,5376]{1,0:T(8,128)(2,1)S(1)} %get-tuple-element.112.refs_0_.refs_2_), channel_id=1, source_target_pairs={{0,1},{1,0},{2,3},{3,2},{4,5},{5,4},{6,7},{7,6},{8,9},{9,8},{10,11... | collective-permute-start | bytes 8257544 | tf_op jit(solution)/shard_map/ppermute | solution.py:824
  90.6 5.7 %collective-permute-start.19 = (bf16[784,256]{1,0:T(8,128)(2,1)S(1)}, bf16[784,256]{1,0:T(8,128)(2,1)S(1)}, u32[]{:S(2)}, u32[]{:S(2)}) collective-permute-start(bf16[784,256]{1,0:T(8,128)(2,1)S(1)} %get-tuple-element.115), channel_id=1, source_target_pairs={{0,1},{1,0},{2,3},{3,2},{4,5},{5,4},{6,7},{7,6},{8,9},{9,8},{10,11... | collective-permute-start | bytes 1204232 | tf_op jit(solution)/shard_map/ppermute | solution.py:824
  91.1 12.6 %collective-permute-start.15 = (bf16[192,256]{1,0:T(8,128)(2,1)S(1)}, bf16[192,256]{1,0:T(8,128)(2,1)S(1)}, u32[]{:S(2)}, u32[]{:S(2)}) collective-permute-start(bf16[192,256]{1,0:T(8,128)(2,1)S(1)} %get-tuple-element.106), channel_id=1, source_target_pairs={{0,6},{1,7},{2,0},{3,1},{4,2},{5,3},{6,4},{7,5},{8,14},{9,15},{10,... | collective-permute-start | bytes 294920 | tf_op jit(solution)/shard_map/ppermute | solution.py:820
  91.2 12.5 %collective-permute-start.16 = (bf16[192,256]{1,0:T(8,128)(2,1)S(1)}, bf16[192,256]{1,0:T(8,128)(2,1)S(1)}, u32[]{:S(2)}, u32[]{:S(2)}) collective-permute-start(bf16[192,256]{1,0:T(8,128)(2,1)S(1)} %get-tuple-element.107), channel_id=1, source_target_pairs={{0,4},{1,5},{2,6},{3,7},{4,0},{5,1},{6,2},{7,3},{8,12},{9,13},{10,... | collective-permute-start | bytes 294920 | tf_op jit(solution)/shard_map/ppermute | solution.py:820
  92.3 11.4 %collective-permute-start.17 = (bf16[192,256]{1,0:T(8,128)(2,1)S(1)}, bf16[192,256]{1,0:T(8,128)(2,1)S(1)}, u32[]{:S(2)}, u32[]{:S(2)}) collective-permute-start(bf16[192,256]{1,0:T(8,128)(2,1)S(1)} %get-tuple-element.108), channel_id=1, source_target_pairs={{0,2},{1,3},{2,4},{3,5},{4,6},{5,7},{6,0},{7,1},{8,10},{9,11},{10,... | collective-permute-start | bytes 294920 | tf_op jit(solution)/shard_map/ppermute | solution.py:820
  105.1 3.2 %collective-permute-start.20 = (f32[3,80,128]{2,1,0:T(8,128)S(1)}, f32[3,80,128]{2,1,0:T(8,128)S(1)}, u32[]{:S(2)}, u32[]{:S(2)}) collective-permute-start(f32[3,80,128]{2,1,0:T(8,128)S(1)} %sums.1.refs_7_), channel_id=1, source_target_pairs={{0,1},{1,0},{2,3},{3,2},{4,5},{5,4},{6,7},{7,6},{8,9},{9,8},{10,11... | collective-permute-start | bytes 368648 | tf_op jit(solution)/shard_map/ppermute | solution.py:824
  105.3 26.1 %collective-permute-start.21 = (bf16[1,4,176,768]{3,2,1,0:T(8,128)(2,1)S(1)}, bf16[1,4,176,768]{3,2,1,0:T(8,128)(2,1)S(1)}, u32[]{:S(2)}, u32[]{:S(2)}) collective-permute-start(bf16[1,4,176,768]{3,2,1,0:T(8,128)(2,1)S(1)} %get-tuple-element.121), channel_id=1, source_target_pairs={{0,8},{8,0},{16,24},{24,16},{1,9},{9,1},{17,25},{25,17},{2,10},{10... | collective-permute-start | bytes 3244040 | tf_op jit(solution)/shard_map/ppermute | solution.py:827
  106.8 25.8 %collective-permute-start.22 = (bf16[1,4,176,768]{3,2,1,0:T(8,128)(2,1)S(1)}, bf16[1,4,176,768]{3,2,1,0:T(8,128)(2,1)S(1)}, u32[]{:S(2)}, u32[]{:S(2)}) collective-permute-start(bf16[1,4,176,768]{3,2,1,0:T(8,128)(2,1)S(1)} %get-tuple-element.122), channel_id=1, source_target_pairs={{0,16},{8,24},{16,0},{24,8},{1,17},{9,25},{17,1},{25,9},{2,18},{10... | collective-permute-start | bytes 3244040 | tf_op jit(solution)/shard_map/ppermute | solution.py:827
  132.6 2.3 collective-permute-start.23
  137.5 2.4 %collective-permute-start.27 = (bf16[4,4,32,768]{3,2,1,0:T(8,128)(2,1)S(1)}, bf16[4,4,32,768]{3,2,1,0:T(8,128)(2,1)S(1)}, u32[]{:S(2)}, u32[]{:S(2)}) collective-permute-start(bf16[4,4,32,768]{3,2,1,0:T(8,128)(2,1)S(1)} %get-tuple-element.131), channel_id=1, source_target_pairs={{0,1},{1,0},{2,3},{3,2},{4,5},{5,4},{6,7},{7,6},{8,9},{9,8},{10,11... | collective-permute-start | bytes 2359304 | tf_op jit(solution)/shard_map/ppermute | solution.py:824
  140.3 33.5 %collective-permute-start.28 = (bf16[4,192,768]{2,1,0:T(8,128)(2,1)S(1)}, bf16[4,192,768]{2,1,0:T(8,128)(2,1)S(1)}, u32[]{:S(2)}, u32[]{:S(2)}) collective-permute-start(bf16[4,192,768]{2,1,0:T(8,128)(2,1)S(1)} %get-tuple-element.134), channel_id=1, source_target_pairs={{0,16},{8,24},{16,0},{24,8},{1,17},{9,25},{17,1},{25,9},{2,18},{10... | collective-permute-start | bytes 3538952 | tf_op jit(solution)/shard_map/ppermute | solution.py:827
  141.9 31.9 %collective-permute-start.29 = (bf16[4,192,768]{2,1,0:T(8,128)(2,1)S(1)}, bf16[4,192,768]{2,1,0:T(8,128)(2,1)S(1)}, u32[]{:S(2)}, u32[]{:S(2)}) collective-permute-start(bf16[4,192,768]{2,1,0:T(8,128)(2,1)S(1)} %get-tuple-element.135), channel_id=1, source_target_pairs={{0,8},{8,0},{16,24},{24,16},{1,9},{9,1},{17,25},{25,17},{2,10},{10... | collective-permute-start | bytes 3538952 | tf_op jit(solution)/shard_map/ppermute | solution.py:827
  142.5 9.9 %collective-permute-start.24 = (bf16[3,192,256]{2,1,0:T(8,128)(2,1)S(1)}, bf16[3,192,256]{2,1,0:T(8,128)(2,1)S(1)}, u32[]{:S(2)}, u32[]{:S(2)}) collective-permute-start(bf16[3,192,256]{2,1,0:T(8,128)(2,1)S(1)} %get-tuple-element.126), channel_id=1, source_target_pairs={{0,2},{1,3},{2,4},{3,5},{4,6},{5,7},{6,0},{7,1},{8,10},{9,11},{10,... | collective-permute-start | bytes 884744 | tf_op jit(solution)/shard_map/ppermute | solution.py:820
  142.5 25.2 %collective-permute-start.25 = (bf16[3,192,256]{2,1,0:T(8,128)(2,1)S(1)}, bf16[3,192,256]{2,1,0:T(8,128)(2,1)S(1)}, u32[]{:S(2)}, u32[]{:S(2)}) collective-permute-start(bf16[3,192,256]{2,1,0:T(8,128)(2,1)S(1)} %get-tuple-element.127), channel_id=1, source_target_pairs={{0,4},{1,5},{2,6},{3,7},{4,0},{5,1},{6,2},{7,3},{8,12},{9,13},{10,... | collective-permute-start | bytes 884744 | tf_op jit(solution)/shard_map/ppermute | solution.py:820
  144.9 25.5 %collective-permute-start.26 = (bf16[3,192,256]{2,1,0:T(8,128)(2,1)S(1)}, bf16[3,192,256]{2,1,0:T(8,128)(2,1)S(1)}, u32[]{:S(2)}, u32[]{:S(2)}) collective-permute-start(bf16[3,192,256]{2,1,0:T(8,128)(2,1)S(1)} %get-tuple-element.128), channel_id=1, source_target_pairs={{0,6},{1,7},{2,0},{3,1},{4,2},{5,3},{6,4},{7,5},{8,14},{9,15},{10,... | collective-permute-start | bytes 884744 | tf_op jit(solution)/shard_map/ppermute | solution.py:820
  152.4 21.4 %collective-permute-start.30 = (bf16[4,32,768]{2,1,0:T(8,128)(2,1)S(1)}, bf16[4,32,768]{2,1,0:T(8,128)(2,1)S(1)}, u32[]{:S(2)}, u32[]{:S(2)}) collective-permute-start(bf16[4,32,768]{2,1,0:T(8,128)(2,1)S(1)} %get-tuple-element.136), channel_id=1, source_target_pairs={{0,24},{8,16},{16,8},{24,0},{1,25},{9,17},{17,9},{25,1},{2,26},{10... | collective-permute-start | bytes 589832 | tf_op jit(solution)/shard_map/ppermute | solution.py:827
  175.0 15.0 %collective-permute-start.31 = (bf16[160,768]{1,0:T(8,128)(2,1)S(1)}, bf16[160,768]{1,0:T(8,128)(2,1)S(1)}, u32[]{:S(2)}, u32[]{:S(2)}) collective-permute-start(bf16[160,768]{1,0:T(8,128)(2,1)S(1)} %get-tuple-element.138), channel_id=1, source_target_pairs={{0,2},{1,3},{2,4},{3,5},{4,6},{5,7},{6,0},{7,1},{8,10},{9,11},{10,... | collective-permute-start | bytes 737288 | tf_op jit(solution)/shard_map/ppermute | solution.py:820
  175.0 22.0 %collective-permute-start.32 = (bf16[160,768]{1,0:T(8,128)(2,1)S(1)}, bf16[160,768]{1,0:T(8,128)(2,1)S(1)}, u32[]{:S(2)}, u32[]{:S(2)}) collective-permute-start(bf16[160,768]{1,0:T(8,128)(2,1)S(1)} %get-tuple-element.139), channel_id=1, source_target_pairs={{0,4},{1,5},{2,6},{3,7},{4,0},{5,1},{6,2},{7,3},{8,12},{9,13},{10,... | collective-permute-start | bytes 737288 | tf_op jit(solution)/shard_map/ppermute | solution.py:820
  177.4 23.8 %collective-permute-start.33 = (bf16[160,768]{1,0:T(8,128)(2,1)S(1)}, bf16[160,768]{1,0:T(8,128)(2,1)S(1)}, u32[]{:S(2)}, u32[]{:S(2)}) collective-permute-start(bf16[160,768]{1,0:T(8,128)(2,1)S(1)} %get-tuple-element.140), channel_id=1, source_target_pairs={{0,6},{1,7},{2,0},{3,1},{4,2},{5,3},{6,4},{7,5},{8,14},{9,15},{10,... | collective-permute-start | bytes 737288 | tf_op jit(solution)/shard_map/ppermute | solution.py:820
  190.0 11.3 %collective-permute-start.34 = (bf16[96,768]{1,0:T(8,128)(2,1)S(1)}, bf16[96,768]{1,0:T(8,128)(2,1)S(1)}, u32[]{:S(2)}, u32[]{:S(2)}) collective-permute-start(bf16[96,768]{1,0:T(8,128)(2,1)S(1)} %get-tuple-element.144), channel_id=1, source_target_pairs={{0,2},{1,3},{2,4},{3,5},{4,6},{5,7},{6,0},{7,1},{8,10},{9,11},{10,... | collective-permute-start | bytes 442376 | tf_op jit(solution)/shard_map/ppermute | solution.py:820
  202.9 12.9 %collective-permute-start.35 = (bf16[160,768]{1,0:T(8,128)(2,1)S(1)}, bf16[160,768]{1,0:T(8,128)(2,1)S(1)}, u32[]{:S(2)}, u32[]{:S(2)}) collective-permute-start(bf16[160,768]{1,0:T(8,128)(2,1)S(1)} %fourth.2.refs_5_.refs_0_), channel_id=1, source_target_pairs={{0,8},{8,0},{16,24},{24,16},{1,9},{9,1},{17,25},{25,17},{2,10},{10... | collective-permute-start | bytes 737288 | tf_op jit(solution)/shard_map/ppermute | solution.py:827
  203.6 12.3 %collective-permute-start.36 = (bf16[160,768]{1,0:T(8,128)(2,1)S(1)}, bf16[160,768]{1,0:T(8,128)(2,1)S(1)}, u32[]{:S(2)}, u32[]{:S(2)}) collective-permute-start(bf16[160,768]{1,0:T(8,128)(2,1)S(1)} %fourth.2.refs_5_.refs_0_), channel_id=1, source_target_pairs={{0,16},{8,24},{16,0},{24,8},{1,17},{9,25},{17,1},{25,9},{2,18},{10... | collective-permute-start | bytes 737288 | tf_op jit(solution)/shard_map/ppermute | solution.py:827
  205.1 12.1 %collective-permute-start.37 = (bf16[160,768]{1,0:T(8,128)(2,1)S(1)}, bf16[160,768]{1,0:T(8,128)(2,1)S(1)}, u32[]{:S(2)}, u32[]{:S(2)}) collective-permute-start(bf16[160,768]{1,0:T(8,128)(2,1)S(1)} %fourth.2.refs_5_.refs_0_), channel_id=1, source_target_pairs={{0,24},{8,16},{16,8},{24,0},{1,25},{9,17},{17,9},{25,1},{2,26},{10... | collective-permute-start | bytes 737288 | tf_op jit(solution)/shard_map/ppermute | solution.py:827
  206.6 9.1 %collective-permute-start.38 = (bf16[96,768]{1,0:T(8,128)(2,1)S(1)}, bf16[96,768]{1,0:T(8,128)(2,1)S(1)}, u32[]{:S(2)}, u32[]{:S(2)}) collective-permute-start(bf16[96,768]{1,0:T(8,128)(2,1)S(1)} %get-tuple-element.146), channel_id=1, source_target_pairs={{0,4},{1,5},{2,6},{3,7},{4,0},{5,1},{6,2},{7,3},{8,12},{9,13},{10,... | collective-permute-start | bytes 442376 | tf_op jit(solution)/shard_map/ppermute | solution.py:820
  206.6 9.3 %collective-permute-start.39 = (bf16[96,768]{1,0:T(8,128)(2,1)S(1)}, bf16[96,768]{1,0:T(8,128)(2,1)S(1)}, u32[]{:S(2)}, u32[]{:S(2)}) collective-permute-start(bf16[96,768]{1,0:T(8,128)(2,1)S(1)} %get-tuple-element.147), channel_id=1, source_target_pairs={{0,6},{1,7},{2,0},{3,1},{4,2},{5,3},{6,4},{7,5},{8,14},{9,15},{10,... | collective-permute-start | bytes 442376 | tf_op jit(solution)/shard_map/ppermute | solution.py:820
  217.8 8.4 %collective-permute-start.40 = (bf16[144,768]{1,0:T(8,128)(2,1)S(1)}, bf16[144,768]{1,0:T(8,128)(2,1)S(1)}, u32[]{:S(2)}, u32[]{:S(2)}) collective-permute-start(bf16[144,768]{1,0:T(8,128)(2,1)S(1)} %fourth.3.refs_4_), channel_id=1, source_target_pairs={{0,8},{8,0},{16,24},{24,16},{1,9},{9,1},{17,25},{25,17},{2,10},{10... | collective-permute-start | bytes 663560 | tf_op jit(solution)/shard_map/ppermute | solution.py:827
  218.7 9.8 %collective-permute-start.41 = (bf16[144,768]{1,0:T(8,128)(2,1)S(1)}, bf16[144,768]{1,0:T(8,128)(2,1)S(1)}, u32[]{:S(2)}, u32[]{:S(2)}) collective-permute-start(bf16[144,768]{1,0:T(8,128)(2,1)S(1)} %fourth.3.refs_4_), channel_id=1, source_target_pairs={{0,16},{8,24},{16,0},{24,8},{1,17},{9,25},{17,1},{25,9},{2,18},{10... | collective-permute-start | bytes 663560 | tf_op jit(solution)/shard_map/ppermute | solution.py:827
  220.2 9.2 %collective-permute-start.42 = (bf16[144,768]{1,0:T(8,128)(2,1)S(1)}, bf16[144,768]{1,0:T(8,128)(2,1)S(1)}, u32[]{:S(2)}, u32[]{:S(2)}) collective-permute-start(bf16[144,768]{1,0:T(8,128)(2,1)S(1)} %fourth.3.refs_4_), channel_id=1, source_target_pairs={{0,24},{8,16},{16,8},{24,0},{1,25},{9,17},{17,9},{25,1},{2,26},{10... | collective-permute-start | bytes 663560 | tf_op jit(solution)/shard_map/ppermute | solution.py:827
  (7 other events, 55.3 us)

commit v13 on v12

--- a/solution.py
+++ b/solution.py
@@ -1314,7 +1314,7 @@
         )
         came_a, came_b = [sums[0]], [sums[groups]]
         came_a += [along_groups(sums[hop], hop) for hop in range(1, groups)]
-        late = after(sums[groups + 1 :], came_a[1])
+        late = after(sums[groups + 1 :], came_a[groups - 1])
         came_b += [along_groups(late[hop - 1], hop) for hop in range(1, groups)]
         spread_a = weight_fourth(came_a, lead, 0, (came_b[1], grad_tokens))
         high = keep_u.shape[2] - lead

time: 235 us -> 232 us (0.987)
    ppermute x11, waiting for transfers between devices: 15.4 us -> 11.9 us  [along_dp(): return lax.ppermute(values, 'dp', [(i, i ^ mask) for i in range(n_dp)])]
  transfers between devices with their start and end apart: 43 -> 43, of which waited for: 24 -> 22; matrix products, arithmetic and copies ran while one was open for 5% -> 6% of each run, Pallas kernels for 19% -> 19%
where the time goes in v13:
time: 232 us; the launch traced here: 231 us
  waiting for transfers between devices  90.1 us (39%)
  Pallas kernels  79.7 us (34%)
  starting transfers between devices  43.4 us (19%)
  local copies, waits for them, and re-layouts  11 us (5%)
  other arithmetic  4.8 us (2%)
    ppermute x21, waiting for transfers between devices, along_groups(): return lax.ppermute(values, 'wide', pairs)  71.5 us
    pallas_call x15, Pallas kernels, prefetched(): return lambda *inputs: call(*inputs, *first)  45.2 us
    ppermute x21, starting transfers between devices, along_groups(): return lax.ppermute(values, 'wide', pairs)  28 us
    pallas_call x1, Pallas kernels, per_device(): pl.pallas_call(functools.partial(back_kernel, size=size, groups=groups, g...  20.6 us
    ppermute x11, starting transfers between devices, along_dp(): return lax.ppermute(values, 'dp', [(i, i ^ mask) for i in range(n_dp)])  13.7 us
    pallas_call x1, Pallas kernels, per_device(): pl.pallas_call(functools.partial(forward_kernel, size=size, groups=groups...  13.4 us
    ppermute x11, waiting for transfers between devices, along_dp(): return lax.ppermute(values, 'dp', [(i, i ^ mask) for i in range(n_dp)])  11.9 us
    unnamed x27, local copies, waits for them, and re-layouts  7.05 us
  transfers between devices with their start and end apart: 43, of which 22 were waited for; matrix products, arithmetic and copies ran while one was open for 6% of the time, Pallas kernels for 19%

profile of v13, /device:TPU:8, one launch (start us, length us, event | category | flops | bytes accessed | tf_op | source)
XLA Modules:
  0.0 230.9 jit_solution(7131809279664736996)
XLA Ops:
  4.6 3.1 %collective-permute-start.2 = (s32[3,40,128]{2,1,0:T(8,128)S(1)}, s32[3,40,128]{2,1,0:T(8,128)S(1)}, u32[]{:S(2)}, u32[]{:S(2)}) collective-permute-start(s32[3,40,128]{2,1,0:T(8,128)S(1)} %get-tuple-element.158), channel_id=1, source_target_pairs={{0,4},{1,5},{2,6},{3,7},{4,0},{5,1},{6,2},{7,3},{8,12},{9,13},{10,... | collective-permute-start | bytes 184328 | tf_op jit(solution)/shard_map/ppermute | solution.py:820
  7.7 2.5 %collective-permute-start.3 = (s32[3,40,128]{2,1,0:T(8,128)S(1)}, s32[3,40,128]{2,1,0:T(8,128)S(1)}, u32[]{:S(2)}, u32[]{:S(2)}) collective-permute-start(s32[3,40,128]{2,1,0:T(8,128)S(1)} %get-tuple-element.157), channel_id=1, source_target_pairs={{0,2},{1,3},{2,4},{3,5},{4,6},{5,7},{6,0},{7,1},{8,10},{9,11},{10,... | collective-permute-start | bytes 184328 | tf_op jit(solution)/shard_map/ppermute | solution.py:820
  10.2 2.0 collective-permute-start.9
  12.2 4.3 %copy.69 = bf16[768,1536]{0,1:T(8,128)(2,1)} copy(bf16[768,1536]{1,0:T(8,128)(2,1)} %param.21) | data formatting | bytes 4718592 | tf_op args[7]
  16.5 1.6 copy.68
  20.0 1.9 pad_maximum_fusion
  22.3 1.7 project.4
  24.0 7.6 %bias.1 = (bf16[3,2048,128]{2,1,0:T(8,128)(2,1)S(1)}, s32[3,1,2048]{2,1,0:T(1,128)S(1)}) custom-call(s32[6]{0:T(128)S(1)} %stack.38.info.refs_0_, s32[3,40,128]{2,1,0:T(8,128)S(1)} %table.1.refs_0_, s32[3,40,128]{2,1,0:T(8,128)S(1)} %collective-permute-done.4.refs_1_), custom_call_target="tpu_custom_call" | custom-call | flops 201326592 | bytes 1572864 | tf_op jit(solution)/shard_map/bias/pallas_call | solution.py:848
  31.7 7.5 %collective-permute-done.7.refs_0_ = bf16[256,768]{1,0:T(8,128)(2,1)S(1)} collective-permute-done((bf16[256,768]{1,0:T(8,128)(2,1)S(1)}, bf16[256,768]{1,0:T(8,128)(2,1)S(1)}, u32[]{:S(2)}, u32[]{:S(2)}) %collective-permute-start.7) | collective-permute-done | bytes 393248 | tf_op jit(solution)/shard_map/ppermute | solution.py:820
  39.6 7.4 %collective-permute-done.5.refs_0_ = bf16[256,768]{1,0:T(8,128)(2,1)S(1)} collective-permute-done((bf16[256,768]{1,0:T(8,128)(2,1)S(1)}, bf16[256,768]{1,0:T(8,128)(2,1)S(1)}, u32[]{:S(2)}, u32[]{:S(2)}) %collective-permute-start.5) | collective-permute-done | bytes 393248 | tf_op jit(solution)/shard_map/ppermute | solution.py:820
  48.8 1.7 project.5
  50.5 1.7 project.6
  52.3 1.7 project.7
  54.1 13.4 %attend.1 = (bf16[192,256]{1,0:T(8,128)(2,1)S(1)}, bf16[192,256]{1,0:T(8,128)(2,1)S(1)}, bf16[192,256]{1,0:T(8,128)(2,1)S(1)}, bf16[192,256]{1,0:T(8,128)(2,1)S(...) custom-call(s32[3,1,2048]{2,1,0:T(1,128)S(1)} %get-tuple-element.84.ids_all.refs_1_, ...), custom_call_target="tpu_custom_call" | custom-call | flops 9663676416 | bytes 8000000 | tf_op jit(solution)/shard_map/attend/pallas_call | solution.py:988
  67.8 4.3 %collective-permute-start.13 = (bf16[192,256]{1,0:T(8,128)(2,1)S(1)}, bf16[192,256]{1,0:T(8,128)(2,1)S(1)}, u32[]{:S(2)}, u32[]{:S(2)}) collective-permute-start(bf16[192,256]{1,0:T(8,128)(2,1)S(1)} %get-tuple-element.102), channel_id=1, source_target_pairs={{0,4},{1,5},{2,6},{3,7},{4,0},{5,1},{6,2},{7,3},{8,12},{9,13},{10,... | collective-permute-start | bytes 294920 | tf_op jit(solution)/shard_map/ppermute | solution.py:820
  73.0 5.5 %collective-permute-done.13.refs_2_ = bf16[192,256]{1,0:T(8,128)(2,1)S(1)} collective-permute-done((bf16[192,256]{1,0:T(8,128)(2,1)S(1)}, bf16[192,256]{1,0:T(8,128)(2,1)S(1)}, u32[]{:S(2)}, u32[]{:S(2)}) %collective-permute-start.13) | collective-permute-done | bytes 98336 | tf_op jit(solution)/shard_map/ppermute | solution.py:820
  78.4 2.2 collective-permute-done.14.refs_3_
  80.7 9.9 %feed.1 = (bf16[256,768]{1,0:T(8,128)(2,1)}, f32[256,768]{1,0:T(8,128)S(1)}, bf16[256,5376]{1,0:T(8,128)(2,1)S(1)}, bf16[784,256]{1,0:T(8,128)(2,1)S(1)}, bf16[2...) custom-call(s32[6]{0:T(128)S(1)} %stack.38.info.refs_0_, ...), custom_call_target="tpu_custom_call" | custom-call | flops 4831838208 | bytes 9437184 | tf_op jit(solution)/shard_map/feed/pallas_call | solution.py:848
  92.3 2.9 %collective-permute-start.17 = (bf16[192,256]{1,0:T(8,128)(2,1)S(1)}, bf16[192,256]{1,0:T(8,128)(2,1)S(1)}, u32[]{:S(2)}, u32[]{:S(2)}) collective-permute-start(bf16[192,256]{1,0:T(8,128)(2,1)S(1)} %get-tuple-element.108), channel_id=1, source_target_pairs={{0,2},{1,3},{2,4},{3,5},{4,6},{5,7},{6,0},{7,1},{8,10},{9,11},{10,... | collective-permute-start | bytes 294920 | tf_op jit(solution)/shard_map/ppermute | solution.py:820
  96.3 7.4 %weights.1 = (bf16[1,4,176,768]{3,2,1,0:T(8,128)(2,1)S(1)}, bf16[1,4,48,768]{3,2,1,0:T(8,128)(2,1)S(1)}, bf16[2,4,112,768]{3,2,1,0:T(8,128)(2,1)S(1)}, bf16[1,4,...) custom-call(s32[6]{0:T(128)S(1)} %stack.38.info.refs_0_, ...), custom_call_target="tpu_custom_call" | custom-call | flops 4831838208 | bytes 14155776 | tf_op jit(solution)/shard_map/weights/pallas_call | solution.py:848
  105.3 1.5 collective-permute-start.21
  106.8 1.5 collective-permute-start.22
  108.3 20.6 %back.1 = (bf16[4,192,256]{2,1,0:T(8,128)(2,1)S(1)}, f32[3,128,1024]{2,1,0:T(8,128)S(1)}, bf16[3,128,1024]{2,1,0:T(8,128)(2,1)S(1)}) custom-call(s32[3,1,2048]{2,1,0:T(1,128)S(1)} %get-tuple-element.84.ids_all.refs_1_, bf16[3,192,2048]{2,1,0:T(8,128)(2,1)S(1)} %get-tuple-element.98.feat, bf16[3,2048,128]{2,1,0:T(8,128)(2,1)S(1)} %get-tuple-element.99.kv, ...), custom_call_target="tpu_custom_call" | custom-call | flops 22548578304 | bytes 10000000 | tf_op jit(solution)/shard_map/back/pallas_call | solution.py:1245
  129.0 2.5 %collective-permute-done.21.got_u.refs_2_ = bf16[1,4,176,768]{3,2,1,0:T(8,128)(2,1)S(1)} collective-permute-done((bf16[1,4,176,768]{3,2,1,0:T(8,128)(2,1)S(1)}, bf16[1,4,176,768]{3,2,1,0:T(8,128)(2,1)S(1)}, u32[]{:S(2)}, u32[]{:S(2)}) %collective-permute-start.21) | collective-permute-done | bytes 1081376 | tf_op jit(solution)/shard_map/ppermute | solution.py:827
  132.7 2.3 collective-permute-done.23.refs_2_
  134.9 2.5 %inward.1 = (bf16[3,192,256]{2,1,0:T(8,128)(2,1)S(1)}, bf16[3,192,256]{2,1,0:T(8,128)(2,1)S(1)}, bf16[3,192,256]{2,1,0:T(8,128)(2,1)S(1)}, bf16[3,192,256]{2,1,0...) custom-call(s32[6]{0:T(128)S(1)} %stack.38.info.refs_0_, ...), custom_call_target="tpu_custom_call" | custom-call | flops 905969664 | bytes 4000000 | tf_op jit(solution)/shard_map/inward/pallas_call | solution.py:848
  137.7 2.2 collective-permute-done.27.inner_got.refs_8_
  140.3 1.6 collective-permute-start.28
  142.5 2.4 %collective-permute-start.25 = (bf16[3,192,256]{2,1,0:T(8,128)(2,1)S(1)}, bf16[3,192,256]{2,1,0:T(8,128)(2,1)S(1)}, u32[]{:S(2)}, u32[]{:S(2)}) collective-permute-start(bf16[3,192,256]{2,1,0:T(8,128)(2,1)S(1)} %get-tuple-element.127), channel_id=1, source_target_pairs={{0,4},{1,5},{2,6},{3,7},{4,0},{5,1},{6,2},{7,3},{8,12},{9,13},{10,... | collective-permute-start | bytes 884744 | tf_op jit(solution)/shard_map/ppermute | solution.py:820
  145.7 6.7 %collective-permute-done.24.refs_1_.refs_11_ = bf16[3,192,256]{2,1,0:T(8,128)(2,1)S(1)} collective-permute-done((bf16[3,192,256]{2,1,0:T(8,128)(2,1)S(1)}, bf16[3,192,256]{2,1,0:T(8,128)(2,1)S(1)}, u32[]{:S(2)}, u32[]{:S(2)}) %collective-permute-start.24) | collective-permute-done | bytes 294944 | tf_op jit(solution)/shard_map/ppermute | solution.py:820
  152.4 1.4 collective-permute-start.30
  153.8 13.9 %collective-permute-done.25.refs_2_.refs_12_ = bf16[3,192,256]{2,1,0:T(8,128)(2,1)S(1)} collective-permute-done((bf16[3,192,256]{2,1,0:T(8,128)(2,1)S(1)}, bf16[3,192,256]{2,1,0:T(8,128)(2,1)S(1)}, u32[]{:S(2)}, u32[]{:S(2)}) %collective-permute-start.25) | collective-permute-done | bytes 294944 | tf_op jit(solution)/shard_map/ppermute | solution.py:820
  167.7 2.7 %collective-permute-done.26.refs_3_.refs_13_ = bf16[3,192,256]{2,1,0:T(8,128)(2,1)S(1)} collective-permute-done((bf16[3,192,256]{2,1,0:T(8,128)(2,1)S(1)}, bf16[3,192,256]{2,1,0:T(8,128)(2,1)S(1)}, u32[]{:S(2)}, u32[]{:S(2)}) %collective-permute-start.26) | collective-permute-done | bytes 294944 | tf_op jit(solution)/shard_map/ppermute | solution.py:820
  170.4 3.4 %collective-permute-done.30.refs_9_ = bf16[4,32,768]{2,1,0:T(8,128)(2,1)S(1)} collective-permute-done((bf16[4,32,768]{2,1,0:T(8,128)(2,1)S(1)}, bf16[4,32,768]{2,1,0:T(8,128)(2,1)S(1)}, u32[]{:S(2)}, u32[]{:S(2)}) %collective-permute-start.30) | collective-permute-done | bytes 196640 | tf_op jit(solution)/shard_map/ppermute | solution.py:827
  175.1 1.9 collective-permute-start.31
  177.0 3.0 %collective-permute-start.32 = (bf16[160,768]{1,0:T(8,128)(2,1)S(1)}, bf16[160,768]{1,0:T(8,128)(2,1)S(1)}, u32[]{:S(2)}, u32[]{:S(2)}) collective-permute-start(bf16[160,768]{1,0:T(8,128)(2,1)S(1)} %get-tuple-element.139), channel_id=1, source_target_pairs={{0,4},{1,5},{2,6},{3,7},{4,0},{5,1},{6,2},{7,3},{8,12},{9,13},{10,... | collective-permute-start | bytes 737288 | tf_op jit(solution)/shard_map/ppermute | solution.py:820
  180.0 17.6 %collective-permute-done.33.refs_4_ = bf16[160,768]{1,0:T(8,128)(2,1)S(1)} collective-permute-done((bf16[160,768]{1,0:T(8,128)(2,1)S(1)}, bf16[160,768]{1,0:T(8,128)(2,1)S(1)}, u32[]{:S(2)}, u32[]{:S(2)}) %collective-permute-start.33) | collective-permute-done | bytes 245792 | tf_op jit(solution)/shard_map/ppermute | solution.py:820
  197.6 3.0 %final.1.refs_6_ = bf16[256,768]{1,0:T(8,128)(2,1)} custom-call(s32[6]{0:T(128)S(1)} %stack.38.info.refs_0_, bf16[3,192,256]{2,1,0:T(8,128)(2,1)S(1)} %get-tuple-element.125.refs_0_.refs_10_, bf16[3,192,256]{2,1,0:T(8,128)(2,1)S(1)} %collective-permute-done.24.refs_1_.refs_11_, bf16[3,192,256]{2,1,0:T(8,128)(2,1)S(1)} %collective-permute-done.25.refs_2_.refs_12_, ...), custom_call_target="tpu_custom_call" | custom-call | flops 905969664 | bytes 3538944 | tf_op jit(solution)/shard_map/final/pallas_call | solution.py:848
  200.6 2.1 collective-permute-done.34.refs_5_.refs_2_
  205.0 1.5 collective-permute-start.36
  206.6 1.4 collective-permute-start.37
  208.1 1.5 collective-permute-start.39
  210.7 3.6 %collective-permute-done.38.refs_3_ = bf16[96,768]{1,0:T(8,128)(2,1)S(1)} collective-permute-done((bf16[96,768]{1,0:T(8,128)(2,1)S(1)}, bf16[96,768]{1,0:T(8,128)(2,1)S(1)}, u32[]{:S(2)}, u32[]{:S(2)}) %collective-permute-start.38) | collective-permute-done | bytes 147488 | tf_op jit(solution)/shard_map/ppermute | solution.py:820
  214.2 1.9 collective-permute-done.39.refs_4_
  217.5 1.5 collective-permute-start.41
  221.4 1.4 collective-permute-done.40.refs_5_
  222.8 2.0 collective-permute-done.41.refs_6_
  226.2 3.4 %spread.1 = (f32[96,3072]{1,0:T(8,128)}, f32[96,768]{1,0:T(8,128)}, f32[384,768]{1,0:T(8,128)}, f32[8,768]{1,0:T(8,128)S(1)}, f32[96,768]{1,0:T(8,128)}, /*index=5*/f32[96,1536]{1,0:T(8,128)}, f32[96,128]{1,0:T(8,128)S(1)}) custom-call(s32[6]{0:T(128)S(1)} %stack.38.info.refs_0_, bf16[160,768]{1,0:T(8,128)(2,1)S(1)} %fourth.2.refs_5_.refs_0_, ...), custom_call_target="tpu_custom_call" | custom-call | flops 1000000 | bytes 3538944 | tf_op jit(solution)/shard_map/spread/pallas_call | solution.py:848
  (114 shorter events, 27.6 us)
Async XLA Ops:
  0.6 3.3 %collective-permute-start = (bf16[256,768]{1,0:T(8,128)(2,1)}, bf16[256,768]{1,0:T(8,128)(2,1)S(1)}, u32[]{:S(2)}, u32[]{:S(2)}) collective-permute-start(bf16[256,768]{1,0:T(8,128)(2,1)} %refs_4_.3), channel_id=1, source_target_pairs={{0,1},{1,0},{2,3},{3,2},{4,5},{5,4},{6,7},{7,6},{8,9},{9,8},{10,11... | collective-permute-start | bytes 1179656 | tf_op jit(solution)/shard_map/ppermute | solution.py:824
  4.6 13.6 %collective-permute-start.1 = (s32[3,40,128]{2,1,0:T(8,128)}, s32[3,40,128]{2,1,0:T(8,128)S(1)}, u32[]{:S(2)}, u32[]{:S(2)}) collective-permute-start(s32[3,40,128]{2,1,0:T(8,128)} %get-tuple-element.159), channel_id=1, source_target_pairs={{0,6},{1,7},{2,0},{3,1},{4,2},{5,3},{6,4},{7,5},{8,14},{9,15},{10,... | collective-permute-start | bytes 184328 | tf_op jit(solution)/shard_map/ppermute | solution.py:820
  4.6 13.6 %collective-permute-start.2 = (s32[3,40,128]{2,1,0:T(8,128)S(1)}, s32[3,40,128]{2,1,0:T(8,128)S(1)}, u32[]{:S(2)}, u32[]{:S(2)}) collective-permute-start(s32[3,40,128]{2,1,0:T(8,128)S(1)} %get-tuple-element.158), channel_id=1, source_target_pairs={{0,4},{1,5},{2,6},{3,7},{4,0},{5,1},{6,2},{7,3},{8,12},{9,13},{10,... | collective-permute-start | bytes 184328 | tf_op jit(solution)/shard_map/ppermute | solution.py:820
  7.7 10.5 %collective-permute-start.3 = (s32[3,40,128]{2,1,0:T(8,128)S(1)}, s32[3,40,128]{2,1,0:T(8,128)S(1)}, u32[]{:S(2)}, u32[]{:S(2)}) collective-permute-start(s32[3,40,128]{2,1,0:T(8,128)S(1)} %get-tuple-element.157), channel_id=1, source_target_pairs={{0,2},{1,3},{2,4},{3,5},{4,6},{5,7},{6,0},{7,1},{8,10},{9,11},{10,... | collective-permute-start | bytes 184328 | tf_op jit(solution)/shard_map/ppermute | solution.py:820
  10.2 29.0 %collective-permute-start.7 = (bf16[256,768]{1,0:T(8,128)(2,1)S(1)}, bf16[256,768]{1,0:T(8,128)(2,1)S(1)}, u32[]{:S(2)}, u32[]{:S(2)}) collective-permute-start(bf16[256,768]{1,0:T(8,128)(2,1)S(1)} %copy-done), channel_id=1, source_target_pairs={{0,2},{1,3},{2,4},{3,5},{4,6},{5,7},{6,0},{7,1},{8,10},{9,11},{10,... | collective-permute-start | bytes 1179656 | tf_op jit(solution)/shard_map/ppermute | solution.py:820
  10.2 29.5 %collective-permute-start.9 = (bf16[256,768]{1,0:T(8,128)(2,1)S(1)}, bf16[256,768]{1,0:T(8,128)(2,1)S(1)}, u32[]{:S(2)}, u32[]{:S(2)}) collective-permute-start(bf16[256,768]{1,0:T(8,128)(2,1)S(1)} %copy-done), channel_id=1, source_target_pairs={{0,6},{1,7},{2,0},{3,1},{4,2},{5,3},{6,4},{7,5},{8,14},{9,15},{10,... | collective-permute-start | bytes 1179656 | tf_op jit(solution)/shard_map/ppermute | solution.py:820
  18.8 5.3 %collective-permute-start.4 = (s32[3,40,128]{2,1,0:T(8,128)S(1)}, s32[3,40,128]{2,1,0:T(8,128)S(1)}, u32[]{:S(2)}, u32[]{:S(2)}) collective-permute-start(s32[3,40,128]{2,1,0:T(8,128)S(1)} %table.1.refs_0_), channel_id=1, source_target_pairs={{0,1},{1,0},{2,3},{3,2},{4,5},{5,4},{6,7},{7,6},{8,9},{9,8},{10,11... | collective-permute-start | bytes 184328 | tf_op jit(solution)/shard_map/ppermute | solution.py:824
  18.9 28.2 %collective-permute-start.5 = (bf16[256,768]{1,0:T(8,128)(2,1)S(1)}, bf16[256,768]{1,0:T(8,128)(2,1)S(1)}, u32[]{:S(2)}, u32[]{:S(2)}) collective-permute-start(bf16[256,768]{1,0:T(8,128)(2,1)S(1)} %copy-done), channel_id=1, source_target_pairs={{0,4},{1,5},{2,6},{3,7},{4,0},{5,1},{6,2},{7,3},{8,12},{9,13},{10,... | collective-permute-start | bytes 1179656 | tf_op jit(solution)/shard_map/ppermute | solution.py:820
  19.8 27.2 %collective-permute-start.10 = (bf16[256,768]{1,0:T(8,128)(2,1)S(1)}, bf16[256,768]{1,0:T(8,128)(2,1)S(1)}, u32[]{:S(2)}, u32[]{:S(2)}) collective-permute-start(bf16[256,768]{1,0:T(8,128)(2,1)S(1)} %copy-done.3), channel_id=1, source_target_pairs={{0,1},{1,0},{2,3},{3,2},{4,5},{5,4},{6,7},{7,6},{8,9},{9,8},{10,11... | collective-permute-start | bytes 1179656 | tf_op jit(solution)/shard_map/ppermute | solution.py:824
  47.1 1.7 collective-permute-start.11
  47.1 3.4 %collective-permute-start.8 = (bf16[256,768]{1,0:T(8,128)(2,1)S(1)}, bf16[256,768]{1,0:T(8,128)(2,1)S(1)}, u32[]{:S(2)}, u32[]{:S(2)}) collective-permute-start(bf16[256,768]{1,0:T(8,128)(2,1)S(1)} %collective-permute-done.7.refs_0_), channel_id=1, source_target_pairs={{0,1},{1,0},{2,3},{3,2},{4,5},{5,4},{6,7},{7,6},{8,9},{9,8},{10,11... | collective-permute-start | bytes 1179656 | tf_op jit(solution)/shard_map/ppermute | solution.py:824
  47.6 4.7 %collective-permute-start.6 = (bf16[256,768]{1,0:T(8,128)(2,1)S(1)}, bf16[256,768]{1,0:T(8,128)(2,1)S(1)}, u32[]{:S(2)}, u32[]{:S(2)}) collective-permute-start(bf16[256,768]{1,0:T(8,128)(2,1)S(1)} %collective-permute-done.5.refs_0_), channel_id=1, source_target_pairs={{0,1},{1,0},{2,3},{3,2},{4,5},{5,4},{6,7},{7,6},{8,9},{9,8},{10,11... | collective-permute-start | bytes 1179656 | tf_op jit(solution)/shard_map/ppermute | solution.py:824
  52.3 28.4 %slice-start = ((s8[4718592]{0:T(1024)(128)(4,1)}), s8[4194304]{0:T(1024)(128)(4,1)S(1)}, s32[]{:S(2)}) async-start(s8[4718592]{0:T(1024)(128)(4,1)} %bitcast.37), calls=%async_computation | async-start | bytes 8388608
  52.3 28.4 %slice-start.2 = ((s8[4718592]{0:T(1024)(128)(4,1)}), s8[4194304]{0:T(1024)(128)(4,1)S(1)}, s32[]{:S(2)}) async-start(s8[4718592]{0:T(1024)(128)(4,1)} %bitcast.39), calls=%async_computation.2 | async-start | bytes 8388608
  54.0 26.6 %slice-start.1 = ((s8[4718592]{0:T(1024)(128)(4,1)}), s8[524288]{0:T(1024)(128)(4,1)S(1)}, s32[]{:S(2)}) async-start(s8[4718592]{0:T(1024)(128)(4,1)} %bitcast.37), calls=%async_computation.1 | async-start | bytes 1048576
  54.1 26.6 %slice-start.3 = ((s8[4718592]{0:T(1024)(128)(4,1)}), s8[524288]{0:T(1024)(128)(4,1)S(1)}, s32[]{:S(2)}) async-start(s8[4718592]{0:T(1024)(128)(4,1)} %bitcast.39), calls=%async_computation.3 | async-start | bytes 1048576
  54.1 26.6 %copy-start.2 = (bf16[768,768]{1,0:T(8,128)(2,1)S(1)}, bf16[768,768]{1,0:T(8,128)(2,1)}, u32[]{:S(2)}) copy-start(bf16[768,768]{1,0:T(8,128)(2,1)} %param.22) | copy-start | bytes 3538948
  67.5 5.5 %collective-permute-start.12 = (bf16[192,256]{1,0:T(8,128)(2,1)S(1)}, bf16[192,256]{1,0:T(8,128)(2,1)S(1)}, u32[]{:S(2)}, u32[]{:S(2)}) collective-permute-start(bf16[192,256]{1,0:T(8,128)(2,1)S(1)} %get-tuple-element.101), channel_id=1, source_target_pairs={{0,2},{1,3},{2,4},{3,5},{4,6},{5,7},{6,0},{7,1},{8,10},{9,11},{10,... | collective-permute-start | bytes 294920 | tf_op jit(solution)/shard_map/ppermute | solution.py:820
  67.8 10.6 %collective-permute-start.13 = (bf16[192,256]{1,0:T(8,128)(2,1)S(1)}, bf16[192,256]{1,0:T(8,128)(2,1)S(1)}, u32[]{:S(2)}, u32[]{:S(2)}) collective-permute-start(bf16[192,256]{1,0:T(8,128)(2,1)S(1)} %get-tuple-element.102), channel_id=1, source_target_pairs={{0,4},{1,5},{2,6},{3,7},{4,0},{5,1},{6,2},{7,3},{8,12},{9,13},{10,... | collective-permute-start | bytes 294920 | tf_op jit(solution)/shard_map/ppermute | solution.py:820
  72.1 8.5 %collective-permute-start.14 = (bf16[192,256]{1,0:T(8,128)(2,1)S(1)}, bf16[192,256]{1,0:T(8,128)(2,1)S(1)}, u32[]{:S(2)}, u32[]{:S(2)}) collective-permute-start(bf16[192,256]{1,0:T(8,128)(2,1)S(1)} %get-tuple-element.103), channel_id=1, source_target_pairs={{0,6},{1,7},{2,0},{3,1},{4,2},{5,3},{6,4},{7,5},{8,14},{9,15},{10,... | collective-permute-start | bytes 294920 | tf_op jit(solution)/shard_map/ppermute | solution.py:820
  90.6 5.7 %collective-permute-start.18 = (bf16[256,5376]{1,0:T(8,128)(2,1)S(1)}, bf16[256,5376]{1,0:T(8,128)(2,1)S(1)}, u32[]{:S(2)}, u32[]{:S(2)}) collective-permute-start(bf16[256,5376]{1,0:T(8,128)(2,1)S(1)} %get-tuple-element.112.refs_0_.refs_2_), channel_id=1, source_target_pairs={{0,1},{1,0},{2,3},{3,2},{4,5},{5,4},{6,7},{7,6},{8,9},{9,8},{10,11... | collective-permute-start | bytes 8257544 | tf_op jit(solution)/shard_map/ppermute | solution.py:824
  90.6 5.7 %collective-permute-start.19 = (bf16[784,256]{1,0:T(8,128)(2,1)S(1)}, bf16[784,256]{1,0:T(8,128)(2,1)S(1)}, u32[]{:S(2)}, u32[]{:S(2)}) collective-permute-start(bf16[784,256]{1,0:T(8,128)(2,1)S(1)} %get-tuple-element.115), channel_id=1, source_target_pairs={{0,1},{1,0},{2,3},{3,2},{4,5},{5,4},{6,7},{7,6},{8,9},{9,8},{10,11... | collective-permute-start | bytes 1204232 | tf_op jit(solution)/shard_map/ppermute | solution.py:824
  91.1 12.6 %collective-permute-start.15 = (bf16[192,256]{1,0:T(8,128)(2,1)S(1)}, bf16[192,256]{1,0:T(8,128)(2,1)S(1)}, u32[]{:S(2)}, u32[]{:S(2)}) collective-permute-start(bf16[192,256]{1,0:T(8,128)(2,1)S(1)} %get-tuple-element.106), channel_id=1, source_target_pairs={{0,6},{1,7},{2,0},{3,1},{4,2},{5,3},{6,4},{7,5},{8,14},{9,15},{10,... | collective-permute-start | bytes 294920 | tf_op jit(solution)/shard_map/ppermute | solution.py:820
  91.2 12.5 %collective-permute-start.16 = (bf16[192,256]{1,0:T(8,128)(2,1)S(1)}, bf16[192,256]{1,0:T(8,128)(2,1)S(1)}, u32[]{:S(2)}, u32[]{:S(2)}) collective-permute-start(bf16[192,256]{1,0:T(8,128)(2,1)S(1)} %get-tuple-element.107), channel_id=1, source_target_pairs={{0,4},{1,5},{2,6},{3,7},{4,0},{5,1},{6,2},{7,3},{8,12},{9,13},{10,... | collective-permute-start | bytes 294920 | tf_op jit(solution)/shard_map/ppermute | solution.py:820
  92.3 11.4 %collective-permute-start.17 = (bf16[192,256]{1,0:T(8,128)(2,1)S(1)}, bf16[192,256]{1,0:T(8,128)(2,1)S(1)}, u32[]{:S(2)}, u32[]{:S(2)}) collective-permute-start(bf16[192,256]{1,0:T(8,128)(2,1)S(1)} %get-tuple-element.108), channel_id=1, source_target_pairs={{0,2},{1,3},{2,4},{3,5},{4,6},{5,7},{6,0},{7,1},{8,10},{9,11},{10,... | collective-permute-start | bytes 294920 | tf_op jit(solution)/shard_map/ppermute | solution.py:820
  105.1 3.2 %collective-permute-start.20 = (f32[3,80,128]{2,1,0:T(8,128)S(1)}, f32[3,80,128]{2,1,0:T(8,128)S(1)}, u32[]{:S(2)}, u32[]{:S(2)}) collective-permute-start(f32[3,80,128]{2,1,0:T(8,128)S(1)} %sums.1.refs_7_), channel_id=1, source_target_pairs={{0,1},{1,0},{2,3},{3,2},{4,5},{5,4},{6,7},{7,6},{8,9},{9,8},{10,11... | collective-permute-start | bytes 368648 | tf_op jit(solution)/shard_map/ppermute | solution.py:824
  105.3 26.1 %collective-permute-start.21 = (bf16[1,4,176,768]{3,2,1,0:T(8,128)(2,1)S(1)}, bf16[1,4,176,768]{3,2,1,0:T(8,128)(2,1)S(1)}, u32[]{:S(2)}, u32[]{:S(2)}) collective-permute-start(bf16[1,4,176,768]{3,2,1,0:T(8,128)(2,1)S(1)} %get-tuple-element.121), channel_id=1, source_target_pairs={{0,8},{8,0},{16,24},{24,16},{1,9},{9,1},{17,25},{25,17},{2,10},{10... | collective-permute-start | bytes 3244040 | tf_op jit(solution)/shard_map/ppermute | solution.py:827
  106.8 25.8 %collective-permute-start.22 = (bf16[1,4,176,768]{3,2,1,0:T(8,128)(2,1)S(1)}, bf16[1,4,176,768]{3,2,1,0:T(8,128)(2,1)S(1)}, u32[]{:S(2)}, u32[]{:S(2)}) collective-permute-start(bf16[1,4,176,768]{3,2,1,0:T(8,128)(2,1)S(1)} %get-tuple-element.122), channel_id=1, source_target_pairs={{0,16},{8,24},{16,0},{24,8},{1,17},{9,25},{17,1},{25,9},{2,18},{10... | collective-permute-start | bytes 3244040 | tf_op jit(solution)/shard_map/ppermute | solution.py:827
  132.6 2.3 collective-permute-start.23
  137.5 2.4 %collective-permute-start.27 = (bf16[4,4,32,768]{3,2,1,0:T(8,128)(2,1)S(1)}, bf16[4,4,32,768]{3,2,1,0:T(8,128)(2,1)S(1)}, u32[]{:S(2)}, u32[]{:S(2)}) collective-permute-start(bf16[4,4,32,768]{3,2,1,0:T(8,128)(2,1)S(1)} %get-tuple-element.131), channel_id=1, source_target_pairs={{0,1},{1,0},{2,3},{3,2},{4,5},{5,4},{6,7},{7,6},{8,9},{9,8},{10,11... | collective-permute-start | bytes 2359304 | tf_op jit(solution)/shard_map/ppermute | solution.py:824
  140.3 33.5 %collective-permute-start.28 = (bf16[4,192,768]{2,1,0:T(8,128)(2,1)S(1)}, bf16[4,192,768]{2,1,0:T(8,128)(2,1)S(1)}, u32[]{:S(2)}, u32[]{:S(2)}) collective-permute-start(bf16[4,192,768]{2,1,0:T(8,128)(2,1)S(1)} %get-tuple-element.134), channel_id=1, source_target_pairs={{0,16},{8,24},{16,0},{24,8},{1,17},{9,25},{17,1},{25,9},{2,18},{10... | collective-permute-start | bytes 3538952 | tf_op jit(solution)/shard_map/ppermute | solution.py:827
  141.9 31.9 %collective-permute-start.29 = (bf16[4,192,768]{2,1,0:T(8,128)(2,1)S(1)}, bf16[4,192,768]{2,1,0:T(8,128)(2,1)S(1)}, u32[]{:S(2)}, u32[]{:S(2)}) collective-permute-start(bf16[4,192,768]{2,1,0:T(8,128)(2,1)S(1)} %get-tuple-element.135), channel_id=1, source_target_pairs={{0,8},{8,0},{16,24},{24,16},{1,9},{9,1},{17,25},{25,17},{2,10},{10... | collective-permute-start | bytes 3538952 | tf_op jit(solution)/shard_map/ppermute | solution.py:827
  142.5 9.9 %collective-permute-start.24 = (bf16[3,192,256]{2,1,0:T(8,128)(2,1)S(1)}, bf16[3,192,256]{2,1,0:T(8,128)(2,1)S(1)}, u32[]{:S(2)}, u32[]{:S(2)}) collective-permute-start(bf16[3,192,256]{2,1,0:T(8,128)(2,1)S(1)} %get-tuple-element.126), channel_id=1, source_target_pairs={{0,2},{1,3},{2,4},{3,5},{4,6},{5,7},{6,0},{7,1},{8,10},{9,11},{10,... | collective-permute-start | bytes 884744 | tf_op jit(solution)/shard_map/ppermute | solution.py:820
  142.5 25.2 %collective-permute-start.25 = (bf16[3,192,256]{2,1,0:T(8,128)(2,1)S(1)}, bf16[3,192,256]{2,1,0:T(8,128)(2,1)S(1)}, u32[]{:S(2)}, u32[]{:S(2)}) collective-permute-start(bf16[3,192,256]{2,1,0:T(8,128)(2,1)S(1)} %get-tuple-element.127), channel_id=1, source_target_pairs={{0,4},{1,5},{2,6},{3,7},{4,0},{5,1},{6,2},{7,3},{8,12},{9,13},{10,... | collective-permute-start | bytes 884744 | tf_op jit(solution)/shard_map/ppermute | solution.py:820
  144.9 25.5 %collective-permute-start.26 = (bf16[3,192,256]{2,1,0:T(8,128)(2,1)S(1)}, bf16[3,192,256]{2,1,0:T(8,128)(2,1)S(1)}, u32[]{:S(2)}, u32[]{:S(2)}) collective-permute-start(bf16[3,192,256]{2,1,0:T(8,128)(2,1)S(1)} %get-tuple-element.128), channel_id=1, source_target_pairs={{0,6},{1,7},{2,0},{3,1},{4,2},{5,3},{6,4},{7,5},{8,14},{9,15},{10,... | collective-permute-start | bytes 884744 | tf_op jit(solution)/shard_map/ppermute | solution.py:820
  152.4 21.4 %collective-permute-start.30 = (bf16[4,32,768]{2,1,0:T(8,128)(2,1)S(1)}, bf16[4,32,768]{2,1,0:T(8,128)(2,1)S(1)}, u32[]{:S(2)}, u32[]{:S(2)}) collective-permute-start(bf16[4,32,768]{2,1,0:T(8,128)(2,1)S(1)} %get-tuple-element.136), channel_id=1, source_target_pairs={{0,24},{8,16},{16,8},{24,0},{1,25},{9,17},{17,9},{25,1},{2,26},{10... | collective-permute-start | bytes 589832 | tf_op jit(solution)/shard_map/ppermute | solution.py:827
  175.0 22.6 %collective-permute-start.33 = (bf16[160,768]{1,0:T(8,128)(2,1)S(1)}, bf16[160,768]{1,0:T(8,128)(2,1)S(1)}, u32[]{:S(2)}, u32[]{:S(2)}) collective-permute-start(bf16[160,768]{1,0:T(8,128)(2,1)S(1)} %get-tuple-element.140), channel_id=1, source_target_pairs={{0,6},{1,7},{2,0},{3,1},{4,2},{5,3},{6,4},{7,5},{8,14},{9,15},{10,... | collective-permute-start | bytes 737288 | tf_op jit(solution)/shard_map/ppermute | solution.py:820
  175.1 25.5 %collective-permute-start.31 = (bf16[160,768]{1,0:T(8,128)(2,1)S(1)}, bf16[160,768]{1,0:T(8,128)(2,1)S(1)}, u32[]{:S(2)}, u32[]{:S(2)}) collective-permute-start(bf16[160,768]{1,0:T(8,128)(2,1)S(1)} %get-tuple-element.138), channel_id=1, source_target_pairs={{0,2},{1,3},{2,4},{3,5},{4,6},{5,7},{6,0},{7,1},{8,10},{9,11},{10,... | collective-permute-start | bytes 737288 | tf_op jit(solution)/shard_map/ppermute | solution.py:820
  177.0 23.6 %collective-permute-start.32 = (bf16[160,768]{1,0:T(8,128)(2,1)S(1)}, bf16[160,768]{1,0:T(8,128)(2,1)S(1)}, u32[]{:S(2)}, u32[]{:S(2)}) collective-permute-start(bf16[160,768]{1,0:T(8,128)(2,1)S(1)} %get-tuple-element.139), channel_id=1, source_target_pairs={{0,4},{1,5},{2,6},{3,7},{4,0},{5,1},{6,2},{7,3},{8,12},{9,13},{10,... | collective-permute-start | bytes 737288 | tf_op jit(solution)/shard_map/ppermute | solution.py:820
  197.6 5.1 %collective-permute-start.34 = (bf16[96,768]{1,0:T(8,128)(2,1)S(1)}, bf16[96,768]{1,0:T(8,128)(2,1)S(1)}, u32[]{:S(2)}, u32[]{:S(2)}) collective-permute-start(bf16[96,768]{1,0:T(8,128)(2,1)S(1)} %get-tuple-element.144), channel_id=1, source_target_pairs={{0,2},{1,3},{2,4},{3,5},{4,6},{5,7},{6,0},{7,1},{8,10},{9,11},{10,... | collective-permute-start | bytes 442376 | tf_op jit(solution)/shard_map/ppermute | solution.py:820
  204.4 11.7 %collective-permute-start.35 = (bf16[160,768]{1,0:T(8,128)(2,1)S(1)}, bf16[160,768]{1,0:T(8,128)(2,1)S(1)}, u32[]{:S(2)}, u32[]{:S(2)}) collective-permute-start(bf16[160,768]{1,0:T(8,128)(2,1)S(1)} %fourth.2.refs_5_.refs_0_), channel_id=1, source_target_pairs={{0,8},{8,0},{16,24},{24,16},{1,9},{9,1},{17,25},{25,17},{2,10},{10... | collective-permute-start | bytes 737288 | tf_op jit(solution)/shard_map/ppermute | solution.py:827
  205.0 11.1 %collective-permute-start.36 = (bf16[160,768]{1,0:T(8,128)(2,1)S(1)}, bf16[160,768]{1,0:T(8,128)(2,1)S(1)}, u32[]{:S(2)}, u32[]{:S(2)}) collective-permute-start(bf16[160,768]{1,0:T(8,128)(2,1)S(1)} %fourth.2.refs_5_.refs_0_), channel_id=1, source_target_pairs={{0,16},{8,24},{16,0},{24,8},{1,17},{9,25},{17,1},{25,9},{2,18},{10... | collective-permute-start | bytes 737288 | tf_op jit(solution)/shard_map/ppermute | solution.py:827
  206.6 9.6 %collective-permute-start.37 = (bf16[160,768]{1,0:T(8,128)(2,1)S(1)}, bf16[160,768]{1,0:T(8,128)(2,1)S(1)}, u32[]{:S(2)}, u32[]{:S(2)}) collective-permute-start(bf16[160,768]{1,0:T(8,128)(2,1)S(1)} %fourth.2.refs_5_.refs_0_), channel_id=1, source_target_pairs={{0,24},{8,16},{16,8},{24,0},{1,25},{9,17},{17,9},{25,1},{2,26},{10... | collective-permute-start | bytes 737288 | tf_op jit(solution)/shard_map/ppermute | solution.py:827
  208.0 6.2 %collective-permute-start.38 = (bf16[96,768]{1,0:T(8,128)(2,1)S(1)}, bf16[96,768]{1,0:T(8,128)(2,1)S(1)}, u32[]{:S(2)}, u32[]{:S(2)}) collective-permute-start(bf16[96,768]{1,0:T(8,128)(2,1)S(1)} %get-tuple-element.146), channel_id=1, source_target_pairs={{0,4},{1,5},{2,6},{3,7},{4,0},{5,1},{6,2},{7,3},{8,12},{9,13},{10,... | collective-permute-start | bytes 442376 | tf_op jit(solution)/shard_map/ppermute | solution.py:820
  208.1 8.0 %collective-permute-start.39 = (bf16[96,768]{1,0:T(8,128)(2,1)S(1)}, bf16[96,768]{1,0:T(8,128)(2,1)S(1)}, u32[]{:S(2)}, u32[]{:S(2)}) collective-permute-start(bf16[96,768]{1,0:T(8,128)(2,1)S(1)} %get-tuple-element.147), channel_id=1, source_target_pairs={{0,6},{1,7},{2,0},{3,1},{4,2},{5,3},{6,4},{7,5},{8,14},{9,15},{10,... | collective-permute-start | bytes 442376 | tf_op jit(solution)/shard_map/ppermute | solution.py:820
  216.8 6.0 %collective-permute-start.40 = (bf16[144,768]{1,0:T(8,128)(2,1)S(1)}, bf16[144,768]{1,0:T(8,128)(2,1)S(1)}, u32[]{:S(2)}, u32[]{:S(2)}) collective-permute-start(bf16[144,768]{1,0:T(8,128)(2,1)S(1)} %fourth.3.refs_4_), channel_id=1, source_target_pairs={{0,8},{8,0},{16,24},{24,16},{1,9},{9,1},{17,25},{25,17},{2,10},{10... | collective-permute-start | bytes 663560 | tf_op jit(solution)/shard_map/ppermute | solution.py:827
  217.5 7.4 %collective-permute-start.41 = (bf16[144,768]{1,0:T(8,128)(2,1)S(1)}, bf16[144,768]{1,0:T(8,128)(2,1)S(1)}, u32[]{:S(2)}, u32[]{:S(2)}) collective-permute-start(bf16[144,768]{1,0:T(8,128)(2,1)S(1)} %fourth.3.refs_4_), channel_id=1, source_target_pairs={{0,16},{8,24},{16,0},{24,8},{1,17},{9,25},{17,1},{25,9},{2,18},{10... | collective-permute-start | bytes 663560 | tf_op jit(solution)/shard_map/ppermute | solution.py:827
  219.0 7.2 %collective-permute-start.42 = (bf16[144,768]{1,0:T(8,128)(2,1)S(1)}, bf16[144,768]{1,0:T(8,128)(2,1)S(1)}, u32[]{:S(2)}, u32[]{:S(2)}) collective-permute-start(bf16[144,768]{1,0:T(8,128)(2,1)S(1)} %fourth.3.refs_4_), channel_id=1, source_target_pairs={{0,24},{8,16},{16,8},{24,0},{1,25},{9,17},{17,9},{25,1},{2,26},{10... | collective-permute-start | bytes 663560 | tf_op jit(solution)/shard_map/ppermute | solution.py:827
  (7 other events, 55.3 us)
